TPU v7x, 32 devices: a whole 2x2x4 slice. The times are simulated.
32 devices in a mesh: dp: 4 (over y, x), expert: 8 (over z, core).
Axes of the slice: x: 2, y: 2, z: 4, core: 2. Of those that a mesh axis runs over, the one named last changes fastest.
Arguments:
- tokens: bfloat16 [4096, 3584], P(('dp', 'expert')), may hold values from -6 to 6
- gate_up: bfloat16 [8, 3584, 2048], P('expert', 'dp'), may hold values from -0.09375 to 0.09375
- down_proj: bfloat16 [8, 1024, 3584], P('expert', None, 'dp'), may hold values from -0.1875 to 0.1875
- expert_ids: int32 [4096, 8], P(('dp', 'expert')), may hold values from 0 to 31, all different within a row; in each aligned block of 128 rows (0 to 127, 128 to 255, ...) at most 64 rows name the same one
- gate_weights: bfloat16 [4096, 8], P(('dp', 'expert')), may hold values from 0.049804688 to 1
Outputs:
- mixed: bfloat16 [4096, 3584], P(('dp', 'expert'))
Inputs may be any that keep to these rules, and one draw needn't show every extreme that they name: `expert_ids`: A row names 8 different experts. Among the rows of one device (aligned blocks of 128 rows), no expert is named by more than 64 rows.
All inputs are finite; a program needn't handle non-finite values.
Results may differ from a plain program's by a relative error of at most 0.0058.
Values may be sent and summed in bfloat16 or wider, within the bound.
No kernel may reach another device: no remote copies, remote signals or barrier semaphores. Data moves between devices by JAX's collectives and lax.ppermute only.
A program may use at most 128 MiB of HBM per device.

v0:
```python
import jax
import jax.numpy as jnp
from jax import lax
from jax.sharding import PartitionSpec as P


def local(tokens, gate_up, down_proj, expert_ids, gate_weights):
    owners = lax.axis_size("expert")
    tok_rows = tokens.shape[0]
    width = tokens.shape[1]
    hidden_units = down_proj.shape[1]
    slots = 4 * tok_rows // owners
    total_rows = owners * slots
    owner_ids = jnp.arange(owners, dtype=jnp.int32)
    matches = expert_ids[:, :, None] == owner_ids[None, None, :]
    hits = jnp.sum(matches.astype(jnp.int32), axis=1)
    pick_weight = jnp.sum(
        jnp.where(matches, gate_weights[:, :, None].astype(jnp.float32), 0.0), axis=1
    )
    before = jnp.cumsum(hits, axis=0) - hits
    target = jnp.where(hits > 0, owner_ids[None, :] * slots + before, -1)
    slot_owner = jnp.arange(total_rows, dtype=jnp.int32) // slots
    slot_ids = jnp.arange(total_rows, dtype=jnp.int32)
    placed = jnp.take(target, slot_owner, axis=1) == slot_ids[None, :]
    place_bf = placed.astype(jnp.bfloat16)
    outgoing = jnp.dot(place_bf.T, tokens, preferred_element_type=jnp.float32).astype(jnp.bfloat16)
    arrived = lax.all_to_all(
        outgoing.reshape(owners, slots, width), "expert", split_axis=0, concat_axis=0, tiled=True
    )
    rows = arrived.reshape(total_rows, width)
    gu = jnp.dot(
        rows,
        lax.all_gather(gate_up, "dp", axis=1, tiled=True)[0],
        preferred_element_type=jnp.float32,
    )
    hidden = (jax.nn.silu(gu[:, :hidden_units]) * gu[:, hidden_units:]).astype(jnp.bfloat16)
    result = jnp.dot(
        hidden,
        lax.all_gather(down_proj, "dp", axis=2, tiled=True)[0],
        preferred_element_type=jnp.float32,
    ).astype(jnp.bfloat16)
    returned = lax.all_to_all(
        result.reshape(owners, slots, width), "expert", split_axis=0, concat_axis=0, tiled=True
    )
    weighted = (place_bf.astype(jnp.float32) * jnp.take(pick_weight, slot_owner, axis=1)).astype(
        jnp.bfloat16
    )
    mixed = jnp.dot(
        weighted, returned.reshape(total_rows, width), preferred_element_type=jnp.float32
    )
    return mixed.astype(jnp.bfloat16)


def solution(mesh):
    placed = (
        P(("dp", "expert"), None),
        P("expert", "dp", None),
        P("expert", None, "dp"),
        P(("dp", "expert"), None),
        P(("dp", "expert"), None),
    )
    return jax.shard_map(
        local, mesh=mesh, in_specs=placed, out_specs=P(("dp", "expert"), None), check_vma=False
    )
```

profile of v0, /device:TPU:0, one launch (start us, length us, event | category | flops | bytes accessed | tf_op | source)
XLA Modules:
  0.0 341.0 jit_solution(3092891940866027433)
XLA Ops:
  6.5 0.0 copy-start
  6.5 0.0 copy-start.1
  6.5 0.0 all-gather.3.cloned.1.call-start
  6.5 0.7 all-gather.3.cloned.1.call-update
  7.3 0.0 all-gather.5.cloned.1.call-start
  7.3 0.7 all-gather.5.cloned.1.call-update
  8.0 0.0 copy-done.1
  8.0 0.1 copy.26
  8.1 0.2 reduce_window_sum.11
  8.4 0.1 add_select_fusion
  8.5 1.0 gather_fusion
  9.5 0.1 bitcast_compare_fusion
  9.7 0.0 copy-done
  9.7 1.1 convolution_convert_fusion
  10.8 89.0 %all_to_all.10 = bf16[8,64,3584]{2,1,0:T(8,128)(2,1)} all-to-all(bf16[8,64,3584]{2,1,0:T(8,128)(2,1)S(1)} %bitcast.24), channel_id=1, replica_groups=mesh['dp'=4,'expert'=8] {'expert'}, dimensions={0} | all-to-all | bytes 7340032 | tf_op jit(solution)/shard_map/all_to_all | solution.py:27
  99.8 52.1 %all-gather.3.cloned.1.call-done = bf16[1,3584,2048]{2,1,0:T(8,128)(2,1)} async-done(((bf16[1,896,2048]{2,1,0:T(8,128)(2,1)}), bf16[1,3584,2048]{2,1,0:T(8,128)(2,1)}) %all-gather.3.cloned.1.call-update) | async-done | bytes 14680080 | tf_op jit(solution)/shard_map/all_gather | solution.py:33
  151.9 13.5 %fusion = f32[512,2048]{1,0:T(8,128)} fusion(bf16[512,3584]{1,0:T(8,128)(2,1)} %bitcast.26, bf16[1,3584,2048]{2,1,0:T(8,128)(2,1)} %all-gather.3.cloned.1.call-done), kind=kOutput, calls=%fused_computation.2 | convolution fusion | flops 7516192768 | bytes 22544384 | tf_op jit(solution)/shard_map/dot_general | solution.py:31
  165.4 67.3 %all-gather.5.cloned.1.call-done = bf16[1,1024,3584]{2,1,0:T(8,128)(2,1)} async-done(((bf16[1,1024,896]{2,1,0:T(8,128)(2,1)}), bf16[1,1024,3584]{2,1,0:T(8,128)(2,1)}) %all-gather.5.cloned.1.call-update) | async-done | bytes 7340048 | tf_op jit(solution)/shard_map/all_gather | solution.py:39
  232.7 10.1 %fusion.4 = bf16[512,3584]{1,0:T(8,128)(2,1)} fusion(bf16[1,1024,3584]{2,1,0:T(8,128)(2,1)} %all-gather.5.cloned.1.call-done, f32[512,2048]{1,0:T(8,128)} %fusion), kind=kOutput, calls=%fused_computation.6 | convolution fusion | flops 3763077120 | bytes 15204352 | tf_op jit(solution)/shard_map/dot_general | solution.py:37
  242.8 0.0 copy-start.2
  242.8 4.7 %all-to-all-start.1 = ((bf16[8,64,3584]{2,1,0:T(8,128)(2,1)}), bf16[8,64,3584]{2,1,0:T(8,128)(2,1)}, u32[]{:S(2)}, u32[]{:S(2)}) async-start(bf16[8,64,3584]{2,1,0:T(8,128)(2,1)} %bitcast.25), calls=%async_computation.1 | async-start | bytes 7340032 | tf_op jit(solution)/shard_map/all_to_all | solution.py:42
  247.5 0.0 copy-done.2
  247.6 1.0 gather_fusion.1
  248.6 81.8 %all-to-all-done.1 = bf16[8,64,3584]{2,1,0:T(8,128)(2,1)} async-done(((bf16[8,64,3584]{2,1,0:T(8,128)(2,1)}), bf16[8,64,3584]{2,1,0:T(8,128)(2,1)}, u32[]{:S(2)}, u32[]{:S(2)}) %all-to-all-start.1) | async-done | bytes 3670048 | tf_op jit(solution)/shard_map/all_to_all | solution.py:42
  330.4 3.8 %convolution_convert_fusion.1 = bf16[128,3584]{1,0:T(8,128)(2,1)} fusion(bf16[512,3584]{1,0:T(8,128)(2,1)} %bitcast.8, f32[512,128]{1,0:T(8,128)S(1)} %gather_fusion.1, pred[128,512]{0,1:T(32,128)(4,1)S(1)} %bitcast_compare_fusion, pred[512]{0:T(512)(128)(4,1)S(1)} %compare_and_fusion), kind=kOutput, calls=%fused_computation.8 | convolution fusion | flops 470548480 | bytes 4915712 | tf_op jit(solution)/shard_map/dot_general | solution.py:48
  (8 shorter events, 0.1 us)
Async XLA Ops:
  6.5 3.1 copy-start
  6.5 1.5 copy-start.1
  6.5 145.4 %all-gather.3.cloned.1.call-start = ((), (), s32[]{:S(2)}) async-start(), calls=%async_computation.2 | async-start | bytes 18350080 | tf_op jit(solution)/shard_map/all_gather | solution.py:33
  7.3 225.4 %all-gather.5.cloned.1.call-start = ((), (), s32[]{:S(2)}) async-start(), calls=%async_computation.3 | async-start | bytes 9175040 | tf_op jit(solution)/shard_map/all_gather | solution.py:39
  242.8 4.7 %copy-start.2 = (bf16[128,8]{0,1:T(8,128)(2,1)S(1)}, bf16[128,8]{0,1:T(8,128)(2,1)}, u32[]{:S(2)}) copy-start(bf16[128,8]{0,1:T(8,128)(2,1)} %param.9) | copy-start | bytes 6148
  242.8 87.6 %all-to-all-start.1 = ((bf16[8,64,3584]{2,1,0:T(8,128)(2,1)}), bf16[8,64,3584]{2,1,0:T(8,128)(2,1)}, u32[]{:S(2)}, u32[]{:S(2)}) async-start(bf16[8,64,3584]{2,1,0:T(8,128)(2,1)} %bitcast.25), calls=%async_computation.1 | async-start | bytes 7340032 | tf_op jit(solution)/shard_map/all_to_all | solution.py:42
Sparse Core Ops, SparseCore 0:
  9.2 142.6 all-gather.2
  153.7 78.8 all-gather.4
where the time goes:
time: 341 us
  waiting for transfers between devices  203 us (60%)
  blocking collectives  89 us (26%)
  matrix products  28.5 us (8%)
  between operations  13.5 us (4%)
  starting transfers between devices  4.77 us (1%)
    all_to_all x1, blocking collectives, local(): lax.all_to_all(outgoing.reshape(owners, slots, width), 'expert', split_ax...  89 us
    all_to_all x1, waiting for transfers between devices, local(): lax.all_to_all(result.reshape(owners, slots, width), 'expert', split_axis...  81.8 us
    all_gather x1, waiting for transfers between devices, local(): lax.all_gather(down_proj, 'dp', axis=2, tiled=True)[0]  67.3 us
    all_gather x1, waiting for transfers between devices, local(): lax.all_gather(gate_up, 'dp', axis=1, tiled=True)[0]  52.1 us
    dot_general x1, matrix products, local(): jnp.dot(rows, lax.all_gather(gate_up, 'dp', axis=1, tiled=True)[0], prefe...  13.5 us
    dot_general x1, matrix products, local(): jnp.dot(hidden, lax.all_gather(down_proj, 'dp', axis=2, tiled=True)[0], p...  10.1 us
  transfers between devices with their start and end apart: 3, of which 3 were waited for; matrix products, arithmetic and copies ran while one was open for 5% of the time, Pallas kernels for 0%

commit v1 on v0

v1 whole, which is shorter than its diff:
```python
import jax
import jax.numpy as jnp
from jax import lax
from jax.sharding import PartitionSpec as P

BF = jnp.bfloat16
F32 = jnp.float32


def gathered(tokens, gate_up, down_proj, expert_ids, gate_weights):
    owners = lax.axis_size("expert")
    tok_rows = tokens.shape[0]
    width = tokens.shape[1]
    hidden_units = down_proj.shape[1]
    slots = 4 * tok_rows // owners
    total_rows = owners * slots
    owner_ids = jnp.arange(owners, dtype=jnp.int32)
    matches = expert_ids[:, :, None] == owner_ids[None, None, :]
    hits = jnp.sum(matches.astype(jnp.int32), axis=1)
    pick_weight = jnp.sum(
        jnp.where(matches, gate_weights[:, :, None].astype(F32), 0.0), axis=1
    )
    before = jnp.cumsum(hits, axis=0) - hits
    target = jnp.where(hits > 0, owner_ids[None, :] * slots + before, -1)
    slot_owner = jnp.arange(total_rows, dtype=jnp.int32) // slots
    slot_ids = jnp.arange(total_rows, dtype=jnp.int32)
    placed = jnp.take(target, slot_owner, axis=1) == slot_ids[None, :]
    place_bf = placed.astype(BF)
    outgoing = jnp.dot(place_bf.T, tokens, preferred_element_type=F32).astype(BF)
    arrived = lax.all_to_all(
        outgoing.reshape(owners, slots, width), "expert", split_axis=0, concat_axis=0, tiled=True
    )
    rows = arrived.reshape(total_rows, width)
    gu = jnp.dot(
        rows,
        lax.all_gather(gate_up, "dp", axis=1, tiled=True)[0],
        preferred_element_type=F32,
    )
    hidden = (jax.nn.silu(gu[:, :hidden_units]) * gu[:, hidden_units:]).astype(BF)
    result = jnp.dot(
        hidden,
        lax.all_gather(down_proj, "dp", axis=2, tiled=True)[0],
        preferred_element_type=F32,
    ).astype(BF)
    returned = lax.all_to_all(
        result.reshape(owners, slots, width), "expert", split_axis=0, concat_axis=0, tiled=True
    )
    weighted = (place_bf.astype(F32) * jnp.take(pick_weight, slot_owner, axis=1)).astype(BF)
    mixed = jnp.dot(weighted, returned.reshape(total_rows, width), preferred_element_type=F32)
    return mixed.astype(BF)


def swap(value, axis, bit):
    return lax.ppermute(value, axis, [(i, i ^ bit) for i in range(lax.axis_size(axis))])


def paired(tokens, gate_up, down_proj, expert_ids, gate_weights):
    owners = lax.axis_size("expert")
    chips = owners // 2
    tok = tokens.shape[0]
    quarter = gate_up.shape[1]
    ff = down_proj.shape[1]
    slots = 4 * tok // owners
    d = lax.axis_index("dp")
    e = lax.axis_index("expert")
    z, core = e // 2, e % 2
    gate, down = gate_up[0], down_proj[0]

    gate_x = swap(gate, "dp", 1)
    parts = [
        lax.dynamic_slice_in_dim(tokens, (d ^ r) * quarter, quarter, axis=1) for r in range(4)
    ]
    theirs = swap(jnp.concatenate(parts[2:], axis=1), "dp", 2)
    both = jnp.stack([jnp.concatenate(parts[:2], axis=1), theirs])
    down_y = swap(down, "dp", 2)

    meta = lax.all_gather(
        jnp.concatenate([expert_ids.astype(BF), gate_weights], axis=1), ("dp", "expert")
    ).reshape(4, chips, 2, tok, -1)
    meta = lax.dynamic_index_in_dim(meta, core, 2, keepdims=False)
    meta = jnp.stack(
        [lax.dynamic_index_in_dim(meta, d ^ r, 0, keepdims=False) for r in range(3)]
    )
    top = expert_ids.shape[1]
    ids = meta[..., :top].astype(jnp.int32)
    chosen = jnp.stack([e, e ^ 1]).astype(jnp.int32)
    matches = ids[..., None] == chosen
    hits = jnp.any(matches, axis=3)
    weight = jnp.sum(jnp.where(matches, meta[..., top:, None].astype(F32), 0.0), axis=3)
    hits = hits.transpose(0, 1, 3, 2)
    weight = weight.transpose(0, 1, 3, 2)
    earlier = jnp.triu(jnp.ones((tok, tok), BF), 1)
    rank = jnp.dot(hits.astype(BF), earlier, preferred_element_type=F32)
    rank = jnp.where(hits, rank, -1.0)
    placed = rank[..., None, :] == jnp.arange(slots, dtype=F32)[:, None]
    place = placed.astype(BF)
    pay = (place * weight[..., None, :].astype(BF))[:2].reshape(2, chips, 2 * slots, tok)

    line = [list(range(c, owners, 2)) for c in range(2)]
    seen = lax.all_gather(both, "expert", axis_index_groups=line)
    sel = place[::2]

    def choose(expert):
        return jnp.einsum(
            "gzst,zgtk->gzsk", sel[:, :, expert], seen, preferred_element_type=F32
        ).astype(BF)

    other = swap(choose(1), "expert", 1)
    rows = jnp.stack([choose(0), other], axis=2).reshape(2 * owners * slots, 2 * quarter)

    part = jnp.dot(rows[:, :quarter], gate, preferred_element_type=F32) + jnp.dot(
        rows[:, quarter:], gate_x, preferred_element_type=F32
    )
    half = owners * slots
    gu = part[:half] + swap(part[half:].astype(BF), "dp", 2).astype(F32)
    hidden = (jax.nn.silu(gu[:, :ff]) * gu[:, ff:]).astype(BF)
    hiddens = [hidden, swap(hidden, "dp", 1)]

    mine = []
    for g in range(2):
        out = jnp.concatenate(
            [jnp.dot(hiddens[g], w, preferred_element_type=F32).astype(BF) for w in (down, down_y)],
            axis=1,
        ).reshape(chips, 2, slots, 2 * quarter)
        back = swap(out[:, 1], "expert", 1)
        out = jnp.concatenate([out[:, 0], back], axis=1)

        def term(chip):
            chip = jnp.clip(chip, 0, chips - 1)
            return lax.dot_general(
                lax.dynamic_index_in_dim(pay[g], chip, 0, keepdims=False),
                lax.dynamic_index_in_dim(out, chip, 0, keepdims=False),
                (((0,), (0,)), ((), ())),
                preferred_element_type=F32,
            )

        up = down_line = 0.0
        for k in range(1, chips):
            up = lax.ppermute(
                (term(z + chips - k) + up).astype(BF),
                "expert",
                [(2 * i + c, 2 * i + 2 + c) for i in range(k) for c in range(2)],
            ).astype(F32)
            down_line = lax.ppermute(
                (term(z - chips + k) + down_line).astype(BF),
                "expert",
                [
                    (2 * i + c, 2 * i - 2 + c)
                    for i in range(chips - k, chips)
                    for c in range(2)
                ],
            ).astype(F32)
        mine.append((term(z) + up + down_line).astype(BF))

    far = swap(mine[1], "dp", 1)
    mixed = jnp.zeros(tokens.shape, BF)
    for r, piece in enumerate(
        [mine[0][:, :quarter], far[:, :quarter], mine[0][:, quarter:], far[:, quarter:]]
    ):
        mixed = lax.dynamic_update_slice_in_dim(mixed, piece, (d ^ r) * quarter, axis=1)
    return mixed


def solution(mesh):
    placed = (
        P(("dp", "expert"), None),
        P("expert", "dp", None),
        P("expert", None, "dp"),
        P(("dp", "expert"), None),
        P(("dp", "expert"), None),
    )
    short = mesh.shape["expert"] <= 8 and mesh.shape["dp"] == 4
    return jax.shard_map(
        paired if short else gathered,
        mesh=mesh,
        in_specs=placed,
        out_specs=P(("dp", "expert"), None),
        check_vma=False,
    )
```

time: 341 us -> 298 us (0.87)
  waiting for transfers between devices: 203 us -> 153 us
  blocking collectives: 89 us -> 42.8 us
  starting transfers between devices: 4.77 us -> 39.1 us
  matrix products: 28.5 us -> 36.4 us
  local copies, waits for them, and re-layouts: 2.23 us -> 8.1 us
  other arithmetic: 0.45 us -> 3.96 us
    ppermute x0 -> x21, waiting for transfers between devices: none -> 124 us  [the longest x9 94.4 us: swap(): lax.ppermute(value, axis, [(i, i ^ bit) for i in range(lax.axis_size(axis...]
    all_gather x2 -> x1, waiting for transfers between devices: 119 us -> 29.4 us  [paired(): seen = lax.all_gather(both, 'expert', axis_index_groups=line)]
    all_to_all x1 -> x0, blocking collectives: 89 us -> none  [local(): lax.all_to_all(outgoing.reshape(owners, slots, width), 'expert', split_ax...]
    all_to_all x1 -> x0, waiting for transfers between devices: 81.8 us -> none  [local(): lax.all_to_all(result.reshape(owners, slots, width), 'expert', split_axis...]
    all_gather x0 -> x1, blocking collectives: none -> 42.8 us  [paired(): lax.all_gather(jnp.concatenate([expert_ids.astype(BF), gate_weights], axi...]
    ppermute x0 -> x21, starting transfers between devices: none -> 39.1 us  [the longest x6 22.7 us: paired(): lax.ppermute((term(z + chips - k) + up).astype(BF), 'expert', [(2 * i + c...]
    dot_general x4 -> x23, matrix products: 28.5 us -> 36.4 us  [the longest x14 16.7 us: term(): lax.dot_general(lax.dynamic_index_in_dim(pay[g], chip, 0, keepdims=False)...]
    all_to_all x1 -> x0, starting transfers between devices: 4.73 us -> none  [local(): lax.all_to_all(result.reshape(owners, slots, width), 'expert', split_axis...]
  transfers between devices with their start and end apart: 3 -> 22, of which waited for: 3 -> 11; matrix products, arithmetic and copies ran while one was open for 5% -> 12% of each run, Pallas kernels for 0% -> 0%
where the time goes in v1:
time: 298 us
  waiting for transfers between devices  153 us (51%)
  blocking collectives  42.8 us (14%)
  starting transfers between devices  39.1 us (13%)
  matrix products  36.4 us (12%)
  between operations  13.9 us (5%)
  local copies, waits for them, and re-layouts  8.1 us (3%)
  other arithmetic  3.96 us (1%)
    ppermute x9, waiting for transfers between devices, swap(): lax.ppermute(value, axis, [(i, i ^ bit) for i in range(lax.axis_size(axis...  94.4 us
    all_gather x1, blocking collectives, paired(): lax.all_gather(jnp.concatenate([expert_ids.astype(BF), gate_weights], axi...  42.8 us
    all_gather x1, waiting for transfers between devices, paired(): seen = lax.all_gather(both, 'expert', axis_index_groups=line)  29.4 us
    ppermute x6, starting transfers between devices, paired(): lax.ppermute((term(z + chips - k) + up).astype(BF), 'expert', [(2 * i + c...  22.7 us
    ppermute x6, waiting for transfers between devices, paired(): lax.ppermute((term(z + chips - k) + up).astype(BF), 'expert', [(2 * i + c...  19 us
    dot_general x14, matrix products, term(): lax.dot_general(lax.dynamic_index_in_dim(pay[g], chip, 0, keepdims=False)...  16.7 us
    ppermute x9, starting transfers between devices, swap(): lax.ppermute(value, axis, [(i, i ^ bit) for i in range(lax.axis_size(axis...  11 us
    ppermute x6, waiting for transfers between devices, paired(): lax.ppermute((term(z - chips + k) + down_line).astype(BF), 'expert', [(2...  10.4 us
  transfers between devices with their start and end apart: 22, of which 11 were waited for; matrix products, arithmetic and copies ran while one was open for 12% of the time, Pallas kernels for 0%

profile of v1, /device:TPU:0, one launch (start us, length us, event | category | flops | bytes accessed | tf_op | source)
XLA Modules:
  0.0 297.5 jit_solution(12790171783303168157)
XLA Ops:
  6.5 1.4 constant_dynamic-slice_fusion.3
  7.9 3.0 %collective-permute-start = (bf16[128,1792]{1,0:T(8,128)(2,1)S(1)}, bf16[128,1792]{1,0:T(8,128)(2,1)S(1)}, u32[]{:S(2)}, u32[]{:S(2)}) collective-permute-start(bf16[128,1792]{1,0:T(8,128)(2,1)S(1)} %pad_maximum_fusion.4), channel_id=1, source_target_pairs={{0,16},{8,24},{16,0},{24,8},{1,17},{9,25},{17,1},{25,9},{2,18},{10... | collective-permute-start | bytes 1376264 | tf_op jit(solution)/shard_map/ppermute | solution.py:54
  11.0 10.5 %collective-permute-done = bf16[128,1792]{1,0:T(8,128)(2,1)S(1)} collective-permute-done((bf16[128,1792]{1,0:T(8,128)(2,1)S(1)}, bf16[128,1792]{1,0:T(8,128)(2,1)S(1)}, u32[]{:S(2)}, u32[]{:S(2)}) %collective-permute-start) | collective-permute-done | bytes 458784 | tf_op jit(solution)/shard_map/ppermute | solution.py:54
  21.5 1.0 pad_maximum_fusion.3
  22.5 1.8 collective-permute-start.2
  24.3 42.8 %all-gather = bf16[4096,16]{0,1:T(8,128)(2,1)S(1)} all-gather(bf16[128,16]{0,1:T(8,128)(2,1)S(1)} %pad_maximum_fusion.6), channel_id=2, replica_groups=mesh['dp'=4,'expert'=8] {'dp','expert'}, dimensions={0}, use_global_device_ids=true | all-gather | bytes 135168 | tf_op jit(solution)/shard_map/all_gather | solution.py:77
  67.8 29.4 %all-gather.4.cloned.1.call-done = bf16[8,128,1792]{2,1,0:T(8,128)(2,1)} async-done(((bf16[2,128,1792]{2,1,0:T(8,128)(2,1)}), bf16[8,128,1792]{2,1,0:T(8,128)(2,1)}) %all-gather.4.cloned.1.call-update) | async-done | bytes 3670032 | tf_op jit(solution)/shard_map/all_gather | solution.py:100
  97.2 2.8 fusion.7
  100.4 0.6 fusion.10
  101.0 2.9 collective-permute-done.1
  103.9 0.3 pad_maximum_fusion
  104.3 0.3 copy.54
  104.6 1.7 copy-done.4
  106.3 4.5 %fusion.27 = f32[1024,2048]{1,0:T(8,128)S(1)} fusion(bf16[1024,1792]{1,0:T(8,128)(2,1)S(1)} %bitcast.155, bf16[1,896,2048]{2,1,0:T(8,128)(2,1)S(1)} %copy-done.4), kind=kOutput, calls=%fused_computation.68 | convolution fusion | flops 3758096384 | bytes 13893632 | tf_op jit(solution)/shard_map/dot_general | solution.py:111
  110.8 6.6 %convolution_add_fusion = f32[1024,2048]{1,0:T(8,128)S(1)} fusion(f32[1024,2048]{1,0:T(8,128)S(1)} %fusion.27, bf16[896,2048]{1,0:T(8,128)(2,1)} %collective-permute-done.2, bf16[1024,1792]{1,0:T(8,128)(2,1)S(1)} %bitcast.156), kind=kOutput, calls=%fused_computation.2 | convolution fusion | flops 3760193536 | bytes 22282240 | tf_op jit(solution)/shard_map/dot_general | solution.py:111
  117.7 1.5 collective-permute-start.3
  119.3 1.1 collective-permute-start.4
  120.4 45.9 %collective-permute-done.3 = bf16[512,2048]{1,0:T(8,128)(2,1)S(1)} collective-permute-done((bf16[512,2048]{1,0:T(8,128)(2,1)S(1)}, bf16[512,2048]{1,0:T(8,128)(2,1)S(1)}, u32[]{:S(2)}, u32[]{:S(2)}) %collective-permute-start.3) | collective-permute-done | bytes 2097184 | tf_op jit(solution)/shard_map/ppermute | solution.py:54
  166.3 0.9 slice_add_fusion
  167.2 0.6 fusion.25
  167.8 1.5 collective-permute-start.12
  169.3 1.3 convolution_convert_fusion.7
  170.6 34.2 %collective-permute-done.4 = bf16[1024,896]{1,0:T(8,128)(2,1)S(1)} collective-permute-done((bf16[1024,896]{1,0:T(8,128)(2,1)S(1)}, bf16[1024,896]{1,0:T(8,128)(2,1)S(1)}, u32[]{:S(2)}, u32[]{:S(2)}) %collective-permute-start.4) | collective-permute-done | bytes 1835040 | tf_op jit(solution)/shard_map/ppermute | solution.py:54
  204.8 1.3 convolution_convert_fusion.6
  206.4 1.1 slice_bitcast_fusion.2
  207.4 1.3 convolution_convert_fusion.4
  208.7 1.3 convolution_convert_fusion.5
  210.1 1.1 slice_bitcast_fusion
  211.2 0.5 collective-permute-start.13
  212.0 1.1 convolution_convert_fusion.3
  213.1 2.1 collective-permute-start.6
  215.2 1.3 convolution_convert_fusion.1
  216.5 1.3 collective-permute-start.14
  217.8 0.3 convolution_convert_fusion.2
  218.1 0.7 collective-permute-start.9
  218.8 1.3 convolution_convert_fusion
  220.1 0.7 collective-permute-start.17
  220.8 4.7 %collective-permute-done.6 = bf16[128,1792]{1,0:T(8,128)(2,1)} collective-permute-done((bf16[128,1792]{1,0:T(8,128)(2,1)}, bf16[128,1792]{1,0:T(8,128)(2,1)}, u32[]{:S(2)}, u32[]{:S(2)}) %collective-permute-start.6) | collective-permute-done | bytes 458784 | tf_op jit(solution)/shard_map/ppermute | solution.py:139
  225.5 1.3 fusion.17
  226.9 4.4 %collective-permute-start.7 = (bf16[128,1792]{1,0:T(8,128)(2,1)S(1)}, bf16[128,1792]{1,0:T(8,128)(2,1)S(1)}, u32[]{:S(2)}, u32[]{:S(2)}) collective-permute-start(bf16[128,1792]{1,0:T(8,128)(2,1)S(1)} %fusion.17), channel_id=1, source_target_pairs={{0,2},{1,3},{2,4},{3,5},{8,10},{9,11},{10,12},{11,13},{16,18},{17,... | collective-permute-start | bytes 1376264 | tf_op jit(solution)/shard_map/ppermute | solution.py:139
  231.3 4.0 %collective-permute-done.14 = bf16[128,1792]{1,0:T(8,128)(2,1)S(1)} collective-permute-done((bf16[128,1792]{1,0:T(8,128)(2,1)S(1)}, bf16[128,1792]{1,0:T(8,128)(2,1)S(1)}, u32[]{:S(2)}, u32[]{:S(2)}) %collective-permute-start.14) | collective-permute-done | bytes 458784 | tf_op jit(solution)/shard_map/ppermute | solution.py:139
  235.3 1.3 fusion.22
  236.5 4.4 %collective-permute-start.15 = (bf16[128,1792]{1,0:T(8,128)(2,1)S(1)}, bf16[128,1792]{1,0:T(8,128)(2,1)S(1)}, u32[]{:S(2)}, u32[]{:S(2)}) collective-permute-start(bf16[128,1792]{1,0:T(8,128)(2,1)S(1)} %fusion.22), channel_id=1, source_target_pairs={{0,2},{1,3},{2,4},{3,5},{8,10},{9,11},{10,12},{11,13},{16,18},{17,... | collective-permute-start | bytes 1376264 | tf_op jit(solution)/shard_map/ppermute | solution.py:139
  241.0 1.3 fusion.24
  242.2 0.7 collective-permute-start.18
  242.9 0.3 fusion.19
  243.3 0.7 collective-permute-start.10
  244.0 10.3 %collective-permute-done.15 = bf16[128,1792]{1,0:T(8,128)(2,1)S(1)} collective-permute-done((bf16[128,1792]{1,0:T(8,128)(2,1)S(1)}, bf16[128,1792]{1,0:T(8,128)(2,1)S(1)}, u32[]{:S(2)}, u32[]{:S(2)}) %collective-permute-start.15) | collective-permute-done | bytes 458784 | tf_op jit(solution)/shard_map/ppermute | solution.py:139
  254.3 1.3 fusion.21
  255.6 5.2 %collective-permute-start.16 = (bf16[128,1792]{1,0:T(8,128)(2,1)S(1)}, bf16[128,1792]{1,0:T(8,128)(2,1)}, u32[]{:S(2)}, u32[]{:S(2)}) collective-permute-start(bf16[128,1792]{1,0:T(8,128)(2,1)S(1)} %fusion.21), channel_id=1, source_target_pairs={{0,2},{1,3},{2,4},{3,5},{4,6},{5,7},{8,10},{9,11},{10,12},{11,13},... | collective-permute-start | bytes 1376264 | tf_op jit(solution)/shard_map/ppermute | solution.py:139
  260.7 2.0 fusion.23
  262.8 1.3 collective-permute-start.19
  264.1 1.1 fusion.16
  265.2 5.3 %collective-permute-start.8 = (bf16[128,1792]{1,0:T(8,128)(2,1)}, bf16[128,1792]{1,0:T(8,128)(2,1)}, u32[]{:S(2)}, u32[]{:S(2)}) collective-permute-start(bf16[128,1792]{1,0:T(8,128)(2,1)} %fusion.16), channel_id=1, source_target_pairs={{0,2},{1,3},{2,4},{3,5},{4,6},{5,7},{8,10},{9,11},{10,12},{11,13},... | collective-permute-start | bytes 1376264 | tf_op jit(solution)/shard_map/ppermute | solution.py:139
  270.5 1.1 fusion.18
  271.6 1.3 collective-permute-start.11
  272.9 5.2 %collective-permute-done.19 = bf16[128,1792]{1,0:T(8,128)(2,1)} collective-permute-done((bf16[128,1792]{1,0:T(8,128)(2,1)}, bf16[128,1792]{1,0:T(8,128)(2,1)}, u32[]{:S(2)}, u32[]{:S(2)}) %collective-permute-start.19) | collective-permute-done | bytes 458784 | tf_op jit(solution)/shard_map/ppermute | solution.py:144
  278.1 1.6 fusion.20
  279.7 1.5 collective-permute-start.20
  281.2 5.2 %collective-permute-done.11 = bf16[128,1792]{1,0:T(8,128)(2,1)} collective-permute-done((bf16[128,1792]{1,0:T(8,128)(2,1)}, bf16[128,1792]{1,0:T(8,128)(2,1)}, u32[]{:S(2)}, u32[]{:S(2)}) %collective-permute-start.11) | collective-permute-done | bytes 458784 | tf_op jit(solution)/shard_map/ppermute | solution.py:144
  286.4 1.5 fusion.15
  288.0 0.9 collective-permute-done.20
  289.0 0.9 copy-done.1
  290.0 0.7 slice_dynamic-update-slice_fusion
  (53 shorter events, 2.3 us)
Async XLA Ops:
  6.5 90.7 %all-gather.4.cloned.1.call-start = ((), (), s32[]{:S(2)}) async-start(), calls=%async_computation | async-start | bytes 4587520 | tf_op jit(solution)/shard_map/all_gather | solution.py:100
  7.9 13.6 %collective-permute-start = (bf16[128,1792]{1,0:T(8,128)(2,1)S(1)}, bf16[128,1792]{1,0:T(8,128)(2,1)S(1)}, u32[]{:S(2)}, u32[]{:S(2)}) collective-permute-start(bf16[128,1792]{1,0:T(8,128)(2,1)S(1)} %pad_maximum_fusion.4), channel_id=1, source_target_pairs={{0,16},{8,24},{16,0},{24,8},{1,17},{9,25},{17,1},{25,9},{2,18},{10... | collective-permute-start | bytes 1376264 | tf_op jit(solution)/shard_map/ppermute | solution.py:54
  11.0 13.3 %copy-start.2 = (s32[128,8]{0,1:T(8,128)S(1)}, s32[128,8]{0,1:T(8,128)}, u32[]{:S(2)}) copy-start(s32[128,8]{0,1:T(8,128)} %param.8) | copy-start | bytes 12292
  11.0 13.3 %copy-start.3 = (bf16[128,8]{0,1:T(8,128)(2,1)S(1)}, bf16[128,8]{0,1:T(8,128)(2,1)}, u32[]{:S(2)}) copy-start(bf16[128,8]{0,1:T(8,128)(2,1)} %param.9) | copy-start | bytes 6148
  22.5 88.3 %collective-permute-start.2 = (bf16[896,2048]{1,0:T(8,128)(2,1)}, bf16[896,2048]{1,0:T(8,128)(2,1)}, u32[]{:S(2)}, u32[]{:S(2)}) collective-permute-start(bf16[896,2048]{1,0:T(8,128)(2,1)} %bitcast.175), channel_id=1, source_target_pairs={{0,8},{8,0},{16,24},{24,16},{1,9},{9,1},{17,25},{25,17},{2,10},{10... | collective-permute-start | bytes 11010056 | tf_op jit(solution)/shard_map/ppermute | solution.py:54
  97.2 3.1 %copy-start = (bf16[8,128,1792]{2,1,0:T(8,128)(2,1)S(1)}, bf16[8,128,1792]{2,1,0:T(8,128)(2,1)}, u32[]{:S(2)}) copy-start(bf16[8,128,1792]{2,1,0:T(8,128)(2,1)} %all-gather.4.cloned.1.call-done) | copy-start | bytes 11010052
  100.1 3.9 %collective-permute-start.1 = (bf16[2,4,64,1792]{3,2,1,0:T(8,128)(2,1)S(1)}, bf16[2,4,64,1792]{3,2,1,0:T(8,128)(2,1)S(1)}, u32[]{:S(2)}, u32[]{:S(2)}) collective-permute-start(bf16[2,4,64,1792]{3,2,1,0:T(8,128)(2,1)S(1)} %fusion.7), channel_id=1, source_target_pairs={{0,1},{1,0},{2,3},{3,2},{4,5},{5,4},{6,7},{7,6},{8,9},{9,8},{10,11... | collective-permute-start | bytes 5505032 | tf_op jit(solution)/shard_map/ppermute | solution.py:54
  104.2 2.0 copy-start.4
  117.4 1.9 copy-start.5
  117.7 48.5 %collective-permute-start.3 = (bf16[512,2048]{1,0:T(8,128)(2,1)S(1)}, bf16[512,2048]{1,0:T(8,128)(2,1)S(1)}, u32[]{:S(2)}, u32[]{:S(2)}) collective-permute-start(bf16[512,2048]{1,0:T(8,128)(2,1)S(1)} %slice.146), channel_id=1, source_target_pairs={{0,16},{8,24},{16,0},{24,8},{1,17},{9,25},{17,1},{25,9},{2,18},{10... | collective-permute-start | bytes 6291464 | tf_op jit(solution)/shard_map/ppermute | solution.py:54
  119.3 85.5 %collective-permute-start.4 = (bf16[1024,896]{1,0:T(8,128)(2,1)S(1)}, bf16[1024,896]{1,0:T(8,128)(2,1)S(1)}, u32[]{:S(2)}, u32[]{:S(2)}) collective-permute-start(bf16[1024,896]{1,0:T(8,128)(2,1)S(1)} %bitcast.176), channel_id=1, source_target_pairs={{0,16},{8,24},{16,0},{24,8},{1,17},{9,25},{17,1},{25,9},{2,18},{10... | collective-permute-start | bytes 5505032 | tf_op jit(solution)/shard_map/ppermute | solution.py:54
  167.8 39.6 %collective-permute-start.12 = (bf16[512,1024]{1,0:T(8,128)(2,1)S(1)}, bf16[512,1024]{1,0:T(8,128)(2,1)S(1)}, u32[]{:S(2)}, u32[]{:S(2)}) collective-permute-start(bf16[512,1024]{1,0:T(8,128)(2,1)S(1)} %fusion.25), channel_id=1, source_target_pairs={{0,8},{8,0},{16,24},{24,16},{1,9},{9,1},{17,25},{25,17},{2,10},{10... | collective-permute-start | bytes 3145736 | tf_op jit(solution)/shard_map/ppermute | solution.py:54
  207.4 4.5 %collective-permute-start.5 = (bf16[4,64,1792]{2,1,0:T(8,128)(2,1)}, bf16[4,64,1792]{2,1,0:T(8,128)(2,1)S(1)}, u32[]{:S(2)}, u32[]{:S(2)}) collective-permute-start(bf16[4,64,1792]{2,1,0:T(8,128)(2,1)} %get-tuple-element.7), channel_id=1, source_target_pairs={{0,1},{1,0},{2,3},{3,2},{4,5},{5,4},{6,7},{7,6},{8,9},{9,8},{10,11... | collective-permute-start | bytes 2752520 | tf_op jit(solution)/shard_map/ppermute | solution.py:54
  211.2 4.0 %collective-permute-start.13 = (bf16[4,64,1792]{2,1,0:T(8,128)(2,1)}, bf16[4,64,1792]{2,1,0:T(8,128)(2,1)}, u32[]{:S(2)}, u32[]{:S(2)}) collective-permute-start(bf16[4,64,1792]{2,1,0:T(8,128)(2,1)} %get-tuple-element.5), channel_id=1, source_target_pairs={{0,1},{1,0},{2,3},{3,2},{4,5},{5,4},{6,7},{7,6},{8,9},{9,8},{10,11... | collective-permute-start | bytes 2752520 | tf_op jit(solution)/shard_map/ppermute | solution.py:54
  213.1 12.5 %collective-permute-start.6 = (bf16[128,1792]{1,0:T(8,128)(2,1)}, bf16[128,1792]{1,0:T(8,128)(2,1)}, u32[]{:S(2)}, u32[]{:S(2)}) collective-permute-start(bf16[128,1792]{1,0:T(8,128)(2,1)} %convolution_convert_fusion.3), channel_id=1, source_target_pairs={{0,2},{1,3},{8,10},{9,11},{16,18},{17,19},{24,26},{25,27}} | collective-permute-start | bytes 1376264 | tf_op jit(solution)/shard_map/ppermute | solution.py:139
  216.5 18.8 %collective-permute-start.14 = (bf16[128,1792]{1,0:T(8,128)(2,1)S(1)}, bf16[128,1792]{1,0:T(8,128)(2,1)S(1)}, u32[]{:S(2)}, u32[]{:S(2)}) collective-permute-start(bf16[128,1792]{1,0:T(8,128)(2,1)S(1)} %convolution_convert_fusion.1), channel_id=1, source_target_pairs={{0,2},{1,3},{8,10},{9,11},{16,18},{17,19},{24,26},{25,27}} | collective-permute-start | bytes 1376264 | tf_op jit(solution)/shard_map/ppermute | solution.py:139
  218.1 24.8 %collective-permute-start.9 = (bf16[128,1792]{1,0:T(8,128)(2,1)S(1)}, bf16[128,1792]{1,0:T(8,128)(2,1)S(1)}, u32[]{:S(2)}, u32[]{:S(2)}) collective-permute-start(bf16[128,1792]{1,0:T(8,128)(2,1)S(1)} %convolution_convert_fusion.2), channel_id=1, source_target_pairs={{6,4},{7,5},{14,12},{15,13},{22,20},{23,21},{30,28},{31,29}} | collective-permute-start | bytes 1376264 | tf_op jit(solution)/shard_map/ppermute | solution.py:144
  220.1 20.9 %collective-permute-start.17 = (bf16[128,1792]{1,0:T(8,128)(2,1)S(1)}, bf16[128,1792]{1,0:T(8,128)(2,1)S(1)}, u32[]{:S(2)}, u32[]{:S(2)}) collective-permute-start(bf16[128,1792]{1,0:T(8,128)(2,1)S(1)} %convolution_convert_fusion), channel_id=1, source_target_pairs={{6,4},{7,5},{14,12},{15,13},{22,20},{23,21},{30,28},{31,29}} | collective-permute-start | bytes 1376264 | tf_op jit(solution)/shard_map/ppermute | solution.py:144
  226.9 37.2 %collective-permute-start.7 = (bf16[128,1792]{1,0:T(8,128)(2,1)S(1)}, bf16[128,1792]{1,0:T(8,128)(2,1)S(1)}, u32[]{:S(2)}, u32[]{:S(2)}) collective-permute-start(bf16[128,1792]{1,0:T(8,128)(2,1)S(1)} %fusion.17), channel_id=1, source_target_pairs={{0,2},{1,3},{2,4},{3,5},{8,10},{9,11},{10,12},{11,13},{16,18},{17,... | collective-permute-start | bytes 1376264 | tf_op jit(solution)/shard_map/ppermute | solution.py:139
  236.5 17.8 %collective-permute-start.15 = (bf16[128,1792]{1,0:T(8,128)(2,1)S(1)}, bf16[128,1792]{1,0:T(8,128)(2,1)S(1)}, u32[]{:S(2)}, u32[]{:S(2)}) collective-permute-start(bf16[128,1792]{1,0:T(8,128)(2,1)S(1)} %fusion.22), channel_id=1, source_target_pairs={{0,2},{1,3},{2,4},{3,5},{8,10},{9,11},{10,12},{11,13},{16,18},{17,... | collective-permute-start | bytes 1376264 | tf_op jit(solution)/shard_map/ppermute | solution.py:139
  242.2 18.5 %collective-permute-start.18 = (bf16[128,1792]{1,0:T(8,128)(2,1)S(1)}, bf16[128,1792]{1,0:T(8,128)(2,1)S(1)}, u32[]{:S(2)}, u32[]{:S(2)}) collective-permute-start(bf16[128,1792]{1,0:T(8,128)(2,1)S(1)} %fusion.24), channel_id=1, source_target_pairs={{4,2},{5,3},{6,4},{7,5},{12,10},{13,11},{14,12},{15,13},{20,18},{2... | collective-permute-start | bytes 1376264 | tf_op jit(solution)/shard_map/ppermute | solution.py:144
  243.3 27.2 %collective-permute-start.10 = (bf16[128,1792]{1,0:T(8,128)(2,1)S(1)}, bf16[128,1792]{1,0:T(8,128)(2,1)S(1)}, u32[]{:S(2)}, u32[]{:S(2)}) collective-permute-start(bf16[128,1792]{1,0:T(8,128)(2,1)S(1)} %fusion.19), channel_id=1, source_target_pairs={{4,2},{5,3},{6,4},{7,5},{12,10},{13,11},{14,12},{15,13},{20,18},{2... | collective-permute-start | bytes 1376264 | tf_op jit(solution)/shard_map/ppermute | solution.py:144
  255.6 17.4 %collective-permute-start.16 = (bf16[128,1792]{1,0:T(8,128)(2,1)S(1)}, bf16[128,1792]{1,0:T(8,128)(2,1)}, u32[]{:S(2)}, u32[]{:S(2)}) collective-permute-start(bf16[128,1792]{1,0:T(8,128)(2,1)S(1)} %fusion.21), channel_id=1, source_target_pairs={{0,2},{1,3},{2,4},{3,5},{4,6},{5,7},{8,10},{9,11},{10,12},{11,13},... | collective-permute-start | bytes 1376264 | tf_op jit(solution)/shard_map/ppermute | solution.py:139
  262.8 15.3 %collective-permute-start.19 = (bf16[128,1792]{1,0:T(8,128)(2,1)}, bf16[128,1792]{1,0:T(8,128)(2,1)}, u32[]{:S(2)}, u32[]{:S(2)}) collective-permute-start(bf16[128,1792]{1,0:T(8,128)(2,1)} %fusion.23), channel_id=1, source_target_pairs={{2,0},{3,1},{4,2},{5,3},{6,4},{7,5},{10,8},{11,9},{12,10},{13,11},... | collective-permute-start | bytes 1376264 | tf_op jit(solution)/shard_map/ppermute | solution.py:144
  265.2 16.0 %collective-permute-start.8 = (bf16[128,1792]{1,0:T(8,128)(2,1)}, bf16[128,1792]{1,0:T(8,128)(2,1)}, u32[]{:S(2)}, u32[]{:S(2)}) collective-permute-start(bf16[128,1792]{1,0:T(8,128)(2,1)} %fusion.16), channel_id=1, source_target_pairs={{0,2},{1,3},{2,4},{3,5},{4,6},{5,7},{8,10},{9,11},{10,12},{11,13},... | collective-permute-start | bytes 1376264 | tf_op jit(solution)/shard_map/ppermute | solution.py:139
  271.6 14.8 %collective-permute-start.11 = (bf16[128,1792]{1,0:T(8,128)(2,1)}, bf16[128,1792]{1,0:T(8,128)(2,1)}, u32[]{:S(2)}, u32[]{:S(2)}) collective-permute-start(bf16[128,1792]{1,0:T(8,128)(2,1)} %fusion.18), channel_id=1, source_target_pairs={{2,0},{3,1},{4,2},{5,3},{6,4},{7,5},{10,8},{11,9},{12,10},{13,11},... | collective-permute-start | bytes 1376264 | tf_op jit(solution)/shard_map/ppermute | solution.py:144
  279.7 9.3 %collective-permute-start.20 = (bf16[128,1792]{1,0:T(8,128)(2,1)S(1)}, bf16[128,1792]{1,0:T(8,128)(2,1)S(1)}, u32[]{:S(2)}, u32[]{:S(2)}) collective-permute-start(bf16[128,1792]{1,0:T(8,128)(2,1)S(1)} %fusion.20), channel_id=1, source_target_pairs={{0,8},{8,0},{16,24},{24,16},{1,9},{9,1},{17,25},{25,17},{2,10},{10... | collective-permute-start | bytes 1376264 | tf_op jit(solution)/shard_map/ppermute | solution.py:54
  289.0 0.9 copy-start.1
Sparse Core Ops, SparseCore 0:
  22.6 74.5 all-gather.3

commit v2 on v1

v2 whole, which is shorter than its diff:
```python
import jax
import jax.numpy as jnp
from jax import lax
from jax.sharding import PartitionSpec as P

BF = jnp.bfloat16
F32 = jnp.float32


def gathered(tokens, gate_up, down_proj, expert_ids, gate_weights):
    owners = lax.axis_size("expert")
    tok_rows = tokens.shape[0]
    width = tokens.shape[1]
    hidden_units = down_proj.shape[1]
    slots = 4 * tok_rows // owners
    total_rows = owners * slots
    owner_ids = jnp.arange(owners, dtype=jnp.int32)
    matches = expert_ids[:, :, None] == owner_ids[None, None, :]
    hits = jnp.sum(matches.astype(jnp.int32), axis=1)
    pick_weight = jnp.sum(
        jnp.where(matches, gate_weights[:, :, None].astype(F32), 0.0), axis=1
    )
    before = jnp.cumsum(hits, axis=0) - hits
    target = jnp.where(hits > 0, owner_ids[None, :] * slots + before, -1)
    slot_owner = jnp.arange(total_rows, dtype=jnp.int32) // slots
    slot_ids = jnp.arange(total_rows, dtype=jnp.int32)
    placed = jnp.take(target, slot_owner, axis=1) == slot_ids[None, :]
    place_bf = placed.astype(BF)
    outgoing = jnp.dot(place_bf.T, tokens, preferred_element_type=F32).astype(BF)
    arrived = lax.all_to_all(
        outgoing.reshape(owners, slots, width), "expert", split_axis=0, concat_axis=0, tiled=True
    )
    rows = arrived.reshape(total_rows, width)
    gu = jnp.dot(
        rows,
        lax.all_gather(gate_up, "dp", axis=1, tiled=True)[0],
        preferred_element_type=F32,
    )
    hidden = (jax.nn.silu(gu[:, :hidden_units]) * gu[:, hidden_units:]).astype(BF)
    result = jnp.dot(
        hidden,
        lax.all_gather(down_proj, "dp", axis=2, tiled=True)[0],
        preferred_element_type=F32,
    ).astype(BF)
    returned = lax.all_to_all(
        result.reshape(owners, slots, width), "expert", split_axis=0, concat_axis=0, tiled=True
    )
    weighted = (place_bf.astype(F32) * jnp.take(pick_weight, slot_owner, axis=1)).astype(BF)
    mixed = jnp.dot(weighted, returned.reshape(total_rows, width), preferred_element_type=F32)
    return mixed.astype(BF)


def swap(value, axis, bit):
    return lax.ppermute(value, axis, [(i, i ^ bit) for i in range(lax.axis_size(axis))])


def order_of(chips):
    def step(chip, to):
        return chips - abs(to - chip) if to != chip else chips

    return [sorted(range(chips), key=lambda to: (step(chip, to), to)) for chip in range(chips)]


def paired(tokens, gate_up, down_proj, expert_ids, gate_weights):
    owners = lax.axis_size("expert")
    chips = owners // 2
    tok = tokens.shape[0]
    top = expert_ids.shape[1]
    quarter = gate_up.shape[1]
    half = 2 * quarter
    ff = down_proj.shape[1]
    slots = 4 * tok // owners
    d = lax.axis_index("dp")
    e = lax.axis_index("expert")
    z = e // 2
    gate, down = gate_up[0], down_proj[0]
    order = jnp.array(order_of(chips), jnp.int32)[z]

    def hop(value, sources, by):
        return lax.ppermute(
            value, "expert", [(2 * i + c, 2 * (i + by) + c) for i in sources for c in range(2)]
        )

    info = jnp.concatenate([expert_ids.astype(BF), gate_weights], axis=1)
    info_x = swap(info, "dp", 1)
    gate_x = swap(gate, "dp", 1)
    parts = [
        lax.dynamic_slice_in_dim(tokens, (d ^ r) * quarter, quarter, axis=1) for r in range(4)
    ]
    first = jnp.concatenate([parts[0], parts[1], info], axis=1)
    second = jnp.concatenate([swap(jnp.concatenate([parts[2], parts[3], info], axis=1), "dp", 2), info_x], axis=1)
    down_y = swap(down, "dp", 2)

    seen = []
    for own in (first, second):
        right = left = own
        rights, lefts = {}, {}
        for k in range(1, chips):
            right = rights[k] = hop(right, range(k - 1, chips - 1), 1)
            left = lefts[k] = hop(left, range(1, chips - k + 1), -1)
        seen.append(
            [own] + [jnp.where(z >= k, rights[k], lefts[chips - k]) for k in range(1, chips)]
        )
    info = jnp.stack(
        [
            jnp.stack([s[:, half : half + 2 * top] for s in seen[0]]),
            jnp.stack([s[:, half + 2 * top :] for s in seen[1]]),
            jnp.stack([s[:, half : half + 2 * top] for s in seen[1]]),
        ]
    )
    seen = jnp.stack([jnp.stack([s[:, :half] for s in seen[g]]) for g in range(2)])
    ids = info[..., :top].astype(jnp.int32)
    chosen = jnp.stack([e, e ^ 1]).astype(jnp.int32)
    matches = ids[..., None] == chosen
    hits = jnp.any(matches, axis=3).transpose(0, 1, 3, 2)
    weight = jnp.sum(jnp.where(matches, info[..., top:, None].astype(F32), 0.0), axis=3)
    weight = weight.transpose(0, 1, 3, 2)
    earlier = jnp.triu(jnp.ones((tok, tok), BF), 1)
    rank = jnp.dot(hits.astype(BF), earlier, preferred_element_type=F32)
    rank = jnp.where(hits, rank, -1.0)
    placed = rank[..., None, :] == jnp.arange(slots, dtype=F32)[:, None]
    place = placed.astype(BF)
    pay = (place * weight[..., None, :].astype(BF))[:2].reshape(2, chips, 2 * slots, tok)

    def choose(expert):
        return jnp.einsum(
            "gzst,gztk->zgsk", place[::2, :, expert], seen, preferred_element_type=F32
        ).astype(BF)

    other = swap(choose(1), "expert", 1)
    rows = jnp.stack([choose(0), other], axis=2)
    rows, down_y = lax.optimization_barrier((rows, down_y))
    chunk = 2 * slots
    near = jnp.dot(
        rows[..., :quarter].reshape(-1, quarter), gate, preferred_element_type=F32
    ).reshape(chips, 2, chunk, 2 * ff)

    def pick(array, q):
        return lax.dynamic_index_in_dim(array, (z - order[q]) % chips, 0, keepdims=False)

    terms = []
    for q in range(chips):
        r = pick(rows, q)[..., quarter:].reshape(2, chunk, quarter)
        n = pick(near, q)
        sent = (jnp.dot(r[1], gate_x, preferred_element_type=F32) + n[1]).astype(BF)
        gu = jnp.dot(r[0], gate_x, preferred_element_type=F32) + n[0]
        gu = gu + swap(sent, "dp", 2).astype(F32)
        hidden = (jax.nn.silu(gu[:, :ff]) * gu[:, ff:]).astype(BF)
        hidden = jnp.concatenate([hidden, swap(hidden, "dp", 1)])
        out = jnp.concatenate(
            [jnp.dot(hidden, w, preferred_element_type=F32).astype(BF) for w in (down, down_y)],
            axis=1,
        ).reshape(2, 2, slots, half)
        back = swap(out[:, 1], "expert", 1)
        out = jnp.concatenate([out[:, 0], back], axis=1)
        paid = lax.dynamic_index_in_dim(pay, (z - order[q]) % chips, 1, keepdims=False)
        terms.append(jnp.einsum("gst,gsk->gtk", paid, out, preferred_element_type=F32))

    def term(step, to):
        total = terms[0]
        for q in range(1, min(step, chips - 1)):
            total = jnp.where(order[q] == to, terms[q], total)
        return total

    right = left = 0.0
    for k in range(1, chips):
        right = hop((term(k, z + chips - k) + right).astype(BF), range(k), 1).astype(F32)
        left = hop((term(k, z - chips + k) + left).astype(BF), range(chips - k, chips), -1).astype(F32)
    mine = (terms[-1] + right + left).astype(BF)

    far = swap(mine[1], "dp", 1)
    mixed = jnp.zeros(tokens.shape, BF)
    for r, piece in enumerate(
        [mine[0, :, :quarter], far[:, :quarter], mine[0, :, quarter:], far[:, quarter:]]
    ):
        mixed = lax.dynamic_update_slice_in_dim(mixed, piece, (d ^ r) * quarter, axis=1)
    return mixed


def solution(mesh):
    placed = (
        P(("dp", "expert"), None),
        P("expert", "dp", None),
        P("expert", None, "dp"),
        P(("dp", "expert"), None),
        P(("dp", "expert"), None),
    )
    short = mesh.shape["expert"] <= 8 and mesh.shape["dp"] == 4
    return jax.shard_map(
        paired if short else gathered,
        mesh=mesh,
        in_specs=placed,
        out_specs=P(("dp", "expert"), None),
        check_vma=False,
    )
```

time: 298 us -> 342 us (1.15)
  waiting for transfers between devices: 153 us -> 200 us
  blocking collectives: 42.8 us -> 0 us
  starting transfers between devices: 39.1 us -> 59.1 us
  matrix products: 36.4 us -> 52.9 us
  between operations: 13.9 us -> 7.07 us
  other arithmetic: 3.96 us -> 9.9 us
  local copies, waits for them, and re-layouts: 8.1 us -> 12 us
    ppermute x12 -> x18, waiting for transfers between devices: 29.4 us -> 85.8 us  [hop(): lax.ppermute(value, 'expert', [(2 * i + c, 2 * (i + by) + c) for i in sou...]
    all_gather x1 -> x0, blocking collectives: 42.8 us -> none  [paired(): lax.all_gather(jnp.concatenate([expert_ids.astype(BF), gate_weights], axi...]
    all_gather x1 -> x0, waiting for transfers between devices: 29.4 us -> none  [paired(): seen = lax.all_gather(both, 'expert', axis_index_groups=line)]
    ppermute x9 -> x18, waiting for transfers between devices: 94.4 us -> 114 us  [swap(): lax.ppermute(value, axis, [(i, i ^ bit) for i in range(lax.axis_size(axis...]
    dot_general x22 -> x23, matrix products: 36.3 us -> 52.8 us  [the longest x8 17.7 us: paired(): jnp.dot(hidden, w, preferred_element_type=F32).astype(BF)]
    ppermute x12 -> x18, starting transfers between devices: 28 us -> 44.5 us  [hop(): lax.ppermute(value, 'expert', [(2 * i + c, 2 * (i + by) + c) for i in sou...]
    ppermute x9 -> x18, starting transfers between devices: 11 us -> 14.6 us  [swap(): lax.ppermute(value, axis, [(i, i ^ bit) for i in range(lax.axis_size(axis...]
  transfers between devices with their start and end apart: 22 -> 36, of which waited for: 11 -> 17; matrix products, arithmetic and copies ran while one was open for 12% -> 17% of each run, Pallas kernels for 0% -> 0%
where the time goes in v2:
time: 342 us; the launch traced here: 340 us
  waiting for transfers between devices  200 us (58%)
  starting transfers between devices  59.1 us (17%)
  matrix products  52.9 us (15%)
  local copies, waits for them, and re-layouts  12 us (4%)
  other arithmetic  9.9 us (3%)
  between operations  7.07 us (2%)
    ppermute x18, waiting for transfers between devices, swap(): lax.ppermute(value, axis, [(i, i ^ bit) for i in range(lax.axis_size(axis...  114 us
    ppermute x18, waiting for transfers between devices, hop(): lax.ppermute(value, 'expert', [(2 * i + c, 2 * (i + by) + c) for i in sou...  85.8 us
    ppermute x18, starting transfers between devices, hop(): lax.ppermute(value, 'expert', [(2 * i + c, 2 * (i + by) + c) for i in sou...  44.5 us
    dot_general x8, matrix products, paired(): jnp.dot(hidden, w, preferred_element_type=F32).astype(BF)  17.7 us
    ppermute x18, starting transfers between devices, swap(): lax.ppermute(value, axis, [(i, i ^ bit) for i in range(lax.axis_size(axis...  14.6 us
    dot_general x4, matrix products, paired(): gu = jnp.dot(r[0], gate_x, preferred_element_type=F32) + n[0]  11.2 us
    dot_general x4, matrix products, paired(): sent = (jnp.dot(r[1], gate_x, preferred_element_type=F32) + n[1]).astype(BF)  11.2 us
  transfers between devices with their start and end apart: 36, of which 17 were waited for; matrix products, arithmetic and copies ran while one was open for 17% of the time, Pallas kernels for 0%

profile of v2, /device:TPU:0, one launch (start us, length us, event | category | flops | bytes accessed | tf_op | source)
XLA Modules:
  0.0 340.5 jit_solution(5669026795262392092)
XLA Ops:
  1.6 1.4 constant_dynamic-slice_fusion.3
  3.1 1.3 collective-permute-start.1
  4.4 6.4 %collective-permute-start = (bf16[128,1808]{1,0:T(8,128)(2,1)S(1)}, bf16[128,1808]{1,0:T(8,128)(2,1)}, u32[]{:S(2)}, u32[]{:S(2)}) collective-permute-start(bf16[128,1808]{1,0:T(8,128)(2,1)S(1)} %concatenate.54), channel_id=1, source_target_pairs={{0,2},{1,3},{2,4},{3,5},{4,6},{5,7},{8,10},{9,11},{10,12},{11,13},... | collective-permute-start | bytes 1388552 | tf_op jit(solution)/shard_map/ppermute | solution.py:80
  10.9 2.0 collective-permute-start.6
  13.0 1.6 collective-permute-start.7
  15.0 10.2 %collective-permute-done.7 = bf16[128,1808]{1,0:T(8,128)(2,1)S(1)} collective-permute-done((bf16[128,1808]{1,0:T(8,128)(2,1)S(1)}, bf16[128,1808]{1,0:T(8,128)(2,1)S(1)}, u32[]{:S(2)}, u32[]{:S(2)}) %collective-permute-start.7) | collective-permute-done | bytes 462880 | tf_op jit(solution)/shard_map/ppermute | solution.py:54
  25.3 1.3 collective-permute-start.9
  26.6 5.4 %collective-permute-start.8 = (bf16[128,1824]{1,0:T(8,128)(2,1)S(1)}, bf16[128,1824]{1,0:T(8,128)(2,1)}, u32[]{:S(2)}, u32[]{:S(2)}) collective-permute-start(bf16[128,1824]{1,0:T(8,128)(2,1)S(1)} %pad_maximum_fusion.12), channel_id=1, source_target_pairs={{0,2},{1,3},{2,4},{3,5},{4,6},{5,7},{8,10},{9,11},{10,12},{11,13},... | collective-permute-start | bytes 1400840 | tf_op jit(solution)/shard_map/ppermute | solution.py:80
  32.0 1.3 collective-permute-start.2
  33.4 1.5 collective-permute-start.4
  34.9 14.1 %collective-permute-done.2 = bf16[128,1808]{1,0:T(8,128)(2,1)S(1)} collective-permute-done((bf16[128,1808]{1,0:T(8,128)(2,1)S(1)}, bf16[128,1808]{1,0:T(8,128)(2,1)S(1)}, u32[]{:S(2)}, u32[]{:S(2)}) %collective-permute-start.2) | collective-permute-done | bytes 462880 | tf_op jit(solution)/shard_map/ppermute | solution.py:80
  49.8 1.3 collective-permute-start.3
  51.2 1.4 collective-permute-start.5
  52.7 1.4 collective-permute-start.10
  54.1 1.5 collective-permute-start.12
  55.6 10.6 %collective-permute-done.3 = bf16[128,1808]{1,0:T(8,128)(2,1)S(1)} collective-permute-done((bf16[128,1808]{1,0:T(8,128)(2,1)}, bf16[128,1808]{1,0:T(8,128)(2,1)S(1)}, u32[]{:S(2)}, u32[]{:S(2)}) %collective-permute-start.3) | collective-permute-done | bytes 462880 | tf_op jit(solution)/shard_map/ppermute | solution.py:80
  68.0 1.4 maximum_bitcast_fusion
  69.4 3.4 %collective-permute-done.10 = bf16[128,1824]{1,0:T(8,128)(2,1)} collective-permute-done((bf16[128,1824]{1,0:T(8,128)(2,1)}, bf16[128,1824]{1,0:T(8,128)(2,1)}, u32[]{:S(2)}, u32[]{:S(2)}) %collective-permute-start.10) | collective-permute-done | bytes 466976 | tf_op jit(solution)/shard_map/ppermute | solution.py:80
  72.9 1.1 broadcast_select_fusion.1
  74.2 1.3 collective-permute-start.11
  76.4 9.2 %collective-permute-done.11 = bf16[128,1824]{1,0:T(8,128)(2,1)S(1)} collective-permute-done((bf16[128,1824]{1,0:T(8,128)(2,1)}, bf16[128,1824]{1,0:T(8,128)(2,1)S(1)}, u32[]{:S(2)}, u32[]{:S(2)}) %collective-permute-start.11) | collective-permute-done | bytes 466976 | tf_op jit(solution)/shard_map/ppermute | solution.py:80
  85.9 1.1 broadcast_select_fusion
  88.6 1.3 maximum_bitcast_fusion.1
  89.9 1.9 convolution_convert_fusion
  91.8 1.5 collective-permute-start.15
  101.7 2.2 fusion.3
  103.9 1.8 pad_maximum_fusion.1
  105.7 28.9 %collective-permute-done.15 = bf16[1024,896]{1,0:T(8,128)(2,1)} collective-permute-done((bf16[1024,896]{1,0:T(8,128)(2,1)}, bf16[1024,896]{1,0:T(8,128)(2,1)}, u32[]{:S(2)}, u32[]{:S(2)}) %collective-permute-start.15) | collective-permute-done | bytes 1835040 | tf_op jit(solution)/shard_map/ppermute | solution.py:54
  135.5 6.6 %fusion = f32[4,2,128,2048]{3,2,1,0:T(8,128)S(1)} fusion(bf16[4,2,128,896]{3,2,1,0:T(8,128)(2,1)S(1)} %bitcast.230, bf16[1,896,2048]{2,1,0:T(8,128)(2,1)} %param.7), kind=kOutput, calls=%fused_computation.2 | convolution fusion | flops 3758096384 | bytes 13893632 | tf_op jit(solution)/shard_map/dot_general | solution.py:134
  142.0 33.1 %collective-permute-done.16 = bf16[896,2048]{1,0:T(8,128)(2,1)} collective-permute-done((bf16[896,2048]{1,0:T(8,128)(2,1)}, bf16[896,2048]{1,0:T(8,128)(2,1)}, u32[]{:S(2)}, u32[]{:S(2)}) %collective-permute-start.16) | collective-permute-done | bytes 3670048 | tf_op jit(solution)/shard_map/ppermute | solution.py:54
  175.1 2.8 fusion.9
  178.5 2.8 fusion.10
  181.3 1.6 collective-permute-start.20
  182.9 2.8 fusion.11
  186.3 2.8 fusion.12
  189.2 1.6 collective-permute-start.26
  190.7 2.1 collective-permute-done.17
  192.9 2.8 fusion.5
  196.4 7.7 %collective-permute-done.20 = bf16[128,2048]{1,0:T(8,128)(2,1)S(1)} collective-permute-done((bf16[128,2048]{1,0:T(8,128)(2,1)S(1)}, bf16[128,2048]{1,0:T(8,128)(2,1)S(1)}, u32[]{:S(2)}, u32[]{:S(2)}) %collective-permute-start.20) | collective-permute-done | bytes 524320 | tf_op jit(solution)/shard_map/ppermute | solution.py:54
  204.1 2.8 fusion.6
  207.7 17.3 %collective-permute-done.26 = bf16[128,2048]{1,0:T(8,128)(2,1)S(1)} collective-permute-done((bf16[128,2048]{1,0:T(8,128)(2,1)S(1)}, bf16[128,2048]{1,0:T(8,128)(2,1)S(1)}, u32[]{:S(2)}, u32[]{:S(2)}) %collective-permute-start.26) | collective-permute-done | bytes 524320 | tf_op jit(solution)/shard_map/ppermute | solution.py:54
  224.9 2.8 fusion.8
  228.7 2.8 fusion.7
  231.7 1.6 collective-permute-start.24
  233.3 4.0 %collective-permute-done.27 = bf16[128,1024]{1,0:T(8,128)(2,1)S(1)} collective-permute-done((bf16[128,1024]{1,0:T(8,128)(2,1)S(1)}, bf16[128,1024]{1,0:T(8,128)(2,1)S(1)}, u32[]{:S(2)}, u32[]{:S(2)}) %collective-permute-start.27) | collective-permute-done | bytes 262176 | tf_op jit(solution)/shard_map/ppermute | solution.py:54
  237.3 2.2 convolution_convert_fusion.3
  239.5 2.2 convolution_convert_fusion.2
  241.9 2.2 convolution_convert_fusion.4
  244.2 2.2 convolution_convert_fusion.5
  247.1 2.2 convolution_convert_fusion.6
  250.5 2.6 collective-permute-start.29
  253.2 2.2 convolution_convert_fusion.7
  256.1 16.8 %collective-permute-done.29 = bf16[2,128,1792]{2,1,0:T(8,128)(2,1)S(1)} collective-permute-done((bf16[2,128,1792]{2,1,0:T(8,128)(2,1)S(1)}, bf16[2,128,1792]{2,1,0:T(8,128)(2,1)S(1)}, u32[]{:S(2)}, u32[]{:S(2)}) %collective-permute-start.29) | collective-permute-done | bytes 917536 | tf_op jit(solution)/shard_map/ppermute | solution.py:80
  273.4 4.4 %collective-permute-start.30 = (bf16[2,128,1792]{2,1,0:T(8,128)(2,1)S(1)}, bf16[2,128,1792]{2,1,0:T(8,128)(2,1)S(1)}, u32[]{:S(2)}, u32[]{:S(2)}) collective-permute-start(bf16[2,128,1792]{2,1,0:T(8,128)(2,1)S(1)} %get-tuple-element.15), channel_id=1, source_target_pairs={{0,2},{1,3},{2,4},{3,5},{8,10},{9,11},{10,12},{11,13},{16,18},{17,... | collective-permute-start | bytes 2752520 | tf_op jit(solution)/shard_map/ppermute | solution.py:80
  278.6 2.2 convolution_convert_fusion.8
  280.8 2.2 convolution_convert_fusion.9
  283.6 13.1 %collective-permute-done.30 = bf16[2,128,1792]{2,1,0:T(8,128)(2,1)S(1)} collective-permute-done((bf16[2,128,1792]{2,1,0:T(8,128)(2,1)S(1)}, bf16[2,128,1792]{2,1,0:T(8,128)(2,1)S(1)}, u32[]{:S(2)}, u32[]{:S(2)}) %collective-permute-start.30) | collective-permute-done | bytes 917536 | tf_op jit(solution)/shard_map/ppermute | solution.py:80
  297.3 9.7 %collective-permute-start.31 = (bf16[2,128,1792]{2,1,0:T(8,128)(2,1)S(1)}, bf16[2,128,1792]{2,1,0:T(8,128)(2,1)S(1)}, u32[]{:S(2)}, u32[]{:S(2)}) collective-permute-start(bf16[2,128,1792]{2,1,0:T(8,128)(2,1)S(1)} %get-tuple-element.9), channel_id=1, source_target_pairs={{0,2},{1,3},{2,4},{3,5},{4,6},{5,7},{8,10},{9,11},{10,12},{11,13},... | collective-permute-start | bytes 2752520 | tf_op jit(solution)/shard_map/ppermute | solution.py:80
  307.0 1.3 collective-permute-start.34
  308.5 1.8 collective-permute-done.19
  310.3 14.4 %collective-permute-done.31 = bf16[2,128,1792]{2,1,0:T(8,128)(2,1)S(1)} collective-permute-done((bf16[2,128,1792]{2,1,0:T(8,128)(2,1)S(1)}, bf16[2,128,1792]{2,1,0:T(8,128)(2,1)S(1)}, u32[]{:S(2)}, u32[]{:S(2)}) %collective-permute-start.31) | collective-permute-done | bytes 917536 | tf_op jit(solution)/shard_map/ppermute | solution.py:80
  324.7 4.2 %collective-permute-done.34 = bf16[2,128,1792]{2,1,0:T(8,128)(2,1)S(1)} collective-permute-done((bf16[2,128,1792]{2,1,0:T(8,128)(2,1)S(1)}, bf16[2,128,1792]{2,1,0:T(8,128)(2,1)S(1)}, u32[]{:S(2)}, u32[]{:S(2)}) %collective-permute-start.34) | collective-permute-done | bytes 917536 | tf_op jit(solution)/shard_map/ppermute | solution.py:80
  330.1 8.6 %collective-permute-done.35 = bf16[128,1792]{1,0:T(8,128)(2,1)S(1)} collective-permute-done((bf16[128,1792]{1,0:T(8,128)(2,1)S(1)}, bf16[128,1792]{1,0:T(8,128)(2,1)S(1)}, u32[]{:S(2)}, u32[]{:S(2)}) %collective-permute-start.35) | collective-permute-done | bytes 458784 | tf_op jit(solution)/shard_map/ppermute | solution.py:54
  338.8 0.9 copy-done.1
  (129 shorter events, 22.1 us)
Async XLA Ops:
  3.1 28.9 %collective-permute-start.1 = (bf16[128,1808]{1,0:T(8,128)(2,1)S(1)}, bf16[128,1808]{1,0:T(8,128)(2,1)S(1)}, u32[]{:S(2)}, u32[]{:S(2)}) collective-permute-start(bf16[128,1808]{1,0:T(8,128)(2,1)S(1)} %concatenate.54), channel_id=1, source_target_pairs={{2,0},{3,1},{4,2},{5,3},{6,4},{7,5},{10,8},{11,9},{12,10},{13,11},... | collective-permute-start | bytes 1388552 | tf_op jit(solution)/shard_map/ppermute | solution.py:80
  4.4 28.9 %collective-permute-start = (bf16[128,1808]{1,0:T(8,128)(2,1)S(1)}, bf16[128,1808]{1,0:T(8,128)(2,1)}, u32[]{:S(2)}, u32[]{:S(2)}) collective-permute-start(bf16[128,1808]{1,0:T(8,128)(2,1)S(1)} %concatenate.54), channel_id=1, source_target_pairs={{0,2},{1,3},{2,4},{3,5},{4,6},{5,7},{8,10},{9,11},{10,12},{11,13},... | collective-permute-start | bytes 1388552 | tf_op jit(solution)/shard_map/ppermute | solution.py:80
  10.9 4.0 %collective-permute-start.6 = (bf16[128,16]{1,0:T(8,128)(2,1)S(1)}, bf16[128,16]{1,0:T(8,128)(2,1)S(1)}, u32[]{:S(2)}, u32[]{:S(2)}) collective-permute-start(bf16[128,16]{1,0:T(8,128)(2,1)S(1)} %pad_maximum_fusion.22), channel_id=1, source_target_pairs={{0,8},{8,0},{16,24},{24,16},{1,9},{9,1},{17,25},{25,17},{2,10},{10... | collective-permute-start | bytes 12296 | tf_op jit(solution)/shard_map/ppermute | solution.py:54
  13.0 12.2 %collective-permute-start.7 = (bf16[128,1808]{1,0:T(8,128)(2,1)S(1)}, bf16[128,1808]{1,0:T(8,128)(2,1)S(1)}, u32[]{:S(2)}, u32[]{:S(2)}) collective-permute-start(bf16[128,1808]{1,0:T(8,128)(2,1)S(1)} %concatenate.55), channel_id=1, source_target_pairs={{0,16},{8,24},{16,0},{24,8},{1,17},{9,25},{17,1},{25,9},{2,18},{10... | collective-permute-start | bytes 1388552 | tf_op jit(solution)/shard_map/ppermute | solution.py:54
  25.3 27.4 %collective-permute-start.9 = (bf16[128,1824]{1,0:T(8,128)(2,1)S(1)}, bf16[128,1824]{1,0:T(8,128)(2,1)}, u32[]{:S(2)}, u32[]{:S(2)}) collective-permute-start(bf16[128,1824]{1,0:T(8,128)(2,1)S(1)} %pad_maximum_fusion.12), channel_id=1, source_target_pairs={{2,0},{3,1},{4,2},{5,3},{6,4},{7,5},{10,8},{11,9},{12,10},{13,11},... | collective-permute-start | bytes 1400840 | tf_op jit(solution)/shard_map/ppermute | solution.py:80
  26.6 27.5 %collective-permute-start.8 = (bf16[128,1824]{1,0:T(8,128)(2,1)S(1)}, bf16[128,1824]{1,0:T(8,128)(2,1)}, u32[]{:S(2)}, u32[]{:S(2)}) collective-permute-start(bf16[128,1824]{1,0:T(8,128)(2,1)S(1)} %pad_maximum_fusion.12), channel_id=1, source_target_pairs={{0,2},{1,3},{2,4},{3,5},{4,6},{5,7},{8,10},{9,11},{10,12},{11,13},... | collective-permute-start | bytes 1400840 | tf_op jit(solution)/shard_map/ppermute | solution.py:80
  32.0 19.1 %copy-start.2 = (bf16[128,1808]{1,0:T(8,128)(2,1)}, bf16[128,1808]{1,0:T(8,128)(2,1)S(1)}, u32[]{:S(2)}) copy-start(bf16[128,1808]{1,0:T(8,128)(2,1)S(1)} %collective-permute-done.1) | copy-start | bytes 1388548
  32.0 16.9 %collective-permute-start.2 = (bf16[128,1808]{1,0:T(8,128)(2,1)S(1)}, bf16[128,1808]{1,0:T(8,128)(2,1)S(1)}, u32[]{:S(2)}, u32[]{:S(2)}) collective-permute-start(bf16[128,1808]{1,0:T(8,128)(2,1)S(1)} %collective-permute-done.1), channel_id=1, source_target_pairs={{2,0},{3,1},{4,2},{5,3},{10,8},{11,9},{12,10},{13,11},{18,16},{19,... | collective-permute-start | bytes 1388552 | tf_op jit(solution)/shard_map/ppermute | solution.py:80
  33.4 15.6 %collective-permute-start.4 = (bf16[128,1808]{1,0:T(8,128)(2,1)}, bf16[128,1808]{1,0:T(8,128)(2,1)}, u32[]{:S(2)}, u32[]{:S(2)}) collective-permute-start(bf16[128,1808]{1,0:T(8,128)(2,1)} %collective-permute-done), channel_id=1, source_target_pairs={{2,4},{3,5},{4,6},{5,7},{10,12},{11,13},{12,14},{13,15},{18,20},{1... | collective-permute-start | bytes 1388552 | tf_op jit(solution)/shard_map/ppermute | solution.py:80
  48.9 0.8 copy-start.4
  49.8 16.3 %collective-permute-start.3 = (bf16[128,1808]{1,0:T(8,128)(2,1)}, bf16[128,1808]{1,0:T(8,128)(2,1)S(1)}, u32[]{:S(2)}, u32[]{:S(2)}) collective-permute-start(bf16[128,1808]{1,0:T(8,128)(2,1)} %copy-done.4), channel_id=1, source_target_pairs={{2,0},{3,1},{10,8},{11,9},{18,16},{19,17},{26,24},{27,25}} | collective-permute-start | bytes 1388552 | tf_op jit(solution)/shard_map/ppermute | solution.py:80
  51.2 15.9 %collective-permute-start.5 = (bf16[128,1808]{1,0:T(8,128)(2,1)}, bf16[128,1808]{1,0:T(8,128)(2,1)}, u32[]{:S(2)}, u32[]{:S(2)}) collective-permute-start(bf16[128,1808]{1,0:T(8,128)(2,1)} %collective-permute-done.4), channel_id=1, source_target_pairs={{4,6},{5,7},{12,14},{13,15},{20,22},{21,23},{28,30},{29,31}} | collective-permute-start | bytes 1388552 | tf_op jit(solution)/shard_map/ppermute | solution.py:80
  52.6 14.5 %copy-start.3 = (bf16[128,1808]{1,0:T(8,128)(2,1)S(1)}, bf16[128,1808]{1,0:T(8,128)(2,1)}, u32[]{:S(2)}) copy-start(bf16[128,1808]{1,0:T(8,128)(2,1)} %copy-done.2) | copy-start | bytes 1388548
  52.7 20.2 %collective-permute-start.10 = (bf16[128,1824]{1,0:T(8,128)(2,1)}, bf16[128,1824]{1,0:T(8,128)(2,1)}, u32[]{:S(2)}, u32[]{:S(2)}) collective-permute-start(bf16[128,1824]{1,0:T(8,128)(2,1)} %collective-permute-done.9), channel_id=1, source_target_pairs={{2,0},{3,1},{4,2},{5,3},{10,8},{11,9},{12,10},{13,11},{18,16},{19,... | collective-permute-start | bytes 1400840 | tf_op jit(solution)/shard_map/ppermute | solution.py:80
  54.1 18.8 %collective-permute-start.12 = (bf16[128,1824]{1,0:T(8,128)(2,1)}, bf16[128,1824]{1,0:T(8,128)(2,1)}, u32[]{:S(2)}, u32[]{:S(2)}) collective-permute-start(bf16[128,1824]{1,0:T(8,128)(2,1)} %collective-permute-done.8), channel_id=1, source_target_pairs={{2,4},{3,5},{4,6},{5,7},{10,12},{11,13},{12,14},{13,15},{18,20},{1... | collective-permute-start | bytes 1400840 | tf_op jit(solution)/shard_map/ppermute | solution.py:80
  74.2 11.5 %collective-permute-start.11 = (bf16[128,1824]{1,0:T(8,128)(2,1)}, bf16[128,1824]{1,0:T(8,128)(2,1)S(1)}, u32[]{:S(2)}, u32[]{:S(2)}) collective-permute-start(bf16[128,1824]{1,0:T(8,128)(2,1)} %collective-permute-done.10), channel_id=1, source_target_pairs={{2,0},{3,1},{10,8},{11,9},{18,16},{19,17},{26,24},{27,25}} | collective-permute-start | bytes 1400840 | tf_op jit(solution)/shard_map/ppermute | solution.py:80
  75.5 10.3 %collective-permute-start.13 = (bf16[128,1824]{1,0:T(8,128)(2,1)}, bf16[128,1824]{1,0:T(8,128)(2,1)S(1)}, u32[]{:S(2)}, u32[]{:S(2)}) collective-permute-start(bf16[128,1824]{1,0:T(8,128)(2,1)} %collective-permute-done.12), channel_id=1, source_target_pairs={{4,6},{5,7},{12,14},{13,15},{20,22},{21,23},{28,30},{29,31}} | collective-permute-start | bytes 1400840 | tf_op jit(solution)/shard_map/ppermute | solution.py:80
  89.9 1.9 copy-start
  91.8 12.0 %collective-permute-start.14 = (bf16[4,2,64,1792]{3,2,1,0:T(8,128)(2,1)}, bf16[4,2,64,1792]{3,2,1,0:T(8,128)(2,1)}, u32[]{:S(2)}, u32[]{:S(2)}) collective-permute-start(bf16[4,2,64,1792]{3,2,1,0:T(8,128)(2,1)} %convolution_convert_fusion), channel_id=1, source_target_pairs={{0,1},{1,0},{2,3},{3,2},{4,5},{5,4},{6,7},{7,6},{8,9},{9,8},{10,11... | collective-permute-start | bytes 5505032 | tf_op jit(solution)/shard_map/ppermute | solution.py:54
  91.8 42.7 %collective-permute-start.15 = (bf16[1024,896]{1,0:T(8,128)(2,1)}, bf16[1024,896]{1,0:T(8,128)(2,1)}, u32[]{:S(2)}, u32[]{:S(2)}) collective-permute-start(bf16[1024,896]{1,0:T(8,128)(2,1)} %bitcast.38), channel_id=1, source_target_pairs={{0,16},{8,24},{16,0},{24,8},{1,17},{9,25},{17,1},{25,9},{2,18},{10... | collective-permute-start | bytes 5505032 | tf_op jit(solution)/shard_map/ppermute | solution.py:54
  93.3 81.8 %collective-permute-start.16 = (bf16[896,2048]{1,0:T(8,128)(2,1)}, bf16[896,2048]{1,0:T(8,128)(2,1)}, u32[]{:S(2)}, u32[]{:S(2)}) collective-permute-start(bf16[896,2048]{1,0:T(8,128)(2,1)} %bitcast.41), channel_id=1, source_target_pairs={{0,8},{8,0},{16,24},{24,16},{1,9},{9,1},{17,25},{25,17},{2,10},{10... | collective-permute-start | bytes 11010056 | tf_op jit(solution)/shard_map/ppermute | solution.py:54
  177.9 14.9 %collective-permute-start.17 = (bf16[128,2048]{1,0:T(8,128)(2,1)S(1)}, bf16[128,2048]{1,0:T(8,128)(2,1)S(1)}, u32[]{:S(2)}, u32[]{:S(2)}) collective-permute-start(bf16[128,2048]{1,0:T(8,128)(2,1)S(1)} %fusion.9), channel_id=1, source_target_pairs={{0,16},{8,24},{16,0},{24,8},{1,17},{9,25},{17,1},{25,9},{2,18},{10... | collective-permute-start | bytes 1572872 | tf_op jit(solution)/shard_map/ppermute | solution.py:54
  181.3 22.8 %collective-permute-start.20 = (bf16[128,2048]{1,0:T(8,128)(2,1)S(1)}, bf16[128,2048]{1,0:T(8,128)(2,1)S(1)}, u32[]{:S(2)}, u32[]{:S(2)}) collective-permute-start(bf16[128,2048]{1,0:T(8,128)(2,1)S(1)} %fusion.10), channel_id=1, source_target_pairs={{0,16},{8,24},{16,0},{24,8},{1,17},{9,25},{17,1},{25,9},{2,18},{10... | collective-permute-start | bytes 1572872 | tf_op jit(solution)/shard_map/ppermute | solution.py:54
  185.7 43.0 %collective-permute-start.23 = (bf16[128,2048]{1,0:T(8,128)(2,1)S(1)}, bf16[128,2048]{1,0:T(8,128)(2,1)S(1)}, u32[]{:S(2)}, u32[]{:S(2)}) collective-permute-start(bf16[128,2048]{1,0:T(8,128)(2,1)S(1)} %fusion.11), channel_id=1, source_target_pairs={{0,16},{8,24},{16,0},{24,8},{1,17},{9,25},{17,1},{25,9},{2,18},{10... | collective-permute-start | bytes 1572872 | tf_op jit(solution)/shard_map/ppermute | solution.py:54
  189.2 35.8 %collective-permute-start.26 = (bf16[128,2048]{1,0:T(8,128)(2,1)S(1)}, bf16[128,2048]{1,0:T(8,128)(2,1)S(1)}, u32[]{:S(2)}, u32[]{:S(2)}) collective-permute-start(bf16[128,2048]{1,0:T(8,128)(2,1)S(1)} %fusion.12), channel_id=1, source_target_pairs={{0,16},{8,24},{16,0},{24,8},{1,17},{9,25},{17,1},{25,9},{2,18},{10... | collective-permute-start | bytes 1572872 | tf_op jit(solution)/shard_map/ppermute | solution.py:54
  195.8 82.7 %collective-permute-start.18 = (bf16[128,1024]{1,0:T(8,128)(2,1)S(1)}, bf16[128,1024]{1,0:T(8,128)(2,1)S(1)}, u32[]{:S(2)}, u32[]{:S(2)}) collective-permute-start(bf16[128,1024]{1,0:T(8,128)(2,1)S(1)} %fusion.31), channel_id=1, source_target_pairs={{0,8},{8,0},{16,24},{24,16},{1,9},{9,1},{17,25},{25,17},{2,10},{10... | collective-permute-start | bytes 786440 | tf_op jit(solution)/shard_map/ppermute | solution.py:54
  207.1 40.0 %collective-permute-start.21 = (bf16[128,1024]{1,0:T(8,128)(2,1)S(1)}, bf16[128,1024]{1,0:T(8,128)(2,1)S(1)}, u32[]{:S(2)}, u32[]{:S(2)}) collective-permute-start(bf16[128,1024]{1,0:T(8,128)(2,1)S(1)} %fusion.30), channel_id=1, source_target_pairs={{0,8},{8,0},{16,24},{24,16},{1,9},{9,1},{17,25},{25,17},{2,10},{10... | collective-permute-start | bytes 786440 | tf_op jit(solution)/shard_map/ppermute | solution.py:54
  228.1 9.1 %collective-permute-start.27 = (bf16[128,1024]{1,0:T(8,128)(2,1)S(1)}, bf16[128,1024]{1,0:T(8,128)(2,1)S(1)}, u32[]{:S(2)}, u32[]{:S(2)}) collective-permute-start(bf16[128,1024]{1,0:T(8,128)(2,1)S(1)} %fusion.28), channel_id=1, source_target_pairs={{0,8},{8,0},{16,24},{24,16},{1,9},{9,1},{17,25},{25,17},{2,10},{10... | collective-permute-start | bytes 786440 | tf_op jit(solution)/shard_map/ppermute | solution.py:54
  231.7 10.2 %collective-permute-start.24 = (bf16[128,1024]{1,0:T(8,128)(2,1)S(1)}, bf16[128,1024]{1,0:T(8,128)(2,1)S(1)}, u32[]{:S(2)}, u32[]{:S(2)}) collective-permute-start(bf16[128,1024]{1,0:T(8,128)(2,1)S(1)} %fusion.29), channel_id=1, source_target_pairs={{0,8},{8,0},{16,24},{24,16},{1,9},{9,1},{17,25},{25,17},{2,10},{10... | collective-permute-start | bytes 786440 | tf_op jit(solution)/shard_map/ppermute | solution.py:54
  241.9 7.5 %collective-permute-start.28 = (bf16[2,64,1792]{2,1,0:T(8,128)(2,1)S(1)}, bf16[2,64,1792]{2,1,0:T(8,128)(2,1)S(1)}, u32[]{:S(2)}, u32[]{:S(2)}) collective-permute-start(bf16[2,64,1792]{2,1,0:T(8,128)(2,1)S(1)} %get-tuple-element.30), channel_id=1, source_target_pairs={{0,1},{1,0},{2,3},{3,2},{4,5},{5,4},{6,7},{7,6},{8,9},{9,8},{10,11... | collective-permute-start | bytes 1376264 | tf_op jit(solution)/shard_map/ppermute | solution.py:54
  246.5 9.1 %collective-permute-start.25 = (bf16[2,64,1792]{2,1,0:T(8,128)(2,1)S(1)}, bf16[2,64,1792]{2,1,0:T(8,128)(2,1)S(1)}, u32[]{:S(2)}, u32[]{:S(2)}) collective-permute-start(bf16[2,64,1792]{2,1,0:T(8,128)(2,1)S(1)} %get-tuple-element.26), channel_id=1, source_target_pairs={{0,1},{1,0},{2,3},{3,2},{4,5},{5,4},{6,7},{7,6},{8,9},{9,8},{10,11... | collective-permute-start | bytes 1376264 | tf_op jit(solution)/shard_map/ppermute | solution.py:54
  249.8 6.3 %collective-permute-start.32 = (bf16[2,128,1792]{2,1,0:T(8,128)(2,1)S(1)}, bf16[2,128,1792]{2,1,0:T(8,128)(2,1)S(1)}, u32[]{:S(2)}, u32[]{:S(2)}) collective-permute-start(bf16[2,128,1792]{2,1,0:T(8,128)(2,1)S(1)} %get-tuple-element.49), channel_id=1, source_target_pairs={{6,4},{7,5},{14,12},{15,13},{22,20},{23,21},{30,28},{31,29}} | collective-permute-start | bytes 2752520 | tf_op jit(solution)/shard_map/ppermute | solution.py:80
  250.5 22.4 %collective-permute-start.29 = (bf16[2,128,1792]{2,1,0:T(8,128)(2,1)S(1)}, bf16[2,128,1792]{2,1,0:T(8,128)(2,1)S(1)}, u32[]{:S(2)}, u32[]{:S(2)}) collective-permute-start(bf16[2,128,1792]{2,1,0:T(8,128)(2,1)S(1)} %get-tuple-element.49), channel_id=1, source_target_pairs={{0,2},{1,3},{8,10},{9,11},{16,18},{17,19},{24,26},{25,27}} | collective-permute-start | bytes 2752520 | tf_op jit(solution)/shard_map/ppermute | solution.py:80
  255.5 27.6 %collective-permute-start.22 = (bf16[2,64,1792]{2,1,0:T(8,128)(2,1)S(1)}, bf16[2,64,1792]{2,1,0:T(8,128)(2,1)S(1)}, u32[]{:S(2)}, u32[]{:S(2)}) collective-permute-start(bf16[2,64,1792]{2,1,0:T(8,128)(2,1)S(1)} %get-tuple-element.22), channel_id=1, source_target_pairs={{0,1},{1,0},{2,3},{3,2},{4,5},{5,4},{6,7},{7,6},{8,9},{9,8},{10,11... | collective-permute-start | bytes 1376264 | tf_op jit(solution)/shard_map/ppermute | solution.py:54
  273.4 23.3 %collective-permute-start.30 = (bf16[2,128,1792]{2,1,0:T(8,128)(2,1)S(1)}, bf16[2,128,1792]{2,1,0:T(8,128)(2,1)S(1)}, u32[]{:S(2)}, u32[]{:S(2)}) collective-permute-start(bf16[2,128,1792]{2,1,0:T(8,128)(2,1)S(1)} %get-tuple-element.15), channel_id=1, source_target_pairs={{0,2},{1,3},{2,4},{3,5},{8,10},{9,11},{10,12},{11,13},{16,18},{17,... | collective-permute-start | bytes 2752520 | tf_op jit(solution)/shard_map/ppermute | solution.py:80
  277.8 18.9 %collective-permute-start.33 = (bf16[2,128,1792]{2,1,0:T(8,128)(2,1)S(1)}, bf16[2,128,1792]{2,1,0:T(8,128)(2,1)S(1)}, u32[]{:S(2)}, u32[]{:S(2)}) collective-permute-start(bf16[2,128,1792]{2,1,0:T(8,128)(2,1)S(1)} %get-tuple-element.16), channel_id=1, source_target_pairs={{4,2},{5,3},{6,4},{7,5},{12,10},{13,11},{14,12},{15,13},{20,18},{2... | collective-permute-start | bytes 2752520 | tf_op jit(solution)/shard_map/ppermute | solution.py:80
  297.3 27.4 %collective-permute-start.31 = (bf16[2,128,1792]{2,1,0:T(8,128)(2,1)S(1)}, bf16[2,128,1792]{2,1,0:T(8,128)(2,1)S(1)}, u32[]{:S(2)}, u32[]{:S(2)}) collective-permute-start(bf16[2,128,1792]{2,1,0:T(8,128)(2,1)S(1)} %get-tuple-element.9), channel_id=1, source_target_pairs={{0,2},{1,3},{2,4},{3,5},{4,6},{5,7},{8,10},{9,11},{10,12},{11,13},... | collective-permute-start | bytes 2752520 | tf_op jit(solution)/shard_map/ppermute | solution.py:80
  307.0 21.8 %collective-permute-start.34 = (bf16[2,128,1792]{2,1,0:T(8,128)(2,1)S(1)}, bf16[2,128,1792]{2,1,0:T(8,128)(2,1)S(1)}, u32[]{:S(2)}, u32[]{:S(2)}) collective-permute-start(bf16[2,128,1792]{2,1,0:T(8,128)(2,1)S(1)} %get-tuple-element.10), channel_id=1, source_target_pairs={{2,0},{3,1},{4,2},{5,3},{6,4},{7,5},{10,8},{11,9},{12,10},{13,11},... | collective-permute-start | bytes 2752520 | tf_op jit(solution)/shard_map/ppermute | solution.py:80
  308.4 1.9 collective-permute-start.19
  329.5 9.3 %collective-permute-start.35 = (bf16[128,1792]{1,0:T(8,128)(2,1)S(1)}, bf16[128,1792]{1,0:T(8,128)(2,1)S(1)}, u32[]{:S(2)}, u32[]{:S(2)}) collective-permute-start(bf16[128,1792]{1,0:T(8,128)(2,1)S(1)} %slice_bitcast_fusion), channel_id=1, source_target_pairs={{0,8},{8,0},{16,24},{24,16},{1,9},{9,1},{17,25},{25,17},{2,10},{10... | collective-permute-start | bytes 1376264 | tf_op jit(solution)/shard_map/ppermute | solution.py:54
  338.8 0.9 copy-start.1

commit v3 on v2

v3 whole, which is shorter than its diff:
```python
import jax
import jax.numpy as jnp
from jax import lax
from jax.sharding import PartitionSpec as P

BF = jnp.bfloat16
F32 = jnp.float32
CUTS = ((0, 1), (1, 3), (3, 5), (5, 6), (6, 7))


def gathered(tokens, gate_up, down_proj, expert_ids, gate_weights):
    owners = lax.axis_size("expert")
    tok_rows = tokens.shape[0]
    width = tokens.shape[1]
    hidden_units = down_proj.shape[1]
    slots = 4 * tok_rows // owners
    total_rows = owners * slots
    owner_ids = jnp.arange(owners, dtype=jnp.int32)
    matches = expert_ids[:, :, None] == owner_ids[None, None, :]
    hits = jnp.sum(matches.astype(jnp.int32), axis=1)
    pick_weight = jnp.sum(
        jnp.where(matches, gate_weights[:, :, None].astype(F32), 0.0), axis=1
    )
    before = jnp.cumsum(hits, axis=0) - hits
    target = jnp.where(hits > 0, owner_ids[None, :] * slots + before, -1)
    slot_owner = jnp.arange(total_rows, dtype=jnp.int32) // slots
    slot_ids = jnp.arange(total_rows, dtype=jnp.int32)
    placed = jnp.take(target, slot_owner, axis=1) == slot_ids[None, :]
    place_bf = placed.astype(BF)
    outgoing = jnp.dot(place_bf.T, tokens, preferred_element_type=F32).astype(BF)
    arrived = lax.all_to_all(
        outgoing.reshape(owners, slots, width), "expert", split_axis=0, concat_axis=0, tiled=True
    )
    rows = arrived.reshape(total_rows, width)
    gu = jnp.dot(
        rows,
        lax.all_gather(gate_up, "dp", axis=1, tiled=True)[0],
        preferred_element_type=F32,
    )
    hidden = (jax.nn.silu(gu[:, :hidden_units]) * gu[:, hidden_units:]).astype(BF)
    result = jnp.dot(
        hidden,
        lax.all_gather(down_proj, "dp", axis=2, tiled=True)[0],
        preferred_element_type=F32,
    ).astype(BF)
    returned = lax.all_to_all(
        result.reshape(owners, slots, width), "expert", split_axis=0, concat_axis=0, tiled=True
    )
    weighted = (place_bf.astype(F32) * jnp.take(pick_weight, slot_owner, axis=1)).astype(BF)
    mixed = jnp.dot(weighted, returned.reshape(total_rows, width), preferred_element_type=F32)
    return mixed.astype(BF)


def swap(value, axis, bit):
    return lax.ppermute(value, axis, [(i, i ^ bit) for i in range(lax.axis_size(axis))])


def order_of(chips):
    def step(chip, to):
        return chips - abs(to - chip) if to != chip else chips

    return [sorted(range(chips), key=lambda to: (step(chip, to), to)) for chip in range(chips)]


def paired(tokens, gate_up, down_proj, expert_ids, gate_weights):
    owners = lax.axis_size("expert")
    chips = owners // 2
    tok = tokens.shape[0]
    top = expert_ids.shape[1]
    quarter = gate_up.shape[1]
    half = 2 * quarter
    ff = down_proj.shape[1]
    slots = 4 * tok // owners
    d = lax.axis_index("dp")
    e = lax.axis_index("expert")
    z = e // 2
    gate, down = gate_up[0], down_proj[0]
    order = jnp.array(order_of(chips), jnp.int32)[z]

    def hop(value, sources, by):
        return lax.ppermute(
            value, "expert", [(2 * i + c, 2 * (i + by) + c) for i in sources for c in range(2)]
        )

    together = lax.optimization_barrier
    parts = [
        lax.dynamic_slice_in_dim(tokens, (d ^ r) * quarter, quarter, axis=1) for r in range(4)
    ]
    info = jnp.concatenate([expert_ids.astype(BF), gate_weights], axis=1)
    first = jnp.concatenate([parts[0], parts[1], info], axis=1)
    gates = [gate[quarter * lo // 7 : quarter * hi // 7] for lo, hi in CUTS]
    downs = jnp.split(down, 2)

    rights, lefts, down_y, gate_x = [{}, {}], [{}, {}], [], []
    own = [first, None]
    for step in range(chips):
        work = {"gate": swap(gates[step], "dp", 1)}
        if step == 0:
            work["info"] = swap(info, "dp", 1)
            work["pair"] = swap(jnp.concatenate([parts[2], parts[3], info], axis=1), "dp", 2)
        elif step <= 2:
            work["down"] = swap(downs[step - 1], "dp", 2)
        for g in range(2):
            k = step + 1 - g
            if 1 <= k < chips:
                source = own[g]
                work[f"right{g}"] = hop(
                    source if k == 1 else rights[g][k - 1], range(k - 1, chips - 1), 1
                )
                work[f"left{g}"] = hop(
                    source if k == 1 else lefts[g][k - 1], range(1, chips - k + 1), -1
                )
        work = together(work)
        gate_x.append(work["gate"])
        if step == 0:
            own[1] = jnp.concatenate([work["pair"], work["info"]], axis=1)
        elif step <= 2:
            down_y.append(work["down"])
        for g in range(2):
            k = step + 1 - g
            if 1 <= k < chips:
                rights[g][k], lefts[g][k] = work[f"right{g}"], work[f"left{g}"]
    gate_last = swap(gates[-1], "dp", 1)
    down_y = jnp.concatenate(down_y)

    seen = [
        [own[g]] + [jnp.where(z >= k, rights[g][k], lefts[g][chips - k]) for k in range(1, chips)]
        for g in range(2)
    ]
    chosen = jnp.stack([e, e ^ 1]).astype(jnp.int32)
    earlier = jnp.triu(jnp.ones((tok, tok), BF), 1)

    def places(group, at):
        info = jnp.stack([s[:, at : at + 2 * top] for s in seen[group]])
        matches = info[..., :top].astype(jnp.int32)[..., None] == chosen
        hits = jnp.any(matches, axis=2).transpose(0, 2, 1)
        weight = jnp.sum(jnp.where(matches, info[..., top:, None].astype(F32), 0.0), axis=2)
        rank = jnp.dot(hits.astype(BF), earlier, preferred_element_type=F32)
        rank = jnp.where(hits, rank, -1.0)
        place = (rank[..., None, :] == jnp.arange(slots, dtype=F32)[:, None]).astype(BF)
        pay = place * weight.transpose(0, 2, 1)[..., None, :].astype(BF)
        return place, pay.reshape(chips, 2 * slots, tok)

    chunk = 2 * slots
    rows, near, pays = [], [], []
    gate_early = jnp.concatenate(gate_x)
    early = quarter + gate_early.shape[0]
    for g in range(2):
        place, pay = places(g, half)
        pays.append(pay)
        held = jnp.stack([s[:, :half] for s in seen[g]])

        def choose(expert):
            return jnp.einsum(
                "zst,ztk->zsk", place[:, expert], held, preferred_element_type=F32
            ).astype(BF)

        other = swap(choose(1), "expert", 1)
        r = jnp.concatenate([choose(0), other], axis=1)
        flat = r.reshape(-1, half)
        n = jnp.dot(flat[:, :quarter], gate, preferred_element_type=F32) + jnp.dot(
            flat[:, quarter:early], gate_early, preferred_element_type=F32
        )
        rows.append(r[..., early:])
        near.append(n.reshape(chips, chunk, 2 * ff))
    pay = jnp.stack([pays[0], places(1, half + 2 * top)[1]])
    rows, near, pay, gate_last, down_y = together((rows, near, pay, gate_last, down_y))

    def product(g, q):
        at = (z - order[q]) % chips
        r = lax.dynamic_index_in_dim(rows[g], at, 0, keepdims=False)
        return jnp.dot(r, gate_last, preferred_element_type=F32) + lax.dynamic_index_in_dim(
            near[g], at, 0, keepdims=False
        )

    def term(step, to):
        total = terms[0]
        for q in range(1, min(step, chips - 1)):
            total = jnp.where(order[q] == to, terms[q], total)
        return total

    right = left = 0.0
    terms, arrived, hidden, joined = [], None, None, None
    sent = product(1, 0).astype(BF)
    for step in range(chips + 2):
        k = step - 2
        work = {}
        if step < chips:
            work["part"] = swap(sent, "dp", 2)
        if step + 1 < chips:
            work["sent"] = product(1, step + 1).astype(BF)
        if arrived is not None:
            gu = product(0, step - 1) + arrived.astype(F32)
            hidden = (jax.nn.silu(gu[:, :ff]) * gu[:, ff:]).astype(BF)
            work["hidden"] = jnp.concatenate([hidden, swap(hidden, "dp", 1)])
        if joined is not None:
            out = jnp.concatenate(
                [
                    jnp.dot(joined, w, preferred_element_type=F32).astype(BF)
                    for w in (down, down_y)
                ],
                axis=1,
            ).reshape(2, 2, slots, half)
            out = jnp.concatenate([out[:, 0], swap(out[:, 1], "expert", 1)], axis=1)
            paid = lax.dynamic_index_in_dim(pay, (z - order[k]) % chips, 1, keepdims=False)
            work["term"] = jnp.einsum("gst,gsk->gtk", paid, out, preferred_element_type=F32)
        if 1 <= k < chips - 1:
            work["right"] = hop((term(k, z + chips - k) + right).astype(BF), range(k), 1)
            work["left"] = hop(
                (term(k, z - chips + k) + left).astype(BF), range(chips - k, chips), -1
            )
        work = together(work)
        sent, arrived, joined = work.get("sent"), work.get("part"), work.get("hidden")
        if "term" in work:
            terms.append(work["term"])
        if "right" in work:
            right, left = work["right"].astype(F32), work["left"].astype(F32)

    k = chips - 1
    mine = []
    upward = (term(k, z + chips - k) + right).astype(BF)
    downward = (term(k, z - chips + k) + left).astype(BF)
    for g in (1, 0):
        came = [hop(upward[g], range(k), 1), hop(downward[g], range(1, chips), -1)]
        if g == 1:
            came, upward, downward = together((came, upward, downward))
        mine.append((terms[-1][g] + came[0].astype(F32) + came[1].astype(F32)).astype(BF))

    far = swap(mine[0], "dp", 1)
    mixed = jnp.zeros(tokens.shape, BF)
    for r, piece in enumerate(
        [mine[1][:, :quarter], far[:, :quarter], mine[1][:, quarter:], far[:, quarter:]]
    ):
        mixed = lax.dynamic_update_slice_in_dim(mixed, piece, (d ^ r) * quarter, axis=1)
    return mixed


def solution(mesh):
    placed = (
        P(("dp", "expert"), None),
        P("expert", "dp", None),
        P("expert", None, "dp"),
        P(("dp", "expert"), None),
        P(("dp", "expert"), None),
    )
    short = mesh.shape["expert"] <= 8 and mesh.shape["dp"] == 4
    return jax.shard_map(
        paired if short else gathered,
        mesh=mesh,
        in_specs=placed,
        out_specs=P(("dp", "expert"), None),
        check_vma=False,
    )
```

time: 342 us -> 277 us (0.81)
  waiting for transfers between devices: 200 us -> 96 us
  local copies, waits for them, and re-layouts: 12 us -> 39.3 us
  starting transfers between devices: 59.1 us -> 74.3 us
  matrix products: 52.9 us -> 38 us
  other arithmetic: 9.9 us -> 20.8 us
    ppermute x18 -> x20, waiting for transfers between devices: 85.8 us -> 28.6 us  [hop(): lax.ppermute(value, 'expert', [(2 * i + c, 2 * (i + by) + c) for i in sou...]
    ppermute x18 -> x24, waiting for transfers between devices: 114 us -> 67.4 us  [swap(): lax.ppermute(value, axis, [(i, i ^ bit) for i in range(lax.axis_size(axis...]
    dot_general x20 -> x27, matrix products: 51 us -> 34.1 us  [the longest x8 14.6 us: product(): jnp.dot(r, gate_last, preferred_element_type=F32)]
    unnamed x13 -> x72, local copies, waits for them, and re-layouts: 3.31 us -> 13.9 us
    ppermute x18 -> x20, starting transfers between devices: 44.5 us -> 53.9 us  [hop(): lax.ppermute(value, 'expert', [(2 * i + c, 2 * (i + by) + c) for i in sou...]
    ppermute x18 -> x24, starting transfers between devices: 14.6 us -> 20.4 us  [swap(): lax.ppermute(value, axis, [(i, i ^ bit) for i in range(lax.axis_size(axis...]
    concatenate x5 -> x14, other arithmetic: 0.36 us -> 6.04 us  [the longest x1 2.55 us: paired(): down_y = jnp.concatenate(down_y)]
    another operation x26, local copies, waits for them, and re-layouts: 3.65 us -> 9.15 us  [the longest x7 5.67 us: paired(): held = jnp.stack([s[:, :half] for s in seen[g]])]
  transfers between devices with their start and end apart: 36 -> 44, of which waited for: 17 -> 20; matrix products, arithmetic and copies ran while one was open for 17% -> 26% of each run, Pallas kernels for 0% -> 0%
where the time goes in v3:
time: 277 us; the launch traced here: 276 us
  waiting for transfers between devices  96 us (35%)
  starting transfers between devices  74.3 us (27%)
  local copies, waits for them, and re-layouts  39.3 us (14%)
  matrix products  38 us (14%)
  other arithmetic  20.8 us (8%)
  between operations  7.22 us (3%)
    ppermute x24, waiting for transfers between devices, swap(): lax.ppermute(value, axis, [(i, i ^ bit) for i in range(lax.axis_size(axis...  67.4 us
    ppermute x20, starting transfers between devices, hop(): lax.ppermute(value, 'expert', [(2 * i + c, 2 * (i + by) + c) for i in sou...  53.9 us
    ppermute x20, waiting for transfers between devices, hop(): lax.ppermute(value, 'expert', [(2 * i + c, 2 * (i + by) + c) for i in sou...  28.6 us
    ppermute x24, starting transfers between devices, swap(): lax.ppermute(value, axis, [(i, i ^ bit) for i in range(lax.axis_size(axis...  20.4 us
    dot_general x8, matrix products, product(): jnp.dot(r, gate_last, preferred_element_type=F32)  14.6 us
    unnamed x72, local copies, waits for them, and re-layouts  13.9 us
    dot_general x2, matrix products, paired(): jnp.dot(flat[:, :quarter], gate, preferred_element_type=F32)  6.63 us
    dot_general x8, matrix products, paired(): jnp.dot(joined, w, preferred_element_type=F32).astype(BF)  5.92 us
  transfers between devices with their start and end apart: 44, of which 20 were waited for; matrix products, arithmetic and copies ran while one was open for 26% of the time, Pallas kernels for 0%

profile of v3, /device:TPU:0, one launch (start us, length us, event | category | flops | bytes accessed | tf_op | source)
XLA Modules:
  0.0 275.6 jit_solution(1062756471140128200)
XLA Ops:
  1.6 1.4 constant_dynamic-slice_fusion.1
  5.2 6.4 %collective-permute-start.4 = (bf16[128,1808]{1,0:T(8,128)(2,1)}, bf16[128,1808]{1,0:T(8,128)(2,1)}, u32[]{:S(2)}, u32[]{:S(2)}) collective-permute-start(bf16[128,1808]{1,0:T(8,128)(2,1)} %concatenate.66), channel_id=1, source_target_pairs={{0,2},{1,3},{2,4},{3,5},{4,6},{5,7},{8,10},{9,11},{10,12},{11,13},... | collective-permute-start | bytes 1388552 | tf_op jit(solution)/shard_map/ppermute | solution.py:81
  11.5 2.6 slice_bitcast_fusion.6
  14.1 1.9 collective-permute-start
  17.2 2.0 collective-permute-start.3
  19.2 3.1 %slice_bitcast_fusion = (bf16[256,2048]{1,0:T(8,128)(2,1)}, bf16[256,2048]{1,0:T(8,128)(2,1)}) fusion(bf16[1,896,2048]{2,1,0:T(8,128)(2,1)} %param.7), kind=kLoop, calls=%fused_computation.58 | loop fusion | bytes 4194304 | tf_op jit(solution)/shard_map/slice | solution.py:91
  22.4 1.4 slice_bitcast_fusion.4
  27.0 1.4 collective-permute-done.1
  28.4 1.7 collective-permute-start.7
  30.9 1.5 collective-permute-start.8
  34.6 5.3 %collective-permute-start.12 = (bf16[128,1824]{1,0:T(8,128)(2,1)}, bf16[128,1824]{1,0:T(8,128)(2,1)}, u32[]{:S(2)}, u32[]{:S(2)}) collective-permute-start(bf16[128,1824]{1,0:T(8,128)(2,1)} %pad_maximum_fusion.13), channel_id=1, source_target_pairs={{0,2},{1,3},{2,4},{3,5},{4,6},{5,7},{8,10},{9,11},{10,12},{11,13},... | collective-permute-start | bytes 1400840 | tf_op jit(solution)/shard_map/ppermute | solution.py:81
  43.4 6.2 %collective-permute-done.7 = bf16[512,896]{1,0:T(8,128)(2,1)} collective-permute-done((bf16[512,896]{1,0:T(8,128)(2,1)}, bf16[512,896]{1,0:T(8,128)(2,1)}, u32[]{:S(2)}, u32[]{:S(2)}) %collective-permute-start.7) | collective-permute-done | bytes 917536 | tf_op jit(solution)/shard_map/ppermute | solution.py:55
  49.6 1.5 collective-permute-start.11
  51.9 4.9 %collective-permute-done.9 = bf16[128,1808]{1,0:T(8,128)(2,1)S(1)} collective-permute-done((bf16[128,1808]{1,0:T(8,128)(2,1)}, bf16[128,1808]{1,0:T(8,128)(2,1)S(1)}, u32[]{:S(2)}, u32[]{:S(2)}) %collective-permute-start.9) | collective-permute-done | bytes 462880 | tf_op jit(solution)/shard_map/ppermute | solution.py:81
  61.4 1.5 collective-permute-start.15
  64.1 2.4 constant_dynamic-update-slice_fusion.2
  66.5 10.6 %collective-permute-done.5 = bf16[512,896]{1,0:T(8,128)(2,1)S(1)} collective-permute-done((bf16[512,896]{1,0:T(8,128)(2,1)}, bf16[512,896]{1,0:T(8,128)(2,1)S(1)}, u32[]{:S(2)}, u32[]{:S(2)}) %collective-permute-start.5) | collective-permute-done | bytes 917536 | tf_op jit(solution)/shard_map/ppermute | solution.py:55
  77.1 1.5 collective-permute-start.16
  79.3 2.1 collective-permute-done.6
  82.2 1.4 collective-permute-start.22
  85.4 1.4 collective-permute-start.20
  88.0 1.3 broadcast_select_fusion.3
  91.7 2.3 constant_dynamic-update-slice_fusion.1
  94.1 2.5 pad_maximum_fusion.4
  102.7 1.7 convolution_convert_fusion.2
  108.8 1.8 fusion.64
  110.9 4.3 %fusion.4 = f32[512,2048]{1,0:T(8,128)} fusion(f32[512,2048]{1,0:T(8,128)S(1)} %fusion.64, bf16[1,896,2048]{2,1,0:T(8,128)(2,1)S(1)} %copy-done.3, bf16[512,1792]{1,0:T(8,128)(2,1)S(1)} %bitcast.278), kind=kOutput, calls=%fused_computation.4 | convolution fusion | flops 1880096768 | bytes 12976128 | tf_op jit(solution)/shard_map/dot_general | solution.py:161
  115.3 1.8 fusion.62
  117.2 2.3 fusion.7
  119.5 2.0 copy-done.2
  122.6 1.5 collective-permute-start.23
  124.8 2.3 fusion.15
  127.1 10.1 %collective-permute-done.23 = bf16[128,2048]{1,0:T(8,128)(2,1)} collective-permute-done((bf16[128,2048]{1,0:T(8,128)(2,1)}, bf16[128,2048]{1,0:T(8,128)(2,1)}, u32[]{:S(2)}, u32[]{:S(2)}) %collective-permute-start.23) | collective-permute-done | bytes 524320 | tf_op jit(solution)/shard_map/ppermute | solution.py:55
  137.2 1.5 collective-permute-start.25
  138.8 1.7 fusion.10
  141.8 2.3 fusion.16
  144.1 4.3 %collective-permute-done.24 = bf16[128,1024]{1,0:T(8,128)(2,1)} collective-permute-done((bf16[128,1024]{1,0:T(8,128)(2,1)S(1)}, bf16[128,1024]{1,0:T(8,128)(2,1)}, u32[]{:S(2)}, u32[]{:S(2)}) %collective-permute-start.24) | collective-permute-done | bytes 262176 | tf_op jit(solution)/shard_map/ppermute | solution.py:55
  149.4 1.7 collective-permute-done.25
  151.1 1.7 fusion.11
  156.9 1.6 collective-permute-start.27
  158.5 2.3 fusion.17
  160.8 3.6 %collective-permute-done.26 = bf16[128,1024]{1,0:T(8,128)(2,1)S(1)} collective-permute-done((bf16[128,1024]{1,0:T(8,128)(2,1)S(1)}, bf16[128,1024]{1,0:T(8,128)(2,1)S(1)}, u32[]{:S(2)}, u32[]{:S(2)}) %collective-permute-start.26) | collective-permute-done | bytes 262176 | tf_op jit(solution)/shard_map/ppermute | solution.py:55
  165.2 1.5 fusion.46
  166.7 4.5 %collective-permute-done.27 = bf16[128,2048]{1,0:T(8,128)(2,1)S(1)} collective-permute-done((bf16[128,2048]{1,0:T(8,128)(2,1)}, bf16[128,2048]{1,0:T(8,128)(2,1)S(1)}, u32[]{:S(2)}, u32[]{:S(2)}) %collective-permute-start.27) | collective-permute-done | bytes 524320 | tf_op jit(solution)/shard_map/ppermute | solution.py:55
  172.2 1.7 collective-permute-start.30
  173.9 8.7 %collective-permute-start.32 = (bf16[2,128,1792]{2,1,0:T(8,128)(2,1)}, bf16[2,128,1792]{2,1,0:T(8,128)(2,1)}, u32[]{:S(2)}, u32[]{:S(2)}) collective-permute-start(bf16[2,128,1792]{2,1,0:T(8,128)(2,1)} %convert_element_type.184), channel_id=1, source_target_pairs={{0,2},{1,3},{8,10},{9,11},{16,18},{17,19},{24,26},{25,27}} | collective-permute-start | bytes 2752520 | tf_op jit(solution)/shard_map/ppermute | solution.py:81
  185.0 1.5 fusion.12
  187.4 1.5 collective-permute-start.31
  190.2 5.5 %collective-permute-done.29 = bf16[128,1024]{1,0:T(8,128)(2,1)} collective-permute-done((bf16[128,1024]{1,0:T(8,128)(2,1)S(1)}, bf16[128,1024]{1,0:T(8,128)(2,1)}, u32[]{:S(2)}, u32[]{:S(2)}) %collective-permute-start.29) | collective-permute-done | bytes 262176 | tf_op jit(solution)/shard_map/ppermute | solution.py:55
  196.7 1.5 fusion.50
  198.2 3.6 %collective-permute-done.31 = bf16[128,2048]{1,0:T(8,128)(2,1)} collective-permute-done((bf16[128,2048]{1,0:T(8,128)(2,1)}, bf16[128,2048]{1,0:T(8,128)(2,1)}, u32[]{:S(2)}, u32[]{:S(2)}) %collective-permute-start.31) | collective-permute-done | bytes 524320 | tf_op jit(solution)/shard_map/ppermute | solution.py:55
  203.2 3.2 %add_convert_fusion.2 = (bf16[2,128,1792]{2,1,0:T(8,128)(2,1)}, bf16[2,128,1792]{2,1,0:T(8,128)(2,1)}) fusion(bf16[2,128,1792]{2,1,0:T(8,128)(2,1)} %collective-permute-done.32, f32[2,128,1792]{2,1,0:T(8,128)S(1)} %fusion.50, f32[2,128,1792]{2,1,0:T(8,128)S(1)} %fusion.46, pred[]{:T(512)S(6)} %eq.157, bf16[2,128,1792]{2,1,0:T(8,128)(2,1)} %collective-permute-done.30, ...), kind=kLoop, calls=%fused_computation.45 | loop fusion | flops 3670016 | bytes 7340034 | tf_op jit(solution)/shard_map/convert_element_type | solution.py:208
  206.4 1.6 collective-permute-start.35
  207.9 4.4 %collective-permute-start.36 = (bf16[2,128,1792]{2,1,0:T(8,128)(2,1)}, bf16[2,128,1792]{2,1,0:T(8,128)(2,1)}, u32[]{:S(2)}, u32[]{:S(2)}) collective-permute-start(bf16[2,128,1792]{2,1,0:T(8,128)(2,1)} %get-tuple-element.110), channel_id=1, source_target_pairs={{0,2},{1,3},{2,4},{3,5},{8,10},{9,11},{10,12},{11,13},{16,18},{17,... | collective-permute-start | bytes 2752520 | tf_op jit(solution)/shard_map/ppermute | solution.py:81
  213.3 1.7 fusion.13
  218.2 5.8 %collective-permute-done.34 = bf16[128,1024]{1,0:T(8,128)(2,1)S(1)} collective-permute-done((bf16[128,1024]{1,0:T(8,128)(2,1)S(1)}, bf16[128,1024]{1,0:T(8,128)(2,1)S(1)}, u32[]{:S(2)}, u32[]{:S(2)}) %collective-permute-start.34) | collective-permute-done | bytes 262176 | tf_op jit(solution)/shard_map/ppermute | solution.py:55
  224.5 5.5 %collective-permute-done.36 = bf16[2,128,1792]{2,1,0:T(8,128)(2,1)} collective-permute-done((bf16[2,128,1792]{2,1,0:T(8,128)(2,1)}, bf16[2,128,1792]{2,1,0:T(8,128)(2,1)}, u32[]{:S(2)}, u32[]{:S(2)}) %collective-permute-start.36) | collective-permute-done | bytes 917536 | tf_op jit(solution)/shard_map/ppermute | solution.py:81
  232.2 2.1 add_convert_fusion
  234.3 5.1 %collective-permute-start.39 = (bf16[128,1792]{1,0:T(8,128)(2,1)S(1)}, bf16[128,1792]{1,0:T(8,128)(2,1)S(1)}, u32[]{:S(2)}, u32[]{:S(2)}) collective-permute-start(bf16[128,1792]{1,0:T(8,128)(2,1)S(1)} %slice_bitcast_fusion.10), channel_id=1, source_target_pairs={{0,2},{1,3},{2,4},{3,5},{4,6},{5,7},{8,10},{9,11},{10,12},{11,13},... | collective-permute-start | bytes 1376264 | tf_op jit(solution)/shard_map/ppermute | solution.py:81
  241.0 5.9 %collective-permute-done.39 = bf16[128,1792]{1,0:T(8,128)(2,1)S(1)} collective-permute-done((bf16[128,1792]{1,0:T(8,128)(2,1)S(1)}, bf16[128,1792]{1,0:T(8,128)(2,1)S(1)}, u32[]{:S(2)}, u32[]{:S(2)}) %collective-permute-start.39) | collective-permute-done | bytes 458784 | tf_op jit(solution)/shard_map/ppermute | solution.py:81
  247.0 5.3 %collective-permute-done.40 = bf16[128,1792]{1,0:T(8,128)(2,1)S(1)} collective-permute-done((bf16[128,1792]{1,0:T(8,128)(2,1)S(1)}, bf16[128,1792]{1,0:T(8,128)(2,1)S(1)}, u32[]{:S(2)}, u32[]{:S(2)}) %collective-permute-start.40) | collective-permute-done | bytes 458784 | tf_op jit(solution)/shard_map/ppermute | solution.py:81
  253.7 4.6 %collective-permute-start.41 = (bf16[128,1792]{1,0:T(8,128)(2,1)S(1)}, bf16[128,1792]{1,0:T(8,128)(2,1)S(1)}, u32[]{:S(2)}, u32[]{:S(2)}) collective-permute-start(bf16[128,1792]{1,0:T(8,128)(2,1)S(1)} %slice_bitcast_fusion.26), channel_id=1, source_target_pairs={{0,2},{1,3},{2,4},{3,5},{4,6},{5,7},{8,10},{9,11},{10,12},{11,13},... | collective-permute-start | bytes 1376264 | tf_op jit(solution)/shard_map/ppermute | solution.py:81
  258.7 5.0 %collective-permute-done.42 = bf16[128,1792]{1,0:T(8,128)(2,1)S(1)} collective-permute-done((bf16[128,1792]{1,0:T(8,128)(2,1)S(1)}, bf16[128,1792]{1,0:T(8,128)(2,1)S(1)}, u32[]{:S(2)}, u32[]{:S(2)}) %collective-permute-start.42) | collective-permute-done | bytes 458784 | tf_op jit(solution)/shard_map/ppermute | solution.py:81
  266.0 7.9 %collective-permute-done.43 = bf16[128,1792]{1,0:T(8,128)(2,1)S(1)} collective-permute-done((bf16[128,1792]{1,0:T(8,128)(2,1)S(1)}, bf16[128,1792]{1,0:T(8,128)(2,1)S(1)}, u32[]{:S(2)}, u32[]{:S(2)}) %collective-permute-start.43) | collective-permute-done | bytes 458784 | tf_op jit(solution)/shard_map/ppermute | solution.py:55
  (224 shorter events, 63.5 us)
Async XLA Ops:
  3.9 27.0 %collective-permute-start.2 = (bf16[128,1808]{1,0:T(8,128)(2,1)}, bf16[128,1808]{1,0:T(8,128)(2,1)}, u32[]{:S(2)}, u32[]{:S(2)}) collective-permute-start(bf16[128,1808]{1,0:T(8,128)(2,1)} %concatenate.66), channel_id=1, source_target_pairs={{2,0},{3,1},{4,2},{5,3},{6,4},{7,5},{10,8},{11,9},{12,10},{13,11},... | collective-permute-start | bytes 1388552 | tf_op jit(solution)/shard_map/ppermute | solution.py:81
  5.2 27.2 %collective-permute-start.4 = (bf16[128,1808]{1,0:T(8,128)(2,1)}, bf16[128,1808]{1,0:T(8,128)(2,1)}, u32[]{:S(2)}, u32[]{:S(2)}) collective-permute-start(bf16[128,1808]{1,0:T(8,128)(2,1)} %concatenate.66), channel_id=1, source_target_pairs={{0,2},{1,3},{2,4},{3,5},{4,6},{5,7},{8,10},{9,11},{10,12},{11,13},... | collective-permute-start | bytes 1388552 | tf_op jit(solution)/shard_map/ppermute | solution.py:81
  14.1 18.3 %collective-permute-start = (bf16[128,2048]{1,0:T(8,128)(2,1)}, bf16[128,2048]{1,0:T(8,128)(2,1)S(1)}, u32[]{:S(2)}, u32[]{:S(2)}) collective-permute-start(bf16[128,2048]{1,0:T(8,128)(2,1)} %get-tuple-element.114), channel_id=1, source_target_pairs={{0,8},{8,0},{16,24},{24,16},{1,9},{9,1},{17,25},{25,17},{2,10},{10... | collective-permute-start | bytes 1572872 | tf_op jit(solution)/shard_map/ppermute | solution.py:55
  16.1 12.3 %collective-permute-start.1 = (bf16[128,16]{1,0:T(8,128)(2,1)S(1)}, bf16[128,16]{1,0:T(8,128)(2,1)S(1)}, u32[]{:S(2)}, u32[]{:S(2)}) collective-permute-start(bf16[128,16]{1,0:T(8,128)(2,1)S(1)} %pad_maximum_fusion.19), channel_id=1, source_target_pairs={{0,8},{8,0},{16,24},{24,16},{1,9},{9,1},{17,25},{25,17},{2,10},{10... | collective-permute-start | bytes 12296 | tf_op jit(solution)/shard_map/ppermute | solution.py:55
  17.2 5.2 %copy-start.4 = (bf16[1,1024,896]{2,1,0:T(8,128)(2,1)S(1)}, bf16[1,1024,896]{2,1,0:T(8,128)(2,1)}, u32[]{:S(2)}) copy-start(bf16[1,1024,896]{2,1,0:T(8,128)(2,1)} %param.8) | copy-start | bytes 5505028
  17.2 15.2 %collective-permute-start.3 = (bf16[128,1808]{1,0:T(8,128)(2,1)}, bf16[128,1808]{1,0:T(8,128)(2,1)S(1)}, u32[]{:S(2)}, u32[]{:S(2)}) collective-permute-start(bf16[128,1808]{1,0:T(8,128)(2,1)} %concatenate.67), channel_id=1, source_target_pairs={{0,16},{8,24},{16,0},{24,8},{1,17},{9,25},{17,1},{25,9},{2,18},{10... | collective-permute-start | bytes 1388552 | tf_op jit(solution)/shard_map/ppermute | solution.py:55
  28.4 21.2 %collective-permute-start.7 = (bf16[512,896]{1,0:T(8,128)(2,1)}, bf16[512,896]{1,0:T(8,128)(2,1)}, u32[]{:S(2)}, u32[]{:S(2)}) collective-permute-start(bf16[512,896]{1,0:T(8,128)(2,1)} %get-tuple-element.119), channel_id=1, source_target_pairs={{0,16},{8,24},{16,0},{24,8},{1,17},{9,25},{17,1},{25,9},{2,18},{10... | collective-permute-start | bytes 2752520 | tf_op jit(solution)/shard_map/ppermute | solution.py:55
  30.9 27.9 %collective-permute-start.8 = (bf16[256,2048]{1,0:T(8,128)(2,1)}, bf16[256,2048]{1,0:T(8,128)(2,1)}, u32[]{:S(2)}, u32[]{:S(2)}) collective-permute-start(bf16[256,2048]{1,0:T(8,128)(2,1)} %get-tuple-element.115), channel_id=1, source_target_pairs={{0,8},{8,0},{16,24},{24,16},{1,9},{9,1},{17,25},{25,17},{2,10},{10... | collective-permute-start | bytes 3145736 | tf_op jit(solution)/shard_map/ppermute | solution.py:55
  33.3 25.5 %collective-permute-start.10 = (bf16[128,1824]{1,0:T(8,128)(2,1)}, bf16[128,1824]{1,0:T(8,128)(2,1)}, u32[]{:S(2)}, u32[]{:S(2)}) collective-permute-start(bf16[128,1824]{1,0:T(8,128)(2,1)} %pad_maximum_fusion.13), channel_id=1, source_target_pairs={{2,0},{3,1},{4,2},{5,3},{6,4},{7,5},{10,8},{11,9},{12,10},{13,11},... | collective-permute-start | bytes 1400840 | tf_op jit(solution)/shard_map/ppermute | solution.py:81
  34.6 24.2 %collective-permute-start.12 = (bf16[128,1824]{1,0:T(8,128)(2,1)}, bf16[128,1824]{1,0:T(8,128)(2,1)}, u32[]{:S(2)}, u32[]{:S(2)}) collective-permute-start(bf16[128,1824]{1,0:T(8,128)(2,1)} %pad_maximum_fusion.13), channel_id=1, source_target_pairs={{0,2},{1,3},{2,4},{3,5},{4,6},{5,7},{8,10},{9,11},{10,12},{11,13},... | collective-permute-start | bytes 1400840 | tf_op jit(solution)/shard_map/ppermute | solution.py:81
  39.9 16.9 %collective-permute-start.9 = (bf16[128,1808]{1,0:T(8,128)(2,1)}, bf16[128,1808]{1,0:T(8,128)(2,1)S(1)}, u32[]{:S(2)}, u32[]{:S(2)}) collective-permute-start(bf16[128,1808]{1,0:T(8,128)(2,1)} %collective-permute-done.2), channel_id=1, source_target_pairs={{2,0},{3,1},{4,2},{5,3},{10,8},{11,9},{12,10},{13,11},{18,16},{19,... | collective-permute-start | bytes 1388552 | tf_op jit(solution)/shard_map/ppermute | solution.py:81
  49.6 8.5 %collective-permute-start.11 = (bf16[128,1808]{1,0:T(8,128)(2,1)}, bf16[128,1808]{1,0:T(8,128)(2,1)}, u32[]{:S(2)}, u32[]{:S(2)}) collective-permute-start(bf16[128,1808]{1,0:T(8,128)(2,1)} %collective-permute-done.4), channel_id=1, source_target_pairs={{2,4},{3,5},{4,6},{5,7},{10,12},{11,13},{12,14},{13,15},{18,20},{1... | collective-permute-start | bytes 1388552 | tf_op jit(solution)/shard_map/ppermute | solution.py:81
  57.6 19.4 %collective-permute-start.5 = (bf16[512,896]{1,0:T(8,128)(2,1)}, bf16[512,896]{1,0:T(8,128)(2,1)S(1)}, u32[]{:S(2)}, u32[]{:S(2)}) collective-permute-start(bf16[512,896]{1,0:T(8,128)(2,1)} %get-tuple-element.120), channel_id=1, source_target_pairs={{0,16},{8,24},{16,0},{24,8},{1,17},{9,25},{17,1},{25,9},{2,18},{10... | collective-permute-start | bytes 2752520 | tf_op jit(solution)/shard_map/ppermute | solution.py:55
  58.2 23.3 %collective-permute-start.6 = (bf16[256,2048]{1,0:T(8,128)(2,1)}, bf16[256,2048]{1,0:T(8,128)(2,1)}, u32[]{:S(2)}, u32[]{:S(2)}) collective-permute-start(bf16[256,2048]{1,0:T(8,128)(2,1)} %get-tuple-element.116), channel_id=1, source_target_pairs={{0,8},{8,0},{16,24},{24,16},{1,9},{9,1},{17,25},{25,17},{2,10},{10... | collective-permute-start | bytes 3145736 | tf_op jit(solution)/shard_map/ppermute | solution.py:55
  58.8 23.3 %collective-permute-start.13 = (bf16[128,1808]{1,0:T(8,128)(2,1)}, bf16[128,1808]{1,0:T(8,128)(2,1)}, u32[]{:S(2)}, u32[]{:S(2)}) collective-permute-start(bf16[128,1808]{1,0:T(8,128)(2,1)} %copy-done.15), channel_id=1, source_target_pairs={{2,0},{3,1},{10,8},{11,9},{18,16},{19,17},{26,24},{27,25}} | collective-permute-start | bytes 1388552 | tf_op jit(solution)/shard_map/ppermute | solution.py:81
  60.1 24.0 %collective-permute-start.14 = (bf16[128,1824]{1,0:T(8,128)(2,1)}, bf16[128,1824]{1,0:T(8,128)(2,1)}, u32[]{:S(2)}, u32[]{:S(2)}) collective-permute-start(bf16[128,1824]{1,0:T(8,128)(2,1)} %collective-permute-done.10), channel_id=1, source_target_pairs={{2,0},{3,1},{4,2},{5,3},{10,8},{11,9},{12,10},{13,11},{18,16},{19,... | collective-permute-start | bytes 1400840 | tf_op jit(solution)/shard_map/ppermute | solution.py:81
  61.4 22.1 %collective-permute-start.15 = (bf16[128,1808]{1,0:T(8,128)(2,1)}, bf16[128,1808]{1,0:T(8,128)(2,1)}, u32[]{:S(2)}, u32[]{:S(2)}) collective-permute-start(bf16[128,1808]{1,0:T(8,128)(2,1)} %collective-permute-done.11), channel_id=1, source_target_pairs={{4,6},{5,7},{12,14},{13,15},{20,22},{21,23},{28,30},{29,31}} | collective-permute-start | bytes 1388552 | tf_op jit(solution)/shard_map/ppermute | solution.py:81
  77.1 8.3 %copy-start.12 = (bf16[512,896]{1,0:T(8,128)(2,1)}, bf16[512,896]{1,0:T(8,128)(2,1)S(1)}, u32[]{:S(2)}) copy-start(bf16[512,896]{1,0:T(8,128)(2,1)S(1)} %collective-permute-done.5) | copy-start | bytes 2752516
  77.1 7.0 %collective-permute-start.16 = (bf16[128,1824]{1,0:T(8,128)(2,1)}, bf16[128,1824]{1,0:T(8,128)(2,1)}, u32[]{:S(2)}, u32[]{:S(2)}) collective-permute-start(bf16[128,1824]{1,0:T(8,128)(2,1)} %collective-permute-done.12), channel_id=1, source_target_pairs={{2,4},{3,5},{4,6},{5,7},{10,12},{11,13},{12,14},{13,15},{18,20},{1... | collective-permute-start | bytes 1400840 | tf_op jit(solution)/shard_map/ppermute | solution.py:81
  81.5 17.3 %collective-permute-start.18 = (bf16[128,2048]{1,0:T(8,128)(2,1)}, bf16[128,2048]{1,0:T(8,128)(2,1)}, u32[]{:S(2)}, u32[]{:S(2)}) collective-permute-start(bf16[128,2048]{1,0:T(8,128)(2,1)} %get-tuple-element.113), channel_id=1, source_target_pairs={{0,8},{8,0},{16,24},{24,16},{1,9},{9,1},{17,25},{25,17},{2,10},{10... | collective-permute-start | bytes 1572872 | tf_op jit(solution)/shard_map/ppermute | solution.py:55
  82.2 37.4 %collective-permute-start.22 = (bf16[128,2048]{1,0:T(8,128)(2,1)}, bf16[128,2048]{1,0:T(8,128)(2,1)S(1)}, u32[]{:S(2)}, u32[]{:S(2)}) collective-permute-start(bf16[128,2048]{1,0:T(8,128)(2,1)} %get-tuple-element.112), channel_id=1, source_target_pairs={{0,8},{8,0},{16,24},{24,16},{1,9},{9,1},{17,25},{25,17},{2,10},{10... | collective-permute-start | bytes 1572872 | tf_op jit(solution)/shard_map/ppermute | solution.py:55
  84.1 14.7 %collective-permute-start.19 = (bf16[128,1824]{1,0:T(8,128)(2,1)}, bf16[128,1824]{1,0:T(8,128)(2,1)}, u32[]{:S(2)}, u32[]{:S(2)}) collective-permute-start(bf16[128,1824]{1,0:T(8,128)(2,1)} %collective-permute-done.14), channel_id=1, source_target_pairs={{2,0},{3,1},{10,8},{11,9},{18,16},{19,17},{26,24},{27,25}} | collective-permute-start | bytes 1400840 | tf_op jit(solution)/shard_map/ppermute | solution.py:81
  85.4 13.4 %collective-permute-start.20 = (bf16[128,1824]{1,0:T(8,128)(2,1)}, bf16[128,1824]{1,0:T(8,128)(2,1)}, u32[]{:S(2)}, u32[]{:S(2)}) collective-permute-start(bf16[128,1824]{1,0:T(8,128)(2,1)} %collective-permute-done.16), channel_id=1, source_target_pairs={{4,6},{5,7},{12,14},{13,15},{20,22},{21,23},{28,30},{29,31}} | collective-permute-start | bytes 1400840 | tf_op jit(solution)/shard_map/ppermute | solution.py:81
  91.1 3.0 %copy-start.13 = (bf16[512,896]{1,0:T(8,128)(2,1)S(1)}, bf16[512,896]{1,0:T(8,128)(2,1)}, u32[]{:S(2)}) copy-start(bf16[512,896]{1,0:T(8,128)(2,1)} %copy-done.12) | copy-start | bytes 2752516
  98.8 3.3 %copy-start.28 = (bf16[1,128,16]{1,2,0:T(8,128)(2,1)S(1)}, bf16[1,128,16]{1,2,0:T(8,128)(2,1)}, u32[]{:S(2)}) copy-start(bf16[1,128,16]{1,2,0:T(8,128)(2,1)} %copy.88) | copy-start | bytes 12292
  98.8 3.3 %copy-start.30 = (bf16[1,128,16]{1,2,0:T(8,128)(2,1)S(1)}, bf16[1,128,16]{1,2,0:T(8,128)(2,1)}, u32[]{:S(2)}) copy-start(bf16[1,128,16]{1,2,0:T(8,128)(2,1)} %copy.90) | copy-start | bytes 12292
  100.1 2.2 copy-start.27
  100.2 2.2 copy-start.29
  100.2 2.2 copy-start.31
  100.2 2.5 copy-start.16
  100.2 2.5 copy-start.18
  104.5 4.2 %collective-permute-start.17 = (bf16[4,64,1792]{2,1,0:T(8,128)(2,1)S(1)}, bf16[4,64,1792]{2,1,0:T(8,128)(2,1)S(1)}, u32[]{:S(2)}, u32[]{:S(2)}) collective-permute-start(bf16[4,64,1792]{2,1,0:T(8,128)(2,1)S(1)} %convolution_convert_fusion.2), channel_id=1, source_target_pairs={{0,1},{1,0},{2,3},{3,2},{4,5},{5,4},{6,7},{7,6},{8,9},{9,8},{10,11... | collective-permute-start | bytes 2752520 | tf_op jit(solution)/shard_map/ppermute | solution.py:55
  105.2 2.5 copy-start.19
  105.3 2.5 copy-start.20
  105.3 9.9 %collective-permute-start.21 = (bf16[4,64,1792]{2,1,0:T(8,128)(2,1)S(1)}, bf16[4,64,1792]{2,1,0:T(8,128)(2,1)S(1)}, u32[]{:S(2)}, u32[]{:S(2)}) collective-permute-start(bf16[4,64,1792]{2,1,0:T(8,128)(2,1)S(1)} %convolution_convert_fusion), channel_id=1, source_target_pairs={{0,1},{1,0},{2,3},{3,2},{4,5},{5,4},{6,7},{7,6},{8,9},{9,8},{10,11... | collective-permute-start | bytes 2752520 | tf_op jit(solution)/shard_map/ppermute | solution.py:55
  108.8 2.0 copy-start.3
  122.6 14.6 %collective-permute-start.23 = (bf16[128,2048]{1,0:T(8,128)(2,1)}, bf16[128,2048]{1,0:T(8,128)(2,1)}, u32[]{:S(2)}, u32[]{:S(2)}) collective-permute-start(bf16[128,2048]{1,0:T(8,128)(2,1)} %fusion.14), channel_id=1, source_target_pairs={{0,16},{8,24},{16,0},{24,8},{1,17},{9,25},{17,1},{25,9},{2,18},{10... | collective-permute-start | bytes 1572872 | tf_op jit(solution)/shard_map/ppermute | solution.py:55
  137.2 13.9 %collective-permute-start.25 = (bf16[128,2048]{1,0:T(8,128)(2,1)}, bf16[128,2048]{1,0:T(8,128)(2,1)}, u32[]{:S(2)}, u32[]{:S(2)}) collective-permute-start(bf16[128,2048]{1,0:T(8,128)(2,1)} %fusion.15), channel_id=1, source_target_pairs={{0,16},{8,24},{16,0},{24,8},{1,17},{9,25},{17,1},{25,9},{2,18},{10... | collective-permute-start | bytes 1572872 | tf_op jit(solution)/shard_map/ppermute | solution.py:55
  140.6 7.8 %collective-permute-start.24 = (bf16[128,1024]{1,0:T(8,128)(2,1)S(1)}, bf16[128,1024]{1,0:T(8,128)(2,1)}, u32[]{:S(2)}, u32[]{:S(2)}) collective-permute-start(bf16[128,1024]{1,0:T(8,128)(2,1)S(1)} %fusion.69), channel_id=1, source_target_pairs={{0,8},{8,0},{16,24},{24,16},{1,9},{9,1},{17,25},{25,17},{2,10},{10... | collective-permute-start | bytes 786440 | tf_op jit(solution)/shard_map/ppermute | solution.py:55
  155.4 9.0 %collective-permute-start.28 = (bf16[2,64,1792]{2,1,0:T(8,128)(2,1)S(1)}, bf16[2,64,1792]{2,1,0:T(8,128)(2,1)S(1)}, u32[]{:S(2)}, u32[]{:S(2)}) collective-permute-start(bf16[2,64,1792]{2,1,0:T(8,128)(2,1)S(1)} %get-tuple-element.128), channel_id=1, source_target_pairs={{0,1},{1,0},{2,3},{3,2},{4,5},{5,4},{6,7},{7,6},{8,9},{9,8},{10,11... | collective-permute-start | bytes 1376264 | tf_op jit(solution)/shard_map/ppermute | solution.py:55
  155.6 8.8 %collective-permute-start.26 = (bf16[128,1024]{1,0:T(8,128)(2,1)S(1)}, bf16[128,1024]{1,0:T(8,128)(2,1)S(1)}, u32[]{:S(2)}, u32[]{:S(2)}) collective-permute-start(bf16[128,1024]{1,0:T(8,128)(2,1)S(1)} %fusion.68), channel_id=1, source_target_pairs={{0,8},{8,0},{16,24},{24,16},{1,9},{9,1},{17,25},{25,17},{2,10},{10... | collective-permute-start | bytes 786440 | tf_op jit(solution)/shard_map/ppermute | solution.py:55
  156.9 14.3 %collective-permute-start.27 = (bf16[128,2048]{1,0:T(8,128)(2,1)}, bf16[128,2048]{1,0:T(8,128)(2,1)S(1)}, u32[]{:S(2)}, u32[]{:S(2)}) collective-permute-start(bf16[128,2048]{1,0:T(8,128)(2,1)} %fusion.16), channel_id=1, source_target_pairs={{0,16},{8,24},{16,0},{24,8},{1,17},{9,25},{17,1},{25,9},{2,18},{10... | collective-permute-start | bytes 1572872 | tf_op jit(solution)/shard_map/ppermute | solution.py:55
  166.7 15.9 %copy-start.9 = (bf16[1024,896]{1,0:T(8,128)(2,1)S(1)}, bf16[1024,896]{1,0:T(8,128)(2,1)}, u32[]{:S(2)}) copy-start(bf16[1024,896]{1,0:T(8,128)(2,1)} %pad_maximum_fusion.4) | copy-start | bytes 5505028
  172.2 11.1 %copy-start.5 = (bf16[1,1024,896]{2,1,0:T(8,128)(2,1)S(1)}, bf16[1,1024,896]{2,1,0:T(8,128)(2,1)}, u32[]{:S(2)}) copy-start(bf16[1,1024,896]{2,1,0:T(8,128)(2,1)} %param.8) | copy-start | bytes 5505028
  172.2 29.5 %collective-permute-start.30 = (bf16[2,128,1792]{2,1,0:T(8,128)(2,1)}, bf16[2,128,1792]{2,1,0:T(8,128)(2,1)}, u32[]{:S(2)}, u32[]{:S(2)}) collective-permute-start(bf16[2,128,1792]{2,1,0:T(8,128)(2,1)} %convert_element_type.184), channel_id=1, source_target_pairs={{6,4},{7,5},{14,12},{15,13},{22,20},{23,21},{30,28},{31,29}} | collective-permute-start | bytes 2752520 | tf_op jit(solution)/shard_map/ppermute | solution.py:81
  173.9 27.8 %collective-permute-start.32 = (bf16[2,128,1792]{2,1,0:T(8,128)(2,1)}, bf16[2,128,1792]{2,1,0:T(8,128)(2,1)}, u32[]{:S(2)}, u32[]{:S(2)}) collective-permute-start(bf16[2,128,1792]{2,1,0:T(8,128)(2,1)} %convert_element_type.184), channel_id=1, source_target_pairs={{0,2},{1,3},{8,10},{9,11},{16,18},{17,19},{24,26},{25,27}} | collective-permute-start | bytes 2752520 | tf_op jit(solution)/shard_map/ppermute | solution.py:81
  186.6 10.1 %collective-permute-start.33 = (bf16[2,64,1792]{2,1,0:T(8,128)(2,1)}, bf16[2,64,1792]{2,1,0:T(8,128)(2,1)}, u32[]{:S(2)}, u32[]{:S(2)}) collective-permute-start(bf16[2,64,1792]{2,1,0:T(8,128)(2,1)} %get-tuple-element.126), channel_id=1, source_target_pairs={{0,1},{1,0},{2,3},{3,2},{4,5},{5,4},{6,7},{7,6},{8,9},{9,8},{10,11... | collective-permute-start | bytes 1376264 | tf_op jit(solution)/shard_map/ppermute | solution.py:55
  186.8 8.9 %collective-permute-start.29 = (bf16[128,1024]{1,0:T(8,128)(2,1)S(1)}, bf16[128,1024]{1,0:T(8,128)(2,1)}, u32[]{:S(2)}, u32[]{:S(2)}) collective-permute-start(bf16[128,1024]{1,0:T(8,128)(2,1)S(1)} %fusion.67), channel_id=1, source_target_pairs={{0,8},{8,0},{16,24},{24,16},{1,9},{9,1},{17,25},{25,17},{2,10},{10... | collective-permute-start | bytes 786440 | tf_op jit(solution)/shard_map/ppermute | solution.py:55
  187.4 14.4 %collective-permute-start.31 = (bf16[128,2048]{1,0:T(8,128)(2,1)}, bf16[128,2048]{1,0:T(8,128)(2,1)}, u32[]{:S(2)}, u32[]{:S(2)}) collective-permute-start(bf16[128,2048]{1,0:T(8,128)(2,1)} %fusion.17), channel_id=1, source_target_pairs={{0,16},{8,24},{16,0},{24,8},{1,17},{9,25},{17,1},{25,9},{2,18},{10... | collective-permute-start | bytes 1572872 | tf_op jit(solution)/shard_map/ppermute | solution.py:55
  190.2 11.6 %copy-start.10 = (bf16[1024,896]{1,0:T(8,128)(2,1)S(1)}, bf16[1024,896]{1,0:T(8,128)(2,1)}, u32[]{:S(2)}) copy-start(bf16[1024,896]{1,0:T(8,128)(2,1)} %pad_maximum_fusion.4) | copy-start | bytes 5505028
  198.1 5.1 %copy-start = (f32[2,128,1792]{2,1,0:T(8,128)}, f32[2,128,1792]{2,1,0:T(8,128)S(1)}, u32[]{:S(2)}) copy-start(f32[2,128,1792]{2,1,0:T(8,128)S(1)} %fusion.50) | copy-start | bytes 5505028
  198.2 4.3 %copy-start.6 = (bf16[1,1024,896]{2,1,0:T(8,128)(2,1)S(1)}, bf16[1,1024,896]{2,1,0:T(8,128)(2,1)}, u32[]{:S(2)}) copy-start(bf16[1,1024,896]{2,1,0:T(8,128)(2,1)} %param.8) | copy-start | bytes 5505028
  206.4 18.1 %collective-permute-start.35 = (bf16[2,128,1792]{2,1,0:T(8,128)(2,1)}, bf16[2,128,1792]{2,1,0:T(8,128)(2,1)}, u32[]{:S(2)}, u32[]{:S(2)}) collective-permute-start(bf16[2,128,1792]{2,1,0:T(8,128)(2,1)} %get-tuple-element.111), channel_id=1, source_target_pairs={{4,2},{5,3},{6,4},{7,5},{12,10},{13,11},{14,12},{15,13},{20,18},{2... | collective-permute-start | bytes 2752520 | tf_op jit(solution)/shard_map/ppermute | solution.py:81
  207.9 22.0 %collective-permute-start.36 = (bf16[2,128,1792]{2,1,0:T(8,128)(2,1)}, bf16[2,128,1792]{2,1,0:T(8,128)(2,1)}, u32[]{:S(2)}, u32[]{:S(2)}) collective-permute-start(bf16[2,128,1792]{2,1,0:T(8,128)(2,1)} %get-tuple-element.110), channel_id=1, source_target_pairs={{0,2},{1,3},{2,4},{3,5},{8,10},{9,11},{10,12},{11,13},{16,18},{17,... | collective-permute-start | bytes 2752520 | tf_op jit(solution)/shard_map/ppermute | solution.py:81
  215.0 9.0 %collective-permute-start.37 = (bf16[2,64,1792]{2,1,0:T(8,128)(2,1)}, bf16[2,64,1792]{2,1,0:T(8,128)(2,1)S(1)}, u32[]{:S(2)}, u32[]{:S(2)}) collective-permute-start(bf16[2,64,1792]{2,1,0:T(8,128)(2,1)} %get-tuple-element.124), channel_id=1, source_target_pairs={{0,1},{1,0},{2,3},{3,2},{4,5},{5,4},{6,7},{7,6},{8,9},{9,8},{10,11... | collective-permute-start | bytes 1376264 | tf_op jit(solution)/shard_map/ppermute | solution.py:55
  215.2 8.8 %collective-permute-start.34 = (bf16[128,1024]{1,0:T(8,128)(2,1)S(1)}, bf16[128,1024]{1,0:T(8,128)(2,1)S(1)}, u32[]{:S(2)}, u32[]{:S(2)}) collective-permute-start(bf16[128,1024]{1,0:T(8,128)(2,1)S(1)} %fusion.66), channel_id=1, source_target_pairs={{0,8},{8,0},{16,24},{24,16},{1,9},{9,1},{17,25},{25,17},{2,10},{10... | collective-permute-start | bytes 786440 | tf_op jit(solution)/shard_map/ppermute | solution.py:55
  218.2 11.8 %copy-start.11 = (bf16[1024,896]{1,0:T(8,128)(2,1)S(1)}, bf16[1024,896]{1,0:T(8,128)(2,1)}, u32[]{:S(2)}) copy-start(bf16[1024,896]{1,0:T(8,128)(2,1)} %pad_maximum_fusion.4) | copy-start | bytes 5505028
  224.5 6.2 %copy-start.7 = (bf16[1,1024,896]{2,1,0:T(8,128)(2,1)S(1)}, bf16[1,1024,896]{2,1,0:T(8,128)(2,1)}, u32[]{:S(2)}) copy-start(bf16[1,1024,896]{2,1,0:T(8,128)(2,1)} %param.8) | copy-start | bytes 5505028
  234.3 12.6 %collective-permute-start.39 = (bf16[128,1792]{1,0:T(8,128)(2,1)S(1)}, bf16[128,1792]{1,0:T(8,128)(2,1)S(1)}, u32[]{:S(2)}, u32[]{:S(2)}) collective-permute-start(bf16[128,1792]{1,0:T(8,128)(2,1)S(1)} %slice_bitcast_fusion.10), channel_id=1, source_target_pairs={{0,2},{1,3},{2,4},{3,5},{4,6},{5,7},{8,10},{9,11},{10,12},{11,13},... | collective-permute-start | bytes 1376264 | tf_op jit(solution)/shard_map/ppermute | solution.py:81
  239.5 12.8 %collective-permute-start.40 = (bf16[128,1792]{1,0:T(8,128)(2,1)S(1)}, bf16[128,1792]{1,0:T(8,128)(2,1)S(1)}, u32[]{:S(2)}, u32[]{:S(2)}) collective-permute-start(bf16[128,1792]{1,0:T(8,128)(2,1)S(1)} %slice_bitcast_fusion.9), channel_id=1, source_target_pairs={{2,0},{3,1},{4,2},{5,3},{6,4},{7,5},{10,8},{11,9},{12,10},{13,11},... | collective-permute-start | bytes 1376264 | tf_op jit(solution)/shard_map/ppermute | solution.py:81
  241.0 17.3 %collective-permute-start.38 = (bf16[2,64,1792]{2,1,0:T(8,128)(2,1)S(1)}, bf16[2,64,1792]{2,1,0:T(8,128)(2,1)S(1)}, u32[]{:S(2)}, u32[]{:S(2)}) collective-permute-start(bf16[2,64,1792]{2,1,0:T(8,128)(2,1)S(1)} %get-tuple-element.122), channel_id=1, source_target_pairs={{0,1},{1,0},{2,3},{3,2},{4,5},{5,4},{6,7},{7,6},{8,9},{9,8},{10,11... | collective-permute-start | bytes 1376264 | tf_op jit(solution)/shard_map/ppermute | solution.py:55
  252.3 11.4 %collective-permute-start.42 = (bf16[128,1792]{1,0:T(8,128)(2,1)S(1)}, bf16[128,1792]{1,0:T(8,128)(2,1)S(1)}, u32[]{:S(2)}, u32[]{:S(2)}) collective-permute-start(bf16[128,1792]{1,0:T(8,128)(2,1)S(1)} %slice_bitcast_fusion.25), channel_id=1, source_target_pairs={{2,0},{3,1},{4,2},{5,3},{6,4},{7,5},{10,8},{11,9},{12,10},{13,11},... | collective-permute-start | bytes 1376264 | tf_op jit(solution)/shard_map/ppermute | solution.py:81
  253.7 11.3 %collective-permute-start.41 = (bf16[128,1792]{1,0:T(8,128)(2,1)S(1)}, bf16[128,1792]{1,0:T(8,128)(2,1)S(1)}, u32[]{:S(2)}, u32[]{:S(2)}) collective-permute-start(bf16[128,1792]{1,0:T(8,128)(2,1)S(1)} %slice_bitcast_fusion.26), channel_id=1, source_target_pairs={{0,2},{1,3},{2,4},{3,5},{4,6},{5,7},{8,10},{9,11},{10,12},{11,13},... | collective-permute-start | bytes 1376264 | tf_op jit(solution)/shard_map/ppermute | solution.py:81
  265.3 8.5 %collective-permute-start.43 = (bf16[128,1792]{1,0:T(8,128)(2,1)S(1)}, bf16[128,1792]{1,0:T(8,128)(2,1)S(1)}, u32[]{:S(2)}, u32[]{:S(2)}) collective-permute-start(bf16[128,1792]{1,0:T(8,128)(2,1)S(1)} %get-tuple-element.117), channel_id=1, source_target_pairs={{0,8},{8,0},{16,24},{24,16},{1,9},{9,1},{17,25},{25,17},{2,10},{10... | collective-permute-start | bytes 1376264 | tf_op jit(solution)/shard_map/ppermute | solution.py:55
  (13 other events, 20.2 us)

commit v4 on v3

--- a/solution.py
+++ b/solution.py
@@ -83,23 +83,29 @@
         )
 
     together = lax.optimization_barrier
-    parts = [
-        lax.dynamic_slice_in_dim(tokens, (d ^ r) * quarter, quarter, axis=1) for r in range(4)
-    ]
+
+    def depths(r):
+        return lax.dynamic_slice_in_dim(tokens, (d ^ r) * quarter, quarter, axis=1)
+
     info = jnp.concatenate([expert_ids.astype(BF), gate_weights], axis=1)
-    first = jnp.concatenate([parts[0], parts[1], info], axis=1)
-    gates = [gate[quarter * lo // 7 : quarter * hi // 7] for lo, hi in CUTS]
-    downs = jnp.split(down, 2)
+    pair = jnp.concatenate([depths(2), depths(3), info], axis=1)
+    pair, tokens, info, gate, down = together((pair, tokens, info, gate, down))
+    first = jnp.concatenate([depths(0), depths(1), info], axis=1)
+
+    def piece(step):
+        lo, hi = CUTS[step]
+        return gate[quarter * lo // 7 : quarter * hi // 7]
 
     rights, lefts, down_y, gate_x = [{}, {}], [{}, {}], [], []
     own = [first, None]
+    ahead = {"gate": piece(0)}
     for step in range(chips):
-        work = {"gate": swap(gates[step], "dp", 1)}
+        work = {"gate": swap(ahead["gate"], "dp", 1)}
         if step == 0:
             work["info"] = swap(info, "dp", 1)
-            work["pair"] = swap(jnp.concatenate([parts[2], parts[3], info], axis=1), "dp", 2)
+            work["pair"] = swap(pair, "dp", 2)
         elif step <= 2:
-            work["down"] = swap(downs[step - 1], "dp", 2)
+            work["down"] = swap(ahead["down"], "dp", 2)
         for g in range(2):
             k = step + 1 - g
             if 1 <= k < chips:
@@ -110,7 +116,10 @@
                 work[f"left{g}"] = hop(
                     source if k == 1 else lefts[g][k - 1], range(1, chips - k + 1), -1
                 )
-        work = together(work)
+        later = {"gate": piece(step + 1)}
+        if step < 2:
+            later["down"] = jnp.split(down, 2)[step]
+        work, ahead, gate, down = together((work, later, gate, down))
         gate_x.append(work["gate"])
         if step == 0:
             own[1] = jnp.concatenate([work["pair"], work["info"]], axis=1)
@@ -120,7 +129,7 @@
             k = step + 1 - g
             if 1 <= k < chips:
                 rights[g][k], lefts[g][k] = work[f"right{g}"], work[f"left{g}"]
-    gate_last = swap(gates[-1], "dp", 1)
+    gate_last = swap(ahead["gate"], "dp", 1)
     down_y = jnp.concatenate(down_y)
 
     seen = [
@@ -142,36 +151,79 @@
         return place, pay.reshape(chips, 2 * slots, tok)
 
     chunk = 2 * slots
-    rows, near, pays = [], [], []
-    gate_early = jnp.concatenate(gate_x)
-    early = quarter + gate_early.shape[0]
-    for g in range(2):
-        place, pay = places(g, half)
-        pays.append(pay)
-        held = jnp.stack([s[:, :half] for s in seen[g]])
-
-        def choose(expert):
+    helds = [jnp.stack([s[:, :half] for s in seen[g]]) for g in range(2)]
+    (place0, pay0), (place1, _), (_, pay1) = (
+        places(0, half), places(1, half), places(1, half + 2 * top)
+    )
+    pay = jnp.stack([pay0, pay1])
+
+    def choose(place, held):
+        def of(expert):
             return jnp.einsum(
                 "zst,ztk->zsk", place[:, expert], held, preferred_element_type=F32
             ).astype(BF)
 
-        other = swap(choose(1), "expert", 1)
-        r = jnp.concatenate([choose(0), other], axis=1)
-        flat = r.reshape(-1, half)
-        n = jnp.dot(flat[:, :quarter], gate, preferred_element_type=F32) + jnp.dot(
-            flat[:, quarter:early], gate_early, preferred_element_type=F32
+        other = swap(of(1), "expert", 1)
+        return jnp.concatenate([of(0), other], axis=1).reshape(-1, half)
+
+    place1, gate_last = together((place1, gate_last))
+    rows = {1: choose(place1, helds[1])}
+    weights = jnp.concatenate([gate, *gate_x, gate_last])
+
+    def pick(array, q, axis=0):
+        return lax.dynamic_index_in_dim(array, (z - order[q]) % chips, axis, keepdims=False)
+
+    def product(g):
+        return jnp.dot(rows[g], weights, preferred_element_type=F32).reshape(chips, chunk, 2 * ff)
+
+    sent = product(1).astype(BF)
+    token = sent
+
+    def in_order(*values):
+        return together((values, token))[0]
+
+    part = []
+    for q in range(chips):
+        (sent,) = in_order(sent)
+        token = pick(sent, q)
+        part.append(swap(token, "dp", 2))
+    place0, held0, weights, pay, down_y = in_order(place0, helds[0], weights, pay, down_y)
+    rows[0] = choose(place0, held0)
+    near = token = product(0)
+
+    hidden, back, out, terms = {}, {}, {}, []
+
+    def finish(q):
+        (came,) = in_order(part[q])
+        gu = pick(near, q) + came.astype(F32)
+        own = (jax.nn.silu(gu[:, :ff]) * gu[:, ff:]).astype(BF)
+        hidden[q] = (own, swap(own, "dp", 1))
+        return own
+
+    def down_product(q):
+        own, theirs = in_order(*hidden[q])
+        if q + 1 < chips:
+            own, part[q + 1] = together((own, part[q + 1]))
+        joined = jnp.concatenate([own, theirs])
+        value = jnp.concatenate(
+            [jnp.dot(joined, w, preferred_element_type=F32).astype(BF) for w in (down, down_y)],
+            axis=1,
+        ).reshape(2, 2, slots, half)
+        out[q], away = value[:, 0], value[:, 1]
+        back[q] = swap(away, "expert", 1)
+        return away
+
+    def weigh(q):
+        own, theirs = in_order(out[q], back[q])
+        terms.append(
+            jnp.einsum(
+                "gst,gsk->gtk",
+                pick(pay, q, 1),
+                jnp.concatenate([own, theirs], axis=1),
+                preferred_element_type=F32,
+            )
         )
-        rows.append(r[..., early:])
-        near.append(n.reshape(chips, chunk, 2 * ff))
-    pay = jnp.stack([pays[0], places(1, half + 2 * top)[1]])
-    rows, near, pay, gate_last, down_y = together((rows, near, pay, gate_last, down_y))
-
-    def product(g, q):
-        at = (z - order[q]) % chips
-        r = lax.dynamic_index_in_dim(rows[g], at, 0, keepdims=False)
-        return jnp.dot(r, gate_last, preferred_element_type=F32) + lax.dynamic_index_in_dim(
-            near[g], at, 0, keepdims=False
-        )
+        return terms[-1]
 
     def term(step, to):
         total = terms[0]
@@ -179,47 +231,33 @@
             total = jnp.where(order[q] == to, terms[q], total)
         return total
 
-    right = left = 0.0
-    terms, arrived, hidden, joined = [], None, None, None
-    sent = product(1, 0).astype(BF)
-    for step in range(chips + 2):
-        k = step - 2
-        work = {}
-        if step < chips:
-            work["part"] = swap(sent, "dp", 2)
-        if step + 1 < chips:
-            work["sent"] = product(1, step + 1).astype(BF)
-        if arrived is not None:
-            gu = product(0, step - 1) + arrived.astype(F32)
-            hidden = (jax.nn.silu(gu[:, :ff]) * gu[:, ff:]).astype(BF)
-            work["hidden"] = jnp.concatenate([hidden, swap(hidden, "dp", 1)])
-        if joined is not None:
-            out = jnp.concatenate(
-                [
-                    jnp.dot(joined, w, preferred_element_type=F32).astype(BF)
-                    for w in (down, down_y)
-                ],
-                axis=1,
-            ).reshape(2, 2, slots, half)
-            out = jnp.concatenate([out[:, 0], swap(out[:, 1], "expert", 1)], axis=1)
-            paid = lax.dynamic_index_in_dim(pay, (z - order[k]) % chips, 1, keepdims=False)
-            work["term"] = jnp.einsum("gst,gsk->gtk", paid, out, preferred_element_type=F32)
+    right = left = None
+
+    def chain(k):
+        upward, downward = term(k, z + chips - k), term(k, z - chips + k)
+        if right is not None:
+            r, l = in_order(right, left)
+            upward, downward = upward + r.astype(F32), downward + l.astype(F32)
+        return upward.astype(BF), downward.astype(BF)
+
+    for q in range(chips):
+        if q == 0:
+            token = finish(0)
+        if q == 2:
+            (right, left), token = together(((right, left), token))
+        token = down_product(q)
+        if q + 1 < chips:
+            token = finish(q + 1)
+        token = weigh(q)
+        k = q if q >= 2 else 1 - q
         if 1 <= k < chips - 1:
-            work["right"] = hop((term(k, z + chips - k) + right).astype(BF), range(k), 1)
-            work["left"] = hop(
-                (term(k, z - chips + k) + left).astype(BF), range(chips - k, chips), -1
-            )
-        work = together(work)
-        sent, arrived, joined = work.get("sent"), work.get("part"), work.get("hidden")
-        if "term" in work:
-            terms.append(work["term"])
-        if "right" in work:
-            right, left = work["right"].astype(F32), work["left"].astype(F32)
+            token = upward, downward = chain(k)
+            right = hop(upward, range(k), 1)
+            left = hop(downward, range(chips - k, chips), -1)
 
     k = chips - 1
     mine = []
-    upward = (term(k, z + chips - k) + right).astype(BF)
-    downward = (term(k, z - chips + k) + left).astype(BF)
+    upward, downward = chain(k)
     for g in (1, 0):
         came = [hop(upward[g], range(k), 1), hop(downward[g], range(1, chips), -1)]
         if g == 1:

time: 277 us -> 270 us (0.975)
  waiting for transfers between devices: 96 us -> 112 us
  matrix products: 38 us -> 23.4 us
  local copies, waits for them, and re-layouts: 39.3 us -> 31.9 us
    ppermute x20, waiting for transfers between devices: 28.6 us -> 76.8 us  [hop(): lax.ppermute(value, 'expert', [(2 * i + c, 2 * (i + by) + c) for i in sou...]
    ppermute x24, waiting for transfers between devices: 67.4 us -> 35.2 us  [swap(): lax.ppermute(value, axis, [(i, i ^ bit) for i in range(lax.axis_size(axis...]
    dot_general x28 -> x18, matrix products: 37.6 us -> 23 us  [the longest x2 8.13 us: product(): jnp.dot(rows[g], weights, preferred_element_type=F32)]
    unnamed x72 -> x44, local copies, waits for them, and re-layouts: 13.9 us -> 8.35 us
    slice x3 -> x6, local copies, waits for them, and re-layouts: 6.33 us -> 11 us  [the longest x5 10.3 us: piece(): return gate[quarter * lo // 7:quarter * hi // 7]]
    another operation x7, local copies, waits for them, and re-layouts: 5.67 us -> 1.79 us  [paired(): helds = [jnp.stack([s[:, :half] for s in seen[g]]) for g in range(2)]]
    ppermute x24, starting transfers between devices: 20.4 us -> 23.6 us  [swap(): lax.ppermute(value, axis, [(i, i ^ bit) for i in range(lax.axis_size(axis...]
    convert_element_type x7 -> x8, other arithmetic: 6.86 us -> 4.75 us  [the longest x2 4.07 us: chain(): return (upward.astype(BF), downward.astype(BF))]
  transfers between devices with their start and end apart: 44 -> 44, of which waited for: 20 -> 19; matrix products, arithmetic and copies ran while one was open for 26% -> 19% of each run, Pallas kernels for 0% -> 0%
where the time goes in v4:
time: 270 us; the launch traced here: 269 us
  waiting for transfers between devices  112 us (41%)
  starting transfers between devices  75.3 us (28%)
  local copies, waits for them, and re-layouts  31.9 us (12%)
  matrix products  23.4 us (9%)
  other arithmetic  18.3 us (7%)
  between operations  7.52 us (3%)
    ppermute x20, waiting for transfers between devices, hop(): lax.ppermute(value, 'expert', [(2 * i + c, 2 * (i + by) + c) for i in sou...  76.8 us
    ppermute x20, starting transfers between devices, hop(): lax.ppermute(value, 'expert', [(2 * i + c, 2 * (i + by) + c) for i in sou...  51.7 us
    ppermute x24, waiting for transfers between devices, swap(): lax.ppermute(value, axis, [(i, i ^ bit) for i in range(lax.axis_size(axis...  35.2 us
    ppermute x24, starting transfers between devices, swap(): lax.ppermute(value, axis, [(i, i ^ bit) for i in range(lax.axis_size(axis...  23.6 us
    slice x5, local copies, waits for them, and re-layouts, piece(): return gate[quarter * lo // 7:quarter * hi // 7]  10.3 us
    unnamed x44, local copies, waits for them, and re-layouts  8.35 us
    dot_general x2, matrix products, product(): jnp.dot(rows[g], weights, preferred_element_type=F32)  8.13 us
    dot_general x8, matrix products, down_product(): jnp.dot(joined, w, preferred_element_type=F32).astype(BF)  7.23 us
  transfers between devices with their start and end apart: 44, of which 19 were waited for; matrix products, arithmetic and copies ran while one was open for 19% of the time, Pallas kernels for 0%

profile of v4, /device:TPU:0, one launch (start us, length us, event | category | flops | bytes accessed | tf_op | source)
XLA Modules:
  0.0 268.5 jit_solution(11945127718367826384)
XLA Ops:
  4.4 1.9 slice.203
  6.3 2.9 %collective-permute-start = (bf16[128,2048]{1,0:T(8,128)(2,1)}, bf16[128,2048]{1,0:T(8,128)(2,1)}, u32[]{:S(2)}, u32[]{:S(2)}) collective-permute-start(bf16[128,2048]{1,0:T(8,128)(2,1)} %slice.203), channel_id=1, source_target_pairs={{0,8},{8,0},{16,24},{24,16},{1,9},{9,1},{17,25},{25,17},{2,10},{10... | collective-permute-start | bytes 1572872 | tf_op jit(solution)/shard_map/ppermute | solution.py:55
  10.7 1.4 collective-permute-start.2
  12.1 5.4 %collective-permute-start.4 = (bf16[128,1808]{0,1:T(8,128)(2,1)}, bf16[128,1808]{0,1:T(8,128)(2,1)}, u32[]{:S(2)}, u32[]{:S(2)}) collective-permute-start(bf16[128,1808]{0,1:T(8,128)(2,1)} %pad_maximum_fusion.8), channel_id=1, source_target_pairs={{0,2},{1,3},{2,4},{3,5},{4,6},{5,7},{8,10},{9,11},{10,12},{11,13},... | collective-permute-start | bytes 1388552 | tf_op jit(solution)/shard_map/ppermute | solution.py:81
  17.7 2.0 collective-permute-start.3
  21.1 2.3 slice.204
  27.2 2.9 %collective-permute-done.3 = bf16[128,1808]{1,0:T(8,128)(2,1)S(1)} collective-permute-done((bf16[128,1808]{1,0:T(8,128)(2,1)}, bf16[128,1808]{1,0:T(8,128)(2,1)S(1)}, u32[]{:S(2)}, u32[]{:S(2)}) %collective-permute-start.3) | collective-permute-done | bytes 462880 | tf_op jit(solution)/shard_map/ppermute | solution.py:55
  30.1 1.6 collective-permute-start.6
  31.8 1.5 collective-permute-start.5
  33.3 1.3 collective-permute-start.7
  35.5 4.6 %collective-permute-start.10 = (bf16[128,1824]{1,0:T(8,128)(2,1)}, bf16[128,1824]{1,0:T(8,128)(2,1)S(1)}, u32[]{:S(2)}, u32[]{:S(2)}) collective-permute-start(bf16[128,1824]{1,0:T(8,128)(2,1)} %pad_maximum_fusion.7), channel_id=1, source_target_pairs={{0,2},{1,3},{2,4},{3,5},{4,6},{5,7},{8,10},{9,11},{10,12},{11,13},... | collective-permute-start | bytes 1400840 | tf_op jit(solution)/shard_map/ppermute | solution.py:81
  40.0 1.3 collective-permute-start.8
  41.3 2.3 slice.205
  44.8 4.1 %collective-permute-done.7 = bf16[128,1808]{0,1:T(8,128)(2,1)} collective-permute-done((bf16[128,1808]{0,1:T(8,128)(2,1)}, bf16[128,1808]{0,1:T(8,128)(2,1)}, u32[]{:S(2)}, u32[]{:S(2)}) %collective-permute-start.7) | collective-permute-done | bytes 462880 | tf_op jit(solution)/shard_map/ppermute | solution.py:81
  50.4 5.4 %collective-permute-done.8 = bf16[128,1824]{1,0:T(8,128)(2,1)} collective-permute-done((bf16[128,1824]{1,0:T(8,128)(2,1)}, bf16[128,1824]{1,0:T(8,128)(2,1)}, u32[]{:S(2)}, u32[]{:S(2)}) %collective-permute-start.8) | collective-permute-done | bytes 466976 | tf_op jit(solution)/shard_map/ppermute | solution.py:81
  57.0 1.9 slice.206
  58.9 1.3 collective-permute-start.14
  60.1 1.3 collective-permute-start.13
  63.2 19.3 %collective-permute-done.13 = bf16[128,1808]{0,1:T(8,128)(2,1)S(1)} collective-permute-done((bf16[128,1808]{0,1:T(8,128)(2,1)}, bf16[128,1808]{0,1:T(8,128)(2,1)S(1)}, u32[]{:S(2)}, u32[]{:S(2)}) %collective-permute-start.13) | collective-permute-done | bytes 462880 | tf_op jit(solution)/shard_map/ppermute | solution.py:81
  82.6 1.5 collective-permute-start.16
  84.1 1.3 collective-permute-start.18
  85.4 1.4 collective-permute-start.19
  89.2 1.4 collective-permute-start.17
  91.0 2.6 pad_maximum_fusion.1
  93.6 1.9 slice.214
  95.7 3.2 %collective-permute-done.18 = bf16[128,1824]{1,0:T(8,128)(2,1)} collective-permute-done((bf16[128,1824]{1,0:T(8,128)(2,1)}, bf16[128,1824]{1,0:T(8,128)(2,1)}, u32[]{:S(2)}, u32[]{:S(2)}) %collective-permute-start.18) | collective-permute-done | bytes 466976 | tf_op jit(solution)/shard_map/ppermute | solution.py:81
  99.4 1.3 broadcast_select_fusion
  102.3 1.3 collective-permute-start.20
  103.6 2.5 constant_dynamic-update-slice_fusion.5
  107.5 1.3 constant_dynamic-update-slice_fusion.3
  109.4 2.3 collective-permute-done.20
  114.7 4.1 %fusion.4 = bf16[4,128,2048]{2,1,0:T(8,128)(2,1)S(1)} fusion(bf16[1792,2048]{1,0:T(8,128)(2,1)S(1)} %constant_dynamic-update-slice_fusion, bf16[4,64,1792]{2,1,0:T(8,128)(2,1)S(1)} %collective-permute-done.21, bf16[4,64,1792]{2,1,0:T(8,128)(2,1)S(1)} %convolution_convert_fusion.3), kind=kOutput, calls=%fused_computation.4 | convolution fusion | flops 3762814976 | bytes 11272192 | tf_op jit(solution)/shard_map/dot_general | solution.py:177
  120.0 1.5 collective-permute-start.23
  122.9 4.0 %fusion = f32[4,128,2048]{2,1,0:T(8,128)S(1)} fusion(bf16[1792,2048]{1,0:T(8,128)(2,1)S(1)} %constant_dynamic-update-slice_fusion, bf16[4,64,1792]{2,1,0:T(8,128)(2,1)S(1)} %collective-permute-done.22, bf16[4,64,1792]{2,1,0:T(8,128)(2,1)S(1)} %convolution_convert_fusion.1), kind=kOutput, calls=%fused_computation | convolution fusion | flops 3761766400 | bytes 13369344 | tf_op jit(solution)/shard_map/dot_general | solution.py:177
  126.9 8.0 %collective-permute-done.23 = bf16[128,2048]{1,0:T(8,128)(2,1)S(1)} collective-permute-done((bf16[128,2048]{1,0:T(8,128)(2,1)S(1)}, bf16[128,2048]{1,0:T(8,128)(2,1)S(1)}, u32[]{:S(2)}, u32[]{:S(2)}) %collective-permute-start.23) | collective-permute-done | bytes 524320 | tf_op jit(solution)/shard_map/ppermute | solution.py:55
  135.1 1.4 collective-permute-start.24
  136.5 1.5 collective-permute-start.28
  138.0 4.4 %collective-permute-done.24 = bf16[128,1024]{1,0:T(8,128)(2,1)S(1)} collective-permute-done((bf16[128,1024]{1,0:T(8,128)(2,1)S(1)}, bf16[128,1024]{1,0:T(8,128)(2,1)S(1)}, u32[]{:S(2)}, u32[]{:S(2)}) %collective-permute-start.24) | collective-permute-done | bytes 262176 | tf_op jit(solution)/shard_map/ppermute | solution.py:55
  142.4 3.7 %collective-permute-done.25 = bf16[128,2048]{1,0:T(8,128)(2,1)S(1)} collective-permute-done((bf16[128,2048]{1,0:T(8,128)(2,1)S(1)}, bf16[128,2048]{1,0:T(8,128)(2,1)S(1)}, u32[]{:S(2)}, u32[]{:S(2)}) %collective-permute-start.25) | collective-permute-done | bytes 524320 | tf_op jit(solution)/shard_map/ppermute | solution.py:55
  148.8 1.4 collective-permute-start.26
  150.2 1.5 collective-permute-start.30
  151.7 1.4 fusion.96
  153.1 4.5 %collective-permute-done.26 = bf16[128,1024]{1,0:T(8,128)(2,1)S(1)} collective-permute-done((bf16[128,1024]{1,0:T(8,128)(2,1)S(1)}, bf16[128,1024]{1,0:T(8,128)(2,1)S(1)}, u32[]{:S(2)}, u32[]{:S(2)}) %collective-permute-start.26) | collective-permute-done | bytes 262176 | tf_op jit(solution)/shard_map/ppermute | solution.py:55
  160.3 1.4 collective-permute-start.29
  163.0 8.6 %collective-permute-start.33 = (bf16[2,128,1792]{2,1,0:T(8,128)(2,1)}, bf16[2,128,1792]{2,1,0:T(8,128)(2,1)S(1)}, u32[]{:S(2)}, u32[]{:S(2)}) collective-permute-start(bf16[2,128,1792]{2,1,0:T(8,128)(2,1)} %get-tuple-element.214), channel_id=1, source_target_pairs={{0,2},{1,3},{8,10},{9,11},{16,18},{17,19},{24,26},{25,27}} | collective-permute-start | bytes 2752520 | tf_op jit(solution)/shard_map/ppermute | solution.py:81
  173.7 2.2 convolution_convert_fusion.7
  177.0 1.5 bitcast_add_fusion.3
  180.0 1.8 fusion.27
  181.8 10.2 %collective-permute-done.33 = bf16[2,128,1792]{2,1,0:T(8,128)(2,1)S(1)} collective-permute-done((bf16[2,128,1792]{2,1,0:T(8,128)(2,1)}, bf16[2,128,1792]{2,1,0:T(8,128)(2,1)S(1)}, u32[]{:S(2)}, u32[]{:S(2)}) %collective-permute-start.33) | collective-permute-done | bytes 917536 | tf_op jit(solution)/shard_map/ppermute | solution.py:81
  192.1 1.7 add_convert_fusion.2
  195.2 4.3 %collective-permute-start.37 = (bf16[2,128,1792]{2,1,0:T(8,128)(2,1)}, bf16[2,128,1792]{2,1,0:T(8,128)(2,1)S(1)}, u32[]{:S(2)}, u32[]{:S(2)}) collective-permute-start(bf16[2,128,1792]{2,1,0:T(8,128)(2,1)} %get-tuple-element.183), channel_id=1, source_target_pairs={{0,2},{1,3},{2,4},{3,5},{8,10},{9,11},{10,12},{11,13},{16,18},{17,... | collective-permute-start | bytes 2752520 | tf_op jit(solution)/shard_map/ppermute | solution.py:81
  199.6 1.6 collective-permute-start.38
  204.8 1.6 fusion.31
  206.4 12.9 %collective-permute-done.37 = bf16[2,128,1792]{2,1,0:T(8,128)(2,1)S(1)} collective-permute-done((bf16[2,128,1792]{2,1,0:T(8,128)(2,1)}, bf16[2,128,1792]{2,1,0:T(8,128)(2,1)S(1)}, u32[]{:S(2)}, u32[]{:S(2)}) %collective-permute-start.37) | collective-permute-done | bytes 917536 | tf_op jit(solution)/shard_map/ppermute | solution.py:81
  219.3 2.4 add_convert_fusion
  221.7 9.4 %collective-permute-start.39 = (bf16[128,1792]{1,0:T(8,128)(2,1)S(1)}, bf16[128,1792]{1,0:T(8,128)(2,1)S(1)}, u32[]{:S(2)}, u32[]{:S(2)}) collective-permute-start(bf16[128,1792]{1,0:T(8,128)(2,1)S(1)} %slice_bitcast_fusion.3), channel_id=1, source_target_pairs={{0,2},{1,3},{2,4},{3,5},{4,6},{5,7},{8,10},{9,11},{10,12},{11,13},... | collective-permute-start | bytes 1376264 | tf_op jit(solution)/shard_map/ppermute | solution.py:81
  231.2 1.3 collective-permute-start.40
  232.5 7.1 %collective-permute-done.39 = bf16[128,1792]{1,0:T(8,128)(2,1)S(1)} collective-permute-done((bf16[128,1792]{1,0:T(8,128)(2,1)S(1)}, bf16[128,1792]{1,0:T(8,128)(2,1)S(1)}, u32[]{:S(2)}, u32[]{:S(2)}) %collective-permute-start.39) | collective-permute-done | bytes 458784 | tf_op jit(solution)/shard_map/ppermute | solution.py:81
  239.5 4.2 %collective-permute-done.40 = bf16[128,1792]{1,0:T(8,128)(2,1)S(1)} collective-permute-done((bf16[128,1792]{1,0:T(8,128)(2,1)S(1)}, bf16[128,1792]{1,0:T(8,128)(2,1)S(1)}, u32[]{:S(2)}, u32[]{:S(2)}) %collective-permute-start.40) | collective-permute-done | bytes 458784 | tf_op jit(solution)/shard_map/ppermute | solution.py:81
  243.7 2.2 collective-permute-start.41
  246.0 1.3 collective-permute-start.42
  247.3 6.1 %collective-permute-done.41 = bf16[128,1792]{1,0:T(8,128)(2,1)S(1)} collective-permute-done((bf16[128,1792]{1,0:T(8,128)(2,1)S(1)}, bf16[128,1792]{1,0:T(8,128)(2,1)S(1)}, u32[]{:S(2)}, u32[]{:S(2)}) %collective-permute-start.41) | collective-permute-done | bytes 458784 | tf_op jit(solution)/shard_map/ppermute | solution.py:81
  253.4 4.2 %collective-permute-done.42 = bf16[128,1792]{1,0:T(8,128)(2,1)S(1)} collective-permute-done((bf16[128,1792]{1,0:T(8,128)(2,1)S(1)}, bf16[128,1792]{1,0:T(8,128)(2,1)S(1)}, u32[]{:S(2)}, u32[]{:S(2)}) %collective-permute-start.42) | collective-permute-done | bytes 458784 | tf_op jit(solution)/shard_map/ppermute | solution.py:81
  258.9 7.9 %collective-permute-done.43 = bf16[128,1792]{1,0:T(8,128)(2,1)S(1)} collective-permute-done((bf16[128,1792]{1,0:T(8,128)(2,1)S(1)}, bf16[128,1792]{1,0:T(8,128)(2,1)S(1)}, u32[]{:S(2)}, u32[]{:S(2)}) %collective-permute-start.43) | collective-permute-done | bytes 458784 | tf_op jit(solution)/shard_map/ppermute | solution.py:55
  (194 shorter events, 43.0 us)
Async XLA Ops:
  0.0 9.2 %copy-start.3 = (bf16[128,3584]{1,0:T(8,128)(2,1)S(1)}, bf16[128,3584]{1,0:T(8,128)(2,1)}, u32[]{:S(2)}) copy-start(bf16[128,3584]{1,0:T(8,128)(2,1)} %param.6) | copy-start | bytes 2752516
  6.3 23.8 %collective-permute-start = (bf16[128,2048]{1,0:T(8,128)(2,1)}, bf16[128,2048]{1,0:T(8,128)(2,1)}, u32[]{:S(2)}, u32[]{:S(2)}) collective-permute-start(bf16[128,2048]{1,0:T(8,128)(2,1)} %slice.203), channel_id=1, source_target_pairs={{0,8},{8,0},{16,24},{24,16},{1,9},{9,1},{17,25},{25,17},{2,10},{10... | collective-permute-start | bytes 1572872 | tf_op jit(solution)/shard_map/ppermute | solution.py:55
  10.7 15.4 %copy-start.4 = (bf16[1,1024,896]{2,1,0:T(8,128)(2,1)S(1)}, bf16[1,1024,896]{2,1,0:T(8,128)(2,1)}, u32[]{:S(2)}) copy-start(bf16[1,1024,896]{2,1,0:T(8,128)(2,1)} %param.8) | copy-start | bytes 5505028
  10.7 16.5 %collective-permute-start.2 = (bf16[128,1808]{0,1:T(8,128)(2,1)}, bf16[128,1808]{0,1:T(8,128)(2,1)}, u32[]{:S(2)}, u32[]{:S(2)}) collective-permute-start(bf16[128,1808]{0,1:T(8,128)(2,1)} %pad_maximum_fusion.8), channel_id=1, source_target_pairs={{2,0},{3,1},{4,2},{5,3},{6,4},{7,5},{10,8},{11,9},{12,10},{13,11},... | collective-permute-start | bytes 1388552 | tf_op jit(solution)/shard_map/ppermute | solution.py:81
  12.1 15.1 %collective-permute-start.4 = (bf16[128,1808]{0,1:T(8,128)(2,1)}, bf16[128,1808]{0,1:T(8,128)(2,1)}, u32[]{:S(2)}, u32[]{:S(2)}) collective-permute-start(bf16[128,1808]{0,1:T(8,128)(2,1)} %pad_maximum_fusion.8), channel_id=1, source_target_pairs={{0,2},{1,3},{2,4},{3,5},{4,6},{5,7},{8,10},{9,11},{10,12},{11,13},... | collective-permute-start | bytes 1388552 | tf_op jit(solution)/shard_map/ppermute | solution.py:81
  17.6 9.6 %collective-permute-start.1 = (bf16[128,16]{1,0:T(8,128)(2,1)S(1)}, bf16[128,16]{1,0:T(8,128)(2,1)S(1)}, u32[]{:S(2)}, u32[]{:S(2)}) collective-permute-start(bf16[128,16]{1,0:T(8,128)(2,1)S(1)} %copy.111), channel_id=1, source_target_pairs={{0,8},{8,0},{16,24},{24,16},{1,9},{9,1},{17,25},{25,17},{2,10},{10... | collective-permute-start | bytes 12296 | tf_op jit(solution)/shard_map/ppermute | solution.py:55
  17.7 12.3 %collective-permute-start.3 = (bf16[128,1808]{1,0:T(8,128)(2,1)}, bf16[128,1808]{1,0:T(8,128)(2,1)S(1)}, u32[]{:S(2)}, u32[]{:S(2)}) collective-permute-start(bf16[128,1808]{1,0:T(8,128)(2,1)} %concatenate.64), channel_id=1, source_target_pairs={{0,16},{8,24},{16,0},{24,8},{1,17},{9,25},{17,1},{25,9},{2,18},{10... | collective-permute-start | bytes 1388552 | tf_op jit(solution)/shard_map/ppermute | solution.py:55
  30.1 25.7 %collective-permute-start.6 = (bf16[256,2048]{1,0:T(8,128)(2,1)}, bf16[256,2048]{1,0:T(8,128)(2,1)}, u32[]{:S(2)}, u32[]{:S(2)}) collective-permute-start(bf16[256,2048]{1,0:T(8,128)(2,1)} %slice.204), channel_id=1, source_target_pairs={{0,8},{8,0},{16,24},{24,16},{1,9},{9,1},{17,25},{25,17},{2,10},{10... | collective-permute-start | bytes 3145736 | tf_op jit(solution)/shard_map/ppermute | solution.py:55
  31.8 24.0 %collective-permute-start.5 = (bf16[512,896]{1,0:T(8,128)(2,1)}, bf16[512,896]{1,0:T(8,128)(2,1)}, u32[]{:S(2)}, u32[]{:S(2)}) collective-permute-start(bf16[512,896]{1,0:T(8,128)(2,1)} %split.6), channel_id=1, source_target_pairs={{0,16},{8,24},{16,0},{24,8},{1,17},{9,25},{17,1},{25,9},{2,18},{10... | collective-permute-start | bytes 2752520 | tf_op jit(solution)/shard_map/ppermute | solution.py:55
  33.3 15.6 %collective-permute-start.7 = (bf16[128,1808]{0,1:T(8,128)(2,1)}, bf16[128,1808]{0,1:T(8,128)(2,1)}, u32[]{:S(2)}, u32[]{:S(2)}) collective-permute-start(bf16[128,1808]{0,1:T(8,128)(2,1)} %collective-permute-done.2), channel_id=1, source_target_pairs={{2,0},{3,1},{4,2},{5,3},{10,8},{11,9},{12,10},{13,11},{18,16},{19,... | collective-permute-start | bytes 1388552 | tf_op jit(solution)/shard_map/ppermute | solution.py:81
  35.5 14.9 %collective-permute-start.10 = (bf16[128,1824]{1,0:T(8,128)(2,1)}, bf16[128,1824]{1,0:T(8,128)(2,1)S(1)}, u32[]{:S(2)}, u32[]{:S(2)}) collective-permute-start(bf16[128,1824]{1,0:T(8,128)(2,1)} %pad_maximum_fusion.7), channel_id=1, source_target_pairs={{0,2},{1,3},{2,4},{3,5},{4,6},{5,7},{8,10},{9,11},{10,12},{11,13},... | collective-permute-start | bytes 1400840 | tf_op jit(solution)/shard_map/ppermute | solution.py:81
  40.0 15.7 %collective-permute-start.8 = (bf16[128,1824]{1,0:T(8,128)(2,1)}, bf16[128,1824]{1,0:T(8,128)(2,1)}, u32[]{:S(2)}, u32[]{:S(2)}) collective-permute-start(bf16[128,1824]{1,0:T(8,128)(2,1)} %pad_maximum_fusion.7), channel_id=1, source_target_pairs={{2,0},{3,1},{4,2},{5,3},{6,4},{7,5},{10,8},{11,9},{12,10},{13,11},... | collective-permute-start | bytes 1400840 | tf_op jit(solution)/shard_map/ppermute | solution.py:81
  48.9 1.5 collective-permute-start.9
  50.4 37.6 %copy-start.12 = (bf16[128,1824]{1,0:T(8,128)(2,1)}, bf16[128,1824]{1,0:T(8,128)(2,1)S(1)}, u32[]{:S(2)}) copy-start(bf16[128,1824]{1,0:T(8,128)(2,1)S(1)} %collective-permute-done.10) | copy-start | bytes 1400836
  55.8 28.3 %collective-permute-start.12 = (bf16[256,2048]{1,0:T(8,128)(2,1)}, bf16[256,2048]{1,0:T(8,128)(2,1)S(1)}, u32[]{:S(2)}, u32[]{:S(2)}) collective-permute-start(bf16[256,2048]{1,0:T(8,128)(2,1)} %slice.205), channel_id=1, source_target_pairs={{0,8},{8,0},{16,24},{24,16},{1,9},{9,1},{17,25},{25,17},{2,10},{10... | collective-permute-start | bytes 3145736 | tf_op jit(solution)/shard_map/ppermute | solution.py:55
  56.3 27.8 %collective-permute-start.11 = (bf16[512,896]{1,0:T(8,128)(2,1)}, bf16[512,896]{1,0:T(8,128)(2,1)S(1)}, u32[]{:S(2)}, u32[]{:S(2)}) collective-permute-start(bf16[512,896]{1,0:T(8,128)(2,1)} %split.7), channel_id=1, source_target_pairs={{0,16},{8,24},{16,0},{24,8},{1,17},{9,25},{17,1},{25,9},{2,18},{10... | collective-permute-start | bytes 2752520 | tf_op jit(solution)/shard_map/ppermute | solution.py:55
  58.9 25.2 %collective-permute-start.14 = (bf16[128,1824]{1,0:T(8,128)(2,1)}, bf16[128,1824]{1,0:T(8,128)(2,1)}, u32[]{:S(2)}, u32[]{:S(2)}) collective-permute-start(bf16[128,1824]{1,0:T(8,128)(2,1)} %collective-permute-done.8), channel_id=1, source_target_pairs={{2,0},{3,1},{4,2},{5,3},{10,8},{11,9},{12,10},{13,11},{18,16},{19,... | collective-permute-start | bytes 1400840 | tf_op jit(solution)/shard_map/ppermute | solution.py:81
  60.1 22.4 %collective-permute-start.13 = (bf16[128,1808]{0,1:T(8,128)(2,1)}, bf16[128,1808]{0,1:T(8,128)(2,1)S(1)}, u32[]{:S(2)}, u32[]{:S(2)}) collective-permute-start(bf16[128,1808]{0,1:T(8,128)(2,1)} %collective-permute-done.7), channel_id=1, source_target_pairs={{2,0},{3,1},{10,8},{11,9},{18,16},{19,17},{26,24},{27,25}} | collective-permute-start | bytes 1388552 | tf_op jit(solution)/shard_map/ppermute | solution.py:81
  61.4 22.6 %collective-permute-start.15 = (bf16[128,1808]{0,1:T(8,128)(2,1)S(1)}, bf16[128,1808]{0,1:T(8,128)(2,1)S(1)}, u32[]{:S(2)}, u32[]{:S(2)}) collective-permute-start(bf16[128,1808]{0,1:T(8,128)(2,1)S(1)} %collective-permute-done.9), channel_id=1, source_target_pairs={{4,6},{5,7},{12,14},{13,15},{20,22},{21,23},{28,30},{29,31}} | collective-permute-start | bytes 1388552 | tf_op jit(solution)/shard_map/ppermute | solution.py:81
  82.6 1.5 collective-permute-start.16
  84.1 2.8 %copy-start.9 = (bf16[256,2048]{1,0:T(8,128)(2,1)}, bf16[256,2048]{1,0:T(8,128)(2,1)S(1)}, u32[]{:S(2)}) copy-start(bf16[256,2048]{1,0:T(8,128)(2,1)S(1)} %collective-permute-done.12) | copy-start | bytes 3145732
  84.1 14.8 %collective-permute-start.18 = (bf16[128,1824]{1,0:T(8,128)(2,1)}, bf16[128,1824]{1,0:T(8,128)(2,1)}, u32[]{:S(2)}, u32[]{:S(2)}) collective-permute-start(bf16[128,1824]{1,0:T(8,128)(2,1)} %collective-permute-done.14), channel_id=1, source_target_pairs={{2,0},{3,1},{10,8},{11,9},{18,16},{19,17},{26,24},{27,25}} | collective-permute-start | bytes 1400840 | tf_op jit(solution)/shard_map/ppermute | solution.py:81
  85.4 13.5 %collective-permute-start.19 = (bf16[128,1824]{1,0:T(8,128)(2,1)}, bf16[128,1824]{1,0:T(8,128)(2,1)}, u32[]{:S(2)}, u32[]{:S(2)}) collective-permute-start(bf16[128,1824]{1,0:T(8,128)(2,1)} %collective-permute-done.16), channel_id=1, source_target_pairs={{4,6},{5,7},{12,14},{13,15},{20,22},{21,23},{28,30},{29,31}} | collective-permute-start | bytes 1400840 | tf_op jit(solution)/shard_map/ppermute | solution.py:81
  89.2 10.2 %collective-permute-start.17 = (bf16[128,2048]{1,0:T(8,128)(2,1)}, bf16[128,2048]{1,0:T(8,128)(2,1)S(1)}, u32[]{:S(2)}, u32[]{:S(2)}) collective-permute-start(bf16[128,2048]{1,0:T(8,128)(2,1)} %slice.206), channel_id=1, source_target_pairs={{0,8},{8,0},{16,24},{24,16},{1,9},{9,1},{17,25},{25,17},{2,10},{10... | collective-permute-start | bytes 1572872 | tf_op jit(solution)/shard_map/ppermute | solution.py:55
  95.7 16.0 %copy-start.14 = (bf16[1,128,1792]{2,1,0:T(8,128)(2,1)}, bf16[1,128,1792]{2,1,0:T(8,128)(2,1)S(1)}, u32[]{:S(2)}) copy-start(bf16[1,128,1792]{2,1,0:T(8,128)(2,1)S(1)} %slice_bitcast_fusion.13) | copy-start | bytes 1376260
  102.3 9.4 %collective-permute-start.20 = (bf16[128,2048]{1,0:T(8,128)(2,1)}, bf16[128,2048]{1,0:T(8,128)(2,1)S(1)}, u32[]{:S(2)}, u32[]{:S(2)}) collective-permute-start(bf16[128,2048]{1,0:T(8,128)(2,1)} %slice.214), channel_id=1, source_target_pairs={{0,8},{8,0},{16,24},{24,16},{1,9},{9,1},{17,25},{25,17},{2,10},{10... | collective-permute-start | bytes 1572872 | tf_op jit(solution)/shard_map/ppermute | solution.py:55
  106.1 2.8 %copy-start.10 = (bf16[256,2048]{1,0:T(8,128)(2,1)S(1)}, bf16[256,2048]{1,0:T(8,128)(2,1)}, u32[]{:S(2)}) copy-start(bf16[256,2048]{1,0:T(8,128)(2,1)} %copy-done.9) | copy-start | bytes 3145732
  108.9 2.8 %copy-start.13 = (bf16[1,128,1792]{2,1,0:T(8,128)(2,1)S(1)}, bf16[1,128,1792]{2,1,0:T(8,128)(2,1)}, u32[]{:S(2)}) copy-start(bf16[1,128,1792]{2,1,0:T(8,128)(2,1)} %slice_bitcast_fusion.20) | copy-start | bytes 1376260
  108.9 2.8 %copy-start.16 = (bf16[1,128,1792]{2,1,0:T(8,128)(2,1)S(1)}, bf16[1,128,1792]{2,1,0:T(8,128)(2,1)}, u32[]{:S(2)}) copy-start(bf16[1,128,1792]{2,1,0:T(8,128)(2,1)} %slice_bitcast_fusion.12) | copy-start | bytes 1376260
  112.2 1.0 copy-start.15
  112.2 2.5 collective-permute-start.21
  119.8 3.0 %collective-permute-start.22 = (bf16[4,64,1792]{2,1,0:T(8,128)(2,1)S(1)}, bf16[4,64,1792]{2,1,0:T(8,128)(2,1)S(1)}, u32[]{:S(2)}, u32[]{:S(2)}) collective-permute-start(bf16[4,64,1792]{2,1,0:T(8,128)(2,1)S(1)} %convolution_convert_fusion), channel_id=1, source_target_pairs={{0,1},{1,0},{2,3},{3,2},{4,5},{5,4},{6,7},{7,6},{8,9},{9,8},{10,11... | collective-permute-start | bytes 2752520 | tf_op jit(solution)/shard_map/ppermute | solution.py:55
  120.0 14.8 %collective-permute-start.23 = (bf16[128,2048]{1,0:T(8,128)(2,1)S(1)}, bf16[128,2048]{1,0:T(8,128)(2,1)S(1)}, u32[]{:S(2)}, u32[]{:S(2)}) collective-permute-start(bf16[128,2048]{1,0:T(8,128)(2,1)S(1)} %dynamic-slice_bitcast_fusion.3), channel_id=1, source_target_pairs={{0,16},{8,24},{16,0},{24,8},{1,17},{9,25},{17,1},{25,9},{2,18},{10... | collective-permute-start | bytes 1572872 | tf_op jit(solution)/shard_map/ppermute | solution.py:55
  121.6 24.5 %collective-permute-start.25 = (bf16[128,2048]{1,0:T(8,128)(2,1)S(1)}, bf16[128,2048]{1,0:T(8,128)(2,1)S(1)}, u32[]{:S(2)}, u32[]{:S(2)}) collective-permute-start(bf16[128,2048]{1,0:T(8,128)(2,1)S(1)} %dynamic-slice_bitcast_fusion.2), channel_id=1, source_target_pairs={{0,16},{8,24},{16,0},{24,8},{1,17},{9,25},{17,1},{25,9},{2,18},{10... | collective-permute-start | bytes 1572872 | tf_op jit(solution)/shard_map/ppermute | solution.py:55
  126.8 33.2 %copy-start.2 = (f32[4,128,2048]{2,1,0:T(8,128)}, f32[4,128,2048]{2,1,0:T(8,128)S(1)}, u32[]{:S(2)}) copy-start(f32[4,128,2048]{2,1,0:T(8,128)S(1)} %fusion) | copy-start | bytes 12582916
  134.9 11.2 %copy-start.5 = (bf16[1,1024,896]{2,1,0:T(8,128)(2,1)S(1)}, bf16[1,1024,896]{2,1,0:T(8,128)(2,1)}, u32[]{:S(2)}) copy-start(bf16[1,1024,896]{2,1,0:T(8,128)(2,1)} %param.8) | copy-start | bytes 5505028
  135.1 7.3 %collective-permute-start.24 = (bf16[128,1024]{1,0:T(8,128)(2,1)S(1)}, bf16[128,1024]{1,0:T(8,128)(2,1)S(1)}, u32[]{:S(2)}, u32[]{:S(2)}) collective-permute-start(bf16[128,1024]{1,0:T(8,128)(2,1)S(1)} %fusion.38), channel_id=1, source_target_pairs={{0,8},{8,0},{16,24},{24,16},{1,9},{9,1},{17,25},{25,17},{2,10},{10... | collective-permute-start | bytes 786440 | tf_op jit(solution)/shard_map/ppermute | solution.py:55
  136.5 21.1 %collective-permute-start.28 = (bf16[128,2048]{1,0:T(8,128)(2,1)S(1)}, bf16[128,2048]{1,0:T(8,128)(2,1)S(1)}, u32[]{:S(2)}, u32[]{:S(2)}) collective-permute-start(bf16[128,2048]{1,0:T(8,128)(2,1)S(1)} %dynamic-slice_bitcast_fusion.1), channel_id=1, source_target_pairs={{0,16},{8,24},{16,0},{24,8},{1,17},{9,25},{17,1},{25,9},{2,18},{10... | collective-permute-start | bytes 1572872 | tf_op jit(solution)/shard_map/ppermute | solution.py:55
  146.1 1.5 copy-start.7
  148.4 3.3 %collective-permute-start.27 = (bf16[2,64,1792]{2,1,0:T(8,128)(2,1)S(1)}, bf16[2,64,1792]{2,1,0:T(8,128)(2,1)S(1)}, u32[]{:S(2)}, u32[]{:S(2)}) collective-permute-start(bf16[2,64,1792]{2,1,0:T(8,128)(2,1)S(1)} %get-tuple-element.193), channel_id=1, source_target_pairs={{0,1},{1,0},{2,3},{3,2},{4,5},{5,4},{6,7},{7,6},{8,9},{9,8},{10,11... | collective-permute-start | bytes 1376264 | tf_op jit(solution)/shard_map/ppermute | solution.py:55
  148.8 8.8 %collective-permute-start.26 = (bf16[128,1024]{1,0:T(8,128)(2,1)S(1)}, bf16[128,1024]{1,0:T(8,128)(2,1)S(1)}, u32[]{:S(2)}, u32[]{:S(2)}) collective-permute-start(bf16[128,1024]{1,0:T(8,128)(2,1)S(1)} %fusion.37), channel_id=1, source_target_pairs={{0,8},{8,0},{16,24},{24,16},{1,9},{9,1},{17,25},{25,17},{2,10},{10... | collective-permute-start | bytes 786440 | tf_op jit(solution)/shard_map/ppermute | solution.py:55
  150.2 22.4 %collective-permute-start.30 = (bf16[128,2048]{1,0:T(8,128)(2,1)S(1)}, bf16[128,2048]{1,0:T(8,128)(2,1)}, u32[]{:S(2)}, u32[]{:S(2)}) collective-permute-start(bf16[128,2048]{1,0:T(8,128)(2,1)S(1)} %dynamic-slice_bitcast_fusion), channel_id=1, source_target_pairs={{0,16},{8,24},{16,0},{24,8},{1,17},{9,25},{17,1},{25,9},{2,18},{10... | collective-permute-start | bytes 1572872 | tf_op jit(solution)/shard_map/ppermute | solution.py:55
  160.3 12.2 %collective-permute-start.29 = (bf16[128,1024]{1,0:T(8,128)(2,1)S(1)}, bf16[128,1024]{1,0:T(8,128)(2,1)}, u32[]{:S(2)}, u32[]{:S(2)}) collective-permute-start(bf16[128,1024]{1,0:T(8,128)(2,1)S(1)} %fusion.36), channel_id=1, source_target_pairs={{0,8},{8,0},{16,24},{24,16},{1,9},{9,1},{17,25},{25,17},{2,10},{10... | collective-permute-start | bytes 786440 | tf_op jit(solution)/shard_map/ppermute | solution.py:55
  162.9 16.6 %collective-permute-start.32 = (bf16[2,64,1792]{2,1,0:T(8,128)(2,1)}, bf16[2,64,1792]{2,1,0:T(8,128)(2,1)S(1)}, u32[]{:S(2)}, u32[]{:S(2)}) collective-permute-start(bf16[2,64,1792]{2,1,0:T(8,128)(2,1)} %get-tuple-element.191), channel_id=1, source_target_pairs={{0,1},{1,0},{2,3},{3,2},{4,5},{5,4},{6,7},{7,6},{8,9},{9,8},{10,11... | collective-permute-start | bytes 1376264 | tf_op jit(solution)/shard_map/ppermute | solution.py:55
  163.0 29.1 %collective-permute-start.33 = (bf16[2,128,1792]{2,1,0:T(8,128)(2,1)}, bf16[2,128,1792]{2,1,0:T(8,128)(2,1)S(1)}, u32[]{:S(2)}, u32[]{:S(2)}) collective-permute-start(bf16[2,128,1792]{2,1,0:T(8,128)(2,1)} %get-tuple-element.214), channel_id=1, source_target_pairs={{0,2},{1,3},{8,10},{9,11},{16,18},{17,19},{24,26},{25,27}} | collective-permute-start | bytes 2752520 | tf_op jit(solution)/shard_map/ppermute | solution.py:81
  171.6 20.5 %collective-permute-start.34 = (bf16[2,128,1792]{2,1,0:T(8,128)(2,1)}, bf16[2,128,1792]{2,1,0:T(8,128)(2,1)S(1)}, u32[]{:S(2)}, u32[]{:S(2)}) collective-permute-start(bf16[2,128,1792]{2,1,0:T(8,128)(2,1)} %get-tuple-element.214), channel_id=1, source_target_pairs={{6,4},{7,5},{14,12},{15,13},{22,20},{23,21},{30,28},{31,29}} | collective-permute-start | bytes 2752520 | tf_op jit(solution)/shard_map/ppermute | solution.py:81
  172.6 3.3 %copy-start.8 = (bf16[1024,896]{1,0:T(8,128)(2,1)S(1)}, bf16[1024,896]{1,0:T(8,128)(2,1)}, u32[]{:S(2)}) copy-start(bf16[1024,896]{1,0:T(8,128)(2,1)} %pad_maximum_fusion.1) | copy-start | bytes 5505028
  176.8 3.2 %collective-permute-start.35 = (bf16[2,64,1792]{2,1,0:T(8,128)(2,1)S(1)}, bf16[2,64,1792]{2,1,0:T(8,128)(2,1)S(1)}, u32[]{:S(2)}, u32[]{:S(2)}) collective-permute-start(bf16[2,64,1792]{2,1,0:T(8,128)(2,1)S(1)} %get-tuple-element.189), channel_id=1, source_target_pairs={{0,1},{1,0},{2,3},{3,2},{4,5},{5,4},{6,7},{7,6},{8,9},{9,8},{10,11... | collective-permute-start | bytes 1376264 | tf_op jit(solution)/shard_map/ppermute | solution.py:55
  178.7 15.1 %collective-permute-start.31 = (bf16[128,1024]{1,0:T(8,128)(2,1)S(1)}, bf16[128,1024]{1,0:T(8,128)(2,1)S(1)}, u32[]{:S(2)}, u32[]{:S(2)}) collective-permute-start(bf16[128,1024]{1,0:T(8,128)(2,1)S(1)} %fusion.35), channel_id=1, source_target_pairs={{0,8},{8,0},{16,24},{24,16},{1,9},{9,1},{17,25},{25,17},{2,10},{10... | collective-permute-start | bytes 786440 | tf_op jit(solution)/shard_map/ppermute | solution.py:55
  180.0 13.8 %copy-start = (f32[2,128,1792]{2,1,0:T(8,128)}, f32[2,128,1792]{2,1,0:T(8,128)S(1)}, u32[]{:S(2)}) copy-start(f32[2,128,1792]{2,1,0:T(8,128)S(1)} %fusion.23) | copy-start | bytes 5505028
  192.1 1.7 copy-start.6
  195.2 24.1 %collective-permute-start.37 = (bf16[2,128,1792]{2,1,0:T(8,128)(2,1)}, bf16[2,128,1792]{2,1,0:T(8,128)(2,1)S(1)}, u32[]{:S(2)}, u32[]{:S(2)}) collective-permute-start(bf16[2,128,1792]{2,1,0:T(8,128)(2,1)} %get-tuple-element.183), channel_id=1, source_target_pairs={{0,2},{1,3},{2,4},{3,5},{8,10},{9,11},{10,12},{11,13},{16,18},{17,... | collective-permute-start | bytes 2752520 | tf_op jit(solution)/shard_map/ppermute | solution.py:81
  199.6 19.7 %collective-permute-start.38 = (bf16[2,128,1792]{2,1,0:T(8,128)(2,1)}, bf16[2,128,1792]{2,1,0:T(8,128)(2,1)}, u32[]{:S(2)}, u32[]{:S(2)}) collective-permute-start(bf16[2,128,1792]{2,1,0:T(8,128)(2,1)} %get-tuple-element.182), channel_id=1, source_target_pairs={{4,2},{5,3},{6,4},{7,5},{12,10},{13,11},{14,12},{15,13},{20,18},{2... | collective-permute-start | bytes 2752520 | tf_op jit(solution)/shard_map/ppermute | solution.py:81
  202.1 2.6 collective-permute-start.36
  204.8 14.6 %copy-start.1 = (f32[2,128,1792]{2,1,0:T(8,128)S(1)}, f32[2,128,1792]{2,1,0:T(8,128)}, u32[]{:S(2)}) copy-start(f32[2,128,1792]{2,1,0:T(8,128)} %copy-done) | copy-start | bytes 5505028
  221.7 17.8 %collective-permute-start.39 = (bf16[128,1792]{1,0:T(8,128)(2,1)S(1)}, bf16[128,1792]{1,0:T(8,128)(2,1)S(1)}, u32[]{:S(2)}, u32[]{:S(2)}) collective-permute-start(bf16[128,1792]{1,0:T(8,128)(2,1)S(1)} %slice_bitcast_fusion.3), channel_id=1, source_target_pairs={{0,2},{1,3},{2,4},{3,5},{4,6},{5,7},{8,10},{9,11},{10,12},{11,13},... | collective-permute-start | bytes 1376264 | tf_op jit(solution)/shard_map/ppermute | solution.py:81
  231.2 12.5 %collective-permute-start.40 = (bf16[128,1792]{1,0:T(8,128)(2,1)S(1)}, bf16[128,1792]{1,0:T(8,128)(2,1)S(1)}, u32[]{:S(2)}, u32[]{:S(2)}) collective-permute-start(bf16[128,1792]{1,0:T(8,128)(2,1)S(1)} %slice_bitcast_fusion.2), channel_id=1, source_target_pairs={{2,0},{3,1},{4,2},{5,3},{6,4},{7,5},{10,8},{11,9},{12,10},{13,11},... | collective-permute-start | bytes 1376264 | tf_op jit(solution)/shard_map/ppermute | solution.py:81
  243.7 9.7 %collective-permute-start.41 = (bf16[128,1792]{1,0:T(8,128)(2,1)S(1)}, bf16[128,1792]{1,0:T(8,128)(2,1)S(1)}, u32[]{:S(2)}, u32[]{:S(2)}) collective-permute-start(bf16[128,1792]{1,0:T(8,128)(2,1)S(1)} %slice_bitcast_fusion.19), channel_id=1, source_target_pairs={{0,2},{1,3},{2,4},{3,5},{4,6},{5,7},{8,10},{9,11},{10,12},{11,13},... | collective-permute-start | bytes 1376264 | tf_op jit(solution)/shard_map/ppermute | solution.py:81
  246.0 11.6 %collective-permute-start.42 = (bf16[128,1792]{1,0:T(8,128)(2,1)S(1)}, bf16[128,1792]{1,0:T(8,128)(2,1)S(1)}, u32[]{:S(2)}, u32[]{:S(2)}) collective-permute-start(bf16[128,1792]{1,0:T(8,128)(2,1)S(1)} %slice_bitcast_fusion.18), channel_id=1, source_target_pairs={{2,0},{3,1},{4,2},{5,3},{6,4},{7,5},{10,8},{11,9},{12,10},{13,11},... | collective-permute-start | bytes 1376264 | tf_op jit(solution)/shard_map/ppermute | solution.py:81
  257.9 8.9 %collective-permute-start.43 = (bf16[128,1792]{1,0:T(8,128)(2,1)S(1)}, bf16[128,1792]{1,0:T(8,128)(2,1)S(1)}, u32[]{:S(2)}, u32[]{:S(2)}) collective-permute-start(bf16[128,1792]{1,0:T(8,128)(2,1)S(1)} %get-tuple-element.184), channel_id=1, source_target_pairs={{0,8},{8,0},{16,24},{24,16},{1,9},{9,1},{17,25},{25,17},{2,10},{10... | collective-permute-start | bytes 1376264 | tf_op jit(solution)/shard_map/ppermute | solution.py:55
  266.9 0.9 copy-start.11

commit v5 on v0

v5 whole, which is shorter than its diff:
```python
import jax
import jax.numpy as jnp
from jax import lax
from jax.sharding import PartitionSpec as P

BF = jnp.bfloat16
F32 = jnp.float32
CUTS = ((0, 3), (3, 6), (6, 7))


def gathered(tokens, gate_up, down_proj, expert_ids, gate_weights):
    owners = lax.axis_size("expert")
    tok_rows = tokens.shape[0]
    width = tokens.shape[1]
    hidden_units = down_proj.shape[1]
    slots = 4 * tok_rows // owners
    total_rows = owners * slots
    owner_ids = jnp.arange(owners, dtype=jnp.int32)
    matches = expert_ids[:, :, None] == owner_ids[None, None, :]
    hits = jnp.sum(matches.astype(jnp.int32), axis=1)
    pick_weight = jnp.sum(
        jnp.where(matches, gate_weights[:, :, None].astype(F32), 0.0), axis=1
    )
    before = jnp.cumsum(hits, axis=0) - hits
    target = jnp.where(hits > 0, owner_ids[None, :] * slots + before, -1)
    slot_owner = jnp.arange(total_rows, dtype=jnp.int32) // slots
    slot_ids = jnp.arange(total_rows, dtype=jnp.int32)
    placed = jnp.take(target, slot_owner, axis=1) == slot_ids[None, :]
    place_bf = placed.astype(BF)
    outgoing = jnp.dot(place_bf.T, tokens, preferred_element_type=F32).astype(BF)
    arrived = lax.all_to_all(
        outgoing.reshape(owners, slots, width), "expert", split_axis=0, concat_axis=0, tiled=True
    )
    rows = arrived.reshape(total_rows, width)
    gu = jnp.dot(
        rows,
        lax.all_gather(gate_up, "dp", axis=1, tiled=True)[0],
        preferred_element_type=F32,
    )
    hidden = (jax.nn.silu(gu[:, :hidden_units]) * gu[:, hidden_units:]).astype(BF)
    result = jnp.dot(
        hidden,
        lax.all_gather(down_proj, "dp", axis=2, tiled=True)[0],
        preferred_element_type=F32,
    ).astype(BF)
    returned = lax.all_to_all(
        result.reshape(owners, slots, width), "expert", split_axis=0, concat_axis=0, tiled=True
    )
    weighted = (place_bf.astype(F32) * jnp.take(pick_weight, slot_owner, axis=1)).astype(BF)
    mixed = jnp.dot(weighted, returned.reshape(total_rows, width), preferred_element_type=F32)
    return mixed.astype(BF)


def paired(tokens, gate_up, down_proj, expert_ids, gate_weights):
    owners = lax.axis_size("expert")
    chips = owners // 2
    tok = tokens.shape[0]
    top = expert_ids.shape[1]
    quarter = gate_up.shape[1]
    half = 2 * quarter
    ff = down_proj.shape[1]
    slots = 4 * tok // owners
    chunk = 2 * slots
    d = lax.axis_index("dp")
    e = lax.axis_index("expert")
    gate, down = gate_up[0], down_proj[0]
    together = lax.optimization_barrier

    def send(value, along=0, flip=0, core=0):
        return lax.ppermute(
            value,
            ("dp", "expert"),
            [
                (i * owners + j, (i ^ flip) * owners + ((j ^ core) + 2 * along) % owners)
                for i in range(4)
                for j in range(owners)
            ],
        )

    def depths(r):
        return lax.dynamic_slice_in_dim(tokens, (d ^ r) * quarter, quarter, axis=1)

    info = jnp.concatenate([expert_ids.astype(BF), gate_weights], axis=1)
    first = jnp.concatenate([depths(0), depths(1), info], axis=1)
    second = jnp.concatenate([depths(2), depths(3), info], axis=1)
    gate_x = [
        send(gate[quarter * lo // 7 : quarter * hi // 7], flip=1) for lo, hi in CUTS
    ]
    down_y = send(down, flip=2)

    seen = [{0: first, 1: send(first, 1)}, {1: send(second, 1, 2), 0: send(second, 0, 2)}]
    seen[0][3], seen[1][3] = send(first, -1), send(second, -1, 2)
    seen[0][1], seen[1][1], gate_x[0] = together((seen[0][1], seen[1][1], gate_x[0]))
    seen[0][2], seen[1][2] = send(seen[0][1], 1), send(seen[1][1], 1)
    seen, gate_x[1], down_y = together((seen, gate_x[1], down_y))

    chosen = jnp.stack([e, e ^ 1]).astype(jnp.int32)
    earlier = jnp.triu(jnp.ones((tok, tok), BF), 1)

    def places(info):
        matches = info[..., :top].astype(jnp.int32)[..., None] == chosen
        hits = jnp.any(matches, axis=2).transpose(0, 2, 1)
        weight = jnp.sum(jnp.where(matches, info[..., top:, None].astype(F32), 0.0), axis=2)
        rank = jnp.dot(hits.astype(BF), earlier, preferred_element_type=F32)
        rank = jnp.where(hits, rank, -1.0)
        place = (rank[..., None, :] == jnp.arange(slots, dtype=F32)[:, None]).astype(BF)
        pay = place * weight.transpose(0, 2, 1)[..., None, :].astype(BF)
        return place, pay.reshape(chips, chunk, tok)

    infos = [jnp.stack([seen[g][k][:, half:] for k in range(chips)]) for g in range(2)]
    helds = [jnp.stack([seen[g][k][:, :half] for k in range(chips)]) for g in range(2)]
    info_x = send(infos[0], flip=1)
    place0, pay0 = places(infos[0])
    place1, _ = places(infos[1])
    place1, gate_x[2] = together((place1, gate_x[2]))

    def choose(place, held):
        def of(expert):
            return jnp.einsum(
                "zst,ztk->zsk", place[:, expert], held, preferred_element_type=F32
            ).astype(BF)

        other = send(of(1), core=1)
        return jnp.concatenate([of(0), other], axis=1).reshape(-1, half)

    weights = jnp.concatenate([gate, *gate_x])

    def product(rows):
        return jnp.dot(rows, weights, preferred_element_type=F32).reshape(chips, chunk, 2 * ff)

    order = (2, 1, 3, 0)
    sent = product(choose(place1, helds[1])).astype(BF)
    sent, place0 = together((sent, place0))
    part = [send(sent[k], flip=2) for k in order]
    near = product(choose(place0, helds[0]))
    pay = jnp.stack([pay0, places(info_x)[1]])

    hidden, away, out = {}, {}, {}

    def finish(q, came):
        gu = near[order[q]] + came.astype(F32)
        own = (jax.nn.silu(gu[:, :ff]) * gu[:, ff:]).astype(BF)
        hidden[q] = (own, send(own, flip=1))

    def down_product(q):
        own = hidden[q][0]
        if q + 1 < chips:
            own, part[q + 1] = together((own, part[q + 1]))
        joined = jnp.concatenate([own, hidden[q][1]])
        value = jnp.concatenate(
            [jnp.dot(joined, w, preferred_element_type=F32).astype(BF) for w in (down, down_y)],
            axis=1,
        ).reshape(2, 2, slots, half)
        out[q], away[q] = value[:, 0], value[:, 1]

    def weigh(q, came):
        rows = jnp.concatenate([out[q], came], axis=1)
        return jnp.einsum("gst,gsk->gtk", pay[:, order[q]], rows, preferred_element_type=F32)

    def before_down(q, value):
        own, value = together((hidden[q][0], value))
        hidden[q] = (own, hidden[q][1])
        return value

    finish(0, part[0])
    down_product(0)
    away[0], part[1] = together((away[0], part[1]))
    finish(1, part[1])
    term = before_down(1, weigh(0, send(away[0], core=1)).astype(BF))
    middle = send(term, 1)
    down_product(1)
    away[1], part[2] = together((away[1], part[2]))
    finish(2, part[2])
    term = weigh(1, before_down(2, send(away[1], core=1))).astype(BF)
    back = [send(term[0], -1), send(term[1], -1, 1)]
    middle = before_down(2, middle)
    down_product(2)
    away[2], part[3] = together((away[2], part[3]))
    finish(3, part[3])
    term = (weigh(2, before_down(3, send(away[2], core=1))) + middle.astype(F32)).astype(BF)
    forth = [send(term[0], 1), send(term[1], 1, 1)]
    back[0] = before_down(3, back[0])
    down_product(3)
    term = weigh(3, send(away[3], core=1))
    theirs = send(term[1].astype(BF), flip=1)
    mine = (term[0] + back[0].astype(F32) + forth[0].astype(F32)).astype(BF)
    far = (theirs.astype(F32) + back[1].astype(F32) + forth[1].astype(F32)).astype(BF)

    mixed = jnp.zeros(tokens.shape, BF)
    for r, piece in enumerate(
        [mine[:, :quarter], far[:, :quarter], mine[:, quarter:], far[:, quarter:]]
    ):
        mixed = lax.dynamic_update_slice_in_dim(mixed, piece, (d ^ r) * quarter, axis=1)
    return mixed


def solution(mesh):
    placed = (
        P(("dp", "expert"), None),
        P("expert", "dp", None),
        P("expert", None, "dp"),
        P(("dp", "expert"), None),
        P(("dp", "expert"), None),
    )
    short = mesh.shape["expert"] == 8 and mesh.shape["dp"] == 4
    return jax.shard_map(
        paired if short else gathered,
        mesh=mesh,
        in_specs=placed,
        out_specs=P(("dp", "expert"), None),
        check_vma=False,
    )
```

time: 341 us -> 262 us (0.77)
  blocking collectives: 89 us -> 0 us
  waiting for transfers between devices: 203 us -> 154 us
  starting transfers between devices: 4.77 us -> 37.7 us
  local copies, waits for them, and re-layouts: 2.23 us -> 26.8 us
  between operations: 13.5 us -> 0.93 us
  matrix products: 28.5 us -> 35.2 us
  other arithmetic: 0.45 us -> 6.01 us
    ppermute x0 -> x32, waiting for transfers between devices: none -> 154 us  [send(): lax.ppermute(value, ('dp', 'expert'), [(i * owners + j, (i ^ flip) * owne...]
    all_gather x2 -> x0, waiting for transfers between devices: 119 us -> none  [the longest x1 67.3 us: local(): lax.all_gather(down_proj, 'dp', axis=2, tiled=True)[0]]
    all_to_all x1 -> x0, blocking collectives: 89 us -> none  [local(): lax.all_to_all(outgoing.reshape(owners, slots, width), 'expert', split_ax...]
    all_to_all x1 -> x0, waiting for transfers between devices: 81.8 us -> none  [local(): lax.all_to_all(result.reshape(owners, slots, width), 'expert', split_axis...]
    ppermute x0 -> x32, starting transfers between devices: none -> 37.7 us  [send(): lax.ppermute(value, ('dp', 'expert'), [(i * owners + j, (i ^ flip) * owne...]
    another operation x1 -> x16, local copies, waits for them, and re-layouts: 0.05 us -> 10 us  [the longest x4 6.32 us: paired(): jnp.stack([seen[g][k][:, :half] for k in range(chips)])]
    dot_general x4 -> x21, matrix products: 28.5 us -> 35.2 us  [the longest x8 17.9 us: down_product(): jnp.dot(joined, w, preferred_element_type=F32).astype(BF)]
    unnamed x6 -> x69, local copies, waits for them, and re-layouts: 0.01 us -> 6.07 us
  transfers between devices with their start and end apart: 3 -> 32, of which waited for: 3 -> 16; matrix products, arithmetic and copies ran while one was open for 5% -> 19% of each run, Pallas kernels for 0% -> 0%
where the time goes in v5:
time: 262 us; the launch traced here: 261 us
  waiting for transfers between devices  154 us (59%)
  starting transfers between devices  37.7 us (14%)
  matrix products  35.2 us (13%)
  local copies, waits for them, and re-layouts  26.8 us (10%)
  other arithmetic  6.01 us (2%)
    ppermute x32, waiting for transfers between devices, send(): lax.ppermute(value, ('dp', 'expert'), [(i * owners + j, (i ^ flip) * owne...  154 us
    ppermute x32, starting transfers between devices, send(): lax.ppermute(value, ('dp', 'expert'), [(i * owners + j, (i ^ flip) * owne...  37.7 us
    dot_general x8, matrix products, down_product(): jnp.dot(joined, w, preferred_element_type=F32).astype(BF)  17.9 us
    dot_general x2, matrix products, product(): jnp.dot(rows, weights, preferred_element_type=F32)  11.5 us
    another operation x4, local copies, waits for them, and re-layouts, paired(): jnp.stack([seen[g][k][:, :half] for k in range(chips)])  6.32 us
    unnamed x69, local copies, waits for them, and re-layouts  6.07 us
  transfers between devices with their start and end apart: 32, of which 16 were waited for; matrix products, arithmetic and copies ran while one was open for 19% of the time, Pallas kernels for 0%

profile of v5, /device:TPU:0, one launch (start us, length us, event | category | flops | bytes accessed | tf_op | source)
XLA Modules:
  0.0 260.9 jit_solution(13845297106437655711)
XLA Ops:
  0.0 3.5 %slice_bitcast_fusion = (bf16[384,2048]{1,0:T(8,128)(2,1)S(1)}, bf16[384,2048]{1,0:T(8,128)(2,1)}) fusion(bf16[1,896,2048]{2,1,0:T(8,128)(2,1)} %param.6), kind=kLoop, calls=%fused_computation.17 | loop fusion | bytes 6291456 | tf_op jit(solution)/shard_map/slice | solution.py:87
  3.5 2.9 %collective-permute-start.2 = (bf16[384,2048]{1,0:T(8,128)(2,1)}, bf16[384,2048]{1,0:T(8,128)(2,1)}, u32[]{:S(2)}, u32[]{:S(2)}) collective-permute-start(bf16[384,2048]{1,0:T(8,128)(2,1)} %get-tuple-element.89), channel_id=1, source_target_pairs={{0,8},{1,9},{2,10},{3,11},{4,12},{5,13},{6,14},{7,15},{8,0},{9,1},... | collective-permute-start | bytes 4718600 | tf_op jit(solution)/shard_map/ppermute | solution.py:70
  6.4 1.5 collective-permute-start.9
  8.9 0.9 concatenate.55
  9.7 1.5 collective-permute-start.1
  11.4 1.6 collective-permute-start
  13.0 13.9 %collective-permute-done.1 = bf16[128,1808]{1,0:T(8,128)(2,1)} collective-permute-done((bf16[128,1808]{1,0:T(8,128)(2,1)}, bf16[128,1808]{1,0:T(8,128)(2,1)}, u32[]{:S(2)}, u32[]{:S(2)}) %collective-permute-start.1) | collective-permute-done | bytes 462880 | tf_op jit(solution)/shard_map/ppermute | solution.py:70
  27.3 7.3 %collective-permute-done = bf16[128,1808]{1,0:T(8,128)(2,1)} collective-permute-done((bf16[128,1808]{1,0:T(8,128)(2,1)S(1)}, bf16[128,1808]{1,0:T(8,128)(2,1)}, u32[]{:S(2)}, u32[]{:S(2)}) %collective-permute-start) | collective-permute-done | bytes 462880 | tf_op jit(solution)/shard_map/ppermute | solution.py:70
  34.6 2.6 %collective-permute-start.7 = (bf16[128,1808]{1,0:T(8,128)(2,1)}, bf16[128,1808]{1,0:T(8,128)(2,1)S(1)}, u32[]{:S(2)}, u32[]{:S(2)}) collective-permute-start(bf16[128,1808]{1,0:T(8,128)(2,1)} %concatenate.55), channel_id=1, source_target_pairs={{0,22},{1,23},{2,16},{3,17},{4,18},{5,19},{6,20},{7,21},{8,30},{9,... | collective-permute-start | bytes 1388552 | tf_op jit(solution)/shard_map/ppermute | solution.py:70
  37.9 4.1 %collective-permute-done.2 = bf16[384,2048]{1,0:T(8,128)(2,1)} collective-permute-done((bf16[384,2048]{1,0:T(8,128)(2,1)}, bf16[384,2048]{1,0:T(8,128)(2,1)}, u32[]{:S(2)}, u32[]{:S(2)}) %collective-permute-start.2) | collective-permute-done | bytes 1572896 | tf_op jit(solution)/shard_map/ppermute | solution.py:70
  42.0 4.2 %collective-permute-start.4 = (bf16[128,1808]{1,0:T(8,128)(2,1)S(1)}, bf16[128,1808]{1,0:T(8,128)(2,1)S(1)}, u32[]{:S(2)}, u32[]{:S(2)}) collective-permute-start(bf16[128,1808]{1,0:T(8,128)(2,1)S(1)} %concatenate.54), channel_id=1, source_target_pairs={{0,6},{1,7},{2,0},{3,1},{4,2},{5,3},{6,4},{7,5},{8,14},{9,15},{10,... | collective-permute-start | bytes 1388552 | tf_op jit(solution)/shard_map/ppermute | solution.py:70
  46.1 33.7 %collective-permute-done.5 = bf16[128,1808]{1,0:T(8,128)(2,1)} collective-permute-done((bf16[128,1808]{1,0:T(8,128)(2,1)}, bf16[128,1808]{1,0:T(8,128)(2,1)}, u32[]{:S(2)}, u32[]{:S(2)}) %collective-permute-start.5) | collective-permute-done | bytes 462880 | tf_op jit(solution)/shard_map/ppermute | solution.py:70
  79.8 1.6 collective-permute-start.3
  81.4 0.8 copy-done.10
  82.2 1.6 collective-permute-start.6
  83.8 1.1 slice_bitcast_fusion.7
  85.5 10.6 %collective-permute-done.3 = bf16[128,1808]{1,0:T(8,128)(2,1)} collective-permute-done((bf16[128,1808]{1,0:T(8,128)(2,1)}, bf16[128,1808]{1,0:T(8,128)(2,1)}, u32[]{:S(2)}, u32[]{:S(2)}) %collective-permute-start.3) | collective-permute-done | bytes 462880 | tf_op jit(solution)/shard_map/ppermute | solution.py:70
  96.1 8.2 %collective-permute-done.6 = bf16[128,1808]{1,0:T(8,128)(2,1)} collective-permute-done((bf16[128,1808]{1,0:T(8,128)(2,1)}, bf16[128,1808]{1,0:T(8,128)(2,1)}, u32[]{:S(2)}, u32[]{:S(2)}) %collective-permute-start.6) | collective-permute-done | bytes 462880 | tf_op jit(solution)/shard_map/ppermute | solution.py:70
  104.3 0.8 slice_bitcast_fusion.34
  105.2 0.8 slice_bitcast_fusion.32
  107.4 0.8 slice_bitcast_fusion.30
  108.2 1.2 slice_bitcast_fusion.26
  109.4 0.8 slice_bitcast_fusion.28
  110.2 2.0 slice_bitcast_fusion.24
  112.2 1.9 slice_bitcast_fusion.22
  115.1 1.3 compare_reduce_fusion
  116.7 1.5 convolution_convert_fusion.2
  118.2 1.1 slice_bitcast_fusion.20
  120.7 1.1 copy-done.2
  121.8 5.7 %fusion.2 = bf16[4,128,2048]{2,1,0:T(8,128)(2,1)S(1)} fusion(bf16[4,64,1792]{2,1,0:T(8,128)(2,1)S(1)} %collective-permute-done.12, bf16[4,64,1792]{2,1,0:T(8,128)(2,1)S(1)} %convolution_convert_fusion.3, bf16[128,2048]{1,0:T(8,128)(2,1)} %collective-permute-done.11, bf16[384,2048]{1,0:T(8,128)(2,1)} %collective-permute-done.8, ...), kind=kOutput, calls=%fused_computation.3 | convolution fusion | flops 3792175104 | bytes 11272192 | tf_op jit(solution)/shard_map/dot_general | solution.py:129
  127.6 1.4 convolution_convert_fusion
  130.7 0.8 fusion.57
  131.6 0.8 copy.77
  132.4 0.8 copy.81
  133.4 1.2 slice_bitcast_fusion.3
  134.6 1.5 collective-permute-start.14
  137.2 1.9 copy-done.3
  139.1 5.8 %fusion.8 = f32[512,2048]{1,0:T(8,128)S(1)} fusion(bf16[512,1792]{1,0:T(8,128)(2,1)S(1)} %bitcast.185, bf16[128,2048]{1,0:T(8,128)(2,1)} %collective-permute-done.11, bf16[384,2048]{1,0:T(8,128)(2,1)} %collective-permute-done.8, bf16[384,2048]{1,0:T(8,128)(2,1)} %collective-permute-done.2, bf16[896,2048]{1,0:T(8,128)(2,1)S(1)} %bitcast.180), kind=kOutput, calls=%fused_computation.27 | convolution fusion | flops 3787456512 | bytes 13369344 | tf_op jit(solution)/shard_map/dot_general | solution.py:129
  145.0 4.4 %collective-permute-done.14 = bf16[128,2048]{1,0:T(8,128)(2,1)S(1)} collective-permute-done((bf16[128,2048]{1,0:T(8,128)(2,1)S(1)}, bf16[128,2048]{1,0:T(8,128)(2,1)S(1)}, u32[]{:S(2)}, u32[]{:S(2)}) %collective-permute-start.14) | collective-permute-done | bytes 524320 | tf_op jit(solution)/shard_map/ppermute | solution.py:70
  149.7 1.5 collective-permute-start.16
  151.5 1.6 collective-permute-start.18
  153.1 7.5 %collective-permute-done.15 = bf16[128,2048]{1,0:T(8,128)(2,1)S(1)} collective-permute-done((bf16[128,2048]{1,0:T(8,128)(2,1)}, bf16[128,2048]{1,0:T(8,128)(2,1)S(1)}, u32[]{:S(2)}, u32[]{:S(2)}) %collective-permute-start.15) | collective-permute-done | bytes 524320 | tf_op jit(solution)/shard_map/ppermute | solution.py:70
  160.6 2.2 convolution_convert_fusion.13
  162.9 2.4 convolution_convert_fusion.12
  165.9 1.5 collective-permute-start.19
  167.5 1.6 collective-permute-start.22
  169.5 2.0 collective-permute-done.18
  171.5 3.1 %collective-permute-done.19 = bf16[128,1024]{1,0:T(8,128)(2,1)S(1)} collective-permute-done((bf16[128,1024]{1,0:T(8,128)(2,1)S(1)}, bf16[128,1024]{1,0:T(8,128)(2,1)S(1)}, u32[]{:S(2)}, u32[]{:S(2)}) %collective-permute-start.19) | collective-permute-done | bytes 262176 | tf_op jit(solution)/shard_map/ppermute | solution.py:70
  174.6 2.2 convolution_convert_fusion.10
  176.9 2.2 convolution_convert_fusion.11
  179.7 1.5 collective-permute-start.23
  181.7 4.0 %collective-permute-start.25 = (bf16[128,1792]{1,0:T(8,128)(2,1)S(1)}, bf16[128,1792]{1,0:T(8,128)(2,1)S(1)}, u32[]{:S(2)}, u32[]{:S(2)}) collective-permute-start(bf16[128,1792]{1,0:T(8,128)(2,1)S(1)} %get-tuple-element.95), channel_id=1, source_target_pairs={{0,6},{1,7},{2,0},{3,1},{4,2},{5,3},{6,4},{7,5},{8,14},{9,15},{10,... | collective-permute-start | bytes 1376264 | tf_op jit(solution)/shard_map/ppermute | solution.py:70
  185.7 18.6 %collective-permute-done.21 = bf16[2,128,1792]{2,1,0:T(8,128)(2,1)S(1)} collective-permute-done((bf16[2,128,1792]{2,1,0:T(8,128)(2,1)S(1)}, bf16[2,128,1792]{2,1,0:T(8,128)(2,1)S(1)}, u32[]{:S(2)}, u32[]{:S(2)}) %collective-permute-start.21) | collective-permute-done | bytes 917536 | tf_op jit(solution)/shard_map/ppermute | solution.py:70
  204.4 2.2 convolution_convert_fusion.8
  206.7 2.2 convolution_convert_fusion.9
  209.4 1.6 collective-permute-start.26
  211.0 2.7 %collective-permute-done.25 = bf16[128,1792]{1,0:T(8,128)(2,1)S(1)} collective-permute-done((bf16[128,1792]{1,0:T(8,128)(2,1)S(1)}, bf16[128,1792]{1,0:T(8,128)(2,1)S(1)}, u32[]{:S(2)}, u32[]{:S(2)}) %collective-permute-start.25) | collective-permute-done | bytes 458784 | tf_op jit(solution)/shard_map/ppermute | solution.py:70
  213.7 14.3 %collective-permute-done.26 = bf16[128,1024]{1,0:T(8,128)(2,1)S(1)} collective-permute-done((bf16[128,1024]{1,0:T(8,128)(2,1)S(1)}, bf16[128,1024]{1,0:T(8,128)(2,1)S(1)}, u32[]{:S(2)}, u32[]{:S(2)}) %collective-permute-start.26) | collective-permute-done | bytes 262176 | tf_op jit(solution)/shard_map/ppermute | solution.py:70
  228.0 2.2 convolution_convert_fusion.6
  230.2 2.2 convolution_convert_fusion.7
  233.3 1.2 collective-permute-done.27
  234.9 1.6 collective-permute-start.29
  236.5 22.2 %collective-permute-done.28 = bf16[128,1792]{1,0:T(8,128)(2,1)S(1)} collective-permute-done((bf16[128,1792]{1,0:T(8,128)(2,1)S(1)}, bf16[128,1792]{1,0:T(8,128)(2,1)S(1)}, u32[]{:S(2)}, u32[]{:S(2)}) %collective-permute-start.28) | collective-permute-done | bytes 458784 | tf_op jit(solution)/shard_map/ppermute | solution.py:70
  259.3 0.9 copy-done.4
  (165 shorter events, 15.3 us)
Async XLA Ops:
  0.0 8.5 %copy-start.27 = (s32[128,8]{0,1:T(8,128)S(1)}, s32[128,8]{0,1:T(8,128)}, u32[]{:S(2)}) copy-start(s32[128,8]{0,1:T(8,128)} %param.8) | copy-start | bytes 12292
  0.0 8.6 %copy-start.29 = (bf16[128,8]{0,1:T(8,128)(2,1)S(1)}, bf16[128,8]{0,1:T(8,128)(2,1)}, u32[]{:S(2)}) copy-start(bf16[128,8]{0,1:T(8,128)(2,1)} %param.9) | copy-start | bytes 6148
  0.0 8.8 %copy-start.5 = (bf16[128,3584]{1,0:T(8,128)(2,1)S(1)}, bf16[128,3584]{1,0:T(8,128)(2,1)}, u32[]{:S(2)}) copy-start(bf16[128,3584]{1,0:T(8,128)(2,1)} %param.5) | copy-start | bytes 2752516
  3.5 38.5 %collective-permute-start.2 = (bf16[384,2048]{1,0:T(8,128)(2,1)}, bf16[384,2048]{1,0:T(8,128)(2,1)}, u32[]{:S(2)}, u32[]{:S(2)}) collective-permute-start(bf16[384,2048]{1,0:T(8,128)(2,1)} %get-tuple-element.89), channel_id=1, source_target_pairs={{0,8},{1,9},{2,10},{3,11},{4,12},{5,13},{6,14},{7,15},{8,0},{9,1},... | collective-permute-start | bytes 4718600 | tf_op jit(solution)/shard_map/ppermute | solution.py:70
  6.4 79.0 %collective-permute-start.9 = (bf16[1024,896]{1,0:T(8,128)(2,1)}, bf16[1024,896]{1,0:T(8,128)(2,1)}, u32[]{:S(2)}, u32[]{:S(2)}) collective-permute-start(bf16[1024,896]{1,0:T(8,128)(2,1)} %bitcast.2), channel_id=1, source_target_pairs={{0,16},{1,17},{2,18},{3,19},{4,20},{5,21},{6,22},{7,23},{8,24},{9,... | collective-permute-start | bytes 5505032 | tf_op jit(solution)/shard_map/ppermute | solution.py:70
  8.0 77.5 %collective-permute-start.8 = (bf16[384,2048]{1,0:T(8,128)(2,1)S(1)}, bf16[384,2048]{1,0:T(8,128)(2,1)}, u32[]{:S(2)}, u32[]{:S(2)}) collective-permute-start(bf16[384,2048]{1,0:T(8,128)(2,1)S(1)} %get-tuple-element.88), channel_id=1, source_target_pairs={{0,8},{1,9},{2,10},{3,11},{4,12},{5,13},{6,14},{7,15},{8,0},{9,1},... | collective-permute-start | bytes 4718600 | tf_op jit(solution)/shard_map/ppermute | solution.py:70
  9.7 17.2 %collective-permute-start.1 = (bf16[128,1808]{1,0:T(8,128)(2,1)}, bf16[128,1808]{1,0:T(8,128)(2,1)}, u32[]{:S(2)}, u32[]{:S(2)}) collective-permute-start(bf16[128,1808]{1,0:T(8,128)(2,1)} %concatenate.55), channel_id=1, source_target_pairs={{0,18},{1,19},{2,20},{3,21},{4,22},{5,23},{6,16},{7,17},{8,26},{9,... | collective-permute-start | bytes 1388552 | tf_op jit(solution)/shard_map/ppermute | solution.py:70
  11.4 23.2 %collective-permute-start = (bf16[128,1808]{1,0:T(8,128)(2,1)S(1)}, bf16[128,1808]{1,0:T(8,128)(2,1)}, u32[]{:S(2)}, u32[]{:S(2)}) collective-permute-start(bf16[128,1808]{1,0:T(8,128)(2,1)S(1)} %concatenate.54), channel_id=1, source_target_pairs={{0,2},{1,3},{2,4},{3,5},{4,6},{5,7},{6,0},{7,1},{8,10},{9,11},{10,... | collective-permute-start | bytes 1388552 | tf_op jit(solution)/shard_map/ppermute | solution.py:70
  27.0 52.9 %collective-permute-start.5 = (bf16[128,1808]{1,0:T(8,128)(2,1)}, bf16[128,1808]{1,0:T(8,128)(2,1)}, u32[]{:S(2)}, u32[]{:S(2)}) collective-permute-start(bf16[128,1808]{1,0:T(8,128)(2,1)} %concatenate.55), channel_id=1, source_target_pairs={{0,16},{1,17},{2,18},{3,19},{4,20},{5,21},{6,22},{7,23},{8,24},{9,... | collective-permute-start | bytes 1388552 | tf_op jit(solution)/shard_map/ppermute | solution.py:70
  34.6 46.8 %collective-permute-start.7 = (bf16[128,1808]{1,0:T(8,128)(2,1)}, bf16[128,1808]{1,0:T(8,128)(2,1)S(1)}, u32[]{:S(2)}, u32[]{:S(2)}) collective-permute-start(bf16[128,1808]{1,0:T(8,128)(2,1)} %concatenate.55), channel_id=1, source_target_pairs={{0,22},{1,23},{2,16},{3,17},{4,18},{5,19},{6,20},{7,21},{8,30},{9,... | collective-permute-start | bytes 1388552 | tf_op jit(solution)/shard_map/ppermute | solution.py:70
  42.0 42.9 %collective-permute-start.4 = (bf16[128,1808]{1,0:T(8,128)(2,1)S(1)}, bf16[128,1808]{1,0:T(8,128)(2,1)S(1)}, u32[]{:S(2)}, u32[]{:S(2)}) collective-permute-start(bf16[128,1808]{1,0:T(8,128)(2,1)S(1)} %concatenate.54), channel_id=1, source_target_pairs={{0,6},{1,7},{2,0},{3,1},{4,2},{5,3},{6,4},{7,5},{8,14},{9,15},{10,... | collective-permute-start | bytes 1388552 | tf_op jit(solution)/shard_map/ppermute | solution.py:70
  79.8 16.3 %collective-permute-start.3 = (bf16[128,1808]{1,0:T(8,128)(2,1)}, bf16[128,1808]{1,0:T(8,128)(2,1)}, u32[]{:S(2)}, u32[]{:S(2)}) collective-permute-start(bf16[128,1808]{1,0:T(8,128)(2,1)} %collective-permute-done), channel_id=1, source_target_pairs={{0,2},{1,3},{2,4},{3,5},{4,6},{5,7},{6,0},{7,1},{8,10},{9,11},{10,... | collective-permute-start | bytes 1388552 | tf_op jit(solution)/shard_map/ppermute | solution.py:70
  81.4 0.8 copy-start.10
  82.2 22.1 %collective-permute-start.6 = (bf16[128,1808]{1,0:T(8,128)(2,1)}, bf16[128,1808]{1,0:T(8,128)(2,1)}, u32[]{:S(2)}, u32[]{:S(2)}) collective-permute-start(bf16[128,1808]{1,0:T(8,128)(2,1)} %collective-permute-done.1), channel_id=1, source_target_pairs={{0,2},{1,3},{2,4},{3,5},{4,6},{5,7},{6,0},{7,1},{8,10},{9,11},{10,... | collective-permute-start | bytes 1388552 | tf_op jit(solution)/shard_map/ppermute | solution.py:70
  84.9 31.8 %collective-permute-start.11 = (bf16[128,2048]{1,0:T(8,128)(2,1)S(1)}, bf16[128,2048]{1,0:T(8,128)(2,1)}, u32[]{:S(2)}, u32[]{:S(2)}) collective-permute-start(bf16[128,2048]{1,0:T(8,128)(2,1)S(1)} %slice_bitcast_fusion.7), channel_id=1, source_target_pairs={{0,8},{1,9},{2,10},{3,11},{4,12},{5,13},{6,14},{7,15},{8,0},{9,1},... | collective-permute-start | bytes 1572872 | tf_op jit(solution)/shard_map/ppermute | solution.py:70
  85.5 24.0 %copy-start.11 = (bf16[128,1808]{1,0:T(8,128)(2,1)S(1)}, bf16[128,1808]{1,0:T(8,128)(2,1)}, u32[]{:S(2)}) copy-start(bf16[128,1808]{1,0:T(8,128)(2,1)} %copy-done.10) | copy-start | bytes 1388548
  106.2 8.3 %collective-permute-start.10 = (bf16[4,128,16]{1,2,0:T(8,128)(2,1)S(1)}, bf16[4,128,16]{1,2,0:T(8,128)(2,1)S(1)}, u32[]{:S(2)}, u32[]{:S(2)}) collective-permute-start(bf16[4,128,16]{1,2,0:T(8,128)(2,1)S(1)} %pad_maximum_fusion.15), channel_id=1, source_target_pairs={{0,8},{1,9},{2,10},{3,11},{4,12},{5,13},{6,14},{7,15},{8,0},{9,1},... | collective-permute-start | bytes 49160 | tf_op jit(solution)/shard_map/ppermute | solution.py:70
  112.2 4.4 %copy-start.20 = (bf16[1,128,1792]{2,1,0:T(8,128)(2,1)S(1)}, bf16[1,128,1792]{2,1,0:T(8,128)(2,1)}, u32[]{:S(2)}) copy-start(bf16[1,128,1792]{2,1,0:T(8,128)(2,1)} %get-tuple-element.120) | copy-start | bytes 1376260
  114.2 13.4 %copy-start.12 = (bf16[1,128,1792]{2,1,0:T(8,128)(2,1)}, bf16[1,128,1792]{2,1,0:T(8,128)(2,1)S(1)}, u32[]{:S(2)}) copy-start(bf16[1,128,1792]{2,1,0:T(8,128)(2,1)S(1)} %get-tuple-element.118) | copy-start | bytes 1376260
  115.1 3.0 %copy-start.22 = (s32[4,128,8]{1,2,0:T(8,128)}, s32[4,128,8]{1,2,0:T(8,128)S(1)}, u32[]{:S(2)}) copy-start(s32[4,128,8]{1,2,0:T(8,128)S(1)} %get-tuple-element.113) | copy-start | bytes 49156
  118.2 1.4 copy-start.21
  118.2 2.5 collective-permute-start.12
  119.4 8.2 %copy-start.16 = (bf16[1,128,1792]{2,1,0:T(8,128)(2,1)}, bf16[1,128,1792]{2,1,0:T(8,128)(2,1)S(1)}, u32[]{:S(2)}) copy-start(bf16[1,128,1792]{2,1,0:T(8,128)(2,1)S(1)} %get-tuple-element.116) | copy-start | bytes 1376260
  119.4 8.2 %copy-start.18 = (bf16[1,128,1792]{2,1,0:T(8,128)(2,1)}, bf16[1,128,1792]{2,1,0:T(8,128)(2,1)S(1)}, u32[]{:S(2)}) copy-start(bf16[1,128,1792]{2,1,0:T(8,128)(2,1)S(1)} %get-tuple-element.117) | copy-start | bytes 1376260
  119.5 0.8 copy-start.26
  119.6 8.0 %copy-start.24 = (bf16[4,2,64,128]{3,2,0,1:T(8,128)(2,1)}, bf16[4,2,64,128]{3,2,0,1:T(8,128)(2,1)S(1)}, u32[]{:S(2)}) copy-start(bf16[4,2,64,128]{3,2,0,1:T(8,128)(2,1)S(1)} %fusion.34) | copy-start | bytes 393220
  119.6 2.2 copy-start.2
  121.8 5.8 %copy-start.14 = (bf16[1,128,1792]{2,1,0:T(8,128)(2,1)S(1)}, bf16[1,128,1792]{2,1,0:T(8,128)(2,1)}, u32[]{:S(2)}) copy-start(bf16[1,128,1792]{2,1,0:T(8,128)(2,1)} %get-tuple-element.119) | copy-start | bytes 1376260
  127.6 3.1 %copy-start.23 = (s32[4,128,8]{1,2,0:T(8,128)S(1)}, s32[4,128,8]{1,2,0:T(8,128)}, u32[]{:S(2)}) copy-start(s32[4,128,8]{1,2,0:T(8,128)} %copy-done.22) | copy-start | bytes 49156
  129.0 8.1 %collective-permute-start.13 = (bf16[4,64,1792]{2,1,0:T(8,128)(2,1)}, bf16[4,64,1792]{2,1,0:T(8,128)(2,1)S(1)}, u32[]{:S(2)}, u32[]{:S(2)}) collective-permute-start(bf16[4,64,1792]{2,1,0:T(8,128)(2,1)} %convolution_convert_fusion), channel_id=1, source_target_pairs={{0,1},{1,0},{2,3},{3,2},{4,5},{5,4},{6,7},{7,6},{8,9},{9,8},{10,11... | collective-permute-start | bytes 2752520 | tf_op jit(solution)/shard_map/ppermute | solution.py:70
  133.3 3.3 %copy-start.13 = (bf16[1,128,1792]{2,1,0:T(8,128)(2,1)S(1)}, bf16[1,128,1792]{2,1,0:T(8,128)(2,1)}, u32[]{:S(2)}) copy-start(bf16[1,128,1792]{2,1,0:T(8,128)(2,1)} %copy-done.12) | copy-start | bytes 1376260
  133.3 3.3 %copy-start.15 = (bf16[1,128,1792]{2,1,0:T(8,128)(2,1)S(1)}, bf16[1,128,1792]{2,1,0:T(8,128)(2,1)}, u32[]{:S(2)}) copy-start(bf16[1,128,1792]{2,1,0:T(8,128)(2,1)} %get-tuple-element.119) | copy-start | bytes 1376260
  133.3 3.3 %copy-start.17 = (bf16[1,128,1792]{2,1,0:T(8,128)(2,1)S(1)}, bf16[1,128,1792]{2,1,0:T(8,128)(2,1)}, u32[]{:S(2)}) copy-start(bf16[1,128,1792]{2,1,0:T(8,128)(2,1)} %copy-done.16) | copy-start | bytes 1376260
  133.4 3.3 %copy-start.19 = (bf16[1,128,1792]{2,1,0:T(8,128)(2,1)S(1)}, bf16[1,128,1792]{2,1,0:T(8,128)(2,1)}, u32[]{:S(2)}) copy-start(bf16[1,128,1792]{2,1,0:T(8,128)(2,1)} %copy-done.18) | copy-start | bytes 1376260
  133.4 3.3 %copy-start.25 = (bf16[4,2,64,128]{3,2,0,1:T(8,128)(2,1)S(1)}, bf16[4,2,64,128]{3,2,0,1:T(8,128)(2,1)}, u32[]{:S(2)}) copy-start(bf16[4,2,64,128]{3,2,0,1:T(8,128)(2,1)} %copy-done.24) | copy-start | bytes 393220
  134.6 14.8 %collective-permute-start.14 = (bf16[128,2048]{1,0:T(8,128)(2,1)S(1)}, bf16[128,2048]{1,0:T(8,128)(2,1)S(1)}, u32[]{:S(2)}, u32[]{:S(2)}) collective-permute-start(bf16[128,2048]{1,0:T(8,128)(2,1)S(1)} %get-tuple-element.93), channel_id=1, source_target_pairs={{0,16},{1,17},{2,18},{3,19},{4,20},{5,21},{6,22},{7,23},{8,24},{9,... | collective-permute-start | bytes 1572872 | tf_op jit(solution)/shard_map/ppermute | solution.py:70
  136.1 24.5 %collective-permute-start.15 = (bf16[128,2048]{1,0:T(8,128)(2,1)}, bf16[128,2048]{1,0:T(8,128)(2,1)S(1)}, u32[]{:S(2)}, u32[]{:S(2)}) collective-permute-start(bf16[128,2048]{1,0:T(8,128)(2,1)} %get-tuple-element.92), channel_id=1, source_target_pairs={{0,16},{1,17},{2,18},{3,19},{4,20},{5,21},{6,22},{7,23},{8,24},{9,... | collective-permute-start | bytes 1572872 | tf_op jit(solution)/shard_map/ppermute | solution.py:70
  137.1 2.0 copy-start.3
  144.9 4.7 %copy-start = (f32[512,2048]{1,0:T(8,128)}, f32[512,2048]{1,0:T(8,128)S(1)}, u32[]{:S(2)}) copy-start(f32[512,2048]{1,0:T(8,128)S(1)} %fusion.8) | copy-start | bytes 12582916
  145.0 6.2 %copy-start.28 = (pred[4,128,2]{1,2,0:T(4,128)(4,1)S(1)}, pred[4,128,2]{1,2,0:T(4,128)(4,1)}, u32[]{:S(2)}) copy-start(pred[4,128,2]{1,2,0:T(4,128)(4,1)} %get-tuple-element.83) | copy-start | bytes 3076
  145.0 6.5 %copy-start.9 = (bf16[128,2048]{1,0:T(8,128)(2,1)S(1)}, bf16[128,2048]{1,0:T(8,128)(2,1)}, u32[]{:S(2)}) copy-start(bf16[128,2048]{1,0:T(8,128)(2,1)} %get-tuple-element.91) | copy-start | bytes 1572868
  149.7 11.0 %collective-permute-start.16 = (bf16[128,1024]{1,0:T(8,128)(2,1)S(1)}, bf16[128,1024]{1,0:T(8,128)(2,1)S(1)}, u32[]{:S(2)}, u32[]{:S(2)}) collective-permute-start(bf16[128,1024]{1,0:T(8,128)(2,1)S(1)} %fusion.31), channel_id=1, source_target_pairs={{0,8},{1,9},{2,10},{3,11},{4,12},{5,13},{6,14},{7,15},{8,0},{9,1},... | collective-permute-start | bytes 786440 | tf_op jit(solution)/shard_map/ppermute | solution.py:70
  151.5 20.0 %collective-permute-start.18 = (bf16[128,2048]{1,0:T(8,128)(2,1)S(1)}, bf16[128,2048]{1,0:T(8,128)(2,1)S(1)}, u32[]{:S(2)}, u32[]{:S(2)}) collective-permute-start(bf16[128,2048]{1,0:T(8,128)(2,1)S(1)} %copy-done.9), channel_id=1, source_target_pairs={{0,16},{1,17},{2,18},{3,19},{4,20},{5,21},{6,22},{7,23},{8,24},{9,... | collective-permute-start | bytes 1572872 | tf_op jit(solution)/shard_map/ppermute | solution.py:70
  162.9 2.7 %copy-start.1 = (f32[512,2048]{1,0:T(8,128)S(1)}, f32[512,2048]{1,0:T(8,128)}, u32[]{:S(2)}) copy-start(f32[512,2048]{1,0:T(8,128)} %copy-done) | copy-start | bytes 12582916
  165.4 2.0 copy-start.6
  165.4 2.0 copy-start.7
  165.4 2.0 copy-start.30
  165.4 3.7 %collective-permute-start.17 = (bf16[2,64,1792]{2,1,0:T(8,128)(2,1)S(1)}, bf16[2,64,1792]{2,1,0:T(8,128)(2,1)S(1)}, u32[]{:S(2)}, u32[]{:S(2)}) collective-permute-start(bf16[2,64,1792]{2,1,0:T(8,128)(2,1)S(1)} %get-tuple-element.64), channel_id=1, source_target_pairs={{0,1},{1,0},{2,3},{3,2},{4,5},{5,4},{6,7},{7,6},{8,9},{9,8},{10,11... | collective-permute-start | bytes 1376264 | tf_op jit(solution)/shard_map/ppermute | solution.py:70
  165.7 1.8 copy-start.8
  165.9 8.7 %collective-permute-start.19 = (bf16[128,1024]{1,0:T(8,128)(2,1)S(1)}, bf16[128,1024]{1,0:T(8,128)(2,1)S(1)}, u32[]{:S(2)}, u32[]{:S(2)}) collective-permute-start(bf16[128,1024]{1,0:T(8,128)(2,1)S(1)} %fusion.30), channel_id=1, source_target_pairs={{0,8},{1,9},{2,10},{3,11},{4,12},{5,13},{6,14},{7,15},{8,0},{9,1},... | collective-permute-start | bytes 786440 | tf_op jit(solution)/shard_map/ppermute | solution.py:70
  167.5 36.8 %collective-permute-start.22 = (bf16[128,2048]{1,0:T(8,128)(2,1)S(1)}, bf16[128,2048]{1,0:T(8,128)(2,1)S(1)}, u32[]{:S(2)}, u32[]{:S(2)}) collective-permute-start(bf16[128,2048]{1,0:T(8,128)(2,1)S(1)} %copy-done.8), channel_id=1, source_target_pairs={{0,16},{1,17},{2,18},{3,19},{4,20},{5,21},{6,22},{7,23},{8,24},{9,... | collective-permute-start | bytes 1572872 | tf_op jit(solution)/shard_map/ppermute | solution.py:70
  179.2 2.0 collective-permute-start.20
  179.3 25.0 %collective-permute-start.21 = (bf16[2,128,1792]{2,1,0:T(8,128)(2,1)S(1)}, bf16[2,128,1792]{2,1,0:T(8,128)(2,1)S(1)}, u32[]{:S(2)}, u32[]{:S(2)}) collective-permute-start(bf16[2,128,1792]{2,1,0:T(8,128)(2,1)S(1)} %convolution_convert_fusion.5), channel_id=1, source_target_pairs={{0,2},{1,3},{2,4},{3,5},{4,6},{5,7},{6,0},{7,1},{8,10},{9,11},{10,... | collective-permute-start | bytes 2752520 | tf_op jit(solution)/shard_map/ppermute | solution.py:70
  179.7 24.7 %collective-permute-start.23 = (bf16[128,1024]{1,0:T(8,128)(2,1)S(1)}, bf16[128,1024]{1,0:T(8,128)(2,1)S(1)}, u32[]{:S(2)}, u32[]{:S(2)}) collective-permute-start(bf16[128,1024]{1,0:T(8,128)(2,1)S(1)} %fusion.29), channel_id=1, source_target_pairs={{0,8},{1,9},{2,10},{3,11},{4,12},{5,13},{6,14},{7,15},{8,0},{9,1},... | collective-permute-start | bytes 786440 | tf_op jit(solution)/shard_map/ppermute | solution.py:70
  181.7 32.0 %collective-permute-start.25 = (bf16[128,1792]{1,0:T(8,128)(2,1)S(1)}, bf16[128,1792]{1,0:T(8,128)(2,1)S(1)}, u32[]{:S(2)}, u32[]{:S(2)}) collective-permute-start(bf16[128,1792]{1,0:T(8,128)(2,1)S(1)} %get-tuple-element.95), channel_id=1, source_target_pairs={{0,6},{1,7},{2,0},{3,1},{4,2},{5,3},{6,4},{7,5},{8,14},{9,15},{10,... | collective-permute-start | bytes 1376264 | tf_op jit(solution)/shard_map/ppermute | solution.py:70
  209.0 1.9 collective-permute-start.24
  209.4 18.6 %collective-permute-start.26 = (bf16[128,1024]{1,0:T(8,128)(2,1)S(1)}, bf16[128,1024]{1,0:T(8,128)(2,1)S(1)}, u32[]{:S(2)}, u32[]{:S(2)}) collective-permute-start(bf16[128,1024]{1,0:T(8,128)(2,1)S(1)} %fusion.28), channel_id=1, source_target_pairs={{0,8},{1,9},{2,10},{3,11},{4,12},{5,13},{6,14},{7,15},{8,0},{9,1},... | collective-permute-start | bytes 786440 | tf_op jit(solution)/shard_map/ppermute | solution.py:70
  211.0 48.0 %collective-permute-start.30 = (bf16[128,1792]{1,0:T(8,128)(2,1)S(1)}, bf16[128,1792]{1,0:T(8,128)(2,1)S(1)}, u32[]{:S(2)}, u32[]{:S(2)}) collective-permute-start(bf16[128,1792]{1,0:T(8,128)(2,1)S(1)} %get-tuple-element.94), channel_id=1, source_target_pairs={{0,14},{1,15},{2,8},{3,9},{4,10},{5,11},{6,12},{7,13},{8,6},{9,7},... | collective-permute-start | bytes 1376264 | tf_op jit(solution)/shard_map/ppermute | solution.py:70
  232.6 1.9 collective-permute-start.27
  233.1 25.9 %collective-permute-start.31 = (bf16[128,1792]{1,0:T(8,128)(2,1)S(1)}, bf16[128,1792]{1,0:T(8,128)(2,1)S(1)}, u32[]{:S(2)}, u32[]{:S(2)}) collective-permute-start(bf16[128,1792]{1,0:T(8,128)(2,1)S(1)} %get-tuple-element.96), channel_id=1, source_target_pairs={{0,10},{1,11},{2,12},{3,13},{4,14},{5,15},{6,8},{7,9},{8,2},{9,3},... | collective-permute-start | bytes 1376264 | tf_op jit(solution)/shard_map/ppermute | solution.py:70
  233.2 25.5 %collective-permute-start.28 = (bf16[128,1792]{1,0:T(8,128)(2,1)S(1)}, bf16[128,1792]{1,0:T(8,128)(2,1)S(1)}, u32[]{:S(2)}, u32[]{:S(2)}) collective-permute-start(bf16[128,1792]{1,0:T(8,128)(2,1)S(1)} %get-tuple-element.97), channel_id=1, source_target_pairs={{0,2},{1,3},{2,4},{3,5},{4,6},{5,7},{6,0},{7,1},{8,10},{9,11},{10,... | collective-permute-start | bytes 1376264 | tf_op jit(solution)/shard_map/ppermute | solution.py:70
  234.9 24.1 %collective-permute-start.29 = (bf16[128,1792]{1,0:T(8,128)(2,1)S(1)}, bf16[128,1792]{1,0:T(8,128)(2,1)S(1)}, u32[]{:S(2)}, u32[]{:S(2)}) collective-permute-start(bf16[128,1792]{1,0:T(8,128)(2,1)S(1)} %fusion.32), channel_id=1, source_target_pairs={{0,8},{1,9},{2,10},{3,11},{4,12},{5,13},{6,14},{7,15},{8,0},{9,1},... | collective-permute-start | bytes 1376264 | tf_op jit(solution)/shard_map/ppermute | solution.py:70
  259.3 0.9 copy-start.4

commit v6 on v5

--- a/solution.py
+++ b/solution.py
@@ -80,9 +80,13 @@
     def depths(r):
         return lax.dynamic_slice_in_dim(tokens, (d ^ r) * quarter, quarter, axis=1)
 
-    info = jnp.concatenate([expert_ids.astype(BF), gate_weights], axis=1)
-    first = jnp.concatenate([depths(0), depths(1), info], axis=1)
-    second = jnp.concatenate([depths(2), depths(3), info], axis=1)
+    info = jnp.concatenate([expert_ids.astype(BF), gate_weights], axis=1).T
+    info = jnp.pad(info, ((0, 0), (0, half - tok)))
+
+    def payload(r):
+        return jnp.concatenate([jnp.concatenate([depths(r), depths(r + 1)], axis=1), info])
+
+    first, second = payload(0), payload(2)
     gate_x = [
         send(gate[quarter * lo // 7 : quarter * hi // 7], flip=1) for lo, hi in CUTS
     ]
@@ -90,25 +94,27 @@
 
     seen = [{0: first, 1: send(first, 1)}, {1: send(second, 1, 2), 0: send(second, 0, 2)}]
     seen[0][3], seen[1][3] = send(first, -1), send(second, -1, 2)
-    seen[0][1], seen[1][1], gate_x[0] = together((seen[0][1], seen[1][1], gate_x[0]))
+    seen, gate_x[0] = together((seen, gate_x[0]))
     seen[0][2], seen[1][2] = send(seen[0][1], 1), send(seen[1][1], 1)
-    seen, gate_x[1], down_y = together((seen, gate_x[1], down_y))
+    seen[0][2], seen[1][2], gate_x[1], down_y = together(
+        (seen[0][2], seen[1][2], gate_x[1], down_y)
+    )
 
     chosen = jnp.stack([e, e ^ 1]).astype(jnp.int32)
     earlier = jnp.triu(jnp.ones((tok, tok), BF), 1)
 
     def places(info):
-        matches = info[..., :top].astype(jnp.int32)[..., None] == chosen
-        hits = jnp.any(matches, axis=2).transpose(0, 2, 1)
-        weight = jnp.sum(jnp.where(matches, info[..., top:, None].astype(F32), 0.0), axis=2)
+        matches = info[:, None, :top].astype(jnp.int32) == chosen[:, None, None]
+        hits = jnp.any(matches, axis=2)
+        weight = jnp.sum(jnp.where(matches, info[:, None, top:].astype(F32), 0.0), axis=2)
         rank = jnp.dot(hits.astype(BF), earlier, preferred_element_type=F32)
         rank = jnp.where(hits, rank, -1.0)
         place = (rank[..., None, :] == jnp.arange(slots, dtype=F32)[:, None]).astype(BF)
-        pay = place * weight.transpose(0, 2, 1)[..., None, :].astype(BF)
+        pay = place * weight[..., None, :].astype(BF)
         return place, pay.reshape(chips, chunk, tok)
 
-    infos = [jnp.stack([seen[g][k][:, half:] for k in range(chips)]) for g in range(2)]
-    helds = [jnp.stack([seen[g][k][:, :half] for k in range(chips)]) for g in range(2)]
+    infos = [jnp.stack([seen[g][k][tok:, :tok] for k in range(chips)]) for g in range(2)]
+    helds = [jnp.stack([seen[g][k][:tok] for k in range(chips)]) for g in range(2)]
     info_x = send(infos[0], flip=1)
     place0, pay0 = places(infos[0])
     place1, _ = places(infos[1])
@@ -121,18 +127,20 @@
             ).astype(BF)
 
         other = send(of(1), core=1)
-        return jnp.concatenate([of(0), other], axis=1).reshape(-1, half)
-
+        return jnp.concatenate([of(0), other], axis=1)
+
+    chosen0, chosen1 = choose(place0, helds[0]), choose(place1, helds[1])
     weights = jnp.concatenate([gate, *gate_x])
 
     def product(rows):
-        return jnp.dot(rows, weights, preferred_element_type=F32).reshape(chips, chunk, 2 * ff)
+        flat = rows.reshape(-1, half)
+        return jnp.dot(flat, weights, preferred_element_type=F32).reshape(chips, chunk, 2 * ff)
 
     order = (2, 1, 3, 0)
-    sent = product(choose(place1, helds[1])).astype(BF)
-    sent, place0 = together((sent, place0))
+    sent = product(chosen1).astype(BF)
+    sent, chosen0 = together((sent, chosen0))
     part = [send(sent[k], flip=2) for k in order]
-    near = product(choose(place0, helds[0]))
+    near = product(chosen0)
     pay = jnp.stack([pay0, places(info_x)[1]])
 
     hidden, away, out = {}, {}, {}
@@ -144,8 +152,6 @@
 
     def down_product(q):
         own = hidden[q][0]
-        if q + 1 < chips:
-            own, part[q + 1] = together((own, part[q + 1]))
         joined = jnp.concatenate([own, hidden[q][1]])
         value = jnp.concatenate(
             [jnp.dot(joined, w, preferred_element_type=F32).astype(BF) for w in (down, down_y)],
@@ -162,26 +168,29 @@
         hidden[q] = (own, hidden[q][1])
         return value
 
+    def cross(q):
+        return send(away[q], core=1)
+
     finish(0, part[0])
     down_product(0)
-    away[0], part[1] = together((away[0], part[1]))
+    came, part[1] = together((cross(0), part[1]))
     finish(1, part[1])
-    term = before_down(1, weigh(0, send(away[0], core=1)).astype(BF))
-    middle = send(term, 1)
+    term = weigh(0, came).astype(BF)
+    middle = [send(term[g], 1) for g in range(2)]
+    middle[0], part[2] = before_down(1, (middle[0], part[2]))
     down_product(1)
-    away[1], part[2] = together((away[1], part[2]))
     finish(2, part[2])
-    term = weigh(1, before_down(2, send(away[1], core=1))).astype(BF)
+    part[3] = before_down(2, part[3])
+    down_product(2)
+    finish(3, part[3])
+    down_product(3)
+    away[3], came, middle[1] = together((away[3], cross(1), middle[1]))
+    term = weigh(1, came).astype(BF)
     back = [send(term[0], -1), send(term[1], -1, 1)]
-    middle = before_down(2, middle)
-    down_product(2)
-    away[2], part[3] = together((away[2], part[3]))
-    finish(3, part[3])
-    term = (weigh(2, before_down(3, send(away[2], core=1))) + middle.astype(F32)).astype(BF)
+    term = weigh(2, cross(2))
+    term = [(term[g] + middle[g].astype(F32)).astype(BF) for g in range(2)]
     forth = [send(term[0], 1), send(term[1], 1, 1)]
-    back[0] = before_down(3, back[0])
-    down_product(3)
-    term = weigh(3, send(away[3], core=1))
+    term = weigh(3, cross(3))
     theirs = send(term[1].astype(BF), flip=1)
     mine = (term[0] + back[0].astype(F32) + forth[0].astype(F32)).astype(BF)
     far = (theirs.astype(F32) + back[1].astype(F32) + forth[1].astype(F32)).astype(BF)

time: 262 us -> 220 us (0.84)
  waiting for transfers between devices: 154 us -> 133 us
  matrix products: 35.2 us -> 22.9 us
  local copies, waits for them, and re-layouts: 26.8 us -> 15.2 us
  starting transfers between devices: 37.7 us -> 45.9 us
  other arithmetic: 6.01 us -> 2.53 us
    ppermute x32 -> x33, waiting for transfers between devices: 154 us -> 133 us  [send(): lax.ppermute(value, ('dp', 'expert'), [(i * owners + j, (i ^ flip) * owne...]
    dot_general x8, matrix products: 17.9 us -> 7.2 us  [down_product(): jnp.dot(joined, w, preferred_element_type=F32).astype(BF)]
    ppermute x32 -> x33, starting transfers between devices: 37.7 us -> 45.9 us  [send(): lax.ppermute(value, ('dp', 'expert'), [(i * owners + j, (i ^ flip) * owne...]
    another operation x16 -> x12, local copies, waits for them, and re-layouts: 10 us -> 5.34 us  [the longest x6 3.3 us: paired(): jnp.stack([seen[g][k][:tok] for k in range(chips)])]
    unnamed x69 -> x25, local copies, waits for them, and re-layouts: 6.07 us -> 2.16 us
  transfers between devices with their start and end apart: 32 -> 33, of which waited for: 16 -> 18; matrix products, arithmetic and copies ran while one was open for 19% -> 12% of each run, Pallas kernels for 0% -> 0%
where the time goes in v6:
time: 220 us
  waiting for transfers between devices  133 us (60%)
  starting transfers between devices  45.9 us (21%)
  matrix products  22.9 us (10%)
  local copies, waits for them, and re-layouts  15.2 us (7%)
  other arithmetic  2.53 us (1%)
    ppermute x33, waiting for transfers between devices, send(): lax.ppermute(value, ('dp', 'expert'), [(i * owners + j, (i ^ flip) * owne...  133 us
    ppermute x33, starting transfers between devices, send(): lax.ppermute(value, ('dp', 'expert'), [(i * owners + j, (i ^ flip) * owne...  45.9 us
    dot_general x2, matrix products, product(): jnp.dot(flat, weights, preferred_element_type=F32)  10.9 us
    dot_general x8, matrix products, down_product(): jnp.dot(joined, w, preferred_element_type=F32).astype(BF)  7.2 us
    slice x2, local copies, waits for them, and re-layouts, paired(): gate[quarter * lo // 7:quarter * hi // 7]  4.61 us
  transfers between devices with their start and end apart: 33, of which 18 were waited for; matrix products, arithmetic and copies ran while one was open for 12% of the time, Pallas kernels for 0%

profile of v6, /device:TPU:0, one launch (start us, length us, event | category | flops | bytes accessed | tf_op | source)
XLA Modules:
  0.0 219.9 jit_solution(14792836807468194457)
XLA Ops:
  0.0 3.5 %slice_bitcast_fusion = (bf16[384,2048]{1,0:T(8,128)(2,1)S(1)}, bf16[384,2048]{1,0:T(8,128)(2,1)}) fusion(bf16[1,896,2048]{2,1,0:T(8,128)(2,1)} %param.6), kind=kLoop, calls=%fused_computation.16 | loop fusion | bytes 6291456 | tf_op jit(solution)/shard_map/slice | solution.py:91
  3.5 2.9 %collective-permute-start.5 = (bf16[384,2048]{1,0:T(8,128)(2,1)}, bf16[384,2048]{1,0:T(8,128)(2,1)}, u32[]{:S(2)}, u32[]{:S(2)}) collective-permute-start(bf16[384,2048]{1,0:T(8,128)(2,1)} %get-tuple-element.61), channel_id=1, source_target_pairs={{0,8},{1,9},{2,10},{3,11},{4,12},{5,13},{6,14},{7,15},{8,0},{9,1},... | collective-permute-start | bytes 4718600 | tf_op jit(solution)/shard_map/ppermute | solution.py:70
  6.7 1.6 collective-permute-start
  8.3 2.2 %collective-permute-start.1 = (bf16[144,1792]{1,0:T(8,128)(2,1)S(1)}, bf16[144,1792]{1,0:T(8,128)(2,1)}, u32[]{:S(2)}, u32[]{:S(2)}) collective-permute-start(bf16[144,1792]{1,0:T(8,128)(2,1)S(1)} %get-tuple-element.30), channel_id=1, source_target_pairs={{0,6},{1,7},{2,0},{3,1},{4,2},{5,3},{6,4},{7,5},{8,14},{9,15},{10,... | collective-permute-start | bytes 1548296 | tf_op jit(solution)/shard_map/ppermute | solution.py:70
  10.6 1.5 collective-permute-start.2
  12.1 11.2 %collective-permute-done = bf16[144,1792]{1,0:T(8,128)(2,1)S(1)} collective-permute-done((bf16[144,1792]{1,0:T(8,128)(2,1)S(1)}, bf16[144,1792]{1,0:T(8,128)(2,1)S(1)}, u32[]{:S(2)}, u32[]{:S(2)}) %collective-permute-start) | collective-permute-done | bytes 516128 | tf_op jit(solution)/shard_map/ppermute | solution.py:70
  23.3 13.8 %collective-permute-start.4 = (bf16[144,1792]{1,0:T(8,128)(2,1)S(1)}, bf16[144,1792]{1,0:T(8,128)(2,1)S(1)}, u32[]{:S(2)}, u32[]{:S(2)}) collective-permute-start(bf16[144,1792]{1,0:T(8,128)(2,1)S(1)} %get-tuple-element.88), channel_id=1, source_target_pairs={{0,22},{1,23},{2,16},{3,17},{4,18},{5,19},{6,20},{7,21},{8,30},{9,... | collective-permute-start | bytes 1548296 | tf_op jit(solution)/shard_map/ppermute | solution.py:70
  37.1 1.1 slice_bitcast_fusion.9
  38.2 4.8 %collective-permute-done.1 = bf16[144,1792]{1,0:T(8,128)(2,1)} collective-permute-done((bf16[144,1792]{1,0:T(8,128)(2,1)S(1)}, bf16[144,1792]{1,0:T(8,128)(2,1)}, u32[]{:S(2)}, u32[]{:S(2)}) %collective-permute-start.1) | collective-permute-done | bytes 516128 | tf_op jit(solution)/shard_map/ppermute | solution.py:70
  43.0 0.8 collective-permute-start.8
  43.8 1.3 collective-permute-start.9
  45.0 1.5 collective-permute-done.3
  47.1 8.4 %collective-permute-done.4 = bf16[144,1792]{1,0:T(8,128)(2,1)S(1)} collective-permute-done((bf16[144,1792]{1,0:T(8,128)(2,1)S(1)}, bf16[144,1792]{1,0:T(8,128)(2,1)S(1)}, u32[]{:S(2)}, u32[]{:S(2)}) %collective-permute-start.4) | collective-permute-done | bytes 516128 | tf_op jit(solution)/shard_map/ppermute | solution.py:70
  55.4 1.1 collective-permute-start.6
  56.6 0.8 collective-permute-start.7
  57.4 1.0 slice_bitcast_fusion.29
  58.4 0.7 slice_bitcast_fusion.38
  59.1 0.7 slice_bitcast_fusion.34
  59.8 1.1 slice_bitcast_fusion.22
  60.9 0.7 slice_bitcast_fusion.37
  61.6 1.1 slice_bitcast_fusion.26
  62.6 17.7 %collective-permute-done.8 = bf16[384,2048]{1,0:T(8,128)(2,1)S(1)} collective-permute-done((bf16[384,2048]{1,0:T(8,128)(2,1)S(1)}, bf16[384,2048]{1,0:T(8,128)(2,1)S(1)}, u32[]{:S(2)}, u32[]{:S(2)}) %collective-permute-start.8) | collective-permute-done | bytes 1572896 | tf_op jit(solution)/shard_map/ppermute | solution.py:70
  80.3 14.2 %collective-permute-done.9 = bf16[1024,896]{1,0:T(8,128)(2,1)S(1)} collective-permute-done((bf16[1024,896]{1,0:T(8,128)(2,1)}, bf16[1024,896]{1,0:T(8,128)(2,1)S(1)}, u32[]{:S(2)}, u32[]{:S(2)}) %collective-permute-start.9) | collective-permute-done | bytes 1835040 | tf_op jit(solution)/shard_map/ppermute | solution.py:70
  94.6 0.8 collective-permute-start.10
  95.4 2.9 %collective-permute-done.10 = bf16[4,16,128]{2,1,0:T(8,128)(2,1)S(1)} collective-permute-done((bf16[4,16,128]{2,1,0:T(8,128)(2,1)S(1)}, bf16[4,16,128]{2,1,0:T(8,128)(2,1)S(1)}, u32[]{:S(2)}, u32[]{:S(2)}) %collective-permute-start.10) | collective-permute-done | bytes 16416 | tf_op jit(solution)/shard_map/ppermute | solution.py:70
  101.8 1.2 collective-permute-done.12
  103.4 5.3 %fusion.2 = bf16[4,128,2048]{2,1,0:T(8,128)(2,1)S(1)} fusion(bf16[4,64,1792]{2,1,0:T(8,128)(2,1)S(1)} %collective-permute-done.12, bf16[4,64,1792]{2,1,0:T(8,128)(2,1)S(1)} %convolution_convert_fusion.3, bf16[128,2048]{1,0:T(8,128)(2,1)S(1)} %collective-permute-done.11, bf16[384,2048]{1,0:T(8,128)(2,1)S(1)} %collective-permute-done.8, ...), kind=kOutput, calls=%fused_computation.3 | convolution fusion | flops 3792175104 | bytes 11272192 | tf_op jit(solution)/shard_map/dot_general | solution.py:137
  108.8 1.0 slice_bitcast_fusion.5
  109.7 0.7 collective-permute-start.14
  110.4 5.6 %fusion.8 = f32[512,2048]{1,0:T(8,128)S(1)} fusion(bf16[512,1792]{1,0:T(8,128)(2,1)S(1)} %bitcast.180, bf16[128,2048]{1,0:T(8,128)(2,1)S(1)} %collective-permute-done.11, bf16[384,2048]{1,0:T(8,128)(2,1)S(1)} %collective-permute-done.8, bf16[384,2048]{1,0:T(8,128)(2,1)} %collective-permute-done.5, bf16[896,2048]{1,0:T(8,128)(2,1)S(1)} %bitcast.175), kind=kOutput, calls=%fused_computation.26 | convolution fusion | flops 3787456512 | bytes 13369344 | tf_op jit(solution)/shard_map/dot_general | solution.py:137
  116.0 7.6 %collective-permute-done.14 = bf16[128,2048]{1,0:T(8,128)(2,1)S(1)} collective-permute-done((bf16[128,2048]{1,0:T(8,128)(2,1)S(1)}, bf16[128,2048]{1,0:T(8,128)(2,1)S(1)}, u32[]{:S(2)}, u32[]{:S(2)}) %collective-permute-start.14) | collective-permute-done | bytes 524320 | tf_op jit(solution)/shard_map/ppermute | solution.py:70
  123.9 0.8 collective-permute-start.15
  125.4 0.6 collective-permute-start.17
  125.9 5.5 %collective-permute-done.15 = bf16[128,1024]{1,0:T(8,128)(2,1)S(1)} collective-permute-done((bf16[128,1024]{1,0:T(8,128)(2,1)S(1)}, bf16[128,1024]{1,0:T(8,128)(2,1)S(1)}, u32[]{:S(2)}, u32[]{:S(2)}) %collective-permute-start.15) | collective-permute-done | bytes 262176 | tf_op jit(solution)/shard_map/ppermute | solution.py:70
  131.4 2.2 %convolution_convert_fusion.13 = bf16[256,896]{1,0:T(8,128)(2,1)S(1)} fusion(bf16[128,1024]{1,0:T(8,128)(2,1)S(1)} %collective-permute-done.15, bf16[128,1024]{1,0:T(8,128)(2,1)S(1)} %fusion.34, bf16[1,1024,896]{2,1,0:T(8,128)(2,1)} %param.7), kind=kOutput, calls=%fused_computation.25 | convolution fusion | flops 471040000 | bytes 2818048 | tf_op jit(solution)/shard_map/dot_general | solution.py:157
  133.6 0.7 convolution_convert_fusion.12
  134.9 0.7 collective-permute-start.19
  135.6 3.0 %collective-permute-done.17 = bf16[128,2048]{1,0:T(8,128)(2,1)S(1)} collective-permute-done((bf16[128,2048]{1,0:T(8,128)(2,1)}, bf16[128,2048]{1,0:T(8,128)(2,1)S(1)}, u32[]{:S(2)}, u32[]{:S(2)}) %collective-permute-start.17) | collective-permute-done | bytes 524320 | tf_op jit(solution)/shard_map/ppermute | solution.py:70
  138.7 1.4 convolution_convert_fusion.5
  140.6 2.5 %collective-permute-start.22 = (bf16[128,1024]{1,0:T(8,128)(2,1)S(1)}, bf16[128,1024]{1,0:T(8,128)(2,1)S(1)}, u32[]{:S(2)}, u32[]{:S(2)}) collective-permute-start(bf16[128,1024]{1,0:T(8,128)(2,1)S(1)} %fusion.33), channel_id=1, source_target_pairs={{0,8},{1,9},{2,10},{3,11},{4,12},{5,13},{6,14},{7,15},{8,0},{9,1},... | collective-permute-start | bytes 786440 | tf_op jit(solution)/shard_map/ppermute | solution.py:70
  143.1 0.6 collective-permute-start.20
  143.7 1.5 collective-permute-start.24
  145.2 4.7 %collective-permute-done.19 = bf16[128,2048]{1,0:T(8,128)(2,1)S(1)} collective-permute-done((bf16[128,2048]{1,0:T(8,128)(2,1)S(1)}, bf16[128,2048]{1,0:T(8,128)(2,1)S(1)}, u32[]{:S(2)}, u32[]{:S(2)}) %collective-permute-start.19) | collective-permute-done | bytes 524320 | tf_op jit(solution)/shard_map/ppermute | solution.py:70
  149.9 5.6 %collective-permute-done.18 = bf16[128,1792]{1,0:T(8,128)(2,1)S(1)} collective-permute-done((bf16[128,1792]{1,0:T(8,128)(2,1)S(1)}, bf16[128,1792]{1,0:T(8,128)(2,1)S(1)}, u32[]{:S(2)}, u32[]{:S(2)}) %collective-permute-start.18) | collective-permute-done | bytes 458784 | tf_op jit(solution)/shard_map/ppermute | solution.py:70
  155.5 0.7 convolution_convert_fusion.8
  156.2 0.7 copy-done.7
  157.0 0.7 convolution_convert_fusion.9
  158.2 2.0 collective-permute-start.27
  160.2 0.7 collective-permute-done.20
  161.1 1.4 collective-permute-start.21
  162.5 4.9 %collective-permute-done.27 = bf16[128,1024]{1,0:T(8,128)(2,1)S(1)} collective-permute-done((bf16[128,1024]{1,0:T(8,128)(2,1)S(1)}, bf16[128,1024]{1,0:T(8,128)(2,1)S(1)}, u32[]{:S(2)}, u32[]{:S(2)}) %collective-permute-start.27) | collective-permute-done | bytes 262176 | tf_op jit(solution)/shard_map/ppermute | solution.py:70
  167.4 0.7 convolution_convert_fusion.6
  168.2 0.7 convolution_convert_fusion.7
  169.1 3.6 %collective-permute-done.21 = bf16[128,1024]{1,0:T(8,128)(2,1)S(1)} collective-permute-done((bf16[128,1024]{1,0:T(8,128)(2,1)S(1)}, bf16[128,1024]{1,0:T(8,128)(2,1)S(1)}, u32[]{:S(2)}, u32[]{:S(2)}) %collective-permute-start.21) | collective-permute-done | bytes 262176 | tf_op jit(solution)/shard_map/ppermute | solution.py:70
  172.7 0.7 convolution_convert_fusion.11
  173.5 0.7 convolution_convert_fusion.10
  174.8 1.0 collective-permute-start.31
  175.8 1.6 collective-permute-start.26
  178.0 1.2 collective-permute-start.32
  179.1 1.3 collective-permute-start.29
  180.9 1.8 collective-permute-start.30
  182.7 35.0 %collective-permute-done.26 = bf16[128,1792]{1,0:T(8,128)(2,1)S(1)} collective-permute-done((bf16[128,1792]{1,0:T(8,128)(2,1)S(1)}, bf16[128,1792]{1,0:T(8,128)(2,1)S(1)}, u32[]{:S(2)}, u32[]{:S(2)}) %collective-permute-start.26) | collective-permute-done | bytes 458784 | tf_op jit(solution)/shard_map/ppermute | solution.py:70
  218.3 0.9 copy-done.3
  219.2 0.7 slice_dynamic-update-slice_fusion
  (118 shorter events, 9.9 us)
Async XLA Ops:
  0.0 6.5 %copy-start.5 = (s32[128,8]{0,1:T(8,128)S(1)}, s32[128,8]{0,1:T(8,128)}, u32[]{:S(2)}) copy-start(s32[128,8]{0,1:T(8,128)} %param.8) | copy-start | bytes 12292
  0.0 6.5 %copy-start.6 = (bf16[128,8]{0,1:T(8,128)(2,1)S(1)}, bf16[128,8]{0,1:T(8,128)(2,1)}, u32[]{:S(2)}) copy-start(bf16[128,8]{0,1:T(8,128)(2,1)} %param.9) | copy-start | bytes 6148
  0.0 6.5 %copy-start.4 = (bf16[128,3584]{1,0:T(8,128)(2,1)S(1)}, bf16[128,3584]{1,0:T(8,128)(2,1)}, u32[]{:S(2)}) copy-start(bf16[128,3584]{1,0:T(8,128)(2,1)} %param.5) | copy-start | bytes 2752516
  3.5 51.9 %collective-permute-start.5 = (bf16[384,2048]{1,0:T(8,128)(2,1)}, bf16[384,2048]{1,0:T(8,128)(2,1)}, u32[]{:S(2)}, u32[]{:S(2)}) collective-permute-start(bf16[384,2048]{1,0:T(8,128)(2,1)} %get-tuple-element.61), channel_id=1, source_target_pairs={{0,8},{1,9},{2,10},{3,11},{4,12},{5,13},{6,14},{7,15},{8,0},{9,1},... | collective-permute-start | bytes 4718600 | tf_op jit(solution)/shard_map/ppermute | solution.py:70
  6.7 16.6 %collective-permute-start = (bf16[144,1792]{1,0:T(8,128)(2,1)S(1)}, bf16[144,1792]{1,0:T(8,128)(2,1)S(1)}, u32[]{:S(2)}, u32[]{:S(2)}) collective-permute-start(bf16[144,1792]{1,0:T(8,128)(2,1)S(1)} %get-tuple-element.30), channel_id=1, source_target_pairs={{0,2},{1,3},{2,4},{3,5},{4,6},{5,7},{6,0},{7,1},{8,10},{9,11},{10,... | collective-permute-start | bytes 1548296 | tf_op jit(solution)/shard_map/ppermute | solution.py:70
  8.3 34.6 %collective-permute-start.1 = (bf16[144,1792]{1,0:T(8,128)(2,1)S(1)}, bf16[144,1792]{1,0:T(8,128)(2,1)}, u32[]{:S(2)}, u32[]{:S(2)}) collective-permute-start(bf16[144,1792]{1,0:T(8,128)(2,1)S(1)} %get-tuple-element.30), channel_id=1, source_target_pairs={{0,6},{1,7},{2,0},{3,1},{4,2},{5,3},{6,4},{7,5},{8,14},{9,15},{10,... | collective-permute-start | bytes 1548296 | tf_op jit(solution)/shard_map/ppermute | solution.py:70
  10.6 33.2 %collective-permute-start.2 = (bf16[144,1792]{1,0:T(8,128)(2,1)S(1)}, bf16[144,1792]{1,0:T(8,128)(2,1)}, u32[]{:S(2)}, u32[]{:S(2)}) collective-permute-start(bf16[144,1792]{1,0:T(8,128)(2,1)S(1)} %get-tuple-element.88), channel_id=1, source_target_pairs={{0,16},{1,17},{2,18},{3,19},{4,20},{5,21},{6,22},{7,23},{8,24},{9,... | collective-permute-start | bytes 1548296 | tf_op jit(solution)/shard_map/ppermute | solution.py:70
  12.1 34.4 %collective-permute-start.3 = (bf16[144,1792]{1,0:T(8,128)(2,1)S(1)}, bf16[144,1792]{1,0:T(8,128)(2,1)}, u32[]{:S(2)}, u32[]{:S(2)}) collective-permute-start(bf16[144,1792]{1,0:T(8,128)(2,1)S(1)} %get-tuple-element.88), channel_id=1, source_target_pairs={{0,18},{1,19},{2,20},{3,21},{4,22},{5,23},{6,16},{7,17},{8,26},{9,... | collective-permute-start | bytes 1548296 | tf_op jit(solution)/shard_map/ppermute | solution.py:70
  23.3 32.2 %collective-permute-start.4 = (bf16[144,1792]{1,0:T(8,128)(2,1)S(1)}, bf16[144,1792]{1,0:T(8,128)(2,1)S(1)}, u32[]{:S(2)}, u32[]{:S(2)}) collective-permute-start(bf16[144,1792]{1,0:T(8,128)(2,1)S(1)} %get-tuple-element.88), channel_id=1, source_target_pairs={{0,22},{1,23},{2,16},{3,17},{4,18},{5,19},{6,20},{7,21},{8,30},{9,... | collective-permute-start | bytes 1548296 | tf_op jit(solution)/shard_map/ppermute | solution.py:70
  43.0 37.3 %collective-permute-start.8 = (bf16[384,2048]{1,0:T(8,128)(2,1)S(1)}, bf16[384,2048]{1,0:T(8,128)(2,1)S(1)}, u32[]{:S(2)}, u32[]{:S(2)}) collective-permute-start(bf16[384,2048]{1,0:T(8,128)(2,1)S(1)} %get-tuple-element.60), channel_id=1, source_target_pairs={{0,8},{1,9},{2,10},{3,11},{4,12},{5,13},{6,14},{7,15},{8,0},{9,1},... | collective-permute-start | bytes 4718600 | tf_op jit(solution)/shard_map/ppermute | solution.py:70
  43.8 50.8 %collective-permute-start.9 = (bf16[1024,896]{1,0:T(8,128)(2,1)}, bf16[1024,896]{1,0:T(8,128)(2,1)S(1)}, u32[]{:S(2)}, u32[]{:S(2)}) collective-permute-start(bf16[1024,896]{1,0:T(8,128)(2,1)} %bitcast.185), channel_id=1, source_target_pairs={{0,16},{1,17},{2,18},{3,19},{4,20},{5,21},{6,22},{7,23},{8,24},{9,... | collective-permute-start | bytes 5505032 | tf_op jit(solution)/shard_map/ppermute | solution.py:70
  46.5 52.9 %collective-permute-start.11 = (bf16[128,2048]{1,0:T(8,128)(2,1)S(1)}, bf16[128,2048]{1,0:T(8,128)(2,1)S(1)}, u32[]{:S(2)}, u32[]{:S(2)}) collective-permute-start(bf16[128,2048]{1,0:T(8,128)(2,1)S(1)} %slice_bitcast_fusion.9), channel_id=1, source_target_pairs={{0,8},{1,9},{2,10},{3,11},{4,12},{5,13},{6,14},{7,15},{8,0},{9,1},... | collective-permute-start | bytes 1572872 | tf_op jit(solution)/shard_map/ppermute | solution.py:70
  55.4 39.1 %collective-permute-start.6 = (bf16[144,1792]{1,0:T(8,128)(2,1)S(1)}, bf16[144,1792]{1,0:T(8,128)(2,1)S(1)}, u32[]{:S(2)}, u32[]{:S(2)}) collective-permute-start(bf16[144,1792]{1,0:T(8,128)(2,1)S(1)} %collective-permute-done), channel_id=1, source_target_pairs={{0,2},{1,3},{2,4},{3,5},{4,6},{5,7},{6,0},{7,1},{8,10},{9,11},{10,... | collective-permute-start | bytes 1548296 | tf_op jit(solution)/shard_map/ppermute | solution.py:70
  56.6 38.0 %collective-permute-start.7 = (bf16[144,1792]{1,0:T(8,128)(2,1)}, bf16[144,1792]{1,0:T(8,128)(2,1)S(1)}, u32[]{:S(2)}, u32[]{:S(2)}) collective-permute-start(bf16[144,1792]{1,0:T(8,128)(2,1)} %collective-permute-done.3), channel_id=1, source_target_pairs={{0,2},{1,3},{2,4},{3,5},{4,6},{5,7},{6,0},{7,1},{8,10},{9,11},{10,... | collective-permute-start | bytes 1548296 | tf_op jit(solution)/shard_map/ppermute | solution.py:70
  94.5 4.1 %copy-start.8 = (bf16[1024,896]{1,0:T(8,128)(2,1)}, bf16[1024,896]{1,0:T(8,128)(2,1)S(1)}, u32[]{:S(2)}) copy-start(bf16[1024,896]{1,0:T(8,128)(2,1)S(1)} %collective-permute-done.9) | copy-start | bytes 5505028
  94.6 3.8 %collective-permute-start.10 = (bf16[4,16,128]{2,1,0:T(8,128)(2,1)S(1)}, bf16[4,16,128]{2,1,0:T(8,128)(2,1)S(1)}, u32[]{:S(2)}, u32[]{:S(2)}) collective-permute-start(bf16[4,16,128]{2,1,0:T(8,128)(2,1)S(1)} %pad_maximum_fusion.21), channel_id=1, source_target_pairs={{0,8},{1,9},{2,10},{3,11},{4,12},{5,13},{6,14},{7,15},{8,0},{9,1},... | collective-permute-start | bytes 49160 | tf_op jit(solution)/shard_map/ppermute | solution.py:70
  99.1 2.5 %collective-permute-start.13 = (bf16[4,64,1792]{2,1,0:T(8,128)(2,1)S(1)}, bf16[4,64,1792]{2,1,0:T(8,128)(2,1)S(1)}, u32[]{:S(2)}, u32[]{:S(2)}) collective-permute-start(bf16[4,64,1792]{2,1,0:T(8,128)(2,1)S(1)} %convolution_convert_fusion), channel_id=1, source_target_pairs={{0,1},{1,0},{2,3},{3,2},{4,5},{5,4},{6,7},{7,6},{8,9},{9,8},{10,11... | collective-permute-start | bytes 2752520 | tf_op jit(solution)/shard_map/ppermute | solution.py:70
  99.9 3.1 %collective-permute-start.12 = (bf16[4,64,1792]{2,1,0:T(8,128)(2,1)S(1)}, bf16[4,64,1792]{2,1,0:T(8,128)(2,1)S(1)}, u32[]{:S(2)}, u32[]{:S(2)}) collective-permute-start(bf16[4,64,1792]{2,1,0:T(8,128)(2,1)S(1)} %convolution_convert_fusion.2), channel_id=1, source_target_pairs={{0,1},{1,0},{2,3},{3,2},{4,5},{5,4},{6,7},{7,6},{8,9},{9,8},{10,11... | collective-permute-start | bytes 2752520 | tf_op jit(solution)/shard_map/ppermute | solution.py:70
  101.4 2.0 copy-start.2
  109.7 13.9 %collective-permute-start.14 = (bf16[128,2048]{1,0:T(8,128)(2,1)S(1)}, bf16[128,2048]{1,0:T(8,128)(2,1)S(1)}, u32[]{:S(2)}, u32[]{:S(2)}) collective-permute-start(bf16[128,2048]{1,0:T(8,128)(2,1)S(1)} %get-tuple-element.65), channel_id=1, source_target_pairs={{0,16},{1,17},{2,18},{3,19},{4,20},{5,21},{6,22},{7,23},{8,24},{9,... | collective-permute-start | bytes 1572872 | tf_op jit(solution)/shard_map/ppermute | solution.py:70
  116.0 7.9 %copy-start = (f32[512,2048]{1,0:T(8,128)}, f32[512,2048]{1,0:T(8,128)S(1)}, u32[]{:S(2)}) copy-start(f32[512,2048]{1,0:T(8,128)S(1)} %fusion.8) | copy-start | bytes 12582916
  123.9 7.5 %collective-permute-start.15 = (bf16[128,1024]{1,0:T(8,128)(2,1)S(1)}, bf16[128,1024]{1,0:T(8,128)(2,1)S(1)}, u32[]{:S(2)}, u32[]{:S(2)}) collective-permute-start(bf16[128,1024]{1,0:T(8,128)(2,1)S(1)} %fusion.34), channel_id=1, source_target_pairs={{0,8},{1,9},{2,10},{3,11},{4,12},{5,13},{6,14},{7,15},{8,0},{9,1},... | collective-permute-start | bytes 786440 | tf_op jit(solution)/shard_map/ppermute | solution.py:70
  125.3 8.3 %copy-start.9 = (bf16[1024,896]{1,0:T(8,128)(2,1)S(1)}, bf16[1024,896]{1,0:T(8,128)(2,1)}, u32[]{:S(2)}) copy-start(bf16[1024,896]{1,0:T(8,128)(2,1)} %copy-done.8) | copy-start | bytes 5505028
  125.4 13.3 %collective-permute-start.17 = (bf16[128,2048]{1,0:T(8,128)(2,1)}, bf16[128,2048]{1,0:T(8,128)(2,1)S(1)}, u32[]{:S(2)}, u32[]{:S(2)}) collective-permute-start(bf16[128,2048]{1,0:T(8,128)(2,1)} %get-tuple-element.64), channel_id=1, source_target_pairs={{0,16},{1,17},{2,18},{3,19},{4,20},{5,21},{6,22},{7,23},{8,24},{9,... | collective-permute-start | bytes 1572872 | tf_op jit(solution)/shard_map/ppermute | solution.py:70
  134.5 4.2 %collective-permute-start.16 = (bf16[2,64,1792]{2,1,0:T(8,128)(2,1)S(1)}, bf16[2,64,1792]{2,1,0:T(8,128)(2,1)}, u32[]{:S(2)}, u32[]{:S(2)}) collective-permute-start(bf16[2,64,1792]{2,1,0:T(8,128)(2,1)S(1)} %get-tuple-element.79), channel_id=1, source_target_pairs={{0,1},{1,0},{2,3},{3,2},{4,5},{5,4},{6,7},{7,6},{8,9},{9,8},{10,11... | collective-permute-start | bytes 1376264 | tf_op jit(solution)/shard_map/ppermute | solution.py:70
  134.9 5.5 %copy-start.1 = (f32[512,2048]{1,0:T(8,128)S(1)}, f32[512,2048]{1,0:T(8,128)}, u32[]{:S(2)}) copy-start(f32[512,2048]{1,0:T(8,128)} %copy-done) | copy-start | bytes 12582916
  134.9 14.9 %collective-permute-start.19 = (bf16[128,2048]{1,0:T(8,128)(2,1)S(1)}, bf16[128,2048]{1,0:T(8,128)(2,1)S(1)}, u32[]{:S(2)}, u32[]{:S(2)}) collective-permute-start(bf16[128,2048]{1,0:T(8,128)(2,1)S(1)} %get-tuple-element.63), channel_id=1, source_target_pairs={{0,16},{1,17},{2,18},{3,19},{4,20},{5,21},{6,22},{7,23},{8,24},{9,... | collective-permute-start | bytes 1572872 | tf_op jit(solution)/shard_map/ppermute | solution.py:70
  140.1 15.3 %collective-permute-start.18 = (bf16[128,1792]{1,0:T(8,128)(2,1)S(1)}, bf16[128,1792]{1,0:T(8,128)(2,1)S(1)}, u32[]{:S(2)}, u32[]{:S(2)}) collective-permute-start(bf16[128,1792]{1,0:T(8,128)(2,1)S(1)} %get-tuple-element.77), channel_id=1, source_target_pairs={{0,2},{1,3},{2,4},{3,5},{4,6},{5,7},{6,0},{7,1},{8,10},{9,11},{10,... | collective-permute-start | bytes 1376264 | tf_op jit(solution)/shard_map/ppermute | solution.py:70
  140.5 15.0 %copy-start.10 = (bf16[1024,896]{1,0:T(8,128)(2,1)S(1)}, bf16[1024,896]{1,0:T(8,128)(2,1)}, u32[]{:S(2)}) copy-start(bf16[1024,896]{1,0:T(8,128)(2,1)} %copy-done.8) | copy-start | bytes 5505028
  140.6 14.8 %collective-permute-start.22 = (bf16[128,1024]{1,0:T(8,128)(2,1)S(1)}, bf16[128,1024]{1,0:T(8,128)(2,1)S(1)}, u32[]{:S(2)}, u32[]{:S(2)}) collective-permute-start(bf16[128,1024]{1,0:T(8,128)(2,1)S(1)} %fusion.33), channel_id=1, source_target_pairs={{0,8},{1,9},{2,10},{3,11},{4,12},{5,13},{6,14},{7,15},{8,0},{9,1},... | collective-permute-start | bytes 786440 | tf_op jit(solution)/shard_map/ppermute | solution.py:70
  143.1 17.7 %collective-permute-start.20 = (bf16[128,2048]{1,0:T(8,128)(2,1)S(1)}, bf16[128,2048]{1,0:T(8,128)(2,1)S(1)}, u32[]{:S(2)}, u32[]{:S(2)}) collective-permute-start(bf16[128,2048]{1,0:T(8,128)(2,1)S(1)} %get-tuple-element.62), channel_id=1, source_target_pairs={{0,16},{1,17},{2,18},{3,19},{4,20},{5,21},{6,22},{7,23},{8,24},{9,... | collective-permute-start | bytes 1572872 | tf_op jit(solution)/shard_map/ppermute | solution.py:70
  143.7 30.6 %collective-permute-start.24 = (bf16[128,1792]{1,0:T(8,128)(2,1)S(1)}, bf16[128,1792]{1,0:T(8,128)(2,1)S(1)}, u32[]{:S(2)}, u32[]{:S(2)}) collective-permute-start(bf16[128,1792]{1,0:T(8,128)(2,1)S(1)} %get-tuple-element.76), channel_id=1, source_target_pairs={{0,2},{1,3},{2,4},{3,5},{4,6},{5,7},{6,0},{7,1},{8,10},{9,11},{10,... | collective-permute-start | bytes 1376264 | tf_op jit(solution)/shard_map/ppermute | solution.py:70
  155.5 1.5 copy-start.7
  157.8 16.5 %collective-permute-start.23 = (bf16[2,64,1792]{2,1,0:T(8,128)(2,1)S(1)}, bf16[2,64,1792]{2,1,0:T(8,128)(2,1)S(1)}, u32[]{:S(2)}, u32[]{:S(2)}) collective-permute-start(bf16[2,64,1792]{2,1,0:T(8,128)(2,1)S(1)} %get-tuple-element.71), channel_id=1, source_target_pairs={{0,1},{1,0},{2,3},{3,2},{4,5},{5,4},{6,7},{7,6},{8,9},{9,8},{10,11... | collective-permute-start | bytes 1376264 | tf_op jit(solution)/shard_map/ppermute | solution.py:70
  158.2 9.2 %collective-permute-start.27 = (bf16[128,1024]{1,0:T(8,128)(2,1)S(1)}, bf16[128,1024]{1,0:T(8,128)(2,1)S(1)}, u32[]{:S(2)}, u32[]{:S(2)}) collective-permute-start(bf16[128,1024]{1,0:T(8,128)(2,1)S(1)} %fusion.32), channel_id=1, source_target_pairs={{0,8},{1,9},{2,10},{3,11},{4,12},{5,13},{6,14},{7,15},{8,0},{9,1},... | collective-permute-start | bytes 786440 | tf_op jit(solution)/shard_map/ppermute | solution.py:70
  161.1 11.6 %collective-permute-start.21 = (bf16[128,1024]{1,0:T(8,128)(2,1)S(1)}, bf16[128,1024]{1,0:T(8,128)(2,1)S(1)}, u32[]{:S(2)}, u32[]{:S(2)}) collective-permute-start(bf16[128,1024]{1,0:T(8,128)(2,1)S(1)} %fusion.31), channel_id=1, source_target_pairs={{0,8},{1,9},{2,10},{3,11},{4,12},{5,13},{6,14},{7,15},{8,0},{9,1},... | collective-permute-start | bytes 786440 | tf_op jit(solution)/shard_map/ppermute | solution.py:70
  169.0 8.3 %collective-permute-start.28 = (bf16[2,64,1792]{2,1,0:T(8,128)(2,1)S(1)}, bf16[2,64,1792]{2,1,0:T(8,128)(2,1)S(1)}, u32[]{:S(2)}, u32[]{:S(2)}) collective-permute-start(bf16[2,64,1792]{2,1,0:T(8,128)(2,1)S(1)} %get-tuple-element.73), channel_id=1, source_target_pairs={{0,1},{1,0},{2,3},{3,2},{4,5},{5,4},{6,7},{7,6},{8,9},{9,8},{10,11... | collective-permute-start | bytes 1376264 | tf_op jit(solution)/shard_map/ppermute | solution.py:70
  174.8 43.2 %collective-permute-start.31 = (bf16[128,1792]{1,0:T(8,128)(2,1)S(1)}, bf16[128,1792]{1,0:T(8,128)(2,1)S(1)}, u32[]{:S(2)}, u32[]{:S(2)}) collective-permute-start(bf16[128,1792]{1,0:T(8,128)(2,1)S(1)} %get-tuple-element.68), channel_id=1, source_target_pairs={{0,14},{1,15},{2,8},{3,9},{4,10},{5,11},{6,12},{7,13},{8,6},{9,7},... | collective-permute-start | bytes 1376264 | tf_op jit(solution)/shard_map/ppermute | solution.py:70
  175.8 4.7 %collective-permute-start.25 = (bf16[2,64,1792]{2,1,0:T(8,128)(2,1)S(1)}, bf16[2,64,1792]{2,1,0:T(8,128)(2,1)S(1)}, u32[]{:S(2)}, u32[]{:S(2)}) collective-permute-start(bf16[2,64,1792]{2,1,0:T(8,128)(2,1)S(1)} %get-tuple-element.50), channel_id=1, source_target_pairs={{0,1},{1,0},{2,3},{3,2},{4,5},{5,4},{6,7},{7,6},{8,9},{9,8},{10,11... | collective-permute-start | bytes 1376264 | tf_op jit(solution)/shard_map/ppermute | solution.py:70
  175.8 41.9 %collective-permute-start.26 = (bf16[128,1792]{1,0:T(8,128)(2,1)S(1)}, bf16[128,1792]{1,0:T(8,128)(2,1)S(1)}, u32[]{:S(2)}, u32[]{:S(2)}) collective-permute-start(bf16[128,1792]{1,0:T(8,128)(2,1)S(1)} %get-tuple-element.69), channel_id=1, source_target_pairs={{0,6},{1,7},{2,0},{3,1},{4,2},{5,3},{6,4},{7,5},{8,14},{9,15},{10,... | collective-permute-start | bytes 1376264 | tf_op jit(solution)/shard_map/ppermute | solution.py:70
  178.0 40.0 %collective-permute-start.32 = (bf16[128,1792]{1,0:T(8,128)(2,1)S(1)}, bf16[128,1792]{1,0:T(8,128)(2,1)S(1)}, u32[]{:S(2)}, u32[]{:S(2)}) collective-permute-start(bf16[128,1792]{1,0:T(8,128)(2,1)S(1)} %get-tuple-element.66), channel_id=1, source_target_pairs={{0,10},{1,11},{2,12},{3,13},{4,14},{5,15},{6,8},{7,9},{8,2},{9,3},... | collective-permute-start | bytes 1376264 | tf_op jit(solution)/shard_map/ppermute | solution.py:70
  179.1 38.6 %collective-permute-start.29 = (bf16[128,1792]{1,0:T(8,128)(2,1)S(1)}, bf16[128,1792]{1,0:T(8,128)(2,1)S(1)}, u32[]{:S(2)}, u32[]{:S(2)}) collective-permute-start(bf16[128,1792]{1,0:T(8,128)(2,1)S(1)} %get-tuple-element.67), channel_id=1, source_target_pairs={{0,2},{1,3},{2,4},{3,5},{4,6},{5,7},{6,0},{7,1},{8,10},{9,11},{10,... | collective-permute-start | bytes 1376264 | tf_op jit(solution)/shard_map/ppermute | solution.py:70
  180.9 37.1 %collective-permute-start.30 = (bf16[128,1792]{1,0:T(8,128)(2,1)S(1)}, bf16[128,1792]{1,0:T(8,128)(2,1)S(1)}, u32[]{:S(2)}, u32[]{:S(2)}) collective-permute-start(bf16[128,1792]{1,0:T(8,128)(2,1)S(1)} %fusion.37), channel_id=1, source_target_pairs={{0,8},{1,9},{2,10},{3,11},{4,12},{5,13},{6,14},{7,15},{8,0},{9,1},... | collective-permute-start | bytes 1376264 | tf_op jit(solution)/shard_map/ppermute | solution.py:70
  218.3 0.9 copy-start.3

commit v7 on v6

--- a/solution.py
+++ b/solution.py
@@ -5,7 +5,7 @@
 
 BF = jnp.bfloat16
 F32 = jnp.float32
-CUTS = ((0, 3), (3, 6), (6, 7))
+CUTS = ((0, 5), (5, 7))
 
 
 def gathered(tokens, gate_up, down_proj, expert_ids, gate_weights):
@@ -92,12 +92,12 @@
     ]
     down_y = send(down, flip=2)
 
-    seen = [{0: first, 1: send(first, 1)}, {1: send(second, 1, 2), 0: send(second, 0, 2)}]
-    seen[0][3], seen[1][3] = send(first, -1), send(second, -1, 2)
-    seen, gate_x[0] = together((seen, gate_x[0]))
-    seen[0][2], seen[1][2] = send(seen[0][1], 1), send(seen[1][1], 1)
-    seen[0][2], seen[1][2], gate_x[1], down_y = together(
-        (seen[0][2], seen[1][2], gate_x[1], down_y)
+    pair = send(second, flip=2)
+    seen = [{0: own, 1: send(own, 1), 3: send(own, -1)} for own in (first, pair)]
+    for held in seen:
+        held[2] = send(held[1], 1)
+    seen[0][2], seen[1][2], seen[1][3], gate_x[0], down_y = together(
+        (seen[0][2], seen[1][2], seen[1][3], gate_x[0], down_y)
     )
 
     chosen = jnp.stack([e, e ^ 1]).astype(jnp.int32)
@@ -118,7 +118,7 @@
     info_x = send(infos[0], flip=1)
     place0, pay0 = places(infos[0])
     place1, _ = places(infos[1])
-    place1, gate_x[2] = together((place1, gate_x[2]))
+    place1, gate_x[1] = together((place1, gate_x[1]))
 
     def choose(place, held):
         def of(expert):
@@ -141,6 +141,7 @@
     sent, chosen0 = together((sent, chosen0))
     part = [send(sent[k], flip=2) for k in order]
     near = product(chosen0)
+    near, info_x = together((near, info_x))
     pay = jnp.stack([pay0, places(info_x)[1]])
 
     hidden, away, out = {}, {}, {}

time: 220 us -> 221 us (level)
  matrix products: 22.9 us -> 37.2 us
  starting transfers between devices: 45.9 us -> 35.2 us
  waiting for transfers between devices: 133 us -> 128 us
  other arithmetic: 2.53 us -> 5.01 us
    ppermute x33 -> x32, starting transfers between devices: 45.9 us -> 35.2 us  [send(): lax.ppermute(value, ('dp', 'expert'), [(i * owners + j, (i ^ flip) * owne...]
    dot_general x8, matrix products: 7.2 us -> 17.7 us  [down_product(): jnp.dot(joined, w, preferred_element_type=F32).astype(BF)]
    ppermute x33 -> x32, waiting for transfers between devices: 133 us -> 128 us  [send(): lax.ppermute(value, ('dp', 'expert'), [(i * owners + j, (i ^ flip) * owne...]
    slice x2, local copies, waits for them, and re-layouts: 4.61 us -> 1.3 us  [paired(): gate[quarter * lo // 7:quarter * hi // 7]]
    dot_general x4, matrix products: 1.84 us -> 5.1 us  [of(): jnp.einsum('zst,ztk->zsk', place[:, expert], held, preferred_element_type...]
  transfers between devices with their start and end apart: 33 -> 32, of which waited for: 18 -> 15; matrix products, arithmetic and copies ran while one was open for 12% -> 22% of each run, Pallas kernels for 0% -> 0%
where the time goes in v7:
time: 221 us
  waiting for transfers between devices  128 us (58%)
  matrix products  37.2 us (17%)
  starting transfers between devices  35.2 us (16%)
  local copies, waits for them, and re-layouts  14.3 us (6%)
  other arithmetic  5.01 us (2%)
    ppermute x32, waiting for transfers between devices, send(): lax.ppermute(value, ('dp', 'expert'), [(i * owners + j, (i ^ flip) * owne...  128 us
    ppermute x32, starting transfers between devices, send(): lax.ppermute(value, ('dp', 'expert'), [(i * owners + j, (i ^ flip) * owne...  35.2 us
    dot_general x8, matrix products, down_product(): jnp.dot(joined, w, preferred_element_type=F32).astype(BF)  17.7 us
    dot_general x2, matrix products, product(): jnp.dot(flat, weights, preferred_element_type=F32)  11.2 us
    dot_general x4, matrix products, of(): jnp.einsum('zst,ztk->zsk', place[:, expert], held, preferred_element_type...  5.1 us
  transfers between devices with their start and end apart: 32, of which 15 were waited for; matrix products, arithmetic and copies ran while one was open for 22% of the time, Pallas kernels for 0%

profile of v7, /device:TPU:0, one launch (start us, length us, event | category | flops | bytes accessed | tf_op | source)
XLA Modules:
  0.0 220.5 jit_solution(13534215246714100917)
XLA Ops:
  0.0 0.7 convert_element_type.155
  0.7 0.7 fusion.69
  1.4 1.5 constant_dynamic-slice_fusion.1
  2.9 1.0 fusion.33
  3.9 3.0 %collective-permute-start = (bf16[144,1792]{1,0:T(8,128)(2,1)}, bf16[144,1792]{1,0:T(8,128)(2,1)}, u32[]{:S(2)}, u32[]{:S(2)}) collective-permute-start(bf16[144,1792]{1,0:T(8,128)(2,1)} %get-tuple-element.80), channel_id=1, source_target_pairs={{0,2},{1,3},{2,4},{3,5},{4,6},{5,7},{6,0},{7,1},{8,10},{9,11},{10,... | collective-permute-start | bytes 1548296 | tf_op jit(solution)/shard_map/ppermute | solution.py:70
  6.9 2.0 collective-permute-start.8
  9.0 1.7 collective-permute-start.2
  10.9 1.6 collective-permute-start.6
  12.4 0.5 collective-permute-start.7
  12.9 1.1 slice_bitcast_fusion.1
  14.2 9.8 %collective-permute-done.2 = bf16[144,1792]{1,0:T(8,128)(2,1)} collective-permute-done((bf16[144,1792]{1,0:T(8,128)(2,1)}, bf16[144,1792]{1,0:T(8,128)(2,1)}, u32[]{:S(2)}, u32[]{:S(2)}) %collective-permute-start.2) | collective-permute-done | bytes 516128 | tf_op jit(solution)/shard_map/ppermute | solution.py:70
  24.0 0.7 slice_bitcast_fusion.33
  24.7 8.2 %collective-permute-start.5 = (bf16[144,1792]{1,0:T(8,128)(2,1)}, bf16[144,1792]{1,0:T(8,128)(2,1)S(1)}, u32[]{:S(2)}, u32[]{:S(2)}) collective-permute-start(bf16[144,1792]{1,0:T(8,128)(2,1)} %collective-permute-done.2), channel_id=1, source_target_pairs={{0,6},{1,7},{2,0},{3,1},{4,2},{5,3},{6,4},{7,5},{8,14},{9,15},{10,... | collective-permute-start | bytes 1548296 | tf_op jit(solution)/shard_map/ppermute | solution.py:70
  33.6 0.7 slice_bitcast_fusion.34
  34.2 1.1 slice_bitcast_fusion.21
  35.4 1.2 slice_bitcast_fusion.22
  36.6 0.7 slice_bitcast_fusion.35
  37.3 1.0 slice_bitcast_fusion.24
  38.4 5.6 %collective-permute-done.3 = bf16[144,1792]{1,0:T(8,128)(2,1)S(1)} collective-permute-done((bf16[144,1792]{1,0:T(8,128)(2,1)}, bf16[144,1792]{1,0:T(8,128)(2,1)S(1)}, u32[]{:S(2)}, u32[]{:S(2)}) %collective-permute-start.3) | collective-permute-done | bytes 516128 | tf_op jit(solution)/shard_map/ppermute | solution.py:70
  44.0 22.1 %collective-permute-done.1 = bf16[144,1792]{1,0:T(8,128)(2,1)S(1)} collective-permute-done((bf16[144,1792]{1,0:T(8,128)(2,1)}, bf16[144,1792]{1,0:T(8,128)(2,1)S(1)}, u32[]{:S(2)}, u32[]{:S(2)}) %collective-permute-start.1) | collective-permute-done | bytes 516128 | tf_op jit(solution)/shard_map/ppermute | solution.py:70
  66.1 1.7 collective-permute-start.9
  67.8 8.5 %collective-permute-done.4 = bf16[144,1792]{1,0:T(8,128)(2,1)S(1)} collective-permute-done((bf16[144,1792]{1,0:T(8,128)(2,1)S(1)}, bf16[144,1792]{1,0:T(8,128)(2,1)S(1)}, u32[]{:S(2)}, u32[]{:S(2)}) %collective-permute-start.4) | collective-permute-done | bytes 516128 | tf_op jit(solution)/shard_map/ppermute | solution.py:70
  76.7 1.4 convolution_convert_fusion
  78.4 12.8 %collective-permute-done.9 = bf16[256,2048]{1,0:T(8,128)(2,1)S(1)} collective-permute-done((bf16[256,2048]{1,0:T(8,128)(2,1)S(1)}, bf16[256,2048]{1,0:T(8,128)(2,1)S(1)}, u32[]{:S(2)}, u32[]{:S(2)}) %collective-permute-start.9) | collective-permute-done | bytes 1048608 | tf_op jit(solution)/shard_map/ppermute | solution.py:70
  91.2 1.4 convolution_convert_fusion.2
  92.8 1.5 collective-permute-start.12
  94.4 1.8 convolution_convert_fusion.1
  96.8 0.6 copy-done.12
  97.4 1.4 copy-done.3
  98.8 5.7 %fusion.2 = bf16[4,128,2048]{2,1,0:T(8,128)(2,1)S(1)} fusion(bf16[256,2048]{1,0:T(8,128)(2,1)S(1)} %copy-done.12, bf16[640,2048]{1,0:T(8,128)(2,1)} %collective-permute-done.6, bf16[896,2048]{1,0:T(8,128)(2,1)S(1)} %bitcast.185, bf16[4,64,1792]{2,1,0:T(8,128)(2,1)} %collective-permute-done.10, bf16[4,64,1792]{2,1,0:T(8,128)(2,1)S(1)} %convolution_convert_fusion.3), kind=kOutput, calls=%fused_computation.3 | convolution fusion | flops 3784835072 | bytes 11272192 | tf_op jit(solution)/shard_map/dot_general | solution.py:137
  104.6 1.0 slice_bitcast_fusion.5
  106.0 5.5 %fusion = f32[4,128,2048]{2,1,0:T(8,128)S(1)} fusion(bf16[4,128,1792]{2,1,0:T(8,128)(2,1)S(1)} %pad_maximum_fusion.2, bf16[256,2048]{1,0:T(8,128)(2,1)S(1)} %copy-done.12, bf16[640,2048]{1,0:T(8,128)(2,1)} %collective-permute-done.6, bf16[896,2048]{1,0:T(8,128)(2,1)S(1)} %bitcast.186), kind=kOutput, calls=%fused_computation.1 | convolution fusion | flops 3780116480 | bytes 13369344 | tf_op jit(solution)/shard_map/dot_general | solution.py:137
  111.5 8.0 %collective-permute-done.13 = bf16[128,2048]{1,0:T(8,128)(2,1)S(1)} collective-permute-done((bf16[128,2048]{1,0:T(8,128)(2,1)S(1)}, bf16[128,2048]{1,0:T(8,128)(2,1)S(1)}, u32[]{:S(2)}, u32[]{:S(2)}) %collective-permute-start.13) | collective-permute-done | bytes 524320 | tf_op jit(solution)/shard_map/ppermute | solution.py:70
  119.9 0.6 collective-permute-start.14
  120.9 0.6 collective-permute-start.16
  121.6 6.0 %collective-permute-done.14 = bf16[128,1024]{1,0:T(8,128)(2,1)S(1)} collective-permute-done((bf16[128,1024]{1,0:T(8,128)(2,1)S(1)}, bf16[128,1024]{1,0:T(8,128)(2,1)S(1)}, u32[]{:S(2)}, u32[]{:S(2)}) %collective-permute-start.14) | collective-permute-done | bytes 262176 | tf_op jit(solution)/shard_map/ppermute | solution.py:70
  127.6 2.2 %convolution_convert_fusion.13 = bf16[256,896]{1,0:T(8,128)(2,1)S(1)} fusion(bf16[128,1024]{1,0:T(8,128)(2,1)S(1)} %collective-permute-done.14, bf16[128,1024]{1,0:T(8,128)(2,1)S(1)} %fusion.31, bf16[1,1024,896]{2,1,0:T(8,128)(2,1)} %param.7), kind=kOutput, calls=%fused_computation.24 | convolution fusion | flops 471040000 | bytes 2818048 | tf_op jit(solution)/shard_map/dot_general | solution.py:158
  129.8 2.2 %convolution_convert_fusion.12 = bf16[256,896]{1,0:T(8,128)(2,1)S(1)} fusion(bf16[1024,896]{1,0:T(8,128)(2,1)} %collective-permute-done.7, bf16[128,1024]{1,0:T(8,128)(2,1)S(1)} %collective-permute-done.14, bf16[128,1024]{1,0:T(8,128)(2,1)S(1)} %fusion.31), kind=kOutput, calls=%fused_computation.23 | convolution fusion | flops 471040000 | bytes 2818048 | tf_op jit(solution)/shard_map/dot_general | solution.py:158
  132.5 0.6 collective-permute-start.18
  133.2 1.0 collective-permute-done.16
  134.2 1.6 convolution_convert_fusion.5
  136.2 1.3 collective-permute-start.21
  137.6 0.8 collective-permute-start.19
  138.4 1.3 collective-permute-start.23
  139.6 7.7 %collective-permute-done.18 = bf16[128,2048]{1,0:T(8,128)(2,1)S(1)} collective-permute-done((bf16[128,2048]{1,0:T(8,128)(2,1)S(1)}, bf16[128,2048]{1,0:T(8,128)(2,1)S(1)}, u32[]{:S(2)}, u32[]{:S(2)}) %collective-permute-start.18) | collective-permute-done | bytes 524320 | tf_op jit(solution)/shard_map/ppermute | solution.py:70
  147.3 3.8 %collective-permute-done.17 = bf16[128,1792]{1,0:T(8,128)(2,1)S(1)} collective-permute-done((bf16[128,1792]{1,0:T(8,128)(2,1)S(1)}, bf16[128,1792]{1,0:T(8,128)(2,1)S(1)}, u32[]{:S(2)}, u32[]{:S(2)}) %collective-permute-start.17) | collective-permute-done | bytes 458784 | tf_op jit(solution)/shard_map/ppermute | solution.py:70
  151.1 2.2 %convolution_convert_fusion.8 = bf16[256,896]{1,0:T(8,128)(2,1)S(1)} fusion(bf16[256,1024]{1,0:T(8,128)(2,1)S(1)} %constant_dynamic-update-slice_fusion, bf16[1024,896]{1,0:T(8,128)(2,1)} %collective-permute-done.7), kind=kOutput, calls=%fused_computation.19 | convolution fusion | flops 469991424 | bytes 2818048 | tf_op jit(solution)/shard_map/dot_general | solution.py:158
  153.3 2.2 %convolution_convert_fusion.9 = bf16[256,896]{1,0:T(8,128)(2,1)S(1)} fusion(bf16[256,1024]{1,0:T(8,128)(2,1)S(1)} %constant_dynamic-update-slice_fusion, bf16[1,1024,896]{2,1,0:T(8,128)(2,1)} %param.7), kind=kOutput, calls=%fused_computation.20 | convolution fusion | flops 469991424 | bytes 2818048 | tf_op jit(solution)/shard_map/dot_general | solution.py:158
  156.1 1.4 collective-permute-start.26
  157.5 0.6 collective-permute-done.19
  158.4 0.6 collective-permute-start.20
  159.1 6.2 %collective-permute-done.26 = bf16[128,1024]{1,0:T(8,128)(2,1)S(1)} collective-permute-done((bf16[128,1024]{1,0:T(8,128)(2,1)S(1)}, bf16[128,1024]{1,0:T(8,128)(2,1)S(1)}, u32[]{:S(2)}, u32[]{:S(2)}) %collective-permute-start.26) | collective-permute-done | bytes 262176 | tf_op jit(solution)/shard_map/ppermute | solution.py:70
  165.2 2.2 %convolution_convert_fusion.6 = bf16[256,896]{1,0:T(8,128)(2,1)S(1)} fusion(bf16[256,1024]{1,0:T(8,128)(2,1)S(1)} %constant_dynamic-update-slice_fusion.2, bf16[1024,896]{1,0:T(8,128)(2,1)} %collective-permute-done.7), kind=kOutput, calls=%fused_computation.17 | convolution fusion | flops 469991424 | bytes 2818048 | tf_op jit(solution)/shard_map/dot_general | solution.py:158
  167.5 2.2 %convolution_convert_fusion.7 = bf16[256,896]{1,0:T(8,128)(2,1)S(1)} fusion(bf16[256,1024]{1,0:T(8,128)(2,1)S(1)} %constant_dynamic-update-slice_fusion.2, bf16[1,1024,896]{2,1,0:T(8,128)(2,1)} %param.7), kind=kOutput, calls=%fused_computation.18 | convolution fusion | flops 469991424 | bytes 2818048 | tf_op jit(solution)/shard_map/dot_general | solution.py:158
  169.9 0.5 collective-permute-done.20
  170.5 2.2 %convolution_convert_fusion.11 = bf16[256,896]{1,0:T(8,128)(2,1)S(1)} fusion(bf16[128,1024]{1,0:T(8,128)(2,1)S(1)} %collective-permute-done.20, bf16[128,1024]{1,0:T(8,128)(2,1)S(1)} %fusion.28, bf16[1,1024,896]{2,1,0:T(8,128)(2,1)} %param.7), kind=kOutput, calls=%fused_computation.22 | convolution fusion | flops 471040000 | bytes 2818048 | tf_op jit(solution)/shard_map/dot_general | solution.py:158
  172.7 2.2 %convolution_convert_fusion.10 = bf16[256,896]{1,0:T(8,128)(2,1)S(1)} fusion(bf16[1024,896]{1,0:T(8,128)(2,1)} %collective-permute-done.7, bf16[128,1024]{1,0:T(8,128)(2,1)S(1)} %collective-permute-done.20, bf16[128,1024]{1,0:T(8,128)(2,1)S(1)} %fusion.28), kind=kOutput, calls=%fused_computation.21 | convolution fusion | flops 471040000 | bytes 2818048 | tf_op jit(solution)/shard_map/dot_general | solution.py:158
  175.5 0.8 collective-permute-start.30
  177.3 1.9 collective-permute-start.31
  179.3 1.9 collective-permute-start.28
  181.6 1.4 collective-permute-start.29
  183.0 35.3 %collective-permute-done.25 = bf16[128,1792]{1,0:T(8,128)(2,1)S(1)} collective-permute-done((bf16[128,1792]{1,0:T(8,128)(2,1)S(1)}, bf16[128,1792]{1,0:T(8,128)(2,1)S(1)}, u32[]{:S(2)}, u32[]{:S(2)}) %collective-permute-start.25) | collective-permute-done | bytes 458784 | tf_op jit(solution)/shard_map/ppermute | solution.py:70
  218.9 0.9 copy-done.5
  219.8 0.7 slice_dynamic-update-slice_fusion
  (122 shorter events, 8.4 us)
Async XLA Ops:
  1.4 9.3 %copy-start.2 = (bf16[1,896,2048]{2,1,0:T(8,128)(2,1)S(1)}, bf16[1,896,2048]{2,1,0:T(8,128)(2,1)}, u32[]{:S(2)}) copy-start(bf16[1,896,2048]{2,1,0:T(8,128)(2,1)} %param.6) | copy-start | bytes 11010052
  3.9 20.8 %collective-permute-start = (bf16[144,1792]{1,0:T(8,128)(2,1)}, bf16[144,1792]{1,0:T(8,128)(2,1)}, u32[]{:S(2)}, u32[]{:S(2)}) collective-permute-start(bf16[144,1792]{1,0:T(8,128)(2,1)} %get-tuple-element.80), channel_id=1, source_target_pairs={{0,2},{1,3},{2,4},{3,5},{4,6},{5,7},{6,0},{7,1},{8,10},{9,11},{10,... | collective-permute-start | bytes 1548296 | tf_op jit(solution)/shard_map/ppermute | solution.py:70
  6.9 26.2 %collective-permute-start.8 = (bf16[144,1792]{1,0:T(8,128)(2,1)}, bf16[144,1792]{1,0:T(8,128)(2,1)}, u32[]{:S(2)}, u32[]{:S(2)}) collective-permute-start(bf16[144,1792]{1,0:T(8,128)(2,1)} %get-tuple-element.80), channel_id=1, source_target_pairs={{0,6},{1,7},{2,0},{3,1},{4,2},{5,3},{6,4},{7,5},{8,14},{9,15},{10,... | collective-permute-start | bytes 1548296 | tf_op jit(solution)/shard_map/ppermute | solution.py:70
  9.0 15.0 %collective-permute-start.2 = (bf16[144,1792]{1,0:T(8,128)(2,1)}, bf16[144,1792]{1,0:T(8,128)(2,1)}, u32[]{:S(2)}, u32[]{:S(2)}) collective-permute-start(bf16[144,1792]{1,0:T(8,128)(2,1)} %get-tuple-element.79), channel_id=1, source_target_pairs={{0,16},{1,17},{2,18},{3,19},{4,20},{5,21},{6,22},{7,23},{8,24},{9,... | collective-permute-start | bytes 1548296 | tf_op jit(solution)/shard_map/ppermute | solution.py:70
  10.9 65.4 %collective-permute-start.6 = (bf16[640,2048]{1,0:T(8,128)(2,1)S(1)}, bf16[640,2048]{1,0:T(8,128)(2,1)}, u32[]{:S(2)}, u32[]{:S(2)}) collective-permute-start(bf16[640,2048]{1,0:T(8,128)(2,1)S(1)} %slice_bitcast_fusion), channel_id=1, source_target_pairs={{0,8},{1,9},{2,10},{3,11},{4,12},{5,13},{6,14},{7,15},{8,0},{9,1},... | collective-permute-start | bytes 7864328 | tf_op jit(solution)/shard_map/ppermute | solution.py:70
  12.4 63.9 %collective-permute-start.7 = (bf16[1024,896]{1,0:T(8,128)(2,1)}, bf16[1024,896]{1,0:T(8,128)(2,1)}, u32[]{:S(2)}, u32[]{:S(2)}) collective-permute-start(bf16[1024,896]{1,0:T(8,128)(2,1)} %bitcast.4), channel_id=1, source_target_pairs={{0,16},{1,17},{2,18},{3,19},{4,20},{5,21},{6,22},{7,23},{8,24},{9,... | collective-permute-start | bytes 5505032 | tf_op jit(solution)/shard_map/ppermute | solution.py:70
  23.9 20.0 %collective-permute-start.3 = (bf16[144,1792]{1,0:T(8,128)(2,1)}, bf16[144,1792]{1,0:T(8,128)(2,1)S(1)}, u32[]{:S(2)}, u32[]{:S(2)}) collective-permute-start(bf16[144,1792]{1,0:T(8,128)(2,1)} %collective-permute-done.2), channel_id=1, source_target_pairs={{0,2},{1,3},{2,4},{3,5},{4,6},{5,7},{6,0},{7,1},{8,10},{9,11},{10,... | collective-permute-start | bytes 1548296 | tf_op jit(solution)/shard_map/ppermute | solution.py:70
  24.7 43.1 %collective-permute-start.5 = (bf16[144,1792]{1,0:T(8,128)(2,1)}, bf16[144,1792]{1,0:T(8,128)(2,1)S(1)}, u32[]{:S(2)}, u32[]{:S(2)}) collective-permute-start(bf16[144,1792]{1,0:T(8,128)(2,1)} %collective-permute-done.2), channel_id=1, source_target_pairs={{0,6},{1,7},{2,0},{3,1},{4,2},{5,3},{6,4},{7,5},{8,14},{9,15},{10,... | collective-permute-start | bytes 1548296 | tf_op jit(solution)/shard_map/ppermute | solution.py:70
  33.1 33.0 %collective-permute-start.1 = (bf16[144,1792]{1,0:T(8,128)(2,1)}, bf16[144,1792]{1,0:T(8,128)(2,1)S(1)}, u32[]{:S(2)}, u32[]{:S(2)}) collective-permute-start(bf16[144,1792]{1,0:T(8,128)(2,1)} %collective-permute-done), channel_id=1, source_target_pairs={{0,2},{1,3},{2,4},{3,5},{4,6},{5,7},{6,0},{7,1},{8,10},{9,11},{10,... | collective-permute-start | bytes 1548296 | tf_op jit(solution)/shard_map/ppermute | solution.py:70
  34.2 31.8 %copy-start.4 = (bf16[256,2048]{1,0:T(8,128)(2,1)S(1)}, bf16[256,2048]{1,0:T(8,128)(2,1)}, u32[]{:S(2)}) copy-start(bf16[256,2048]{1,0:T(8,128)(2,1)} %slice_bitcast_fusion.1) | copy-start | bytes 3145732
  35.4 41.3 %copy-start.6 = (bf16[1,128,1792]{2,1,0:T(8,128)(2,1)}, bf16[1,128,1792]{2,1,0:T(8,128)(2,1)S(1)}, u32[]{:S(2)}) copy-start(bf16[1,128,1792]{2,1,0:T(8,128)(2,1)S(1)} %slice_bitcast_fusion.21) | copy-start | bytes 1376260
  36.6 41.6 %copy-start.7 = (bf16[1,128,1792]{2,1,0:T(8,128)(2,1)}, bf16[1,128,1792]{2,1,0:T(8,128)(2,1)S(1)}, u32[]{:S(2)}) copy-start(bf16[1,128,1792]{2,1,0:T(8,128)(2,1)S(1)} %slice_bitcast_fusion.22) | copy-start | bytes 1376260
  43.9 32.3 %collective-permute-start.4 = (bf16[144,1792]{1,0:T(8,128)(2,1)S(1)}, bf16[144,1792]{1,0:T(8,128)(2,1)S(1)}, u32[]{:S(2)}, u32[]{:S(2)}) collective-permute-start(bf16[144,1792]{1,0:T(8,128)(2,1)S(1)} %collective-permute-done.3), channel_id=1, source_target_pairs={{0,2},{1,3},{2,4},{3,5},{4,6},{5,7},{6,0},{7,1},{8,10},{9,11},{10,... | collective-permute-start | bytes 1548296 | tf_op jit(solution)/shard_map/ppermute | solution.py:70
  44.0 47.3 %copy-start.8 = (bf16[1,128,1792]{2,1,0:T(8,128)(2,1)}, bf16[1,128,1792]{2,1,0:T(8,128)(2,1)S(1)}, u32[]{:S(2)}) copy-start(bf16[1,128,1792]{2,1,0:T(8,128)(2,1)S(1)} %slice_bitcast_fusion.23) | copy-start | bytes 1376260
  66.1 25.2 %collective-permute-start.9 = (bf16[256,2048]{1,0:T(8,128)(2,1)S(1)}, bf16[256,2048]{1,0:T(8,128)(2,1)S(1)}, u32[]{:S(2)}, u32[]{:S(2)}) collective-permute-start(bf16[256,2048]{1,0:T(8,128)(2,1)S(1)} %copy-done.4), channel_id=1, source_target_pairs={{0,8},{1,9},{2,10},{3,11},{4,12},{5,13},{6,14},{7,15},{8,0},{9,1},... | collective-permute-start | bytes 3145736 | tf_op jit(solution)/shard_map/ppermute | solution.py:70
  76.3 1.8 copy-start.10
  78.2 18.5 %collective-permute-start.11 = (bf16[4,64,1792]{2,1,0:T(8,128)(2,1)}, bf16[4,64,1792]{2,1,0:T(8,128)(2,1)S(1)}, u32[]{:S(2)}, u32[]{:S(2)}) collective-permute-start(bf16[4,64,1792]{2,1,0:T(8,128)(2,1)} %convolution_convert_fusion), channel_id=1, source_target_pairs={{0,1},{1,0},{2,3},{3,2},{4,5},{5,4},{6,7},{7,6},{8,9},{9,8},{10,11... | collective-permute-start | bytes 2752520 | tf_op jit(solution)/shard_map/ppermute | solution.py:70
  91.2 1.4 copy-start.11
  92.7 4.2 %collective-permute-start.10 = (bf16[4,64,1792]{2,1,0:T(8,128)(2,1)}, bf16[4,64,1792]{2,1,0:T(8,128)(2,1)}, u32[]{:S(2)}, u32[]{:S(2)}) collective-permute-start(bf16[4,64,1792]{2,1,0:T(8,128)(2,1)} %convolution_convert_fusion.2), channel_id=1, source_target_pairs={{0,1},{1,0},{2,3},{3,2},{4,5},{5,4},{6,7},{7,6},{8,9},{9,8},{10,11... | collective-permute-start | bytes 2752520 | tf_op jit(solution)/shard_map/ppermute | solution.py:70
  92.8 18.8 %collective-permute-start.12 = (bf16[4,16,128]{2,1,0:T(8,128)(2,1)S(1)}, bf16[4,16,128]{2,1,0:T(8,128)(2,1)S(1)}, u32[]{:S(2)}, u32[]{:S(2)}) collective-permute-start(bf16[4,16,128]{2,1,0:T(8,128)(2,1)S(1)} %pad_maximum_fusion.18), channel_id=1, source_target_pairs={{0,8},{1,9},{2,10},{3,11},{4,12},{5,13},{6,14},{7,15},{8,0},{9,1},... | collective-permute-start | bytes 49160 | tf_op jit(solution)/shard_map/ppermute | solution.py:70
  94.4 1.8 copy-start.9
  96.2 1.2 copy-start.12
  96.7 2.1 copy-start.3
  105.5 14.1 %collective-permute-start.13 = (bf16[128,2048]{1,0:T(8,128)(2,1)S(1)}, bf16[128,2048]{1,0:T(8,128)(2,1)S(1)}, u32[]{:S(2)}, u32[]{:S(2)}) collective-permute-start(bf16[128,2048]{1,0:T(8,128)(2,1)S(1)} %get-tuple-element.54), channel_id=1, source_target_pairs={{0,16},{1,17},{2,18},{3,19},{4,20},{5,21},{6,22},{7,23},{8,24},{9,... | collective-permute-start | bytes 1572872 | tf_op jit(solution)/shard_map/ppermute | solution.py:70
  111.5 8.4 %copy-start = (f32[4,128,2048]{2,1,0:T(8,128)}, f32[4,128,2048]{2,1,0:T(8,128)S(1)}, u32[]{:S(2)}) copy-start(f32[4,128,2048]{2,1,0:T(8,128)S(1)} %fusion) | copy-start | bytes 12582916
  119.9 7.7 %collective-permute-start.14 = (bf16[128,1024]{1,0:T(8,128)(2,1)S(1)}, bf16[128,1024]{1,0:T(8,128)(2,1)S(1)}, u32[]{:S(2)}, u32[]{:S(2)}) collective-permute-start(bf16[128,1024]{1,0:T(8,128)(2,1)S(1)} %fusion.31), channel_id=1, source_target_pairs={{0,8},{1,9},{2,10},{3,11},{4,12},{5,13},{6,14},{7,15},{8,0},{9,1},... | collective-permute-start | bytes 786440 | tf_op jit(solution)/shard_map/ppermute | solution.py:70
  120.9 13.2 %collective-permute-start.16 = (bf16[128,2048]{1,0:T(8,128)(2,1)}, bf16[128,2048]{1,0:T(8,128)(2,1)S(1)}, u32[]{:S(2)}, u32[]{:S(2)}) collective-permute-start(bf16[128,2048]{1,0:T(8,128)(2,1)} %get-tuple-element.53), channel_id=1, source_target_pairs={{0,16},{1,17},{2,18},{3,19},{4,20},{5,21},{6,22},{7,23},{8,24},{9,... | collective-permute-start | bytes 1572872 | tf_op jit(solution)/shard_map/ppermute | solution.py:70
  132.1 2.0 collective-permute-start.15
  132.5 14.8 %collective-permute-start.18 = (bf16[128,2048]{1,0:T(8,128)(2,1)S(1)}, bf16[128,2048]{1,0:T(8,128)(2,1)S(1)}, u32[]{:S(2)}, u32[]{:S(2)}) collective-permute-start(bf16[128,2048]{1,0:T(8,128)(2,1)S(1)} %get-tuple-element.52), channel_id=1, source_target_pairs={{0,16},{1,17},{2,18},{3,19},{4,20},{5,21},{6,22},{7,23},{8,24},{9,... | collective-permute-start | bytes 1572872 | tf_op jit(solution)/shard_map/ppermute | solution.py:70
  133.1 2.8 %copy-start.1 = (f32[4,128,2048]{2,1,0:T(8,128)S(1)}, f32[4,128,2048]{2,1,0:T(8,128)}, u32[]{:S(2)}) copy-start(f32[4,128,2048]{2,1,0:T(8,128)} %copy-done) | copy-start | bytes 12582916
  135.8 15.2 %collective-permute-start.17 = (bf16[128,1792]{1,0:T(8,128)(2,1)S(1)}, bf16[128,1792]{1,0:T(8,128)(2,1)S(1)}, u32[]{:S(2)}, u32[]{:S(2)}) collective-permute-start(bf16[128,1792]{1,0:T(8,128)(2,1)S(1)} %get-tuple-element.66), channel_id=1, source_target_pairs={{0,2},{1,3},{2,4},{3,5},{4,6},{5,7},{6,0},{7,1},{8,10},{9,11},{10,... | collective-permute-start | bytes 1376264 | tf_op jit(solution)/shard_map/ppermute | solution.py:70
  136.2 14.8 %collective-permute-start.21 = (bf16[128,1024]{1,0:T(8,128)(2,1)S(1)}, bf16[128,1024]{1,0:T(8,128)(2,1)S(1)}, u32[]{:S(2)}, u32[]{:S(2)}) collective-permute-start(bf16[128,1024]{1,0:T(8,128)(2,1)S(1)} %fusion.30), channel_id=1, source_target_pairs={{0,8},{1,9},{2,10},{3,11},{4,12},{5,13},{6,14},{7,15},{8,0},{9,1},... | collective-permute-start | bytes 786440 | tf_op jit(solution)/shard_map/ppermute | solution.py:70
  137.6 20.6 %collective-permute-start.19 = (bf16[128,2048]{1,0:T(8,128)(2,1)S(1)}, bf16[128,2048]{1,0:T(8,128)(2,1)S(1)}, u32[]{:S(2)}, u32[]{:S(2)}) collective-permute-start(bf16[128,2048]{1,0:T(8,128)(2,1)S(1)} %get-tuple-element.51), channel_id=1, source_target_pairs={{0,16},{1,17},{2,18},{3,19},{4,20},{5,21},{6,22},{7,23},{8,24},{9,... | collective-permute-start | bytes 1572872 | tf_op jit(solution)/shard_map/ppermute | solution.py:70
  138.4 36.7 %collective-permute-start.23 = (bf16[128,1792]{1,0:T(8,128)(2,1)S(1)}, bf16[128,1792]{1,0:T(8,128)(2,1)S(1)}, u32[]{:S(2)}, u32[]{:S(2)}) collective-permute-start(bf16[128,1792]{1,0:T(8,128)(2,1)S(1)} %get-tuple-element.65), channel_id=1, source_target_pairs={{0,2},{1,3},{2,4},{3,5},{4,6},{5,7},{6,0},{7,1},{8,10},{9,11},{10,... | collective-permute-start | bytes 1376264 | tf_op jit(solution)/shard_map/ppermute | solution.py:70
  155.7 19.4 %collective-permute-start.22 = (bf16[2,64,1792]{2,1,0:T(8,128)(2,1)S(1)}, bf16[2,64,1792]{2,1,0:T(8,128)(2,1)S(1)}, u32[]{:S(2)}, u32[]{:S(2)}) collective-permute-start(bf16[2,64,1792]{2,1,0:T(8,128)(2,1)S(1)} %get-tuple-element.60), channel_id=1, source_target_pairs={{0,1},{1,0},{2,3},{3,2},{4,5},{5,4},{6,7},{7,6},{8,9},{9,8},{10,11... | collective-permute-start | bytes 1376264 | tf_op jit(solution)/shard_map/ppermute | solution.py:70
  156.1 9.2 %collective-permute-start.26 = (bf16[128,1024]{1,0:T(8,128)(2,1)S(1)}, bf16[128,1024]{1,0:T(8,128)(2,1)S(1)}, u32[]{:S(2)}, u32[]{:S(2)}) collective-permute-start(bf16[128,1024]{1,0:T(8,128)(2,1)S(1)} %fusion.29), channel_id=1, source_target_pairs={{0,8},{1,9},{2,10},{3,11},{4,12},{5,13},{6,14},{7,15},{8,0},{9,1},... | collective-permute-start | bytes 786440 | tf_op jit(solution)/shard_map/ppermute | solution.py:70
  158.4 12.0 %collective-permute-start.20 = (bf16[128,1024]{1,0:T(8,128)(2,1)S(1)}, bf16[128,1024]{1,0:T(8,128)(2,1)S(1)}, u32[]{:S(2)}, u32[]{:S(2)}) collective-permute-start(bf16[128,1024]{1,0:T(8,128)(2,1)S(1)} %fusion.28), channel_id=1, source_target_pairs={{0,8},{1,9},{2,10},{3,11},{4,12},{5,13},{6,14},{7,15},{8,0},{9,1},... | collective-permute-start | bytes 786440 | tf_op jit(solution)/shard_map/ppermute | solution.py:70
  169.9 6.9 %collective-permute-start.27 = (bf16[2,64,1792]{2,1,0:T(8,128)(2,1)S(1)}, bf16[2,64,1792]{2,1,0:T(8,128)(2,1)S(1)}, u32[]{:S(2)}, u32[]{:S(2)}) collective-permute-start(bf16[2,64,1792]{2,1,0:T(8,128)(2,1)S(1)} %get-tuple-element.62), channel_id=1, source_target_pairs={{0,1},{1,0},{2,3},{3,2},{4,5},{5,4},{6,7},{7,6},{8,9},{9,8},{10,11... | collective-permute-start | bytes 1376264 | tf_op jit(solution)/shard_map/ppermute | solution.py:70
  175.5 43.1 %collective-permute-start.30 = (bf16[128,1792]{1,0:T(8,128)(2,1)S(1)}, bf16[128,1792]{1,0:T(8,128)(2,1)S(1)}, u32[]{:S(2)}, u32[]{:S(2)}) collective-permute-start(bf16[128,1792]{1,0:T(8,128)(2,1)S(1)} %get-tuple-element.57), channel_id=1, source_target_pairs={{0,14},{1,15},{2,8},{3,9},{4,10},{5,11},{6,12},{7,13},{8,6},{9,7},... | collective-permute-start | bytes 1376264 | tf_op jit(solution)/shard_map/ppermute | solution.py:70
  176.3 4.8 %collective-permute-start.24 = (bf16[2,64,1792]{2,1,0:T(8,128)(2,1)S(1)}, bf16[2,64,1792]{2,1,0:T(8,128)(2,1)S(1)}, u32[]{:S(2)}, u32[]{:S(2)}) collective-permute-start(bf16[2,64,1792]{2,1,0:T(8,128)(2,1)S(1)} %get-tuple-element.42), channel_id=1, source_target_pairs={{0,1},{1,0},{2,3},{3,2},{4,5},{5,4},{6,7},{7,6},{8,9},{9,8},{10,11... | collective-permute-start | bytes 1376264 | tf_op jit(solution)/shard_map/ppermute | solution.py:70
  176.3 42.0 %collective-permute-start.25 = (bf16[128,1792]{1,0:T(8,128)(2,1)S(1)}, bf16[128,1792]{1,0:T(8,128)(2,1)S(1)}, u32[]{:S(2)}, u32[]{:S(2)}) collective-permute-start(bf16[128,1792]{1,0:T(8,128)(2,1)S(1)} %get-tuple-element.58), channel_id=1, source_target_pairs={{0,6},{1,7},{2,0},{3,1},{4,2},{5,3},{6,4},{7,5},{8,14},{9,15},{10,... | collective-permute-start | bytes 1376264 | tf_op jit(solution)/shard_map/ppermute | solution.py:70
  177.3 41.3 %collective-permute-start.31 = (bf16[128,1792]{1,0:T(8,128)(2,1)S(1)}, bf16[128,1792]{1,0:T(8,128)(2,1)S(1)}, u32[]{:S(2)}, u32[]{:S(2)}) collective-permute-start(bf16[128,1792]{1,0:T(8,128)(2,1)S(1)} %get-tuple-element.55), channel_id=1, source_target_pairs={{0,10},{1,11},{2,12},{3,13},{4,14},{5,15},{6,8},{7,9},{8,2},{9,3},... | collective-permute-start | bytes 1376264 | tf_op jit(solution)/shard_map/ppermute | solution.py:70
  179.3 39.0 %collective-permute-start.28 = (bf16[128,1792]{1,0:T(8,128)(2,1)S(1)}, bf16[128,1792]{1,0:T(8,128)(2,1)S(1)}, u32[]{:S(2)}, u32[]{:S(2)}) collective-permute-start(bf16[128,1792]{1,0:T(8,128)(2,1)S(1)} %get-tuple-element.56), channel_id=1, source_target_pairs={{0,2},{1,3},{2,4},{3,5},{4,6},{5,7},{6,0},{7,1},{8,10},{9,11},{10,... | collective-permute-start | bytes 1376264 | tf_op jit(solution)/shard_map/ppermute | solution.py:70
  181.6 37.0 %collective-permute-start.29 = (bf16[128,1792]{1,0:T(8,128)(2,1)S(1)}, bf16[128,1792]{1,0:T(8,128)(2,1)S(1)}, u32[]{:S(2)}, u32[]{:S(2)}) collective-permute-start(bf16[128,1792]{1,0:T(8,128)(2,1)S(1)} %fusion.34), channel_id=1, source_target_pairs={{0,8},{1,9},{2,10},{3,11},{4,12},{5,13},{6,14},{7,15},{8,0},{9,1},... | collective-permute-start | bytes 1376264 | tf_op jit(solution)/shard_map/ppermute | solution.py:70
  218.9 0.9 copy-start.5

commit v8 on v7

--- a/solution.py
+++ b/solution.py
@@ -5,8 +5,6 @@
 
 BF = jnp.bfloat16
 F32 = jnp.float32
-CUTS = ((0, 5), (5, 7))
-
 
 def gathered(tokens, gate_up, down_proj, expert_ids, gate_weights):
     owners = lax.axis_size("expert")
@@ -55,7 +53,6 @@
     owners = lax.axis_size("expert")
     chips = owners // 2
     tok = tokens.shape[0]
-    top = expert_ids.shape[1]
     quarter = gate_up.shape[1]
     half = 2 * quarter
     ff = down_proj.shape[1]
@@ -80,45 +77,40 @@
     def depths(r):
         return lax.dynamic_slice_in_dim(tokens, (d ^ r) * quarter, quarter, axis=1)
 
-    info = jnp.concatenate([expert_ids.astype(BF), gate_weights], axis=1).T
-    info = jnp.pad(info, ((0, 0), (0, half - tok)))
+    info = jnp.concatenate([expert_ids.T.astype(BF), gate_weights.T], axis=1)
+    info = jnp.pad(info, ((0, 0), (0, half - 2 * tok)))
 
     def payload(r):
         return jnp.concatenate([jnp.concatenate([depths(r), depths(r + 1)], axis=1), info])
 
     first, second = payload(0), payload(2)
-    gate_x = [
-        send(gate[quarter * lo // 7 : quarter * hi // 7], flip=1) for lo, hi in CUTS
-    ]
+    gate_x = send(gate, flip=1)
     down_y = send(down, flip=2)
 
     pair = send(second, flip=2)
     seen = [{0: own, 1: send(own, 1), 3: send(own, -1)} for own in (first, pair)]
     for held in seen:
         held[2] = send(held[1], 1)
-    seen[0][2], seen[1][2], seen[1][3], gate_x[0], down_y = together(
-        (seen[0][2], seen[1][2], seen[1][3], gate_x[0], down_y)
-    )
+    seen[1][2], down_y = together((seen[1][2], down_y))
 
     chosen = jnp.stack([e, e ^ 1]).astype(jnp.int32)
     earlier = jnp.triu(jnp.ones((tok, tok), BF), 1)
 
     def places(info):
-        matches = info[:, None, :top].astype(jnp.int32) == chosen[:, None, None]
+        matches = info[:, None, :, :tok].astype(jnp.int32) == chosen[:, None, None]
         hits = jnp.any(matches, axis=2)
-        weight = jnp.sum(jnp.where(matches, info[:, None, top:].astype(F32), 0.0), axis=2)
+        weight = jnp.sum(jnp.where(matches, info[:, None, :, tok:].astype(F32), 0.0), axis=2)
         rank = jnp.dot(hits.astype(BF), earlier, preferred_element_type=F32)
         rank = jnp.where(hits, rank, -1.0)
         place = (rank[..., None, :] == jnp.arange(slots, dtype=F32)[:, None]).astype(BF)
         pay = place * weight[..., None, :].astype(BF)
         return place, pay.reshape(chips, chunk, tok)
 
-    infos = [jnp.stack([seen[g][k][tok:, :tok] for k in range(chips)]) for g in range(2)]
+    infos = [jnp.stack([seen[g][k][tok:, : 2 * tok] for k in range(chips)]) for g in range(2)]
     helds = [jnp.stack([seen[g][k][:tok] for k in range(chips)]) for g in range(2)]
     info_x = send(infos[0], flip=1)
     place0, pay0 = places(infos[0])
     place1, _ = places(infos[1])
-    place1, gate_x[1] = together((place1, gate_x[1]))
 
     def choose(place, held):
         def of(expert):
@@ -130,7 +122,9 @@
         return jnp.concatenate([of(0), other], axis=1)
 
     chosen0, chosen1 = choose(place0, helds[0]), choose(place1, helds[1])
-    weights = jnp.concatenate([gate, *gate_x])
+    downs = jnp.concatenate([down, down_y], axis=1)
+    chosen1, gate_x, downs = together((chosen1, gate_x, downs))
+    weights = jnp.concatenate([gate, gate_x])
 
     def product(rows):
         flat = rows.reshape(-1, half)
@@ -154,10 +148,8 @@
     def down_product(q):
         own = hidden[q][0]
         joined = jnp.concatenate([own, hidden[q][1]])
-        value = jnp.concatenate(
-            [jnp.dot(joined, w, preferred_element_type=F32).astype(BF) for w in (down, down_y)],
-            axis=1,
-        ).reshape(2, 2, slots, half)
+        value = jnp.dot(joined, downs, preferred_element_type=F32).astype(BF)
+        value = value.reshape(2, 2, slots, half)
         out[q], away[q] = value[:, 0], value[:, 1]
 
     def weigh(q, came):

time: 221 us -> 206 us (0.932)
  waiting for transfers between devices: 128 us -> 117 us
  matrix products: 37.2 us -> 27.2 us
  other arithmetic: 5.01 us -> 9.75 us
  starting transfers between devices: 35.2 us -> 38.7 us
  local copies, waits for them, and re-layouts: 14.3 us -> 11.6 us
    dot_general x8 -> x4, matrix products: 17.7 us -> 6.51 us  [down_product(): value = jnp.dot(joined, downs, preferred_element_type=F32).astype(BF)]
    ppermute x32 -> x31, waiting for transfers between devices: 128 us -> 117 us  [send(): lax.ppermute(value, ('dp', 'expert'), [(i * owners + j, (i ^ flip) * owne...]
    ppermute x32 -> x31, starting transfers between devices: 35.2 us -> 38.7 us  [send(): lax.ppermute(value, ('dp', 'expert'), [(i * owners + j, (i ^ flip) * owne...]
    concatenate x4 -> x1, other arithmetic: 0.27 us -> 3.72 us  [paired(): downs = jnp.concatenate([down, down_y], axis=1)]
  transfers between devices with their start and end apart: 32 -> 31, of which waited for: 15 -> 14; matrix products, arithmetic and copies ran while one was open for 22% -> 21% of each run, Pallas kernels for 0% -> 0%
where the time goes in v8:
time: 206 us; the launch traced here: 205 us
  waiting for transfers between devices  117 us (57%)
  starting transfers between devices  38.7 us (19%)
  matrix products  27.2 us (13%)
  local copies, waits for them, and re-layouts  11.6 us (6%)
  other arithmetic  9.75 us (5%)
    ppermute x31, waiting for transfers between devices, send(): lax.ppermute(value, ('dp', 'expert'), [(i * owners + j, (i ^ flip) * owne...  117 us
    ppermute x31, starting transfers between devices, send(): lax.ppermute(value, ('dp', 'expert'), [(i * owners + j, (i ^ flip) * owne...  38.7 us
    dot_general x2, matrix products, product(): jnp.dot(flat, weights, preferred_element_type=F32)  11.7 us
    dot_general x4, matrix products, down_product(): value = jnp.dot(joined, downs, preferred_element_type=F32).astype(BF)  6.51 us
    dot_general x4, matrix products, of(): jnp.einsum('zst,ztk->zsk', place[:, expert], held, preferred_element_type...  6.01 us
  transfers between devices with their start and end apart: 31, of which 14 were waited for; matrix products, arithmetic and copies ran while one was open for 21% of the time, Pallas kernels for 0%

profile of v8, /device:TPU:0, one launch (start us, length us, event | category | flops | bytes accessed | tf_op | source)
XLA Modules:
  0.0 205.1 jit_solution(10995743969895652140)
XLA Ops:
  0.0 0.7 convert_bitcast_fusion
  0.7 0.7 fusion.93
  1.4 1.5 constant_dynamic-slice_fusion.3
  2.9 3.0 %collective-permute-start.3 = (bf16[136,1792]{1,0:T(8,128)(2,1)S(1)}, bf16[136,1792]{1,0:T(8,128)(2,1)}, u32[]{:S(2)}, u32[]{:S(2)}) collective-permute-start(bf16[136,1792]{1,0:T(8,128)(2,1)S(1)} %get-tuple-element.76), channel_id=1, source_target_pairs={{0,16},{1,17},{2,18},{3,19},{4,20},{5,21},{6,22},{7,23},{8,24},{9,... | collective-permute-start | bytes 1462280 | tf_op jit(solution)/shard_map/ppermute | solution.py:67
  6.0 1.6 collective-permute-start
  7.5 2.2 %collective-permute-start.2 = (bf16[136,1792]{1,0:T(8,128)(2,1)S(1)}, bf16[136,1792]{1,0:T(8,128)(2,1)}, u32[]{:S(2)}, u32[]{:S(2)}) collective-permute-start(bf16[136,1792]{1,0:T(8,128)(2,1)S(1)} %get-tuple-element.75), channel_id=1, source_target_pairs={{0,6},{1,7},{2,0},{3,1},{4,2},{5,3},{6,4},{7,5},{8,14},{9,15},{10,... | collective-permute-start | bytes 1462280 | tf_op jit(solution)/shard_map/ppermute | solution.py:67
  9.8 0.3 collective-permute-start.6
  10.1 1.7 collective-permute-start.9
  11.8 0.8 maximum_bitcast_fusion.5
  12.8 5.3 %collective-permute-done.3 = bf16[136,1792]{1,0:T(8,128)(2,1)} collective-permute-done((bf16[136,1792]{1,0:T(8,128)(2,1)S(1)}, bf16[136,1792]{1,0:T(8,128)(2,1)}, u32[]{:S(2)}, u32[]{:S(2)}) %collective-permute-start.3) | collective-permute-done | bytes 487456 | tf_op jit(solution)/shard_map/ppermute | solution.py:67
  18.0 2.1 %collective-permute-start.4 = (bf16[136,1792]{1,0:T(8,128)(2,1)}, bf16[136,1792]{1,0:T(8,128)(2,1)S(1)}, u32[]{:S(2)}, u32[]{:S(2)}) collective-permute-start(bf16[136,1792]{1,0:T(8,128)(2,1)} %collective-permute-done.3), channel_id=1, source_target_pairs={{0,2},{1,3},{2,4},{3,5},{4,6},{5,7},{6,0},{7,1},{8,10},{9,11},{10,... | collective-permute-start | bytes 1462280 | tf_op jit(solution)/shard_map/ppermute | solution.py:67
  20.2 1.1 slice_bitcast_fusion.24
  21.2 0.7 collective-permute-done
  22.0 10.4 %collective-permute-start.7 = (bf16[136,1792]{1,0:T(8,128)(2,1)}, bf16[136,1792]{1,0:T(8,128)(2,1)S(1)}, u32[]{:S(2)}, u32[]{:S(2)}) collective-permute-start(bf16[136,1792]{1,0:T(8,128)(2,1)} %collective-permute-done.3), channel_id=1, source_target_pairs={{0,6},{1,7},{2,0},{3,1},{4,2},{5,3},{6,4},{7,5},{8,14},{9,15},{10,... | collective-permute-start | bytes 1462280 | tf_op jit(solution)/shard_map/ppermute | solution.py:67
  32.3 1.0 slice_bitcast_fusion.21
  33.5 1.1 slice_bitcast_fusion.19
  34.6 0.7 slice_bitcast_fusion.36
  35.3 0.7 slice_bitcast_fusion.37
  35.9 0.7 slice_bitcast_fusion.39
  36.6 25.7 %collective-permute-done.1 = bf16[136,1792]{1,0:T(8,128)(2,1)S(1)} collective-permute-done((bf16[136,1792]{1,0:T(8,128)(2,1)}, bf16[136,1792]{1,0:T(8,128)(2,1)S(1)}, u32[]{:S(2)}, u32[]{:S(2)}) %collective-permute-start.1) | collective-permute-done | bytes 487456 | tf_op jit(solution)/shard_map/ppermute | solution.py:67
  62.3 1.6 collective-permute-start.11
  64.0 13.1 %collective-permute-done.5 = bf16[136,1792]{1,0:T(8,128)(2,1)S(1)} collective-permute-done((bf16[136,1792]{1,0:T(8,128)(2,1)S(1)}, bf16[136,1792]{1,0:T(8,128)(2,1)S(1)}, u32[]{:S(2)}, u32[]{:S(2)}) %collective-permute-start.5) | collective-permute-done | bytes 487456 | tf_op jit(solution)/shard_map/ppermute | solution.py:67
  77.5 1.4 convolution_convert_fusion
  79.1 1.4 convolution_convert_fusion.2
  80.5 0.5 collective-permute-start.8
  81.0 1.4 convolution_convert_fusion.1
  82.6 1.9 convolution_convert_fusion.3
  84.4 3.7 %pad_maximum_fusion = bf16[1024,1792]{1,0:T(8,128)(2,1)} fusion(bf16[1024,896]{1,0:T(8,128)(2,1)} %collective-permute-done.6, bf16[1024,896]{1,0:T(8,128)(2,1)S(1)} %bitcast.167), kind=kLoop, calls=%fused_computation.3 | loop fusion | flops 7340032 | bytes 7340032 | tf_op jit(solution)/shard_map/concatenate | solution.py:125
  88.3 1.5 pad_maximum_fusion.2
  89.8 1.0 collective-permute-done.9
  90.8 6.0 %fusion.2 = bf16[4,128,2048]{2,1,0:T(8,128)(2,1)S(1)} fusion(bf16[4,128,1792]{2,1,0:T(8,128)(2,1)S(1)} %pad_maximum_fusion.2, bf16[896,2048]{1,0:T(8,128)(2,1)} %collective-permute-done.9, bf16[896,2048]{1,0:T(8,128)(2,1)S(1)} %bitcast.178), kind=kOutput, calls=%fused_computation.4 | convolution fusion | flops 3773825024 | bytes 11272192 | tf_op jit(solution)/shard_map/dot_general | solution.py:131
  96.8 1.0 slice_bitcast_fusion.3
  97.8 1.5 collective-permute-start.12
  99.3 5.7 %fusion = f32[4,128,2048]{2,1,0:T(8,128)S(1)} fusion(bf16[4,128,1792]{2,1,0:T(8,128)(2,1)S(1)} %pad_maximum_fusion.4, bf16[896,2048]{1,0:T(8,128)(2,1)} %collective-permute-done.9, bf16[896,2048]{1,0:T(8,128)(2,1)S(1)} %bitcast.179), kind=kOutput, calls=%fused_computation.1 | convolution fusion | flops 3772776448 | bytes 13369344 | tf_op jit(solution)/shard_map/dot_general | solution.py:131
  105.1 6.4 %collective-permute-done.12 = bf16[128,2048]{1,0:T(8,128)(2,1)S(1)} collective-permute-done((bf16[128,2048]{1,0:T(8,128)(2,1)S(1)}, bf16[128,2048]{1,0:T(8,128)(2,1)S(1)}, u32[]{:S(2)}, u32[]{:S(2)}) %collective-permute-start.12) | collective-permute-done | bytes 524320 | tf_op jit(solution)/shard_map/ppermute | solution.py:67
  111.7 0.6 collective-permute-start.13
  112.8 0.8 collective-permute-start.15
  113.7 5.2 %collective-permute-done.13 = bf16[128,1024]{1,0:T(8,128)(2,1)S(1)} collective-permute-done((bf16[128,1024]{1,0:T(8,128)(2,1)S(1)}, bf16[128,1024]{1,0:T(8,128)(2,1)S(1)}, u32[]{:S(2)}, u32[]{:S(2)}) %collective-permute-start.13) | collective-permute-done | bytes 262176 | tf_op jit(solution)/shard_map/ppermute | solution.py:67
  118.9 3.1 %convolution_convert_fusion.9 = bf16[256,1792]{1,0:T(8,128)(2,1)S(1)} fusion(bf16[1024,1792]{1,0:T(8,128)(2,1)} %pad_maximum_fusion, bf16[128,1024]{1,0:T(8,128)(2,1)S(1)} %collective-permute-done.13, bf16[128,1024]{1,0:T(8,128)(2,1)S(1)} %fusion.28), kind=kOutput, calls=%fused_computation.14 | convolution fusion | flops 941031424 | bytes 5111808 | tf_op jit(solution)/shard_map/dot_general | solution.py:151
  122.1 0.8 slice_bitcast_fusion.17
  123.4 1.9 collective-permute-done.15
  125.3 1.4 convolution_convert_fusion.5
  127.2 2.0 collective-permute-start.20
  129.2 0.3 collective-permute-start.18
  129.5 8.5 %collective-permute-done.17 = bf16[128,2048]{1,0:T(8,128)(2,1)S(1)} collective-permute-done((bf16[128,2048]{1,0:T(8,128)(2,1)S(1)}, bf16[128,2048]{1,0:T(8,128)(2,1)S(1)}, u32[]{:S(2)}, u32[]{:S(2)}) %collective-permute-start.17) | collective-permute-done | bytes 524320 | tf_op jit(solution)/shard_map/ppermute | solution.py:67
  138.0 4.0 %collective-permute-done.16 = bf16[128,1792]{1,0:T(8,128)(2,1)S(1)} collective-permute-done((bf16[128,1792]{1,0:T(8,128)(2,1)S(1)}, bf16[128,1792]{1,0:T(8,128)(2,1)S(1)}, u32[]{:S(2)}, u32[]{:S(2)}) %collective-permute-start.16) | collective-permute-done | bytes 458784 | tf_op jit(solution)/shard_map/ppermute | solution.py:67
  142.0 1.1 convolution_convert_fusion.7
  143.6 2.1 %collective-permute-start.25 = (bf16[128,1024]{1,0:T(8,128)(2,1)S(1)}, bf16[128,1024]{1,0:T(8,128)(2,1)S(1)}, u32[]{:S(2)}, u32[]{:S(2)}) collective-permute-start(bf16[128,1024]{1,0:T(8,128)(2,1)S(1)} %fusion.26), channel_id=1, source_target_pairs={{0,8},{1,9},{2,10},{3,11},{4,12},{5,13},{6,14},{7,15},{8,0},{9,1},... | collective-permute-start | bytes 786440 | tf_op jit(solution)/shard_map/ppermute | solution.py:67
  145.7 3.1 %collective-permute-done.18 = bf16[128,2048]{1,0:T(8,128)(2,1)S(1)} collective-permute-done((bf16[128,2048]{1,0:T(8,128)(2,1)S(1)}, bf16[128,2048]{1,0:T(8,128)(2,1)S(1)}, u32[]{:S(2)}, u32[]{:S(2)}) %collective-permute-start.18) | collective-permute-done | bytes 524320 | tf_op jit(solution)/shard_map/ppermute | solution.py:67
  149.1 0.7 collective-permute-start.19
  149.8 3.1 %collective-permute-done.25 = bf16[128,1024]{1,0:T(8,128)(2,1)S(1)} collective-permute-done((bf16[128,1024]{1,0:T(8,128)(2,1)S(1)}, bf16[128,1024]{1,0:T(8,128)(2,1)S(1)}, u32[]{:S(2)}, u32[]{:S(2)}) %collective-permute-start.25) | collective-permute-done | bytes 262176 | tf_op jit(solution)/shard_map/ppermute | solution.py:67
  152.9 1.1 convolution_convert_fusion.6
  154.2 4.1 %collective-permute-done.19 = bf16[128,1024]{1,0:T(8,128)(2,1)S(1)} collective-permute-done((bf16[128,1024]{1,0:T(8,128)(2,1)S(1)}, bf16[128,1024]{1,0:T(8,128)(2,1)S(1)}, u32[]{:S(2)}, u32[]{:S(2)}) %collective-permute-start.19) | collective-permute-done | bytes 262176 | tf_op jit(solution)/shard_map/ppermute | solution.py:67
  158.3 1.1 convolution_convert_fusion.8
  159.5 0.4 convolution_convert_fusion.4
  160.0 0.8 collective-permute-start.29
  160.8 0.4 fusion.21
  161.3 2.7 %collective-permute-start.30 = (bf16[128,1792]{1,0:T(8,128)(2,1)S(1)}, bf16[128,1792]{1,0:T(8,128)(2,1)S(1)}, u32[]{:S(2)}, u32[]{:S(2)}) collective-permute-start(bf16[128,1792]{1,0:T(8,128)(2,1)S(1)} %get-tuple-element.51), channel_id=1, source_target_pairs={{0,10},{1,11},{2,12},{3,13},{4,14},{5,15},{6,8},{7,9},{8,2},{9,3},... | collective-permute-start | bytes 1376264 | tf_op jit(solution)/shard_map/ppermute | solution.py:67
  164.0 1.6 collective-permute-start.27
  165.6 0.4 fusion.14
  166.1 1.8 collective-permute-start.28
  167.9 35.0 %collective-permute-done.24 = bf16[128,1792]{1,0:T(8,128)(2,1)S(1)} collective-permute-done((bf16[128,1792]{1,0:T(8,128)(2,1)S(1)}, bf16[128,1792]{1,0:T(8,128)(2,1)S(1)}, u32[]{:S(2)}, u32[]{:S(2)}) %collective-permute-start.24) | collective-permute-done | bytes 458784 | tf_op jit(solution)/shard_map/ppermute | solution.py:67
  203.5 0.9 copy-done.5
  204.4 0.7 slice_dynamic-update-slice_fusion
  (108 shorter events, 4.6 us)
Async XLA Ops:
  1.4 8.4 %copy-start.3 = (bf16[1,1024,896]{2,1,0:T(8,128)(2,1)S(1)}, bf16[1,1024,896]{2,1,0:T(8,128)(2,1)}, u32[]{:S(2)}) copy-start(bf16[1,1024,896]{2,1,0:T(8,128)(2,1)} %param.7) | copy-start | bytes 5505028
  2.9 15.1 %collective-permute-start.3 = (bf16[136,1792]{1,0:T(8,128)(2,1)S(1)}, bf16[136,1792]{1,0:T(8,128)(2,1)}, u32[]{:S(2)}, u32[]{:S(2)}) collective-permute-start(bf16[136,1792]{1,0:T(8,128)(2,1)S(1)} %get-tuple-element.76), channel_id=1, source_target_pairs={{0,16},{1,17},{2,18},{3,19},{4,20},{5,21},{6,22},{7,23},{8,24},{9,... | collective-permute-start | bytes 1462280 | tf_op jit(solution)/shard_map/ppermute | solution.py:67
  6.0 16.0 %collective-permute-start = (bf16[136,1792]{1,0:T(8,128)(2,1)S(1)}, bf16[136,1792]{1,0:T(8,128)(2,1)}, u32[]{:S(2)}, u32[]{:S(2)}) collective-permute-start(bf16[136,1792]{1,0:T(8,128)(2,1)S(1)} %get-tuple-element.75), channel_id=1, source_target_pairs={{0,2},{1,3},{2,4},{3,5},{4,6},{5,7},{6,0},{7,1},{8,10},{9,11},{10,... | collective-permute-start | bytes 1462280 | tf_op jit(solution)/shard_map/ppermute | solution.py:67
  7.5 25.9 %collective-permute-start.2 = (bf16[136,1792]{1,0:T(8,128)(2,1)S(1)}, bf16[136,1792]{1,0:T(8,128)(2,1)}, u32[]{:S(2)}, u32[]{:S(2)}) collective-permute-start(bf16[136,1792]{1,0:T(8,128)(2,1)S(1)} %get-tuple-element.75), channel_id=1, source_target_pairs={{0,6},{1,7},{2,0},{3,1},{4,2},{5,3},{6,4},{7,5},{8,14},{9,15},{10,... | collective-permute-start | bytes 1462280 | tf_op jit(solution)/shard_map/ppermute | solution.py:67
  9.8 67.3 %collective-permute-start.6 = (bf16[1024,896]{1,0:T(8,128)(2,1)S(1)}, bf16[1024,896]{1,0:T(8,128)(2,1)}, u32[]{:S(2)}, u32[]{:S(2)}) collective-permute-start(bf16[1024,896]{1,0:T(8,128)(2,1)S(1)} %bitcast.166), channel_id=1, source_target_pairs={{0,16},{1,17},{2,18},{3,19},{4,20},{5,21},{6,22},{7,23},{8,24},{9,... | collective-permute-start | bytes 5505032 | tf_op jit(solution)/shard_map/ppermute | solution.py:67
  10.1 80.7 %collective-permute-start.9 = (bf16[896,2048]{1,0:T(8,128)(2,1)}, bf16[896,2048]{1,0:T(8,128)(2,1)}, u32[]{:S(2)}, u32[]{:S(2)}) collective-permute-start(bf16[896,2048]{1,0:T(8,128)(2,1)} %bitcast.177), channel_id=1, source_target_pairs={{0,8},{1,9},{2,10},{3,11},{4,12},{5,13},{6,14},{7,15},{8,0},{9,1},... | collective-permute-start | bytes 11010056 | tf_op jit(solution)/shard_map/ppermute | solution.py:67
  18.0 45.8 %collective-permute-start.4 = (bf16[136,1792]{1,0:T(8,128)(2,1)}, bf16[136,1792]{1,0:T(8,128)(2,1)S(1)}, u32[]{:S(2)}, u32[]{:S(2)}) collective-permute-start(bf16[136,1792]{1,0:T(8,128)(2,1)} %collective-permute-done.3), channel_id=1, source_target_pairs={{0,2},{1,3},{2,4},{3,5},{4,6},{5,7},{6,0},{7,1},{8,10},{9,11},{10,... | collective-permute-start | bytes 1462280 | tf_op jit(solution)/shard_map/ppermute | solution.py:67
  21.2 57.8 %copy-start.7 = (bf16[1,128,1792]{2,1,0:T(8,128)(2,1)}, bf16[1,128,1792]{2,1,0:T(8,128)(2,1)S(1)}, u32[]{:S(2)}) copy-start(bf16[1,128,1792]{2,1,0:T(8,128)(2,1)S(1)} %slice_bitcast_fusion.24) | copy-start | bytes 1376260
  22.0 41.9 %collective-permute-start.7 = (bf16[136,1792]{1,0:T(8,128)(2,1)}, bf16[136,1792]{1,0:T(8,128)(2,1)S(1)}, u32[]{:S(2)}, u32[]{:S(2)}) collective-permute-start(bf16[136,1792]{1,0:T(8,128)(2,1)} %collective-permute-done.3), channel_id=1, source_target_pairs={{0,6},{1,7},{2,0},{3,1},{4,2},{5,3},{6,4},{7,5},{8,14},{9,15},{10,... | collective-permute-start | bytes 1462280 | tf_op jit(solution)/shard_map/ppermute | solution.py:67
  33.4 44.1 %copy-start.6 = (bf16[1,128,1792]{2,1,0:T(8,128)(2,1)S(1)}, bf16[1,128,1792]{2,1,0:T(8,128)(2,1)}, u32[]{:S(2)}) copy-start(bf16[1,128,1792]{2,1,0:T(8,128)(2,1)} %maximum_bitcast_fusion.5) | copy-start | bytes 1376260
  33.4 28.9 %collective-permute-start.1 = (bf16[136,1792]{1,0:T(8,128)(2,1)}, bf16[136,1792]{1,0:T(8,128)(2,1)S(1)}, u32[]{:S(2)}, u32[]{:S(2)}) collective-permute-start(bf16[136,1792]{1,0:T(8,128)(2,1)} %collective-permute-done), channel_id=1, source_target_pairs={{0,2},{1,3},{2,4},{3,5},{4,6},{5,7},{6,0},{7,1},{8,10},{9,11},{10,... | collective-permute-start | bytes 1462280 | tf_op jit(solution)/shard_map/ppermute | solution.py:67
  62.3 42.7 %collective-permute-start.11 = (bf16[4,8,256]{2,1,0:T(8,128)(2,1)S(1)}, bf16[4,8,256]{2,1,0:T(8,128)(2,1)S(1)}, u32[]{:S(2)}, u32[]{:S(2)}) collective-permute-start(bf16[4,8,256]{2,1,0:T(8,128)(2,1)S(1)} %pad_maximum_fusion.10), channel_id=1, source_target_pairs={{0,8},{1,9},{2,10},{3,11},{4,12},{5,13},{6,14},{7,15},{8,0},{9,1},... | collective-permute-start | bytes 49160 | tf_op jit(solution)/shard_map/ppermute | solution.py:67
  63.9 13.3 %collective-permute-start.5 = (bf16[136,1792]{1,0:T(8,128)(2,1)S(1)}, bf16[136,1792]{1,0:T(8,128)(2,1)S(1)}, u32[]{:S(2)}, u32[]{:S(2)}) collective-permute-start(bf16[136,1792]{1,0:T(8,128)(2,1)S(1)} %collective-permute-done.4), channel_id=1, source_target_pairs={{0,2},{1,3},{2,4},{3,5},{4,6},{5,7},{6,0},{7,1},{8,10},{9,11},{10,... | collective-permute-start | bytes 1462280 | tf_op jit(solution)/shard_map/ppermute | solution.py:67
  64.0 15.1 %copy-start.8 = (bf16[1,128,1792]{2,1,0:T(8,128)(2,1)}, bf16[1,128,1792]{2,1,0:T(8,128)(2,1)S(1)}, u32[]{:S(2)}) copy-start(bf16[1,128,1792]{2,1,0:T(8,128)(2,1)S(1)} %slice_bitcast_fusion.22) | copy-start | bytes 1376260
  64.0 15.1 %copy-start.9 = (bf16[1,128,1792]{2,1,0:T(8,128)(2,1)}, bf16[1,128,1792]{2,1,0:T(8,128)(2,1)S(1)}, u32[]{:S(2)}) copy-start(bf16[1,128,1792]{2,1,0:T(8,128)(2,1)S(1)} %slice_bitcast_fusion.23) | copy-start | bytes 1376260
  78.8 9.3 %collective-permute-start.10 = (bf16[4,64,1792]{2,1,0:T(8,128)(2,1)}, bf16[4,64,1792]{2,1,0:T(8,128)(2,1)S(1)}, u32[]{:S(2)}, u32[]{:S(2)}) collective-permute-start(bf16[4,64,1792]{2,1,0:T(8,128)(2,1)} %convolution_convert_fusion), channel_id=1, source_target_pairs={{0,1},{1,0},{2,3},{3,2},{4,5},{5,4},{6,7},{7,6},{8,9},{9,8},{10,11... | collective-permute-start | bytes 2752520 | tf_op jit(solution)/shard_map/ppermute | solution.py:67
  79.1 1.4 copy-start.10
  80.5 7.8 %collective-permute-start.8 = (bf16[4,64,1792]{2,1,0:T(8,128)(2,1)}, bf16[4,64,1792]{2,1,0:T(8,128)(2,1)}, u32[]{:S(2)}, u32[]{:S(2)}) collective-permute-start(bf16[4,64,1792]{2,1,0:T(8,128)(2,1)} %convolution_convert_fusion.2), channel_id=1, source_target_pairs={{0,1},{1,0},{2,3},{3,2},{4,5},{5,4},{6,7},{7,6},{8,9},{9,8},{10,11... | collective-permute-start | bytes 2752520 | tf_op jit(solution)/shard_map/ppermute | solution.py:67
  84.4 3.7 %copy-start.4 = (bf16[4,64,1792]{2,1,0:T(8,128)(2,1)S(1)}, bf16[4,64,1792]{2,1,0:T(8,128)(2,1)}, u32[]{:S(2)}) copy-start(bf16[4,64,1792]{2,1,0:T(8,128)(2,1)} %convolution_convert_fusion.1) | copy-start | bytes 2752516
  88.3 2.5 %copy-start.11 = (bf16[1,896,2048]{2,1,0:T(8,128)(2,1)S(1)}, bf16[1,896,2048]{2,1,0:T(8,128)(2,1)}, u32[]{:S(2)}) copy-start(bf16[1,896,2048]{2,1,0:T(8,128)(2,1)} %param.6) | copy-start | bytes 11010052
  97.8 13.6 %collective-permute-start.12 = (bf16[128,2048]{1,0:T(8,128)(2,1)S(1)}, bf16[128,2048]{1,0:T(8,128)(2,1)S(1)}, u32[]{:S(2)}, u32[]{:S(2)}) collective-permute-start(bf16[128,2048]{1,0:T(8,128)(2,1)S(1)} %get-tuple-element.50), channel_id=1, source_target_pairs={{0,16},{1,17},{2,18},{3,19},{4,20},{5,21},{6,22},{7,23},{8,24},{9,... | collective-permute-start | bytes 1572872 | tf_op jit(solution)/shard_map/ppermute | solution.py:67
  105.0 6.7 %copy-start = (f32[4,128,2048]{2,1,0:T(8,128)}, f32[4,128,2048]{2,1,0:T(8,128)S(1)}, u32[]{:S(2)}) copy-start(f32[4,128,2048]{2,1,0:T(8,128)S(1)} %fusion) | copy-start | bytes 12582916
  111.7 7.2 %collective-permute-start.13 = (bf16[128,1024]{1,0:T(8,128)(2,1)S(1)}, bf16[128,1024]{1,0:T(8,128)(2,1)S(1)}, u32[]{:S(2)}, u32[]{:S(2)}) collective-permute-start(bf16[128,1024]{1,0:T(8,128)(2,1)S(1)} %fusion.28), channel_id=1, source_target_pairs={{0,8},{1,9},{2,10},{3,11},{4,12},{5,13},{6,14},{7,15},{8,0},{9,1},... | collective-permute-start | bytes 786440 | tf_op jit(solution)/shard_map/ppermute | solution.py:67
  112.8 12.5 %collective-permute-start.15 = (bf16[128,2048]{1,0:T(8,128)(2,1)}, bf16[128,2048]{1,0:T(8,128)(2,1)S(1)}, u32[]{:S(2)}, u32[]{:S(2)}) collective-permute-start(bf16[128,2048]{1,0:T(8,128)(2,1)} %get-tuple-element.49), channel_id=1, source_target_pairs={{0,16},{1,17},{2,18},{3,19},{4,20},{5,21},{6,22},{7,23},{8,24},{9,... | collective-permute-start | bytes 1572872 | tf_op jit(solution)/shard_map/ppermute | solution.py:67
  122.9 2.4 %collective-permute-start.14 = (bf16[2,64,1792]{2,1,0:T(8,128)(2,1)}, bf16[2,64,1792]{2,1,0:T(8,128)(2,1)}, u32[]{:S(2)}, u32[]{:S(2)}) collective-permute-start(bf16[2,64,1792]{2,1,0:T(8,128)(2,1)} %get-tuple-element.64), channel_id=1, source_target_pairs={{0,1},{1,0},{2,3},{3,2},{4,5},{5,4},{6,7},{7,6},{8,9},{9,8},{10,11... | collective-permute-start | bytes 1376264 | tf_op jit(solution)/shard_map/ppermute | solution.py:67
  123.2 14.8 %collective-permute-start.17 = (bf16[128,2048]{1,0:T(8,128)(2,1)S(1)}, bf16[128,2048]{1,0:T(8,128)(2,1)S(1)}, u32[]{:S(2)}, u32[]{:S(2)}) collective-permute-start(bf16[128,2048]{1,0:T(8,128)(2,1)S(1)} %get-tuple-element.48), channel_id=1, source_target_pairs={{0,16},{1,17},{2,18},{3,19},{4,20},{5,21},{6,22},{7,23},{8,24},{9,... | collective-permute-start | bytes 1572872 | tf_op jit(solution)/shard_map/ppermute | solution.py:67
  123.3 3.5 %copy-start.1 = (f32[4,128,2048]{2,1,0:T(8,128)S(1)}, f32[4,128,2048]{2,1,0:T(8,128)}, u32[]{:S(2)}) copy-start(f32[4,128,2048]{2,1,0:T(8,128)} %copy-done) | copy-start | bytes 12582916
  126.8 15.3 %copy-start.2 = (bf16[1024,1792]{1,0:T(8,128)(2,1)S(1)}, bf16[1024,1792]{1,0:T(8,128)(2,1)}, u32[]{:S(2)}) copy-start(bf16[1024,1792]{1,0:T(8,128)(2,1)} %pad_maximum_fusion) | copy-start | bytes 11010052
  126.8 15.2 %collective-permute-start.16 = (bf16[128,1792]{1,0:T(8,128)(2,1)S(1)}, bf16[128,1792]{1,0:T(8,128)(2,1)S(1)}, u32[]{:S(2)}, u32[]{:S(2)}) collective-permute-start(bf16[128,1792]{1,0:T(8,128)(2,1)S(1)} %get-tuple-element.62), channel_id=1, source_target_pairs={{0,2},{1,3},{2,4},{3,5},{4,6},{5,7},{6,0},{7,1},{8,10},{9,11},{10,... | collective-permute-start | bytes 1376264 | tf_op jit(solution)/shard_map/ppermute | solution.py:67
  127.2 14.9 %collective-permute-start.20 = (bf16[128,1024]{1,0:T(8,128)(2,1)S(1)}, bf16[128,1024]{1,0:T(8,128)(2,1)S(1)}, u32[]{:S(2)}, u32[]{:S(2)}) collective-permute-start(bf16[128,1024]{1,0:T(8,128)(2,1)S(1)} %fusion.27), channel_id=1, source_target_pairs={{0,8},{1,9},{2,10},{3,11},{4,12},{5,13},{6,14},{7,15},{8,0},{9,1},... | collective-permute-start | bytes 786440 | tf_op jit(solution)/shard_map/ppermute | solution.py:67
  129.2 19.6 %collective-permute-start.18 = (bf16[128,2048]{1,0:T(8,128)(2,1)S(1)}, bf16[128,2048]{1,0:T(8,128)(2,1)S(1)}, u32[]{:S(2)}, u32[]{:S(2)}) collective-permute-start(bf16[128,2048]{1,0:T(8,128)(2,1)S(1)} %get-tuple-element.47), channel_id=1, source_target_pairs={{0,16},{1,17},{2,18},{3,19},{4,20},{5,21},{6,22},{7,23},{8,24},{9,... | collective-permute-start | bytes 1572872 | tf_op jit(solution)/shard_map/ppermute | solution.py:67
  129.5 30.0 %collective-permute-start.22 = (bf16[128,1792]{1,0:T(8,128)(2,1)S(1)}, bf16[128,1792]{1,0:T(8,128)(2,1)S(1)}, u32[]{:S(2)}, u32[]{:S(2)}) collective-permute-start(bf16[128,1792]{1,0:T(8,128)(2,1)S(1)} %get-tuple-element.61), channel_id=1, source_target_pairs={{0,2},{1,3},{2,4},{3,5},{4,6},{5,7},{6,0},{7,1},{8,10},{9,11},{10,... | collective-permute-start | bytes 1376264 | tf_op jit(solution)/shard_map/ppermute | solution.py:67
  143.2 16.3 %collective-permute-start.21 = (bf16[2,64,1792]{2,1,0:T(8,128)(2,1)S(1)}, bf16[2,64,1792]{2,1,0:T(8,128)(2,1)S(1)}, u32[]{:S(2)}, u32[]{:S(2)}) collective-permute-start(bf16[2,64,1792]{2,1,0:T(8,128)(2,1)S(1)} %get-tuple-element.56), channel_id=1, source_target_pairs={{0,1},{1,0},{2,3},{3,2},{4,5},{5,4},{6,7},{7,6},{8,9},{9,8},{10,11... | collective-permute-start | bytes 1376264 | tf_op jit(solution)/shard_map/ppermute | solution.py:67
  143.6 9.3 %collective-permute-start.25 = (bf16[128,1024]{1,0:T(8,128)(2,1)S(1)}, bf16[128,1024]{1,0:T(8,128)(2,1)S(1)}, u32[]{:S(2)}, u32[]{:S(2)}) collective-permute-start(bf16[128,1024]{1,0:T(8,128)(2,1)S(1)} %fusion.26), channel_id=1, source_target_pairs={{0,8},{1,9},{2,10},{3,11},{4,12},{5,13},{6,14},{7,15},{8,0},{9,1},... | collective-permute-start | bytes 786440 | tf_op jit(solution)/shard_map/ppermute | solution.py:67
  149.1 9.2 %collective-permute-start.19 = (bf16[128,1024]{1,0:T(8,128)(2,1)S(1)}, bf16[128,1024]{1,0:T(8,128)(2,1)S(1)}, u32[]{:S(2)}, u32[]{:S(2)}) collective-permute-start(bf16[128,1024]{1,0:T(8,128)(2,1)S(1)} %fusion.25), channel_id=1, source_target_pairs={{0,8},{1,9},{2,10},{3,11},{4,12},{5,13},{6,14},{7,15},{8,0},{9,1},... | collective-permute-start | bytes 786440 | tf_op jit(solution)/shard_map/ppermute | solution.py:67
  154.1 6.7 %collective-permute-start.26 = (bf16[2,64,1792]{2,1,0:T(8,128)(2,1)S(1)}, bf16[2,64,1792]{2,1,0:T(8,128)(2,1)S(1)}, u32[]{:S(2)}, u32[]{:S(2)}) collective-permute-start(bf16[2,64,1792]{2,1,0:T(8,128)(2,1)S(1)} %get-tuple-element.58), channel_id=1, source_target_pairs={{0,1},{1,0},{2,3},{3,2},{4,5},{5,4},{6,7},{7,6},{8,9},{9,8},{10,11... | collective-permute-start | bytes 1376264 | tf_op jit(solution)/shard_map/ppermute | solution.py:67
  160.0 43.2 %collective-permute-start.29 = (bf16[128,1792]{1,0:T(8,128)(2,1)S(1)}, bf16[128,1792]{1,0:T(8,128)(2,1)S(1)}, u32[]{:S(2)}, u32[]{:S(2)}) collective-permute-start(bf16[128,1792]{1,0:T(8,128)(2,1)S(1)} %get-tuple-element.53), channel_id=1, source_target_pairs={{0,14},{1,15},{2,8},{3,9},{4,10},{5,11},{6,12},{7,13},{8,6},{9,7},... | collective-permute-start | bytes 1376264 | tf_op jit(solution)/shard_map/ppermute | solution.py:67
  160.8 4.9 %collective-permute-start.23 = (bf16[2,64,1792]{2,1,0:T(8,128)(2,1)S(1)}, bf16[2,64,1792]{2,1,0:T(8,128)(2,1)S(1)}, u32[]{:S(2)}, u32[]{:S(2)}) collective-permute-start(bf16[2,64,1792]{2,1,0:T(8,128)(2,1)S(1)} %get-tuple-element.38), channel_id=1, source_target_pairs={{0,1},{1,0},{2,3},{3,2},{4,5},{5,4},{6,7},{7,6},{8,9},{9,8},{10,11... | collective-permute-start | bytes 1376264 | tf_op jit(solution)/shard_map/ppermute | solution.py:67
  160.8 42.1 %collective-permute-start.24 = (bf16[128,1792]{1,0:T(8,128)(2,1)S(1)}, bf16[128,1792]{1,0:T(8,128)(2,1)S(1)}, u32[]{:S(2)}, u32[]{:S(2)}) collective-permute-start(bf16[128,1792]{1,0:T(8,128)(2,1)S(1)} %get-tuple-element.54), channel_id=1, source_target_pairs={{0,6},{1,7},{2,0},{3,1},{4,2},{5,3},{6,4},{7,5},{8,14},{9,15},{10,... | collective-permute-start | bytes 1376264 | tf_op jit(solution)/shard_map/ppermute | solution.py:67
  161.3 41.8 %collective-permute-start.30 = (bf16[128,1792]{1,0:T(8,128)(2,1)S(1)}, bf16[128,1792]{1,0:T(8,128)(2,1)S(1)}, u32[]{:S(2)}, u32[]{:S(2)}) collective-permute-start(bf16[128,1792]{1,0:T(8,128)(2,1)S(1)} %get-tuple-element.51), channel_id=1, source_target_pairs={{0,10},{1,11},{2,12},{3,13},{4,14},{5,15},{6,8},{7,9},{8,2},{9,3},... | collective-permute-start | bytes 1376264 | tf_op jit(solution)/shard_map/ppermute | solution.py:67
  164.0 38.9 %collective-permute-start.27 = (bf16[128,1792]{1,0:T(8,128)(2,1)S(1)}, bf16[128,1792]{1,0:T(8,128)(2,1)S(1)}, u32[]{:S(2)}, u32[]{:S(2)}) collective-permute-start(bf16[128,1792]{1,0:T(8,128)(2,1)S(1)} %get-tuple-element.52), channel_id=1, source_target_pairs={{0,2},{1,3},{2,4},{3,5},{4,6},{5,7},{6,0},{7,1},{8,10},{9,11},{10,... | collective-permute-start | bytes 1376264 | tf_op jit(solution)/shard_map/ppermute | solution.py:67
  166.1 37.1 %collective-permute-start.28 = (bf16[128,1792]{1,0:T(8,128)(2,1)S(1)}, bf16[128,1792]{1,0:T(8,128)(2,1)S(1)}, u32[]{:S(2)}, u32[]{:S(2)}) collective-permute-start(bf16[128,1792]{1,0:T(8,128)(2,1)S(1)} %fusion.43), channel_id=1, source_target_pairs={{0,8},{1,9},{2,10},{3,11},{4,12},{5,13},{6,14},{7,15},{8,0},{9,1},... | collective-permute-start | bytes 1376264 | tf_op jit(solution)/shard_map/ppermute | solution.py:67
  203.5 0.9 copy-start.5

commit v9 on v8

--- a/solution.py
+++ b/solution.py
@@ -85,13 +85,16 @@
 
     first, second = payload(0), payload(2)
     gate_x = send(gate, flip=1)
+
+    seen = [{0: first, 1: send(first, 1)}, {0: send(second, flip=2)}]
+    seen[0][0], seen[1][0], down = together((seen[0][0], seen[1][0], down))
     down_y = send(down, flip=2)
-
-    pair = send(second, flip=2)
-    seen = [{0: own, 1: send(own, 1), 3: send(own, -1)} for own in (first, pair)]
+    seen[1][1] = send(seen[1][0], 1)
     for held in seen:
+        held[3] = send(held[0], -1)
         held[2] = send(held[1], 1)
-    seen[1][2], down_y = together((seen[1][2], down_y))
+    downs = jnp.concatenate([down, down_y], axis=1)
+    seen[1][2], downs = together((seen[1][2], downs))
 
     chosen = jnp.stack([e, e ^ 1]).astype(jnp.int32)
     earlier = jnp.triu(jnp.ones((tok, tok), BF), 1)
@@ -122,8 +125,8 @@
         return jnp.concatenate([of(0), other], axis=1)
 
     chosen0, chosen1 = choose(place0, helds[0]), choose(place1, helds[1])
-    downs = jnp.concatenate([down, down_y], axis=1)
-    chosen1, gate_x, downs = together((chosen1, gate_x, downs))
+
+    chosen1, gate_x = together((chosen1, gate_x))
     weights = jnp.concatenate([gate, gate_x])
 
     def product(rows):
@@ -136,54 +139,60 @@
     part = [send(sent[k], flip=2) for k in order]
     near = product(chosen0)
     near, info_x = together((near, info_x))
-    pay = jnp.stack([pay0, places(info_x)[1]])
-
-    hidden, away, out = {}, {}, {}
-
-    def finish(q, came):
-        gu = near[order[q]] + came.astype(F32)
+    pays = [pay0, places(info_x)[1]]
+
+    hidden, out, came = {}, {}, {}
+
+    def finish(q):
+        gu = near[order[q]] + part[q].astype(F32)
         own = (jax.nn.silu(gu[:, :ff]) * gu[:, ff:]).astype(BF)
-        hidden[q] = (own, send(own, flip=1))
-
-    def down_product(q):
-        own = hidden[q][0]
-        joined = jnp.concatenate([own, hidden[q][1]])
-        value = jnp.dot(joined, downs, preferred_element_type=F32).astype(BF)
-        value = value.reshape(2, 2, slots, half)
-        out[q], away[q] = value[:, 0], value[:, 1]
-
-    def weigh(q, came):
-        rows = jnp.concatenate([out[q], came], axis=1)
-        return jnp.einsum("gst,gsk->gtk", pay[:, order[q]], rows, preferred_element_type=F32)
+        hidden[q, 0], hidden[q, 1] = own, send(own, flip=1)
+
+    def down_product(q, g):
+        value = jnp.dot(hidden[q, g], downs, preferred_element_type=F32).astype(BF)
+        value = value.reshape(2, slots, half)
+        out[q, g], came[q, g] = value[0], send(value[1], core=1)
+
+    def weigh(q, g):
+        rows = jnp.concatenate([out[q, g], came[q, g]])
+        return lax.dot_general(
+            pays[g][order[q]], rows, (((0,), (0,)), ((), ())), preferred_element_type=F32
+        )
+
+    def before_weigh(q, value):
+        came[q, 1], value = together((came[q, 1], value))
+        return value
 
     def before_down(q, value):
-        own, value = together((hidden[q][0], value))
-        hidden[q] = (own, hidden[q][1])
+        hidden[q, 1], value = together((hidden[q, 1], value))
         return value
 
-    def cross(q):
-        return send(away[q], core=1)
-
-    finish(0, part[0])
-    down_product(0)
-    came, part[1] = together((cross(0), part[1]))
-    finish(1, part[1])
-    term = weigh(0, came).astype(BF)
-    middle = [send(term[g], 1) for g in range(2)]
-    middle[0], part[2] = before_down(1, (middle[0], part[2]))
-    down_product(1)
-    finish(2, part[2])
+    middle, back, forth = {}, {}, {}
+    finish(0)
+    down_product(0, 0)
+    middle[0] = send(weigh(0, 0).astype(BF), 1)
+    down_product(0, 1)
+    middle[0], part[1] = before_weigh(0, (middle[0], part[1]))
+    middle[1] = send(weigh(0, 1).astype(BF), 1)
+    finish(1)
+    down_product(1, 0)
+    back[0] = send(weigh(1, 0).astype(BF), -1)
+    part[2] = before_down(1, part[2])
+    down_product(1, 1)
+    middle[1] = before_weigh(1, middle[1])
+    back[1] = send(weigh(1, 1).astype(BF), -1, 1)
+    finish(2)
+    down_product(2, 0)
+    forth[0] = send((weigh(2, 0) + middle[0].astype(F32)).astype(BF), 1)
     part[3] = before_down(2, part[3])
-    down_product(2)
-    finish(3, part[3])
-    down_product(3)
-    away[3], came, middle[1] = together((away[3], cross(1), middle[1]))
-    term = weigh(1, came).astype(BF)
-    back = [send(term[0], -1), send(term[1], -1, 1)]
-    term = weigh(2, cross(2))
-    term = [(term[g] + middle[g].astype(F32)).astype(BF) for g in range(2)]
-    forth = [send(term[0], 1), send(term[1], 1, 1)]
-    term = weigh(3, cross(3))
+    down_product(2, 1)
+    back[0] = before_weigh(2, back[0])
+    forth[1] = send((weigh(2, 1) + middle[1].astype(F32)).astype(BF), 1, 1)
+    finish(3)
+    down_product(3, 0)
+    down_product(3, 1)
+    back[1] = before_weigh(3, back[1])
+    term = [weigh(3, g) for g in range(2)]
     theirs = send(term[1].astype(BF), flip=1)
     mine = (term[0] + back[0].astype(F32) + forth[0].astype(F32)).astype(BF)
     far = (theirs.astype(F32) + back[1].astype(F32) + forth[1].astype(F32)).astype(BF)

time: 206 us -> 199 us (0.966)
  waiting for transfers between devices: 117 us -> 132 us
  local copies, waits for them, and re-layouts: 11.6 us -> 5.56 us
  other arithmetic: 9.75 us -> 3.93 us
  matrix products: 27.2 us -> 21.8 us
  starting transfers between devices: 38.7 us -> 34.7 us
    ppermute x31 -> x35, waiting for transfers between devices: 117 us -> 132 us  [send(): lax.ppermute(value, ('dp', 'expert'), [(i * owners + j, (i ^ flip) * owne...]
    dot_general x4, matrix products: 6.01 us -> 1.78 us  [of(): jnp.einsum('zst,ztk->zsk', place[:, expert], held, preferred_element_type...]
    ppermute x31 -> x35, starting transfers between devices: 38.7 us -> 34.7 us  [send(): lax.ppermute(value, ('dp', 'expert'), [(i * owners + j, (i ^ flip) * owne...]
    concatenate x1, other arithmetic: 3.72 us -> 0.26 us  [paired(): downs = jnp.concatenate([down, down_y], axis=1)]
    another operation x7 -> x8, local copies, waits for them, and re-layouts: 3.35 us -> 1.27 us  [paired(): jnp.stack([seen[g][k][:tok] for k in range(chips)])]
    dot_general x8 -> x16, matrix products: 9.08 us -> 7.8 us  [the longest x8 5.23 us: down_product(): value = jnp.dot(hidden[q, g], downs, preferred_element_type=F32).astype(BF)]
  transfers between devices with their start and end apart: 31 -> 35, of which waited for: 14 -> 20; matrix products, arithmetic and copies ran while one was open for 21% -> 13% of each run, Pallas kernels for 0% -> 0%
where the time goes in v9:
time: 199 us; the launch traced here: 198 us
  waiting for transfers between devices  132 us (66%)
  starting transfers between devices  34.7 us (17%)
  matrix products  21.8 us (11%)
  local copies, waits for them, and re-layouts  5.56 us (3%)
  other arithmetic  3.93 us (2%)
    ppermute x35, waiting for transfers between devices, send(): lax.ppermute(value, ('dp', 'expert'), [(i * owners + j, (i ^ flip) * owne...  132 us
    ppermute x35, starting transfers between devices, send(): lax.ppermute(value, ('dp', 'expert'), [(i * owners + j, (i ^ flip) * owne...  34.7 us
    dot_general x2, matrix products, product(): jnp.dot(flat, weights, preferred_element_type=F32)  11.8 us
    dot_general x8, matrix products, down_product(): value = jnp.dot(hidden[q, g], downs, preferred_element_type=F32).astype(BF)  5.23 us
  transfers between devices with their start and end apart: 35, of which 20 were waited for; matrix products, arithmetic and copies ran while one was open for 13% of the time, Pallas kernels for 0%

profile of v9, /device:TPU:0, one launch (start us, length us, event | category | flops | bytes accessed | tf_op | source)
XLA Modules:
  0.0 198.4 jit_solution(12411018562702346591)
XLA Ops:
  0.0 0.8 convert_bitcast_fusion
  0.8 0.7 fusion.47
  1.5 1.4 constant_dynamic-slice_fusion.1
  3.0 3.0 %collective-permute-start = (bf16[136,1792]{1,0:T(8,128)(2,1)S(1)}, bf16[136,1792]{1,0:T(8,128)(2,1)S(1)}, u32[]{:S(2)}, u32[]{:S(2)}) collective-permute-start(bf16[136,1792]{1,0:T(8,128)(2,1)S(1)} %get-tuple-element.89), channel_id=1, source_target_pairs={{0,16},{1,17},{2,18},{3,19},{4,20},{5,21},{6,22},{7,23},{8,24},{9,... | collective-permute-start | bytes 1462280 | tf_op jit(solution)/shard_map/ppermute | solution.py:67
  6.0 1.6 collective-permute-start.1
  7.6 1.5 collective-permute-start.9
  9.1 8.0 %collective-permute-done = bf16[136,1792]{1,0:T(8,128)(2,1)S(1)} collective-permute-done((bf16[136,1792]{1,0:T(8,128)(2,1)S(1)}, bf16[136,1792]{1,0:T(8,128)(2,1)S(1)}, u32[]{:S(2)}, u32[]{:S(2)}) %collective-permute-start) | collective-permute-done | bytes 487456 | tf_op jit(solution)/shard_map/ppermute | solution.py:67
  17.1 3.8 %collective-permute-start.3 = (bf16[136,1792]{1,0:T(8,128)(2,1)S(1)}, bf16[136,1792]{1,0:T(8,128)(2,1)S(1)}, u32[]{:S(2)}, u32[]{:S(2)}) collective-permute-start(bf16[136,1792]{1,0:T(8,128)(2,1)S(1)} %get-tuple-element.29), channel_id=1, source_target_pairs={{0,6},{1,7},{2,0},{3,1},{4,2},{5,3},{6,4},{7,5},{8,14},{9,15},{10,... | collective-permute-start | bytes 1462280 | tf_op jit(solution)/shard_map/ppermute | solution.py:67
  20.9 3.8 %collective-permute-start.7 = (bf16[136,1792]{1,0:T(8,128)(2,1)S(1)}, bf16[136,1792]{1,0:T(8,128)(2,1)S(1)}, u32[]{:S(2)}, u32[]{:S(2)}) collective-permute-start(bf16[136,1792]{1,0:T(8,128)(2,1)S(1)} %collective-permute-done), channel_id=1, source_target_pairs={{0,6},{1,7},{2,0},{3,1},{4,2},{5,3},{6,4},{7,5},{8,14},{9,15},{10,... | collective-permute-start | bytes 1462280 | tf_op jit(solution)/shard_map/ppermute | solution.py:67
  24.8 1.0 slice_bitcast_fusion.6
  26.0 0.7 slice_bitcast_fusion.24
  26.7 6.1 %collective-permute-done.3 = bf16[136,1792]{1,0:T(8,128)(2,1)S(1)} collective-permute-done((bf16[136,1792]{1,0:T(8,128)(2,1)S(1)}, bf16[136,1792]{1,0:T(8,128)(2,1)S(1)}, u32[]{:S(2)}, u32[]{:S(2)}) %collective-permute-start.3) | collective-permute-done | bytes 487456 | tf_op jit(solution)/shard_map/ppermute | solution.py:67
  32.7 2.1 %collective-permute-start.6 = (bf16[1024,896]{1,0:T(8,128)(2,1)S(1)}, bf16[1024,896]{1,0:T(8,128)(2,1)S(1)}, u32[]{:S(2)}, u32[]{:S(2)}) collective-permute-start(bf16[1024,896]{1,0:T(8,128)(2,1)S(1)} %bitcast.112), channel_id=1, source_target_pairs={{0,16},{1,17},{2,18},{3,19},{4,20},{5,21},{6,22},{7,23},{8,24},{9,... | collective-permute-start | bytes 5505032 | tf_op jit(solution)/shard_map/ppermute | solution.py:67
  34.8 28.0 %collective-permute-done.2 = bf16[136,1792]{1,0:T(8,128)(2,1)S(1)} collective-permute-done((bf16[136,1792]{1,0:T(8,128)(2,1)}, bf16[136,1792]{1,0:T(8,128)(2,1)S(1)}, u32[]{:S(2)}, u32[]{:S(2)}) %collective-permute-start.2) | collective-permute-done | bytes 487456 | tf_op jit(solution)/shard_map/ppermute | solution.py:67
  62.9 1.7 collective-permute-start.5
  64.7 9.2 %collective-permute-done.6 = bf16[1024,896]{1,0:T(8,128)(2,1)S(1)} collective-permute-done((bf16[1024,896]{1,0:T(8,128)(2,1)S(1)}, bf16[1024,896]{1,0:T(8,128)(2,1)S(1)}, u32[]{:S(2)}, u32[]{:S(2)}) %collective-permute-start.6) | collective-permute-done | bytes 1835040 | tf_op jit(solution)/shard_map/ppermute | solution.py:67
  74.2 1.8 collective-permute-done.5
  76.2 0.4 convolution_convert_fusion
  77.0 0.4 convolution_convert_fusion.2
  77.4 0.6 collective-permute-start.8
  78.0 1.5 collective-permute-start.11
  79.5 0.4 convolution_convert_fusion.1
  79.9 0.4 convolution_convert_fusion.3
  80.7 7.9 %collective-permute-done.9 = bf16[896,2048]{1,0:T(8,128)(2,1)} collective-permute-done((bf16[896,2048]{1,0:T(8,128)(2,1)}, bf16[896,2048]{1,0:T(8,128)(2,1)}, u32[]{:S(2)}, u32[]{:S(2)}) %collective-permute-start.9) | collective-permute-done | bytes 3670048 | tf_op jit(solution)/shard_map/ppermute | solution.py:67
  88.6 6.1 %fusion.2 = bf16[4,128,2048]{2,1,0:T(8,128)(2,1)S(1)} fusion(bf16[4,128,1792]{2,1,0:T(8,128)(2,1)S(1)} %pad_maximum_fusion.2, bf16[896,2048]{1,0:T(8,128)(2,1)} %collective-permute-done.9, bf16[896,2048]{1,0:T(8,128)(2,1)S(1)} %bitcast.124), kind=kOutput, calls=%fused_computation.4 | convolution fusion | flops 3773825024 | bytes 11272192 | tf_op jit(solution)/shard_map/dot_general | solution.py:134
  94.6 5.8 %fusion = f32[4,128,2048]{2,1,0:T(8,128)S(1)} fusion(bf16[4,128,1792]{2,1,0:T(8,128)(2,1)S(1)} %pad_maximum_fusion.4, bf16[896,2048]{1,0:T(8,128)(2,1)} %collective-permute-done.9, bf16[896,2048]{1,0:T(8,128)(2,1)S(1)} %bitcast.125), kind=kOutput, calls=%fused_computation.1 | convolution fusion | flops 3772776448 | bytes 13369344 | tf_op jit(solution)/shard_map/dot_general | solution.py:134
  100.6 0.6 collective-permute-start.12
  101.3 11.3 %collective-permute-done.12 = bf16[128,2048]{1,0:T(8,128)(2,1)S(1)} collective-permute-done((bf16[128,2048]{1,0:T(8,128)(2,1)S(1)}, bf16[128,2048]{1,0:T(8,128)(2,1)S(1)}, u32[]{:S(2)}, u32[]{:S(2)}) %collective-permute-start.12) | collective-permute-done | bytes 524320 | tf_op jit(solution)/shard_map/ppermute | solution.py:67
  112.9 0.7 convolution_convert_fusion.10
  113.8 1.6 collective-permute-start.13
  115.5 0.5 collective-permute-start.17
  116.0 1.5 collective-permute-start.19
  117.5 0.5 collective-permute-start.21
  118.4 1.8 collective-permute-start.16
  120.2 2.4 %collective-permute-done.13 = bf16[128,1024]{1,0:T(8,128)(2,1)S(1)} collective-permute-done((bf16[128,1024]{1,0:T(8,128)(2,1)S(1)}, bf16[128,1024]{1,0:T(8,128)(2,1)S(1)}, u32[]{:S(2)}, u32[]{:S(2)}) %collective-permute-start.13) | collective-permute-done | bytes 262176 | tf_op jit(solution)/shard_map/ppermute | solution.py:67
  122.6 0.7 convolution_convert_fusion.11
  123.4 6.8 %collective-permute-done.17 = bf16[128,2048]{1,0:T(8,128)(2,1)S(1)} collective-permute-done((bf16[128,2048]{1,0:T(8,128)(2,1)S(1)}, bf16[128,2048]{1,0:T(8,128)(2,1)S(1)}, u32[]{:S(2)}, u32[]{:S(2)}) %collective-permute-start.17) | collective-permute-done | bytes 524320 | tf_op jit(solution)/shard_map/ppermute | solution.py:67
  130.3 1.9 collective-permute-done.16
  132.5 0.6 collective-permute-start.18
  133.1 0.7 convolution_convert_fusion.7
  134.2 1.1 collective-permute-done.24
  135.7 2.8 %collective-permute-start.25 = (bf16[128,1792]{1,0:T(8,128)(2,1)S(1)}, bf16[128,1792]{1,0:T(8,128)(2,1)S(1)}, u32[]{:S(2)}, u32[]{:S(2)}) collective-permute-start(bf16[128,1792]{1,0:T(8,128)(2,1)S(1)} %convolution_convert_fusion.15), channel_id=1, source_target_pairs={{0,6},{1,7},{2,0},{3,1},{4,2},{5,3},{6,4},{7,5},{8,14},{9,15},{10,... | collective-permute-start | bytes 1376264 | tf_op jit(solution)/shard_map/ppermute | solution.py:67
  138.4 3.0 %collective-permute-done.19 = bf16[128,2048]{1,0:T(8,128)(2,1)S(1)} collective-permute-done((bf16[128,2048]{1,0:T(8,128)(2,1)S(1)}, bf16[128,2048]{1,0:T(8,128)(2,1)S(1)}, u32[]{:S(2)}, u32[]{:S(2)}) %collective-permute-start.19) | collective-permute-done | bytes 524320 | tf_op jit(solution)/shard_map/ppermute | solution.py:67
  141.8 0.6 collective-permute-start.20
  142.4 0.7 convolution_convert_fusion.6
  143.0 0.7 convolution_convert_fusion.4
  143.9 5.5 %collective-permute-done.31 = bf16[128,1792]{1,0:T(8,128)(2,1)S(1)} collective-permute-done((bf16[128,1792]{1,0:T(8,128)(2,1)S(1)}, bf16[128,1792]{1,0:T(8,128)(2,1)S(1)}, u32[]{:S(2)}, u32[]{:S(2)}) %collective-permute-start.31) | collective-permute-done | bytes 458784 | tf_op jit(solution)/shard_map/ppermute | solution.py:67
  149.7 0.5 collective-permute-start.32
  150.3 0.6 collective-permute-done.26
  151.2 1.9 collective-permute-start.27
  153.4 0.6 collective-permute-start.28
  154.0 0.7 convolution_convert_fusion.9
  154.7 0.7 convolution_convert_fusion.8
  155.5 3.4 %collective-permute-done.25 = bf16[128,1792]{1,0:T(8,128)(2,1)S(1)} collective-permute-done((bf16[128,1792]{1,0:T(8,128)(2,1)S(1)}, bf16[128,1792]{1,0:T(8,128)(2,1)S(1)}, u32[]{:S(2)}, u32[]{:S(2)}) %collective-permute-start.25) | collective-permute-done | bytes 458784 | tf_op jit(solution)/shard_map/ppermute | solution.py:67
  158.9 12.6 %collective-permute-done.28 = bf16[128,1024]{1,0:T(8,128)(2,1)S(1)} collective-permute-done((bf16[128,1024]{1,0:T(8,128)(2,1)S(1)}, bf16[128,1024]{1,0:T(8,128)(2,1)S(1)}, u32[]{:S(2)}, u32[]{:S(2)}) %collective-permute-start.28) | collective-permute-done | bytes 262176 | tf_op jit(solution)/shard_map/ppermute | solution.py:67
  171.5 0.7 convolution_convert_fusion.5
  172.9 0.8 collective-permute-done.29
  174.1 0.7 collective-permute-start.33
  174.8 4.1 %collective-permute-done.27 = bf16[128,1792]{1,0:T(8,128)(2,1)S(1)} collective-permute-done((bf16[128,1792]{1,0:T(8,128)(2,1)S(1)}, bf16[128,1792]{1,0:T(8,128)(2,1)S(1)}, u32[]{:S(2)}, u32[]{:S(2)}) %collective-permute-start.27) | collective-permute-done | bytes 458784 | tf_op jit(solution)/shard_map/ppermute | solution.py:67
  178.9 0.3 fusion.4
  179.4 10.0 %collective-permute-done.34 = bf16[128,1792]{1,0:T(8,128)(2,1)S(1)} collective-permute-done((bf16[128,1792]{1,0:T(8,128)(2,1)S(1)}, bf16[128,1792]{1,0:T(8,128)(2,1)S(1)}, u32[]{:S(2)}, u32[]{:S(2)}) %collective-permute-start.34) | collective-permute-done | bytes 458784 | tf_op jit(solution)/shard_map/ppermute | solution.py:67
  189.4 7.1 %collective-permute-done.33 = bf16[128,1792]{1,0:T(8,128)(2,1)S(1)} collective-permute-done((bf16[128,1792]{1,0:T(8,128)(2,1)S(1)}, bf16[128,1792]{1,0:T(8,128)(2,1)S(1)}, u32[]{:S(2)}, u32[]{:S(2)}) %collective-permute-start.33) | collective-permute-done | bytes 458784 | tf_op jit(solution)/shard_map/ppermute | solution.py:67
  196.8 0.9 copy-done.1
  197.7 0.7 slice_dynamic-update-slice_fusion
  (99 shorter events, 6.9 us)
Async XLA Ops:
  0.0 32.7 %copy-start = (bf16[1,1024,896]{2,1,0:T(8,128)(2,1)S(1)}, bf16[1,1024,896]{2,1,0:T(8,128)(2,1)}, u32[]{:S(2)}) copy-start(bf16[1,1024,896]{2,1,0:T(8,128)(2,1)} %param.7) | copy-start | bytes 5505028
  3.0 14.2 %collective-permute-start = (bf16[136,1792]{1,0:T(8,128)(2,1)S(1)}, bf16[136,1792]{1,0:T(8,128)(2,1)S(1)}, u32[]{:S(2)}, u32[]{:S(2)}) collective-permute-start(bf16[136,1792]{1,0:T(8,128)(2,1)S(1)} %get-tuple-element.89), channel_id=1, source_target_pairs={{0,16},{1,17},{2,18},{3,19},{4,20},{5,21},{6,22},{7,23},{8,24},{9,... | collective-permute-start | bytes 1462280 | tf_op jit(solution)/shard_map/ppermute | solution.py:67
  6.0 18.8 %collective-permute-start.1 = (bf16[136,1792]{1,0:T(8,128)(2,1)S(1)}, bf16[136,1792]{1,0:T(8,128)(2,1)}, u32[]{:S(2)}, u32[]{:S(2)}) collective-permute-start(bf16[136,1792]{1,0:T(8,128)(2,1)S(1)} %get-tuple-element.29), channel_id=1, source_target_pairs={{0,2},{1,3},{2,4},{3,5},{4,6},{5,7},{6,0},{7,1},{8,10},{9,11},{10,... | collective-permute-start | bytes 1462280 | tf_op jit(solution)/shard_map/ppermute | solution.py:67
  7.6 81.0 %collective-permute-start.9 = (bf16[896,2048]{1,0:T(8,128)(2,1)}, bf16[896,2048]{1,0:T(8,128)(2,1)}, u32[]{:S(2)}, u32[]{:S(2)}) collective-permute-start(bf16[896,2048]{1,0:T(8,128)(2,1)} %bitcast.123), channel_id=1, source_target_pairs={{0,8},{1,9},{2,10},{3,11},{4,12},{5,13},{6,14},{7,15},{8,0},{9,1},... | collective-permute-start | bytes 11010056 | tf_op jit(solution)/shard_map/ppermute | solution.py:67
  17.1 15.6 %collective-permute-start.3 = (bf16[136,1792]{1,0:T(8,128)(2,1)S(1)}, bf16[136,1792]{1,0:T(8,128)(2,1)S(1)}, u32[]{:S(2)}, u32[]{:S(2)}) collective-permute-start(bf16[136,1792]{1,0:T(8,128)(2,1)S(1)} %get-tuple-element.29), channel_id=1, source_target_pairs={{0,6},{1,7},{2,0},{3,1},{4,2},{5,3},{6,4},{7,5},{8,14},{9,15},{10,... | collective-permute-start | bytes 1462280 | tf_op jit(solution)/shard_map/ppermute | solution.py:67
  20.9 41.9 %collective-permute-start.4 = (bf16[136,1792]{1,0:T(8,128)(2,1)S(1)}, bf16[136,1792]{1,0:T(8,128)(2,1)S(1)}, u32[]{:S(2)}, u32[]{:S(2)}) collective-permute-start(bf16[136,1792]{1,0:T(8,128)(2,1)S(1)} %collective-permute-done), channel_id=1, source_target_pairs={{0,2},{1,3},{2,4},{3,5},{4,6},{5,7},{6,0},{7,1},{8,10},{9,11},{10,... | collective-permute-start | bytes 1462280 | tf_op jit(solution)/shard_map/ppermute | solution.py:67
  20.9 43.7 %collective-permute-start.7 = (bf16[136,1792]{1,0:T(8,128)(2,1)S(1)}, bf16[136,1792]{1,0:T(8,128)(2,1)S(1)}, u32[]{:S(2)}, u32[]{:S(2)}) collective-permute-start(bf16[136,1792]{1,0:T(8,128)(2,1)S(1)} %collective-permute-done), channel_id=1, source_target_pairs={{0,6},{1,7},{2,0},{3,1},{4,2},{5,3},{6,4},{7,5},{8,14},{9,15},{10,... | collective-permute-start | bytes 1462280 | tf_op jit(solution)/shard_map/ppermute | solution.py:67
  25.9 36.9 %collective-permute-start.2 = (bf16[136,1792]{1,0:T(8,128)(2,1)}, bf16[136,1792]{1,0:T(8,128)(2,1)S(1)}, u32[]{:S(2)}, u32[]{:S(2)}) collective-permute-start(bf16[136,1792]{1,0:T(8,128)(2,1)} %collective-permute-done.1), channel_id=1, source_target_pairs={{0,2},{1,3},{2,4},{3,5},{4,6},{5,7},{6,0},{7,1},{8,10},{9,11},{10,... | collective-permute-start | bytes 1462280 | tf_op jit(solution)/shard_map/ppermute | solution.py:67
  32.7 41.2 %collective-permute-start.6 = (bf16[1024,896]{1,0:T(8,128)(2,1)S(1)}, bf16[1024,896]{1,0:T(8,128)(2,1)S(1)}, u32[]{:S(2)}, u32[]{:S(2)}) collective-permute-start(bf16[1024,896]{1,0:T(8,128)(2,1)S(1)} %bitcast.112), channel_id=1, source_target_pairs={{0,16},{1,17},{2,18},{3,19},{4,20},{5,21},{6,22},{7,23},{8,24},{9,... | collective-permute-start | bytes 5505032 | tf_op jit(solution)/shard_map/ppermute | solution.py:67
  62.9 13.0 %collective-permute-start.5 = (bf16[136,1792]{1,0:T(8,128)(2,1)S(1)}, bf16[136,1792]{1,0:T(8,128)(2,1)S(1)}, u32[]{:S(2)}, u32[]{:S(2)}) collective-permute-start(bf16[136,1792]{1,0:T(8,128)(2,1)S(1)} %collective-permute-done.4), channel_id=1, source_target_pairs={{0,2},{1,3},{2,4},{3,5},{4,6},{5,7},{6,0},{7,1},{8,10},{9,11},{10,... | collective-permute-start | bytes 1462280 | tf_op jit(solution)/shard_map/ppermute | solution.py:67
  76.7 3.7 %collective-permute-start.10 = (bf16[4,64,1792]{2,1,0:T(8,128)(2,1)S(1)}, bf16[4,64,1792]{2,1,0:T(8,128)(2,1)S(1)}, u32[]{:S(2)}, u32[]{:S(2)}) collective-permute-start(bf16[4,64,1792]{2,1,0:T(8,128)(2,1)S(1)} %convolution_convert_fusion), channel_id=1, source_target_pairs={{0,1},{1,0},{2,3},{3,2},{4,5},{5,4},{6,7},{7,6},{8,9},{9,8},{10,11... | collective-permute-start | bytes 2752520 | tf_op jit(solution)/shard_map/ppermute | solution.py:67
  77.4 3.1 %collective-permute-start.8 = (bf16[4,64,1792]{2,1,0:T(8,128)(2,1)S(1)}, bf16[4,64,1792]{2,1,0:T(8,128)(2,1)S(1)}, u32[]{:S(2)}, u32[]{:S(2)}) collective-permute-start(bf16[4,64,1792]{2,1,0:T(8,128)(2,1)S(1)} %convolution_convert_fusion.2), channel_id=1, source_target_pairs={{0,1},{1,0},{2,3},{3,2},{4,5},{5,4},{6,7},{7,6},{8,9},{9,8},{10,11... | collective-permute-start | bytes 2752520 | tf_op jit(solution)/shard_map/ppermute | solution.py:67
  78.0 22.4 %collective-permute-start.11 = (bf16[4,8,256]{2,1,0:T(8,128)(2,1)S(1)}, bf16[4,8,256]{2,1,0:T(8,128)(2,1)S(1)}, u32[]{:S(2)}, u32[]{:S(2)}) collective-permute-start(bf16[4,8,256]{2,1,0:T(8,128)(2,1)S(1)} %pad_maximum_fusion.11), channel_id=1, source_target_pairs={{0,8},{1,9},{2,10},{3,11},{4,12},{5,13},{6,14},{7,15},{8,0},{9,1},... | collective-permute-start | bytes 49160 | tf_op jit(solution)/shard_map/ppermute | solution.py:67
  80.4 8.2 %copy-start.2 = (bf16[1,896,2048]{2,1,0:T(8,128)(2,1)S(1)}, bf16[1,896,2048]{2,1,0:T(8,128)(2,1)}, u32[]{:S(2)}) copy-start(bf16[1,896,2048]{2,1,0:T(8,128)(2,1)} %param.6) | copy-start | bytes 11010052
  100.6 12.1 %collective-permute-start.12 = (bf16[128,2048]{1,0:T(8,128)(2,1)S(1)}, bf16[128,2048]{1,0:T(8,128)(2,1)S(1)}, u32[]{:S(2)}, u32[]{:S(2)}) collective-permute-start(bf16[128,2048]{1,0:T(8,128)(2,1)S(1)} %get-tuple-element.60), channel_id=1, source_target_pairs={{0,16},{1,17},{2,18},{3,19},{4,20},{5,21},{6,22},{7,23},{8,24},{9,... | collective-permute-start | bytes 1572872 | tf_op jit(solution)/shard_map/ppermute | solution.py:67
  113.6 4.4 %collective-permute-start.15 = (bf16[64,1792]{1,0:T(8,128)(2,1)S(1)}, bf16[64,1792]{1,0:T(8,128)(2,1)S(1)}, u32[]{:S(2)}, u32[]{:S(2)}) collective-permute-start(bf16[64,1792]{1,0:T(8,128)(2,1)S(1)} %get-tuple-element.80), channel_id=1, source_target_pairs={{0,1},{1,0},{2,3},{3,2},{4,5},{5,4},{6,7},{7,6},{8,9},{9,8},{10,11... | collective-permute-start | bytes 688136 | tf_op jit(solution)/shard_map/ppermute | solution.py:67
  113.8 8.8 %collective-permute-start.13 = (bf16[128,1024]{1,0:T(8,128)(2,1)S(1)}, bf16[128,1024]{1,0:T(8,128)(2,1)S(1)}, u32[]{:S(2)}, u32[]{:S(2)}) collective-permute-start(bf16[128,1024]{1,0:T(8,128)(2,1)S(1)} %fusion.9), channel_id=1, source_target_pairs={{0,8},{1,9},{2,10},{3,11},{4,12},{5,13},{6,14},{7,15},{8,0},{9,1},... | collective-permute-start | bytes 786440 | tf_op jit(solution)/shard_map/ppermute | solution.py:67
  115.5 14.8 %collective-permute-start.17 = (bf16[128,2048]{1,0:T(8,128)(2,1)S(1)}, bf16[128,2048]{1,0:T(8,128)(2,1)S(1)}, u32[]{:S(2)}, u32[]{:S(2)}) collective-permute-start(bf16[128,2048]{1,0:T(8,128)(2,1)S(1)} %get-tuple-element.59), channel_id=1, source_target_pairs={{0,16},{1,17},{2,18},{3,19},{4,20},{5,21},{6,22},{7,23},{8,24},{9,... | collective-permute-start | bytes 1572872 | tf_op jit(solution)/shard_map/ppermute | solution.py:67
  116.0 25.5 %collective-permute-start.19 = (bf16[128,2048]{1,0:T(8,128)(2,1)S(1)}, bf16[128,2048]{1,0:T(8,128)(2,1)S(1)}, u32[]{:S(2)}, u32[]{:S(2)}) collective-permute-start(bf16[128,2048]{1,0:T(8,128)(2,1)S(1)} %get-tuple-element.58), channel_id=1, source_target_pairs={{0,16},{1,17},{2,18},{3,19},{4,20},{5,21},{6,22},{7,23},{8,24},{9,... | collective-permute-start | bytes 1572872 | tf_op jit(solution)/shard_map/ppermute | solution.py:67
  117.5 35.6 %collective-permute-start.21 = (bf16[128,2048]{1,0:T(8,128)(2,1)S(1)}, bf16[128,2048]{1,0:T(8,128)(2,1)S(1)}, u32[]{:S(2)}, u32[]{:S(2)}) collective-permute-start(bf16[128,2048]{1,0:T(8,128)(2,1)S(1)} %get-tuple-element.57), channel_id=1, source_target_pairs={{0,16},{1,17},{2,18},{3,19},{4,20},{5,21},{6,22},{7,23},{8,24},{9,... | collective-permute-start | bytes 1572872 | tf_op jit(solution)/shard_map/ppermute | solution.py:67
  118.4 13.8 %collective-permute-start.16 = (bf16[128,1792]{1,0:T(8,128)(2,1)S(1)}, bf16[128,1792]{1,0:T(8,128)(2,1)S(1)}, u32[]{:S(2)}, u32[]{:S(2)}) collective-permute-start(bf16[128,1792]{1,0:T(8,128)(2,1)S(1)} %convolution_convert_fusion.16), channel_id=1, source_target_pairs={{0,2},{1,3},{2,4},{3,5},{4,6},{5,7},{6,0},{7,1},{8,10},{9,11},{10,... | collective-permute-start | bytes 1376264 | tf_op jit(solution)/shard_map/ppermute | solution.py:67
  123.3 7.0 %collective-permute-start.14 = (bf16[64,1792]{1,0:T(8,128)(2,1)S(1)}, bf16[64,1792]{1,0:T(8,128)(2,1)S(1)}, u32[]{:S(2)}, u32[]{:S(2)}) collective-permute-start(bf16[64,1792]{1,0:T(8,128)(2,1)S(1)} %get-tuple-element.72), channel_id=1, source_target_pairs={{0,1},{1,0},{2,3},{3,2},{4,5},{5,4},{6,7},{7,6},{8,9},{9,8},{10,11... | collective-permute-start | bytes 688136 | tf_op jit(solution)/shard_map/ppermute | solution.py:67
  132.5 9.0 %collective-permute-start.18 = (bf16[128,1024]{1,0:T(8,128)(2,1)S(1)}, bf16[128,1024]{1,0:T(8,128)(2,1)S(1)}, u32[]{:S(2)}, u32[]{:S(2)}) collective-permute-start(bf16[128,1024]{1,0:T(8,128)(2,1)S(1)} %fusion.8), channel_id=1, source_target_pairs={{0,8},{1,9},{2,10},{3,11},{4,12},{5,13},{6,14},{7,15},{8,0},{9,1},... | collective-permute-start | bytes 786440 | tf_op jit(solution)/shard_map/ppermute | solution.py:67
  133.8 1.6 collective-permute-start.24
  134.2 15.2 %collective-permute-start.31 = (bf16[128,1792]{1,0:T(8,128)(2,1)S(1)}, bf16[128,1792]{1,0:T(8,128)(2,1)S(1)}, u32[]{:S(2)}, u32[]{:S(2)}) collective-permute-start(bf16[128,1792]{1,0:T(8,128)(2,1)S(1)} %convolution_convert_fusion.14), channel_id=1, source_target_pairs={{0,2},{1,3},{2,4},{3,5},{4,6},{5,7},{6,0},{7,1},{8,10},{9,11},{10,... | collective-permute-start | bytes 1376264 | tf_op jit(solution)/shard_map/ppermute | solution.py:67
  135.7 23.2 %collective-permute-start.25 = (bf16[128,1792]{1,0:T(8,128)(2,1)S(1)}, bf16[128,1792]{1,0:T(8,128)(2,1)S(1)}, u32[]{:S(2)}, u32[]{:S(2)}) collective-permute-start(bf16[128,1792]{1,0:T(8,128)(2,1)S(1)} %convolution_convert_fusion.15), channel_id=1, source_target_pairs={{0,6},{1,7},{2,0},{3,1},{4,2},{5,3},{6,4},{7,5},{8,14},{9,15},{10,... | collective-permute-start | bytes 1376264 | tf_op jit(solution)/shard_map/ppermute | solution.py:67
  141.8 11.3 %collective-permute-start.20 = (bf16[128,1024]{1,0:T(8,128)(2,1)S(1)}, bf16[128,1024]{1,0:T(8,128)(2,1)S(1)}, u32[]{:S(2)}, u32[]{:S(2)}) collective-permute-start(bf16[128,1024]{1,0:T(8,128)(2,1)S(1)} %fusion.7), channel_id=1, source_target_pairs={{0,8},{1,9},{2,10},{3,11},{4,12},{5,13},{6,14},{7,15},{8,0},{9,1},... | collective-permute-start | bytes 786440 | tf_op jit(solution)/shard_map/ppermute | solution.py:67
  143.7 5.7 %collective-permute-start.30 = (bf16[64,1792]{1,0:T(8,128)(2,1)S(1)}, bf16[64,1792]{1,0:T(8,128)(2,1)S(1)}, u32[]{:S(2)}, u32[]{:S(2)}) collective-permute-start(bf16[64,1792]{1,0:T(8,128)(2,1)S(1)} %get-tuple-element.68), channel_id=1, source_target_pairs={{0,1},{1,0},{2,3},{3,2},{4,5},{5,4},{6,7},{7,6},{8,9},{9,8},{10,11... | collective-permute-start | bytes 688136 | tf_op jit(solution)/shard_map/ppermute | solution.py:67
  149.4 1.5 collective-permute-start.26
  149.7 23.2 %collective-permute-start.32 = (bf16[128,1792]{1,0:T(8,128)(2,1)S(1)}, bf16[128,1792]{1,0:T(8,128)(2,1)S(1)}, u32[]{:S(2)}, u32[]{:S(2)}) collective-permute-start(bf16[128,1792]{1,0:T(8,128)(2,1)S(1)} %convolution_convert_fusion.13), channel_id=1, source_target_pairs={{0,14},{1,15},{2,8},{3,9},{4,10},{5,11},{6,12},{7,13},{8,6},{9,7},... | collective-permute-start | bytes 1376264 | tf_op jit(solution)/shard_map/ppermute | solution.py:67
  151.2 27.7 %collective-permute-start.27 = (bf16[128,1792]{1,0:T(8,128)(2,1)S(1)}, bf16[128,1792]{1,0:T(8,128)(2,1)S(1)}, u32[]{:S(2)}, u32[]{:S(2)}) collective-permute-start(bf16[128,1792]{1,0:T(8,128)(2,1)S(1)} %fusion.5), channel_id=1, source_target_pairs={{0,2},{1,3},{2,4},{3,5},{4,6},{5,7},{6,0},{7,1},{8,10},{9,11},{10,... | collective-permute-start | bytes 1376264 | tf_op jit(solution)/shard_map/ppermute | solution.py:67
  153.4 18.1 %collective-permute-start.28 = (bf16[128,1024]{1,0:T(8,128)(2,1)S(1)}, bf16[128,1024]{1,0:T(8,128)(2,1)S(1)}, u32[]{:S(2)}, u32[]{:S(2)}) collective-permute-start(bf16[128,1024]{1,0:T(8,128)(2,1)S(1)} %fusion.6), channel_id=1, source_target_pairs={{0,8},{1,9},{2,10},{3,11},{4,12},{5,13},{6,14},{7,15},{8,0},{9,1},... | collective-permute-start | bytes 786440 | tf_op jit(solution)/shard_map/ppermute | solution.py:67
  155.4 3.5 %collective-permute-start.23 = (bf16[64,1792]{1,0:T(8,128)(2,1)S(1)}, bf16[64,1792]{1,0:T(8,128)(2,1)S(1)}, u32[]{:S(2)}, u32[]{:S(2)}) collective-permute-start(bf16[64,1792]{1,0:T(8,128)(2,1)S(1)} %get-tuple-element.70), channel_id=1, source_target_pairs={{0,1},{1,0},{2,3},{3,2},{4,5},{5,4},{6,7},{7,6},{8,9},{9,8},{10,11... | collective-permute-start | bytes 688136 | tf_op jit(solution)/shard_map/ppermute | solution.py:67
  158.9 16.0 %collective-permute-start.22 = (bf16[64,1792]{1,0:T(8,128)(2,1)S(1)}, bf16[64,1792]{1,0:T(8,128)(2,1)S(1)}, u32[]{:S(2)}, u32[]{:S(2)}) collective-permute-start(bf16[64,1792]{1,0:T(8,128)(2,1)S(1)} %get-tuple-element.74), channel_id=1, source_target_pairs={{0,1},{1,0},{2,3},{3,2},{4,5},{5,4},{6,7},{7,6},{8,9},{9,8},{10,11... | collective-permute-start | bytes 688136 | tf_op jit(solution)/shard_map/ppermute | solution.py:67
  172.2 1.6 collective-permute-start.29
  172.6 16.8 %collective-permute-start.34 = (bf16[128,1792]{1,0:T(8,128)(2,1)S(1)}, bf16[128,1792]{1,0:T(8,128)(2,1)S(1)}, u32[]{:S(2)}, u32[]{:S(2)}) collective-permute-start(bf16[128,1792]{1,0:T(8,128)(2,1)S(1)} %add_convert_fusion.1), channel_id=1, source_target_pairs={{0,10},{1,11},{2,12},{3,13},{4,14},{5,15},{6,8},{7,9},{8,2},{9,3},... | collective-permute-start | bytes 1376264 | tf_op jit(solution)/shard_map/ppermute | solution.py:67
  174.1 22.5 %collective-permute-start.33 = (bf16[128,1792]{1,0:T(8,128)(2,1)S(1)}, bf16[128,1792]{1,0:T(8,128)(2,1)S(1)}, u32[]{:S(2)}, u32[]{:S(2)}) collective-permute-start(bf16[128,1792]{1,0:T(8,128)(2,1)S(1)} %convolution_convert_fusion.12), channel_id=1, source_target_pairs={{0,8},{1,9},{2,10},{3,11},{4,12},{5,13},{6,14},{7,15},{8,0},{9,1},... | collective-permute-start | bytes 1376264 | tf_op jit(solution)/shard_map/ppermute | solution.py:67
  196.8 0.9 copy-start.1

commit v10 on v9

--- a/solution.py
+++ b/solution.py
@@ -133,13 +133,13 @@
         flat = rows.reshape(-1, half)
         return jnp.dot(flat, weights, preferred_element_type=F32).reshape(chips, chunk, 2 * ff)
 
-    order = (2, 1, 3, 0)
+    order = (2, 1, 0, 3)
     sent = product(chosen1).astype(BF)
     sent, chosen0 = together((sent, chosen0))
-    part = [send(sent[k], flip=2) for k in order]
+    sent = [sent[k] for k in order]
+    part = [send(value, flip=2) for value in sent[:2]]
     near = product(chosen0)
-    near, info_x = together((near, info_x))
-    pays = [pay0, places(info_x)[1]]
+    pays = [pay0]
 
     hidden, out, came = {}, {}, {}
 
@@ -170,7 +170,12 @@
     middle, back, forth = {}, {}, {}
     finish(0)
     down_product(0, 0)
-    middle[0] = send(weigh(0, 0).astype(BF), 1)
+    hidden[0, 1], info_x = together((hidden[0, 1], info_x))
+    pays.append(places(info_x)[1])
+    middle[0] = weigh(0, 0).astype(BF)
+    middle[0], sent = together((middle[0], sent))
+    part += [send(value, flip=2) for value in sent[2:]]
+    middle[0] = send(middle[0], 1)
     down_product(0, 1)
     middle[0], part[1] = before_weigh(0, (middle[0], part[1]))
     middle[1] = send(weigh(0, 1).astype(BF), 1)
@@ -183,17 +188,17 @@
     back[1] = send(weigh(1, 1).astype(BF), -1, 1)
     finish(2)
     down_product(2, 0)
-    forth[0] = send((weigh(2, 0) + middle[0].astype(F32)).astype(BF), 1)
     part[3] = before_down(2, part[3])
     down_product(2, 1)
-    back[0] = before_weigh(2, back[0])
-    forth[1] = send((weigh(2, 1) + middle[1].astype(F32)).astype(BF), 1, 1)
     finish(3)
     down_product(3, 0)
+    forth[0] = send((weigh(3, 0) + middle[0].astype(F32)).astype(BF), 1)
+    hidden[3, 1] = before_weigh(2, hidden[3, 1])
+    term = [weigh(2, g) for g in range(2)]
+    theirs = send(term[1].astype(BF), flip=1)
     down_product(3, 1)
-    back[1] = before_weigh(3, back[1])
-    term = [weigh(3, g) for g in range(2)]
-    theirs = send(term[1].astype(BF), flip=1)
+    back = before_weigh(3, back)
+    forth[1] = send((weigh(3, 1) + middle[1].astype(F32)).astype(BF), 1, 1)
     mine = (term[0] + back[0].astype(F32) + forth[0].astype(F32)).astype(BF)
     far = (theirs.astype(F32) + back[1].astype(F32) + forth[1].astype(F32)).astype(BF)
 

time: 199 us -> 191 us (0.960)
  waiting for transfers between devices: 132 us -> 117 us
  starting transfers between devices: 34.7 us -> 41.5 us
    ppermute x35, waiting for transfers between devices: 132 us -> 117 us  [send(): lax.ppermute(value, ('dp', 'expert'), [(i * owners + j, (i ^ flip) * owne...]
    ppermute x35, starting transfers between devices: 34.7 us -> 41.5 us  [send(): lax.ppermute(value, ('dp', 'expert'), [(i * owners + j, (i ^ flip) * owne...]
  transfers between devices with their start and end apart: 35 -> 35, of which waited for: 20 -> 17; matrix products, arithmetic and copies ran while one was open for 13% -> 14% of each run, Pallas kernels for 0% -> 0%
where the time goes in v10:
time: 191 us
  waiting for transfers between devices  117 us (61%)
  starting transfers between devices  41.5 us (22%)
  matrix products  21.8 us (11%)
  local copies, waits for them, and re-layouts  5.61 us (3%)
  other arithmetic  3.94 us (2%)
    ppermute x35, waiting for transfers between devices, send(): lax.ppermute(value, ('dp', 'expert'), [(i * owners + j, (i ^ flip) * owne...  117 us
    ppermute x35, starting transfers between devices, send(): lax.ppermute(value, ('dp', 'expert'), [(i * owners + j, (i ^ flip) * owne...  41.5 us
    dot_general x2, matrix products, product(): jnp.dot(flat, weights, preferred_element_type=F32)  11.8 us
    dot_general x8, matrix products, down_product(): value = jnp.dot(hidden[q, g], downs, preferred_element_type=F32).astype(BF)  5.25 us
  transfers between devices with their start and end apart: 35, of which 17 were waited for; matrix products, arithmetic and copies ran while one was open for 14% of the time, Pallas kernels for 0%

profile of v10, /device:TPU:0, one launch (start us, length us, event | category | flops | bytes accessed | tf_op | source)
XLA Modules:
  0.0 190.9 jit_solution(13605740677396566089)
XLA Ops:
  0.0 0.8 convert_bitcast_fusion
  0.8 0.7 fusion.50
  1.5 1.4 constant_dynamic-slice_fusion.1
  3.0 3.0 %collective-permute-start = (bf16[136,1792]{1,0:T(8,128)(2,1)S(1)}, bf16[136,1792]{1,0:T(8,128)(2,1)S(1)}, u32[]{:S(2)}, u32[]{:S(2)}) collective-permute-start(bf16[136,1792]{1,0:T(8,128)(2,1)S(1)} %get-tuple-element.97), channel_id=1, source_target_pairs={{0,16},{1,17},{2,18},{3,19},{4,20},{5,21},{6,22},{7,23},{8,24},{9,... | collective-permute-start | bytes 1462280 | tf_op jit(solution)/shard_map/ppermute | solution.py:67
  6.0 1.6 collective-permute-start.1
  7.6 1.5 collective-permute-start.9
  9.1 8.0 %collective-permute-done = bf16[136,1792]{1,0:T(8,128)(2,1)S(1)} collective-permute-done((bf16[136,1792]{1,0:T(8,128)(2,1)S(1)}, bf16[136,1792]{1,0:T(8,128)(2,1)S(1)}, u32[]{:S(2)}, u32[]{:S(2)}) %collective-permute-start) | collective-permute-done | bytes 487456 | tf_op jit(solution)/shard_map/ppermute | solution.py:67
  17.1 3.8 %collective-permute-start.3 = (bf16[136,1792]{1,0:T(8,128)(2,1)S(1)}, bf16[136,1792]{1,0:T(8,128)(2,1)S(1)}, u32[]{:S(2)}, u32[]{:S(2)}) collective-permute-start(bf16[136,1792]{1,0:T(8,128)(2,1)S(1)} %get-tuple-element.33), channel_id=1, source_target_pairs={{0,6},{1,7},{2,0},{3,1},{4,2},{5,3},{6,4},{7,5},{8,14},{9,15},{10,... | collective-permute-start | bytes 1462280 | tf_op jit(solution)/shard_map/ppermute | solution.py:67
  20.9 3.8 %collective-permute-start.7 = (bf16[136,1792]{1,0:T(8,128)(2,1)S(1)}, bf16[136,1792]{1,0:T(8,128)(2,1)S(1)}, u32[]{:S(2)}, u32[]{:S(2)}) collective-permute-start(bf16[136,1792]{1,0:T(8,128)(2,1)S(1)} %collective-permute-done), channel_id=1, source_target_pairs={{0,6},{1,7},{2,0},{3,1},{4,2},{5,3},{6,4},{7,5},{8,14},{9,15},{10,... | collective-permute-start | bytes 1462280 | tf_op jit(solution)/shard_map/ppermute | solution.py:67
  24.8 1.0 slice_bitcast_fusion.6
  26.0 0.7 slice_bitcast_fusion.24
  26.7 6.1 %collective-permute-done.3 = bf16[136,1792]{1,0:T(8,128)(2,1)S(1)} collective-permute-done((bf16[136,1792]{1,0:T(8,128)(2,1)S(1)}, bf16[136,1792]{1,0:T(8,128)(2,1)S(1)}, u32[]{:S(2)}, u32[]{:S(2)}) %collective-permute-start.3) | collective-permute-done | bytes 487456 | tf_op jit(solution)/shard_map/ppermute | solution.py:67
  32.7 2.1 %collective-permute-start.6 = (bf16[1024,896]{1,0:T(8,128)(2,1)S(1)}, bf16[1024,896]{1,0:T(8,128)(2,1)S(1)}, u32[]{:S(2)}, u32[]{:S(2)}) collective-permute-start(bf16[1024,896]{1,0:T(8,128)(2,1)S(1)} %bitcast.104), channel_id=1, source_target_pairs={{0,16},{1,17},{2,18},{3,19},{4,20},{5,21},{6,22},{7,23},{8,24},{9,... | collective-permute-start | bytes 5505032 | tf_op jit(solution)/shard_map/ppermute | solution.py:67
  34.8 28.0 %collective-permute-done.2 = bf16[136,1792]{1,0:T(8,128)(2,1)S(1)} collective-permute-done((bf16[136,1792]{1,0:T(8,128)(2,1)}, bf16[136,1792]{1,0:T(8,128)(2,1)S(1)}, u32[]{:S(2)}, u32[]{:S(2)}) %collective-permute-start.2) | collective-permute-done | bytes 487456 | tf_op jit(solution)/shard_map/ppermute | solution.py:67
  62.9 1.7 collective-permute-start.5
  64.7 9.2 %collective-permute-done.6 = bf16[1024,896]{1,0:T(8,128)(2,1)S(1)} collective-permute-done((bf16[1024,896]{1,0:T(8,128)(2,1)S(1)}, bf16[1024,896]{1,0:T(8,128)(2,1)S(1)}, u32[]{:S(2)}, u32[]{:S(2)}) %collective-permute-start.6) | collective-permute-done | bytes 1835040 | tf_op jit(solution)/shard_map/ppermute | solution.py:67
  74.2 1.8 collective-permute-done.5
  76.2 0.4 convolution_convert_fusion
  77.0 0.4 convolution_convert_fusion.2
  77.4 0.6 collective-permute-start.8
  78.0 1.5 collective-permute-start.13
  79.5 0.4 convolution_convert_fusion.1
  79.9 0.4 convolution_convert_fusion.3
  80.7 7.9 %collective-permute-done.9 = bf16[896,2048]{1,0:T(8,128)(2,1)} collective-permute-done((bf16[896,2048]{1,0:T(8,128)(2,1)}, bf16[896,2048]{1,0:T(8,128)(2,1)}, u32[]{:S(2)}, u32[]{:S(2)}) %collective-permute-start.9) | collective-permute-done | bytes 3670048 | tf_op jit(solution)/shard_map/ppermute | solution.py:67
  88.6 6.1 %fusion.3 = bf16[4,128,2048]{2,1,0:T(8,128)(2,1)S(1)} fusion(bf16[4,128,1792]{2,1,0:T(8,128)(2,1)S(1)} %pad_maximum_fusion.5, bf16[896,2048]{1,0:T(8,128)(2,1)} %collective-permute-done.9, bf16[896,2048]{1,0:T(8,128)(2,1)S(1)} %bitcast.117), kind=kOutput, calls=%fused_computation.5 | convolution fusion | flops 3773825024 | bytes 11272192 | tf_op jit(solution)/shard_map/dot_general | solution.py:134
  94.8 0.6 collective-permute-start.11
  95.4 5.7 %fusion.2 = f32[512,2048]{1,0:T(8,128)S(1)} fusion(bf16[512,1792]{1,0:T(8,128)(2,1)S(1)} %bitcast.106, bf16[896,2048]{1,0:T(8,128)(2,1)} %collective-permute-done.9, bf16[896,2048]{1,0:T(8,128)(2,1)S(1)} %bitcast.118), kind=kOutput, calls=%fused_computation.3 | convolution fusion | flops 3772776448 | bytes 13369344 | tf_op jit(solution)/shard_map/dot_general | solution.py:134
  101.2 1.6 collective-permute-start.17
  102.7 7.0 %collective-permute-done.11 = bf16[128,2048]{1,0:T(8,128)(2,1)S(1)} collective-permute-done((bf16[128,2048]{1,0:T(8,128)(2,1)S(1)}, bf16[128,2048]{1,0:T(8,128)(2,1)S(1)}, u32[]{:S(2)}, u32[]{:S(2)}) %collective-permute-start.11) | collective-permute-done | bytes 524320 | tf_op jit(solution)/shard_map/ppermute | solution.py:67
  110.1 1.6 collective-permute-start.12
  111.6 0.7 convolution_convert_fusion.10
  112.4 4.1 %collective-permute-done.12 = bf16[128,1024]{1,0:T(8,128)(2,1)S(1)} collective-permute-done((bf16[128,1024]{1,0:T(8,128)(2,1)S(1)}, bf16[128,1024]{1,0:T(8,128)(2,1)S(1)}, u32[]{:S(2)}, u32[]{:S(2)}) %collective-permute-start.12) | collective-permute-done | bytes 262176 | tf_op jit(solution)/shard_map/ppermute | solution.py:67
  117.1 1.8 collective-permute-start.16
  118.9 0.7 convolution_convert_fusion.11
  119.8 0.6 collective-permute-start.19
  120.3 1.5 collective-permute-start.22
  121.9 6.9 %collective-permute-done.16 = bf16[128,1792]{1,0:T(8,128)(2,1)S(1)} collective-permute-done((bf16[128,1792]{1,0:T(8,128)(2,1)S(1)}, bf16[128,1792]{1,0:T(8,128)(2,1)S(1)}, u32[]{:S(2)}, u32[]{:S(2)}) %collective-permute-start.16) | collective-permute-done | bytes 458784 | tf_op jit(solution)/shard_map/ppermute | solution.py:67
  129.1 0.6 collective-permute-start.18
  129.7 0.7 convolution_convert_fusion.6
  130.8 1.1 collective-permute-done.26
  132.3 2.8 %collective-permute-start.27 = (bf16[128,1792]{1,0:T(8,128)(2,1)S(1)}, bf16[128,1792]{1,0:T(8,128)(2,1)S(1)}, u32[]{:S(2)}, u32[]{:S(2)}) collective-permute-start(bf16[128,1792]{1,0:T(8,128)(2,1)S(1)} %convolution_convert_fusion.15), channel_id=1, source_target_pairs={{0,6},{1,7},{2,0},{3,1},{4,2},{5,3},{6,4},{7,5},{8,14},{9,15},{10,... | collective-permute-start | bytes 1376264 | tf_op jit(solution)/shard_map/ppermute | solution.py:67
  135.0 0.5 collective-permute-done.18
  135.8 1.1 collective-permute-start.21
  136.9 0.7 convolution_convert_fusion.9
  137.6 0.7 convolution_convert_fusion.5
  138.4 7.6 %collective-permute-done.29 = bf16[128,1792]{1,0:T(8,128)(2,1)S(1)} collective-permute-done((bf16[128,1792]{1,0:T(8,128)(2,1)S(1)}, bf16[128,1792]{1,0:T(8,128)(2,1)S(1)}, u32[]{:S(2)}, u32[]{:S(2)}) %collective-permute-start.29) | collective-permute-done | bytes 458784 | tf_op jit(solution)/shard_map/ppermute | solution.py:67
  146.3 0.5 collective-permute-start.30
  147.1 1.1 collective-permute-start.24
  148.3 0.7 convolution_convert_fusion.4
  148.9 0.7 convolution_convert_fusion.8
  150.0 1.2 collective-permute-done.31
  151.4 0.3 fusion.8
  151.7 0.9 collective-permute-done.23
  152.7 2.0 %collective-permute-start.32 = (bf16[128,1792]{1,0:T(8,128)(2,1)S(1)}, bf16[128,1792]{1,0:T(8,128)(2,1)S(1)}, u32[]{:S(2)}, u32[]{:S(2)}) collective-permute-start(bf16[128,1792]{1,0:T(8,128)(2,1)S(1)} %fusion.8), channel_id=1, source_target_pairs={{0,2},{1,3},{2,4},{3,5},{4,6},{5,7},{6,0},{7,1},{8,10},{9,11},{10,... | collective-permute-start | bytes 1376264 | tf_op jit(solution)/shard_map/ppermute | solution.py:67
  154.7 9.7 %collective-permute-done.24 = bf16[128,1024]{1,0:T(8,128)(2,1)S(1)} collective-permute-done((bf16[128,1024]{1,0:T(8,128)(2,1)S(1)}, bf16[128,1024]{1,0:T(8,128)(2,1)S(1)}, u32[]{:S(2)}, u32[]{:S(2)}) %collective-permute-start.24) | collective-permute-done | bytes 262176 | tf_op jit(solution)/shard_map/ppermute | solution.py:67
  164.3 0.7 convolution_convert_fusion.7
  165.5 2.5 %collective-permute-start.33 = (bf16[128,1792]{1,0:T(8,128)(2,1)S(1)}, bf16[128,1792]{1,0:T(8,128)(2,1)S(1)}, u32[]{:S(2)}, u32[]{:S(2)}) collective-permute-start(bf16[128,1792]{1,0:T(8,128)(2,1)S(1)} %convolution_convert_fusion.12), channel_id=1, source_target_pairs={{0,8},{1,9},{2,10},{3,11},{4,12},{5,13},{6,14},{7,15},{8,0},{9,1},... | collective-permute-start | bytes 1376264 | tf_op jit(solution)/shard_map/ppermute | solution.py:67
  168.0 0.3 add_convert_fusion.1
  168.3 2.7 %collective-permute-start.34 = (bf16[128,1792]{1,0:T(8,128)(2,1)S(1)}, bf16[128,1792]{1,0:T(8,128)(2,1)S(1)}, u32[]{:S(2)}, u32[]{:S(2)}) collective-permute-start(bf16[128,1792]{1,0:T(8,128)(2,1)S(1)} %add_convert_fusion.1), channel_id=1, source_target_pairs={{0,10},{1,11},{2,12},{3,13},{4,14},{5,15},{6,8},{7,9},{8,2},{9,3},... | collective-permute-start | bytes 1376264 | tf_op jit(solution)/shard_map/ppermute | solution.py:67
  171.0 4.5 %collective-permute-done.32 = bf16[128,1792]{1,0:T(8,128)(2,1)S(1)} collective-permute-done((bf16[128,1792]{1,0:T(8,128)(2,1)S(1)}, bf16[128,1792]{1,0:T(8,128)(2,1)S(1)}, u32[]{:S(2)}, u32[]{:S(2)}) %collective-permute-start.32) | collective-permute-done | bytes 458784 | tf_op jit(solution)/shard_map/ppermute | solution.py:67
  175.5 0.3 fusion.7
  176.0 13.0 %collective-permute-done.33 = bf16[128,1792]{1,0:T(8,128)(2,1)S(1)} collective-permute-done((bf16[128,1792]{1,0:T(8,128)(2,1)S(1)}, bf16[128,1792]{1,0:T(8,128)(2,1)S(1)}, u32[]{:S(2)}, u32[]{:S(2)}) %collective-permute-start.33) | collective-permute-done | bytes 458784 | tf_op jit(solution)/shard_map/ppermute | solution.py:67
  189.3 0.9 copy-done.1
  190.2 0.7 slice_dynamic-update-slice_fusion
  (99 shorter events, 6.3 us)
Async XLA Ops:
  0.0 32.7 %copy-start = (bf16[1,1024,896]{2,1,0:T(8,128)(2,1)S(1)}, bf16[1,1024,896]{2,1,0:T(8,128)(2,1)}, u32[]{:S(2)}) copy-start(bf16[1,1024,896]{2,1,0:T(8,128)(2,1)} %param.7) | copy-start | bytes 5505028
  3.0 14.2 %collective-permute-start = (bf16[136,1792]{1,0:T(8,128)(2,1)S(1)}, bf16[136,1792]{1,0:T(8,128)(2,1)S(1)}, u32[]{:S(2)}, u32[]{:S(2)}) collective-permute-start(bf16[136,1792]{1,0:T(8,128)(2,1)S(1)} %get-tuple-element.97), channel_id=1, source_target_pairs={{0,16},{1,17},{2,18},{3,19},{4,20},{5,21},{6,22},{7,23},{8,24},{9,... | collective-permute-start | bytes 1462280 | tf_op jit(solution)/shard_map/ppermute | solution.py:67
  6.0 18.8 %collective-permute-start.1 = (bf16[136,1792]{1,0:T(8,128)(2,1)S(1)}, bf16[136,1792]{1,0:T(8,128)(2,1)}, u32[]{:S(2)}, u32[]{:S(2)}) collective-permute-start(bf16[136,1792]{1,0:T(8,128)(2,1)S(1)} %get-tuple-element.33), channel_id=1, source_target_pairs={{0,2},{1,3},{2,4},{3,5},{4,6},{5,7},{6,0},{7,1},{8,10},{9,11},{10,... | collective-permute-start | bytes 1462280 | tf_op jit(solution)/shard_map/ppermute | solution.py:67
  7.6 81.0 %collective-permute-start.9 = (bf16[896,2048]{1,0:T(8,128)(2,1)}, bf16[896,2048]{1,0:T(8,128)(2,1)}, u32[]{:S(2)}, u32[]{:S(2)}) collective-permute-start(bf16[896,2048]{1,0:T(8,128)(2,1)} %bitcast.116), channel_id=1, source_target_pairs={{0,8},{1,9},{2,10},{3,11},{4,12},{5,13},{6,14},{7,15},{8,0},{9,1},... | collective-permute-start | bytes 11010056 | tf_op jit(solution)/shard_map/ppermute | solution.py:67
  17.1 15.6 %collective-permute-start.3 = (bf16[136,1792]{1,0:T(8,128)(2,1)S(1)}, bf16[136,1792]{1,0:T(8,128)(2,1)S(1)}, u32[]{:S(2)}, u32[]{:S(2)}) collective-permute-start(bf16[136,1792]{1,0:T(8,128)(2,1)S(1)} %get-tuple-element.33), channel_id=1, source_target_pairs={{0,6},{1,7},{2,0},{3,1},{4,2},{5,3},{6,4},{7,5},{8,14},{9,15},{10,... | collective-permute-start | bytes 1462280 | tf_op jit(solution)/shard_map/ppermute | solution.py:67
  20.9 41.9 %collective-permute-start.4 = (bf16[136,1792]{1,0:T(8,128)(2,1)S(1)}, bf16[136,1792]{1,0:T(8,128)(2,1)S(1)}, u32[]{:S(2)}, u32[]{:S(2)}) collective-permute-start(bf16[136,1792]{1,0:T(8,128)(2,1)S(1)} %collective-permute-done), channel_id=1, source_target_pairs={{0,2},{1,3},{2,4},{3,5},{4,6},{5,7},{6,0},{7,1},{8,10},{9,11},{10,... | collective-permute-start | bytes 1462280 | tf_op jit(solution)/shard_map/ppermute | solution.py:67
  20.9 43.7 %collective-permute-start.7 = (bf16[136,1792]{1,0:T(8,128)(2,1)S(1)}, bf16[136,1792]{1,0:T(8,128)(2,1)S(1)}, u32[]{:S(2)}, u32[]{:S(2)}) collective-permute-start(bf16[136,1792]{1,0:T(8,128)(2,1)S(1)} %collective-permute-done), channel_id=1, source_target_pairs={{0,6},{1,7},{2,0},{3,1},{4,2},{5,3},{6,4},{7,5},{8,14},{9,15},{10,... | collective-permute-start | bytes 1462280 | tf_op jit(solution)/shard_map/ppermute | solution.py:67
  25.9 36.9 %collective-permute-start.2 = (bf16[136,1792]{1,0:T(8,128)(2,1)}, bf16[136,1792]{1,0:T(8,128)(2,1)S(1)}, u32[]{:S(2)}, u32[]{:S(2)}) collective-permute-start(bf16[136,1792]{1,0:T(8,128)(2,1)} %collective-permute-done.1), channel_id=1, source_target_pairs={{0,2},{1,3},{2,4},{3,5},{4,6},{5,7},{6,0},{7,1},{8,10},{9,11},{10,... | collective-permute-start | bytes 1462280 | tf_op jit(solution)/shard_map/ppermute | solution.py:67
  32.7 41.2 %collective-permute-start.6 = (bf16[1024,896]{1,0:T(8,128)(2,1)S(1)}, bf16[1024,896]{1,0:T(8,128)(2,1)S(1)}, u32[]{:S(2)}, u32[]{:S(2)}) collective-permute-start(bf16[1024,896]{1,0:T(8,128)(2,1)S(1)} %bitcast.104), channel_id=1, source_target_pairs={{0,16},{1,17},{2,18},{3,19},{4,20},{5,21},{6,22},{7,23},{8,24},{9,... | collective-permute-start | bytes 5505032 | tf_op jit(solution)/shard_map/ppermute | solution.py:67
  62.9 13.0 %collective-permute-start.5 = (bf16[136,1792]{1,0:T(8,128)(2,1)S(1)}, bf16[136,1792]{1,0:T(8,128)(2,1)S(1)}, u32[]{:S(2)}, u32[]{:S(2)}) collective-permute-start(bf16[136,1792]{1,0:T(8,128)(2,1)S(1)} %collective-permute-done.4), channel_id=1, source_target_pairs={{0,2},{1,3},{2,4},{3,5},{4,6},{5,7},{6,0},{7,1},{8,10},{9,11},{10,... | collective-permute-start | bytes 1462280 | tf_op jit(solution)/shard_map/ppermute | solution.py:67
  76.7 3.7 %collective-permute-start.10 = (bf16[4,64,1792]{2,1,0:T(8,128)(2,1)S(1)}, bf16[4,64,1792]{2,1,0:T(8,128)(2,1)S(1)}, u32[]{:S(2)}, u32[]{:S(2)}) collective-permute-start(bf16[4,64,1792]{2,1,0:T(8,128)(2,1)S(1)} %convolution_convert_fusion), channel_id=1, source_target_pairs={{0,1},{1,0},{2,3},{3,2},{4,5},{5,4},{6,7},{7,6},{8,9},{9,8},{10,11... | collective-permute-start | bytes 2752520 | tf_op jit(solution)/shard_map/ppermute | solution.py:67
  77.4 3.1 %collective-permute-start.8 = (bf16[4,64,1792]{2,1,0:T(8,128)(2,1)S(1)}, bf16[4,64,1792]{2,1,0:T(8,128)(2,1)S(1)}, u32[]{:S(2)}, u32[]{:S(2)}) collective-permute-start(bf16[4,64,1792]{2,1,0:T(8,128)(2,1)S(1)} %convolution_convert_fusion.2), channel_id=1, source_target_pairs={{0,1},{1,0},{2,3},{3,2},{4,5},{5,4},{6,7},{7,6},{8,9},{9,8},{10,11... | collective-permute-start | bytes 2752520 | tf_op jit(solution)/shard_map/ppermute | solution.py:67
  78.0 34.4 %collective-permute-start.13 = (bf16[4,8,256]{2,1,0:T(8,128)(2,1)S(1)}, bf16[4,8,256]{2,1,0:T(8,128)(2,1)S(1)}, u32[]{:S(2)}, u32[]{:S(2)}) collective-permute-start(bf16[4,8,256]{2,1,0:T(8,128)(2,1)S(1)} %pad_maximum_fusion.14), channel_id=1, source_target_pairs={{0,8},{1,9},{2,10},{3,11},{4,12},{5,13},{6,14},{7,15},{8,0},{9,1},... | collective-permute-start | bytes 49160 | tf_op jit(solution)/shard_map/ppermute | solution.py:67
  80.4 8.2 %copy-start.2 = (bf16[1,896,2048]{2,1,0:T(8,128)(2,1)S(1)}, bf16[1,896,2048]{2,1,0:T(8,128)(2,1)}, u32[]{:S(2)}) copy-start(bf16[1,896,2048]{2,1,0:T(8,128)(2,1)} %param.6) | copy-start | bytes 11010052
  94.8 14.9 %collective-permute-start.11 = (bf16[128,2048]{1,0:T(8,128)(2,1)S(1)}, bf16[128,2048]{1,0:T(8,128)(2,1)S(1)}, u32[]{:S(2)}, u32[]{:S(2)}) collective-permute-start(bf16[128,2048]{1,0:T(8,128)(2,1)S(1)} %get-tuple-element.68), channel_id=1, source_target_pairs={{0,16},{1,17},{2,18},{3,19},{4,20},{5,21},{6,22},{7,23},{8,24},{9,... | collective-permute-start | bytes 1572872 | tf_op jit(solution)/shard_map/ppermute | solution.py:67
  101.2 20.8 %collective-permute-start.17 = (bf16[128,2048]{1,0:T(8,128)(2,1)S(1)}, bf16[128,2048]{1,0:T(8,128)(2,1)S(1)}, u32[]{:S(2)}, u32[]{:S(2)}) collective-permute-start(bf16[128,2048]{1,0:T(8,128)(2,1)S(1)} %get-tuple-element.67), channel_id=1, source_target_pairs={{0,16},{1,17},{2,18},{3,19},{4,20},{5,21},{6,22},{7,23},{8,24},{9,... | collective-permute-start | bytes 1572872 | tf_op jit(solution)/shard_map/ppermute | solution.py:67
  110.1 6.4 %collective-permute-start.12 = (bf16[128,1024]{1,0:T(8,128)(2,1)S(1)}, bf16[128,1024]{1,0:T(8,128)(2,1)S(1)}, u32[]{:S(2)}, u32[]{:S(2)}) collective-permute-start(bf16[128,1024]{1,0:T(8,128)(2,1)S(1)} %fusion.12), channel_id=1, source_target_pairs={{0,8},{1,9},{2,10},{3,11},{4,12},{5,13},{6,14},{7,15},{8,0},{9,1},... | collective-permute-start | bytes 786440 | tf_op jit(solution)/shard_map/ppermute | solution.py:67
  112.3 4.5 %collective-permute-start.15 = (bf16[64,1792]{1,0:T(8,128)(2,1)S(1)}, bf16[64,1792]{1,0:T(8,128)(2,1)S(1)}, u32[]{:S(2)}, u32[]{:S(2)}) collective-permute-start(bf16[64,1792]{1,0:T(8,128)(2,1)S(1)} %get-tuple-element.88), channel_id=1, source_target_pairs={{0,1},{1,0},{2,3},{3,2},{4,5},{5,4},{6,7},{7,6},{8,9},{9,8},{10,11... | collective-permute-start | bytes 688136 | tf_op jit(solution)/shard_map/ppermute | solution.py:67
  117.1 11.7 %collective-permute-start.16 = (bf16[128,1792]{1,0:T(8,128)(2,1)S(1)}, bf16[128,1792]{1,0:T(8,128)(2,1)S(1)}, u32[]{:S(2)}, u32[]{:S(2)}) collective-permute-start(bf16[128,1792]{1,0:T(8,128)(2,1)S(1)} %convolution_convert_fusion.16), channel_id=1, source_target_pairs={{0,2},{1,3},{2,4},{3,5},{4,6},{5,7},{6,0},{7,1},{8,10},{9,11},{10,... | collective-permute-start | bytes 1376264 | tf_op jit(solution)/shard_map/ppermute | solution.py:67
  119.8 2.2 %collective-permute-start.14 = (bf16[64,1792]{1,0:T(8,128)(2,1)S(1)}, bf16[64,1792]{1,0:T(8,128)(2,1)S(1)}, u32[]{:S(2)}, u32[]{:S(2)}) collective-permute-start(bf16[64,1792]{1,0:T(8,128)(2,1)S(1)} %get-tuple-element.82), channel_id=1, source_target_pairs={{0,1},{1,0},{2,3},{3,2},{4,5},{5,4},{6,7},{7,6},{8,9},{9,8},{10,11... | collective-permute-start | bytes 688136 | tf_op jit(solution)/shard_map/ppermute | solution.py:67
  119.8 15.3 %collective-permute-start.19 = (bf16[128,2048]{1,0:T(8,128)(2,1)S(1)}, bf16[128,2048]{1,0:T(8,128)(2,1)S(1)}, u32[]{:S(2)}, u32[]{:S(2)}) collective-permute-start(bf16[128,2048]{1,0:T(8,128)(2,1)S(1)} %get-tuple-element.45), channel_id=1, source_target_pairs={{0,16},{1,17},{2,18},{3,19},{4,20},{5,21},{6,22},{7,23},{8,24},{9,... | collective-permute-start | bytes 1572872 | tf_op jit(solution)/shard_map/ppermute | solution.py:67
  120.3 26.5 %collective-permute-start.22 = (bf16[128,2048]{1,0:T(8,128)(2,1)S(1)}, bf16[128,2048]{1,0:T(8,128)(2,1)S(1)}, u32[]{:S(2)}, u32[]{:S(2)}) collective-permute-start(bf16[128,2048]{1,0:T(8,128)(2,1)S(1)} %get-tuple-element.47), channel_id=1, source_target_pairs={{0,16},{1,17},{2,18},{3,19},{4,20},{5,21},{6,22},{7,23},{8,24},{9,... | collective-permute-start | bytes 1572872 | tf_op jit(solution)/shard_map/ppermute | solution.py:67
  129.1 6.4 %collective-permute-start.18 = (bf16[128,1024]{1,0:T(8,128)(2,1)S(1)}, bf16[128,1024]{1,0:T(8,128)(2,1)S(1)}, u32[]{:S(2)}, u32[]{:S(2)}) collective-permute-start(bf16[128,1024]{1,0:T(8,128)(2,1)S(1)} %fusion.11), channel_id=1, source_target_pairs={{0,8},{1,9},{2,10},{3,11},{4,12},{5,13},{6,14},{7,15},{8,0},{9,1},... | collective-permute-start | bytes 786440 | tf_op jit(solution)/shard_map/ppermute | solution.py:67
  130.4 1.6 collective-permute-start.26
  130.8 15.2 %collective-permute-start.29 = (bf16[128,1792]{1,0:T(8,128)(2,1)S(1)}, bf16[128,1792]{1,0:T(8,128)(2,1)S(1)}, u32[]{:S(2)}, u32[]{:S(2)}) collective-permute-start(bf16[128,1792]{1,0:T(8,128)(2,1)S(1)} %convolution_convert_fusion.14), channel_id=1, source_target_pairs={{0,2},{1,3},{2,4},{3,5},{4,6},{5,7},{6,0},{7,1},{8,10},{9,11},{10,... | collective-permute-start | bytes 1376264 | tf_op jit(solution)/shard_map/ppermute | solution.py:67
  132.3 33.2 %collective-permute-start.27 = (bf16[128,1792]{1,0:T(8,128)(2,1)S(1)}, bf16[128,1792]{1,0:T(8,128)(2,1)S(1)}, u32[]{:S(2)}, u32[]{:S(2)}) collective-permute-start(bf16[128,1792]{1,0:T(8,128)(2,1)S(1)} %convolution_convert_fusion.15), channel_id=1, source_target_pairs={{0,6},{1,7},{2,0},{3,1},{4,2},{5,3},{6,4},{7,5},{8,14},{9,15},{10,... | collective-permute-start | bytes 1376264 | tf_op jit(solution)/shard_map/ppermute | solution.py:67
  135.8 11.0 %collective-permute-start.21 = (bf16[128,1024]{1,0:T(8,128)(2,1)S(1)}, bf16[128,1024]{1,0:T(8,128)(2,1)S(1)}, u32[]{:S(2)}, u32[]{:S(2)}) collective-permute-start(bf16[128,1024]{1,0:T(8,128)(2,1)S(1)} %fusion.10), channel_id=1, source_target_pairs={{0,8},{1,9},{2,10},{3,11},{4,12},{5,13},{6,14},{7,15},{8,0},{9,1},... | collective-permute-start | bytes 786440 | tf_op jit(solution)/shard_map/ppermute | solution.py:67
  138.3 7.7 %collective-permute-start.28 = (bf16[64,1792]{1,0:T(8,128)(2,1)S(1)}, bf16[64,1792]{1,0:T(8,128)(2,1)S(1)}, u32[]{:S(2)}, u32[]{:S(2)}) collective-permute-start(bf16[64,1792]{1,0:T(8,128)(2,1)S(1)} %get-tuple-element.80), channel_id=1, source_target_pairs={{0,1},{1,0},{2,3},{3,2},{4,5},{5,4},{6,7},{7,6},{8,9},{9,8},{10,11... | collective-permute-start | bytes 688136 | tf_op jit(solution)/shard_map/ppermute | solution.py:67
  146.0 25.0 %collective-permute-start.20 = (bf16[64,1792]{1,0:T(8,128)(2,1)S(1)}, bf16[64,1792]{1,0:T(8,128)(2,1)S(1)}, u32[]{:S(2)}, u32[]{:S(2)}) collective-permute-start(bf16[64,1792]{1,0:T(8,128)(2,1)S(1)} %get-tuple-element.78), channel_id=1, source_target_pairs={{0,1},{1,0},{2,3},{3,2},{4,5},{5,4},{6,7},{7,6},{8,9},{9,8},{10,11... | collective-permute-start | bytes 688136 | tf_op jit(solution)/shard_map/ppermute | solution.py:67
  146.3 21.7 %collective-permute-start.30 = (bf16[128,1792]{1,0:T(8,128)(2,1)S(1)}, bf16[128,1792]{1,0:T(8,128)(2,1)S(1)}, u32[]{:S(2)}, u32[]{:S(2)}) collective-permute-start(bf16[128,1792]{1,0:T(8,128)(2,1)S(1)} %convolution_convert_fusion.13), channel_id=1, source_target_pairs={{0,14},{1,15},{2,8},{3,9},{4,10},{5,11},{6,12},{7,13},{8,6},{9,7},... | collective-permute-start | bytes 1376264 | tf_op jit(solution)/shard_map/ppermute | solution.py:67
  147.1 17.2 %collective-permute-start.24 = (bf16[128,1024]{1,0:T(8,128)(2,1)S(1)}, bf16[128,1024]{1,0:T(8,128)(2,1)S(1)}, u32[]{:S(2)}, u32[]{:S(2)}) collective-permute-start(bf16[128,1024]{1,0:T(8,128)(2,1)S(1)} %fusion.9), channel_id=1, source_target_pairs={{0,8},{1,9},{2,10},{3,11},{4,12},{5,13},{6,14},{7,15},{8,0},{9,1},... | collective-permute-start | bytes 786440 | tf_op jit(solution)/shard_map/ppermute | solution.py:67
  149.6 1.6 collective-permute-start.31
  151.2 1.5 collective-permute-start.23
  152.7 22.9 %collective-permute-start.32 = (bf16[128,1792]{1,0:T(8,128)(2,1)S(1)}, bf16[128,1792]{1,0:T(8,128)(2,1)S(1)}, u32[]{:S(2)}, u32[]{:S(2)}) collective-permute-start(bf16[128,1792]{1,0:T(8,128)(2,1)S(1)} %fusion.8), channel_id=1, source_target_pairs={{0,2},{1,3},{2,4},{3,5},{4,6},{5,7},{6,0},{7,1},{8,10},{9,11},{10,... | collective-permute-start | bytes 1376264 | tf_op jit(solution)/shard_map/ppermute | solution.py:67
  165.0 3.0 %collective-permute-start.25 = (bf16[64,1792]{1,0:T(8,128)(2,1)S(1)}, bf16[64,1792]{1,0:T(8,128)(2,1)S(1)}, u32[]{:S(2)}, u32[]{:S(2)}) collective-permute-start(bf16[64,1792]{1,0:T(8,128)(2,1)S(1)} %get-tuple-element.76), channel_id=1, source_target_pairs={{0,1},{1,0},{2,3},{3,2},{4,5},{5,4},{6,7},{7,6},{8,9},{9,8},{10,11... | collective-permute-start | bytes 688136 | tf_op jit(solution)/shard_map/ppermute | solution.py:67
  165.5 23.6 %collective-permute-start.33 = (bf16[128,1792]{1,0:T(8,128)(2,1)S(1)}, bf16[128,1792]{1,0:T(8,128)(2,1)S(1)}, u32[]{:S(2)}, u32[]{:S(2)}) collective-permute-start(bf16[128,1792]{1,0:T(8,128)(2,1)S(1)} %convolution_convert_fusion.12), channel_id=1, source_target_pairs={{0,8},{1,9},{2,10},{3,11},{4,12},{5,13},{6,14},{7,15},{8,0},{9,1},... | collective-permute-start | bytes 1376264 | tf_op jit(solution)/shard_map/ppermute | solution.py:67
  168.3 20.7 %collective-permute-start.34 = (bf16[128,1792]{1,0:T(8,128)(2,1)S(1)}, bf16[128,1792]{1,0:T(8,128)(2,1)S(1)}, u32[]{:S(2)}, u32[]{:S(2)}) collective-permute-start(bf16[128,1792]{1,0:T(8,128)(2,1)S(1)} %add_convert_fusion.1), channel_id=1, source_target_pairs={{0,10},{1,11},{2,12},{3,13},{4,14},{5,15},{6,8},{7,9},{8,2},{9,3},... | collective-permute-start | bytes 1376264 | tf_op jit(solution)/shard_map/ppermute | solution.py:67
  189.3 0.9 copy-start.1

commit v11 on v10

--- a/solution.py
+++ b/solution.py
@@ -169,8 +169,8 @@
 
     middle, back, forth = {}, {}, {}
     finish(0)
+    hidden[0, 0], info_x = together((hidden[0, 0], info_x))
     down_product(0, 0)
-    hidden[0, 1], info_x = together((hidden[0, 1], info_x))
     pays.append(places(info_x)[1])
     middle[0] = weigh(0, 0).astype(BF)
     middle[0], sent = together((middle[0], sent))
@@ -185,7 +185,7 @@
     part[2] = before_down(1, part[2])
     down_product(1, 1)
     middle[1] = before_weigh(1, middle[1])
-    back[1] = send(weigh(1, 1).astype(BF), -1, 1)
+    back[1] = send(weigh(1, 1).astype(BF), -1)
     finish(2)
     down_product(2, 0)
     part[3] = before_down(2, part[3])
@@ -195,12 +195,12 @@
     forth[0] = send((weigh(3, 0) + middle[0].astype(F32)).astype(BF), 1)
     hidden[3, 1] = before_weigh(2, hidden[3, 1])
     term = [weigh(2, g) for g in range(2)]
-    theirs = send(term[1].astype(BF), flip=1)
     down_product(3, 1)
     back = before_weigh(3, back)
+    theirs = send((term[1] + back[1].astype(F32)).astype(BF), flip=1)
     forth[1] = send((weigh(3, 1) + middle[1].astype(F32)).astype(BF), 1, 1)
     mine = (term[0] + back[0].astype(F32) + forth[0].astype(F32)).astype(BF)
-    far = (theirs.astype(F32) + back[1].astype(F32) + forth[1].astype(F32)).astype(BF)
+    far = (theirs.astype(F32) + forth[1].astype(F32)).astype(BF)
 
     mixed = jnp.zeros(tokens.shape, BF)
     for r, piece in enumerate(

time: 191 us -> 189 us (0.990)
  starting transfers between devices: 41.5 us -> 37.5 us
  waiting for transfers between devices: 117 us -> 119 us
    ppermute x35, starting transfers between devices: 41.5 us -> 37.5 us  [send(): lax.ppermute(value, ('dp', 'expert'), [(i * owners + j, (i ^ flip) * owne...]
  transfers between devices with their start and end apart: 35 -> 35, of which waited for: 17 -> 18; matrix products, arithmetic and copies ran while one was open for 14% -> 14% of each run, Pallas kernels for 0% -> 0%
where the time goes in v11:
time: 189 us; the launch traced here: 188 us
  waiting for transfers between devices  119 us (63%)
  starting transfers between devices  37.5 us (20%)
  matrix products  21.8 us (12%)
  local copies, waits for them, and re-layouts  5.61 us (3%)
  other arithmetic  3.87 us (2%)
    ppermute x35, waiting for transfers between devices, send(): lax.ppermute(value, ('dp', 'expert'), [(i * owners + j, (i ^ flip) * owne...  119 us
    ppermute x35, starting transfers between devices, send(): lax.ppermute(value, ('dp', 'expert'), [(i * owners + j, (i ^ flip) * owne...  37.5 us
    dot_general x2, matrix products, product(): jnp.dot(flat, weights, preferred_element_type=F32)  11.8 us
    dot_general x8, matrix products, down_product(): value = jnp.dot(hidden[q, g], downs, preferred_element_type=F32).astype(BF)  5.25 us
  transfers between devices with their start and end apart: 35, of which 18 were waited for; matrix products, arithmetic and copies ran while one was open for 14% of the time, Pallas kernels for 0%

profile of v11, /device:TPU:0, one launch (start us, length us, event | category | flops | bytes accessed | tf_op | source)
XLA Modules:
  0.0 188.4 jit_solution(18130368872856427454)
XLA Ops:
  0.0 0.8 convert_bitcast_fusion
  0.8 0.7 fusion.53
  1.5 1.4 constant_dynamic-slice_fusion.1
  3.0 3.0 %collective-permute-start = (bf16[136,1792]{1,0:T(8,128)(2,1)S(1)}, bf16[136,1792]{1,0:T(8,128)(2,1)S(1)}, u32[]{:S(2)}, u32[]{:S(2)}) collective-permute-start(bf16[136,1792]{1,0:T(8,128)(2,1)S(1)} %get-tuple-element.97), channel_id=1, source_target_pairs={{0,16},{1,17},{2,18},{3,19},{4,20},{5,21},{6,22},{7,23},{8,24},{9,... | collective-permute-start | bytes 1462280 | tf_op jit(solution)/shard_map/ppermute | solution.py:67
  6.0 1.6 collective-permute-start.1
  7.6 1.5 collective-permute-start.9
  9.1 8.0 %collective-permute-done = bf16[136,1792]{1,0:T(8,128)(2,1)S(1)} collective-permute-done((bf16[136,1792]{1,0:T(8,128)(2,1)S(1)}, bf16[136,1792]{1,0:T(8,128)(2,1)S(1)}, u32[]{:S(2)}, u32[]{:S(2)}) %collective-permute-start) | collective-permute-done | bytes 487456 | tf_op jit(solution)/shard_map/ppermute | solution.py:67
  17.1 3.8 %collective-permute-start.3 = (bf16[136,1792]{1,0:T(8,128)(2,1)S(1)}, bf16[136,1792]{1,0:T(8,128)(2,1)S(1)}, u32[]{:S(2)}, u32[]{:S(2)}) collective-permute-start(bf16[136,1792]{1,0:T(8,128)(2,1)S(1)} %get-tuple-element.33), channel_id=1, source_target_pairs={{0,6},{1,7},{2,0},{3,1},{4,2},{5,3},{6,4},{7,5},{8,14},{9,15},{10,... | collective-permute-start | bytes 1462280 | tf_op jit(solution)/shard_map/ppermute | solution.py:67
  20.9 3.8 %collective-permute-start.7 = (bf16[136,1792]{1,0:T(8,128)(2,1)S(1)}, bf16[136,1792]{1,0:T(8,128)(2,1)S(1)}, u32[]{:S(2)}, u32[]{:S(2)}) collective-permute-start(bf16[136,1792]{1,0:T(8,128)(2,1)S(1)} %collective-permute-done), channel_id=1, source_target_pairs={{0,6},{1,7},{2,0},{3,1},{4,2},{5,3},{6,4},{7,5},{8,14},{9,15},{10,... | collective-permute-start | bytes 1462280 | tf_op jit(solution)/shard_map/ppermute | solution.py:67
  24.8 1.0 slice_bitcast_fusion.6
  26.0 0.7 slice_bitcast_fusion.24
  26.7 6.1 %collective-permute-done.3 = bf16[136,1792]{1,0:T(8,128)(2,1)S(1)} collective-permute-done((bf16[136,1792]{1,0:T(8,128)(2,1)S(1)}, bf16[136,1792]{1,0:T(8,128)(2,1)S(1)}, u32[]{:S(2)}, u32[]{:S(2)}) %collective-permute-start.3) | collective-permute-done | bytes 487456 | tf_op jit(solution)/shard_map/ppermute | solution.py:67
  32.7 2.1 %collective-permute-start.6 = (bf16[1024,896]{1,0:T(8,128)(2,1)S(1)}, bf16[1024,896]{1,0:T(8,128)(2,1)S(1)}, u32[]{:S(2)}, u32[]{:S(2)}) collective-permute-start(bf16[1024,896]{1,0:T(8,128)(2,1)S(1)} %bitcast.104), channel_id=1, source_target_pairs={{0,16},{1,17},{2,18},{3,19},{4,20},{5,21},{6,22},{7,23},{8,24},{9,... | collective-permute-start | bytes 5505032 | tf_op jit(solution)/shard_map/ppermute | solution.py:67
  34.8 28.0 %collective-permute-done.2 = bf16[136,1792]{1,0:T(8,128)(2,1)S(1)} collective-permute-done((bf16[136,1792]{1,0:T(8,128)(2,1)}, bf16[136,1792]{1,0:T(8,128)(2,1)S(1)}, u32[]{:S(2)}, u32[]{:S(2)}) %collective-permute-start.2) | collective-permute-done | bytes 487456 | tf_op jit(solution)/shard_map/ppermute | solution.py:67
  62.9 1.7 collective-permute-start.5
  64.7 9.2 %collective-permute-done.6 = bf16[1024,896]{1,0:T(8,128)(2,1)S(1)} collective-permute-done((bf16[1024,896]{1,0:T(8,128)(2,1)S(1)}, bf16[1024,896]{1,0:T(8,128)(2,1)S(1)}, u32[]{:S(2)}, u32[]{:S(2)}) %collective-permute-start.6) | collective-permute-done | bytes 1835040 | tf_op jit(solution)/shard_map/ppermute | solution.py:67
  74.2 1.8 collective-permute-done.5
  76.2 0.4 convolution_convert_fusion
  77.0 0.4 convolution_convert_fusion.2
  77.4 0.6 collective-permute-start.8
  78.0 1.5 collective-permute-start.14
  79.5 0.4 convolution_convert_fusion.1
  79.9 0.4 convolution_convert_fusion.3
  80.7 7.9 %collective-permute-done.9 = bf16[896,2048]{1,0:T(8,128)(2,1)} collective-permute-done((bf16[896,2048]{1,0:T(8,128)(2,1)}, bf16[896,2048]{1,0:T(8,128)(2,1)}, u32[]{:S(2)}, u32[]{:S(2)}) %collective-permute-start.9) | collective-permute-done | bytes 3670048 | tf_op jit(solution)/shard_map/ppermute | solution.py:67
  88.6 6.1 %fusion.3 = bf16[4,128,2048]{2,1,0:T(8,128)(2,1)S(1)} fusion(bf16[4,128,1792]{2,1,0:T(8,128)(2,1)S(1)} %pad_maximum_fusion.5, bf16[896,2048]{1,0:T(8,128)(2,1)} %collective-permute-done.9, bf16[896,2048]{1,0:T(8,128)(2,1)S(1)} %bitcast.117), kind=kOutput, calls=%fused_computation.5 | convolution fusion | flops 3773825024 | bytes 11272192 | tf_op jit(solution)/shard_map/dot_general | solution.py:134
  94.8 0.6 collective-permute-start.11
  95.4 5.7 %fusion.2 = f32[512,2048]{1,0:T(8,128)S(1)} fusion(bf16[512,1792]{1,0:T(8,128)(2,1)S(1)} %bitcast.106, bf16[896,2048]{1,0:T(8,128)(2,1)} %collective-permute-done.9, bf16[896,2048]{1,0:T(8,128)(2,1)S(1)} %bitcast.118), kind=kOutput, calls=%fused_computation.3 | convolution fusion | flops 3772776448 | bytes 13369344 | tf_op jit(solution)/shard_map/dot_general | solution.py:134
  101.2 1.6 collective-permute-start.17
  102.7 7.0 %collective-permute-done.11 = bf16[128,2048]{1,0:T(8,128)(2,1)S(1)} collective-permute-done((bf16[128,2048]{1,0:T(8,128)(2,1)S(1)}, bf16[128,2048]{1,0:T(8,128)(2,1)S(1)}, u32[]{:S(2)}, u32[]{:S(2)}) %collective-permute-start.11) | collective-permute-done | bytes 524320 | tf_op jit(solution)/shard_map/ppermute | solution.py:67
  110.1 1.6 collective-permute-start.12
  111.6 0.7 convolution_convert_fusion.10
  112.8 1.1 collective-permute-done.15
  114.2 1.8 collective-permute-start.16
  116.0 0.5 collective-permute-done.12
  116.5 0.7 convolution_convert_fusion.11
  117.3 0.6 collective-permute-start.19
  117.9 1.5 collective-permute-start.22
  119.4 9.4 %collective-permute-done.16 = bf16[128,1792]{1,0:T(8,128)(2,1)S(1)} collective-permute-done((bf16[128,1792]{1,0:T(8,128)(2,1)S(1)}, bf16[128,1792]{1,0:T(8,128)(2,1)S(1)}, u32[]{:S(2)}, u32[]{:S(2)}) %collective-permute-start.16) | collective-permute-done | bytes 458784 | tf_op jit(solution)/shard_map/ppermute | solution.py:67
  129.1 0.6 collective-permute-start.18
  129.7 0.7 convolution_convert_fusion.6
  130.9 1.1 collective-permute-done.26
  132.3 2.8 %collective-permute-start.27 = (bf16[128,1792]{1,0:T(8,128)(2,1)S(1)}, bf16[128,1792]{1,0:T(8,128)(2,1)S(1)}, u32[]{:S(2)}, u32[]{:S(2)}) collective-permute-start(bf16[128,1792]{1,0:T(8,128)(2,1)S(1)} %convolution_convert_fusion.14), channel_id=1, source_target_pairs={{0,6},{1,7},{2,0},{3,1},{4,2},{5,3},{6,4},{7,5},{8,14},{9,15},{10,... | collective-permute-start | bytes 1376264 | tf_op jit(solution)/shard_map/ppermute | solution.py:67
  135.0 1.6 collective-permute-done.18
  137.0 0.6 collective-permute-start.21
  137.6 0.7 convolution_convert_fusion.9
  138.2 0.7 convolution_convert_fusion.5
  139.1 6.9 %collective-permute-done.29 = bf16[128,1792]{1,0:T(8,128)(2,1)S(1)} collective-permute-done((bf16[128,1792]{1,0:T(8,128)(2,1)S(1)}, bf16[128,1792]{1,0:T(8,128)(2,1)S(1)}, u32[]{:S(2)}, u32[]{:S(2)}) %collective-permute-start.29) | collective-permute-done | bytes 458784 | tf_op jit(solution)/shard_map/ppermute | solution.py:67
  146.7 1.6 collective-permute-start.24
  148.3 0.7 convolution_convert_fusion.4
  148.9 0.7 convolution_convert_fusion.8
  150.0 1.2 collective-permute-done.23
  151.4 4.1 %collective-permute-done.24 = bf16[128,1024]{1,0:T(8,128)(2,1)S(1)} collective-permute-done((bf16[128,1024]{1,0:T(8,128)(2,1)S(1)}, bf16[128,1024]{1,0:T(8,128)(2,1)S(1)}, u32[]{:S(2)}, u32[]{:S(2)}) %collective-permute-start.24) | collective-permute-done | bytes 262176 | tf_op jit(solution)/shard_map/ppermute | solution.py:67
  155.5 0.7 convolution_convert_fusion.7
  156.3 0.3 fusion.8
  156.6 1.8 collective-permute-start.32
  158.4 6.1 %collective-permute-done.30 = bf16[128,1792]{1,0:T(8,128)(2,1)S(1)} collective-permute-done((bf16[128,1792]{1,0:T(8,128)(2,1)S(1)}, bf16[128,1792]{1,0:T(8,128)(2,1)S(1)}, u32[]{:S(2)}, u32[]{:S(2)}) %collective-permute-start.30) | collective-permute-done | bytes 458784 | tf_op jit(solution)/shard_map/ppermute | solution.py:67
  164.5 0.3 add_convert_fusion.2
  164.9 1.6 collective-permute-start.33
  166.8 0.4 collective-permute-start.34
  167.1 8.4 %collective-permute-done.32 = bf16[128,1792]{1,0:T(8,128)(2,1)S(1)} collective-permute-done((bf16[128,1792]{1,0:T(8,128)(2,1)S(1)}, bf16[128,1792]{1,0:T(8,128)(2,1)S(1)}, u32[]{:S(2)}, u32[]{:S(2)}) %collective-permute-start.32) | collective-permute-done | bytes 458784 | tf_op jit(solution)/shard_map/ppermute | solution.py:67
  175.5 0.3 fusion.7
  175.9 10.6 %collective-permute-done.33 = bf16[128,1792]{1,0:T(8,128)(2,1)S(1)} collective-permute-done((bf16[128,1792]{1,0:T(8,128)(2,1)S(1)}, bf16[128,1792]{1,0:T(8,128)(2,1)S(1)}, u32[]{:S(2)}, u32[]{:S(2)}) %collective-permute-start.33) | collective-permute-done | bytes 458784 | tf_op jit(solution)/shard_map/ppermute | solution.py:67
  186.8 0.9 copy-done.1
  187.7 0.7 slice_dynamic-update-slice_fusion
  (99 shorter events, 6.4 us)
Async XLA Ops:
  0.0 32.7 %copy-start = (bf16[1,1024,896]{2,1,0:T(8,128)(2,1)S(1)}, bf16[1,1024,896]{2,1,0:T(8,128)(2,1)}, u32[]{:S(2)}) copy-start(bf16[1,1024,896]{2,1,0:T(8,128)(2,1)} %param.7) | copy-start | bytes 5505028
  3.0 14.2 %collective-permute-start = (bf16[136,1792]{1,0:T(8,128)(2,1)S(1)}, bf16[136,1792]{1,0:T(8,128)(2,1)S(1)}, u32[]{:S(2)}, u32[]{:S(2)}) collective-permute-start(bf16[136,1792]{1,0:T(8,128)(2,1)S(1)} %get-tuple-element.97), channel_id=1, source_target_pairs={{0,16},{1,17},{2,18},{3,19},{4,20},{5,21},{6,22},{7,23},{8,24},{9,... | collective-permute-start | bytes 1462280 | tf_op jit(solution)/shard_map/ppermute | solution.py:67
  6.0 18.8 %collective-permute-start.1 = (bf16[136,1792]{1,0:T(8,128)(2,1)S(1)}, bf16[136,1792]{1,0:T(8,128)(2,1)}, u32[]{:S(2)}, u32[]{:S(2)}) collective-permute-start(bf16[136,1792]{1,0:T(8,128)(2,1)S(1)} %get-tuple-element.33), channel_id=1, source_target_pairs={{0,2},{1,3},{2,4},{3,5},{4,6},{5,7},{6,0},{7,1},{8,10},{9,11},{10,... | collective-permute-start | bytes 1462280 | tf_op jit(solution)/shard_map/ppermute | solution.py:67
  7.6 81.0 %collective-permute-start.9 = (bf16[896,2048]{1,0:T(8,128)(2,1)}, bf16[896,2048]{1,0:T(8,128)(2,1)}, u32[]{:S(2)}, u32[]{:S(2)}) collective-permute-start(bf16[896,2048]{1,0:T(8,128)(2,1)} %bitcast.116), channel_id=1, source_target_pairs={{0,8},{1,9},{2,10},{3,11},{4,12},{5,13},{6,14},{7,15},{8,0},{9,1},... | collective-permute-start | bytes 11010056 | tf_op jit(solution)/shard_map/ppermute | solution.py:67
  17.1 15.6 %collective-permute-start.3 = (bf16[136,1792]{1,0:T(8,128)(2,1)S(1)}, bf16[136,1792]{1,0:T(8,128)(2,1)S(1)}, u32[]{:S(2)}, u32[]{:S(2)}) collective-permute-start(bf16[136,1792]{1,0:T(8,128)(2,1)S(1)} %get-tuple-element.33), channel_id=1, source_target_pairs={{0,6},{1,7},{2,0},{3,1},{4,2},{5,3},{6,4},{7,5},{8,14},{9,15},{10,... | collective-permute-start | bytes 1462280 | tf_op jit(solution)/shard_map/ppermute | solution.py:67
  20.9 41.9 %collective-permute-start.4 = (bf16[136,1792]{1,0:T(8,128)(2,1)S(1)}, bf16[136,1792]{1,0:T(8,128)(2,1)S(1)}, u32[]{:S(2)}, u32[]{:S(2)}) collective-permute-start(bf16[136,1792]{1,0:T(8,128)(2,1)S(1)} %collective-permute-done), channel_id=1, source_target_pairs={{0,2},{1,3},{2,4},{3,5},{4,6},{5,7},{6,0},{7,1},{8,10},{9,11},{10,... | collective-permute-start | bytes 1462280 | tf_op jit(solution)/shard_map/ppermute | solution.py:67
  20.9 43.7 %collective-permute-start.7 = (bf16[136,1792]{1,0:T(8,128)(2,1)S(1)}, bf16[136,1792]{1,0:T(8,128)(2,1)S(1)}, u32[]{:S(2)}, u32[]{:S(2)}) collective-permute-start(bf16[136,1792]{1,0:T(8,128)(2,1)S(1)} %collective-permute-done), channel_id=1, source_target_pairs={{0,6},{1,7},{2,0},{3,1},{4,2},{5,3},{6,4},{7,5},{8,14},{9,15},{10,... | collective-permute-start | bytes 1462280 | tf_op jit(solution)/shard_map/ppermute | solution.py:67
  25.9 36.9 %collective-permute-start.2 = (bf16[136,1792]{1,0:T(8,128)(2,1)}, bf16[136,1792]{1,0:T(8,128)(2,1)S(1)}, u32[]{:S(2)}, u32[]{:S(2)}) collective-permute-start(bf16[136,1792]{1,0:T(8,128)(2,1)} %collective-permute-done.1), channel_id=1, source_target_pairs={{0,2},{1,3},{2,4},{3,5},{4,6},{5,7},{6,0},{7,1},{8,10},{9,11},{10,... | collective-permute-start | bytes 1462280 | tf_op jit(solution)/shard_map/ppermute | solution.py:67
  32.7 41.2 %collective-permute-start.6 = (bf16[1024,896]{1,0:T(8,128)(2,1)S(1)}, bf16[1024,896]{1,0:T(8,128)(2,1)S(1)}, u32[]{:S(2)}, u32[]{:S(2)}) collective-permute-start(bf16[1024,896]{1,0:T(8,128)(2,1)S(1)} %bitcast.104), channel_id=1, source_target_pairs={{0,16},{1,17},{2,18},{3,19},{4,20},{5,21},{6,22},{7,23},{8,24},{9,... | collective-permute-start | bytes 5505032 | tf_op jit(solution)/shard_map/ppermute | solution.py:67
  62.9 13.0 %collective-permute-start.5 = (bf16[136,1792]{1,0:T(8,128)(2,1)S(1)}, bf16[136,1792]{1,0:T(8,128)(2,1)S(1)}, u32[]{:S(2)}, u32[]{:S(2)}) collective-permute-start(bf16[136,1792]{1,0:T(8,128)(2,1)S(1)} %collective-permute-done.4), channel_id=1, source_target_pairs={{0,2},{1,3},{2,4},{3,5},{4,6},{5,7},{6,0},{7,1},{8,10},{9,11},{10,... | collective-permute-start | bytes 1462280 | tf_op jit(solution)/shard_map/ppermute | solution.py:67
  76.7 3.7 %collective-permute-start.10 = (bf16[4,64,1792]{2,1,0:T(8,128)(2,1)S(1)}, bf16[4,64,1792]{2,1,0:T(8,128)(2,1)S(1)}, u32[]{:S(2)}, u32[]{:S(2)}) collective-permute-start(bf16[4,64,1792]{2,1,0:T(8,128)(2,1)S(1)} %convolution_convert_fusion), channel_id=1, source_target_pairs={{0,1},{1,0},{2,3},{3,2},{4,5},{5,4},{6,7},{7,6},{8,9},{9,8},{10,11... | collective-permute-start | bytes 2752520 | tf_op jit(solution)/shard_map/ppermute | solution.py:67
  77.4 3.1 %collective-permute-start.8 = (bf16[4,64,1792]{2,1,0:T(8,128)(2,1)S(1)}, bf16[4,64,1792]{2,1,0:T(8,128)(2,1)S(1)}, u32[]{:S(2)}, u32[]{:S(2)}) collective-permute-start(bf16[4,64,1792]{2,1,0:T(8,128)(2,1)S(1)} %convolution_convert_fusion.2), channel_id=1, source_target_pairs={{0,1},{1,0},{2,3},{3,2},{4,5},{5,4},{6,7},{7,6},{8,9},{9,8},{10,11... | collective-permute-start | bytes 2752520 | tf_op jit(solution)/shard_map/ppermute | solution.py:67
  78.0 33.6 %collective-permute-start.14 = (bf16[4,8,256]{2,1,0:T(8,128)(2,1)S(1)}, bf16[4,8,256]{2,1,0:T(8,128)(2,1)S(1)}, u32[]{:S(2)}, u32[]{:S(2)}) collective-permute-start(bf16[4,8,256]{2,1,0:T(8,128)(2,1)S(1)} %pad_maximum_fusion.14), channel_id=1, source_target_pairs={{0,8},{1,9},{2,10},{3,11},{4,12},{5,13},{6,14},{7,15},{8,0},{9,1},... | collective-permute-start | bytes 49160 | tf_op jit(solution)/shard_map/ppermute | solution.py:67
  80.4 8.2 %copy-start.2 = (bf16[1,896,2048]{2,1,0:T(8,128)(2,1)S(1)}, bf16[1,896,2048]{2,1,0:T(8,128)(2,1)}, u32[]{:S(2)}) copy-start(bf16[1,896,2048]{2,1,0:T(8,128)(2,1)} %param.6) | copy-start | bytes 11010052
  94.8 14.9 %collective-permute-start.11 = (bf16[128,2048]{1,0:T(8,128)(2,1)S(1)}, bf16[128,2048]{1,0:T(8,128)(2,1)S(1)}, u32[]{:S(2)}, u32[]{:S(2)}) collective-permute-start(bf16[128,2048]{1,0:T(8,128)(2,1)S(1)} %get-tuple-element.68), channel_id=1, source_target_pairs={{0,16},{1,17},{2,18},{3,19},{4,20},{5,21},{6,22},{7,23},{8,24},{9,... | collective-permute-start | bytes 1572872 | tf_op jit(solution)/shard_map/ppermute | solution.py:67
  101.2 18.3 %collective-permute-start.17 = (bf16[128,2048]{1,0:T(8,128)(2,1)S(1)}, bf16[128,2048]{1,0:T(8,128)(2,1)S(1)}, u32[]{:S(2)}, u32[]{:S(2)}) collective-permute-start(bf16[128,2048]{1,0:T(8,128)(2,1)S(1)} %get-tuple-element.67), channel_id=1, source_target_pairs={{0,16},{1,17},{2,18},{3,19},{4,20},{5,21},{6,22},{7,23},{8,24},{9,... | collective-permute-start | bytes 1572872 | tf_op jit(solution)/shard_map/ppermute | solution.py:67
  110.1 6.4 %collective-permute-start.12 = (bf16[128,1024]{1,0:T(8,128)(2,1)S(1)}, bf16[128,1024]{1,0:T(8,128)(2,1)S(1)}, u32[]{:S(2)}, u32[]{:S(2)}) collective-permute-start(bf16[128,1024]{1,0:T(8,128)(2,1)S(1)} %fusion.12), channel_id=1, source_target_pairs={{0,8},{1,9},{2,10},{3,11},{4,12},{5,13},{6,14},{7,15},{8,0},{9,1},... | collective-permute-start | bytes 786440 | tf_op jit(solution)/shard_map/ppermute | solution.py:67
  112.3 1.6 collective-permute-start.15
  114.2 14.6 %collective-permute-start.16 = (bf16[128,1792]{1,0:T(8,128)(2,1)S(1)}, bf16[128,1792]{1,0:T(8,128)(2,1)S(1)}, u32[]{:S(2)}, u32[]{:S(2)}) collective-permute-start(bf16[128,1792]{1,0:T(8,128)(2,1)S(1)} %convolution_convert_fusion.15), channel_id=1, source_target_pairs={{0,2},{1,3},{2,4},{3,5},{4,6},{5,7},{6,0},{7,1},{8,10},{9,11},{10,... | collective-permute-start | bytes 1376264 | tf_op jit(solution)/shard_map/ppermute | solution.py:67
  117.2 2.2 %collective-permute-start.13 = (bf16[64,1792]{1,0:T(8,128)(2,1)S(1)}, bf16[64,1792]{1,0:T(8,128)(2,1)S(1)}, u32[]{:S(2)}, u32[]{:S(2)}) collective-permute-start(bf16[64,1792]{1,0:T(8,128)(2,1)S(1)} %get-tuple-element.82), channel_id=1, source_target_pairs={{0,1},{1,0},{2,3},{3,2},{4,5},{5,4},{6,7},{7,6},{8,9},{9,8},{10,11... | collective-permute-start | bytes 688136 | tf_op jit(solution)/shard_map/ppermute | solution.py:67
  117.3 17.7 %collective-permute-start.19 = (bf16[128,2048]{1,0:T(8,128)(2,1)S(1)}, bf16[128,2048]{1,0:T(8,128)(2,1)S(1)}, u32[]{:S(2)}, u32[]{:S(2)}) collective-permute-start(bf16[128,2048]{1,0:T(8,128)(2,1)S(1)} %get-tuple-element.45), channel_id=1, source_target_pairs={{0,16},{1,17},{2,18},{3,19},{4,20},{5,21},{6,22},{7,23},{8,24},{9,... | collective-permute-start | bytes 1572872 | tf_op jit(solution)/shard_map/ppermute | solution.py:67
  117.9 28.5 %collective-permute-start.22 = (bf16[128,2048]{1,0:T(8,128)(2,1)S(1)}, bf16[128,2048]{1,0:T(8,128)(2,1)S(1)}, u32[]{:S(2)}, u32[]{:S(2)}) collective-permute-start(bf16[128,2048]{1,0:T(8,128)(2,1)S(1)} %get-tuple-element.47), channel_id=1, source_target_pairs={{0,16},{1,17},{2,18},{3,19},{4,20},{5,21},{6,22},{7,23},{8,24},{9,... | collective-permute-start | bytes 1572872 | tf_op jit(solution)/shard_map/ppermute | solution.py:67
  129.1 7.6 %collective-permute-start.18 = (bf16[128,1024]{1,0:T(8,128)(2,1)S(1)}, bf16[128,1024]{1,0:T(8,128)(2,1)S(1)}, u32[]{:S(2)}, u32[]{:S(2)}) collective-permute-start(bf16[128,1024]{1,0:T(8,128)(2,1)S(1)} %fusion.11), channel_id=1, source_target_pairs={{0,8},{1,9},{2,10},{3,11},{4,12},{5,13},{6,14},{7,15},{8,0},{9,1},... | collective-permute-start | bytes 786440 | tf_op jit(solution)/shard_map/ppermute | solution.py:67
  130.4 1.6 collective-permute-start.26
  130.8 15.2 %collective-permute-start.29 = (bf16[128,1792]{1,0:T(8,128)(2,1)S(1)}, bf16[128,1792]{1,0:T(8,128)(2,1)S(1)}, u32[]{:S(2)}, u32[]{:S(2)}) collective-permute-start(bf16[128,1792]{1,0:T(8,128)(2,1)S(1)} %convolution_convert_fusion.13), channel_id=1, source_target_pairs={{0,2},{1,3},{2,4},{3,5},{4,6},{5,7},{6,0},{7,1},{8,10},{9,11},{10,... | collective-permute-start | bytes 1376264 | tf_op jit(solution)/shard_map/ppermute | solution.py:67
  132.3 26.1 %collective-permute-start.27 = (bf16[128,1792]{1,0:T(8,128)(2,1)S(1)}, bf16[128,1792]{1,0:T(8,128)(2,1)S(1)}, u32[]{:S(2)}, u32[]{:S(2)}) collective-permute-start(bf16[128,1792]{1,0:T(8,128)(2,1)S(1)} %convolution_convert_fusion.14), channel_id=1, source_target_pairs={{0,6},{1,7},{2,0},{3,1},{4,2},{5,3},{6,4},{7,5},{8,14},{9,15},{10,... | collective-permute-start | bytes 1376264 | tf_op jit(solution)/shard_map/ppermute | solution.py:67
  137.0 9.4 %collective-permute-start.21 = (bf16[128,1024]{1,0:T(8,128)(2,1)S(1)}, bf16[128,1024]{1,0:T(8,128)(2,1)S(1)}, u32[]{:S(2)}, u32[]{:S(2)}) collective-permute-start(bf16[128,1024]{1,0:T(8,128)(2,1)S(1)} %fusion.10), channel_id=1, source_target_pairs={{0,8},{1,9},{2,10},{3,11},{4,12},{5,13},{6,14},{7,15},{8,0},{9,1},... | collective-permute-start | bytes 786440 | tf_op jit(solution)/shard_map/ppermute | solution.py:67
  138.9 7.1 %collective-permute-start.28 = (bf16[64,1792]{1,0:T(8,128)(2,1)S(1)}, bf16[64,1792]{1,0:T(8,128)(2,1)S(1)}, u32[]{:S(2)}, u32[]{:S(2)}) collective-permute-start(bf16[64,1792]{1,0:T(8,128)(2,1)S(1)} %get-tuple-element.80), channel_id=1, source_target_pairs={{0,1},{1,0},{2,3},{3,2},{4,5},{5,4},{6,7},{7,6},{8,9},{9,8},{10,11... | collective-permute-start | bytes 688136 | tf_op jit(solution)/shard_map/ppermute | solution.py:67
  146.0 21.1 %collective-permute-start.20 = (bf16[64,1792]{1,0:T(8,128)(2,1)S(1)}, bf16[64,1792]{1,0:T(8,128)(2,1)S(1)}, u32[]{:S(2)}, u32[]{:S(2)}) collective-permute-start(bf16[64,1792]{1,0:T(8,128)(2,1)S(1)} %get-tuple-element.78), channel_id=1, source_target_pairs={{0,1},{1,0},{2,3},{3,2},{4,5},{5,4},{6,7},{7,6},{8,9},{9,8},{10,11... | collective-permute-start | bytes 688136 | tf_op jit(solution)/shard_map/ppermute | solution.py:67
  146.3 18.2 %collective-permute-start.30 = (bf16[128,1792]{1,0:T(8,128)(2,1)S(1)}, bf16[128,1792]{1,0:T(8,128)(2,1)S(1)}, u32[]{:S(2)}, u32[]{:S(2)}) collective-permute-start(bf16[128,1792]{1,0:T(8,128)(2,1)S(1)} %convolution_convert_fusion.12), channel_id=1, source_target_pairs={{0,6},{1,7},{2,0},{3,1},{4,2},{5,3},{6,4},{7,5},{8,14},{9,15},{10,... | collective-permute-start | bytes 1376264 | tf_op jit(solution)/shard_map/ppermute | solution.py:67
  146.7 8.8 %collective-permute-start.24 = (bf16[128,1024]{1,0:T(8,128)(2,1)S(1)}, bf16[128,1024]{1,0:T(8,128)(2,1)S(1)}, u32[]{:S(2)}, u32[]{:S(2)}) collective-permute-start(bf16[128,1024]{1,0:T(8,128)(2,1)S(1)} %fusion.9), channel_id=1, source_target_pairs={{0,8},{1,9},{2,10},{3,11},{4,12},{5,13},{6,14},{7,15},{8,0},{9,1},... | collective-permute-start | bytes 786440 | tf_op jit(solution)/shard_map/ppermute | solution.py:67
  149.7 1.6 collective-permute-start.23
  151.2 5.1 %collective-permute-start.31 = (bf16[64,1792]{1,0:T(8,128)(2,1)S(1)}, bf16[64,1792]{1,0:T(8,128)(2,1)S(1)}, u32[]{:S(2)}, u32[]{:S(2)}) collective-permute-start(bf16[64,1792]{1,0:T(8,128)(2,1)S(1)} %get-tuple-element.86), channel_id=1, source_target_pairs={{0,1},{1,0},{2,3},{3,2},{4,5},{5,4},{6,7},{7,6},{8,9},{9,8},{10,11... | collective-permute-start | bytes 688136 | tf_op jit(solution)/shard_map/ppermute | solution.py:67
  156.2 8.3 %collective-permute-start.25 = (bf16[64,1792]{1,0:T(8,128)(2,1)S(1)}, bf16[64,1792]{1,0:T(8,128)(2,1)S(1)}, u32[]{:S(2)}, u32[]{:S(2)}) collective-permute-start(bf16[64,1792]{1,0:T(8,128)(2,1)S(1)} %get-tuple-element.76), channel_id=1, source_target_pairs={{0,1},{1,0},{2,3},{3,2},{4,5},{5,4},{6,7},{7,6},{8,9},{9,8},{10,11... | collective-permute-start | bytes 688136 | tf_op jit(solution)/shard_map/ppermute | solution.py:67
  156.6 18.9 %collective-permute-start.32 = (bf16[128,1792]{1,0:T(8,128)(2,1)S(1)}, bf16[128,1792]{1,0:T(8,128)(2,1)S(1)}, u32[]{:S(2)}, u32[]{:S(2)}) collective-permute-start(bf16[128,1792]{1,0:T(8,128)(2,1)S(1)} %fusion.8), channel_id=1, source_target_pairs={{0,2},{1,3},{2,4},{3,5},{4,6},{5,7},{6,0},{7,1},{8,10},{9,11},{10,... | collective-permute-start | bytes 1376264 | tf_op jit(solution)/shard_map/ppermute | solution.py:67
  164.9 21.7 %collective-permute-start.33 = (bf16[128,1792]{1,0:T(8,128)(2,1)S(1)}, bf16[128,1792]{1,0:T(8,128)(2,1)S(1)}, u32[]{:S(2)}, u32[]{:S(2)}) collective-permute-start(bf16[128,1792]{1,0:T(8,128)(2,1)S(1)} %add_convert_fusion.2), channel_id=1, source_target_pairs={{0,8},{1,9},{2,10},{3,11},{4,12},{5,13},{6,14},{7,15},{8,0},{9,1},... | collective-permute-start | bytes 1376264 | tf_op jit(solution)/shard_map/ppermute | solution.py:67
  166.8 19.8 %collective-permute-start.34 = (bf16[128,1792]{1,0:T(8,128)(2,1)S(1)}, bf16[128,1792]{1,0:T(8,128)(2,1)S(1)}, u32[]{:S(2)}, u32[]{:S(2)}) collective-permute-start(bf16[128,1792]{1,0:T(8,128)(2,1)S(1)} %add_convert_fusion.1), channel_id=1, source_target_pairs={{0,10},{1,11},{2,12},{3,13},{4,14},{5,15},{6,8},{7,9},{8,2},{9,3},... | collective-permute-start | bytes 1376264 | tf_op jit(solution)/shard_map/ppermute | solution.py:67
  186.7 0.9 copy-start.1

commit v12 on v11

--- a/solution.py
+++ b/solution.py
@@ -137,7 +137,7 @@
     sent = product(chosen1).astype(BF)
     sent, chosen0 = together((sent, chosen0))
     sent = [sent[k] for k in order]
-    part = [send(value, flip=2) for value in sent[:2]]
+    part = [send(sent[0], flip=2)]
     near = product(chosen0)
     pays = [pay0]
 
@@ -169,7 +169,8 @@
 
     middle, back, forth = {}, {}, {}
     finish(0)
-    hidden[0, 0], info_x = together((hidden[0, 0], info_x))
+    hidden[0, 0], info_x, sent = together((hidden[0, 0], info_x, sent))
+    part.append(send(sent[1], flip=2))
     down_product(0, 0)
     pays.append(places(info_x)[1])
     middle[0] = weigh(0, 0).astype(BF)
@@ -177,10 +178,12 @@
     part += [send(value, flip=2) for value in sent[2:]]
     middle[0] = send(middle[0], 1)
     down_product(0, 1)
-    middle[0], part[1] = before_weigh(0, (middle[0], part[1]))
-    middle[1] = send(weigh(0, 1).astype(BF), 1)
+    middle[1], part[1] = together((weigh(0, 1).astype(BF), part[1]))
+    middle[1] = send(middle[1], 1)
+    middle[0], part[1] = together((middle[0], part[1]))
     finish(1)
     down_product(1, 0)
+    came[1, 0], middle[1] = together((came[1, 0], middle[1]))
     back[0] = send(weigh(1, 0).astype(BF), -1)
     part[2] = before_down(1, part[2])
     down_product(1, 1)

time: 189 us -> 188 us (level)
  transfers between devices with their start and end apart: 35 -> 35, of which waited for: 18 -> 17; matrix products, arithmetic and copies ran while one was open for 14% -> 14% of each run, Pallas kernels for 0% -> 0%
where the time goes in v12:
time: 188 us
  waiting for transfers between devices  119 us (63%)
  starting transfers between devices  37.5 us (20%)
  matrix products  21.8 us (12%)
  local copies, waits for them, and re-layouts  5.6 us (3%)
  other arithmetic  3.87 us (2%)
    ppermute x35, waiting for transfers between devices, send(): lax.ppermute(value, ('dp', 'expert'), [(i * owners + j, (i ^ flip) * owne...  119 us
    ppermute x35, starting transfers between devices, send(): lax.ppermute(value, ('dp', 'expert'), [(i * owners + j, (i ^ flip) * owne...  37.5 us
    dot_general x2, matrix products, product(): jnp.dot(flat, weights, preferred_element_type=F32)  11.8 us
    dot_general x8, matrix products, down_product(): value = jnp.dot(hidden[q, g], downs, preferred_element_type=F32).astype(BF)  5.25 us
  transfers between devices with their start and end apart: 35, of which 17 were waited for; matrix products, arithmetic and copies ran while one was open for 14% of the time, Pallas kernels for 0%

profile of v12, /device:TPU:0, one launch (start us, length us, event | category | flops | bytes accessed | tf_op | source)
XLA Modules:
  0.0 188.0 jit_solution(8944619867200334598)
XLA Ops:
  0.0 0.8 convert_bitcast_fusion
  0.8 0.7 fusion.53
  1.5 1.4 constant_dynamic-slice_fusion.1
  3.0 3.0 %collective-permute-start = (bf16[136,1792]{1,0:T(8,128)(2,1)S(1)}, bf16[136,1792]{1,0:T(8,128)(2,1)S(1)}, u32[]{:S(2)}, u32[]{:S(2)}) collective-permute-start(bf16[136,1792]{1,0:T(8,128)(2,1)S(1)} %get-tuple-element.109), channel_id=1, source_target_pairs={{0,16},{1,17},{2,18},{3,19},{4,20},{5,21},{6,22},{7,23},{8,24},{9,... | collective-permute-start | bytes 1462280 | tf_op jit(solution)/shard_map/ppermute | solution.py:67
  6.0 1.6 collective-permute-start.1
  7.6 1.5 collective-permute-start.9
  9.1 8.0 %collective-permute-done = bf16[136,1792]{1,0:T(8,128)(2,1)S(1)} collective-permute-done((bf16[136,1792]{1,0:T(8,128)(2,1)S(1)}, bf16[136,1792]{1,0:T(8,128)(2,1)S(1)}, u32[]{:S(2)}, u32[]{:S(2)}) %collective-permute-start) | collective-permute-done | bytes 487456 | tf_op jit(solution)/shard_map/ppermute | solution.py:67
  17.1 3.8 %collective-permute-start.3 = (bf16[136,1792]{1,0:T(8,128)(2,1)S(1)}, bf16[136,1792]{1,0:T(8,128)(2,1)S(1)}, u32[]{:S(2)}, u32[]{:S(2)}) collective-permute-start(bf16[136,1792]{1,0:T(8,128)(2,1)S(1)} %get-tuple-element.39), channel_id=1, source_target_pairs={{0,6},{1,7},{2,0},{3,1},{4,2},{5,3},{6,4},{7,5},{8,14},{9,15},{10,... | collective-permute-start | bytes 1462280 | tf_op jit(solution)/shard_map/ppermute | solution.py:67
  20.9 3.8 %collective-permute-start.7 = (bf16[136,1792]{1,0:T(8,128)(2,1)S(1)}, bf16[136,1792]{1,0:T(8,128)(2,1)S(1)}, u32[]{:S(2)}, u32[]{:S(2)}) collective-permute-start(bf16[136,1792]{1,0:T(8,128)(2,1)S(1)} %collective-permute-done), channel_id=1, source_target_pairs={{0,6},{1,7},{2,0},{3,1},{4,2},{5,3},{6,4},{7,5},{8,14},{9,15},{10,... | collective-permute-start | bytes 1462280 | tf_op jit(solution)/shard_map/ppermute | solution.py:67
  24.8 1.0 slice_bitcast_fusion.6
  26.0 0.7 slice_bitcast_fusion.24
  26.7 6.1 %collective-permute-done.3 = bf16[136,1792]{1,0:T(8,128)(2,1)S(1)} collective-permute-done((bf16[136,1792]{1,0:T(8,128)(2,1)S(1)}, bf16[136,1792]{1,0:T(8,128)(2,1)S(1)}, u32[]{:S(2)}, u32[]{:S(2)}) %collective-permute-start.3) | collective-permute-done | bytes 487456 | tf_op jit(solution)/shard_map/ppermute | solution.py:67
  32.7 2.1 %collective-permute-start.6 = (bf16[1024,896]{1,0:T(8,128)(2,1)S(1)}, bf16[1024,896]{1,0:T(8,128)(2,1)S(1)}, u32[]{:S(2)}, u32[]{:S(2)}) collective-permute-start(bf16[1024,896]{1,0:T(8,128)(2,1)S(1)} %bitcast.104), channel_id=1, source_target_pairs={{0,16},{1,17},{2,18},{3,19},{4,20},{5,21},{6,22},{7,23},{8,24},{9,... | collective-permute-start | bytes 5505032 | tf_op jit(solution)/shard_map/ppermute | solution.py:67
  34.8 28.0 %collective-permute-done.2 = bf16[136,1792]{1,0:T(8,128)(2,1)S(1)} collective-permute-done((bf16[136,1792]{1,0:T(8,128)(2,1)}, bf16[136,1792]{1,0:T(8,128)(2,1)S(1)}, u32[]{:S(2)}, u32[]{:S(2)}) %collective-permute-start.2) | collective-permute-done | bytes 487456 | tf_op jit(solution)/shard_map/ppermute | solution.py:67
  62.9 1.7 collective-permute-start.5
  64.7 9.2 %collective-permute-done.6 = bf16[1024,896]{1,0:T(8,128)(2,1)S(1)} collective-permute-done((bf16[1024,896]{1,0:T(8,128)(2,1)S(1)}, bf16[1024,896]{1,0:T(8,128)(2,1)S(1)}, u32[]{:S(2)}, u32[]{:S(2)}) %collective-permute-start.6) | collective-permute-done | bytes 1835040 | tf_op jit(solution)/shard_map/ppermute | solution.py:67
  74.2 1.8 collective-permute-done.5
  76.2 0.4 convolution_convert_fusion
  77.0 0.4 convolution_convert_fusion.2
  77.4 0.6 collective-permute-start.8
  78.0 1.5 collective-permute-start.12
  79.5 0.4 convolution_convert_fusion.1
  79.9 0.4 convolution_convert_fusion.3
  80.7 7.9 %collective-permute-done.9 = bf16[896,2048]{1,0:T(8,128)(2,1)} collective-permute-done((bf16[896,2048]{1,0:T(8,128)(2,1)}, bf16[896,2048]{1,0:T(8,128)(2,1)}, u32[]{:S(2)}, u32[]{:S(2)}) %collective-permute-start.9) | collective-permute-done | bytes 3670048 | tf_op jit(solution)/shard_map/ppermute | solution.py:67
  88.6 6.1 %fusion.3 = bf16[4,128,2048]{2,1,0:T(8,128)(2,1)S(1)} fusion(bf16[4,128,1792]{2,1,0:T(8,128)(2,1)S(1)} %pad_maximum_fusion.5, bf16[896,2048]{1,0:T(8,128)(2,1)} %collective-permute-done.9, bf16[896,2048]{1,0:T(8,128)(2,1)S(1)} %bitcast.117), kind=kOutput, calls=%fused_computation.5 | convolution fusion | flops 3773825024 | bytes 11272192 | tf_op jit(solution)/shard_map/dot_general | solution.py:134
  94.8 0.6 collective-permute-start.11
  95.4 5.7 %fusion.2 = f32[512,2048]{1,0:T(8,128)S(1)} fusion(bf16[512,1792]{1,0:T(8,128)(2,1)S(1)} %bitcast.106, bf16[896,2048]{1,0:T(8,128)(2,1)} %collective-permute-done.9, bf16[896,2048]{1,0:T(8,128)(2,1)S(1)} %bitcast.118), kind=kOutput, calls=%fused_computation.3 | convolution fusion | flops 3772776448 | bytes 13369344 | tf_op jit(solution)/shard_map/dot_general | solution.py:134
  101.2 5.8 %collective-permute-done.11 = bf16[128,2048]{1,0:T(8,128)(2,1)S(1)} collective-permute-done((bf16[128,2048]{1,0:T(8,128)(2,1)S(1)}, bf16[128,2048]{1,0:T(8,128)(2,1)S(1)}, u32[]{:S(2)}, u32[]{:S(2)}) %collective-permute-start.11) | collective-permute-done | bytes 524320 | tf_op jit(solution)/shard_map/ppermute | solution.py:67
  107.2 1.6 collective-permute-start.15
  109.1 0.6 collective-permute-start.17
  109.7 0.7 convolution_convert_fusion.11
  110.6 3.0 %collective-permute-done.15 = bf16[128,1024]{1,0:T(8,128)(2,1)S(1)} collective-permute-done((bf16[128,1024]{1,0:T(8,128)(2,1)S(1)}, bf16[128,1024]{1,0:T(8,128)(2,1)S(1)}, u32[]{:S(2)}, u32[]{:S(2)}) %collective-permute-start.15) | collective-permute-done | bytes 262176 | tf_op jit(solution)/shard_map/ppermute | solution.py:67
  113.6 0.7 convolution_convert_fusion.10
  114.7 1.6 collective-permute-start.14
  116.4 0.6 collective-permute-start.19
  117.0 1.5 collective-permute-start.22
  118.8 1.8 collective-permute-done.17
  120.6 1.6 collective-permute-start.27
  122.2 7.7 %collective-permute-done.14 = bf16[128,1792]{1,0:T(8,128)(2,1)S(1)} collective-permute-done((bf16[128,1792]{1,0:T(8,128)(2,1)S(1)}, bf16[128,1792]{1,0:T(8,128)(2,1)S(1)}, u32[]{:S(2)}, u32[]{:S(2)}) %collective-permute-start.14) | collective-permute-done | bytes 458784 | tf_op jit(solution)/shard_map/ppermute | solution.py:67
  130.2 1.6 collective-permute-start.18
  131.8 0.7 convolution_convert_fusion.6
  132.5 5.2 %collective-permute-done.18 = bf16[128,1024]{1,0:T(8,128)(2,1)S(1)} collective-permute-done((bf16[128,1024]{1,0:T(8,128)(2,1)S(1)}, bf16[128,1024]{1,0:T(8,128)(2,1)S(1)}, u32[]{:S(2)}, u32[]{:S(2)}) %collective-permute-start.18) | collective-permute-done | bytes 262176 | tf_op jit(solution)/shard_map/ppermute | solution.py:67
  138.1 1.6 collective-permute-start.21
  139.6 0.7 convolution_convert_fusion.9
  140.3 0.7 convolution_convert_fusion.5
  141.1 0.6 collective-permute-start.20
  142.0 0.6 collective-permute-start.28
  143.0 1.7 collective-permute-start.30
  145.0 1.6 collective-permute-start.24
  146.6 0.7 convolution_convert_fusion.4
  147.3 0.7 convolution_convert_fusion.8
  148.1 1.4 collective-permute-done.23
  149.7 3.1 %collective-permute-done.24 = bf16[128,1024]{1,0:T(8,128)(2,1)S(1)} collective-permute-done((bf16[128,1024]{1,0:T(8,128)(2,1)S(1)}, bf16[128,1024]{1,0:T(8,128)(2,1)S(1)}, u32[]{:S(2)}, u32[]{:S(2)}) %collective-permute-start.24) | collective-permute-done | bytes 262176 | tf_op jit(solution)/shard_map/ppermute | solution.py:67
  152.7 0.7 convolution_convert_fusion.7
  153.9 0.7 collective-permute-start.32
  154.6 0.9 collective-permute-done.28
  155.5 9.6 %collective-permute-done.30 = bf16[128,1792]{1,0:T(8,128)(2,1)S(1)} collective-permute-done((bf16[128,1792]{1,0:T(8,128)(2,1)S(1)}, bf16[128,1792]{1,0:T(8,128)(2,1)S(1)}, u32[]{:S(2)}, u32[]{:S(2)}) %collective-permute-start.30) | collective-permute-done | bytes 458784 | tf_op jit(solution)/shard_map/ppermute | solution.py:67
  165.4 0.6 collective-permute-start.33
  166.3 0.4 collective-permute-start.34
  166.7 8.6 %collective-permute-done.32 = bf16[128,1792]{1,0:T(8,128)(2,1)S(1)} collective-permute-done((bf16[128,1792]{1,0:T(8,128)(2,1)S(1)}, bf16[128,1792]{1,0:T(8,128)(2,1)S(1)}, u32[]{:S(2)}, u32[]{:S(2)}) %collective-permute-start.32) | collective-permute-done | bytes 458784 | tf_op jit(solution)/shard_map/ppermute | solution.py:67
  175.3 0.3 fusion.7
  175.8 10.4 %collective-permute-done.33 = bf16[128,1792]{1,0:T(8,128)(2,1)S(1)} collective-permute-done((bf16[128,1792]{1,0:T(8,128)(2,1)S(1)}, bf16[128,1792]{1,0:T(8,128)(2,1)S(1)}, u32[]{:S(2)}, u32[]{:S(2)}) %collective-permute-start.33) | collective-permute-done | bytes 458784 | tf_op jit(solution)/shard_map/ppermute | solution.py:67
  186.4 0.9 copy-done.1
  187.3 0.7 slice_dynamic-update-slice_fusion
  (99 shorter events, 6.6 us)
Async XLA Ops:
  0.0 32.7 %copy-start = (bf16[1,1024,896]{2,1,0:T(8,128)(2,1)S(1)}, bf16[1,1024,896]{2,1,0:T(8,128)(2,1)}, u32[]{:S(2)}) copy-start(bf16[1,1024,896]{2,1,0:T(8,128)(2,1)} %param.7) | copy-start | bytes 5505028
  3.0 14.2 %collective-permute-start = (bf16[136,1792]{1,0:T(8,128)(2,1)S(1)}, bf16[136,1792]{1,0:T(8,128)(2,1)S(1)}, u32[]{:S(2)}, u32[]{:S(2)}) collective-permute-start(bf16[136,1792]{1,0:T(8,128)(2,1)S(1)} %get-tuple-element.109), channel_id=1, source_target_pairs={{0,16},{1,17},{2,18},{3,19},{4,20},{5,21},{6,22},{7,23},{8,24},{9,... | collective-permute-start | bytes 1462280 | tf_op jit(solution)/shard_map/ppermute | solution.py:67
  6.0 18.8 %collective-permute-start.1 = (bf16[136,1792]{1,0:T(8,128)(2,1)S(1)}, bf16[136,1792]{1,0:T(8,128)(2,1)}, u32[]{:S(2)}, u32[]{:S(2)}) collective-permute-start(bf16[136,1792]{1,0:T(8,128)(2,1)S(1)} %get-tuple-element.39), channel_id=1, source_target_pairs={{0,2},{1,3},{2,4},{3,5},{4,6},{5,7},{6,0},{7,1},{8,10},{9,11},{10,... | collective-permute-start | bytes 1462280 | tf_op jit(solution)/shard_map/ppermute | solution.py:67
  7.6 81.0 %collective-permute-start.9 = (bf16[896,2048]{1,0:T(8,128)(2,1)}, bf16[896,2048]{1,0:T(8,128)(2,1)}, u32[]{:S(2)}, u32[]{:S(2)}) collective-permute-start(bf16[896,2048]{1,0:T(8,128)(2,1)} %bitcast.116), channel_id=1, source_target_pairs={{0,8},{1,9},{2,10},{3,11},{4,12},{5,13},{6,14},{7,15},{8,0},{9,1},... | collective-permute-start | bytes 11010056 | tf_op jit(solution)/shard_map/ppermute | solution.py:67
  17.1 15.6 %collective-permute-start.3 = (bf16[136,1792]{1,0:T(8,128)(2,1)S(1)}, bf16[136,1792]{1,0:T(8,128)(2,1)S(1)}, u32[]{:S(2)}, u32[]{:S(2)}) collective-permute-start(bf16[136,1792]{1,0:T(8,128)(2,1)S(1)} %get-tuple-element.39), channel_id=1, source_target_pairs={{0,6},{1,7},{2,0},{3,1},{4,2},{5,3},{6,4},{7,5},{8,14},{9,15},{10,... | collective-permute-start | bytes 1462280 | tf_op jit(solution)/shard_map/ppermute | solution.py:67
  20.9 41.9 %collective-permute-start.4 = (bf16[136,1792]{1,0:T(8,128)(2,1)S(1)}, bf16[136,1792]{1,0:T(8,128)(2,1)S(1)}, u32[]{:S(2)}, u32[]{:S(2)}) collective-permute-start(bf16[136,1792]{1,0:T(8,128)(2,1)S(1)} %collective-permute-done), channel_id=1, source_target_pairs={{0,2},{1,3},{2,4},{3,5},{4,6},{5,7},{6,0},{7,1},{8,10},{9,11},{10,... | collective-permute-start | bytes 1462280 | tf_op jit(solution)/shard_map/ppermute | solution.py:67
  20.9 43.7 %collective-permute-start.7 = (bf16[136,1792]{1,0:T(8,128)(2,1)S(1)}, bf16[136,1792]{1,0:T(8,128)(2,1)S(1)}, u32[]{:S(2)}, u32[]{:S(2)}) collective-permute-start(bf16[136,1792]{1,0:T(8,128)(2,1)S(1)} %collective-permute-done), channel_id=1, source_target_pairs={{0,6},{1,7},{2,0},{3,1},{4,2},{5,3},{6,4},{7,5},{8,14},{9,15},{10,... | collective-permute-start | bytes 1462280 | tf_op jit(solution)/shard_map/ppermute | solution.py:67
  25.9 36.9 %collective-permute-start.2 = (bf16[136,1792]{1,0:T(8,128)(2,1)}, bf16[136,1792]{1,0:T(8,128)(2,1)S(1)}, u32[]{:S(2)}, u32[]{:S(2)}) collective-permute-start(bf16[136,1792]{1,0:T(8,128)(2,1)} %collective-permute-done.1), channel_id=1, source_target_pairs={{0,2},{1,3},{2,4},{3,5},{4,6},{5,7},{6,0},{7,1},{8,10},{9,11},{10,... | collective-permute-start | bytes 1462280 | tf_op jit(solution)/shard_map/ppermute | solution.py:67
  32.7 41.2 %collective-permute-start.6 = (bf16[1024,896]{1,0:T(8,128)(2,1)S(1)}, bf16[1024,896]{1,0:T(8,128)(2,1)S(1)}, u32[]{:S(2)}, u32[]{:S(2)}) collective-permute-start(bf16[1024,896]{1,0:T(8,128)(2,1)S(1)} %bitcast.104), channel_id=1, source_target_pairs={{0,16},{1,17},{2,18},{3,19},{4,20},{5,21},{6,22},{7,23},{8,24},{9,... | collective-permute-start | bytes 5505032 | tf_op jit(solution)/shard_map/ppermute | solution.py:67
  62.9 13.0 %collective-permute-start.5 = (bf16[136,1792]{1,0:T(8,128)(2,1)S(1)}, bf16[136,1792]{1,0:T(8,128)(2,1)S(1)}, u32[]{:S(2)}, u32[]{:S(2)}) collective-permute-start(bf16[136,1792]{1,0:T(8,128)(2,1)S(1)} %collective-permute-done.4), channel_id=1, source_target_pairs={{0,2},{1,3},{2,4},{3,5},{4,6},{5,7},{6,0},{7,1},{8,10},{9,11},{10,... | collective-permute-start | bytes 1462280 | tf_op jit(solution)/shard_map/ppermute | solution.py:67
  76.7 3.7 %collective-permute-start.10 = (bf16[4,64,1792]{2,1,0:T(8,128)(2,1)S(1)}, bf16[4,64,1792]{2,1,0:T(8,128)(2,1)S(1)}, u32[]{:S(2)}, u32[]{:S(2)}) collective-permute-start(bf16[4,64,1792]{2,1,0:T(8,128)(2,1)S(1)} %convolution_convert_fusion), channel_id=1, source_target_pairs={{0,1},{1,0},{2,3},{3,2},{4,5},{5,4},{6,7},{7,6},{8,9},{9,8},{10,11... | collective-permute-start | bytes 2752520 | tf_op jit(solution)/shard_map/ppermute | solution.py:67
  77.4 3.1 %collective-permute-start.8 = (bf16[4,64,1792]{2,1,0:T(8,128)(2,1)S(1)}, bf16[4,64,1792]{2,1,0:T(8,128)(2,1)S(1)}, u32[]{:S(2)}, u32[]{:S(2)}) collective-permute-start(bf16[4,64,1792]{2,1,0:T(8,128)(2,1)S(1)} %convolution_convert_fusion.2), channel_id=1, source_target_pairs={{0,1},{1,0},{2,3},{3,2},{4,5},{5,4},{6,7},{7,6},{8,9},{9,8},{10,11... | collective-permute-start | bytes 2752520 | tf_op jit(solution)/shard_map/ppermute | solution.py:67
  78.0 30.7 %collective-permute-start.12 = (bf16[4,8,256]{2,1,0:T(8,128)(2,1)S(1)}, bf16[4,8,256]{2,1,0:T(8,128)(2,1)S(1)}, u32[]{:S(2)}, u32[]{:S(2)}) collective-permute-start(bf16[4,8,256]{2,1,0:T(8,128)(2,1)S(1)} %pad_maximum_fusion.14), channel_id=1, source_target_pairs={{0,8},{1,9},{2,10},{3,11},{4,12},{5,13},{6,14},{7,15},{8,0},{9,1},... | collective-permute-start | bytes 49160 | tf_op jit(solution)/shard_map/ppermute | solution.py:67
  80.4 8.2 %copy-start.2 = (bf16[1,896,2048]{2,1,0:T(8,128)(2,1)S(1)}, bf16[1,896,2048]{2,1,0:T(8,128)(2,1)}, u32[]{:S(2)}) copy-start(bf16[1,896,2048]{2,1,0:T(8,128)(2,1)} %param.6) | copy-start | bytes 11010052
  94.8 12.1 %collective-permute-start.11 = (bf16[128,2048]{1,0:T(8,128)(2,1)S(1)}, bf16[128,2048]{1,0:T(8,128)(2,1)S(1)}, u32[]{:S(2)}, u32[]{:S(2)}) collective-permute-start(bf16[128,2048]{1,0:T(8,128)(2,1)S(1)} %get-tuple-element.80), channel_id=1, source_target_pairs={{0,16},{1,17},{2,18},{3,19},{4,20},{5,21},{6,22},{7,23},{8,24},{9,... | collective-permute-start | bytes 1572872 | tf_op jit(solution)/shard_map/ppermute | solution.py:67
  107.2 6.4 %collective-permute-start.15 = (bf16[128,1024]{1,0:T(8,128)(2,1)S(1)}, bf16[128,1024]{1,0:T(8,128)(2,1)S(1)}, u32[]{:S(2)}, u32[]{:S(2)}) collective-permute-start(bf16[128,1024]{1,0:T(8,128)(2,1)S(1)} %fusion.12), channel_id=1, source_target_pairs={{0,8},{1,9},{2,10},{3,11},{4,12},{5,13},{6,14},{7,15},{8,0},{9,1},... | collective-permute-start | bytes 786440 | tf_op jit(solution)/shard_map/ppermute | solution.py:67
  109.1 11.5 %collective-permute-start.17 = (bf16[128,2048]{1,0:T(8,128)(2,1)S(1)}, bf16[128,2048]{1,0:T(8,128)(2,1)S(1)}, u32[]{:S(2)}, u32[]{:S(2)}) collective-permute-start(bf16[128,2048]{1,0:T(8,128)(2,1)S(1)} %get-tuple-element.49), channel_id=1, source_target_pairs={{0,16},{1,17},{2,18},{3,19},{4,20},{5,21},{6,22},{7,23},{8,24},{9,... | collective-permute-start | bytes 1572872 | tf_op jit(solution)/shard_map/ppermute | solution.py:67
  110.4 4.0 %collective-permute-start.13 = (bf16[64,1792]{1,0:T(8,128)(2,1)S(1)}, bf16[64,1792]{1,0:T(8,128)(2,1)S(1)}, u32[]{:S(2)}, u32[]{:S(2)}) collective-permute-start(bf16[64,1792]{1,0:T(8,128)(2,1)S(1)} %get-tuple-element.100), channel_id=1, source_target_pairs={{0,1},{1,0},{2,3},{3,2},{4,5},{5,4},{6,7},{7,6},{8,9},{9,8},{10,11... | collective-permute-start | bytes 688136 | tf_op jit(solution)/shard_map/ppermute | solution.py:67
  114.3 4.2 %collective-permute-start.16 = (bf16[64,1792]{1,0:T(8,128)(2,1)S(1)}, bf16[64,1792]{1,0:T(8,128)(2,1)S(1)}, u32[]{:S(2)}, u32[]{:S(2)}) collective-permute-start(bf16[64,1792]{1,0:T(8,128)(2,1)S(1)} %get-tuple-element.98), channel_id=1, source_target_pairs={{0,1},{1,0},{2,3},{3,2},{4,5},{5,4},{6,7},{7,6},{8,9},{9,8},{10,11... | collective-permute-start | bytes 688136 | tf_op jit(solution)/shard_map/ppermute | solution.py:67
  114.7 15.2 %collective-permute-start.14 = (bf16[128,1792]{1,0:T(8,128)(2,1)S(1)}, bf16[128,1792]{1,0:T(8,128)(2,1)S(1)}, u32[]{:S(2)}, u32[]{:S(2)}) collective-permute-start(bf16[128,1792]{1,0:T(8,128)(2,1)S(1)} %convolution_convert_fusion.15), channel_id=1, source_target_pairs={{0,2},{1,3},{2,4},{3,5},{4,6},{5,7},{6,0},{7,1},{8,10},{9,11},{10,... | collective-permute-start | bytes 1376264 | tf_op jit(solution)/shard_map/ppermute | solution.py:67
  116.4 16.1 %collective-permute-start.19 = (bf16[128,2048]{1,0:T(8,128)(2,1)S(1)}, bf16[128,2048]{1,0:T(8,128)(2,1)S(1)}, u32[]{:S(2)}, u32[]{:S(2)}) collective-permute-start(bf16[128,2048]{1,0:T(8,128)(2,1)S(1)} %get-tuple-element.56), channel_id=1, source_target_pairs={{0,16},{1,17},{2,18},{3,19},{4,20},{5,21},{6,22},{7,23},{8,24},{9,... | collective-permute-start | bytes 1572872 | tf_op jit(solution)/shard_map/ppermute | solution.py:67
  117.0 27.7 %collective-permute-start.22 = (bf16[128,2048]{1,0:T(8,128)(2,1)S(1)}, bf16[128,2048]{1,0:T(8,128)(2,1)S(1)}, u32[]{:S(2)}, u32[]{:S(2)}) collective-permute-start(bf16[128,2048]{1,0:T(8,128)(2,1)S(1)} %get-tuple-element.58), channel_id=1, source_target_pairs={{0,16},{1,17},{2,18},{3,19},{4,20},{5,21},{6,22},{7,23},{8,24},{9,... | collective-permute-start | bytes 1572872 | tf_op jit(solution)/shard_map/ppermute | solution.py:67
  120.6 21.1 %collective-permute-start.27 = (bf16[128,1792]{1,0:T(8,128)(2,1)S(1)}, bf16[128,1792]{1,0:T(8,128)(2,1)S(1)}, u32[]{:S(2)}, u32[]{:S(2)}) collective-permute-start(bf16[128,1792]{1,0:T(8,128)(2,1)S(1)} %convolution_convert_fusion.14), channel_id=1, source_target_pairs={{0,2},{1,3},{2,4},{3,5},{4,6},{5,7},{6,0},{7,1},{8,10},{9,11},{10,... | collective-permute-start | bytes 1376264 | tf_op jit(solution)/shard_map/ppermute | solution.py:67
  130.2 7.6 %collective-permute-start.18 = (bf16[128,1024]{1,0:T(8,128)(2,1)S(1)}, bf16[128,1024]{1,0:T(8,128)(2,1)S(1)}, u32[]{:S(2)}, u32[]{:S(2)}) collective-permute-start(bf16[128,1024]{1,0:T(8,128)(2,1)S(1)} %fusion.11), channel_id=1, source_target_pairs={{0,8},{1,9},{2,10},{3,11},{4,12},{5,13},{6,14},{7,15},{8,0},{9,1},... | collective-permute-start | bytes 786440 | tf_op jit(solution)/shard_map/ppermute | solution.py:67
  132.5 8.7 %collective-permute-start.26 = (bf16[64,1792]{1,0:T(8,128)(2,1)S(1)}, bf16[64,1792]{1,0:T(8,128)(2,1)S(1)}, u32[]{:S(2)}, u32[]{:S(2)}) collective-permute-start(bf16[64,1792]{1,0:T(8,128)(2,1)S(1)} %get-tuple-element.94), channel_id=1, source_target_pairs={{0,1},{1,0},{2,3},{3,2},{4,5},{5,4},{6,7},{7,6},{8,9},{9,8},{10,11... | collective-permute-start | bytes 688136 | tf_op jit(solution)/shard_map/ppermute | solution.py:67
  138.1 6.7 %collective-permute-start.21 = (bf16[128,1024]{1,0:T(8,128)(2,1)S(1)}, bf16[128,1024]{1,0:T(8,128)(2,1)S(1)}, u32[]{:S(2)}, u32[]{:S(2)}) collective-permute-start(bf16[128,1024]{1,0:T(8,128)(2,1)S(1)} %fusion.10), channel_id=1, source_target_pairs={{0,8},{1,9},{2,10},{3,11},{4,12},{5,13},{6,14},{7,15},{8,0},{9,1},... | collective-permute-start | bytes 786440 | tf_op jit(solution)/shard_map/ppermute | solution.py:67
  141.0 1.6 collective-permute-start.29
  141.1 25.6 %collective-permute-start.20 = (bf16[64,1792]{1,0:T(8,128)(2,1)S(1)}, bf16[64,1792]{1,0:T(8,128)(2,1)S(1)}, u32[]{:S(2)}, u32[]{:S(2)}) collective-permute-start(bf16[64,1792]{1,0:T(8,128)(2,1)S(1)} %get-tuple-element.90), channel_id=1, source_target_pairs={{0,1},{1,0},{2,3},{3,2},{4,5},{5,4},{6,7},{7,6},{8,9},{9,8},{10,11... | collective-permute-start | bytes 688136 | tf_op jit(solution)/shard_map/ppermute | solution.py:67
  142.0 13.4 %collective-permute-start.28 = (bf16[128,1792]{1,0:T(8,128)(2,1)S(1)}, bf16[128,1792]{1,0:T(8,128)(2,1)S(1)}, u32[]{:S(2)}, u32[]{:S(2)}) collective-permute-start(bf16[128,1792]{1,0:T(8,128)(2,1)S(1)} %convolution_convert_fusion.13), channel_id=1, source_target_pairs={{0,6},{1,7},{2,0},{3,1},{4,2},{5,3},{6,4},{7,5},{8,14},{9,15},{10,... | collective-permute-start | bytes 1376264 | tf_op jit(solution)/shard_map/ppermute | solution.py:67
  143.0 22.1 %collective-permute-start.30 = (bf16[128,1792]{1,0:T(8,128)(2,1)S(1)}, bf16[128,1792]{1,0:T(8,128)(2,1)S(1)}, u32[]{:S(2)}, u32[]{:S(2)}) collective-permute-start(bf16[128,1792]{1,0:T(8,128)(2,1)S(1)} %convolution_convert_fusion.12), channel_id=1, source_target_pairs={{0,6},{1,7},{2,0},{3,1},{4,2},{5,3},{6,4},{7,5},{8,14},{9,15},{10,... | collective-permute-start | bytes 1376264 | tf_op jit(solution)/shard_map/ppermute | solution.py:67
  145.0 7.7 %collective-permute-start.24 = (bf16[128,1024]{1,0:T(8,128)(2,1)S(1)}, bf16[128,1024]{1,0:T(8,128)(2,1)S(1)}, u32[]{:S(2)}, u32[]{:S(2)}) collective-permute-start(bf16[128,1024]{1,0:T(8,128)(2,1)S(1)} %fusion.9), channel_id=1, source_target_pairs={{0,8},{1,9},{2,10},{3,11},{4,12},{5,13},{6,14},{7,15},{8,0},{9,1},... | collective-permute-start | bytes 786440 | tf_op jit(solution)/shard_map/ppermute | solution.py:67
  148.0 1.6 collective-permute-start.23
  149.5 4.0 %collective-permute-start.31 = (bf16[64,1792]{1,0:T(8,128)(2,1)S(1)}, bf16[64,1792]{1,0:T(8,128)(2,1)S(1)}, u32[]{:S(2)}, u32[]{:S(2)}) collective-permute-start(bf16[64,1792]{1,0:T(8,128)(2,1)S(1)} %get-tuple-element.96), channel_id=1, source_target_pairs={{0,1},{1,0},{2,3},{3,2},{4,5},{5,4},{6,7},{7,6},{8,9},{9,8},{10,11... | collective-permute-start | bytes 688136 | tf_op jit(solution)/shard_map/ppermute | solution.py:67
  153.4 11.6 %collective-permute-start.25 = (bf16[64,1792]{1,0:T(8,128)(2,1)S(1)}, bf16[64,1792]{1,0:T(8,128)(2,1)S(1)}, u32[]{:S(2)}, u32[]{:S(2)}) collective-permute-start(bf16[64,1792]{1,0:T(8,128)(2,1)S(1)} %get-tuple-element.88), channel_id=1, source_target_pairs={{0,1},{1,0},{2,3},{3,2},{4,5},{5,4},{6,7},{7,6},{8,9},{9,8},{10,11... | collective-permute-start | bytes 688136 | tf_op jit(solution)/shard_map/ppermute | solution.py:67
  153.9 21.5 %collective-permute-start.32 = (bf16[128,1792]{1,0:T(8,128)(2,1)S(1)}, bf16[128,1792]{1,0:T(8,128)(2,1)S(1)}, u32[]{:S(2)}, u32[]{:S(2)}) collective-permute-start(bf16[128,1792]{1,0:T(8,128)(2,1)S(1)} %fusion.8), channel_id=1, source_target_pairs={{0,2},{1,3},{2,4},{3,5},{4,6},{5,7},{6,0},{7,1},{8,10},{9,11},{10,... | collective-permute-start | bytes 1376264 | tf_op jit(solution)/shard_map/ppermute | solution.py:67
  165.4 20.8 %collective-permute-start.33 = (bf16[128,1792]{1,0:T(8,128)(2,1)S(1)}, bf16[128,1792]{1,0:T(8,128)(2,1)S(1)}, u32[]{:S(2)}, u32[]{:S(2)}) collective-permute-start(bf16[128,1792]{1,0:T(8,128)(2,1)S(1)} %add_convert_fusion.2), channel_id=1, source_target_pairs={{0,8},{1,9},{2,10},{3,11},{4,12},{5,13},{6,14},{7,15},{8,0},{9,1},... | collective-permute-start | bytes 1376264 | tf_op jit(solution)/shard_map/ppermute | solution.py:67
  166.3 19.9 %collective-permute-start.34 = (bf16[128,1792]{1,0:T(8,128)(2,1)S(1)}, bf16[128,1792]{1,0:T(8,128)(2,1)S(1)}, u32[]{:S(2)}, u32[]{:S(2)}) collective-permute-start(bf16[128,1792]{1,0:T(8,128)(2,1)S(1)} %add_convert_fusion.1), channel_id=1, source_target_pairs={{0,10},{1,11},{2,12},{3,13},{4,14},{5,15},{6,8},{7,9},{8,2},{9,3},... | collective-permute-start | bytes 1376264 | tf_op jit(solution)/shard_map/ppermute | solution.py:67
  186.4 0.9 copy-start.1

commit v13 on v11

--- a/solution.py
+++ b/solution.py
@@ -129,15 +129,21 @@
     chosen1, gate_x = together((chosen1, gate_x))
     weights = jnp.concatenate([gate, gate_x])
 
-    def product(rows):
+    def product(rows, lo=0, hi=2 * ff):
         flat = rows.reshape(-1, half)
-        return jnp.dot(flat, weights, preferred_element_type=F32).reshape(chips, chunk, 2 * ff)
+        return jnp.dot(flat, weights[:, lo:hi], preferred_element_type=F32).reshape(
+            chips, chunk, hi - lo
+        )
 
     order = (2, 1, 0, 3)
-    sent = product(chosen1).astype(BF)
-    sent, chosen0 = together((sent, chosen0))
-    sent = [sent[k] for k in order]
-    part = [send(value, flip=2) for value in sent[:2]]
+    gates = product(chosen1, 0, ff).astype(BF)
+    gates, chosen1 = together((gates, chosen1))
+    gate_part = send(gates[order[0]], flip=2)
+    ups = product(chosen1, ff).astype(BF)
+    ups, chosen0 = together((ups, chosen0))
+    part = [send(ups[order[0]], flip=2)]
+    chosen0, gate_part = together((chosen0, gate_part))
+    part[0] = jnp.concatenate([gate_part, part[0]], axis=1)
     near = product(chosen0)
     pays = [pay0]
 
@@ -171,10 +177,16 @@
     finish(0)
     hidden[0, 0], info_x = together((hidden[0, 0], info_x))
     down_product(0, 0)
+    out[0, 0], gates, ups = together((out[0, 0], gates, ups))
+
+    def whole(q):
+        return jnp.concatenate([gates[order[q]], ups[order[q]]], axis=1)
+
+    part.append(send(whole(1), flip=2))
     pays.append(places(info_x)[1])
     middle[0] = weigh(0, 0).astype(BF)
-    middle[0], sent = together((middle[0], sent))
-    part += [send(value, flip=2) for value in sent[2:]]
+    middle[0], gates, ups = together((middle[0], gates, ups))
+    part += [send(whole(q), flip=2) for q in range(2, chips)]
     middle[0] = send(middle[0], 1)
     down_product(0, 1)
     middle[0], part[1] = before_weigh(0, (middle[0], part[1]))

time: 189 us -> 186 us (0.984)
  waiting for transfers between devices: 119 us -> 116 us
  starting transfers between devices: 37.5 us -> 35.6 us
    ppermute x35 -> x36, waiting for transfers between devices: 119 us -> 116 us  [send(): lax.ppermute(value, ('dp', 'expert'), [(i * owners + j, (i ^ flip) * owne...]
    ppermute x35 -> x36, starting transfers between devices: 37.5 us -> 35.6 us  [send(): lax.ppermute(value, ('dp', 'expert'), [(i * owners + j, (i ^ flip) * owne...]
    dot_general x2 -> x3, matrix products: 11.8 us -> 12.9 us  [product(): jnp.dot(flat, weights[:, lo:hi], preferred_element_type=F32)]
  transfers between devices with their start and end apart: 35 -> 36, of which waited for: 18 -> 19; matrix products, arithmetic and copies ran while one was open for 14% -> 15% of each run, Pallas kernels for 0% -> 0%
where the time goes in v13:
time: 186 us; the launch traced here: 185 us
  waiting for transfers between devices  116 us (62%)
  starting transfers between devices  35.6 us (19%)
  matrix products  22.9 us (12%)
  local copies, waits for them, and re-layouts  5.6 us (3%)
  other arithmetic  3.96 us (2%)
    ppermute x36, waiting for transfers between devices, send(): lax.ppermute(value, ('dp', 'expert'), [(i * owners + j, (i ^ flip) * owne...  116 us
    ppermute x36, starting transfers between devices, send(): lax.ppermute(value, ('dp', 'expert'), [(i * owners + j, (i ^ flip) * owne...  35.6 us
    dot_general x3, matrix products, product(): jnp.dot(flat, weights[:, lo:hi], preferred_element_type=F32)  12.9 us
    dot_general x8, matrix products, down_product(): value = jnp.dot(hidden[q, g], downs, preferred_element_type=F32).astype(BF)  5.26 us
  transfers between devices with their start and end apart: 36, of which 19 were waited for; matrix products, arithmetic and copies ran while one was open for 15% of the time, Pallas kernels for 0%

profile of v13, /device:TPU:0, one launch (start us, length us, event | category | flops | bytes accessed | tf_op | source)
XLA Modules:
  0.0 185.2 jit_solution(15092738535125696252)
XLA Ops:
  0.0 0.8 convert_bitcast_fusion
  0.8 0.7 fusion.62
  1.5 1.4 constant_dynamic-slice_fusion.1
  3.0 3.0 %collective-permute-start = (bf16[136,1792]{1,0:T(8,128)(2,1)S(1)}, bf16[136,1792]{1,0:T(8,128)(2,1)S(1)}, u32[]{:S(2)}, u32[]{:S(2)}) collective-permute-start(bf16[136,1792]{1,0:T(8,128)(2,1)S(1)} %get-tuple-element.111), channel_id=1, source_target_pairs={{0,16},{1,17},{2,18},{3,19},{4,20},{5,21},{6,22},{7,23},{8,24},{9,... | collective-permute-start | bytes 1462280 | tf_op jit(solution)/shard_map/ppermute | solution.py:67
  6.0 1.6 collective-permute-start.1
  7.6 1.5 collective-permute-start.9
  9.1 8.0 %collective-permute-done = bf16[136,1792]{1,0:T(8,128)(2,1)S(1)} collective-permute-done((bf16[136,1792]{1,0:T(8,128)(2,1)S(1)}, bf16[136,1792]{1,0:T(8,128)(2,1)S(1)}, u32[]{:S(2)}, u32[]{:S(2)}) %collective-permute-start) | collective-permute-done | bytes 487456 | tf_op jit(solution)/shard_map/ppermute | solution.py:67
  17.1 3.8 %collective-permute-start.3 = (bf16[136,1792]{1,0:T(8,128)(2,1)S(1)}, bf16[136,1792]{1,0:T(8,128)(2,1)S(1)}, u32[]{:S(2)}, u32[]{:S(2)}) collective-permute-start(bf16[136,1792]{1,0:T(8,128)(2,1)S(1)} %get-tuple-element.40), channel_id=1, source_target_pairs={{0,6},{1,7},{2,0},{3,1},{4,2},{5,3},{6,4},{7,5},{8,14},{9,15},{10,... | collective-permute-start | bytes 1462280 | tf_op jit(solution)/shard_map/ppermute | solution.py:67
  21.0 0.5 collective-permute-start.7
  21.5 1.0 slice_bitcast_fusion.2
  22.6 1.6 collective-permute-start.4
  24.3 0.7 slice_bitcast_fusion.28
  25.0 7.6 %collective-permute-done.3 = bf16[136,1792]{1,0:T(8,128)(2,1)S(1)} collective-permute-done((bf16[136,1792]{1,0:T(8,128)(2,1)S(1)}, bf16[136,1792]{1,0:T(8,128)(2,1)S(1)}, u32[]{:S(2)}, u32[]{:S(2)}) %collective-permute-start.3) | collective-permute-done | bytes 487456 | tf_op jit(solution)/shard_map/ppermute | solution.py:67
  32.6 1.6 collective-permute-start.6
  34.1 28.7 %collective-permute-done.2 = bf16[136,1792]{1,0:T(8,128)(2,1)S(1)} collective-permute-done((bf16[136,1792]{1,0:T(8,128)(2,1)}, bf16[136,1792]{1,0:T(8,128)(2,1)S(1)}, u32[]{:S(2)}, u32[]{:S(2)}) %collective-permute-start.2) | collective-permute-done | bytes 487456 | tf_op jit(solution)/shard_map/ppermute | solution.py:67
  62.8 1.7 collective-permute-start.5
  64.7 8.1 %collective-permute-done.6 = bf16[1024,896]{1,0:T(8,128)(2,1)S(1)} collective-permute-done((bf16[1024,896]{1,0:T(8,128)(2,1)S(1)}, bf16[1024,896]{1,0:T(8,128)(2,1)S(1)}, u32[]{:S(2)}, u32[]{:S(2)}) %collective-permute-start.6) | collective-permute-done | bytes 1835040 | tf_op jit(solution)/shard_map/ppermute | solution.py:67
  73.0 4.6 %collective-permute-done.5 = bf16[136,1792]{1,0:T(8,128)(2,1)S(1)} collective-permute-done((bf16[136,1792]{1,0:T(8,128)(2,1)S(1)}, bf16[136,1792]{1,0:T(8,128)(2,1)S(1)}, u32[]{:S(2)}, u32[]{:S(2)}) %collective-permute-start.5) | collective-permute-done | bytes 487456 | tf_op jit(solution)/shard_map/ppermute | solution.py:67
  78.0 0.4 convolution_convert_fusion
  78.7 0.4 convolution_convert_fusion.2
  79.2 0.6 collective-permute-start.8
  79.7 1.5 collective-permute-start.15
  81.2 0.4 convolution_convert_fusion.1
  81.7 0.4 convolution_convert_fusion.3
  82.4 6.2 %collective-permute-done.9 = bf16[896,2048]{1,0:T(8,128)(2,1)} collective-permute-done((bf16[896,2048]{1,0:T(8,128)(2,1)}, bf16[896,2048]{1,0:T(8,128)(2,1)}, u32[]{:S(2)}, u32[]{:S(2)}) %collective-permute-start.9) | collective-permute-done | bytes 3670048 | tf_op jit(solution)/shard_map/ppermute | solution.py:67
  88.6 3.6 %fusion.15 = bf16[4,128,1024]{2,1,0:T(8,128)(2,1)S(1)} fusion(bf16[4,128,1792]{2,1,0:T(8,128)(2,1)S(1)} %pad_maximum_fusion.4, bf16[896,2048]{1,0:T(8,128)(2,1)S(1)} %bitcast.131, bf16[896,2048]{1,0:T(8,128)(2,1)} %collective-permute-done.9), kind=kOutput, calls=%fused_computation.39 | convolution fusion | flops 1886912512 | bytes 10223616 | tf_op jit(solution)/shard_map/dot_general | solution.py:134
  92.2 0.6 collective-permute-start.11
  92.8 3.6 %fusion.12 = bf16[4,128,1024]{2,1,0:T(8,128)(2,1)S(1)} fusion(bf16[4,128,1792]{2,1,0:T(8,128)(2,1)S(1)} %pad_maximum_fusion.4, bf16[896,2048]{1,0:T(8,128)(2,1)S(1)} %bitcast.132, bf16[896,2048]{1,0:T(8,128)(2,1)} %collective-permute-done.9), kind=kOutput, calls=%fused_computation.38 | convolution fusion | flops 1886912512 | bytes 10223616 | tf_op jit(solution)/shard_map/dot_general | solution.py:134
  96.4 1.6 collective-permute-start.12
  98.0 2.4 %collective-permute-done.11 = bf16[128,1024]{1,0:T(8,128)(2,1)S(1)} collective-permute-done((bf16[128,1024]{1,0:T(8,128)(2,1)S(1)}, bf16[128,1024]{1,0:T(8,128)(2,1)S(1)}, u32[]{:S(2)}, u32[]{:S(2)}) %collective-permute-start.11) | collective-permute-done | bytes 262176 | tf_op jit(solution)/shard_map/ppermute | solution.py:67
  100.3 5.7 %fusion = f32[512,2048]{1,0:T(8,128)S(1)} fusion(bf16[512,1792]{1,0:T(8,128)(2,1)S(1)} %bitcast.120, bf16[896,2048]{1,0:T(8,128)(2,1)} %collective-permute-done.9, bf16[896,2048]{1,0:T(8,128)(2,1)S(1)} %bitcast.133), kind=kOutput, calls=%fused_computation.5 | convolution fusion | flops 3772776448 | bytes 13369344 | tf_op jit(solution)/shard_map/dot_general | solution.py:134
  106.4 1.6 collective-permute-start.13
  108.3 0.7 convolution_convert_fusion.10
  109.4 1.4 collective-permute-done.16
  111.1 1.8 collective-permute-start.17
  113.0 2.0 %collective-permute-start.20 = (bf16[128,2048]{1,0:T(8,128)(2,1)S(1)}, bf16[128,2048]{1,0:T(8,128)(2,1)S(1)}, u32[]{:S(2)}, u32[]{:S(2)}) collective-permute-start(bf16[128,2048]{1,0:T(8,128)(2,1)S(1)} %pad_maximum_fusion.10), channel_id=1, source_target_pairs={{0,16},{1,17},{2,18},{3,19},{4,20},{5,21},{6,22},{7,23},{8,24},{9,... | collective-permute-start | bytes 1572872 | tf_op jit(solution)/shard_map/ppermute | solution.py:67
  115.0 0.7 convolution_convert_fusion.11
  116.0 1.3 collective-permute-done.14
  117.3 5.6 %collective-permute-done.18 = bf16[128,2048]{1,0:T(8,128)(2,1)S(1)} collective-permute-done((bf16[128,2048]{1,0:T(8,128)(2,1)S(1)}, bf16[128,2048]{1,0:T(8,128)(2,1)S(1)}, u32[]{:S(2)}, u32[]{:S(2)}) %collective-permute-start.18) | collective-permute-done | bytes 524320 | tf_op jit(solution)/shard_map/ppermute | solution.py:67
  122.9 2.8 %collective-permute-done.17 = bf16[128,1792]{1,0:T(8,128)(2,1)S(1)} collective-permute-done((bf16[128,1792]{1,0:T(8,128)(2,1)S(1)}, bf16[128,1792]{1,0:T(8,128)(2,1)S(1)}, u32[]{:S(2)}, u32[]{:S(2)}) %collective-permute-start.17) | collective-permute-done | bytes 458784 | tf_op jit(solution)/shard_map/ppermute | solution.py:67
  125.9 0.6 collective-permute-start.19
  126.5 0.7 convolution_convert_fusion.6
  127.7 1.1 collective-permute-done.27
  129.1 2.8 %collective-permute-start.28 = (bf16[128,1792]{1,0:T(8,128)(2,1)S(1)}, bf16[128,1792]{1,0:T(8,128)(2,1)S(1)}, u32[]{:S(2)}, u32[]{:S(2)}) collective-permute-start(bf16[128,1792]{1,0:T(8,128)(2,1)S(1)} %convolution_convert_fusion.14), channel_id=1, source_target_pairs={{0,6},{1,7},{2,0},{3,1},{4,2},{5,3},{6,4},{7,5},{8,14},{9,15},{10,... | collective-permute-start | bytes 1376264 | tf_op jit(solution)/shard_map/ppermute | solution.py:67
  131.9 2.2 %collective-permute-done.20 = bf16[128,2048]{1,0:T(8,128)(2,1)S(1)} collective-permute-done((bf16[128,2048]{1,0:T(8,128)(2,1)S(1)}, bf16[128,2048]{1,0:T(8,128)(2,1)S(1)}, u32[]{:S(2)}, u32[]{:S(2)}) %collective-permute-start.20) | collective-permute-done | bytes 524320 | tf_op jit(solution)/shard_map/ppermute | solution.py:67
  134.4 0.6 collective-permute-start.22
  135.0 0.7 convolution_convert_fusion.9
  135.7 0.7 convolution_convert_fusion.5
  136.5 6.4 %collective-permute-done.30 = bf16[128,1792]{1,0:T(8,128)(2,1)S(1)} collective-permute-done((bf16[128,1792]{1,0:T(8,128)(2,1)S(1)}, bf16[128,1792]{1,0:T(8,128)(2,1)S(1)}, u32[]{:S(2)}, u32[]{:S(2)}) %collective-permute-start.30) | collective-permute-done | bytes 458784 | tf_op jit(solution)/shard_map/ppermute | solution.py:67
  143.6 1.5 collective-permute-start.25
  145.1 0.7 convolution_convert_fusion.4
  145.8 0.7 convolution_convert_fusion.8
  146.8 1.2 collective-permute-done.24
  148.3 4.1 %collective-permute-done.25 = bf16[128,1024]{1,0:T(8,128)(2,1)S(1)} collective-permute-done((bf16[128,1024]{1,0:T(8,128)(2,1)S(1)}, bf16[128,1024]{1,0:T(8,128)(2,1)S(1)}, u32[]{:S(2)}, u32[]{:S(2)}) %collective-permute-start.25) | collective-permute-done | bytes 262176 | tf_op jit(solution)/shard_map/ppermute | solution.py:67
  152.4 0.7 convolution_convert_fusion.7
  153.5 1.8 collective-permute-start.33
  155.3 6.1 %collective-permute-done.31 = bf16[128,1792]{1,0:T(8,128)(2,1)S(1)} collective-permute-done((bf16[128,1792]{1,0:T(8,128)(2,1)S(1)}, bf16[128,1792]{1,0:T(8,128)(2,1)S(1)}, u32[]{:S(2)}, u32[]{:S(2)}) %collective-permute-start.31) | collective-permute-done | bytes 458784 | tf_op jit(solution)/shard_map/ppermute | solution.py:67
  161.7 1.5 collective-permute-start.34
  163.6 0.6 collective-permute-start.35
  164.2 8.2 %collective-permute-done.33 = bf16[128,1792]{1,0:T(8,128)(2,1)S(1)} collective-permute-done((bf16[128,1792]{1,0:T(8,128)(2,1)S(1)}, bf16[128,1792]{1,0:T(8,128)(2,1)S(1)}, u32[]{:S(2)}, u32[]{:S(2)}) %collective-permute-start.33) | collective-permute-done | bytes 458784 | tf_op jit(solution)/shard_map/ppermute | solution.py:67
  172.4 0.3 fusion.10
  172.8 10.6 %collective-permute-done.34 = bf16[128,1792]{1,0:T(8,128)(2,1)S(1)} collective-permute-done((bf16[128,1792]{1,0:T(8,128)(2,1)S(1)}, bf16[128,1792]{1,0:T(8,128)(2,1)S(1)}, u32[]{:S(2)}, u32[]{:S(2)}) %collective-permute-start.34) | collective-permute-done | bytes 458784 | tf_op jit(solution)/shard_map/ppermute | solution.py:67
  183.6 0.9 copy-done.1
  184.5 0.7 slice_dynamic-update-slice_fusion
  (108 shorter events, 7.3 us)
Async XLA Ops:
  0.0 32.6 %copy-start = (bf16[1,1024,896]{2,1,0:T(8,128)(2,1)S(1)}, bf16[1,1024,896]{2,1,0:T(8,128)(2,1)}, u32[]{:S(2)}) copy-start(bf16[1,1024,896]{2,1,0:T(8,128)(2,1)} %param.7) | copy-start | bytes 5505028
  3.0 14.2 %collective-permute-start = (bf16[136,1792]{1,0:T(8,128)(2,1)S(1)}, bf16[136,1792]{1,0:T(8,128)(2,1)S(1)}, u32[]{:S(2)}, u32[]{:S(2)}) collective-permute-start(bf16[136,1792]{1,0:T(8,128)(2,1)S(1)} %get-tuple-element.111), channel_id=1, source_target_pairs={{0,16},{1,17},{2,18},{3,19},{4,20},{5,21},{6,22},{7,23},{8,24},{9,... | collective-permute-start | bytes 1462280 | tf_op jit(solution)/shard_map/ppermute | solution.py:67
  6.0 15.5 %collective-permute-start.1 = (bf16[136,1792]{1,0:T(8,128)(2,1)S(1)}, bf16[136,1792]{1,0:T(8,128)(2,1)}, u32[]{:S(2)}, u32[]{:S(2)}) collective-permute-start(bf16[136,1792]{1,0:T(8,128)(2,1)S(1)} %get-tuple-element.40), channel_id=1, source_target_pairs={{0,2},{1,3},{2,4},{3,5},{4,6},{5,7},{6,0},{7,1},{8,10},{9,11},{10,... | collective-permute-start | bytes 1462280 | tf_op jit(solution)/shard_map/ppermute | solution.py:67
  7.6 81.0 %collective-permute-start.9 = (bf16[896,2048]{1,0:T(8,128)(2,1)}, bf16[896,2048]{1,0:T(8,128)(2,1)}, u32[]{:S(2)}, u32[]{:S(2)}) collective-permute-start(bf16[896,2048]{1,0:T(8,128)(2,1)} %bitcast.130), channel_id=1, source_target_pairs={{0,8},{1,9},{2,10},{3,11},{4,12},{5,13},{6,14},{7,15},{8,0},{9,1},... | collective-permute-start | bytes 11010056 | tf_op jit(solution)/shard_map/ppermute | solution.py:67
  17.1 15.5 %collective-permute-start.3 = (bf16[136,1792]{1,0:T(8,128)(2,1)S(1)}, bf16[136,1792]{1,0:T(8,128)(2,1)S(1)}, u32[]{:S(2)}, u32[]{:S(2)}) collective-permute-start(bf16[136,1792]{1,0:T(8,128)(2,1)S(1)} %get-tuple-element.40), channel_id=1, source_target_pairs={{0,6},{1,7},{2,0},{3,1},{4,2},{5,3},{6,4},{7,5},{8,14},{9,15},{10,... | collective-permute-start | bytes 1462280 | tf_op jit(solution)/shard_map/ppermute | solution.py:67
  21.0 43.6 %collective-permute-start.7 = (bf16[136,1792]{1,0:T(8,128)(2,1)S(1)}, bf16[136,1792]{1,0:T(8,128)(2,1)S(1)}, u32[]{:S(2)}, u32[]{:S(2)}) collective-permute-start(bf16[136,1792]{1,0:T(8,128)(2,1)S(1)} %collective-permute-done), channel_id=1, source_target_pairs={{0,6},{1,7},{2,0},{3,1},{4,2},{5,3},{6,4},{7,5},{8,14},{9,15},{10,... | collective-permute-start | bytes 1462280 | tf_op jit(solution)/shard_map/ppermute | solution.py:67
  22.6 40.3 %collective-permute-start.4 = (bf16[136,1792]{1,0:T(8,128)(2,1)S(1)}, bf16[136,1792]{1,0:T(8,128)(2,1)S(1)}, u32[]{:S(2)}, u32[]{:S(2)}) collective-permute-start(bf16[136,1792]{1,0:T(8,128)(2,1)S(1)} %collective-permute-done), channel_id=1, source_target_pairs={{0,2},{1,3},{2,4},{3,5},{4,6},{5,7},{6,0},{7,1},{8,10},{9,11},{10,... | collective-permute-start | bytes 1462280 | tf_op jit(solution)/shard_map/ppermute | solution.py:67
  24.2 38.6 %collective-permute-start.2 = (bf16[136,1792]{1,0:T(8,128)(2,1)}, bf16[136,1792]{1,0:T(8,128)(2,1)S(1)}, u32[]{:S(2)}, u32[]{:S(2)}) collective-permute-start(bf16[136,1792]{1,0:T(8,128)(2,1)} %collective-permute-done.1), channel_id=1, source_target_pairs={{0,2},{1,3},{2,4},{3,5},{4,6},{5,7},{6,0},{7,1},{8,10},{9,11},{10,... | collective-permute-start | bytes 1462280 | tf_op jit(solution)/shard_map/ppermute | solution.py:67
  32.6 40.2 %collective-permute-start.6 = (bf16[1024,896]{1,0:T(8,128)(2,1)S(1)}, bf16[1024,896]{1,0:T(8,128)(2,1)S(1)}, u32[]{:S(2)}, u32[]{:S(2)}) collective-permute-start(bf16[1024,896]{1,0:T(8,128)(2,1)S(1)} %bitcast.118), channel_id=1, source_target_pairs={{0,16},{1,17},{2,18},{3,19},{4,20},{5,21},{6,22},{7,23},{8,24},{9,... | collective-permute-start | bytes 5505032 | tf_op jit(solution)/shard_map/ppermute | solution.py:67
  62.8 14.8 %collective-permute-start.5 = (bf16[136,1792]{1,0:T(8,128)(2,1)S(1)}, bf16[136,1792]{1,0:T(8,128)(2,1)S(1)}, u32[]{:S(2)}, u32[]{:S(2)}) collective-permute-start(bf16[136,1792]{1,0:T(8,128)(2,1)S(1)} %collective-permute-done.4), channel_id=1, source_target_pairs={{0,2},{1,3},{2,4},{3,5},{4,6},{5,7},{6,0},{7,1},{8,10},{9,11},{10,... | collective-permute-start | bytes 1462280 | tf_op jit(solution)/shard_map/ppermute | solution.py:67
  78.4 3.7 %collective-permute-start.10 = (bf16[4,64,1792]{2,1,0:T(8,128)(2,1)S(1)}, bf16[4,64,1792]{2,1,0:T(8,128)(2,1)S(1)}, u32[]{:S(2)}, u32[]{:S(2)}) collective-permute-start(bf16[4,64,1792]{2,1,0:T(8,128)(2,1)S(1)} %convolution_convert_fusion), channel_id=1, source_target_pairs={{0,1},{1,0},{2,3},{3,2},{4,5},{5,4},{6,7},{7,6},{8,9},{9,8},{10,11... | collective-permute-start | bytes 2752520 | tf_op jit(solution)/shard_map/ppermute | solution.py:67
  79.2 3.1 %collective-permute-start.8 = (bf16[4,64,1792]{2,1,0:T(8,128)(2,1)S(1)}, bf16[4,64,1792]{2,1,0:T(8,128)(2,1)S(1)}, u32[]{:S(2)}, u32[]{:S(2)}) collective-permute-start(bf16[4,64,1792]{2,1,0:T(8,128)(2,1)S(1)} %convolution_convert_fusion.2), channel_id=1, source_target_pairs={{0,1},{1,0},{2,3},{3,2},{4,5},{5,4},{6,7},{7,6},{8,9},{9,8},{10,11... | collective-permute-start | bytes 2752520 | tf_op jit(solution)/shard_map/ppermute | solution.py:67
  79.7 28.2 %collective-permute-start.15 = (bf16[4,8,256]{2,1,0:T(8,128)(2,1)S(1)}, bf16[4,8,256]{2,1,0:T(8,128)(2,1)S(1)}, u32[]{:S(2)}, u32[]{:S(2)}) collective-permute-start(bf16[4,8,256]{2,1,0:T(8,128)(2,1)S(1)} %pad_maximum_fusion.16), channel_id=1, source_target_pairs={{0,8},{1,9},{2,10},{3,11},{4,12},{5,13},{6,14},{7,15},{8,0},{9,1},... | collective-permute-start | bytes 49160 | tf_op jit(solution)/shard_map/ppermute | solution.py:67
  82.1 6.5 %copy-start.2 = (bf16[1,896,2048]{2,1,0:T(8,128)(2,1)S(1)}, bf16[1,896,2048]{2,1,0:T(8,128)(2,1)}, u32[]{:S(2)}) copy-start(bf16[1,896,2048]{2,1,0:T(8,128)(2,1)} %param.6) | copy-start | bytes 11010052
  92.2 8.1 %collective-permute-start.11 = (bf16[128,1024]{1,0:T(8,128)(2,1)S(1)}, bf16[128,1024]{1,0:T(8,128)(2,1)S(1)}, u32[]{:S(2)}, u32[]{:S(2)}) collective-permute-start(bf16[128,1024]{1,0:T(8,128)(2,1)S(1)} %slice_bitcast_fusion.15), channel_id=1, source_target_pairs={{0,16},{1,17},{2,18},{3,19},{4,20},{5,21},{6,22},{7,23},{8,24},{9,... | collective-permute-start | bytes 786440 | tf_op jit(solution)/shard_map/ppermute | solution.py:67
  96.4 9.7 %collective-permute-start.12 = (bf16[128,1024]{1,0:T(8,128)(2,1)S(1)}, bf16[128,1024]{1,0:T(8,128)(2,1)S(1)}, u32[]{:S(2)}, u32[]{:S(2)}) collective-permute-start(bf16[128,1024]{1,0:T(8,128)(2,1)S(1)} %slice_bitcast_fusion.14), channel_id=1, source_target_pairs={{0,16},{1,17},{2,18},{3,19},{4,20},{5,21},{6,22},{7,23},{8,24},{9,... | collective-permute-start | bytes 786440 | tf_op jit(solution)/shard_map/ppermute | solution.py:67
  106.4 8.7 %collective-permute-start.13 = (bf16[128,1024]{1,0:T(8,128)(2,1)S(1)}, bf16[128,1024]{1,0:T(8,128)(2,1)S(1)}, u32[]{:S(2)}, u32[]{:S(2)}) collective-permute-start(bf16[128,1024]{1,0:T(8,128)(2,1)S(1)} %fusion.21), channel_id=1, source_target_pairs={{0,8},{1,9},{2,10},{3,11},{4,12},{5,13},{6,14},{7,15},{8,0},{9,1},... | collective-permute-start | bytes 786440 | tf_op jit(solution)/shard_map/ppermute | solution.py:67
  109.1 13.8 %collective-permute-start.18 = (bf16[128,2048]{1,0:T(8,128)(2,1)S(1)}, bf16[128,2048]{1,0:T(8,128)(2,1)S(1)}, u32[]{:S(2)}, u32[]{:S(2)}) collective-permute-start(bf16[128,2048]{1,0:T(8,128)(2,1)S(1)} %pad_maximum_fusion.9), channel_id=1, source_target_pairs={{0,16},{1,17},{2,18},{3,19},{4,20},{5,21},{6,22},{7,23},{8,24},{9,... | collective-permute-start | bytes 1572872 | tf_op jit(solution)/shard_map/ppermute | solution.py:67
  109.2 1.6 collective-permute-start.16
  111.1 14.6 %collective-permute-start.17 = (bf16[128,1792]{1,0:T(8,128)(2,1)S(1)}, bf16[128,1792]{1,0:T(8,128)(2,1)S(1)}, u32[]{:S(2)}, u32[]{:S(2)}) collective-permute-start(bf16[128,1792]{1,0:T(8,128)(2,1)S(1)} %convolution_convert_fusion.15), channel_id=1, source_target_pairs={{0,2},{1,3},{2,4},{3,5},{4,6},{5,7},{6,0},{7,1},{8,10},{9,11},{10,... | collective-permute-start | bytes 1376264 | tf_op jit(solution)/shard_map/ppermute | solution.py:67
  113.0 21.1 %collective-permute-start.20 = (bf16[128,2048]{1,0:T(8,128)(2,1)S(1)}, bf16[128,2048]{1,0:T(8,128)(2,1)S(1)}, u32[]{:S(2)}, u32[]{:S(2)}) collective-permute-start(bf16[128,2048]{1,0:T(8,128)(2,1)S(1)} %pad_maximum_fusion.10), channel_id=1, source_target_pairs={{0,16},{1,17},{2,18},{3,19},{4,20},{5,21},{6,22},{7,23},{8,24},{9,... | collective-permute-start | bytes 1572872 | tf_op jit(solution)/shard_map/ppermute | solution.py:67
  115.7 1.6 collective-permute-start.14
  115.9 27.4 %collective-permute-start.23 = (bf16[128,2048]{1,0:T(8,128)(2,1)S(1)}, bf16[128,2048]{1,0:T(8,128)(2,1)S(1)}, u32[]{:S(2)}, u32[]{:S(2)}) collective-permute-start(bf16[128,2048]{1,0:T(8,128)(2,1)S(1)} %pad_maximum_fusion.11), channel_id=1, source_target_pairs={{0,16},{1,17},{2,18},{3,19},{4,20},{5,21},{6,22},{7,23},{8,24},{9,... | collective-permute-start | bytes 1572872 | tf_op jit(solution)/shard_map/ppermute | solution.py:67
  125.9 8.2 %collective-permute-start.19 = (bf16[128,1024]{1,0:T(8,128)(2,1)S(1)}, bf16[128,1024]{1,0:T(8,128)(2,1)S(1)}, u32[]{:S(2)}, u32[]{:S(2)}) collective-permute-start(bf16[128,1024]{1,0:T(8,128)(2,1)S(1)} %fusion.20), channel_id=1, source_target_pairs={{0,8},{1,9},{2,10},{3,11},{4,12},{5,13},{6,14},{7,15},{8,0},{9,1},... | collective-permute-start | bytes 786440 | tf_op jit(solution)/shard_map/ppermute | solution.py:67
  127.3 1.6 collective-permute-start.27
  127.7 15.2 %collective-permute-start.30 = (bf16[128,1792]{1,0:T(8,128)(2,1)S(1)}, bf16[128,1792]{1,0:T(8,128)(2,1)S(1)}, u32[]{:S(2)}, u32[]{:S(2)}) collective-permute-start(bf16[128,1792]{1,0:T(8,128)(2,1)S(1)} %convolution_convert_fusion.13), channel_id=1, source_target_pairs={{0,2},{1,3},{2,4},{3,5},{4,6},{5,7},{6,0},{7,1},{8,10},{9,11},{10,... | collective-permute-start | bytes 1376264 | tf_op jit(solution)/shard_map/ppermute | solution.py:67
  129.1 26.1 %collective-permute-start.28 = (bf16[128,1792]{1,0:T(8,128)(2,1)S(1)}, bf16[128,1792]{1,0:T(8,128)(2,1)S(1)}, u32[]{:S(2)}, u32[]{:S(2)}) collective-permute-start(bf16[128,1792]{1,0:T(8,128)(2,1)S(1)} %convolution_convert_fusion.14), channel_id=1, source_target_pairs={{0,6},{1,7},{2,0},{3,1},{4,2},{5,3},{6,4},{7,5},{8,14},{9,15},{10,... | collective-permute-start | bytes 1376264 | tf_op jit(solution)/shard_map/ppermute | solution.py:67
  134.4 8.8 %collective-permute-start.22 = (bf16[128,1024]{1,0:T(8,128)(2,1)S(1)}, bf16[128,1024]{1,0:T(8,128)(2,1)S(1)}, u32[]{:S(2)}, u32[]{:S(2)}) collective-permute-start(bf16[128,1024]{1,0:T(8,128)(2,1)S(1)} %fusion.19), channel_id=1, source_target_pairs={{0,8},{1,9},{2,10},{3,11},{4,12},{5,13},{6,14},{7,15},{8,0},{9,1},... | collective-permute-start | bytes 786440 | tf_op jit(solution)/shard_map/ppermute | solution.py:67
  136.4 6.5 %collective-permute-start.29 = (bf16[64,1792]{1,0:T(8,128)(2,1)S(1)}, bf16[64,1792]{1,0:T(8,128)(2,1)S(1)}, u32[]{:S(2)}, u32[]{:S(2)}) collective-permute-start(bf16[64,1792]{1,0:T(8,128)(2,1)S(1)} %get-tuple-element.94), channel_id=1, source_target_pairs={{0,1},{1,0},{2,3},{3,2},{4,5},{5,4},{6,7},{7,6},{8,9},{9,8},{10,11... | collective-permute-start | bytes 688136 | tf_op jit(solution)/shard_map/ppermute | solution.py:67
  142.9 21.3 %collective-permute-start.21 = (bf16[64,1792]{1,0:T(8,128)(2,1)S(1)}, bf16[64,1792]{1,0:T(8,128)(2,1)S(1)}, u32[]{:S(2)}, u32[]{:S(2)}) collective-permute-start(bf16[64,1792]{1,0:T(8,128)(2,1)S(1)} %get-tuple-element.92), channel_id=1, source_target_pairs={{0,1},{1,0},{2,3},{3,2},{4,5},{5,4},{6,7},{7,6},{8,9},{9,8},{10,11... | collective-permute-start | bytes 688136 | tf_op jit(solution)/shard_map/ppermute | solution.py:67
  143.2 18.2 %collective-permute-start.31 = (bf16[128,1792]{1,0:T(8,128)(2,1)S(1)}, bf16[128,1792]{1,0:T(8,128)(2,1)S(1)}, u32[]{:S(2)}, u32[]{:S(2)}) collective-permute-start(bf16[128,1792]{1,0:T(8,128)(2,1)S(1)} %convolution_convert_fusion.12), channel_id=1, source_target_pairs={{0,6},{1,7},{2,0},{3,1},{4,2},{5,3},{6,4},{7,5},{8,14},{9,15},{10,... | collective-permute-start | bytes 1376264 | tf_op jit(solution)/shard_map/ppermute | solution.py:67
  143.6 8.8 %collective-permute-start.25 = (bf16[128,1024]{1,0:T(8,128)(2,1)S(1)}, bf16[128,1024]{1,0:T(8,128)(2,1)S(1)}, u32[]{:S(2)}, u32[]{:S(2)}) collective-permute-start(bf16[128,1024]{1,0:T(8,128)(2,1)S(1)} %fusion.18), channel_id=1, source_target_pairs={{0,8},{1,9},{2,10},{3,11},{4,12},{5,13},{6,14},{7,15},{8,0},{9,1},... | collective-permute-start | bytes 786440 | tf_op jit(solution)/shard_map/ppermute | solution.py:67
  146.5 1.6 collective-permute-start.24
  148.1 5.1 %collective-permute-start.32 = (bf16[64,1792]{1,0:T(8,128)(2,1)S(1)}, bf16[64,1792]{1,0:T(8,128)(2,1)S(1)}, u32[]{:S(2)}, u32[]{:S(2)}) collective-permute-start(bf16[64,1792]{1,0:T(8,128)(2,1)S(1)} %get-tuple-element.100), channel_id=1, source_target_pairs={{0,1},{1,0},{2,3},{3,2},{4,5},{5,4},{6,7},{7,6},{8,9},{9,8},{10,11... | collective-permute-start | bytes 688136 | tf_op jit(solution)/shard_map/ppermute | solution.py:67
  153.1 8.3 %collective-permute-start.26 = (bf16[64,1792]{1,0:T(8,128)(2,1)S(1)}, bf16[64,1792]{1,0:T(8,128)(2,1)S(1)}, u32[]{:S(2)}, u32[]{:S(2)}) collective-permute-start(bf16[64,1792]{1,0:T(8,128)(2,1)S(1)} %get-tuple-element.90), channel_id=1, source_target_pairs={{0,1},{1,0},{2,3},{3,2},{4,5},{5,4},{6,7},{7,6},{8,9},{9,8},{10,11... | collective-permute-start | bytes 688136 | tf_op jit(solution)/shard_map/ppermute | solution.py:67
  153.5 18.9 %collective-permute-start.33 = (bf16[128,1792]{1,0:T(8,128)(2,1)S(1)}, bf16[128,1792]{1,0:T(8,128)(2,1)S(1)}, u32[]{:S(2)}, u32[]{:S(2)}) collective-permute-start(bf16[128,1792]{1,0:T(8,128)(2,1)S(1)} %fusion.11), channel_id=1, source_target_pairs={{0,2},{1,3},{2,4},{3,5},{4,6},{5,7},{6,0},{7,1},{8,10},{9,11},{10,... | collective-permute-start | bytes 1376264 | tf_op jit(solution)/shard_map/ppermute | solution.py:67
  161.7 21.7 %collective-permute-start.34 = (bf16[128,1792]{1,0:T(8,128)(2,1)S(1)}, bf16[128,1792]{1,0:T(8,128)(2,1)S(1)}, u32[]{:S(2)}, u32[]{:S(2)}) collective-permute-start(bf16[128,1792]{1,0:T(8,128)(2,1)S(1)} %add_convert_fusion.2), channel_id=1, source_target_pairs={{0,8},{1,9},{2,10},{3,11},{4,12},{5,13},{6,14},{7,15},{8,0},{9,1},... | collective-permute-start | bytes 1376264 | tf_op jit(solution)/shard_map/ppermute | solution.py:67
  163.6 19.8 %collective-permute-start.35 = (bf16[128,1792]{1,0:T(8,128)(2,1)S(1)}, bf16[128,1792]{1,0:T(8,128)(2,1)S(1)}, u32[]{:S(2)}, u32[]{:S(2)}) collective-permute-start(bf16[128,1792]{1,0:T(8,128)(2,1)S(1)} %add_convert_fusion.1), channel_id=1, source_target_pairs={{0,10},{1,11},{2,12},{3,13},{4,14},{5,15},{6,8},{7,9},{8,2},{9,3},... | collective-permute-start | bytes 1376264 | tf_op jit(solution)/shard_map/ppermute | solution.py:67
  183.6 0.9 copy-start.1

commit v14 on v13

--- a/solution.py
+++ b/solution.py
@@ -177,16 +177,13 @@
     finish(0)
     hidden[0, 0], info_x = together((hidden[0, 0], info_x))
     down_product(0, 0)
-    out[0, 0], gates, ups = together((out[0, 0], gates, ups))
-
-    def whole(q):
-        return jnp.concatenate([gates[order[q]], ups[order[q]]], axis=1)
-
-    part.append(send(whole(1), flip=2))
     pays.append(places(info_x)[1])
     middle[0] = weigh(0, 0).astype(BF)
-    middle[0], gates, ups = together((middle[0], gates, ups))
-    part += [send(whole(q), flip=2) for q in range(2, chips)]
+    hidden[0, 1], gates, ups = together((hidden[0, 1], gates, ups))
+    part += [
+        send(jnp.concatenate([gates[order[q]], ups[order[q]]], axis=1), flip=2)
+        for q in range(1, chips)
+    ]
     middle[0] = send(middle[0], 1)
     down_product(0, 1)
     middle[0], part[1] = before_weigh(0, (middle[0], part[1]))

time: 186 us -> 201 us (1.081)
  starting transfers between devices: 35.6 us -> 49.7 us
    ppermute x36, starting transfers between devices: 35.6 us -> 49.7 us  [send(): lax.ppermute(value, ('dp', 'expert'), [(i * owners + j, (i ^ flip) * owne...]
  transfers between devices with their start and end apart: 36 -> 36, of which waited for: 19 -> 19; matrix products, arithmetic and copies ran while one was open for 15% -> 14% of each run, Pallas kernels for 0% -> 0%
where the time goes in v14:
time: 201 us; the launch traced here: 200 us
  waiting for transfers between devices  117 us (58%)
  starting transfers between devices  49.7 us (25%)
  matrix products  22.9 us (11%)
  local copies, waits for them, and re-layouts  5.63 us (3%)
  other arithmetic  4 us (2%)
    ppermute x36, waiting for transfers between devices, send(): lax.ppermute(value, ('dp', 'expert'), [(i * owners + j, (i ^ flip) * owne...  117 us
    ppermute x36, starting transfers between devices, send(): lax.ppermute(value, ('dp', 'expert'), [(i * owners + j, (i ^ flip) * owne...  49.7 us
    dot_general x3, matrix products, product(): jnp.dot(flat, weights[:, lo:hi], preferred_element_type=F32)  12.9 us
    dot_general x8, matrix products, down_product(): value = jnp.dot(hidden[q, g], downs, preferred_element_type=F32).astype(BF)  5.24 us
  transfers between devices with their start and end apart: 36, of which 19 were waited for; matrix products, arithmetic and copies ran while one was open for 14% of the time, Pallas kernels for 0%

profile of v14, /device:TPU:0, one launch (start us, length us, event | category | flops | bytes accessed | tf_op | source)
XLA Modules:
  0.0 200.5 jit_solution(1703593302604750879)
XLA Ops:
  0.0 0.8 convert_bitcast_fusion
  0.8 0.7 fusion.62
  1.5 1.4 constant_dynamic-slice_fusion.1
  3.0 3.0 %collective-permute-start = (bf16[136,1792]{1,0:T(8,128)(2,1)S(1)}, bf16[136,1792]{1,0:T(8,128)(2,1)S(1)}, u32[]{:S(2)}, u32[]{:S(2)}) collective-permute-start(bf16[136,1792]{1,0:T(8,128)(2,1)S(1)} %get-tuple-element.107), channel_id=1, source_target_pairs={{0,16},{1,17},{2,18},{3,19},{4,20},{5,21},{6,22},{7,23},{8,24},{9,... | collective-permute-start | bytes 1462280 | tf_op jit(solution)/shard_map/ppermute | solution.py:67
  6.0 1.6 collective-permute-start.1
  7.6 1.5 collective-permute-start.9
  9.1 8.0 %collective-permute-done = bf16[136,1792]{1,0:T(8,128)(2,1)S(1)} collective-permute-done((bf16[136,1792]{1,0:T(8,128)(2,1)S(1)}, bf16[136,1792]{1,0:T(8,128)(2,1)S(1)}, u32[]{:S(2)}, u32[]{:S(2)}) %collective-permute-start) | collective-permute-done | bytes 487456 | tf_op jit(solution)/shard_map/ppermute | solution.py:67
  17.1 3.8 %collective-permute-start.3 = (bf16[136,1792]{1,0:T(8,128)(2,1)S(1)}, bf16[136,1792]{1,0:T(8,128)(2,1)S(1)}, u32[]{:S(2)}, u32[]{:S(2)}) collective-permute-start(bf16[136,1792]{1,0:T(8,128)(2,1)S(1)} %get-tuple-element.37), channel_id=1, source_target_pairs={{0,6},{1,7},{2,0},{3,1},{4,2},{5,3},{6,4},{7,5},{8,14},{9,15},{10,... | collective-permute-start | bytes 1462280 | tf_op jit(solution)/shard_map/ppermute | solution.py:67
  21.0 0.5 collective-permute-start.7
  21.5 1.0 slice_bitcast_fusion.2
  22.6 1.6 collective-permute-start.4
  24.3 0.7 slice_bitcast_fusion.28
  25.0 7.6 %collective-permute-done.3 = bf16[136,1792]{1,0:T(8,128)(2,1)S(1)} collective-permute-done((bf16[136,1792]{1,0:T(8,128)(2,1)S(1)}, bf16[136,1792]{1,0:T(8,128)(2,1)S(1)}, u32[]{:S(2)}, u32[]{:S(2)}) %collective-permute-start.3) | collective-permute-done | bytes 487456 | tf_op jit(solution)/shard_map/ppermute | solution.py:67
  32.6 1.6 collective-permute-start.6
  34.1 28.7 %collective-permute-done.2 = bf16[136,1792]{1,0:T(8,128)(2,1)S(1)} collective-permute-done((bf16[136,1792]{1,0:T(8,128)(2,1)}, bf16[136,1792]{1,0:T(8,128)(2,1)S(1)}, u32[]{:S(2)}, u32[]{:S(2)}) %collective-permute-start.2) | collective-permute-done | bytes 487456 | tf_op jit(solution)/shard_map/ppermute | solution.py:67
  62.8 1.7 collective-permute-start.5
  64.7 8.1 %collective-permute-done.6 = bf16[1024,896]{1,0:T(8,128)(2,1)S(1)} collective-permute-done((bf16[1024,896]{1,0:T(8,128)(2,1)S(1)}, bf16[1024,896]{1,0:T(8,128)(2,1)S(1)}, u32[]{:S(2)}, u32[]{:S(2)}) %collective-permute-start.6) | collective-permute-done | bytes 1835040 | tf_op jit(solution)/shard_map/ppermute | solution.py:67
  73.0 4.6 %collective-permute-done.5 = bf16[136,1792]{1,0:T(8,128)(2,1)S(1)} collective-permute-done((bf16[136,1792]{1,0:T(8,128)(2,1)S(1)}, bf16[136,1792]{1,0:T(8,128)(2,1)S(1)}, u32[]{:S(2)}, u32[]{:S(2)}) %collective-permute-start.5) | collective-permute-done | bytes 487456 | tf_op jit(solution)/shard_map/ppermute | solution.py:67
  78.0 0.4 convolution_convert_fusion
  78.7 0.4 convolution_convert_fusion.2
  79.2 0.6 collective-permute-start.8
  79.7 1.5 collective-permute-start.15
  81.2 0.4 convolution_convert_fusion.1
  81.7 0.4 convolution_convert_fusion.3
  82.4 6.2 %collective-permute-done.9 = bf16[896,2048]{1,0:T(8,128)(2,1)} collective-permute-done((bf16[896,2048]{1,0:T(8,128)(2,1)}, bf16[896,2048]{1,0:T(8,128)(2,1)}, u32[]{:S(2)}, u32[]{:S(2)}) %collective-permute-start.9) | collective-permute-done | bytes 3670048 | tf_op jit(solution)/shard_map/ppermute | solution.py:67
  88.6 3.6 %fusion.15 = bf16[4,128,1024]{2,1,0:T(8,128)(2,1)S(1)} fusion(bf16[4,128,1792]{2,1,0:T(8,128)(2,1)S(1)} %pad_maximum_fusion.4, bf16[896,2048]{1,0:T(8,128)(2,1)S(1)} %bitcast.131, bf16[896,2048]{1,0:T(8,128)(2,1)} %collective-permute-done.9), kind=kOutput, calls=%fused_computation.39 | convolution fusion | flops 1886912512 | bytes 10223616 | tf_op jit(solution)/shard_map/dot_general | solution.py:134
  92.2 0.6 collective-permute-start.11
  92.8 3.6 %fusion.12 = bf16[4,128,1024]{2,1,0:T(8,128)(2,1)S(1)} fusion(bf16[4,128,1792]{2,1,0:T(8,128)(2,1)S(1)} %pad_maximum_fusion.4, bf16[896,2048]{1,0:T(8,128)(2,1)S(1)} %bitcast.132, bf16[896,2048]{1,0:T(8,128)(2,1)} %collective-permute-done.9), kind=kOutput, calls=%fused_computation.38 | convolution fusion | flops 1886912512 | bytes 10223616 | tf_op jit(solution)/shard_map/dot_general | solution.py:134
  96.4 1.6 collective-permute-start.12
  98.0 2.4 %collective-permute-done.11 = bf16[128,1024]{1,0:T(8,128)(2,1)S(1)} collective-permute-done((bf16[128,1024]{1,0:T(8,128)(2,1)S(1)}, bf16[128,1024]{1,0:T(8,128)(2,1)S(1)}, u32[]{:S(2)}, u32[]{:S(2)}) %collective-permute-start.11) | collective-permute-done | bytes 262176 | tf_op jit(solution)/shard_map/ppermute | solution.py:67
  100.3 5.7 %fusion = f32[512,2048]{1,0:T(8,128)S(1)} fusion(bf16[512,1792]{1,0:T(8,128)(2,1)S(1)} %bitcast.120, bf16[896,2048]{1,0:T(8,128)(2,1)} %collective-permute-done.9, bf16[896,2048]{1,0:T(8,128)(2,1)S(1)} %bitcast.133), kind=kOutput, calls=%fused_computation.5 | convolution fusion | flops 3772776448 | bytes 13369344 | tf_op jit(solution)/shard_map/dot_general | solution.py:134
  106.4 1.6 collective-permute-start.13
  108.3 0.7 convolution_convert_fusion.10
  109.2 1.4 collective-permute-done.16
  110.9 1.8 collective-permute-start.17
  113.1 0.7 convolution_convert_fusion.11
  113.9 2.1 %collective-permute-start.20 = (bf16[128,2048]{1,0:T(8,128)(2,1)S(1)}, bf16[128,2048]{1,0:T(8,128)(2,1)S(1)}, u32[]{:S(2)}, u32[]{:S(2)}) collective-permute-start(bf16[128,2048]{1,0:T(8,128)(2,1)S(1)} %pad_maximum_fusion.10), channel_id=1, source_target_pairs={{0,16},{1,17},{2,18},{3,19},{4,20},{5,21},{6,22},{7,23},{8,24},{9,... | collective-permute-start | bytes 1572872 | tf_op jit(solution)/shard_map/ppermute | solution.py:67
  116.1 9.4 %collective-permute-done.17 = bf16[128,1792]{1,0:T(8,128)(2,1)S(1)} collective-permute-done((bf16[128,1792]{1,0:T(8,128)(2,1)S(1)}, bf16[128,1792]{1,0:T(8,128)(2,1)S(1)}, u32[]{:S(2)}, u32[]{:S(2)}) %collective-permute-start.17) | collective-permute-done | bytes 458784 | tf_op jit(solution)/shard_map/ppermute | solution.py:67
  125.5 2.4 %collective-permute-done.18 = bf16[128,2048]{1,0:T(8,128)(2,1)S(1)} collective-permute-done((bf16[128,2048]{1,0:T(8,128)(2,1)S(1)}, bf16[128,2048]{1,0:T(8,128)(2,1)S(1)}, u32[]{:S(2)}, u32[]{:S(2)}) %collective-permute-start.18) | collective-permute-done | bytes 524320 | tf_op jit(solution)/shard_map/ppermute | solution.py:67
  128.2 1.6 collective-permute-start.19
  129.8 0.7 convolution_convert_fusion.6
  130.9 1.6 collective-permute-start.30
  132.8 2.3 %collective-permute-start.28 = (bf16[128,1792]{1,0:T(8,128)(2,1)S(1)}, bf16[128,1792]{1,0:T(8,128)(2,1)S(1)}, u32[]{:S(2)}, u32[]{:S(2)}) collective-permute-start(bf16[128,1792]{1,0:T(8,128)(2,1)S(1)} %convolution_convert_fusion.14), channel_id=1, source_target_pairs={{0,6},{1,7},{2,0},{3,1},{4,2},{5,3},{6,4},{7,5},{8,14},{9,15},{10,... | collective-permute-start | bytes 1376264 | tf_op jit(solution)/shard_map/ppermute | solution.py:67
  135.2 4.0 %collective-permute-done.20 = bf16[128,2048]{1,0:T(8,128)(2,1)S(1)} collective-permute-done((bf16[128,2048]{1,0:T(8,128)(2,1)S(1)}, bf16[128,2048]{1,0:T(8,128)(2,1)S(1)}, u32[]{:S(2)}, u32[]{:S(2)}) %collective-permute-start.20) | collective-permute-done | bytes 524320 | tf_op jit(solution)/shard_map/ppermute | solution.py:67
  139.4 1.6 collective-permute-start.22
  141.0 0.7 convolution_convert_fusion.9
  141.7 0.7 convolution_convert_fusion.5
  142.5 3.6 %collective-permute-done.30 = bf16[128,1792]{1,0:T(8,128)(2,1)S(1)} collective-permute-done((bf16[128,1792]{1,0:T(8,128)(2,1)S(1)}, bf16[128,1792]{1,0:T(8,128)(2,1)S(1)}, u32[]{:S(2)}, u32[]{:S(2)}) %collective-permute-start.30) | collective-permute-done | bytes 458784 | tf_op jit(solution)/shard_map/ppermute | solution.py:67
  146.7 2.5 %collective-permute-done.23 = bf16[128,2048]{1,0:T(8,128)(2,1)S(1)} collective-permute-done((bf16[128,2048]{1,0:T(8,128)(2,1)S(1)}, bf16[128,2048]{1,0:T(8,128)(2,1)S(1)}, u32[]{:S(2)}, u32[]{:S(2)}) %collective-permute-start.23) | collective-permute-done | bytes 524320 | tf_op jit(solution)/shard_map/ppermute | solution.py:67
  149.5 0.6 collective-permute-start.25
  150.1 0.7 convolution_convert_fusion.4
  150.7 0.7 convolution_convert_fusion.8
  151.5 1.4 collective-permute-done.24
  153.1 3.5 %collective-permute-done.25 = bf16[128,1024]{1,0:T(8,128)(2,1)S(1)} collective-permute-done((bf16[128,1024]{1,0:T(8,128)(2,1)S(1)}, bf16[128,1024]{1,0:T(8,128)(2,1)S(1)}, u32[]{:S(2)}, u32[]{:S(2)}) %collective-permute-start.25) | collective-permute-done | bytes 262176 | tf_op jit(solution)/shard_map/ppermute | solution.py:67
  156.6 0.7 convolution_convert_fusion.7
  157.8 1.6 collective-permute-start.33
  159.4 5.8 %collective-permute-done.31 = bf16[128,1792]{1,0:T(8,128)(2,1)S(1)} collective-permute-done((bf16[128,1792]{1,0:T(8,128)(2,1)S(1)}, bf16[128,1792]{1,0:T(8,128)(2,1)S(1)}, u32[]{:S(2)}, u32[]{:S(2)}) %collective-permute-start.31) | collective-permute-done | bytes 458784 | tf_op jit(solution)/shard_map/ppermute | solution.py:67
  165.5 0.6 collective-permute-start.34
  166.4 13.7 %collective-permute-start.35 = (bf16[128,1792]{1,0:T(8,128)(2,1)S(1)}, bf16[128,1792]{1,0:T(8,128)(2,1)S(1)}, u32[]{:S(2)}, u32[]{:S(2)}) collective-permute-start(bf16[128,1792]{1,0:T(8,128)(2,1)S(1)} %add_convert_fusion.1), channel_id=1, source_target_pairs={{0,10},{1,11},{2,12},{3,13},{4,14},{5,15},{6,8},{7,9},{8,2},{9,3},... | collective-permute-start | bytes 1376264 | tf_op jit(solution)/shard_map/ppermute | solution.py:67
  180.2 8.8 %collective-permute-done.33 = bf16[128,1792]{1,0:T(8,128)(2,1)S(1)} collective-permute-done((bf16[128,1792]{1,0:T(8,128)(2,1)S(1)}, bf16[128,1792]{1,0:T(8,128)(2,1)S(1)}, u32[]{:S(2)}, u32[]{:S(2)}) %collective-permute-start.33) | collective-permute-done | bytes 458784 | tf_op jit(solution)/shard_map/ppermute | solution.py:67
  189.0 0.3 fusion.10
  189.5 9.2 %collective-permute-done.35 = bf16[128,1792]{1,0:T(8,128)(2,1)S(1)} collective-permute-done((bf16[128,1792]{1,0:T(8,128)(2,1)S(1)}, bf16[128,1792]{1,0:T(8,128)(2,1)S(1)}, u32[]{:S(2)}, u32[]{:S(2)}) %collective-permute-start.35) | collective-permute-done | bytes 458784 | tf_op jit(solution)/shard_map/ppermute | solution.py:67
  198.8 0.9 copy-done.1
  199.7 0.7 slice_dynamic-update-slice_fusion
  (107 shorter events, 7.3 us)
Async XLA Ops:
  0.0 32.6 %copy-start = (bf16[1,1024,896]{2,1,0:T(8,128)(2,1)S(1)}, bf16[1,1024,896]{2,1,0:T(8,128)(2,1)}, u32[]{:S(2)}) copy-start(bf16[1,1024,896]{2,1,0:T(8,128)(2,1)} %param.7) | copy-start | bytes 5505028
  3.0 14.2 %collective-permute-start = (bf16[136,1792]{1,0:T(8,128)(2,1)S(1)}, bf16[136,1792]{1,0:T(8,128)(2,1)S(1)}, u32[]{:S(2)}, u32[]{:S(2)}) collective-permute-start(bf16[136,1792]{1,0:T(8,128)(2,1)S(1)} %get-tuple-element.107), channel_id=1, source_target_pairs={{0,16},{1,17},{2,18},{3,19},{4,20},{5,21},{6,22},{7,23},{8,24},{9,... | collective-permute-start | bytes 1462280 | tf_op jit(solution)/shard_map/ppermute | solution.py:67
  6.0 15.5 %collective-permute-start.1 = (bf16[136,1792]{1,0:T(8,128)(2,1)S(1)}, bf16[136,1792]{1,0:T(8,128)(2,1)}, u32[]{:S(2)}, u32[]{:S(2)}) collective-permute-start(bf16[136,1792]{1,0:T(8,128)(2,1)S(1)} %get-tuple-element.37), channel_id=1, source_target_pairs={{0,2},{1,3},{2,4},{3,5},{4,6},{5,7},{6,0},{7,1},{8,10},{9,11},{10,... | collective-permute-start | bytes 1462280 | tf_op jit(solution)/shard_map/ppermute | solution.py:67
  7.6 81.0 %collective-permute-start.9 = (bf16[896,2048]{1,0:T(8,128)(2,1)}, bf16[896,2048]{1,0:T(8,128)(2,1)}, u32[]{:S(2)}, u32[]{:S(2)}) collective-permute-start(bf16[896,2048]{1,0:T(8,128)(2,1)} %bitcast.130), channel_id=1, source_target_pairs={{0,8},{1,9},{2,10},{3,11},{4,12},{5,13},{6,14},{7,15},{8,0},{9,1},... | collective-permute-start | bytes 11010056 | tf_op jit(solution)/shard_map/ppermute | solution.py:67
  17.1 15.5 %collective-permute-start.3 = (bf16[136,1792]{1,0:T(8,128)(2,1)S(1)}, bf16[136,1792]{1,0:T(8,128)(2,1)S(1)}, u32[]{:S(2)}, u32[]{:S(2)}) collective-permute-start(bf16[136,1792]{1,0:T(8,128)(2,1)S(1)} %get-tuple-element.37), channel_id=1, source_target_pairs={{0,6},{1,7},{2,0},{3,1},{4,2},{5,3},{6,4},{7,5},{8,14},{9,15},{10,... | collective-permute-start | bytes 1462280 | tf_op jit(solution)/shard_map/ppermute | solution.py:67
  21.0 43.6 %collective-permute-start.7 = (bf16[136,1792]{1,0:T(8,128)(2,1)S(1)}, bf16[136,1792]{1,0:T(8,128)(2,1)S(1)}, u32[]{:S(2)}, u32[]{:S(2)}) collective-permute-start(bf16[136,1792]{1,0:T(8,128)(2,1)S(1)} %collective-permute-done), channel_id=1, source_target_pairs={{0,6},{1,7},{2,0},{3,1},{4,2},{5,3},{6,4},{7,5},{8,14},{9,15},{10,... | collective-permute-start | bytes 1462280 | tf_op jit(solution)/shard_map/ppermute | solution.py:67
  22.6 40.3 %collective-permute-start.4 = (bf16[136,1792]{1,0:T(8,128)(2,1)S(1)}, bf16[136,1792]{1,0:T(8,128)(2,1)S(1)}, u32[]{:S(2)}, u32[]{:S(2)}) collective-permute-start(bf16[136,1792]{1,0:T(8,128)(2,1)S(1)} %collective-permute-done), channel_id=1, source_target_pairs={{0,2},{1,3},{2,4},{3,5},{4,6},{5,7},{6,0},{7,1},{8,10},{9,11},{10,... | collective-permute-start | bytes 1462280 | tf_op jit(solution)/shard_map/ppermute | solution.py:67
  24.2 38.6 %collective-permute-start.2 = (bf16[136,1792]{1,0:T(8,128)(2,1)}, bf16[136,1792]{1,0:T(8,128)(2,1)S(1)}, u32[]{:S(2)}, u32[]{:S(2)}) collective-permute-start(bf16[136,1792]{1,0:T(8,128)(2,1)} %collective-permute-done.1), channel_id=1, source_target_pairs={{0,2},{1,3},{2,4},{3,5},{4,6},{5,7},{6,0},{7,1},{8,10},{9,11},{10,... | collective-permute-start | bytes 1462280 | tf_op jit(solution)/shard_map/ppermute | solution.py:67
  32.6 40.2 %collective-permute-start.6 = (bf16[1024,896]{1,0:T(8,128)(2,1)S(1)}, bf16[1024,896]{1,0:T(8,128)(2,1)S(1)}, u32[]{:S(2)}, u32[]{:S(2)}) collective-permute-start(bf16[1024,896]{1,0:T(8,128)(2,1)S(1)} %bitcast.118), channel_id=1, source_target_pairs={{0,16},{1,17},{2,18},{3,19},{4,20},{5,21},{6,22},{7,23},{8,24},{9,... | collective-permute-start | bytes 5505032 | tf_op jit(solution)/shard_map/ppermute | solution.py:67
  62.8 14.8 %collective-permute-start.5 = (bf16[136,1792]{1,0:T(8,128)(2,1)S(1)}, bf16[136,1792]{1,0:T(8,128)(2,1)S(1)}, u32[]{:S(2)}, u32[]{:S(2)}) collective-permute-start(bf16[136,1792]{1,0:T(8,128)(2,1)S(1)} %collective-permute-done.4), channel_id=1, source_target_pairs={{0,2},{1,3},{2,4},{3,5},{4,6},{5,7},{6,0},{7,1},{8,10},{9,11},{10,... | collective-permute-start | bytes 1462280 | tf_op jit(solution)/shard_map/ppermute | solution.py:67
  78.4 3.7 %collective-permute-start.10 = (bf16[4,64,1792]{2,1,0:T(8,128)(2,1)S(1)}, bf16[4,64,1792]{2,1,0:T(8,128)(2,1)S(1)}, u32[]{:S(2)}, u32[]{:S(2)}) collective-permute-start(bf16[4,64,1792]{2,1,0:T(8,128)(2,1)S(1)} %convolution_convert_fusion), channel_id=1, source_target_pairs={{0,1},{1,0},{2,3},{3,2},{4,5},{5,4},{6,7},{7,6},{8,9},{9,8},{10,11... | collective-permute-start | bytes 2752520 | tf_op jit(solution)/shard_map/ppermute | solution.py:67
  79.2 3.1 %collective-permute-start.8 = (bf16[4,64,1792]{2,1,0:T(8,128)(2,1)S(1)}, bf16[4,64,1792]{2,1,0:T(8,128)(2,1)S(1)}, u32[]{:S(2)}, u32[]{:S(2)}) collective-permute-start(bf16[4,64,1792]{2,1,0:T(8,128)(2,1)S(1)} %convolution_convert_fusion.2), channel_id=1, source_target_pairs={{0,1},{1,0},{2,3},{3,2},{4,5},{5,4},{6,7},{7,6},{8,9},{9,8},{10,11... | collective-permute-start | bytes 2752520 | tf_op jit(solution)/shard_map/ppermute | solution.py:67
  79.7 28.2 %collective-permute-start.15 = (bf16[4,8,256]{2,1,0:T(8,128)(2,1)S(1)}, bf16[4,8,256]{2,1,0:T(8,128)(2,1)S(1)}, u32[]{:S(2)}, u32[]{:S(2)}) collective-permute-start(bf16[4,8,256]{2,1,0:T(8,128)(2,1)S(1)} %pad_maximum_fusion.16), channel_id=1, source_target_pairs={{0,8},{1,9},{2,10},{3,11},{4,12},{5,13},{6,14},{7,15},{8,0},{9,1},... | collective-permute-start | bytes 49160 | tf_op jit(solution)/shard_map/ppermute | solution.py:67
  82.1 6.5 %copy-start.2 = (bf16[1,896,2048]{2,1,0:T(8,128)(2,1)S(1)}, bf16[1,896,2048]{2,1,0:T(8,128)(2,1)}, u32[]{:S(2)}) copy-start(bf16[1,896,2048]{2,1,0:T(8,128)(2,1)} %param.6) | copy-start | bytes 11010052
  92.2 8.1 %collective-permute-start.11 = (bf16[128,1024]{1,0:T(8,128)(2,1)S(1)}, bf16[128,1024]{1,0:T(8,128)(2,1)S(1)}, u32[]{:S(2)}, u32[]{:S(2)}) collective-permute-start(bf16[128,1024]{1,0:T(8,128)(2,1)S(1)} %slice_bitcast_fusion.15), channel_id=1, source_target_pairs={{0,16},{1,17},{2,18},{3,19},{4,20},{5,21},{6,22},{7,23},{8,24},{9,... | collective-permute-start | bytes 786440 | tf_op jit(solution)/shard_map/ppermute | solution.py:67
  96.4 9.7 %collective-permute-start.12 = (bf16[128,1024]{1,0:T(8,128)(2,1)S(1)}, bf16[128,1024]{1,0:T(8,128)(2,1)S(1)}, u32[]{:S(2)}, u32[]{:S(2)}) collective-permute-start(bf16[128,1024]{1,0:T(8,128)(2,1)S(1)} %slice_bitcast_fusion.14), channel_id=1, source_target_pairs={{0,16},{1,17},{2,18},{3,19},{4,20},{5,21},{6,22},{7,23},{8,24},{9,... | collective-permute-start | bytes 786440 | tf_op jit(solution)/shard_map/ppermute | solution.py:67
  106.4 6.4 %collective-permute-start.13 = (bf16[128,1024]{1,0:T(8,128)(2,1)S(1)}, bf16[128,1024]{1,0:T(8,128)(2,1)S(1)}, u32[]{:S(2)}, u32[]{:S(2)}) collective-permute-start(bf16[128,1024]{1,0:T(8,128)(2,1)S(1)} %fusion.21), channel_id=1, source_target_pairs={{0,8},{1,9},{2,10},{3,11},{4,12},{5,13},{6,14},{7,15},{8,0},{9,1},... | collective-permute-start | bytes 786440 | tf_op jit(solution)/shard_map/ppermute | solution.py:67
  109.0 1.6 collective-permute-start.16
  110.9 14.6 %collective-permute-start.17 = (bf16[128,1792]{1,0:T(8,128)(2,1)S(1)}, bf16[128,1792]{1,0:T(8,128)(2,1)S(1)}, u32[]{:S(2)}, u32[]{:S(2)}) collective-permute-start(bf16[128,1792]{1,0:T(8,128)(2,1)S(1)} %convolution_convert_fusion.15), channel_id=1, source_target_pairs={{0,2},{1,3},{2,4},{3,5},{4,6},{5,7},{6,0},{7,1},{8,10},{9,11},{10,... | collective-permute-start | bytes 1376264 | tf_op jit(solution)/shard_map/ppermute | solution.py:67
  113.0 14.9 %collective-permute-start.18 = (bf16[128,2048]{1,0:T(8,128)(2,1)S(1)}, bf16[128,2048]{1,0:T(8,128)(2,1)S(1)}, u32[]{:S(2)}, u32[]{:S(2)}) collective-permute-start(bf16[128,2048]{1,0:T(8,128)(2,1)S(1)} %pad_maximum_fusion.9), channel_id=1, source_target_pairs={{0,16},{1,17},{2,18},{3,19},{4,20},{5,21},{6,22},{7,23},{8,24},{9,... | collective-permute-start | bytes 1572872 | tf_op jit(solution)/shard_map/ppermute | solution.py:67
  113.8 2.3 %collective-permute-start.14 = (bf16[64,1792]{1,0:T(8,128)(2,1)S(1)}, bf16[64,1792]{1,0:T(8,128)(2,1)S(1)}, u32[]{:S(2)}, u32[]{:S(2)}) collective-permute-start(bf16[64,1792]{1,0:T(8,128)(2,1)S(1)} %get-tuple-element.92), channel_id=1, source_target_pairs={{0,1},{1,0},{2,3},{3,2},{4,5},{5,4},{6,7},{7,6},{8,9},{9,8},{10,11... | collective-permute-start | bytes 688136 | tf_op jit(solution)/shard_map/ppermute | solution.py:67
  113.9 25.2 %collective-permute-start.20 = (bf16[128,2048]{1,0:T(8,128)(2,1)S(1)}, bf16[128,2048]{1,0:T(8,128)(2,1)S(1)}, u32[]{:S(2)}, u32[]{:S(2)}) collective-permute-start(bf16[128,2048]{1,0:T(8,128)(2,1)S(1)} %pad_maximum_fusion.10), channel_id=1, source_target_pairs={{0,16},{1,17},{2,18},{3,19},{4,20},{5,21},{6,22},{7,23},{8,24},{9,... | collective-permute-start | bytes 1572872 | tf_op jit(solution)/shard_map/ppermute | solution.py:67
  116.0 33.1 %collective-permute-start.23 = (bf16[128,2048]{1,0:T(8,128)(2,1)S(1)}, bf16[128,2048]{1,0:T(8,128)(2,1)S(1)}, u32[]{:S(2)}, u32[]{:S(2)}) collective-permute-start(bf16[128,2048]{1,0:T(8,128)(2,1)S(1)} %pad_maximum_fusion.11), channel_id=1, source_target_pairs={{0,16},{1,17},{2,18},{3,19},{4,20},{5,21},{6,22},{7,23},{8,24},{9,... | collective-permute-start | bytes 1572872 | tf_op jit(solution)/shard_map/ppermute | solution.py:67
  128.2 10.9 %collective-permute-start.19 = (bf16[128,1024]{1,0:T(8,128)(2,1)S(1)}, bf16[128,1024]{1,0:T(8,128)(2,1)S(1)}, u32[]{:S(2)}, u32[]{:S(2)}) collective-permute-start(bf16[128,1024]{1,0:T(8,128)(2,1)S(1)} %fusion.20), channel_id=1, source_target_pairs={{0,8},{1,9},{2,10},{3,11},{4,12},{5,13},{6,14},{7,15},{8,0},{9,1},... | collective-permute-start | bytes 786440 | tf_op jit(solution)/shard_map/ppermute | solution.py:67
  130.5 2.0 %collective-permute-start.27 = (bf16[64,1792]{1,0:T(8,128)(2,1)S(1)}, bf16[64,1792]{1,0:T(8,128)(2,1)S(1)}, u32[]{:S(2)}, u32[]{:S(2)}) collective-permute-start(bf16[64,1792]{1,0:T(8,128)(2,1)S(1)} %get-tuple-element.94), channel_id=1, source_target_pairs={{0,1},{1,0},{2,3},{3,2},{4,5},{5,4},{6,7},{7,6},{8,9},{9,8},{10,11... | collective-permute-start | bytes 688136 | tf_op jit(solution)/shard_map/ppermute | solution.py:67
  130.9 15.2 %collective-permute-start.30 = (bf16[128,1792]{1,0:T(8,128)(2,1)S(1)}, bf16[128,1792]{1,0:T(8,128)(2,1)S(1)}, u32[]{:S(2)}, u32[]{:S(2)}) collective-permute-start(bf16[128,1792]{1,0:T(8,128)(2,1)S(1)} %convolution_convert_fusion.13), channel_id=1, source_target_pairs={{0,2},{1,3},{2,4},{3,5},{4,6},{5,7},{6,0},{7,1},{8,10},{9,11},{10,... | collective-permute-start | bytes 1376264 | tf_op jit(solution)/shard_map/ppermute | solution.py:67
  132.8 26.6 %collective-permute-start.28 = (bf16[128,1792]{1,0:T(8,128)(2,1)S(1)}, bf16[128,1792]{1,0:T(8,128)(2,1)S(1)}, u32[]{:S(2)}, u32[]{:S(2)}) collective-permute-start(bf16[128,1792]{1,0:T(8,128)(2,1)S(1)} %convolution_convert_fusion.14), channel_id=1, source_target_pairs={{0,6},{1,7},{2,0},{3,1},{4,2},{5,3},{6,4},{7,5},{8,14},{9,15},{10,... | collective-permute-start | bytes 1376264 | tf_op jit(solution)/shard_map/ppermute | solution.py:67
  139.4 9.7 %collective-permute-start.22 = (bf16[128,1024]{1,0:T(8,128)(2,1)S(1)}, bf16[128,1024]{1,0:T(8,128)(2,1)S(1)}, u32[]{:S(2)}, u32[]{:S(2)}) collective-permute-start(bf16[128,1024]{1,0:T(8,128)(2,1)S(1)} %fusion.19), channel_id=1, source_target_pairs={{0,8},{1,9},{2,10},{3,11},{4,12},{5,13},{6,14},{7,15},{8,0},{9,1},... | collective-permute-start | bytes 786440 | tf_op jit(solution)/shard_map/ppermute | solution.py:67
  142.4 3.7 %collective-permute-start.29 = (bf16[64,1792]{1,0:T(8,128)(2,1)S(1)}, bf16[64,1792]{1,0:T(8,128)(2,1)S(1)}, u32[]{:S(2)}, u32[]{:S(2)}) collective-permute-start(bf16[64,1792]{1,0:T(8,128)(2,1)S(1)} %get-tuple-element.90), channel_id=1, source_target_pairs={{0,1},{1,0},{2,3},{3,2},{4,5},{5,4},{6,7},{7,6},{8,9},{9,8},{10,11... | collective-permute-start | bytes 688136 | tf_op jit(solution)/shard_map/ppermute | solution.py:67
  146.1 34.1 %collective-permute-start.21 = (bf16[64,1792]{1,0:T(8,128)(2,1)S(1)}, bf16[64,1792]{1,0:T(8,128)(2,1)S(1)}, u32[]{:S(2)}, u32[]{:S(2)}) collective-permute-start(bf16[64,1792]{1,0:T(8,128)(2,1)S(1)} %get-tuple-element.88), channel_id=1, source_target_pairs={{0,1},{1,0},{2,3},{3,2},{4,5},{5,4},{6,7},{7,6},{8,9},{9,8},{10,11... | collective-permute-start | bytes 688136 | tf_op jit(solution)/shard_map/ppermute | solution.py:67
  146.4 18.8 %collective-permute-start.31 = (bf16[128,1792]{1,0:T(8,128)(2,1)S(1)}, bf16[128,1792]{1,0:T(8,128)(2,1)S(1)}, u32[]{:S(2)}, u32[]{:S(2)}) collective-permute-start(bf16[128,1792]{1,0:T(8,128)(2,1)S(1)} %convolution_convert_fusion.12), channel_id=1, source_target_pairs={{0,6},{1,7},{2,0},{3,1},{4,2},{5,3},{6,4},{7,5},{8,14},{9,15},{10,... | collective-permute-start | bytes 1376264 | tf_op jit(solution)/shard_map/ppermute | solution.py:67
  149.5 7.2 %collective-permute-start.25 = (bf16[128,1024]{1,0:T(8,128)(2,1)S(1)}, bf16[128,1024]{1,0:T(8,128)(2,1)S(1)}, u32[]{:S(2)}, u32[]{:S(2)}) collective-permute-start(bf16[128,1024]{1,0:T(8,128)(2,1)S(1)} %fusion.18), channel_id=1, source_target_pairs={{0,8},{1,9},{2,10},{3,11},{4,12},{5,13},{6,14},{7,15},{8,0},{9,1},... | collective-permute-start | bytes 786440 | tf_op jit(solution)/shard_map/ppermute | solution.py:67
  151.4 1.6 collective-permute-start.24
  153.0 4.5 %collective-permute-start.32 = (bf16[64,1792]{1,0:T(8,128)(2,1)S(1)}, bf16[64,1792]{1,0:T(8,128)(2,1)S(1)}, u32[]{:S(2)}, u32[]{:S(2)}) collective-permute-start(bf16[64,1792]{1,0:T(8,128)(2,1)S(1)} %get-tuple-element.96), channel_id=1, source_target_pairs={{0,1},{1,0},{2,3},{3,2},{4,5},{5,4},{6,7},{7,6},{8,9},{9,8},{10,11... | collective-permute-start | bytes 688136 | tf_op jit(solution)/shard_map/ppermute | solution.py:67
  157.4 7.8 %collective-permute-start.26 = (bf16[64,1792]{1,0:T(8,128)(2,1)S(1)}, bf16[64,1792]{1,0:T(8,128)(2,1)S(1)}, u32[]{:S(2)}, u32[]{:S(2)}) collective-permute-start(bf16[64,1792]{1,0:T(8,128)(2,1)S(1)} %get-tuple-element.86), channel_id=1, source_target_pairs={{0,1},{1,0},{2,3},{3,2},{4,5},{5,4},{6,7},{7,6},{8,9},{9,8},{10,11... | collective-permute-start | bytes 688136 | tf_op jit(solution)/shard_map/ppermute | solution.py:67
  157.8 31.2 %collective-permute-start.33 = (bf16[128,1792]{1,0:T(8,128)(2,1)S(1)}, bf16[128,1792]{1,0:T(8,128)(2,1)S(1)}, u32[]{:S(2)}, u32[]{:S(2)}) collective-permute-start(bf16[128,1792]{1,0:T(8,128)(2,1)S(1)} %fusion.11), channel_id=1, source_target_pairs={{0,2},{1,3},{2,4},{3,5},{4,6},{5,7},{6,0},{7,1},{8,10},{9,11},{10,... | collective-permute-start | bytes 1376264 | tf_op jit(solution)/shard_map/ppermute | solution.py:67
  165.5 23.9 %collective-permute-start.34 = (bf16[128,1792]{1,0:T(8,128)(2,1)S(1)}, bf16[128,1792]{1,0:T(8,128)(2,1)S(1)}, u32[]{:S(2)}, u32[]{:S(2)}) collective-permute-start(bf16[128,1792]{1,0:T(8,128)(2,1)S(1)} %add_convert_fusion.2), channel_id=1, source_target_pairs={{0,8},{1,9},{2,10},{3,11},{4,12},{5,13},{6,14},{7,15},{8,0},{9,1},... | collective-permute-start | bytes 1376264 | tf_op jit(solution)/shard_map/ppermute | solution.py:67
  166.4 32.2 %collective-permute-start.35 = (bf16[128,1792]{1,0:T(8,128)(2,1)S(1)}, bf16[128,1792]{1,0:T(8,128)(2,1)S(1)}, u32[]{:S(2)}, u32[]{:S(2)}) collective-permute-start(bf16[128,1792]{1,0:T(8,128)(2,1)S(1)} %add_convert_fusion.1), channel_id=1, source_target_pairs={{0,10},{1,11},{2,12},{3,13},{4,14},{5,15},{6,8},{7,9},{8,2},{9,3},... | collective-permute-start | bytes 1376264 | tf_op jit(solution)/shard_map/ppermute | solution.py:67
  198.8 0.9 copy-start.1

commit v15 on v14

--- a/solution.py
+++ b/solution.py
@@ -180,13 +180,16 @@
     pays.append(places(info_x)[1])
     middle[0] = weigh(0, 0).astype(BF)
     hidden[0, 1], gates, ups = together((hidden[0, 1], gates, ups))
-    part += [
-        send(jnp.concatenate([gates[order[q]], ups[order[q]]], axis=1), flip=2)
-        for q in range(1, chips)
-    ]
+
+    def whole(q):
+        return jnp.concatenate([gates[order[q]], ups[order[q]]], axis=1)
+
+    part.append(send(whole(1), flip=2))
     middle[0] = send(middle[0], 1)
     down_product(0, 1)
     middle[0], part[1] = before_weigh(0, (middle[0], part[1]))
+    middle[0], gates, ups = together((middle[0], gates, ups))
+    part += [send(whole(q), flip=2) for q in range(2, chips)]
     middle[1] = send(weigh(0, 1).astype(BF), 1)
     finish(1)
     down_product(1, 0)

time: 201 us -> 188 us (0.935)
  starting transfers between devices: 49.7 us -> 38.2 us
    ppermute x36, starting transfers between devices: 49.7 us -> 38.2 us  [send(): lax.ppermute(value, ('dp', 'expert'), [(i * owners + j, (i ^ flip) * owne...]
  transfers between devices with their start and end apart: 36 -> 36, of which waited for: 19 -> 21; matrix products, arithmetic and copies ran while one was open for 14% -> 15% of each run, Pallas kernels for 0% -> 0%
where the time goes in v15:
time: 188 us
  waiting for transfers between devices  117 us (62%)
  starting transfers between devices  38.2 us (20%)
  matrix products  22.9 us (12%)
  local copies, waits for them, and re-layouts  5.58 us (3%)
  other arithmetic  3.96 us (2%)
    ppermute x36, waiting for transfers between devices, send(): lax.ppermute(value, ('dp', 'expert'), [(i * owners + j, (i ^ flip) * owne...  117 us
    ppermute x36, starting transfers between devices, send(): lax.ppermute(value, ('dp', 'expert'), [(i * owners + j, (i ^ flip) * owne...  38.2 us
    dot_general x3, matrix products, product(): jnp.dot(flat, weights[:, lo:hi], preferred_element_type=F32)  12.9 us
    dot_general x8, matrix products, down_product(): value = jnp.dot(hidden[q, g], downs, preferred_element_type=F32).astype(BF)  5.24 us
  transfers between devices with their start and end apart: 36, of which 21 were waited for; matrix products, arithmetic and copies ran while one was open for 15% of the time, Pallas kernels for 0%

profile of v15, /device:TPU:0, one launch (start us, length us, event | category | flops | bytes accessed | tf_op | source)
XLA Modules:
  0.0 188.0 jit_solution(17437767320100818422)
XLA Ops:
  0.0 0.8 convert_bitcast_fusion
  0.8 0.7 fusion.62
  1.5 1.4 constant_dynamic-slice_fusion.1
  3.0 3.0 %collective-permute-start = (bf16[136,1792]{1,0:T(8,128)(2,1)S(1)}, bf16[136,1792]{1,0:T(8,128)(2,1)S(1)}, u32[]{:S(2)}, u32[]{:S(2)}) collective-permute-start(bf16[136,1792]{1,0:T(8,128)(2,1)S(1)} %get-tuple-element.111), channel_id=1, source_target_pairs={{0,16},{1,17},{2,18},{3,19},{4,20},{5,21},{6,22},{7,23},{8,24},{9,... | collective-permute-start | bytes 1462280 | tf_op jit(solution)/shard_map/ppermute | solution.py:67
  6.0 1.6 collective-permute-start.1
  7.6 1.5 collective-permute-start.9
  9.1 8.0 %collective-permute-done = bf16[136,1792]{1,0:T(8,128)(2,1)S(1)} collective-permute-done((bf16[136,1792]{1,0:T(8,128)(2,1)S(1)}, bf16[136,1792]{1,0:T(8,128)(2,1)S(1)}, u32[]{:S(2)}, u32[]{:S(2)}) %collective-permute-start) | collective-permute-done | bytes 487456 | tf_op jit(solution)/shard_map/ppermute | solution.py:67
  17.1 3.8 %collective-permute-start.3 = (bf16[136,1792]{1,0:T(8,128)(2,1)S(1)}, bf16[136,1792]{1,0:T(8,128)(2,1)S(1)}, u32[]{:S(2)}, u32[]{:S(2)}) collective-permute-start(bf16[136,1792]{1,0:T(8,128)(2,1)S(1)} %get-tuple-element.40), channel_id=1, source_target_pairs={{0,6},{1,7},{2,0},{3,1},{4,2},{5,3},{6,4},{7,5},{8,14},{9,15},{10,... | collective-permute-start | bytes 1462280 | tf_op jit(solution)/shard_map/ppermute | solution.py:67
  21.0 0.5 collective-permute-start.7
  21.5 1.0 slice_bitcast_fusion.2
  22.6 1.6 collective-permute-start.4
  24.3 0.7 slice_bitcast_fusion.28
  25.0 7.6 %collective-permute-done.3 = bf16[136,1792]{1,0:T(8,128)(2,1)S(1)} collective-permute-done((bf16[136,1792]{1,0:T(8,128)(2,1)S(1)}, bf16[136,1792]{1,0:T(8,128)(2,1)S(1)}, u32[]{:S(2)}, u32[]{:S(2)}) %collective-permute-start.3) | collective-permute-done | bytes 487456 | tf_op jit(solution)/shard_map/ppermute | solution.py:67
  32.6 1.6 collective-permute-start.6
  34.1 28.7 %collective-permute-done.2 = bf16[136,1792]{1,0:T(8,128)(2,1)S(1)} collective-permute-done((bf16[136,1792]{1,0:T(8,128)(2,1)}, bf16[136,1792]{1,0:T(8,128)(2,1)S(1)}, u32[]{:S(2)}, u32[]{:S(2)}) %collective-permute-start.2) | collective-permute-done | bytes 487456 | tf_op jit(solution)/shard_map/ppermute | solution.py:67
  62.8 1.7 collective-permute-start.5
  64.7 8.1 %collective-permute-done.6 = bf16[1024,896]{1,0:T(8,128)(2,1)S(1)} collective-permute-done((bf16[1024,896]{1,0:T(8,128)(2,1)S(1)}, bf16[1024,896]{1,0:T(8,128)(2,1)S(1)}, u32[]{:S(2)}, u32[]{:S(2)}) %collective-permute-start.6) | collective-permute-done | bytes 1835040 | tf_op jit(solution)/shard_map/ppermute | solution.py:67
  73.0 4.6 %collective-permute-done.5 = bf16[136,1792]{1,0:T(8,128)(2,1)S(1)} collective-permute-done((bf16[136,1792]{1,0:T(8,128)(2,1)S(1)}, bf16[136,1792]{1,0:T(8,128)(2,1)S(1)}, u32[]{:S(2)}, u32[]{:S(2)}) %collective-permute-start.5) | collective-permute-done | bytes 487456 | tf_op jit(solution)/shard_map/ppermute | solution.py:67
  78.0 0.4 convolution_convert_fusion
  78.7 0.4 convolution_convert_fusion.2
  79.2 0.6 collective-permute-start.8
  79.7 1.5 collective-permute-start.15
  81.7 0.4 convolution_convert_fusion.3
  82.4 6.2 %collective-permute-done.9 = bf16[896,2048]{1,0:T(8,128)(2,1)} collective-permute-done((bf16[896,2048]{1,0:T(8,128)(2,1)}, bf16[896,2048]{1,0:T(8,128)(2,1)}, u32[]{:S(2)}, u32[]{:S(2)}) %collective-permute-start.9) | collective-permute-done | bytes 3670048 | tf_op jit(solution)/shard_map/ppermute | solution.py:67
  88.6 3.6 %fusion.15 = bf16[4,128,1024]{2,1,0:T(8,128)(2,1)S(1)} fusion(bf16[4,128,1792]{2,1,0:T(8,128)(2,1)S(1)} %pad_maximum_fusion.4, bf16[896,2048]{1,0:T(8,128)(2,1)S(1)} %bitcast.131, bf16[896,2048]{1,0:T(8,128)(2,1)} %collective-permute-done.9), kind=kOutput, calls=%fused_computation.39 | convolution fusion | flops 1886912512 | bytes 10223616 | tf_op jit(solution)/shard_map/dot_general | solution.py:134
  92.2 0.6 collective-permute-start.11
  92.8 3.6 %fusion.12 = bf16[4,128,1024]{2,1,0:T(8,128)(2,1)S(1)} fusion(bf16[4,128,1792]{2,1,0:T(8,128)(2,1)S(1)} %pad_maximum_fusion.4, bf16[896,2048]{1,0:T(8,128)(2,1)S(1)} %bitcast.132, bf16[896,2048]{1,0:T(8,128)(2,1)} %collective-permute-done.9), kind=kOutput, calls=%fused_computation.38 | convolution fusion | flops 1886912512 | bytes 10223616 | tf_op jit(solution)/shard_map/dot_general | solution.py:134
  96.4 1.6 collective-permute-start.12
  98.0 2.4 %collective-permute-done.11 = bf16[128,1024]{1,0:T(8,128)(2,1)S(1)} collective-permute-done((bf16[128,1024]{1,0:T(8,128)(2,1)S(1)}, bf16[128,1024]{1,0:T(8,128)(2,1)S(1)}, u32[]{:S(2)}, u32[]{:S(2)}) %collective-permute-start.11) | collective-permute-done | bytes 262176 | tf_op jit(solution)/shard_map/ppermute | solution.py:67
  100.3 5.7 %fusion = f32[512,2048]{1,0:T(8,128)S(1)} fusion(bf16[512,1792]{1,0:T(8,128)(2,1)S(1)} %bitcast.120, bf16[896,2048]{1,0:T(8,128)(2,1)} %collective-permute-done.9, bf16[896,2048]{1,0:T(8,128)(2,1)S(1)} %bitcast.133), kind=kOutput, calls=%fused_computation.5 | convolution fusion | flops 3772776448 | bytes 13369344 | tf_op jit(solution)/shard_map/dot_general | solution.py:134
  106.4 1.6 collective-permute-start.13
  107.9 0.7 convolution_convert_fusion.10
  109.1 1.1 collective-permute-done.16
  110.5 1.6 collective-permute-start.17
  112.1 0.7 collective-permute-done.13
  113.0 0.7 convolution_convert_fusion.11
  113.8 1.4 collective-permute-done.14
  115.2 9.7 %collective-permute-done.17 = bf16[128,1792]{1,0:T(8,128)(2,1)S(1)} collective-permute-done((bf16[128,1792]{1,0:T(8,128)(2,1)S(1)}, bf16[128,1792]{1,0:T(8,128)(2,1)S(1)}, u32[]{:S(2)}, u32[]{:S(2)}) %collective-permute-start.17) | collective-permute-done | bytes 458784 | tf_op jit(solution)/shard_map/ppermute | solution.py:67
  124.9 1.1 collective-permute-done.18
  126.2 0.6 collective-permute-start.19
  126.8 0.7 convolution_convert_fusion.6
  127.8 1.8 collective-permute-start.30
  130.3 1.8 collective-permute-start.23
  132.4 2.3 %collective-permute-start.28 = (bf16[128,1792]{1,0:T(8,128)(2,1)S(1)}, bf16[128,1792]{1,0:T(8,128)(2,1)S(1)}, u32[]{:S(2)}, u32[]{:S(2)}) collective-permute-start(bf16[128,1792]{1,0:T(8,128)(2,1)S(1)} %convolution_convert_fusion.14), channel_id=1, source_target_pairs={{0,6},{1,7},{2,0},{3,1},{4,2},{5,3},{6,4},{7,5},{8,14},{9,15},{10,... | collective-permute-start | bytes 1376264 | tf_op jit(solution)/shard_map/ppermute | solution.py:67
  134.7 10.0 %collective-permute-done.20 = bf16[128,2048]{1,0:T(8,128)(2,1)S(1)} collective-permute-done((bf16[128,2048]{1,0:T(8,128)(2,1)S(1)}, bf16[128,2048]{1,0:T(8,128)(2,1)S(1)}, u32[]{:S(2)}, u32[]{:S(2)}) %collective-permute-start.20) | collective-permute-done | bytes 524320 | tf_op jit(solution)/shard_map/ppermute | solution.py:67
  145.0 1.6 collective-permute-start.22
  146.5 0.7 convolution_convert_fusion.9
  147.2 0.7 convolution_convert_fusion.5
  148.0 0.6 collective-permute-start.21
  148.6 0.9 collective-permute-done.29
  149.8 2.3 %collective-permute-start.31 = (bf16[128,1792]{1,0:T(8,128)(2,1)S(1)}, bf16[128,1792]{1,0:T(8,128)(2,1)S(1)}, u32[]{:S(2)}, u32[]{:S(2)}) collective-permute-start(bf16[128,1792]{1,0:T(8,128)(2,1)S(1)} %convolution_convert_fusion.12), channel_id=1, source_target_pairs={{0,6},{1,7},{2,0},{3,1},{4,2},{5,3},{6,4},{7,5},{8,14},{9,15},{10,... | collective-permute-start | bytes 1376264 | tf_op jit(solution)/shard_map/ppermute | solution.py:67
  152.7 1.8 collective-permute-start.25
  154.5 0.7 convolution_convert_fusion.4
  155.1 0.7 convolution_convert_fusion.8
  156.0 1.4 collective-permute-done.24
  157.5 3.0 %collective-permute-done.25 = bf16[128,1024]{1,0:T(8,128)(2,1)S(1)} collective-permute-done((bf16[128,1024]{1,0:T(8,128)(2,1)S(1)}, bf16[128,1024]{1,0:T(8,128)(2,1)S(1)}, u32[]{:S(2)}, u32[]{:S(2)}) %collective-permute-start.25) | collective-permute-done | bytes 262176 | tf_op jit(solution)/shard_map/ppermute | solution.py:67
  160.5 0.7 convolution_convert_fusion.7
  161.7 0.7 collective-permute-done.31
  163.1 0.6 collective-permute-start.34
  164.0 0.9 collective-permute-start.35
  165.0 11.8 %collective-permute-done.33 = bf16[128,1792]{1,0:T(8,128)(2,1)S(1)} collective-permute-done((bf16[128,1792]{1,0:T(8,128)(2,1)S(1)}, bf16[128,1792]{1,0:T(8,128)(2,1)S(1)}, u32[]{:S(2)}, u32[]{:S(2)}) %collective-permute-start.33) | collective-permute-done | bytes 458784 | tf_op jit(solution)/shard_map/ppermute | solution.py:67
  177.3 8.9 %collective-permute-done.35 = bf16[128,1792]{1,0:T(8,128)(2,1)S(1)} collective-permute-done((bf16[128,1792]{1,0:T(8,128)(2,1)S(1)}, bf16[128,1792]{1,0:T(8,128)(2,1)S(1)}, u32[]{:S(2)}, u32[]{:S(2)}) %collective-permute-start.35) | collective-permute-done | bytes 458784 | tf_op jit(solution)/shard_map/ppermute | solution.py:67
  186.4 0.9 copy-done.1
  187.3 0.7 slice_dynamic-update-slice_fusion
  (109 shorter events, 8.6 us)
Async XLA Ops:
  0.0 32.6 %copy-start = (bf16[1,1024,896]{2,1,0:T(8,128)(2,1)S(1)}, bf16[1,1024,896]{2,1,0:T(8,128)(2,1)}, u32[]{:S(2)}) copy-start(bf16[1,1024,896]{2,1,0:T(8,128)(2,1)} %param.7) | copy-start | bytes 5505028
  3.0 14.2 %collective-permute-start = (bf16[136,1792]{1,0:T(8,128)(2,1)S(1)}, bf16[136,1792]{1,0:T(8,128)(2,1)S(1)}, u32[]{:S(2)}, u32[]{:S(2)}) collective-permute-start(bf16[136,1792]{1,0:T(8,128)(2,1)S(1)} %get-tuple-element.111), channel_id=1, source_target_pairs={{0,16},{1,17},{2,18},{3,19},{4,20},{5,21},{6,22},{7,23},{8,24},{9,... | collective-permute-start | bytes 1462280 | tf_op jit(solution)/shard_map/ppermute | solution.py:67
  6.0 15.5 %collective-permute-start.1 = (bf16[136,1792]{1,0:T(8,128)(2,1)S(1)}, bf16[136,1792]{1,0:T(8,128)(2,1)}, u32[]{:S(2)}, u32[]{:S(2)}) collective-permute-start(bf16[136,1792]{1,0:T(8,128)(2,1)S(1)} %get-tuple-element.40), channel_id=1, source_target_pairs={{0,2},{1,3},{2,4},{3,5},{4,6},{5,7},{6,0},{7,1},{8,10},{9,11},{10,... | collective-permute-start | bytes 1462280 | tf_op jit(solution)/shard_map/ppermute | solution.py:67
  7.6 81.0 %collective-permute-start.9 = (bf16[896,2048]{1,0:T(8,128)(2,1)}, bf16[896,2048]{1,0:T(8,128)(2,1)}, u32[]{:S(2)}, u32[]{:S(2)}) collective-permute-start(bf16[896,2048]{1,0:T(8,128)(2,1)} %bitcast.130), channel_id=1, source_target_pairs={{0,8},{1,9},{2,10},{3,11},{4,12},{5,13},{6,14},{7,15},{8,0},{9,1},... | collective-permute-start | bytes 11010056 | tf_op jit(solution)/shard_map/ppermute | solution.py:67
  17.1 15.5 %collective-permute-start.3 = (bf16[136,1792]{1,0:T(8,128)(2,1)S(1)}, bf16[136,1792]{1,0:T(8,128)(2,1)S(1)}, u32[]{:S(2)}, u32[]{:S(2)}) collective-permute-start(bf16[136,1792]{1,0:T(8,128)(2,1)S(1)} %get-tuple-element.40), channel_id=1, source_target_pairs={{0,6},{1,7},{2,0},{3,1},{4,2},{5,3},{6,4},{7,5},{8,14},{9,15},{10,... | collective-permute-start | bytes 1462280 | tf_op jit(solution)/shard_map/ppermute | solution.py:67
  21.0 43.6 %collective-permute-start.7 = (bf16[136,1792]{1,0:T(8,128)(2,1)S(1)}, bf16[136,1792]{1,0:T(8,128)(2,1)S(1)}, u32[]{:S(2)}, u32[]{:S(2)}) collective-permute-start(bf16[136,1792]{1,0:T(8,128)(2,1)S(1)} %collective-permute-done), channel_id=1, source_target_pairs={{0,6},{1,7},{2,0},{3,1},{4,2},{5,3},{6,4},{7,5},{8,14},{9,15},{10,... | collective-permute-start | bytes 1462280 | tf_op jit(solution)/shard_map/ppermute | solution.py:67
  22.6 40.3 %collective-permute-start.4 = (bf16[136,1792]{1,0:T(8,128)(2,1)S(1)}, bf16[136,1792]{1,0:T(8,128)(2,1)S(1)}, u32[]{:S(2)}, u32[]{:S(2)}) collective-permute-start(bf16[136,1792]{1,0:T(8,128)(2,1)S(1)} %collective-permute-done), channel_id=1, source_target_pairs={{0,2},{1,3},{2,4},{3,5},{4,6},{5,7},{6,0},{7,1},{8,10},{9,11},{10,... | collective-permute-start | bytes 1462280 | tf_op jit(solution)/shard_map/ppermute | solution.py:67
  24.2 38.6 %collective-permute-start.2 = (bf16[136,1792]{1,0:T(8,128)(2,1)}, bf16[136,1792]{1,0:T(8,128)(2,1)S(1)}, u32[]{:S(2)}, u32[]{:S(2)}) collective-permute-start(bf16[136,1792]{1,0:T(8,128)(2,1)} %collective-permute-done.1), channel_id=1, source_target_pairs={{0,2},{1,3},{2,4},{3,5},{4,6},{5,7},{6,0},{7,1},{8,10},{9,11},{10,... | collective-permute-start | bytes 1462280 | tf_op jit(solution)/shard_map/ppermute | solution.py:67
  32.6 40.2 %collective-permute-start.6 = (bf16[1024,896]{1,0:T(8,128)(2,1)S(1)}, bf16[1024,896]{1,0:T(8,128)(2,1)S(1)}, u32[]{:S(2)}, u32[]{:S(2)}) collective-permute-start(bf16[1024,896]{1,0:T(8,128)(2,1)S(1)} %bitcast.118), channel_id=1, source_target_pairs={{0,16},{1,17},{2,18},{3,19},{4,20},{5,21},{6,22},{7,23},{8,24},{9,... | collective-permute-start | bytes 5505032 | tf_op jit(solution)/shard_map/ppermute | solution.py:67
  62.8 14.8 %collective-permute-start.5 = (bf16[136,1792]{1,0:T(8,128)(2,1)S(1)}, bf16[136,1792]{1,0:T(8,128)(2,1)S(1)}, u32[]{:S(2)}, u32[]{:S(2)}) collective-permute-start(bf16[136,1792]{1,0:T(8,128)(2,1)S(1)} %collective-permute-done.4), channel_id=1, source_target_pairs={{0,2},{1,3},{2,4},{3,5},{4,6},{5,7},{6,0},{7,1},{8,10},{9,11},{10,... | collective-permute-start | bytes 1462280 | tf_op jit(solution)/shard_map/ppermute | solution.py:67
  78.4 3.7 %collective-permute-start.10 = (bf16[4,64,1792]{2,1,0:T(8,128)(2,1)S(1)}, bf16[4,64,1792]{2,1,0:T(8,128)(2,1)S(1)}, u32[]{:S(2)}, u32[]{:S(2)}) collective-permute-start(bf16[4,64,1792]{2,1,0:T(8,128)(2,1)S(1)} %convolution_convert_fusion), channel_id=1, source_target_pairs={{0,1},{1,0},{2,3},{3,2},{4,5},{5,4},{6,7},{7,6},{8,9},{9,8},{10,11... | collective-permute-start | bytes 2752520 | tf_op jit(solution)/shard_map/ppermute | solution.py:67
  79.2 3.1 %collective-permute-start.8 = (bf16[4,64,1792]{2,1,0:T(8,128)(2,1)S(1)}, bf16[4,64,1792]{2,1,0:T(8,128)(2,1)S(1)}, u32[]{:S(2)}, u32[]{:S(2)}) collective-permute-start(bf16[4,64,1792]{2,1,0:T(8,128)(2,1)S(1)} %convolution_convert_fusion.2), channel_id=1, source_target_pairs={{0,1},{1,0},{2,3},{3,2},{4,5},{5,4},{6,7},{7,6},{8,9},{9,8},{10,11... | collective-permute-start | bytes 2752520 | tf_op jit(solution)/shard_map/ppermute | solution.py:67
  79.7 28.2 %collective-permute-start.15 = (bf16[4,8,256]{2,1,0:T(8,128)(2,1)S(1)}, bf16[4,8,256]{2,1,0:T(8,128)(2,1)S(1)}, u32[]{:S(2)}, u32[]{:S(2)}) collective-permute-start(bf16[4,8,256]{2,1,0:T(8,128)(2,1)S(1)} %pad_maximum_fusion.16), channel_id=1, source_target_pairs={{0,8},{1,9},{2,10},{3,11},{4,12},{5,13},{6,14},{7,15},{8,0},{9,1},... | collective-permute-start | bytes 49160 | tf_op jit(solution)/shard_map/ppermute | solution.py:67
  82.1 6.5 %copy-start.2 = (bf16[1,896,2048]{2,1,0:T(8,128)(2,1)S(1)}, bf16[1,896,2048]{2,1,0:T(8,128)(2,1)}, u32[]{:S(2)}) copy-start(bf16[1,896,2048]{2,1,0:T(8,128)(2,1)} %param.6) | copy-start | bytes 11010052
  92.2 8.1 %collective-permute-start.11 = (bf16[128,1024]{1,0:T(8,128)(2,1)S(1)}, bf16[128,1024]{1,0:T(8,128)(2,1)S(1)}, u32[]{:S(2)}, u32[]{:S(2)}) collective-permute-start(bf16[128,1024]{1,0:T(8,128)(2,1)S(1)} %slice_bitcast_fusion.15), channel_id=1, source_target_pairs={{0,16},{1,17},{2,18},{3,19},{4,20},{5,21},{6,22},{7,23},{8,24},{9,... | collective-permute-start | bytes 786440 | tf_op jit(solution)/shard_map/ppermute | solution.py:67
  96.4 9.7 %collective-permute-start.12 = (bf16[128,1024]{1,0:T(8,128)(2,1)S(1)}, bf16[128,1024]{1,0:T(8,128)(2,1)S(1)}, u32[]{:S(2)}, u32[]{:S(2)}) collective-permute-start(bf16[128,1024]{1,0:T(8,128)(2,1)S(1)} %slice_bitcast_fusion.14), channel_id=1, source_target_pairs={{0,16},{1,17},{2,18},{3,19},{4,20},{5,21},{6,22},{7,23},{8,24},{9,... | collective-permute-start | bytes 786440 | tf_op jit(solution)/shard_map/ppermute | solution.py:67
  106.4 6.4 %collective-permute-start.13 = (bf16[128,1024]{1,0:T(8,128)(2,1)S(1)}, bf16[128,1024]{1,0:T(8,128)(2,1)S(1)}, u32[]{:S(2)}, u32[]{:S(2)}) collective-permute-start(bf16[128,1024]{1,0:T(8,128)(2,1)S(1)} %fusion.21), channel_id=1, source_target_pairs={{0,8},{1,9},{2,10},{3,11},{4,12},{5,13},{6,14},{7,15},{8,0},{9,1},... | collective-permute-start | bytes 786440 | tf_op jit(solution)/shard_map/ppermute | solution.py:67
  108.6 1.6 collective-permute-start.16
  110.5 14.4 %collective-permute-start.17 = (bf16[128,1792]{1,0:T(8,128)(2,1)S(1)}, bf16[128,1792]{1,0:T(8,128)(2,1)S(1)}, u32[]{:S(2)}, u32[]{:S(2)}) collective-permute-start(bf16[128,1792]{1,0:T(8,128)(2,1)S(1)} %convolution_convert_fusion.15), channel_id=1, source_target_pairs={{0,2},{1,3},{2,4},{3,5},{4,6},{5,7},{6,0},{7,1},{8,10},{9,11},{10,... | collective-permute-start | bytes 1376264 | tf_op jit(solution)/shard_map/ppermute | solution.py:67
  112.9 13.1 %collective-permute-start.18 = (bf16[128,2048]{1,0:T(8,128)(2,1)S(1)}, bf16[128,2048]{1,0:T(8,128)(2,1)S(1)}, u32[]{:S(2)}, u32[]{:S(2)}) collective-permute-start(bf16[128,2048]{1,0:T(8,128)(2,1)S(1)} %pad_maximum_fusion.9), channel_id=1, source_target_pairs={{0,16},{1,17},{2,18},{3,19},{4,20},{5,21},{6,22},{7,23},{8,24},{9,... | collective-permute-start | bytes 1572872 | tf_op jit(solution)/shard_map/ppermute | solution.py:67
  113.7 1.6 collective-permute-start.14
  126.2 8.5 %collective-permute-start.19 = (bf16[128,1024]{1,0:T(8,128)(2,1)S(1)}, bf16[128,1024]{1,0:T(8,128)(2,1)S(1)}, u32[]{:S(2)}, u32[]{:S(2)}) collective-permute-start(bf16[128,1024]{1,0:T(8,128)(2,1)S(1)} %fusion.20), channel_id=1, source_target_pairs={{0,8},{1,9},{2,10},{3,11},{4,12},{5,13},{6,14},{7,15},{8,0},{9,1},... | collective-permute-start | bytes 786440 | tf_op jit(solution)/shard_map/ppermute | solution.py:67
  127.8 20.2 %collective-permute-start.30 = (bf16[128,1792]{1,0:T(8,128)(2,1)S(1)}, bf16[128,1792]{1,0:T(8,128)(2,1)S(1)}, u32[]{:S(2)}, u32[]{:S(2)}) collective-permute-start(bf16[128,1792]{1,0:T(8,128)(2,1)S(1)} %convolution_convert_fusion.13), channel_id=1, source_target_pairs={{0,2},{1,3},{2,4},{3,5},{4,6},{5,7},{6,0},{7,1},{8,10},{9,11},{10,... | collective-permute-start | bytes 1376264 | tf_op jit(solution)/shard_map/ppermute | solution.py:67
  129.8 14.9 %collective-permute-start.20 = (bf16[128,2048]{1,0:T(8,128)(2,1)S(1)}, bf16[128,2048]{1,0:T(8,128)(2,1)S(1)}, u32[]{:S(2)}, u32[]{:S(2)}) collective-permute-start(bf16[128,2048]{1,0:T(8,128)(2,1)S(1)} %pad_maximum_fusion.10), channel_id=1, source_target_pairs={{0,16},{1,17},{2,18},{3,19},{4,20},{5,21},{6,22},{7,23},{8,24},{9,... | collective-permute-start | bytes 1572872 | tf_op jit(solution)/shard_map/ppermute | solution.py:67
  130.2 1.9 %collective-permute-start.27 = (bf16[64,1792]{1,0:T(8,128)(2,1)S(1)}, bf16[64,1792]{1,0:T(8,128)(2,1)S(1)}, u32[]{:S(2)}, u32[]{:S(2)}) collective-permute-start(bf16[64,1792]{1,0:T(8,128)(2,1)S(1)} %get-tuple-element.98), channel_id=1, source_target_pairs={{0,1},{1,0},{2,3},{3,2},{4,5},{5,4},{6,7},{7,6},{8,9},{9,8},{10,11... | collective-permute-start | bytes 688136 | tf_op jit(solution)/shard_map/ppermute | solution.py:67
  130.3 22.1 %collective-permute-start.23 = (bf16[128,2048]{1,0:T(8,128)(2,1)S(1)}, bf16[128,2048]{1,0:T(8,128)(2,1)S(1)}, u32[]{:S(2)}, u32[]{:S(2)}) collective-permute-start(bf16[128,2048]{1,0:T(8,128)(2,1)S(1)} %pad_maximum_fusion.11), channel_id=1, source_target_pairs={{0,16},{1,17},{2,18},{3,19},{4,20},{5,21},{6,22},{7,23},{8,24},{9,... | collective-permute-start | bytes 1572872 | tf_op jit(solution)/shard_map/ppermute | solution.py:67
  132.4 29.3 %collective-permute-start.28 = (bf16[128,1792]{1,0:T(8,128)(2,1)S(1)}, bf16[128,1792]{1,0:T(8,128)(2,1)S(1)}, u32[]{:S(2)}, u32[]{:S(2)}) collective-permute-start(bf16[128,1792]{1,0:T(8,128)(2,1)S(1)} %convolution_convert_fusion.14), channel_id=1, source_target_pairs={{0,6},{1,7},{2,0},{3,1},{4,2},{5,3},{6,4},{7,5},{8,14},{9,15},{10,... | collective-permute-start | bytes 1376264 | tf_op jit(solution)/shard_map/ppermute | solution.py:67
  145.0 7.4 %collective-permute-start.22 = (bf16[128,1024]{1,0:T(8,128)(2,1)S(1)}, bf16[128,1024]{1,0:T(8,128)(2,1)S(1)}, u32[]{:S(2)}, u32[]{:S(2)}) collective-permute-start(bf16[128,1024]{1,0:T(8,128)(2,1)S(1)} %fusion.19), channel_id=1, source_target_pairs={{0,8},{1,9},{2,10},{3,11},{4,12},{5,13},{6,14},{7,15},{8,0},{9,1},... | collective-permute-start | bytes 786440 | tf_op jit(solution)/shard_map/ppermute | solution.py:67
  147.9 1.6 collective-permute-start.29
  148.0 16.9 %collective-permute-start.21 = (bf16[64,1792]{1,0:T(8,128)(2,1)S(1)}, bf16[64,1792]{1,0:T(8,128)(2,1)S(1)}, u32[]{:S(2)}, u32[]{:S(2)}) collective-permute-start(bf16[64,1792]{1,0:T(8,128)(2,1)S(1)} %get-tuple-element.92), channel_id=1, source_target_pairs={{0,1},{1,0},{2,3},{3,2},{4,5},{5,4},{6,7},{7,6},{8,9},{9,8},{10,11... | collective-permute-start | bytes 688136 | tf_op jit(solution)/shard_map/ppermute | solution.py:67
  149.8 12.6 %collective-permute-start.31 = (bf16[128,1792]{1,0:T(8,128)(2,1)S(1)}, bf16[128,1792]{1,0:T(8,128)(2,1)S(1)}, u32[]{:S(2)}, u32[]{:S(2)}) collective-permute-start(bf16[128,1792]{1,0:T(8,128)(2,1)S(1)} %convolution_convert_fusion.12), channel_id=1, source_target_pairs={{0,6},{1,7},{2,0},{3,1},{4,2},{5,3},{6,4},{7,5},{8,14},{9,15},{10,... | collective-permute-start | bytes 1376264 | tf_op jit(solution)/shard_map/ppermute | solution.py:67
  152.7 7.8 %collective-permute-start.25 = (bf16[128,1024]{1,0:T(8,128)(2,1)S(1)}, bf16[128,1024]{1,0:T(8,128)(2,1)S(1)}, u32[]{:S(2)}, u32[]{:S(2)}) collective-permute-start(bf16[128,1024]{1,0:T(8,128)(2,1)S(1)} %fusion.18), channel_id=1, source_target_pairs={{0,8},{1,9},{2,10},{3,11},{4,12},{5,13},{6,14},{7,15},{8,0},{9,1},... | collective-permute-start | bytes 786440 | tf_op jit(solution)/shard_map/ppermute | solution.py:67
  155.9 1.6 collective-permute-start.24
  157.4 3.9 %collective-permute-start.32 = (bf16[64,1792]{1,0:T(8,128)(2,1)S(1)}, bf16[64,1792]{1,0:T(8,128)(2,1)S(1)}, u32[]{:S(2)}, u32[]{:S(2)}) collective-permute-start(bf16[64,1792]{1,0:T(8,128)(2,1)S(1)} %get-tuple-element.100), channel_id=1, source_target_pairs={{0,1},{1,0},{2,3},{3,2},{4,5},{5,4},{6,7},{7,6},{8,9},{9,8},{10,11... | collective-permute-start | bytes 688136 | tf_op jit(solution)/shard_map/ppermute | solution.py:67
  161.2 1.6 collective-permute-start.26
  161.6 15.2 %collective-permute-start.33 = (bf16[128,1792]{1,0:T(8,128)(2,1)S(1)}, bf16[128,1792]{1,0:T(8,128)(2,1)S(1)}, u32[]{:S(2)}, u32[]{:S(2)}) collective-permute-start(bf16[128,1792]{1,0:T(8,128)(2,1)S(1)} %fusion.11), channel_id=1, source_target_pairs={{0,2},{1,3},{2,4},{3,5},{4,6},{5,7},{6,0},{7,1},{8,10},{9,11},{10,... | collective-permute-start | bytes 1376264 | tf_op jit(solution)/shard_map/ppermute | solution.py:67
  163.1 14.2 %collective-permute-start.34 = (bf16[128,1792]{1,0:T(8,128)(2,1)S(1)}, bf16[128,1792]{1,0:T(8,128)(2,1)S(1)}, u32[]{:S(2)}, u32[]{:S(2)}) collective-permute-start(bf16[128,1792]{1,0:T(8,128)(2,1)S(1)} %add_convert_fusion.2), channel_id=1, source_target_pairs={{0,8},{1,9},{2,10},{3,11},{4,12},{5,13},{6,14},{7,15},{8,0},{9,1},... | collective-permute-start | bytes 1376264 | tf_op jit(solution)/shard_map/ppermute | solution.py:67
  164.0 22.2 %collective-permute-start.35 = (bf16[128,1792]{1,0:T(8,128)(2,1)S(1)}, bf16[128,1792]{1,0:T(8,128)(2,1)S(1)}, u32[]{:S(2)}, u32[]{:S(2)}) collective-permute-start(bf16[128,1792]{1,0:T(8,128)(2,1)S(1)} %add_convert_fusion.1), channel_id=1, source_target_pairs={{0,10},{1,11},{2,12},{3,13},{4,14},{5,15},{6,8},{7,9},{8,2},{9,3},... | collective-permute-start | bytes 1376264 | tf_op jit(solution)/shard_map/ppermute | solution.py:67
  186.4 0.9 copy-start.1

commit v16 on v13

--- a/solution.py
+++ b/solution.py
@@ -142,8 +142,15 @@
     ups = product(chosen1, ff).astype(BF)
     ups, chosen0 = together((ups, chosen0))
     part = [send(ups[order[0]], flip=2)]
-    chosen0, gate_part = together((chosen0, gate_part))
+    chosen0, gate_part, gates, ups = together((chosen0, gate_part, gates, ups))
     part[0] = jnp.concatenate([gate_part, part[0]], axis=1)
+
+    def whole(q):
+        return jnp.concatenate([gates[order[q]], ups[order[q]]], axis=1)
+
+    second = whole(1)
+    chosen0, second = together((chosen0, second))
+    part.append(send(second, flip=2))
     near = product(chosen0)
     pays = [pay0]
 
@@ -177,19 +184,14 @@
     finish(0)
     hidden[0, 0], info_x = together((hidden[0, 0], info_x))
     down_product(0, 0)
-    out[0, 0], gates, ups = together((out[0, 0], gates, ups))
-
-    def whole(q):
-        return jnp.concatenate([gates[order[q]], ups[order[q]]], axis=1)
-
-    part.append(send(whole(1), flip=2))
     pays.append(places(info_x)[1])
     middle[0] = weigh(0, 0).astype(BF)
     middle[0], gates, ups = together((middle[0], gates, ups))
     part += [send(whole(q), flip=2) for q in range(2, chips)]
     middle[0] = send(middle[0], 1)
+    part[1] = before_down(0, part[1])
     down_product(0, 1)
-    middle[0], part[1] = before_weigh(0, (middle[0], part[1]))
+    middle[0] = before_weigh(0, middle[0])
     middle[1] = send(weigh(0, 1).astype(BF), 1)
     finish(1)
     down_product(1, 0)

time: 186 us -> 189 us (1.016)
  starting transfers between devices: 35.6 us -> 40 us
    ppermute x36, starting transfers between devices: 35.6 us -> 40 us  [send(): lax.ppermute(value, ('dp', 'expert'), [(i * owners + j, (i ^ flip) * owne...]
  transfers between devices with their start and end apart: 36 -> 36, of which waited for: 19 -> 17; matrix products, arithmetic and copies ran while one was open for 15% -> 15% of each run, Pallas kernels for 0% -> 0%
where the time goes in v16:
time: 189 us; the launch traced here: 188 us
  waiting for transfers between devices  115 us (61%)
  starting transfers between devices  40 us (21%)
  matrix products  22.9 us (12%)
  local copies, waits for them, and re-layouts  5.58 us (3%)
  other arithmetic  3.96 us (2%)
    ppermute x36, waiting for transfers between devices, send(): lax.ppermute(value, ('dp', 'expert'), [(i * owners + j, (i ^ flip) * owne...  115 us
    ppermute x36, starting transfers between devices, send(): lax.ppermute(value, ('dp', 'expert'), [(i * owners + j, (i ^ flip) * owne...  40 us
    dot_general x3, matrix products, product(): jnp.dot(flat, weights[:, lo:hi], preferred_element_type=F32)  12.9 us
    dot_general x8, matrix products, down_product(): value = jnp.dot(hidden[q, g], downs, preferred_element_type=F32).astype(BF)  5.24 us
  transfers between devices with their start and end apart: 36, of which 17 were waited for; matrix products, arithmetic and copies ran while one was open for 15% of the time, Pallas kernels for 0%

profile of v16, /device:TPU:0, one launch (start us, length us, event | category | flops | bytes accessed | tf_op | source)
XLA Modules:
  0.0 188.4 jit_solution(14434206687357529169)
XLA Ops:
  0.0 0.8 convert_bitcast_fusion
  0.8 0.7 fusion.62
  1.5 1.4 constant_dynamic-slice_fusion.1
  3.0 3.0 %collective-permute-start = (bf16[136,1792]{1,0:T(8,128)(2,1)S(1)}, bf16[136,1792]{1,0:T(8,128)(2,1)S(1)}, u32[]{:S(2)}, u32[]{:S(2)}) collective-permute-start(bf16[136,1792]{1,0:T(8,128)(2,1)S(1)} %get-tuple-element.115), channel_id=1, source_target_pairs={{0,16},{1,17},{2,18},{3,19},{4,20},{5,21},{6,22},{7,23},{8,24},{9,... | collective-permute-start | bytes 1462280 | tf_op jit(solution)/shard_map/ppermute | solution.py:67
  6.0 1.6 collective-permute-start.1
  7.6 1.5 collective-permute-start.9
  9.1 8.0 %collective-permute-done = bf16[136,1792]{1,0:T(8,128)(2,1)S(1)} collective-permute-done((bf16[136,1792]{1,0:T(8,128)(2,1)S(1)}, bf16[136,1792]{1,0:T(8,128)(2,1)S(1)}, u32[]{:S(2)}, u32[]{:S(2)}) %collective-permute-start) | collective-permute-done | bytes 487456 | tf_op jit(solution)/shard_map/ppermute | solution.py:67
  17.1 3.8 %collective-permute-start.3 = (bf16[136,1792]{1,0:T(8,128)(2,1)S(1)}, bf16[136,1792]{1,0:T(8,128)(2,1)S(1)}, u32[]{:S(2)}, u32[]{:S(2)}) collective-permute-start(bf16[136,1792]{1,0:T(8,128)(2,1)S(1)} %get-tuple-element.42), channel_id=1, source_target_pairs={{0,6},{1,7},{2,0},{3,1},{4,2},{5,3},{6,4},{7,5},{8,14},{9,15},{10,... | collective-permute-start | bytes 1462280 | tf_op jit(solution)/shard_map/ppermute | solution.py:67
  21.0 0.5 collective-permute-start.7
  21.5 1.0 slice_bitcast_fusion.2
  22.6 1.6 collective-permute-start.4
  24.3 0.7 slice_bitcast_fusion.28
  25.0 7.6 %collective-permute-done.3 = bf16[136,1792]{1,0:T(8,128)(2,1)S(1)} collective-permute-done((bf16[136,1792]{1,0:T(8,128)(2,1)S(1)}, bf16[136,1792]{1,0:T(8,128)(2,1)S(1)}, u32[]{:S(2)}, u32[]{:S(2)}) %collective-permute-start.3) | collective-permute-done | bytes 487456 | tf_op jit(solution)/shard_map/ppermute | solution.py:67
  32.6 1.6 collective-permute-start.6
  34.1 28.7 %collective-permute-done.2 = bf16[136,1792]{1,0:T(8,128)(2,1)S(1)} collective-permute-done((bf16[136,1792]{1,0:T(8,128)(2,1)}, bf16[136,1792]{1,0:T(8,128)(2,1)S(1)}, u32[]{:S(2)}, u32[]{:S(2)}) %collective-permute-start.2) | collective-permute-done | bytes 487456 | tf_op jit(solution)/shard_map/ppermute | solution.py:67
  62.8 1.7 collective-permute-start.5
  64.7 8.1 %collective-permute-done.6 = bf16[1024,896]{1,0:T(8,128)(2,1)S(1)} collective-permute-done((bf16[1024,896]{1,0:T(8,128)(2,1)S(1)}, bf16[1024,896]{1,0:T(8,128)(2,1)S(1)}, u32[]{:S(2)}, u32[]{:S(2)}) %collective-permute-start.6) | collective-permute-done | bytes 1835040 | tf_op jit(solution)/shard_map/ppermute | solution.py:67
  73.0 4.6 %collective-permute-done.5 = bf16[136,1792]{1,0:T(8,128)(2,1)S(1)} collective-permute-done((bf16[136,1792]{1,0:T(8,128)(2,1)S(1)}, bf16[136,1792]{1,0:T(8,128)(2,1)S(1)}, u32[]{:S(2)}, u32[]{:S(2)}) %collective-permute-start.5) | collective-permute-done | bytes 487456 | tf_op jit(solution)/shard_map/ppermute | solution.py:67
  78.0 0.4 convolution_convert_fusion
  78.7 0.4 convolution_convert_fusion.2
  79.2 0.6 collective-permute-start.8
  79.7 1.5 collective-permute-start.16
  81.7 0.4 convolution_convert_fusion.3
  82.4 6.2 %collective-permute-done.9 = bf16[896,2048]{1,0:T(8,128)(2,1)} collective-permute-done((bf16[896,2048]{1,0:T(8,128)(2,1)}, bf16[896,2048]{1,0:T(8,128)(2,1)}, u32[]{:S(2)}, u32[]{:S(2)}) %collective-permute-start.9) | collective-permute-done | bytes 3670048 | tf_op jit(solution)/shard_map/ppermute | solution.py:67
  88.6 3.6 %fusion.15 = bf16[4,128,1024]{2,1,0:T(8,128)(2,1)S(1)} fusion(bf16[4,128,1792]{2,1,0:T(8,128)(2,1)S(1)} %pad_maximum_fusion.4, bf16[896,2048]{1,0:T(8,128)(2,1)S(1)} %bitcast.131, bf16[896,2048]{1,0:T(8,128)(2,1)} %collective-permute-done.9), kind=kOutput, calls=%fused_computation.39 | convolution fusion | flops 1886912512 | bytes 10223616 | tf_op jit(solution)/shard_map/dot_general | solution.py:134
  92.2 0.6 collective-permute-start.11
  92.8 3.6 %fusion.12 = bf16[4,128,1024]{2,1,0:T(8,128)(2,1)S(1)} fusion(bf16[4,128,1792]{2,1,0:T(8,128)(2,1)S(1)} %pad_maximum_fusion.4, bf16[896,2048]{1,0:T(8,128)(2,1)S(1)} %bitcast.132, bf16[896,2048]{1,0:T(8,128)(2,1)} %collective-permute-done.9), kind=kOutput, calls=%fused_computation.38 | convolution fusion | flops 1886912512 | bytes 10223616 | tf_op jit(solution)/shard_map/dot_general | solution.py:134
  96.4 1.6 collective-permute-start.12
  98.0 2.4 %collective-permute-done.11 = bf16[128,1024]{1,0:T(8,128)(2,1)S(1)} collective-permute-done((bf16[128,1024]{1,0:T(8,128)(2,1)S(1)}, bf16[128,1024]{1,0:T(8,128)(2,1)S(1)}, u32[]{:S(2)}, u32[]{:S(2)}) %collective-permute-start.11) | collective-permute-done | bytes 262176 | tf_op jit(solution)/shard_map/ppermute | solution.py:67
  100.4 5.7 %fusion = f32[512,2048]{1,0:T(8,128)S(1)} fusion(bf16[512,1792]{1,0:T(8,128)(2,1)S(1)} %bitcast.120, bf16[896,2048]{1,0:T(8,128)(2,1)} %collective-permute-done.9, bf16[896,2048]{1,0:T(8,128)(2,1)S(1)} %bitcast.133), kind=kOutput, calls=%fused_computation.5 | convolution fusion | flops 3772776448 | bytes 13369344 | tf_op jit(solution)/shard_map/dot_general | solution.py:134
  106.4 1.6 collective-permute-start.13
  108.4 0.7 convolution_convert_fusion.11
  109.3 1.3 collective-permute-done.17
  111.0 1.8 collective-permute-start.29
  112.9 0.8 collective-permute-start.18
  113.7 1.4 collective-permute-start.21
  115.1 8.9 %collective-permute-done.14 = bf16[128,2048]{1,0:T(8,128)(2,1)S(1)} collective-permute-done((bf16[128,2048]{1,0:T(8,128)(2,1)S(1)}, bf16[128,2048]{1,0:T(8,128)(2,1)S(1)}, u32[]{:S(2)}, u32[]{:S(2)}) %collective-permute-start.14) | collective-permute-done | bytes 524320 | tf_op jit(solution)/shard_map/ppermute | solution.py:67
  124.3 0.6 collective-permute-start.15
  124.9 0.7 convolution_convert_fusion.7
  125.6 0.7 convolution_convert_fusion.5
  126.4 0.6 collective-permute-start.25
  127.0 0.9 collective-permute-done.28
  128.2 1.6 collective-permute-start.30
  130.1 2.3 %collective-permute-start.26 = (bf16[128,1792]{1,0:T(8,128)(2,1)S(1)}, bf16[128,1792]{1,0:T(8,128)(2,1)S(1)}, u32[]{:S(2)}, u32[]{:S(2)}) collective-permute-start(bf16[128,1792]{1,0:T(8,128)(2,1)S(1)} %convolution_convert_fusion.14), channel_id=1, source_target_pairs={{0,6},{1,7},{2,0},{3,1},{4,2},{5,3},{6,4},{7,5},{8,14},{9,15},{10,... | collective-permute-start | bytes 1376264 | tf_op jit(solution)/shard_map/ppermute | solution.py:67
  132.4 2.9 %collective-permute-done.18 = bf16[128,2048]{1,0:T(8,128)(2,1)S(1)} collective-permute-done((bf16[128,2048]{1,0:T(8,128)(2,1)S(1)}, bf16[128,2048]{1,0:T(8,128)(2,1)S(1)}, u32[]{:S(2)}, u32[]{:S(2)}) %collective-permute-start.18) | collective-permute-done | bytes 524320 | tf_op jit(solution)/shard_map/ppermute | solution.py:67
  135.3 0.7 convolution_convert_fusion.6
  136.3 0.6 collective-permute-start.20
  136.9 0.7 convolution_convert_fusion.10
  137.6 8.5 %collective-permute-done.21 = bf16[128,2048]{1,0:T(8,128)(2,1)S(1)} collective-permute-done((bf16[128,2048]{1,0:T(8,128)(2,1)S(1)}, bf16[128,2048]{1,0:T(8,128)(2,1)S(1)}, u32[]{:S(2)}, u32[]{:S(2)}) %collective-permute-start.21) | collective-permute-done | bytes 524320 | tf_op jit(solution)/shard_map/ppermute | solution.py:67
  146.4 0.6 collective-permute-start.23
  147.0 0.7 convolution_convert_fusion.4
  147.7 0.7 convolution_convert_fusion.9
  149.3 0.7 collective-permute-done.22
  150.0 2.1 %collective-permute-start.31 = (bf16[128,1792]{1,0:T(8,128)(2,1)S(1)}, bf16[128,1792]{1,0:T(8,128)(2,1)S(1)}, u32[]{:S(2)}, u32[]{:S(2)}) collective-permute-start(bf16[128,1792]{1,0:T(8,128)(2,1)S(1)} %convolution_convert_fusion.12), channel_id=1, source_target_pairs={{0,6},{1,7},{2,0},{3,1},{4,2},{5,3},{6,4},{7,5},{8,14},{9,15},{10,... | collective-permute-start | bytes 1376264 | tf_op jit(solution)/shard_map/ppermute | solution.py:67
  152.1 3.1 %collective-permute-done.23 = bf16[128,1024]{1,0:T(8,128)(2,1)S(1)} collective-permute-done((bf16[128,1024]{1,0:T(8,128)(2,1)S(1)}, bf16[128,1024]{1,0:T(8,128)(2,1)S(1)}, u32[]{:S(2)}, u32[]{:S(2)}) %collective-permute-start.23) | collective-permute-done | bytes 262176 | tf_op jit(solution)/shard_map/ppermute | solution.py:67
  155.2 0.7 convolution_convert_fusion.8
  156.3 1.6 collective-permute-start.33
  157.9 5.1 %collective-permute-done.31 = bf16[128,1792]{1,0:T(8,128)(2,1)S(1)} collective-permute-done((bf16[128,1792]{1,0:T(8,128)(2,1)S(1)}, bf16[128,1792]{1,0:T(8,128)(2,1)S(1)}, u32[]{:S(2)}, u32[]{:S(2)}) %collective-permute-start.31) | collective-permute-done | bytes 458784 | tf_op jit(solution)/shard_map/ppermute | solution.py:67
  163.3 1.8 collective-permute-start.34
  165.5 2.1 %collective-permute-start.35 = (bf16[128,1792]{1,0:T(8,128)(2,1)S(1)}, bf16[128,1792]{1,0:T(8,128)(2,1)S(1)}, u32[]{:S(2)}, u32[]{:S(2)}) collective-permute-start(bf16[128,1792]{1,0:T(8,128)(2,1)S(1)} %add_convert_fusion.1), channel_id=1, source_target_pairs={{0,10},{1,11},{2,12},{3,13},{4,14},{5,15},{6,8},{7,9},{8,2},{9,3},... | collective-permute-start | bytes 1376264 | tf_op jit(solution)/shard_map/ppermute | solution.py:67
  167.6 8.6 %collective-permute-done.33 = bf16[128,1792]{1,0:T(8,128)(2,1)S(1)} collective-permute-done((bf16[128,1792]{1,0:T(8,128)(2,1)S(1)}, bf16[128,1792]{1,0:T(8,128)(2,1)S(1)}, u32[]{:S(2)}, u32[]{:S(2)}) %collective-permute-start.33) | collective-permute-done | bytes 458784 | tf_op jit(solution)/shard_map/ppermute | solution.py:67
  176.6 9.9 %collective-permute-done.35 = bf16[128,1792]{1,0:T(8,128)(2,1)S(1)} collective-permute-done((bf16[128,1792]{1,0:T(8,128)(2,1)S(1)}, bf16[128,1792]{1,0:T(8,128)(2,1)S(1)}, u32[]{:S(2)}, u32[]{:S(2)}) %collective-permute-start.35) | collective-permute-done | bytes 458784 | tf_op jit(solution)/shard_map/ppermute | solution.py:67
  186.7 0.9 copy-done.1
  187.7 0.7 slice_dynamic-update-slice_fusion
  (109 shorter events, 7.8 us)
Async XLA Ops:
  0.0 32.6 %copy-start = (bf16[1,1024,896]{2,1,0:T(8,128)(2,1)S(1)}, bf16[1,1024,896]{2,1,0:T(8,128)(2,1)}, u32[]{:S(2)}) copy-start(bf16[1,1024,896]{2,1,0:T(8,128)(2,1)} %param.7) | copy-start | bytes 5505028
  3.0 14.2 %collective-permute-start = (bf16[136,1792]{1,0:T(8,128)(2,1)S(1)}, bf16[136,1792]{1,0:T(8,128)(2,1)S(1)}, u32[]{:S(2)}, u32[]{:S(2)}) collective-permute-start(bf16[136,1792]{1,0:T(8,128)(2,1)S(1)} %get-tuple-element.115), channel_id=1, source_target_pairs={{0,16},{1,17},{2,18},{3,19},{4,20},{5,21},{6,22},{7,23},{8,24},{9,... | collective-permute-start | bytes 1462280 | tf_op jit(solution)/shard_map/ppermute | solution.py:67
  6.0 15.5 %collective-permute-start.1 = (bf16[136,1792]{1,0:T(8,128)(2,1)S(1)}, bf16[136,1792]{1,0:T(8,128)(2,1)}, u32[]{:S(2)}, u32[]{:S(2)}) collective-permute-start(bf16[136,1792]{1,0:T(8,128)(2,1)S(1)} %get-tuple-element.42), channel_id=1, source_target_pairs={{0,2},{1,3},{2,4},{3,5},{4,6},{5,7},{6,0},{7,1},{8,10},{9,11},{10,... | collective-permute-start | bytes 1462280 | tf_op jit(solution)/shard_map/ppermute | solution.py:67
  7.6 81.0 %collective-permute-start.9 = (bf16[896,2048]{1,0:T(8,128)(2,1)}, bf16[896,2048]{1,0:T(8,128)(2,1)}, u32[]{:S(2)}, u32[]{:S(2)}) collective-permute-start(bf16[896,2048]{1,0:T(8,128)(2,1)} %bitcast.130), channel_id=1, source_target_pairs={{0,8},{1,9},{2,10},{3,11},{4,12},{5,13},{6,14},{7,15},{8,0},{9,1},... | collective-permute-start | bytes 11010056 | tf_op jit(solution)/shard_map/ppermute | solution.py:67
  17.1 15.5 %collective-permute-start.3 = (bf16[136,1792]{1,0:T(8,128)(2,1)S(1)}, bf16[136,1792]{1,0:T(8,128)(2,1)S(1)}, u32[]{:S(2)}, u32[]{:S(2)}) collective-permute-start(bf16[136,1792]{1,0:T(8,128)(2,1)S(1)} %get-tuple-element.42), channel_id=1, source_target_pairs={{0,6},{1,7},{2,0},{3,1},{4,2},{5,3},{6,4},{7,5},{8,14},{9,15},{10,... | collective-permute-start | bytes 1462280 | tf_op jit(solution)/shard_map/ppermute | solution.py:67
  21.0 43.6 %collective-permute-start.7 = (bf16[136,1792]{1,0:T(8,128)(2,1)S(1)}, bf16[136,1792]{1,0:T(8,128)(2,1)S(1)}, u32[]{:S(2)}, u32[]{:S(2)}) collective-permute-start(bf16[136,1792]{1,0:T(8,128)(2,1)S(1)} %collective-permute-done), channel_id=1, source_target_pairs={{0,6},{1,7},{2,0},{3,1},{4,2},{5,3},{6,4},{7,5},{8,14},{9,15},{10,... | collective-permute-start | bytes 1462280 | tf_op jit(solution)/shard_map/ppermute | solution.py:67
  22.6 40.3 %collective-permute-start.4 = (bf16[136,1792]{1,0:T(8,128)(2,1)S(1)}, bf16[136,1792]{1,0:T(8,128)(2,1)S(1)}, u32[]{:S(2)}, u32[]{:S(2)}) collective-permute-start(bf16[136,1792]{1,0:T(8,128)(2,1)S(1)} %collective-permute-done), channel_id=1, source_target_pairs={{0,2},{1,3},{2,4},{3,5},{4,6},{5,7},{6,0},{7,1},{8,10},{9,11},{10,... | collective-permute-start | bytes 1462280 | tf_op jit(solution)/shard_map/ppermute | solution.py:67
  24.2 38.6 %collective-permute-start.2 = (bf16[136,1792]{1,0:T(8,128)(2,1)}, bf16[136,1792]{1,0:T(8,128)(2,1)S(1)}, u32[]{:S(2)}, u32[]{:S(2)}) collective-permute-start(bf16[136,1792]{1,0:T(8,128)(2,1)} %collective-permute-done.1), channel_id=1, source_target_pairs={{0,2},{1,3},{2,4},{3,5},{4,6},{5,7},{6,0},{7,1},{8,10},{9,11},{10,... | collective-permute-start | bytes 1462280 | tf_op jit(solution)/shard_map/ppermute | solution.py:67
  32.6 40.2 %collective-permute-start.6 = (bf16[1024,896]{1,0:T(8,128)(2,1)S(1)}, bf16[1024,896]{1,0:T(8,128)(2,1)S(1)}, u32[]{:S(2)}, u32[]{:S(2)}) collective-permute-start(bf16[1024,896]{1,0:T(8,128)(2,1)S(1)} %bitcast.118), channel_id=1, source_target_pairs={{0,16},{1,17},{2,18},{3,19},{4,20},{5,21},{6,22},{7,23},{8,24},{9,... | collective-permute-start | bytes 5505032 | tf_op jit(solution)/shard_map/ppermute | solution.py:67
  62.8 14.8 %collective-permute-start.5 = (bf16[136,1792]{1,0:T(8,128)(2,1)S(1)}, bf16[136,1792]{1,0:T(8,128)(2,1)S(1)}, u32[]{:S(2)}, u32[]{:S(2)}) collective-permute-start(bf16[136,1792]{1,0:T(8,128)(2,1)S(1)} %collective-permute-done.4), channel_id=1, source_target_pairs={{0,2},{1,3},{2,4},{3,5},{4,6},{5,7},{6,0},{7,1},{8,10},{9,11},{10,... | collective-permute-start | bytes 1462280 | tf_op jit(solution)/shard_map/ppermute | solution.py:67
  78.4 3.7 %collective-permute-start.10 = (bf16[4,64,1792]{2,1,0:T(8,128)(2,1)S(1)}, bf16[4,64,1792]{2,1,0:T(8,128)(2,1)S(1)}, u32[]{:S(2)}, u32[]{:S(2)}) collective-permute-start(bf16[4,64,1792]{2,1,0:T(8,128)(2,1)S(1)} %convolution_convert_fusion), channel_id=1, source_target_pairs={{0,1},{1,0},{2,3},{3,2},{4,5},{5,4},{6,7},{7,6},{8,9},{9,8},{10,11... | collective-permute-start | bytes 2752520 | tf_op jit(solution)/shard_map/ppermute | solution.py:67
  79.2 3.1 %collective-permute-start.8 = (bf16[4,64,1792]{2,1,0:T(8,128)(2,1)S(1)}, bf16[4,64,1792]{2,1,0:T(8,128)(2,1)S(1)}, u32[]{:S(2)}, u32[]{:S(2)}) collective-permute-start(bf16[4,64,1792]{2,1,0:T(8,128)(2,1)S(1)} %convolution_convert_fusion.2), channel_id=1, source_target_pairs={{0,1},{1,0},{2,3},{3,2},{4,5},{5,4},{6,7},{7,6},{8,9},{9,8},{10,11... | collective-permute-start | bytes 2752520 | tf_op jit(solution)/shard_map/ppermute | solution.py:67
  79.7 28.3 %collective-permute-start.16 = (bf16[4,8,256]{2,1,0:T(8,128)(2,1)S(1)}, bf16[4,8,256]{2,1,0:T(8,128)(2,1)S(1)}, u32[]{:S(2)}, u32[]{:S(2)}) collective-permute-start(bf16[4,8,256]{2,1,0:T(8,128)(2,1)S(1)} %pad_maximum_fusion.16), channel_id=1, source_target_pairs={{0,8},{1,9},{2,10},{3,11},{4,12},{5,13},{6,14},{7,15},{8,0},{9,1},... | collective-permute-start | bytes 49160 | tf_op jit(solution)/shard_map/ppermute | solution.py:67
  82.1 6.5 %copy-start.2 = (bf16[1,896,2048]{2,1,0:T(8,128)(2,1)S(1)}, bf16[1,896,2048]{2,1,0:T(8,128)(2,1)}, u32[]{:S(2)}) copy-start(bf16[1,896,2048]{2,1,0:T(8,128)(2,1)} %param.6) | copy-start | bytes 11010052
  92.2 8.1 %collective-permute-start.11 = (bf16[128,1024]{1,0:T(8,128)(2,1)S(1)}, bf16[128,1024]{1,0:T(8,128)(2,1)S(1)}, u32[]{:S(2)}, u32[]{:S(2)}) collective-permute-start(bf16[128,1024]{1,0:T(8,128)(2,1)S(1)} %slice_bitcast_fusion.15), channel_id=1, source_target_pairs={{0,16},{1,17},{2,18},{3,19},{4,20},{5,21},{6,22},{7,23},{8,24},{9,... | collective-permute-start | bytes 786440 | tf_op jit(solution)/shard_map/ppermute | solution.py:67
  96.4 9.8 %collective-permute-start.12 = (bf16[128,1024]{1,0:T(8,128)(2,1)S(1)}, bf16[128,1024]{1,0:T(8,128)(2,1)S(1)}, u32[]{:S(2)}, u32[]{:S(2)}) collective-permute-start(bf16[128,1024]{1,0:T(8,128)(2,1)S(1)} %slice_bitcast_fusion.12), channel_id=1, source_target_pairs={{0,16},{1,17},{2,18},{3,19},{4,20},{5,21},{6,22},{7,23},{8,24},{9,... | collective-permute-start | bytes 786440 | tf_op jit(solution)/shard_map/ppermute | solution.py:67
  106.4 8.7 %collective-permute-start.13 = (bf16[128,1024]{1,0:T(8,128)(2,1)S(1)}, bf16[128,1024]{1,0:T(8,128)(2,1)S(1)}, u32[]{:S(2)}, u32[]{:S(2)}) collective-permute-start(bf16[128,1024]{1,0:T(8,128)(2,1)S(1)} %fusion.21), channel_id=1, source_target_pairs={{0,8},{1,9},{2,10},{3,11},{4,12},{5,13},{6,14},{7,15},{8,0},{9,1},... | collective-permute-start | bytes 786440 | tf_op jit(solution)/shard_map/ppermute | solution.py:67
  109.1 1.6 collective-permute-start.17
  109.2 14.8 %collective-permute-start.14 = (bf16[128,2048]{1,0:T(8,128)(2,1)S(1)}, bf16[128,2048]{1,0:T(8,128)(2,1)S(1)}, u32[]{:S(2)}, u32[]{:S(2)}) collective-permute-start(bf16[128,2048]{1,0:T(8,128)(2,1)S(1)} %pad_maximum_fusion.9), channel_id=1, source_target_pairs={{0,16},{1,17},{2,18},{3,19},{4,20},{5,21},{6,22},{7,23},{8,24},{9,... | collective-permute-start | bytes 1572872 | tf_op jit(solution)/shard_map/ppermute | solution.py:67
  111.0 15.4 %collective-permute-start.29 = (bf16[128,1792]{1,0:T(8,128)(2,1)S(1)}, bf16[128,1792]{1,0:T(8,128)(2,1)S(1)}, u32[]{:S(2)}, u32[]{:S(2)}) collective-permute-start(bf16[128,1792]{1,0:T(8,128)(2,1)S(1)} %convolution_convert_fusion.15), channel_id=1, source_target_pairs={{0,2},{1,3},{2,4},{3,5},{4,6},{5,7},{6,0},{7,1},{8,10},{9,11},{10,... | collective-permute-start | bytes 1376264 | tf_op jit(solution)/shard_map/ppermute | solution.py:67
  112.9 22.3 %collective-permute-start.18 = (bf16[128,2048]{1,0:T(8,128)(2,1)S(1)}, bf16[128,2048]{1,0:T(8,128)(2,1)S(1)}, u32[]{:S(2)}, u32[]{:S(2)}) collective-permute-start(bf16[128,2048]{1,0:T(8,128)(2,1)S(1)} %pad_maximum_fusion.10), channel_id=1, source_target_pairs={{0,16},{1,17},{2,18},{3,19},{4,20},{5,21},{6,22},{7,23},{8,24},{9,... | collective-permute-start | bytes 1572872 | tf_op jit(solution)/shard_map/ppermute | solution.py:67
  113.7 32.4 %collective-permute-start.21 = (bf16[128,2048]{1,0:T(8,128)(2,1)S(1)}, bf16[128,2048]{1,0:T(8,128)(2,1)S(1)}, u32[]{:S(2)}, u32[]{:S(2)}) collective-permute-start(bf16[128,2048]{1,0:T(8,128)(2,1)S(1)} %pad_maximum_fusion.11), channel_id=1, source_target_pairs={{0,16},{1,17},{2,18},{3,19},{4,20},{5,21},{6,22},{7,23},{8,24},{9,... | collective-permute-start | bytes 1572872 | tf_op jit(solution)/shard_map/ppermute | solution.py:67
  124.3 10.9 %collective-permute-start.15 = (bf16[128,1024]{1,0:T(8,128)(2,1)S(1)}, bf16[128,1024]{1,0:T(8,128)(2,1)S(1)}, u32[]{:S(2)}, u32[]{:S(2)}) collective-permute-start(bf16[128,1024]{1,0:T(8,128)(2,1)S(1)} %fusion.20), channel_id=1, source_target_pairs={{0,8},{1,9},{2,10},{3,11},{4,12},{5,13},{6,14},{7,15},{8,0},{9,1},... | collective-permute-start | bytes 786440 | tf_op jit(solution)/shard_map/ppermute | solution.py:67
  126.3 1.6 collective-permute-start.28
  126.4 3.4 %collective-permute-start.25 = (bf16[64,1792]{1,0:T(8,128)(2,1)S(1)}, bf16[64,1792]{1,0:T(8,128)(2,1)S(1)}, u32[]{:S(2)}, u32[]{:S(2)}) collective-permute-start(bf16[64,1792]{1,0:T(8,128)(2,1)S(1)} %get-tuple-element.102), channel_id=1, source_target_pairs={{0,1},{1,0},{2,3},{3,2},{4,5},{5,4},{6,7},{7,6},{8,9},{9,8},{10,11... | collective-permute-start | bytes 688136 | tf_op jit(solution)/shard_map/ppermute | solution.py:67
  128.2 20.5 %collective-permute-start.30 = (bf16[128,1792]{1,0:T(8,128)(2,1)S(1)}, bf16[128,1792]{1,0:T(8,128)(2,1)S(1)}, u32[]{:S(2)}, u32[]{:S(2)}) collective-permute-start(bf16[128,1792]{1,0:T(8,128)(2,1)S(1)} %convolution_convert_fusion.13), channel_id=1, source_target_pairs={{0,2},{1,3},{2,4},{3,5},{4,6},{5,7},{6,0},{7,1},{8,10},{9,11},{10,... | collective-permute-start | bytes 1376264 | tf_op jit(solution)/shard_map/ppermute | solution.py:67
  130.1 27.8 %collective-permute-start.26 = (bf16[128,1792]{1,0:T(8,128)(2,1)S(1)}, bf16[128,1792]{1,0:T(8,128)(2,1)S(1)}, u32[]{:S(2)}, u32[]{:S(2)}) collective-permute-start(bf16[128,1792]{1,0:T(8,128)(2,1)S(1)} %convolution_convert_fusion.14), channel_id=1, source_target_pairs={{0,6},{1,7},{2,0},{3,1},{4,2},{5,3},{6,4},{7,5},{8,14},{9,15},{10,... | collective-permute-start | bytes 1376264 | tf_op jit(solution)/shard_map/ppermute | solution.py:67
  136.3 9.8 %collective-permute-start.20 = (bf16[128,1024]{1,0:T(8,128)(2,1)S(1)}, bf16[128,1024]{1,0:T(8,128)(2,1)S(1)}, u32[]{:S(2)}, u32[]{:S(2)}) collective-permute-start(bf16[128,1024]{1,0:T(8,128)(2,1)S(1)} %fusion.19), channel_id=1, source_target_pairs={{0,8},{1,9},{2,10},{3,11},{4,12},{5,13},{6,14},{7,15},{8,0},{9,1},... | collective-permute-start | bytes 786440 | tf_op jit(solution)/shard_map/ppermute | solution.py:67
  137.5 10.9 %collective-permute-start.27 = (bf16[64,1792]{1,0:T(8,128)(2,1)S(1)}, bf16[64,1792]{1,0:T(8,128)(2,1)S(1)}, u32[]{:S(2)}, u32[]{:S(2)}) collective-permute-start(bf16[64,1792]{1,0:T(8,128)(2,1)S(1)} %get-tuple-element.98), channel_id=1, source_target_pairs={{0,1},{1,0},{2,3},{3,2},{4,5},{5,4},{6,7},{7,6},{8,9},{9,8},{10,11... | collective-permute-start | bytes 688136 | tf_op jit(solution)/shard_map/ppermute | solution.py:67
  146.1 21.5 %collective-permute-start.19 = (bf16[64,1792]{1,0:T(8,128)(2,1)S(1)}, bf16[64,1792]{1,0:T(8,128)(2,1)S(1)}, u32[]{:S(2)}, u32[]{:S(2)}) collective-permute-start(bf16[64,1792]{1,0:T(8,128)(2,1)S(1)} %get-tuple-element.96), channel_id=1, source_target_pairs={{0,1},{1,0},{2,3},{3,2},{4,5},{5,4},{6,7},{7,6},{8,9},{9,8},{10,11... | collective-permute-start | bytes 688136 | tf_op jit(solution)/shard_map/ppermute | solution.py:67
  146.4 8.8 %collective-permute-start.23 = (bf16[128,1024]{1,0:T(8,128)(2,1)S(1)}, bf16[128,1024]{1,0:T(8,128)(2,1)S(1)}, u32[]{:S(2)}, u32[]{:S(2)}) collective-permute-start(bf16[128,1024]{1,0:T(8,128)(2,1)S(1)} %fusion.18), channel_id=1, source_target_pairs={{0,8},{1,9},{2,10},{3,11},{4,12},{5,13},{6,14},{7,15},{8,0},{9,1},... | collective-permute-start | bytes 786440 | tf_op jit(solution)/shard_map/ppermute | solution.py:67
  148.4 1.6 collective-permute-start.22
  148.7 7.3 %collective-permute-start.32 = (bf16[64,1792]{1,0:T(8,128)(2,1)S(1)}, bf16[64,1792]{1,0:T(8,128)(2,1)S(1)}, u32[]{:S(2)}, u32[]{:S(2)}) collective-permute-start(bf16[64,1792]{1,0:T(8,128)(2,1)S(1)} %get-tuple-element.104), channel_id=1, source_target_pairs={{0,1},{1,0},{2,3},{3,2},{4,5},{5,4},{6,7},{7,6},{8,9},{9,8},{10,11... | collective-permute-start | bytes 688136 | tf_op jit(solution)/shard_map/ppermute | solution.py:67
  150.0 13.0 %collective-permute-start.31 = (bf16[128,1792]{1,0:T(8,128)(2,1)S(1)}, bf16[128,1792]{1,0:T(8,128)(2,1)S(1)}, u32[]{:S(2)}, u32[]{:S(2)}) collective-permute-start(bf16[128,1792]{1,0:T(8,128)(2,1)S(1)} %convolution_convert_fusion.12), channel_id=1, source_target_pairs={{0,6},{1,7},{2,0},{3,1},{4,2},{5,3},{6,4},{7,5},{8,14},{9,15},{10,... | collective-permute-start | bytes 1376264 | tf_op jit(solution)/shard_map/ppermute | solution.py:67
  155.9 2.0 %collective-permute-start.24 = (bf16[64,1792]{1,0:T(8,128)(2,1)S(1)}, bf16[64,1792]{1,0:T(8,128)(2,1)S(1)}, u32[]{:S(2)}, u32[]{:S(2)}) collective-permute-start(bf16[64,1792]{1,0:T(8,128)(2,1)S(1)} %get-tuple-element.94), channel_id=1, source_target_pairs={{0,1},{1,0},{2,3},{3,2},{4,5},{5,4},{6,7},{7,6},{8,9},{9,8},{10,11... | collective-permute-start | bytes 688136 | tf_op jit(solution)/shard_map/ppermute | solution.py:67
  156.3 19.8 %collective-permute-start.33 = (bf16[128,1792]{1,0:T(8,128)(2,1)S(1)}, bf16[128,1792]{1,0:T(8,128)(2,1)S(1)}, u32[]{:S(2)}, u32[]{:S(2)}) collective-permute-start(bf16[128,1792]{1,0:T(8,128)(2,1)S(1)} %fusion.11), channel_id=1, source_target_pairs={{0,2},{1,3},{2,4},{3,5},{4,6},{5,7},{6,0},{7,1},{8,10},{9,11},{10,... | collective-permute-start | bytes 1376264 | tf_op jit(solution)/shard_map/ppermute | solution.py:67
  163.3 13.3 %collective-permute-start.34 = (bf16[128,1792]{1,0:T(8,128)(2,1)S(1)}, bf16[128,1792]{1,0:T(8,128)(2,1)S(1)}, u32[]{:S(2)}, u32[]{:S(2)}) collective-permute-start(bf16[128,1792]{1,0:T(8,128)(2,1)S(1)} %add_convert_fusion.2), channel_id=1, source_target_pairs={{0,8},{1,9},{2,10},{3,11},{4,12},{5,13},{6,14},{7,15},{8,0},{9,1},... | collective-permute-start | bytes 1376264 | tf_op jit(solution)/shard_map/ppermute | solution.py:67
  165.5 21.1 %collective-permute-start.35 = (bf16[128,1792]{1,0:T(8,128)(2,1)S(1)}, bf16[128,1792]{1,0:T(8,128)(2,1)S(1)}, u32[]{:S(2)}, u32[]{:S(2)}) collective-permute-start(bf16[128,1792]{1,0:T(8,128)(2,1)S(1)} %add_convert_fusion.1), channel_id=1, source_target_pairs={{0,10},{1,11},{2,12},{3,13},{4,14},{5,15},{6,8},{7,9},{8,2},{9,3},... | collective-permute-start | bytes 1376264 | tf_op jit(solution)/shard_map/ppermute | solution.py:67
  186.7 0.9 copy-start.1

commit v17 on v16

--- a/solution.py
+++ b/solution.py
@@ -189,9 +189,8 @@
     middle[0], gates, ups = together((middle[0], gates, ups))
     part += [send(whole(q), flip=2) for q in range(2, chips)]
     middle[0] = send(middle[0], 1)
-    part[1] = before_down(0, part[1])
     down_product(0, 1)
-    middle[0] = before_weigh(0, middle[0])
+    middle[0], part[1] = before_weigh(0, (middle[0], part[1]))
     middle[1] = send(weigh(0, 1).astype(BF), 1)
     finish(1)
     down_product(1, 0)

time: 189 us -> 185 us (0.979)
  starting transfers between devices: 40 us -> 34.3 us
  waiting for transfers between devices: 115 us -> 118 us
    ppermute x36, starting transfers between devices: 40 us -> 34.3 us  [send(): lax.ppermute(value, ('dp', 'expert'), [(i * owners + j, (i ^ flip) * owne...]
    ppermute x36, waiting for transfers between devices: 115 us -> 118 us  [send(): lax.ppermute(value, ('dp', 'expert'), [(i * owners + j, (i ^ flip) * owne...]
  transfers between devices with their start and end apart: 36 -> 36, of which waited for: 17 -> 19; matrix products, arithmetic and copies ran while one was open for 15% -> 15% of each run, Pallas kernels for 0% -> 0%
where the time goes in v17:
time: 185 us
  waiting for transfers between devices  118 us (64%)
  starting transfers between devices  34.3 us (19%)
  matrix products  22.9 us (12%)
  local copies, waits for them, and re-layouts  5.58 us (3%)
  other arithmetic  3.94 us (2%)
    ppermute x36, waiting for transfers between devices, send(): lax.ppermute(value, ('dp', 'expert'), [(i * owners + j, (i ^ flip) * owne...  118 us
    ppermute x36, starting transfers between devices, send(): lax.ppermute(value, ('dp', 'expert'), [(i * owners + j, (i ^ flip) * owne...  34.3 us
    dot_general x3, matrix products, product(): jnp.dot(flat, weights[:, lo:hi], preferred_element_type=F32)  12.9 us
    dot_general x8, matrix products, down_product(): value = jnp.dot(hidden[q, g], downs, preferred_element_type=F32).astype(BF)  5.25 us
  transfers between devices with their start and end apart: 36, of which 19 were waited for; matrix products, arithmetic and copies ran while one was open for 15% of the time, Pallas kernels for 0%

profile of v17, /device:TPU:0, one launch (start us, length us, event | category | flops | bytes accessed | tf_op | source)
XLA Modules:
  0.0 185.1 jit_solution(16003164575472554567)
XLA Ops:
  0.0 0.8 convert_bitcast_fusion
  0.8 0.7 fusion.62
  1.5 1.4 constant_dynamic-slice_fusion.1
  3.0 3.0 %collective-permute-start = (bf16[136,1792]{1,0:T(8,128)(2,1)S(1)}, bf16[136,1792]{1,0:T(8,128)(2,1)S(1)}, u32[]{:S(2)}, u32[]{:S(2)}) collective-permute-start(bf16[136,1792]{1,0:T(8,128)(2,1)S(1)} %get-tuple-element.113), channel_id=1, source_target_pairs={{0,16},{1,17},{2,18},{3,19},{4,20},{5,21},{6,22},{7,23},{8,24},{9,... | collective-permute-start | bytes 1462280 | tf_op jit(solution)/shard_map/ppermute | solution.py:67
  6.0 1.6 collective-permute-start.1
  7.6 1.5 collective-permute-start.9
  9.1 8.0 %collective-permute-done = bf16[136,1792]{1,0:T(8,128)(2,1)S(1)} collective-permute-done((bf16[136,1792]{1,0:T(8,128)(2,1)S(1)}, bf16[136,1792]{1,0:T(8,128)(2,1)S(1)}, u32[]{:S(2)}, u32[]{:S(2)}) %collective-permute-start) | collective-permute-done | bytes 487456 | tf_op jit(solution)/shard_map/ppermute | solution.py:67
  17.1 3.8 %collective-permute-start.3 = (bf16[136,1792]{1,0:T(8,128)(2,1)S(1)}, bf16[136,1792]{1,0:T(8,128)(2,1)S(1)}, u32[]{:S(2)}, u32[]{:S(2)}) collective-permute-start(bf16[136,1792]{1,0:T(8,128)(2,1)S(1)} %get-tuple-element.41), channel_id=1, source_target_pairs={{0,6},{1,7},{2,0},{3,1},{4,2},{5,3},{6,4},{7,5},{8,14},{9,15},{10,... | collective-permute-start | bytes 1462280 | tf_op jit(solution)/shard_map/ppermute | solution.py:67
  21.0 0.5 collective-permute-start.7
  21.5 1.0 slice_bitcast_fusion.2
  22.6 1.6 collective-permute-start.4
  24.3 0.7 slice_bitcast_fusion.28
  25.0 7.6 %collective-permute-done.3 = bf16[136,1792]{1,0:T(8,128)(2,1)S(1)} collective-permute-done((bf16[136,1792]{1,0:T(8,128)(2,1)S(1)}, bf16[136,1792]{1,0:T(8,128)(2,1)S(1)}, u32[]{:S(2)}, u32[]{:S(2)}) %collective-permute-start.3) | collective-permute-done | bytes 487456 | tf_op jit(solution)/shard_map/ppermute | solution.py:67
  32.6 1.6 collective-permute-start.6
  34.1 28.7 %collective-permute-done.2 = bf16[136,1792]{1,0:T(8,128)(2,1)S(1)} collective-permute-done((bf16[136,1792]{1,0:T(8,128)(2,1)}, bf16[136,1792]{1,0:T(8,128)(2,1)S(1)}, u32[]{:S(2)}, u32[]{:S(2)}) %collective-permute-start.2) | collective-permute-done | bytes 487456 | tf_op jit(solution)/shard_map/ppermute | solution.py:67
  62.8 1.7 collective-permute-start.5
  64.7 8.1 %collective-permute-done.6 = bf16[1024,896]{1,0:T(8,128)(2,1)S(1)} collective-permute-done((bf16[1024,896]{1,0:T(8,128)(2,1)S(1)}, bf16[1024,896]{1,0:T(8,128)(2,1)S(1)}, u32[]{:S(2)}, u32[]{:S(2)}) %collective-permute-start.6) | collective-permute-done | bytes 1835040 | tf_op jit(solution)/shard_map/ppermute | solution.py:67
  73.0 4.6 %collective-permute-done.5 = bf16[136,1792]{1,0:T(8,128)(2,1)S(1)} collective-permute-done((bf16[136,1792]{1,0:T(8,128)(2,1)S(1)}, bf16[136,1792]{1,0:T(8,128)(2,1)S(1)}, u32[]{:S(2)}, u32[]{:S(2)}) %collective-permute-start.5) | collective-permute-done | bytes 487456 | tf_op jit(solution)/shard_map/ppermute | solution.py:67
  78.0 0.4 convolution_convert_fusion
  78.7 0.4 convolution_convert_fusion.2
  79.2 0.6 collective-permute-start.8
  79.7 1.5 collective-permute-start.15
  81.2 0.4 convolution_convert_fusion.1
  81.7 0.4 convolution_convert_fusion.3
  82.4 6.2 %collective-permute-done.9 = bf16[896,2048]{1,0:T(8,128)(2,1)} collective-permute-done((bf16[896,2048]{1,0:T(8,128)(2,1)}, bf16[896,2048]{1,0:T(8,128)(2,1)}, u32[]{:S(2)}, u32[]{:S(2)}) %collective-permute-start.9) | collective-permute-done | bytes 3670048 | tf_op jit(solution)/shard_map/ppermute | solution.py:67
  88.6 3.6 %fusion.15 = bf16[4,128,1024]{2,1,0:T(8,128)(2,1)S(1)} fusion(bf16[4,128,1792]{2,1,0:T(8,128)(2,1)S(1)} %pad_maximum_fusion.4, bf16[896,2048]{1,0:T(8,128)(2,1)S(1)} %bitcast.131, bf16[896,2048]{1,0:T(8,128)(2,1)} %collective-permute-done.9), kind=kOutput, calls=%fused_computation.39 | convolution fusion | flops 1886912512 | bytes 10223616 | tf_op jit(solution)/shard_map/dot_general | solution.py:134
  92.2 0.6 collective-permute-start.11
  92.8 3.6 %fusion.12 = bf16[4,128,1024]{2,1,0:T(8,128)(2,1)S(1)} fusion(bf16[4,128,1792]{2,1,0:T(8,128)(2,1)S(1)} %pad_maximum_fusion.4, bf16[896,2048]{1,0:T(8,128)(2,1)S(1)} %bitcast.132, bf16[896,2048]{1,0:T(8,128)(2,1)} %collective-permute-done.9), kind=kOutput, calls=%fused_computation.38 | convolution fusion | flops 1886912512 | bytes 10223616 | tf_op jit(solution)/shard_map/dot_general | solution.py:134
  96.4 1.6 collective-permute-start.12
  98.0 2.4 %collective-permute-done.11 = bf16[128,1024]{1,0:T(8,128)(2,1)S(1)} collective-permute-done((bf16[128,1024]{1,0:T(8,128)(2,1)S(1)}, bf16[128,1024]{1,0:T(8,128)(2,1)S(1)}, u32[]{:S(2)}, u32[]{:S(2)}) %collective-permute-start.11) | collective-permute-done | bytes 262176 | tf_op jit(solution)/shard_map/ppermute | solution.py:67
  100.4 5.7 %fusion = f32[512,2048]{1,0:T(8,128)S(1)} fusion(bf16[512,1792]{1,0:T(8,128)(2,1)S(1)} %bitcast.120, bf16[896,2048]{1,0:T(8,128)(2,1)} %collective-permute-done.9, bf16[896,2048]{1,0:T(8,128)(2,1)S(1)} %bitcast.133), kind=kOutput, calls=%fused_computation.5 | convolution fusion | flops 3772776448 | bytes 13369344 | tf_op jit(solution)/shard_map/dot_general | solution.py:134
  106.4 1.6 collective-permute-start.13
  108.4 0.7 convolution_convert_fusion.10
  109.3 1.3 collective-permute-done.16
  111.0 1.8 collective-permute-start.17
  112.9 0.8 collective-permute-start.20
  113.7 0.7 convolution_convert_fusion.11
  114.5 1.4 collective-permute-start.23
  115.9 8.1 %collective-permute-done.18 = bf16[128,2048]{1,0:T(8,128)(2,1)S(1)} collective-permute-done((bf16[128,2048]{1,0:T(8,128)(2,1)S(1)}, bf16[128,2048]{1,0:T(8,128)(2,1)S(1)}, u32[]{:S(2)}, u32[]{:S(2)}) %collective-permute-start.18) | collective-permute-done | bytes 524320 | tf_op jit(solution)/shard_map/ppermute | solution.py:67
  124.0 1.6 collective-permute-done.17
  125.9 0.6 collective-permute-start.19
  126.4 0.7 convolution_convert_fusion.6
  127.6 1.1 collective-permute-done.27
  129.0 2.8 %collective-permute-start.28 = (bf16[128,1792]{1,0:T(8,128)(2,1)S(1)}, bf16[128,1792]{1,0:T(8,128)(2,1)S(1)}, u32[]{:S(2)}, u32[]{:S(2)}) collective-permute-start(bf16[128,1792]{1,0:T(8,128)(2,1)S(1)} %convolution_convert_fusion.14), channel_id=1, source_target_pairs={{0,6},{1,7},{2,0},{3,1},{4,2},{5,3},{6,4},{7,5},{8,14},{9,15},{10,... | collective-permute-start | bytes 1376264 | tf_op jit(solution)/shard_map/ppermute | solution.py:67
  131.8 3.5 %collective-permute-done.20 = bf16[128,2048]{1,0:T(8,128)(2,1)S(1)} collective-permute-done((bf16[128,2048]{1,0:T(8,128)(2,1)S(1)}, bf16[128,2048]{1,0:T(8,128)(2,1)S(1)}, u32[]{:S(2)}, u32[]{:S(2)}) %collective-permute-start.20) | collective-permute-done | bytes 524320 | tf_op jit(solution)/shard_map/ppermute | solution.py:67
  135.6 0.6 collective-permute-start.22
  136.2 0.7 convolution_convert_fusion.9
  136.8 0.7 convolution_convert_fusion.5
  137.6 5.1 %collective-permute-done.30 = bf16[128,1792]{1,0:T(8,128)(2,1)S(1)} collective-permute-done((bf16[128,1792]{1,0:T(8,128)(2,1)S(1)}, bf16[128,1792]{1,0:T(8,128)(2,1)S(1)}, u32[]{:S(2)}, u32[]{:S(2)}) %collective-permute-start.30) | collective-permute-done | bytes 458784 | tf_op jit(solution)/shard_map/ppermute | solution.py:67
  143.2 2.9 %collective-permute-done.23 = bf16[128,2048]{1,0:T(8,128)(2,1)S(1)} collective-permute-done((bf16[128,2048]{1,0:T(8,128)(2,1)S(1)}, bf16[128,2048]{1,0:T(8,128)(2,1)S(1)}, u32[]{:S(2)}, u32[]{:S(2)}) %collective-permute-start.23) | collective-permute-done | bytes 524320 | tf_op jit(solution)/shard_map/ppermute | solution.py:67
  146.4 0.6 collective-permute-start.25
  147.0 0.7 convolution_convert_fusion.4
  147.7 0.7 convolution_convert_fusion.8
  148.5 1.4 collective-permute-done.24
  150.1 4.3 %collective-permute-done.25 = bf16[128,1024]{1,0:T(8,128)(2,1)S(1)} collective-permute-done((bf16[128,1024]{1,0:T(8,128)(2,1)S(1)}, bf16[128,1024]{1,0:T(8,128)(2,1)S(1)}, u32[]{:S(2)}, u32[]{:S(2)}) %collective-permute-start.25) | collective-permute-done | bytes 262176 | tf_op jit(solution)/shard_map/ppermute | solution.py:67
  154.4 0.7 convolution_convert_fusion.7
  155.5 1.6 collective-permute-start.33
  157.1 4.2 %collective-permute-done.31 = bf16[128,1792]{1,0:T(8,128)(2,1)S(1)} collective-permute-done((bf16[128,1792]{1,0:T(8,128)(2,1)S(1)}, bf16[128,1792]{1,0:T(8,128)(2,1)S(1)}, u32[]{:S(2)}, u32[]{:S(2)}) %collective-permute-start.31) | collective-permute-done | bytes 458784 | tf_op jit(solution)/shard_map/ppermute | solution.py:67
  161.6 1.6 collective-permute-start.34
  163.5 0.6 collective-permute-start.35
  164.1 8.1 %collective-permute-done.33 = bf16[128,1792]{1,0:T(8,128)(2,1)S(1)} collective-permute-done((bf16[128,1792]{1,0:T(8,128)(2,1)S(1)}, bf16[128,1792]{1,0:T(8,128)(2,1)S(1)}, u32[]{:S(2)}, u32[]{:S(2)}) %collective-permute-start.33) | collective-permute-done | bytes 458784 | tf_op jit(solution)/shard_map/ppermute | solution.py:67
  172.7 10.6 %collective-permute-done.34 = bf16[128,1792]{1,0:T(8,128)(2,1)S(1)} collective-permute-done((bf16[128,1792]{1,0:T(8,128)(2,1)S(1)}, bf16[128,1792]{1,0:T(8,128)(2,1)S(1)}, u32[]{:S(2)}, u32[]{:S(2)}) %collective-permute-start.34) | collective-permute-done | bytes 458784 | tf_op jit(solution)/shard_map/ppermute | solution.py:67
  183.5 0.9 copy-done.1
  184.4 0.7 slice_dynamic-update-slice_fusion
  (109 shorter events, 7.2 us)
Async XLA Ops:
  0.0 32.6 %copy-start = (bf16[1,1024,896]{2,1,0:T(8,128)(2,1)S(1)}, bf16[1,1024,896]{2,1,0:T(8,128)(2,1)}, u32[]{:S(2)}) copy-start(bf16[1,1024,896]{2,1,0:T(8,128)(2,1)} %param.7) | copy-start | bytes 5505028
  3.0 14.2 %collective-permute-start = (bf16[136,1792]{1,0:T(8,128)(2,1)S(1)}, bf16[136,1792]{1,0:T(8,128)(2,1)S(1)}, u32[]{:S(2)}, u32[]{:S(2)}) collective-permute-start(bf16[136,1792]{1,0:T(8,128)(2,1)S(1)} %get-tuple-element.113), channel_id=1, source_target_pairs={{0,16},{1,17},{2,18},{3,19},{4,20},{5,21},{6,22},{7,23},{8,24},{9,... | collective-permute-start | bytes 1462280 | tf_op jit(solution)/shard_map/ppermute | solution.py:67
  6.0 15.5 %collective-permute-start.1 = (bf16[136,1792]{1,0:T(8,128)(2,1)S(1)}, bf16[136,1792]{1,0:T(8,128)(2,1)}, u32[]{:S(2)}, u32[]{:S(2)}) collective-permute-start(bf16[136,1792]{1,0:T(8,128)(2,1)S(1)} %get-tuple-element.41), channel_id=1, source_target_pairs={{0,2},{1,3},{2,4},{3,5},{4,6},{5,7},{6,0},{7,1},{8,10},{9,11},{10,... | collective-permute-start | bytes 1462280 | tf_op jit(solution)/shard_map/ppermute | solution.py:67
  7.6 81.0 %collective-permute-start.9 = (bf16[896,2048]{1,0:T(8,128)(2,1)}, bf16[896,2048]{1,0:T(8,128)(2,1)}, u32[]{:S(2)}, u32[]{:S(2)}) collective-permute-start(bf16[896,2048]{1,0:T(8,128)(2,1)} %bitcast.130), channel_id=1, source_target_pairs={{0,8},{1,9},{2,10},{3,11},{4,12},{5,13},{6,14},{7,15},{8,0},{9,1},... | collective-permute-start | bytes 11010056 | tf_op jit(solution)/shard_map/ppermute | solution.py:67
  17.1 15.5 %collective-permute-start.3 = (bf16[136,1792]{1,0:T(8,128)(2,1)S(1)}, bf16[136,1792]{1,0:T(8,128)(2,1)S(1)}, u32[]{:S(2)}, u32[]{:S(2)}) collective-permute-start(bf16[136,1792]{1,0:T(8,128)(2,1)S(1)} %get-tuple-element.41), channel_id=1, source_target_pairs={{0,6},{1,7},{2,0},{3,1},{4,2},{5,3},{6,4},{7,5},{8,14},{9,15},{10,... | collective-permute-start | bytes 1462280 | tf_op jit(solution)/shard_map/ppermute | solution.py:67
  21.0 43.6 %collective-permute-start.7 = (bf16[136,1792]{1,0:T(8,128)(2,1)S(1)}, bf16[136,1792]{1,0:T(8,128)(2,1)S(1)}, u32[]{:S(2)}, u32[]{:S(2)}) collective-permute-start(bf16[136,1792]{1,0:T(8,128)(2,1)S(1)} %collective-permute-done), channel_id=1, source_target_pairs={{0,6},{1,7},{2,0},{3,1},{4,2},{5,3},{6,4},{7,5},{8,14},{9,15},{10,... | collective-permute-start | bytes 1462280 | tf_op jit(solution)/shard_map/ppermute | solution.py:67
  22.6 40.3 %collective-permute-start.4 = (bf16[136,1792]{1,0:T(8,128)(2,1)S(1)}, bf16[136,1792]{1,0:T(8,128)(2,1)S(1)}, u32[]{:S(2)}, u32[]{:S(2)}) collective-permute-start(bf16[136,1792]{1,0:T(8,128)(2,1)S(1)} %collective-permute-done), channel_id=1, source_target_pairs={{0,2},{1,3},{2,4},{3,5},{4,6},{5,7},{6,0},{7,1},{8,10},{9,11},{10,... | collective-permute-start | bytes 1462280 | tf_op jit(solution)/shard_map/ppermute | solution.py:67
  24.2 38.6 %collective-permute-start.2 = (bf16[136,1792]{1,0:T(8,128)(2,1)}, bf16[136,1792]{1,0:T(8,128)(2,1)S(1)}, u32[]{:S(2)}, u32[]{:S(2)}) collective-permute-start(bf16[136,1792]{1,0:T(8,128)(2,1)} %collective-permute-done.1), channel_id=1, source_target_pairs={{0,2},{1,3},{2,4},{3,5},{4,6},{5,7},{6,0},{7,1},{8,10},{9,11},{10,... | collective-permute-start | bytes 1462280 | tf_op jit(solution)/shard_map/ppermute | solution.py:67
  32.6 40.2 %collective-permute-start.6 = (bf16[1024,896]{1,0:T(8,128)(2,1)S(1)}, bf16[1024,896]{1,0:T(8,128)(2,1)S(1)}, u32[]{:S(2)}, u32[]{:S(2)}) collective-permute-start(bf16[1024,896]{1,0:T(8,128)(2,1)S(1)} %bitcast.118), channel_id=1, source_target_pairs={{0,16},{1,17},{2,18},{3,19},{4,20},{5,21},{6,22},{7,23},{8,24},{9,... | collective-permute-start | bytes 5505032 | tf_op jit(solution)/shard_map/ppermute | solution.py:67
  62.8 14.8 %collective-permute-start.5 = (bf16[136,1792]{1,0:T(8,128)(2,1)S(1)}, bf16[136,1792]{1,0:T(8,128)(2,1)S(1)}, u32[]{:S(2)}, u32[]{:S(2)}) collective-permute-start(bf16[136,1792]{1,0:T(8,128)(2,1)S(1)} %collective-permute-done.4), channel_id=1, source_target_pairs={{0,2},{1,3},{2,4},{3,5},{4,6},{5,7},{6,0},{7,1},{8,10},{9,11},{10,... | collective-permute-start | bytes 1462280 | tf_op jit(solution)/shard_map/ppermute | solution.py:67
  78.4 3.7 %collective-permute-start.10 = (bf16[4,64,1792]{2,1,0:T(8,128)(2,1)S(1)}, bf16[4,64,1792]{2,1,0:T(8,128)(2,1)S(1)}, u32[]{:S(2)}, u32[]{:S(2)}) collective-permute-start(bf16[4,64,1792]{2,1,0:T(8,128)(2,1)S(1)} %convolution_convert_fusion), channel_id=1, source_target_pairs={{0,1},{1,0},{2,3},{3,2},{4,5},{5,4},{6,7},{7,6},{8,9},{9,8},{10,11... | collective-permute-start | bytes 2752520 | tf_op jit(solution)/shard_map/ppermute | solution.py:67
  79.2 3.1 %collective-permute-start.8 = (bf16[4,64,1792]{2,1,0:T(8,128)(2,1)S(1)}, bf16[4,64,1792]{2,1,0:T(8,128)(2,1)S(1)}, u32[]{:S(2)}, u32[]{:S(2)}) collective-permute-start(bf16[4,64,1792]{2,1,0:T(8,128)(2,1)S(1)} %convolution_convert_fusion.2), channel_id=1, source_target_pairs={{0,1},{1,0},{2,3},{3,2},{4,5},{5,4},{6,7},{7,6},{8,9},{9,8},{10,11... | collective-permute-start | bytes 2752520 | tf_op jit(solution)/shard_map/ppermute | solution.py:67
  79.7 28.3 %collective-permute-start.15 = (bf16[4,8,256]{2,1,0:T(8,128)(2,1)S(1)}, bf16[4,8,256]{2,1,0:T(8,128)(2,1)S(1)}, u32[]{:S(2)}, u32[]{:S(2)}) collective-permute-start(bf16[4,8,256]{2,1,0:T(8,128)(2,1)S(1)} %pad_maximum_fusion.16), channel_id=1, source_target_pairs={{0,8},{1,9},{2,10},{3,11},{4,12},{5,13},{6,14},{7,15},{8,0},{9,1},... | collective-permute-start | bytes 49160 | tf_op jit(solution)/shard_map/ppermute | solution.py:67
  82.1 6.5 %copy-start.2 = (bf16[1,896,2048]{2,1,0:T(8,128)(2,1)S(1)}, bf16[1,896,2048]{2,1,0:T(8,128)(2,1)}, u32[]{:S(2)}) copy-start(bf16[1,896,2048]{2,1,0:T(8,128)(2,1)} %param.6) | copy-start | bytes 11010052
  92.2 8.1 %collective-permute-start.11 = (bf16[128,1024]{1,0:T(8,128)(2,1)S(1)}, bf16[128,1024]{1,0:T(8,128)(2,1)S(1)}, u32[]{:S(2)}, u32[]{:S(2)}) collective-permute-start(bf16[128,1024]{1,0:T(8,128)(2,1)S(1)} %slice_bitcast_fusion.15), channel_id=1, source_target_pairs={{0,16},{1,17},{2,18},{3,19},{4,20},{5,21},{6,22},{7,23},{8,24},{9,... | collective-permute-start | bytes 786440 | tf_op jit(solution)/shard_map/ppermute | solution.py:67
  96.4 9.8 %collective-permute-start.12 = (bf16[128,1024]{1,0:T(8,128)(2,1)S(1)}, bf16[128,1024]{1,0:T(8,128)(2,1)S(1)}, u32[]{:S(2)}, u32[]{:S(2)}) collective-permute-start(bf16[128,1024]{1,0:T(8,128)(2,1)S(1)} %slice_bitcast_fusion.12), channel_id=1, source_target_pairs={{0,16},{1,17},{2,18},{3,19},{4,20},{5,21},{6,22},{7,23},{8,24},{9,... | collective-permute-start | bytes 786440 | tf_op jit(solution)/shard_map/ppermute | solution.py:67
  106.4 7.3 %collective-permute-start.13 = (bf16[128,1024]{1,0:T(8,128)(2,1)S(1)}, bf16[128,1024]{1,0:T(8,128)(2,1)S(1)}, u32[]{:S(2)}, u32[]{:S(2)}) collective-permute-start(bf16[128,1024]{1,0:T(8,128)(2,1)S(1)} %fusion.21), channel_id=1, source_target_pairs={{0,8},{1,9},{2,10},{3,11},{4,12},{5,13},{6,14},{7,15},{8,0},{9,1},... | collective-permute-start | bytes 786440 | tf_op jit(solution)/shard_map/ppermute | solution.py:67
  109.1 1.6 collective-permute-start.16
  109.2 14.8 %collective-permute-start.18 = (bf16[128,2048]{1,0:T(8,128)(2,1)S(1)}, bf16[128,2048]{1,0:T(8,128)(2,1)S(1)}, u32[]{:S(2)}, u32[]{:S(2)}) collective-permute-start(bf16[128,2048]{1,0:T(8,128)(2,1)S(1)} %pad_maximum_fusion.9), channel_id=1, source_target_pairs={{0,16},{1,17},{2,18},{3,19},{4,20},{5,21},{6,22},{7,23},{8,24},{9,... | collective-permute-start | bytes 1572872 | tf_op jit(solution)/shard_map/ppermute | solution.py:67
  111.0 14.6 %collective-permute-start.17 = (bf16[128,1792]{1,0:T(8,128)(2,1)S(1)}, bf16[128,1792]{1,0:T(8,128)(2,1)S(1)}, u32[]{:S(2)}, u32[]{:S(2)}) collective-permute-start(bf16[128,1792]{1,0:T(8,128)(2,1)S(1)} %convolution_convert_fusion.15), channel_id=1, source_target_pairs={{0,2},{1,3},{2,4},{3,5},{4,6},{5,7},{6,0},{7,1},{8,10},{9,11},{10,... | collective-permute-start | bytes 1376264 | tf_op jit(solution)/shard_map/ppermute | solution.py:67
  112.9 22.3 %collective-permute-start.20 = (bf16[128,2048]{1,0:T(8,128)(2,1)S(1)}, bf16[128,2048]{1,0:T(8,128)(2,1)S(1)}, u32[]{:S(2)}, u32[]{:S(2)}) collective-permute-start(bf16[128,2048]{1,0:T(8,128)(2,1)S(1)} %pad_maximum_fusion.10), channel_id=1, source_target_pairs={{0,16},{1,17},{2,18},{3,19},{4,20},{5,21},{6,22},{7,23},{8,24},{9,... | collective-permute-start | bytes 1572872 | tf_op jit(solution)/shard_map/ppermute | solution.py:67
  114.4 1.6 collective-permute-start.14
  114.5 31.6 %collective-permute-start.23 = (bf16[128,2048]{1,0:T(8,128)(2,1)S(1)}, bf16[128,2048]{1,0:T(8,128)(2,1)S(1)}, u32[]{:S(2)}, u32[]{:S(2)}) collective-permute-start(bf16[128,2048]{1,0:T(8,128)(2,1)S(1)} %pad_maximum_fusion.11), channel_id=1, source_target_pairs={{0,16},{1,17},{2,18},{3,19},{4,20},{5,21},{6,22},{7,23},{8,24},{9,... | collective-permute-start | bytes 1572872 | tf_op jit(solution)/shard_map/ppermute | solution.py:67
  125.9 9.4 %collective-permute-start.19 = (bf16[128,1024]{1,0:T(8,128)(2,1)S(1)}, bf16[128,1024]{1,0:T(8,128)(2,1)S(1)}, u32[]{:S(2)}, u32[]{:S(2)}) collective-permute-start(bf16[128,1024]{1,0:T(8,128)(2,1)S(1)} %fusion.20), channel_id=1, source_target_pairs={{0,8},{1,9},{2,10},{3,11},{4,12},{5,13},{6,14},{7,15},{8,0},{9,1},... | collective-permute-start | bytes 786440 | tf_op jit(solution)/shard_map/ppermute | solution.py:67
  127.1 1.6 collective-permute-start.27
  127.5 15.2 %collective-permute-start.30 = (bf16[128,1792]{1,0:T(8,128)(2,1)S(1)}, bf16[128,1792]{1,0:T(8,128)(2,1)S(1)}, u32[]{:S(2)}, u32[]{:S(2)}) collective-permute-start(bf16[128,1792]{1,0:T(8,128)(2,1)S(1)} %convolution_convert_fusion.13), channel_id=1, source_target_pairs={{0,2},{1,3},{2,4},{3,5},{4,6},{5,7},{6,0},{7,1},{8,10},{9,11},{10,... | collective-permute-start | bytes 1376264 | tf_op jit(solution)/shard_map/ppermute | solution.py:67
  129.0 28.1 %collective-permute-start.28 = (bf16[128,1792]{1,0:T(8,128)(2,1)S(1)}, bf16[128,1792]{1,0:T(8,128)(2,1)S(1)}, u32[]{:S(2)}, u32[]{:S(2)}) collective-permute-start(bf16[128,1792]{1,0:T(8,128)(2,1)S(1)} %convolution_convert_fusion.14), channel_id=1, source_target_pairs={{0,6},{1,7},{2,0},{3,1},{4,2},{5,3},{6,4},{7,5},{8,14},{9,15},{10,... | collective-permute-start | bytes 1376264 | tf_op jit(solution)/shard_map/ppermute | solution.py:67
  135.6 10.5 %collective-permute-start.22 = (bf16[128,1024]{1,0:T(8,128)(2,1)S(1)}, bf16[128,1024]{1,0:T(8,128)(2,1)S(1)}, u32[]{:S(2)}, u32[]{:S(2)}) collective-permute-start(bf16[128,1024]{1,0:T(8,128)(2,1)S(1)} %fusion.19), channel_id=1, source_target_pairs={{0,8},{1,9},{2,10},{3,11},{4,12},{5,13},{6,14},{7,15},{8,0},{9,1},... | collective-permute-start | bytes 786440 | tf_op jit(solution)/shard_map/ppermute | solution.py:67
  137.5 5.2 %collective-permute-start.29 = (bf16[64,1792]{1,0:T(8,128)(2,1)S(1)}, bf16[64,1792]{1,0:T(8,128)(2,1)S(1)}, u32[]{:S(2)}, u32[]{:S(2)}) collective-permute-start(bf16[64,1792]{1,0:T(8,128)(2,1)S(1)} %get-tuple-element.96), channel_id=1, source_target_pairs={{0,1},{1,0},{2,3},{3,2},{4,5},{5,4},{6,7},{7,6},{8,9},{9,8},{10,11... | collective-permute-start | bytes 688136 | tf_op jit(solution)/shard_map/ppermute | solution.py:67
  142.8 21.4 %collective-permute-start.21 = (bf16[64,1792]{1,0:T(8,128)(2,1)S(1)}, bf16[64,1792]{1,0:T(8,128)(2,1)S(1)}, u32[]{:S(2)}, u32[]{:S(2)}) collective-permute-start(bf16[64,1792]{1,0:T(8,128)(2,1)S(1)} %get-tuple-element.94), channel_id=1, source_target_pairs={{0,1},{1,0},{2,3},{3,2},{4,5},{5,4},{6,7},{7,6},{8,9},{9,8},{10,11... | collective-permute-start | bytes 688136 | tf_op jit(solution)/shard_map/ppermute | solution.py:67
  143.1 18.2 %collective-permute-start.31 = (bf16[128,1792]{1,0:T(8,128)(2,1)S(1)}, bf16[128,1792]{1,0:T(8,128)(2,1)S(1)}, u32[]{:S(2)}, u32[]{:S(2)}) collective-permute-start(bf16[128,1792]{1,0:T(8,128)(2,1)S(1)} %convolution_convert_fusion.12), channel_id=1, source_target_pairs={{0,6},{1,7},{2,0},{3,1},{4,2},{5,3},{6,4},{7,5},{8,14},{9,15},{10,... | collective-permute-start | bytes 1376264 | tf_op jit(solution)/shard_map/ppermute | solution.py:67
  146.4 8.0 %collective-permute-start.25 = (bf16[128,1024]{1,0:T(8,128)(2,1)S(1)}, bf16[128,1024]{1,0:T(8,128)(2,1)S(1)}, u32[]{:S(2)}, u32[]{:S(2)}) collective-permute-start(bf16[128,1024]{1,0:T(8,128)(2,1)S(1)} %fusion.18), channel_id=1, source_target_pairs={{0,8},{1,9},{2,10},{3,11},{4,12},{5,13},{6,14},{7,15},{8,0},{9,1},... | collective-permute-start | bytes 786440 | tf_op jit(solution)/shard_map/ppermute | solution.py:67
  148.4 1.6 collective-permute-start.24
  149.9 5.3 %collective-permute-start.32 = (bf16[64,1792]{1,0:T(8,128)(2,1)S(1)}, bf16[64,1792]{1,0:T(8,128)(2,1)S(1)}, u32[]{:S(2)}, u32[]{:S(2)}) collective-permute-start(bf16[64,1792]{1,0:T(8,128)(2,1)S(1)} %get-tuple-element.102), channel_id=1, source_target_pairs={{0,1},{1,0},{2,3},{3,2},{4,5},{5,4},{6,7},{7,6},{8,9},{9,8},{10,11... | collective-permute-start | bytes 688136 | tf_op jit(solution)/shard_map/ppermute | solution.py:67
  155.1 6.2 %collective-permute-start.26 = (bf16[64,1792]{1,0:T(8,128)(2,1)S(1)}, bf16[64,1792]{1,0:T(8,128)(2,1)S(1)}, u32[]{:S(2)}, u32[]{:S(2)}) collective-permute-start(bf16[64,1792]{1,0:T(8,128)(2,1)S(1)} %get-tuple-element.92), channel_id=1, source_target_pairs={{0,1},{1,0},{2,3},{3,2},{4,5},{5,4},{6,7},{7,6},{8,9},{9,8},{10,11... | collective-permute-start | bytes 688136 | tf_op jit(solution)/shard_map/ppermute | solution.py:67
  155.5 16.7 %collective-permute-start.33 = (bf16[128,1792]{1,0:T(8,128)(2,1)S(1)}, bf16[128,1792]{1,0:T(8,128)(2,1)S(1)}, u32[]{:S(2)}, u32[]{:S(2)}) collective-permute-start(bf16[128,1792]{1,0:T(8,128)(2,1)S(1)} %fusion.11), channel_id=1, source_target_pairs={{0,2},{1,3},{2,4},{3,5},{4,6},{5,7},{6,0},{7,1},{8,10},{9,11},{10,... | collective-permute-start | bytes 1376264 | tf_op jit(solution)/shard_map/ppermute | solution.py:67
  161.6 21.7 %collective-permute-start.34 = (bf16[128,1792]{1,0:T(8,128)(2,1)S(1)}, bf16[128,1792]{1,0:T(8,128)(2,1)S(1)}, u32[]{:S(2)}, u32[]{:S(2)}) collective-permute-start(bf16[128,1792]{1,0:T(8,128)(2,1)S(1)} %add_convert_fusion.2), channel_id=1, source_target_pairs={{0,8},{1,9},{2,10},{3,11},{4,12},{5,13},{6,14},{7,15},{8,0},{9,1},... | collective-permute-start | bytes 1376264 | tf_op jit(solution)/shard_map/ppermute | solution.py:67
  163.5 19.8 %collective-permute-start.35 = (bf16[128,1792]{1,0:T(8,128)(2,1)S(1)}, bf16[128,1792]{1,0:T(8,128)(2,1)S(1)}, u32[]{:S(2)}, u32[]{:S(2)}) collective-permute-start(bf16[128,1792]{1,0:T(8,128)(2,1)S(1)} %add_convert_fusion.1), channel_id=1, source_target_pairs={{0,10},{1,11},{2,12},{3,13},{4,14},{5,15},{6,8},{7,9},{8,2},{9,3},... | collective-permute-start | bytes 1376264 | tf_op jit(solution)/shard_map/ppermute | solution.py:67
  183.5 0.9 copy-start.1

commit v18 on v17

--- a/solution.py
+++ b/solution.py
@@ -159,7 +159,9 @@
     def finish(q):
         gu = near[order[q]] + part[q].astype(F32)
         own = (jax.nn.silu(gu[:, :ff]) * gu[:, ff:]).astype(BF)
-        hidden[q, 0], hidden[q, 1] = own, send(own, flip=1)
+        hidden[q, 0] = own
+        if q > 0:
+            hidden[q, 1] = send(own, flip=1)
 
     def down_product(q, g):
         value = jnp.dot(hidden[q, g], downs, preferred_element_type=F32).astype(BF)
@@ -184,6 +186,8 @@
     finish(0)
     hidden[0, 0], info_x = together((hidden[0, 0], info_x))
     down_product(0, 0)
+    out[0, 0], own = together((out[0, 0], hidden[0, 0]))
+    hidden[0, 1] = send(own, flip=1)
     pays.append(places(info_x)[1])
     middle[0] = weigh(0, 0).astype(BF)
     middle[0], gates, ups = together((middle[0], gates, ups))

time: 185 us -> 197 us (1.065)
  starting transfers between devices: 34.3 us -> 47.2 us
  waiting for transfers between devices: 118 us -> 116 us
    ppermute x36, starting transfers between devices: 34.3 us -> 47.2 us  [send(): lax.ppermute(value, ('dp', 'expert'), [(i * owners + j, (i ^ flip) * owne...]
  transfers between devices with their start and end apart: 36 -> 36, of which waited for: 19 -> 20; matrix products, arithmetic and copies ran while one was open for 15% -> 14% of each run, Pallas kernels for 0% -> 0%
where the time goes in v18:
time: 197 us; the launch traced here: 196 us
  waiting for transfers between devices  116 us (59%)
  starting transfers between devices  47.2 us (24%)
  matrix products  22.9 us (12%)
  local copies, waits for them, and re-layouts  5.58 us (3%)
  other arithmetic  3.94 us (2%)
    ppermute x36, waiting for transfers between devices, send(): lax.ppermute(value, ('dp', 'expert'), [(i * owners + j, (i ^ flip) * owne...  116 us
    ppermute x36, starting transfers between devices, send(): lax.ppermute(value, ('dp', 'expert'), [(i * owners + j, (i ^ flip) * owne...  47.2 us
    dot_general x3, matrix products, product(): jnp.dot(flat, weights[:, lo:hi], preferred_element_type=F32)  12.9 us
    dot_general x8, matrix products, down_product(): value = jnp.dot(hidden[q, g], downs, preferred_element_type=F32).astype(BF)  5.24 us
  transfers between devices with their start and end apart: 36, of which 20 were waited for; matrix products, arithmetic and copies ran while one was open for 14% of the time, Pallas kernels for 0%

profile of v18, /device:TPU:0, one launch (start us, length us, event | category | flops | bytes accessed | tf_op | source)
XLA Modules:
  0.0 196.5 jit_solution(8364346928524055070)
XLA Ops:
  0.0 0.8 convert_bitcast_fusion
  0.8 0.7 fusion.62
  1.5 1.4 constant_dynamic-slice_fusion.1
  3.0 3.0 %collective-permute-start = (bf16[136,1792]{1,0:T(8,128)(2,1)S(1)}, bf16[136,1792]{1,0:T(8,128)(2,1)S(1)}, u32[]{:S(2)}, u32[]{:S(2)}) collective-permute-start(bf16[136,1792]{1,0:T(8,128)(2,1)S(1)} %get-tuple-element.117), channel_id=1, source_target_pairs={{0,16},{1,17},{2,18},{3,19},{4,20},{5,21},{6,22},{7,23},{8,24},{9,... | collective-permute-start | bytes 1462280 | tf_op jit(solution)/shard_map/ppermute | solution.py:67
  6.0 1.6 collective-permute-start.1
  7.6 1.5 collective-permute-start.9
  9.1 8.0 %collective-permute-done = bf16[136,1792]{1,0:T(8,128)(2,1)S(1)} collective-permute-done((bf16[136,1792]{1,0:T(8,128)(2,1)S(1)}, bf16[136,1792]{1,0:T(8,128)(2,1)S(1)}, u32[]{:S(2)}, u32[]{:S(2)}) %collective-permute-start) | collective-permute-done | bytes 487456 | tf_op jit(solution)/shard_map/ppermute | solution.py:67
  17.1 3.8 %collective-permute-start.3 = (bf16[136,1792]{1,0:T(8,128)(2,1)S(1)}, bf16[136,1792]{1,0:T(8,128)(2,1)S(1)}, u32[]{:S(2)}, u32[]{:S(2)}) collective-permute-start(bf16[136,1792]{1,0:T(8,128)(2,1)S(1)} %get-tuple-element.43), channel_id=1, source_target_pairs={{0,6},{1,7},{2,0},{3,1},{4,2},{5,3},{6,4},{7,5},{8,14},{9,15},{10,... | collective-permute-start | bytes 1462280 | tf_op jit(solution)/shard_map/ppermute | solution.py:67
  21.0 0.5 collective-permute-start.7
  21.5 1.0 slice_bitcast_fusion.2
  22.6 1.6 collective-permute-start.4
  24.3 0.7 slice_bitcast_fusion.28
  25.0 7.6 %collective-permute-done.3 = bf16[136,1792]{1,0:T(8,128)(2,1)S(1)} collective-permute-done((bf16[136,1792]{1,0:T(8,128)(2,1)S(1)}, bf16[136,1792]{1,0:T(8,128)(2,1)S(1)}, u32[]{:S(2)}, u32[]{:S(2)}) %collective-permute-start.3) | collective-permute-done | bytes 487456 | tf_op jit(solution)/shard_map/ppermute | solution.py:67
  32.6 1.6 collective-permute-start.6
  34.1 28.7 %collective-permute-done.2 = bf16[136,1792]{1,0:T(8,128)(2,1)S(1)} collective-permute-done((bf16[136,1792]{1,0:T(8,128)(2,1)}, bf16[136,1792]{1,0:T(8,128)(2,1)S(1)}, u32[]{:S(2)}, u32[]{:S(2)}) %collective-permute-start.2) | collective-permute-done | bytes 487456 | tf_op jit(solution)/shard_map/ppermute | solution.py:67
  62.8 1.7 collective-permute-start.5
  64.7 8.1 %collective-permute-done.6 = bf16[1024,896]{1,0:T(8,128)(2,1)S(1)} collective-permute-done((bf16[1024,896]{1,0:T(8,128)(2,1)S(1)}, bf16[1024,896]{1,0:T(8,128)(2,1)S(1)}, u32[]{:S(2)}, u32[]{:S(2)}) %collective-permute-start.6) | collective-permute-done | bytes 1835040 | tf_op jit(solution)/shard_map/ppermute | solution.py:67
  73.0 4.6 %collective-permute-done.5 = bf16[136,1792]{1,0:T(8,128)(2,1)S(1)} collective-permute-done((bf16[136,1792]{1,0:T(8,128)(2,1)S(1)}, bf16[136,1792]{1,0:T(8,128)(2,1)S(1)}, u32[]{:S(2)}, u32[]{:S(2)}) %collective-permute-start.5) | collective-permute-done | bytes 487456 | tf_op jit(solution)/shard_map/ppermute | solution.py:67
  78.0 0.4 convolution_convert_fusion
  78.7 0.4 convolution_convert_fusion.2
  79.2 0.6 collective-permute-start.8
  79.7 1.5 collective-permute-start.13
  81.2 0.4 convolution_convert_fusion.1
  81.7 0.4 convolution_convert_fusion.3
  82.4 6.2 %collective-permute-done.9 = bf16[896,2048]{1,0:T(8,128)(2,1)} collective-permute-done((bf16[896,2048]{1,0:T(8,128)(2,1)}, bf16[896,2048]{1,0:T(8,128)(2,1)}, u32[]{:S(2)}, u32[]{:S(2)}) %collective-permute-start.9) | collective-permute-done | bytes 3670048 | tf_op jit(solution)/shard_map/ppermute | solution.py:67
  88.6 3.6 %fusion.15 = bf16[4,128,1024]{2,1,0:T(8,128)(2,1)S(1)} fusion(bf16[4,128,1792]{2,1,0:T(8,128)(2,1)S(1)} %pad_maximum_fusion.4, bf16[896,2048]{1,0:T(8,128)(2,1)S(1)} %bitcast.131, bf16[896,2048]{1,0:T(8,128)(2,1)} %collective-permute-done.9), kind=kOutput, calls=%fused_computation.39 | convolution fusion | flops 1886912512 | bytes 10223616 | tf_op jit(solution)/shard_map/dot_general | solution.py:134
  92.2 0.6 collective-permute-start.11
  92.8 3.6 %fusion.12 = bf16[4,128,1024]{2,1,0:T(8,128)(2,1)S(1)} fusion(bf16[4,128,1792]{2,1,0:T(8,128)(2,1)S(1)} %pad_maximum_fusion.4, bf16[896,2048]{1,0:T(8,128)(2,1)S(1)} %bitcast.132, bf16[896,2048]{1,0:T(8,128)(2,1)} %collective-permute-done.9), kind=kOutput, calls=%fused_computation.38 | convolution fusion | flops 1886912512 | bytes 10223616 | tf_op jit(solution)/shard_map/dot_general | solution.py:134
  96.4 1.6 collective-permute-start.12
  98.0 2.4 %collective-permute-done.11 = bf16[128,1024]{1,0:T(8,128)(2,1)S(1)} collective-permute-done((bf16[128,1024]{1,0:T(8,128)(2,1)S(1)}, bf16[128,1024]{1,0:T(8,128)(2,1)S(1)}, u32[]{:S(2)}, u32[]{:S(2)}) %collective-permute-start.11) | collective-permute-done | bytes 262176 | tf_op jit(solution)/shard_map/ppermute | solution.py:67
  100.4 5.7 %fusion = f32[512,2048]{1,0:T(8,128)S(1)} fusion(bf16[512,1792]{1,0:T(8,128)(2,1)S(1)} %bitcast.120, bf16[896,2048]{1,0:T(8,128)(2,1)} %collective-permute-done.9, bf16[896,2048]{1,0:T(8,128)(2,1)S(1)} %bitcast.133), kind=kOutput, calls=%fused_computation.5 | convolution fusion | flops 3772776448 | bytes 13369344 | tf_op jit(solution)/shard_map/dot_general | solution.py:134
  106.9 0.7 convolution_convert_fusion.11
  107.7 1.6 collective-permute-start.14
  109.6 1.8 collective-permute-start.17
  111.5 2.1 %collective-permute-start.20 = (bf16[128,2048]{1,0:T(8,128)(2,1)S(1)}, bf16[128,2048]{1,0:T(8,128)(2,1)S(1)}, u32[]{:S(2)}, u32[]{:S(2)}) collective-permute-start(bf16[128,2048]{1,0:T(8,128)(2,1)S(1)} %pad_maximum_fusion.10), channel_id=1, source_target_pairs={{0,16},{1,17},{2,18},{3,19},{4,20},{5,21},{6,22},{7,23},{8,24},{9,... | collective-permute-start | bytes 1572872 | tf_op jit(solution)/shard_map/ppermute | solution.py:67
  113.6 2.8 %collective-permute-done.14 = bf16[128,1024]{1,0:T(8,128)(2,1)S(1)} collective-permute-done((bf16[128,1024]{1,0:T(8,128)(2,1)S(1)}, bf16[128,1024]{1,0:T(8,128)(2,1)S(1)}, u32[]{:S(2)}, u32[]{:S(2)}) %collective-permute-start.14) | collective-permute-done | bytes 262176 | tf_op jit(solution)/shard_map/ppermute | solution.py:67
  116.5 0.7 convolution_convert_fusion.10
  117.4 1.4 collective-permute-done.15
  118.7 5.3 %collective-permute-done.18 = bf16[128,2048]{1,0:T(8,128)(2,1)S(1)} collective-permute-done((bf16[128,2048]{1,0:T(8,128)(2,1)S(1)}, bf16[128,2048]{1,0:T(8,128)(2,1)S(1)}, u32[]{:S(2)}, u32[]{:S(2)}) %collective-permute-start.18) | collective-permute-done | bytes 524320 | tf_op jit(solution)/shard_map/ppermute | solution.py:67
  124.5 1.3 collective-permute-start.19
  125.9 0.7 convolution_convert_fusion.6
  127.0 0.7 collective-permute-start.30
  127.6 0.5 collective-permute-done.27
  128.4 2.8 %collective-permute-start.28 = (bf16[128,1792]{1,0:T(8,128)(2,1)S(1)}, bf16[128,1792]{1,0:T(8,128)(2,1)S(1)}, u32[]{:S(2)}, u32[]{:S(2)}) collective-permute-start(bf16[128,1792]{1,0:T(8,128)(2,1)S(1)} %convolution_convert_fusion.14), channel_id=1, source_target_pairs={{0,6},{1,7},{2,0},{3,1},{4,2},{5,3},{6,4},{7,5},{8,14},{9,15},{10,... | collective-permute-start | bytes 1376264 | tf_op jit(solution)/shard_map/ppermute | solution.py:67
  131.2 4.0 %collective-permute-done.20 = bf16[128,2048]{1,0:T(8,128)(2,1)S(1)} collective-permute-done((bf16[128,2048]{1,0:T(8,128)(2,1)S(1)}, bf16[128,2048]{1,0:T(8,128)(2,1)S(1)}, u32[]{:S(2)}, u32[]{:S(2)}) %collective-permute-start.20) | collective-permute-done | bytes 524320 | tf_op jit(solution)/shard_map/ppermute | solution.py:67
  135.6 0.6 collective-permute-start.22
  136.2 0.7 convolution_convert_fusion.9
  136.8 0.7 convolution_convert_fusion.5
  137.6 4.5 %collective-permute-done.30 = bf16[128,1792]{1,0:T(8,128)(2,1)S(1)} collective-permute-done((bf16[128,1792]{1,0:T(8,128)(2,1)S(1)}, bf16[128,1792]{1,0:T(8,128)(2,1)S(1)}, u32[]{:S(2)}, u32[]{:S(2)}) %collective-permute-start.30) | collective-permute-done | bytes 458784 | tf_op jit(solution)/shard_map/ppermute | solution.py:67
  142.6 3.2 %collective-permute-done.23 = bf16[128,2048]{1,0:T(8,128)(2,1)S(1)} collective-permute-done((bf16[128,2048]{1,0:T(8,128)(2,1)S(1)}, bf16[128,2048]{1,0:T(8,128)(2,1)S(1)}, u32[]{:S(2)}, u32[]{:S(2)}) %collective-permute-start.23) | collective-permute-done | bytes 524320 | tf_op jit(solution)/shard_map/ppermute | solution.py:67
  146.1 0.6 collective-permute-start.25
  146.7 0.7 convolution_convert_fusion.4
  147.3 0.7 convolution_convert_fusion.8
  148.1 1.4 collective-permute-done.24
  149.7 4.0 %collective-permute-done.25 = bf16[128,1024]{1,0:T(8,128)(2,1)S(1)} collective-permute-done((bf16[128,1024]{1,0:T(8,128)(2,1)S(1)}, bf16[128,1024]{1,0:T(8,128)(2,1)S(1)}, u32[]{:S(2)}, u32[]{:S(2)}) %collective-permute-start.25) | collective-permute-done | bytes 262176 | tf_op jit(solution)/shard_map/ppermute | solution.py:67
  153.7 0.7 convolution_convert_fusion.7
  154.8 1.6 collective-permute-start.33
  156.5 4.3 %collective-permute-done.31 = bf16[128,1792]{1,0:T(8,128)(2,1)S(1)} collective-permute-done((bf16[128,1792]{1,0:T(8,128)(2,1)S(1)}, bf16[128,1792]{1,0:T(8,128)(2,1)S(1)}, u32[]{:S(2)}, u32[]{:S(2)}) %collective-permute-start.31) | collective-permute-done | bytes 458784 | tf_op jit(solution)/shard_map/ppermute | solution.py:67
  161.1 1.1 collective-permute-start.34
  162.5 12.7 %collective-permute-start.35 = (bf16[128,1792]{1,0:T(8,128)(2,1)S(1)}, bf16[128,1792]{1,0:T(8,128)(2,1)S(1)}, u32[]{:S(2)}, u32[]{:S(2)}) collective-permute-start(bf16[128,1792]{1,0:T(8,128)(2,1)S(1)} %add_convert_fusion.1), channel_id=1, source_target_pairs={{0,10},{1,11},{2,12},{3,13},{4,14},{5,15},{6,8},{7,9},{8,2},{9,3},... | collective-permute-start | bytes 1376264 | tf_op jit(solution)/shard_map/ppermute | solution.py:67
  175.3 8.8 %collective-permute-done.33 = bf16[128,1792]{1,0:T(8,128)(2,1)S(1)} collective-permute-done((bf16[128,1792]{1,0:T(8,128)(2,1)S(1)}, bf16[128,1792]{1,0:T(8,128)(2,1)S(1)}, u32[]{:S(2)}, u32[]{:S(2)}) %collective-permute-start.33) | collective-permute-done | bytes 458784 | tf_op jit(solution)/shard_map/ppermute | solution.py:67
  184.5 10.1 %collective-permute-done.35 = bf16[128,1792]{1,0:T(8,128)(2,1)S(1)} collective-permute-done((bf16[128,1792]{1,0:T(8,128)(2,1)S(1)}, bf16[128,1792]{1,0:T(8,128)(2,1)S(1)}, u32[]{:S(2)}, u32[]{:S(2)}) %collective-permute-start.35) | collective-permute-done | bytes 458784 | tf_op jit(solution)/shard_map/ppermute | solution.py:67
  194.8 0.9 copy-done.1
  195.8 0.7 slice_dynamic-update-slice_fusion
  (109 shorter events, 7.4 us)
Async XLA Ops:
  0.0 32.6 %copy-start = (bf16[1,1024,896]{2,1,0:T(8,128)(2,1)S(1)}, bf16[1,1024,896]{2,1,0:T(8,128)(2,1)}, u32[]{:S(2)}) copy-start(bf16[1,1024,896]{2,1,0:T(8,128)(2,1)} %param.7) | copy-start | bytes 5505028
  3.0 14.2 %collective-permute-start = (bf16[136,1792]{1,0:T(8,128)(2,1)S(1)}, bf16[136,1792]{1,0:T(8,128)(2,1)S(1)}, u32[]{:S(2)}, u32[]{:S(2)}) collective-permute-start(bf16[136,1792]{1,0:T(8,128)(2,1)S(1)} %get-tuple-element.117), channel_id=1, source_target_pairs={{0,16},{1,17},{2,18},{3,19},{4,20},{5,21},{6,22},{7,23},{8,24},{9,... | collective-permute-start | bytes 1462280 | tf_op jit(solution)/shard_map/ppermute | solution.py:67
  6.0 15.5 %collective-permute-start.1 = (bf16[136,1792]{1,0:T(8,128)(2,1)S(1)}, bf16[136,1792]{1,0:T(8,128)(2,1)}, u32[]{:S(2)}, u32[]{:S(2)}) collective-permute-start(bf16[136,1792]{1,0:T(8,128)(2,1)S(1)} %get-tuple-element.43), channel_id=1, source_target_pairs={{0,2},{1,3},{2,4},{3,5},{4,6},{5,7},{6,0},{7,1},{8,10},{9,11},{10,... | collective-permute-start | bytes 1462280 | tf_op jit(solution)/shard_map/ppermute | solution.py:67
  7.6 81.0 %collective-permute-start.9 = (bf16[896,2048]{1,0:T(8,128)(2,1)}, bf16[896,2048]{1,0:T(8,128)(2,1)}, u32[]{:S(2)}, u32[]{:S(2)}) collective-permute-start(bf16[896,2048]{1,0:T(8,128)(2,1)} %bitcast.130), channel_id=1, source_target_pairs={{0,8},{1,9},{2,10},{3,11},{4,12},{5,13},{6,14},{7,15},{8,0},{9,1},... | collective-permute-start | bytes 11010056 | tf_op jit(solution)/shard_map/ppermute | solution.py:67
  17.1 15.5 %collective-permute-start.3 = (bf16[136,1792]{1,0:T(8,128)(2,1)S(1)}, bf16[136,1792]{1,0:T(8,128)(2,1)S(1)}, u32[]{:S(2)}, u32[]{:S(2)}) collective-permute-start(bf16[136,1792]{1,0:T(8,128)(2,1)S(1)} %get-tuple-element.43), channel_id=1, source_target_pairs={{0,6},{1,7},{2,0},{3,1},{4,2},{5,3},{6,4},{7,5},{8,14},{9,15},{10,... | collective-permute-start | bytes 1462280 | tf_op jit(solution)/shard_map/ppermute | solution.py:67
  21.0 43.6 %collective-permute-start.7 = (bf16[136,1792]{1,0:T(8,128)(2,1)S(1)}, bf16[136,1792]{1,0:T(8,128)(2,1)S(1)}, u32[]{:S(2)}, u32[]{:S(2)}) collective-permute-start(bf16[136,1792]{1,0:T(8,128)(2,1)S(1)} %collective-permute-done), channel_id=1, source_target_pairs={{0,6},{1,7},{2,0},{3,1},{4,2},{5,3},{6,4},{7,5},{8,14},{9,15},{10,... | collective-permute-start | bytes 1462280 | tf_op jit(solution)/shard_map/ppermute | solution.py:67
  22.6 40.3 %collective-permute-start.4 = (bf16[136,1792]{1,0:T(8,128)(2,1)S(1)}, bf16[136,1792]{1,0:T(8,128)(2,1)S(1)}, u32[]{:S(2)}, u32[]{:S(2)}) collective-permute-start(bf16[136,1792]{1,0:T(8,128)(2,1)S(1)} %collective-permute-done), channel_id=1, source_target_pairs={{0,2},{1,3},{2,4},{3,5},{4,6},{5,7},{6,0},{7,1},{8,10},{9,11},{10,... | collective-permute-start | bytes 1462280 | tf_op jit(solution)/shard_map/ppermute | solution.py:67
  24.2 38.6 %collective-permute-start.2 = (bf16[136,1792]{1,0:T(8,128)(2,1)}, bf16[136,1792]{1,0:T(8,128)(2,1)S(1)}, u32[]{:S(2)}, u32[]{:S(2)}) collective-permute-start(bf16[136,1792]{1,0:T(8,128)(2,1)} %collective-permute-done.1), channel_id=1, source_target_pairs={{0,2},{1,3},{2,4},{3,5},{4,6},{5,7},{6,0},{7,1},{8,10},{9,11},{10,... | collective-permute-start | bytes 1462280 | tf_op jit(solution)/shard_map/ppermute | solution.py:67
  32.6 40.2 %collective-permute-start.6 = (bf16[1024,896]{1,0:T(8,128)(2,1)S(1)}, bf16[1024,896]{1,0:T(8,128)(2,1)S(1)}, u32[]{:S(2)}, u32[]{:S(2)}) collective-permute-start(bf16[1024,896]{1,0:T(8,128)(2,1)S(1)} %bitcast.118), channel_id=1, source_target_pairs={{0,16},{1,17},{2,18},{3,19},{4,20},{5,21},{6,22},{7,23},{8,24},{9,... | collective-permute-start | bytes 5505032 | tf_op jit(solution)/shard_map/ppermute | solution.py:67
  62.8 14.8 %collective-permute-start.5 = (bf16[136,1792]{1,0:T(8,128)(2,1)S(1)}, bf16[136,1792]{1,0:T(8,128)(2,1)S(1)}, u32[]{:S(2)}, u32[]{:S(2)}) collective-permute-start(bf16[136,1792]{1,0:T(8,128)(2,1)S(1)} %collective-permute-done.4), channel_id=1, source_target_pairs={{0,2},{1,3},{2,4},{3,5},{4,6},{5,7},{6,0},{7,1},{8,10},{9,11},{10,... | collective-permute-start | bytes 1462280 | tf_op jit(solution)/shard_map/ppermute | solution.py:67
  78.4 3.7 %collective-permute-start.10 = (bf16[4,64,1792]{2,1,0:T(8,128)(2,1)S(1)}, bf16[4,64,1792]{2,1,0:T(8,128)(2,1)S(1)}, u32[]{:S(2)}, u32[]{:S(2)}) collective-permute-start(bf16[4,64,1792]{2,1,0:T(8,128)(2,1)S(1)} %convolution_convert_fusion), channel_id=1, source_target_pairs={{0,1},{1,0},{2,3},{3,2},{4,5},{5,4},{6,7},{7,6},{8,9},{9,8},{10,11... | collective-permute-start | bytes 2752520 | tf_op jit(solution)/shard_map/ppermute | solution.py:67
  79.2 3.1 %collective-permute-start.8 = (bf16[4,64,1792]{2,1,0:T(8,128)(2,1)S(1)}, bf16[4,64,1792]{2,1,0:T(8,128)(2,1)S(1)}, u32[]{:S(2)}, u32[]{:S(2)}) collective-permute-start(bf16[4,64,1792]{2,1,0:T(8,128)(2,1)S(1)} %convolution_convert_fusion.2), channel_id=1, source_target_pairs={{0,1},{1,0},{2,3},{3,2},{4,5},{5,4},{6,7},{7,6},{8,9},{9,8},{10,11... | collective-permute-start | bytes 2752520 | tf_op jit(solution)/shard_map/ppermute | solution.py:67
  79.7 26.7 %collective-permute-start.13 = (bf16[4,8,256]{2,1,0:T(8,128)(2,1)S(1)}, bf16[4,8,256]{2,1,0:T(8,128)(2,1)S(1)}, u32[]{:S(2)}, u32[]{:S(2)}) collective-permute-start(bf16[4,8,256]{2,1,0:T(8,128)(2,1)S(1)} %pad_maximum_fusion.16), channel_id=1, source_target_pairs={{0,8},{1,9},{2,10},{3,11},{4,12},{5,13},{6,14},{7,15},{8,0},{9,1},... | collective-permute-start | bytes 49160 | tf_op jit(solution)/shard_map/ppermute | solution.py:67
  82.1 6.5 %copy-start.2 = (bf16[1,896,2048]{2,1,0:T(8,128)(2,1)S(1)}, bf16[1,896,2048]{2,1,0:T(8,128)(2,1)}, u32[]{:S(2)}) copy-start(bf16[1,896,2048]{2,1,0:T(8,128)(2,1)} %param.6) | copy-start | bytes 11010052
  92.2 8.1 %collective-permute-start.11 = (bf16[128,1024]{1,0:T(8,128)(2,1)S(1)}, bf16[128,1024]{1,0:T(8,128)(2,1)S(1)}, u32[]{:S(2)}, u32[]{:S(2)}) collective-permute-start(bf16[128,1024]{1,0:T(8,128)(2,1)S(1)} %slice_bitcast_fusion.15), channel_id=1, source_target_pairs={{0,16},{1,17},{2,18},{3,19},{4,20},{5,21},{6,22},{7,23},{8,24},{9,... | collective-permute-start | bytes 786440 | tf_op jit(solution)/shard_map/ppermute | solution.py:67
  96.4 9.8 %collective-permute-start.12 = (bf16[128,1024]{1,0:T(8,128)(2,1)S(1)}, bf16[128,1024]{1,0:T(8,128)(2,1)S(1)}, u32[]{:S(2)}, u32[]{:S(2)}) collective-permute-start(bf16[128,1024]{1,0:T(8,128)(2,1)S(1)} %slice_bitcast_fusion.12), channel_id=1, source_target_pairs={{0,16},{1,17},{2,18},{3,19},{4,20},{5,21},{6,22},{7,23},{8,24},{9,... | collective-permute-start | bytes 786440 | tf_op jit(solution)/shard_map/ppermute | solution.py:67
  107.6 1.7 collective-permute-start.16
  107.7 8.8 %collective-permute-start.14 = (bf16[128,1024]{1,0:T(8,128)(2,1)S(1)}, bf16[128,1024]{1,0:T(8,128)(2,1)S(1)}, u32[]{:S(2)}, u32[]{:S(2)}) collective-permute-start(bf16[128,1024]{1,0:T(8,128)(2,1)S(1)} %fusion.21), channel_id=1, source_target_pairs={{0,8},{1,9},{2,10},{3,11},{4,12},{5,13},{6,14},{7,15},{8,0},{9,1},... | collective-permute-start | bytes 786440 | tf_op jit(solution)/shard_map/ppermute | solution.py:67
  109.3 14.8 %collective-permute-start.18 = (bf16[128,2048]{1,0:T(8,128)(2,1)S(1)}, bf16[128,2048]{1,0:T(8,128)(2,1)S(1)}, u32[]{:S(2)}, u32[]{:S(2)}) collective-permute-start(bf16[128,2048]{1,0:T(8,128)(2,1)S(1)} %pad_maximum_fusion.9), channel_id=1, source_target_pairs={{0,16},{1,17},{2,18},{3,19},{4,20},{5,21},{6,22},{7,23},{8,24},{9,... | collective-permute-start | bytes 1572872 | tf_op jit(solution)/shard_map/ppermute | solution.py:67
  109.6 14.7 %collective-permute-start.17 = (bf16[128,1792]{1,0:T(8,128)(2,1)S(1)}, bf16[128,1792]{1,0:T(8,128)(2,1)S(1)}, u32[]{:S(2)}, u32[]{:S(2)}) collective-permute-start(bf16[128,1792]{1,0:T(8,128)(2,1)S(1)} %convolution_convert_fusion.15), channel_id=1, source_target_pairs={{0,2},{1,3},{2,4},{3,5},{4,6},{5,7},{6,0},{7,1},{8,10},{9,11},{10,... | collective-permute-start | bytes 1376264 | tf_op jit(solution)/shard_map/ppermute | solution.py:67
  111.5 23.7 %collective-permute-start.20 = (bf16[128,2048]{1,0:T(8,128)(2,1)S(1)}, bf16[128,2048]{1,0:T(8,128)(2,1)S(1)}, u32[]{:S(2)}, u32[]{:S(2)}) collective-permute-start(bf16[128,2048]{1,0:T(8,128)(2,1)S(1)} %pad_maximum_fusion.10), channel_id=1, source_target_pairs={{0,16},{1,17},{2,18},{3,19},{4,20},{5,21},{6,22},{7,23},{8,24},{9,... | collective-permute-start | bytes 1572872 | tf_op jit(solution)/shard_map/ppermute | solution.py:67
  117.2 1.6 collective-permute-start.15
  117.3 28.5 %collective-permute-start.23 = (bf16[128,2048]{1,0:T(8,128)(2,1)S(1)}, bf16[128,2048]{1,0:T(8,128)(2,1)S(1)}, u32[]{:S(2)}, u32[]{:S(2)}) collective-permute-start(bf16[128,2048]{1,0:T(8,128)(2,1)S(1)} %pad_maximum_fusion.11), channel_id=1, source_target_pairs={{0,16},{1,17},{2,18},{3,19},{4,20},{5,21},{6,22},{7,23},{8,24},{9,... | collective-permute-start | bytes 1572872 | tf_op jit(solution)/shard_map/ppermute | solution.py:67
  124.5 10.7 %collective-permute-start.19 = (bf16[128,1024]{1,0:T(8,128)(2,1)S(1)}, bf16[128,1024]{1,0:T(8,128)(2,1)S(1)}, u32[]{:S(2)}, u32[]{:S(2)}) collective-permute-start(bf16[128,1024]{1,0:T(8,128)(2,1)S(1)} %fusion.20), channel_id=1, source_target_pairs={{0,8},{1,9},{2,10},{3,11},{4,12},{5,13},{6,14},{7,15},{8,0},{9,1},... | collective-permute-start | bytes 786440 | tf_op jit(solution)/shard_map/ppermute | solution.py:67
  126.6 1.6 collective-permute-start.27
  127.0 15.2 %collective-permute-start.30 = (bf16[128,1792]{1,0:T(8,128)(2,1)S(1)}, bf16[128,1792]{1,0:T(8,128)(2,1)S(1)}, u32[]{:S(2)}, u32[]{:S(2)}) collective-permute-start(bf16[128,1792]{1,0:T(8,128)(2,1)S(1)} %convolution_convert_fusion.13), channel_id=1, source_target_pairs={{0,2},{1,3},{2,4},{3,5},{4,6},{5,7},{6,0},{7,1},{8,10},{9,11},{10,... | collective-permute-start | bytes 1376264 | tf_op jit(solution)/shard_map/ppermute | solution.py:67
  128.4 28.0 %collective-permute-start.28 = (bf16[128,1792]{1,0:T(8,128)(2,1)S(1)}, bf16[128,1792]{1,0:T(8,128)(2,1)S(1)}, u32[]{:S(2)}, u32[]{:S(2)}) collective-permute-start(bf16[128,1792]{1,0:T(8,128)(2,1)S(1)} %convolution_convert_fusion.14), channel_id=1, source_target_pairs={{0,6},{1,7},{2,0},{3,1},{4,2},{5,3},{6,4},{7,5},{8,14},{9,15},{10,... | collective-permute-start | bytes 1376264 | tf_op jit(solution)/shard_map/ppermute | solution.py:67
  135.6 10.2 %collective-permute-start.22 = (bf16[128,1024]{1,0:T(8,128)(2,1)S(1)}, bf16[128,1024]{1,0:T(8,128)(2,1)S(1)}, u32[]{:S(2)}, u32[]{:S(2)}) collective-permute-start(bf16[128,1024]{1,0:T(8,128)(2,1)S(1)} %fusion.19), channel_id=1, source_target_pairs={{0,8},{1,9},{2,10},{3,11},{4,12},{5,13},{6,14},{7,15},{8,0},{9,1},... | collective-permute-start | bytes 786440 | tf_op jit(solution)/shard_map/ppermute | solution.py:67
  137.5 4.7 %collective-permute-start.29 = (bf16[64,1792]{1,0:T(8,128)(2,1)S(1)}, bf16[64,1792]{1,0:T(8,128)(2,1)S(1)}, u32[]{:S(2)}, u32[]{:S(2)}) collective-permute-start(bf16[64,1792]{1,0:T(8,128)(2,1)S(1)} %get-tuple-element.100), channel_id=1, source_target_pairs={{0,1},{1,0},{2,3},{3,2},{4,5},{5,4},{6,7},{7,6},{8,9},{9,8},{10,11... | collective-permute-start | bytes 688136 | tf_op jit(solution)/shard_map/ppermute | solution.py:67
  142.2 33.1 %collective-permute-start.21 = (bf16[64,1792]{1,0:T(8,128)(2,1)S(1)}, bf16[64,1792]{1,0:T(8,128)(2,1)S(1)}, u32[]{:S(2)}, u32[]{:S(2)}) collective-permute-start(bf16[64,1792]{1,0:T(8,128)(2,1)S(1)} %get-tuple-element.98), channel_id=1, source_target_pairs={{0,1},{1,0},{2,3},{3,2},{4,5},{5,4},{6,7},{7,6},{8,9},{9,8},{10,11... | collective-permute-start | bytes 688136 | tf_op jit(solution)/shard_map/ppermute | solution.py:67
  142.5 18.2 %collective-permute-start.31 = (bf16[128,1792]{1,0:T(8,128)(2,1)S(1)}, bf16[128,1792]{1,0:T(8,128)(2,1)S(1)}, u32[]{:S(2)}, u32[]{:S(2)}) collective-permute-start(bf16[128,1792]{1,0:T(8,128)(2,1)S(1)} %convolution_convert_fusion.12), channel_id=1, source_target_pairs={{0,6},{1,7},{2,0},{3,1},{4,2},{5,3},{6,4},{7,5},{8,14},{9,15},{10,... | collective-permute-start | bytes 1376264 | tf_op jit(solution)/shard_map/ppermute | solution.py:67
  146.1 7.7 %collective-permute-start.25 = (bf16[128,1024]{1,0:T(8,128)(2,1)S(1)}, bf16[128,1024]{1,0:T(8,128)(2,1)S(1)}, u32[]{:S(2)}, u32[]{:S(2)}) collective-permute-start(bf16[128,1024]{1,0:T(8,128)(2,1)S(1)} %fusion.18), channel_id=1, source_target_pairs={{0,8},{1,9},{2,10},{3,11},{4,12},{5,13},{6,14},{7,15},{8,0},{9,1},... | collective-permute-start | bytes 786440 | tf_op jit(solution)/shard_map/ppermute | solution.py:67
  148.0 1.6 collective-permute-start.24
  149.6 4.9 %collective-permute-start.32 = (bf16[64,1792]{1,0:T(8,128)(2,1)S(1)}, bf16[64,1792]{1,0:T(8,128)(2,1)S(1)}, u32[]{:S(2)}, u32[]{:S(2)}) collective-permute-start(bf16[64,1792]{1,0:T(8,128)(2,1)S(1)} %get-tuple-element.106), channel_id=1, source_target_pairs={{0,1},{1,0},{2,3},{3,2},{4,5},{5,4},{6,7},{7,6},{8,9},{9,8},{10,11... | collective-permute-start | bytes 688136 | tf_op jit(solution)/shard_map/ppermute | solution.py:67
  154.4 6.3 %collective-permute-start.26 = (bf16[64,1792]{1,0:T(8,128)(2,1)S(1)}, bf16[64,1792]{1,0:T(8,128)(2,1)S(1)}, u32[]{:S(2)}, u32[]{:S(2)}) collective-permute-start(bf16[64,1792]{1,0:T(8,128)(2,1)S(1)} %get-tuple-element.96), channel_id=1, source_target_pairs={{0,1},{1,0},{2,3},{3,2},{4,5},{5,4},{6,7},{7,6},{8,9},{9,8},{10,11... | collective-permute-start | bytes 688136 | tf_op jit(solution)/shard_map/ppermute | solution.py:67
  154.8 29.2 %collective-permute-start.33 = (bf16[128,1792]{1,0:T(8,128)(2,1)S(1)}, bf16[128,1792]{1,0:T(8,128)(2,1)S(1)}, u32[]{:S(2)}, u32[]{:S(2)}) collective-permute-start(bf16[128,1792]{1,0:T(8,128)(2,1)S(1)} %fusion.11), channel_id=1, source_target_pairs={{0,2},{1,3},{2,4},{3,5},{4,6},{5,7},{6,0},{7,1},{8,10},{9,11},{10,... | collective-permute-start | bytes 1376264 | tf_op jit(solution)/shard_map/ppermute | solution.py:67
  161.1 23.5 %collective-permute-start.34 = (bf16[128,1792]{1,0:T(8,128)(2,1)S(1)}, bf16[128,1792]{1,0:T(8,128)(2,1)S(1)}, u32[]{:S(2)}, u32[]{:S(2)}) collective-permute-start(bf16[128,1792]{1,0:T(8,128)(2,1)S(1)} %add_convert_fusion.2), channel_id=1, source_target_pairs={{0,8},{1,9},{2,10},{3,11},{4,12},{5,13},{6,14},{7,15},{8,0},{9,1},... | collective-permute-start | bytes 1376264 | tf_op jit(solution)/shard_map/ppermute | solution.py:67
  162.5 32.1 %collective-permute-start.35 = (bf16[128,1792]{1,0:T(8,128)(2,1)S(1)}, bf16[128,1792]{1,0:T(8,128)(2,1)S(1)}, u32[]{:S(2)}, u32[]{:S(2)}) collective-permute-start(bf16[128,1792]{1,0:T(8,128)(2,1)S(1)} %add_convert_fusion.1), channel_id=1, source_target_pairs={{0,10},{1,11},{2,12},{3,13},{4,14},{5,15},{6,8},{7,9},{8,2},{9,3},... | collective-permute-start | bytes 1376264 | tf_op jit(solution)/shard_map/ppermute | solution.py:67
  194.8 0.9 copy-start.1

commit v19 on v17

--- a/solution.py
+++ b/solution.py
@@ -187,10 +187,12 @@
     pays.append(places(info_x)[1])
     middle[0] = weigh(0, 0).astype(BF)
     middle[0], gates, ups = together((middle[0], gates, ups))
-    part += [send(whole(q), flip=2) for q in range(2, chips)]
+    part.append(send(whole(2), flip=2))
     middle[0] = send(middle[0], 1)
     down_product(0, 1)
     middle[0], part[1] = before_weigh(0, (middle[0], part[1]))
+    middle[0], gates, ups = together((middle[0], gates, ups))
+    part.append(send(whole(3), flip=2))
     middle[1] = send(weigh(0, 1).astype(BF), 1)
     finish(1)
     down_product(1, 0)

time: 185 us -> 186 us (level)
  transfers between devices with their start and end apart: 36 -> 36, of which waited for: 19 -> 20; matrix products, arithmetic and copies ran while one was open for 15% -> 15% of each run, Pallas kernels for 0% -> 0%
where the time goes in v19:
time: 186 us; the launch traced here: 185 us
  waiting for transfers between devices  117 us (63%)
  starting transfers between devices  35.1 us (19%)
  matrix products  22.9 us (12%)
  local copies, waits for them, and re-layouts  5.57 us (3%)
  other arithmetic  3.92 us (2%)
    ppermute x36, waiting for transfers between devices, send(): lax.ppermute(value, ('dp', 'expert'), [(i * owners + j, (i ^ flip) * owne...  117 us
    ppermute x36, starting transfers between devices, send(): lax.ppermute(value, ('dp', 'expert'), [(i * owners + j, (i ^ flip) * owne...  35.1 us
    dot_general x3, matrix products, product(): jnp.dot(flat, weights[:, lo:hi], preferred_element_type=F32)  12.9 us
    dot_general x8, matrix products, down_product(): value = jnp.dot(hidden[q, g], downs, preferred_element_type=F32).astype(BF)  5.25 us
  transfers between devices with their start and end apart: 36, of which 20 were waited for; matrix products, arithmetic and copies ran while one was open for 15% of the time, Pallas kernels for 0%

profile of v19, /device:TPU:0, one launch (start us, length us, event | category | flops | bytes accessed | tf_op | source)
XLA Modules:
  0.0 185.5 jit_solution(1925688865477922325)
XLA Ops:
  0.0 0.8 convert_bitcast_fusion
  0.8 0.7 fusion.62
  1.5 1.4 constant_dynamic-slice_fusion.1
  3.0 3.0 %collective-permute-start = (bf16[136,1792]{1,0:T(8,128)(2,1)S(1)}, bf16[136,1792]{1,0:T(8,128)(2,1)S(1)}, u32[]{:S(2)}, u32[]{:S(2)}) collective-permute-start(bf16[136,1792]{1,0:T(8,128)(2,1)S(1)} %get-tuple-element.115), channel_id=1, source_target_pairs={{0,16},{1,17},{2,18},{3,19},{4,20},{5,21},{6,22},{7,23},{8,24},{9,... | collective-permute-start | bytes 1462280 | tf_op jit(solution)/shard_map/ppermute | solution.py:67
  6.0 1.6 collective-permute-start.1
  7.6 1.5 collective-permute-start.9
  9.1 8.0 %collective-permute-done = bf16[136,1792]{1,0:T(8,128)(2,1)S(1)} collective-permute-done((bf16[136,1792]{1,0:T(8,128)(2,1)S(1)}, bf16[136,1792]{1,0:T(8,128)(2,1)S(1)}, u32[]{:S(2)}, u32[]{:S(2)}) %collective-permute-start) | collective-permute-done | bytes 487456 | tf_op jit(solution)/shard_map/ppermute | solution.py:67
  17.1 3.8 %collective-permute-start.3 = (bf16[136,1792]{1,0:T(8,128)(2,1)S(1)}, bf16[136,1792]{1,0:T(8,128)(2,1)S(1)}, u32[]{:S(2)}, u32[]{:S(2)}) collective-permute-start(bf16[136,1792]{1,0:T(8,128)(2,1)S(1)} %get-tuple-element.44), channel_id=1, source_target_pairs={{0,6},{1,7},{2,0},{3,1},{4,2},{5,3},{6,4},{7,5},{8,14},{9,15},{10,... | collective-permute-start | bytes 1462280 | tf_op jit(solution)/shard_map/ppermute | solution.py:67
  21.0 0.5 collective-permute-start.7
  21.5 1.0 slice_bitcast_fusion.2
  22.6 1.6 collective-permute-start.4
  24.3 0.7 slice_bitcast_fusion.28
  25.0 7.6 %collective-permute-done.3 = bf16[136,1792]{1,0:T(8,128)(2,1)S(1)} collective-permute-done((bf16[136,1792]{1,0:T(8,128)(2,1)S(1)}, bf16[136,1792]{1,0:T(8,128)(2,1)S(1)}, u32[]{:S(2)}, u32[]{:S(2)}) %collective-permute-start.3) | collective-permute-done | bytes 487456 | tf_op jit(solution)/shard_map/ppermute | solution.py:67
  32.6 1.6 collective-permute-start.6
  34.1 28.7 %collective-permute-done.2 = bf16[136,1792]{1,0:T(8,128)(2,1)S(1)} collective-permute-done((bf16[136,1792]{1,0:T(8,128)(2,1)}, bf16[136,1792]{1,0:T(8,128)(2,1)S(1)}, u32[]{:S(2)}, u32[]{:S(2)}) %collective-permute-start.2) | collective-permute-done | bytes 487456 | tf_op jit(solution)/shard_map/ppermute | solution.py:67
  62.8 1.7 collective-permute-start.5
  64.7 8.1 %collective-permute-done.6 = bf16[1024,896]{1,0:T(8,128)(2,1)S(1)} collective-permute-done((bf16[1024,896]{1,0:T(8,128)(2,1)S(1)}, bf16[1024,896]{1,0:T(8,128)(2,1)S(1)}, u32[]{:S(2)}, u32[]{:S(2)}) %collective-permute-start.6) | collective-permute-done | bytes 1835040 | tf_op jit(solution)/shard_map/ppermute | solution.py:67
  73.0 4.6 %collective-permute-done.5 = bf16[136,1792]{1,0:T(8,128)(2,1)S(1)} collective-permute-done((bf16[136,1792]{1,0:T(8,128)(2,1)S(1)}, bf16[136,1792]{1,0:T(8,128)(2,1)S(1)}, u32[]{:S(2)}, u32[]{:S(2)}) %collective-permute-start.5) | collective-permute-done | bytes 487456 | tf_op jit(solution)/shard_map/ppermute | solution.py:67
  78.0 0.4 convolution_convert_fusion
  78.7 0.4 convolution_convert_fusion.2
  79.2 0.6 collective-permute-start.8
  79.7 1.5 collective-permute-start.15
  81.2 0.4 convolution_convert_fusion.1
  81.7 0.4 convolution_convert_fusion.3
  82.4 6.2 %collective-permute-done.9 = bf16[896,2048]{1,0:T(8,128)(2,1)} collective-permute-done((bf16[896,2048]{1,0:T(8,128)(2,1)}, bf16[896,2048]{1,0:T(8,128)(2,1)}, u32[]{:S(2)}, u32[]{:S(2)}) %collective-permute-start.9) | collective-permute-done | bytes 3670048 | tf_op jit(solution)/shard_map/ppermute | solution.py:67
  88.6 3.6 %fusion.15 = bf16[4,128,1024]{2,1,0:T(8,128)(2,1)S(1)} fusion(bf16[4,128,1792]{2,1,0:T(8,128)(2,1)S(1)} %pad_maximum_fusion.4, bf16[896,2048]{1,0:T(8,128)(2,1)S(1)} %bitcast.131, bf16[896,2048]{1,0:T(8,128)(2,1)} %collective-permute-done.9), kind=kOutput, calls=%fused_computation.39 | convolution fusion | flops 1886912512 | bytes 10223616 | tf_op jit(solution)/shard_map/dot_general | solution.py:134
  92.2 0.6 collective-permute-start.11
  92.8 3.6 %fusion.12 = bf16[4,128,1024]{2,1,0:T(8,128)(2,1)S(1)} fusion(bf16[4,128,1792]{2,1,0:T(8,128)(2,1)S(1)} %pad_maximum_fusion.4, bf16[896,2048]{1,0:T(8,128)(2,1)S(1)} %bitcast.132, bf16[896,2048]{1,0:T(8,128)(2,1)} %collective-permute-done.9), kind=kOutput, calls=%fused_computation.38 | convolution fusion | flops 1886912512 | bytes 10223616 | tf_op jit(solution)/shard_map/dot_general | solution.py:134
  96.4 1.6 collective-permute-start.12
  98.0 2.4 %collective-permute-done.11 = bf16[128,1024]{1,0:T(8,128)(2,1)S(1)} collective-permute-done((bf16[128,1024]{1,0:T(8,128)(2,1)S(1)}, bf16[128,1024]{1,0:T(8,128)(2,1)S(1)}, u32[]{:S(2)}, u32[]{:S(2)}) %collective-permute-start.11) | collective-permute-done | bytes 262176 | tf_op jit(solution)/shard_map/ppermute | solution.py:67
  100.4 5.7 %fusion = f32[512,2048]{1,0:T(8,128)S(1)} fusion(bf16[512,1792]{1,0:T(8,128)(2,1)S(1)} %bitcast.120, bf16[896,2048]{1,0:T(8,128)(2,1)} %collective-permute-done.9, bf16[896,2048]{1,0:T(8,128)(2,1)S(1)} %bitcast.133), kind=kOutput, calls=%fused_computation.5 | convolution fusion | flops 3772776448 | bytes 13369344 | tf_op jit(solution)/shard_map/dot_general | solution.py:134
  106.4 1.6 collective-permute-start.13
  108.4 0.7 convolution_convert_fusion.10
  109.3 1.3 collective-permute-done.16
  111.0 1.8 collective-permute-start.17
  112.9 0.7 convolution_convert_fusion.11
  113.7 0.8 collective-permute-start.20
  114.4 0.7 collective-permute-done.14
  115.1 8.9 %collective-permute-done.18 = bf16[128,2048]{1,0:T(8,128)(2,1)S(1)} collective-permute-done((bf16[128,2048]{1,0:T(8,128)(2,1)S(1)}, bf16[128,2048]{1,0:T(8,128)(2,1)S(1)}, u32[]{:S(2)}, u32[]{:S(2)}) %collective-permute-start.18) | collective-permute-done | bytes 524320 | tf_op jit(solution)/shard_map/ppermute | solution.py:67
  124.0 1.6 collective-permute-done.17
  125.9 0.6 collective-permute-start.19
  126.4 0.7 convolution_convert_fusion.6
  127.7 0.8 collective-permute-start.23
  128.5 0.6 collective-permute-done.27
  129.4 3.8 %collective-permute-start.28 = (bf16[128,1792]{1,0:T(8,128)(2,1)S(1)}, bf16[128,1792]{1,0:T(8,128)(2,1)S(1)}, u32[]{:S(2)}, u32[]{:S(2)}) collective-permute-start(bf16[128,1792]{1,0:T(8,128)(2,1)S(1)} %convolution_convert_fusion.14), channel_id=1, source_target_pairs={{0,6},{1,7},{2,0},{3,1},{4,2},{5,3},{6,4},{7,5},{8,14},{9,15},{10,... | collective-permute-start | bytes 1376264 | tf_op jit(solution)/shard_map/ppermute | solution.py:67
  133.3 2.0 %collective-permute-done.20 = bf16[128,2048]{1,0:T(8,128)(2,1)S(1)} collective-permute-done((bf16[128,2048]{1,0:T(8,128)(2,1)S(1)}, bf16[128,2048]{1,0:T(8,128)(2,1)S(1)}, u32[]{:S(2)}, u32[]{:S(2)}) %collective-permute-start.20) | collective-permute-done | bytes 524320 | tf_op jit(solution)/shard_map/ppermute | solution.py:67
  135.5 0.6 collective-permute-start.22
  136.1 0.7 convolution_convert_fusion.9
  136.8 0.7 convolution_convert_fusion.5
  137.6 5.2 %collective-permute-done.30 = bf16[128,1792]{1,0:T(8,128)(2,1)S(1)} collective-permute-done((bf16[128,1792]{1,0:T(8,128)(2,1)S(1)}, bf16[128,1792]{1,0:T(8,128)(2,1)S(1)}, u32[]{:S(2)}, u32[]{:S(2)}) %collective-permute-start.30) | collective-permute-done | bytes 458784 | tf_op jit(solution)/shard_map/ppermute | solution.py:67
  143.2 2.9 %collective-permute-done.23 = bf16[128,2048]{1,0:T(8,128)(2,1)S(1)} collective-permute-done((bf16[128,2048]{1,0:T(8,128)(2,1)S(1)}, bf16[128,2048]{1,0:T(8,128)(2,1)S(1)}, u32[]{:S(2)}, u32[]{:S(2)}) %collective-permute-start.23) | collective-permute-done | bytes 524320 | tf_op jit(solution)/shard_map/ppermute | solution.py:67
  146.4 0.6 collective-permute-start.25
  147.0 0.7 convolution_convert_fusion.4
  147.7 0.7 convolution_convert_fusion.8
  148.5 1.4 collective-permute-done.24
  150.0 4.3 %collective-permute-done.25 = bf16[128,1024]{1,0:T(8,128)(2,1)S(1)} collective-permute-done((bf16[128,1024]{1,0:T(8,128)(2,1)S(1)}, bf16[128,1024]{1,0:T(8,128)(2,1)S(1)}, u32[]{:S(2)}, u32[]{:S(2)}) %collective-permute-start.25) | collective-permute-done | bytes 262176 | tf_op jit(solution)/shard_map/ppermute | solution.py:67
  154.4 0.7 convolution_convert_fusion.7
  155.5 1.6 collective-permute-start.33
  157.1 3.3 %collective-permute-done.31 = bf16[128,1792]{1,0:T(8,128)(2,1)S(1)} collective-permute-done((bf16[128,1792]{1,0:T(8,128)(2,1)S(1)}, bf16[128,1792]{1,0:T(8,128)(2,1)S(1)}, u32[]{:S(2)}, u32[]{:S(2)}) %collective-permute-start.31) | collective-permute-done | bytes 458784 | tf_op jit(solution)/shard_map/ppermute | solution.py:67
  160.7 2.4 %collective-permute-start.34 = (bf16[128,1792]{1,0:T(8,128)(2,1)S(1)}, bf16[128,1792]{1,0:T(8,128)(2,1)S(1)}, u32[]{:S(2)}, u32[]{:S(2)}) collective-permute-start(bf16[128,1792]{1,0:T(8,128)(2,1)S(1)} %add_convert_fusion.2), channel_id=1, source_target_pairs={{0,8},{1,9},{2,10},{3,11},{4,12},{5,13},{6,14},{7,15},{8,0},{9,1},... | collective-permute-start | bytes 1376264 | tf_op jit(solution)/shard_map/ppermute | solution.py:67
  163.6 7.1 %collective-permute-done.33 = bf16[128,1792]{1,0:T(8,128)(2,1)S(1)} collective-permute-done((bf16[128,1792]{1,0:T(8,128)(2,1)S(1)}, bf16[128,1792]{1,0:T(8,128)(2,1)S(1)}, u32[]{:S(2)}, u32[]{:S(2)}) %collective-permute-start.33) | collective-permute-done | bytes 458784 | tf_op jit(solution)/shard_map/ppermute | solution.py:67
  171.1 12.5 %collective-permute-done.34 = bf16[128,1792]{1,0:T(8,128)(2,1)S(1)} collective-permute-done((bf16[128,1792]{1,0:T(8,128)(2,1)S(1)}, bf16[128,1792]{1,0:T(8,128)(2,1)S(1)}, u32[]{:S(2)}, u32[]{:S(2)}) %collective-permute-start.34) | collective-permute-done | bytes 458784 | tf_op jit(solution)/shard_map/ppermute | solution.py:67
  183.8 0.9 copy-done.1
  184.8 0.7 slice_dynamic-update-slice_fusion
  (111 shorter events, 7.3 us)
Async XLA Ops:
  0.0 32.6 %copy-start = (bf16[1,1024,896]{2,1,0:T(8,128)(2,1)S(1)}, bf16[1,1024,896]{2,1,0:T(8,128)(2,1)}, u32[]{:S(2)}) copy-start(bf16[1,1024,896]{2,1,0:T(8,128)(2,1)} %param.7) | copy-start | bytes 5505028
  3.0 14.2 %collective-permute-start = (bf16[136,1792]{1,0:T(8,128)(2,1)S(1)}, bf16[136,1792]{1,0:T(8,128)(2,1)S(1)}, u32[]{:S(2)}, u32[]{:S(2)}) collective-permute-start(bf16[136,1792]{1,0:T(8,128)(2,1)S(1)} %get-tuple-element.115), channel_id=1, source_target_pairs={{0,16},{1,17},{2,18},{3,19},{4,20},{5,21},{6,22},{7,23},{8,24},{9,... | collective-permute-start | bytes 1462280 | tf_op jit(solution)/shard_map/ppermute | solution.py:67
  6.0 15.5 %collective-permute-start.1 = (bf16[136,1792]{1,0:T(8,128)(2,1)S(1)}, bf16[136,1792]{1,0:T(8,128)(2,1)}, u32[]{:S(2)}, u32[]{:S(2)}) collective-permute-start(bf16[136,1792]{1,0:T(8,128)(2,1)S(1)} %get-tuple-element.44), channel_id=1, source_target_pairs={{0,2},{1,3},{2,4},{3,5},{4,6},{5,7},{6,0},{7,1},{8,10},{9,11},{10,... | collective-permute-start | bytes 1462280 | tf_op jit(solution)/shard_map/ppermute | solution.py:67
  7.6 81.0 %collective-permute-start.9 = (bf16[896,2048]{1,0:T(8,128)(2,1)}, bf16[896,2048]{1,0:T(8,128)(2,1)}, u32[]{:S(2)}, u32[]{:S(2)}) collective-permute-start(bf16[896,2048]{1,0:T(8,128)(2,1)} %bitcast.130), channel_id=1, source_target_pairs={{0,8},{1,9},{2,10},{3,11},{4,12},{5,13},{6,14},{7,15},{8,0},{9,1},... | collective-permute-start | bytes 11010056 | tf_op jit(solution)/shard_map/ppermute | solution.py:67
  17.1 15.5 %collective-permute-start.3 = (bf16[136,1792]{1,0:T(8,128)(2,1)S(1)}, bf16[136,1792]{1,0:T(8,128)(2,1)S(1)}, u32[]{:S(2)}, u32[]{:S(2)}) collective-permute-start(bf16[136,1792]{1,0:T(8,128)(2,1)S(1)} %get-tuple-element.44), channel_id=1, source_target_pairs={{0,6},{1,7},{2,0},{3,1},{4,2},{5,3},{6,4},{7,5},{8,14},{9,15},{10,... | collective-permute-start | bytes 1462280 | tf_op jit(solution)/shard_map/ppermute | solution.py:67
  21.0 43.6 %collective-permute-start.7 = (bf16[136,1792]{1,0:T(8,128)(2,1)S(1)}, bf16[136,1792]{1,0:T(8,128)(2,1)S(1)}, u32[]{:S(2)}, u32[]{:S(2)}) collective-permute-start(bf16[136,1792]{1,0:T(8,128)(2,1)S(1)} %collective-permute-done), channel_id=1, source_target_pairs={{0,6},{1,7},{2,0},{3,1},{4,2},{5,3},{6,4},{7,5},{8,14},{9,15},{10,... | collective-permute-start | bytes 1462280 | tf_op jit(solution)/shard_map/ppermute | solution.py:67
  22.6 40.3 %collective-permute-start.4 = (bf16[136,1792]{1,0:T(8,128)(2,1)S(1)}, bf16[136,1792]{1,0:T(8,128)(2,1)S(1)}, u32[]{:S(2)}, u32[]{:S(2)}) collective-permute-start(bf16[136,1792]{1,0:T(8,128)(2,1)S(1)} %collective-permute-done), channel_id=1, source_target_pairs={{0,2},{1,3},{2,4},{3,5},{4,6},{5,7},{6,0},{7,1},{8,10},{9,11},{10,... | collective-permute-start | bytes 1462280 | tf_op jit(solution)/shard_map/ppermute | solution.py:67
  24.2 38.6 %collective-permute-start.2 = (bf16[136,1792]{1,0:T(8,128)(2,1)}, bf16[136,1792]{1,0:T(8,128)(2,1)S(1)}, u32[]{:S(2)}, u32[]{:S(2)}) collective-permute-start(bf16[136,1792]{1,0:T(8,128)(2,1)} %collective-permute-done.1), channel_id=1, source_target_pairs={{0,2},{1,3},{2,4},{3,5},{4,6},{5,7},{6,0},{7,1},{8,10},{9,11},{10,... | collective-permute-start | bytes 1462280 | tf_op jit(solution)/shard_map/ppermute | solution.py:67
  32.6 40.2 %collective-permute-start.6 = (bf16[1024,896]{1,0:T(8,128)(2,1)S(1)}, bf16[1024,896]{1,0:T(8,128)(2,1)S(1)}, u32[]{:S(2)}, u32[]{:S(2)}) collective-permute-start(bf16[1024,896]{1,0:T(8,128)(2,1)S(1)} %bitcast.118), channel_id=1, source_target_pairs={{0,16},{1,17},{2,18},{3,19},{4,20},{5,21},{6,22},{7,23},{8,24},{9,... | collective-permute-start | bytes 5505032 | tf_op jit(solution)/shard_map/ppermute | solution.py:67
  62.8 14.8 %collective-permute-start.5 = (bf16[136,1792]{1,0:T(8,128)(2,1)S(1)}, bf16[136,1792]{1,0:T(8,128)(2,1)S(1)}, u32[]{:S(2)}, u32[]{:S(2)}) collective-permute-start(bf16[136,1792]{1,0:T(8,128)(2,1)S(1)} %collective-permute-done.4), channel_id=1, source_target_pairs={{0,2},{1,3},{2,4},{3,5},{4,6},{5,7},{6,0},{7,1},{8,10},{9,11},{10,... | collective-permute-start | bytes 1462280 | tf_op jit(solution)/shard_map/ppermute | solution.py:67
  78.4 3.7 %collective-permute-start.10 = (bf16[4,64,1792]{2,1,0:T(8,128)(2,1)S(1)}, bf16[4,64,1792]{2,1,0:T(8,128)(2,1)S(1)}, u32[]{:S(2)}, u32[]{:S(2)}) collective-permute-start(bf16[4,64,1792]{2,1,0:T(8,128)(2,1)S(1)} %convolution_convert_fusion), channel_id=1, source_target_pairs={{0,1},{1,0},{2,3},{3,2},{4,5},{5,4},{6,7},{7,6},{8,9},{9,8},{10,11... | collective-permute-start | bytes 2752520 | tf_op jit(solution)/shard_map/ppermute | solution.py:67
  79.2 3.1 %collective-permute-start.8 = (bf16[4,64,1792]{2,1,0:T(8,128)(2,1)S(1)}, bf16[4,64,1792]{2,1,0:T(8,128)(2,1)S(1)}, u32[]{:S(2)}, u32[]{:S(2)}) collective-permute-start(bf16[4,64,1792]{2,1,0:T(8,128)(2,1)S(1)} %convolution_convert_fusion.2), channel_id=1, source_target_pairs={{0,1},{1,0},{2,3},{3,2},{4,5},{5,4},{6,7},{7,6},{8,9},{9,8},{10,11... | collective-permute-start | bytes 2752520 | tf_op jit(solution)/shard_map/ppermute | solution.py:67
  79.7 28.3 %collective-permute-start.15 = (bf16[4,8,256]{2,1,0:T(8,128)(2,1)S(1)}, bf16[4,8,256]{2,1,0:T(8,128)(2,1)S(1)}, u32[]{:S(2)}, u32[]{:S(2)}) collective-permute-start(bf16[4,8,256]{2,1,0:T(8,128)(2,1)S(1)} %pad_maximum_fusion.16), channel_id=1, source_target_pairs={{0,8},{1,9},{2,10},{3,11},{4,12},{5,13},{6,14},{7,15},{8,0},{9,1},... | collective-permute-start | bytes 49160 | tf_op jit(solution)/shard_map/ppermute | solution.py:67
  82.1 6.5 %copy-start.2 = (bf16[1,896,2048]{2,1,0:T(8,128)(2,1)S(1)}, bf16[1,896,2048]{2,1,0:T(8,128)(2,1)}, u32[]{:S(2)}) copy-start(bf16[1,896,2048]{2,1,0:T(8,128)(2,1)} %param.6) | copy-start | bytes 11010052
  92.2 8.1 %collective-permute-start.11 = (bf16[128,1024]{1,0:T(8,128)(2,1)S(1)}, bf16[128,1024]{1,0:T(8,128)(2,1)S(1)}, u32[]{:S(2)}, u32[]{:S(2)}) collective-permute-start(bf16[128,1024]{1,0:T(8,128)(2,1)S(1)} %slice_bitcast_fusion.15), channel_id=1, source_target_pairs={{0,16},{1,17},{2,18},{3,19},{4,20},{5,21},{6,22},{7,23},{8,24},{9,... | collective-permute-start | bytes 786440 | tf_op jit(solution)/shard_map/ppermute | solution.py:67
  96.4 9.8 %collective-permute-start.12 = (bf16[128,1024]{1,0:T(8,128)(2,1)S(1)}, bf16[128,1024]{1,0:T(8,128)(2,1)S(1)}, u32[]{:S(2)}, u32[]{:S(2)}) collective-permute-start(bf16[128,1024]{1,0:T(8,128)(2,1)S(1)} %slice_bitcast_fusion.12), channel_id=1, source_target_pairs={{0,16},{1,17},{2,18},{3,19},{4,20},{5,21},{6,22},{7,23},{8,24},{9,... | collective-permute-start | bytes 786440 | tf_op jit(solution)/shard_map/ppermute | solution.py:67
  106.4 6.4 %collective-permute-start.13 = (bf16[128,1024]{1,0:T(8,128)(2,1)S(1)}, bf16[128,1024]{1,0:T(8,128)(2,1)S(1)}, u32[]{:S(2)}, u32[]{:S(2)}) collective-permute-start(bf16[128,1024]{1,0:T(8,128)(2,1)S(1)} %fusion.21), channel_id=1, source_target_pairs={{0,8},{1,9},{2,10},{3,11},{4,12},{5,13},{6,14},{7,15},{8,0},{9,1},... | collective-permute-start | bytes 786440 | tf_op jit(solution)/shard_map/ppermute | solution.py:67
  109.1 1.6 collective-permute-start.16
  109.2 14.8 %collective-permute-start.18 = (bf16[128,2048]{1,0:T(8,128)(2,1)S(1)}, bf16[128,2048]{1,0:T(8,128)(2,1)S(1)}, u32[]{:S(2)}, u32[]{:S(2)}) collective-permute-start(bf16[128,2048]{1,0:T(8,128)(2,1)S(1)} %pad_maximum_fusion.9), channel_id=1, source_target_pairs={{0,16},{1,17},{2,18},{3,19},{4,20},{5,21},{6,22},{7,23},{8,24},{9,... | collective-permute-start | bytes 1572872 | tf_op jit(solution)/shard_map/ppermute | solution.py:67
  111.0 14.6 %collective-permute-start.17 = (bf16[128,1792]{1,0:T(8,128)(2,1)S(1)}, bf16[128,1792]{1,0:T(8,128)(2,1)S(1)}, u32[]{:S(2)}, u32[]{:S(2)}) collective-permute-start(bf16[128,1792]{1,0:T(8,128)(2,1)S(1)} %convolution_convert_fusion.15), channel_id=1, source_target_pairs={{0,2},{1,3},{2,4},{3,5},{4,6},{5,7},{6,0},{7,1},{8,10},{9,11},{10,... | collective-permute-start | bytes 1376264 | tf_op jit(solution)/shard_map/ppermute | solution.py:67
  113.6 1.6 collective-permute-start.14
  113.7 21.6 %collective-permute-start.20 = (bf16[128,2048]{1,0:T(8,128)(2,1)S(1)}, bf16[128,2048]{1,0:T(8,128)(2,1)S(1)}, u32[]{:S(2)}, u32[]{:S(2)}) collective-permute-start(bf16[128,2048]{1,0:T(8,128)(2,1)S(1)} %pad_maximum_fusion.10), channel_id=1, source_target_pairs={{0,16},{1,17},{2,18},{3,19},{4,20},{5,21},{6,22},{7,23},{8,24},{9,... | collective-permute-start | bytes 1572872 | tf_op jit(solution)/shard_map/ppermute | solution.py:67
  125.9 9.4 %collective-permute-start.19 = (bf16[128,1024]{1,0:T(8,128)(2,1)S(1)}, bf16[128,1024]{1,0:T(8,128)(2,1)S(1)}, u32[]{:S(2)}, u32[]{:S(2)}) collective-permute-start(bf16[128,1024]{1,0:T(8,128)(2,1)S(1)} %fusion.20), channel_id=1, source_target_pairs={{0,8},{1,9},{2,10},{3,11},{4,12},{5,13},{6,14},{7,15},{8,0},{9,1},... | collective-permute-start | bytes 786440 | tf_op jit(solution)/shard_map/ppermute | solution.py:67
  127.4 15.4 %collective-permute-start.30 = (bf16[128,1792]{1,0:T(8,128)(2,1)S(1)}, bf16[128,1792]{1,0:T(8,128)(2,1)S(1)}, u32[]{:S(2)}, u32[]{:S(2)}) collective-permute-start(bf16[128,1792]{1,0:T(8,128)(2,1)S(1)} %convolution_convert_fusion.13), channel_id=1, source_target_pairs={{0,2},{1,3},{2,4},{3,5},{4,6},{5,7},{6,0},{7,1},{8,10},{9,11},{10,... | collective-permute-start | bytes 1376264 | tf_op jit(solution)/shard_map/ppermute | solution.py:67
  127.6 1.6 collective-permute-start.27
  127.7 18.4 %collective-permute-start.23 = (bf16[128,2048]{1,0:T(8,128)(2,1)S(1)}, bf16[128,2048]{1,0:T(8,128)(2,1)S(1)}, u32[]{:S(2)}, u32[]{:S(2)}) collective-permute-start(bf16[128,2048]{1,0:T(8,128)(2,1)S(1)} %pad_maximum_fusion.11), channel_id=1, source_target_pairs={{0,16},{1,17},{2,18},{3,19},{4,20},{5,21},{6,22},{7,23},{8,24},{9,... | collective-permute-start | bytes 1572872 | tf_op jit(solution)/shard_map/ppermute | solution.py:67
  129.4 27.7 %collective-permute-start.28 = (bf16[128,1792]{1,0:T(8,128)(2,1)S(1)}, bf16[128,1792]{1,0:T(8,128)(2,1)S(1)}, u32[]{:S(2)}, u32[]{:S(2)}) collective-permute-start(bf16[128,1792]{1,0:T(8,128)(2,1)S(1)} %convolution_convert_fusion.14), channel_id=1, source_target_pairs={{0,6},{1,7},{2,0},{3,1},{4,2},{5,3},{6,4},{7,5},{8,14},{9,15},{10,... | collective-permute-start | bytes 1376264 | tf_op jit(solution)/shard_map/ppermute | solution.py:67
  135.5 10.6 %collective-permute-start.22 = (bf16[128,1024]{1,0:T(8,128)(2,1)S(1)}, bf16[128,1024]{1,0:T(8,128)(2,1)S(1)}, u32[]{:S(2)}, u32[]{:S(2)}) collective-permute-start(bf16[128,1024]{1,0:T(8,128)(2,1)S(1)} %fusion.19), channel_id=1, source_target_pairs={{0,8},{1,9},{2,10},{3,11},{4,12},{5,13},{6,14},{7,15},{8,0},{9,1},... | collective-permute-start | bytes 786440 | tf_op jit(solution)/shard_map/ppermute | solution.py:67
  137.5 5.3 %collective-permute-start.29 = (bf16[64,1792]{1,0:T(8,128)(2,1)S(1)}, bf16[64,1792]{1,0:T(8,128)(2,1)S(1)}, u32[]{:S(2)}, u32[]{:S(2)}) collective-permute-start(bf16[64,1792]{1,0:T(8,128)(2,1)S(1)} %get-tuple-element.98), channel_id=1, source_target_pairs={{0,1},{1,0},{2,3},{3,2},{4,5},{5,4},{6,7},{7,6},{8,9},{9,8},{10,11... | collective-permute-start | bytes 688136 | tf_op jit(solution)/shard_map/ppermute | solution.py:67
  142.8 20.8 %collective-permute-start.21 = (bf16[64,1792]{1,0:T(8,128)(2,1)S(1)}, bf16[64,1792]{1,0:T(8,128)(2,1)S(1)}, u32[]{:S(2)}, u32[]{:S(2)}) collective-permute-start(bf16[64,1792]{1,0:T(8,128)(2,1)S(1)} %get-tuple-element.96), channel_id=1, source_target_pairs={{0,1},{1,0},{2,3},{3,2},{4,5},{5,4},{6,7},{7,6},{8,9},{9,8},{10,11... | collective-permute-start | bytes 688136 | tf_op jit(solution)/shard_map/ppermute | solution.py:67
  143.1 17.3 %collective-permute-start.31 = (bf16[128,1792]{1,0:T(8,128)(2,1)S(1)}, bf16[128,1792]{1,0:T(8,128)(2,1)S(1)}, u32[]{:S(2)}, u32[]{:S(2)}) collective-permute-start(bf16[128,1792]{1,0:T(8,128)(2,1)S(1)} %convolution_convert_fusion.12), channel_id=1, source_target_pairs={{0,6},{1,7},{2,0},{3,1},{4,2},{5,3},{6,4},{7,5},{8,14},{9,15},{10,... | collective-permute-start | bytes 1376264 | tf_op jit(solution)/shard_map/ppermute | solution.py:67
  146.4 8.0 %collective-permute-start.25 = (bf16[128,1024]{1,0:T(8,128)(2,1)S(1)}, bf16[128,1024]{1,0:T(8,128)(2,1)S(1)}, u32[]{:S(2)}, u32[]{:S(2)}) collective-permute-start(bf16[128,1024]{1,0:T(8,128)(2,1)S(1)} %fusion.18), channel_id=1, source_target_pairs={{0,8},{1,9},{2,10},{3,11},{4,12},{5,13},{6,14},{7,15},{8,0},{9,1},... | collective-permute-start | bytes 786440 | tf_op jit(solution)/shard_map/ppermute | solution.py:67
  148.4 1.6 collective-permute-start.24
  149.9 5.3 %collective-permute-start.32 = (bf16[64,1792]{1,0:T(8,128)(2,1)S(1)}, bf16[64,1792]{1,0:T(8,128)(2,1)S(1)}, u32[]{:S(2)}, u32[]{:S(2)}) collective-permute-start(bf16[64,1792]{1,0:T(8,128)(2,1)S(1)} %get-tuple-element.104), channel_id=1, source_target_pairs={{0,1},{1,0},{2,3},{3,2},{4,5},{5,4},{6,7},{7,6},{8,9},{9,8},{10,11... | collective-permute-start | bytes 688136 | tf_op jit(solution)/shard_map/ppermute | solution.py:67
  155.1 5.3 %collective-permute-start.26 = (bf16[64,1792]{1,0:T(8,128)(2,1)S(1)}, bf16[64,1792]{1,0:T(8,128)(2,1)S(1)}, u32[]{:S(2)}, u32[]{:S(2)}) collective-permute-start(bf16[64,1792]{1,0:T(8,128)(2,1)S(1)} %get-tuple-element.94), channel_id=1, source_target_pairs={{0,1},{1,0},{2,3},{3,2},{4,5},{5,4},{6,7},{7,6},{8,9},{9,8},{10,11... | collective-permute-start | bytes 688136 | tf_op jit(solution)/shard_map/ppermute | solution.py:67
  155.5 15.2 %collective-permute-start.33 = (bf16[128,1792]{1,0:T(8,128)(2,1)S(1)}, bf16[128,1792]{1,0:T(8,128)(2,1)S(1)}, u32[]{:S(2)}, u32[]{:S(2)}) collective-permute-start(bf16[128,1792]{1,0:T(8,128)(2,1)S(1)} %fusion.11), channel_id=1, source_target_pairs={{0,2},{1,3},{2,4},{3,5},{4,6},{5,7},{6,0},{7,1},{8,10},{9,11},{10,... | collective-permute-start | bytes 1376264 | tf_op jit(solution)/shard_map/ppermute | solution.py:67
  160.7 22.9 %collective-permute-start.34 = (bf16[128,1792]{1,0:T(8,128)(2,1)S(1)}, bf16[128,1792]{1,0:T(8,128)(2,1)S(1)}, u32[]{:S(2)}, u32[]{:S(2)}) collective-permute-start(bf16[128,1792]{1,0:T(8,128)(2,1)S(1)} %add_convert_fusion.2), channel_id=1, source_target_pairs={{0,8},{1,9},{2,10},{3,11},{4,12},{5,13},{6,14},{7,15},{8,0},{9,1},... | collective-permute-start | bytes 1376264 | tf_op jit(solution)/shard_map/ppermute | solution.py:67
  163.5 20.1 %collective-permute-start.35 = (bf16[128,1792]{1,0:T(8,128)(2,1)S(1)}, bf16[128,1792]{1,0:T(8,128)(2,1)S(1)}, u32[]{:S(2)}, u32[]{:S(2)}) collective-permute-start(bf16[128,1792]{1,0:T(8,128)(2,1)S(1)} %add_convert_fusion.1), channel_id=1, source_target_pairs={{0,10},{1,11},{2,12},{3,13},{4,14},{5,15},{6,8},{7,9},{8,2},{9,3},... | collective-permute-start | bytes 1376264 | tf_op jit(solution)/shard_map/ppermute | solution.py:67
  183.8 0.9 copy-start.1
